TPU v7x, 32 devices: a whole 2x2x4 slice. The times are simulated.
32 devices in a mesh: groups: 2 (over x), pool: 8 (over z, y), tp: 2 (over core).
Axes of the slice: x: 2, y: 2, z: 4, core: 2. Of those that a mesh axis runs over, the one named last changes fastest.
Arguments:
- x_prompt: bfloat16 [4096, 8192], P(('groups', 'pool')), parts along dimension 0, may hold values from -6 to 6
- kv_weight: bfloat16 [8192, 8, 256], P('pool', 'tp'), may hold values from -0.0625 to 0.0625
- block_dest: int32 [512, 1], P('groups'), parts along dimension 0, may hold values from 0 to 7; in each aligned block of 32 rows (0 to 31, 32 to 63, ...) at most 8 rows name the same one
- block_row: int32 [512], P('groups'), parts along dimension 0, may hold values from 0 to 7
- block_fill: int32 [512], P('groups'), parts along dimension 0, may hold values from 1 to 8
- queries: bfloat16 [128, 64, 128], P(('groups', 'pool'), 'tp'), parts along dimension 0
- kv_cache: bfloat16 [128, 256, 8, 256], P(('groups', 'pool'), None, 'tp'), parts along dimension 0
- cache_len: int32 [128], P(('groups', 'pool')), parts along dimension 0, may hold values from 2 to 256, as said below
- out_weight: bfloat16 [8192, 8192], P('tp', 'pool'), may hold values from -0.0625 to 0.0625
Outputs:
- decode_out: bfloat16 [128, 8192], P('groups', ('pool', 'tp')), parts along dimension 0
There are 2 independent parts, one for each index of `groups`. A program takes and returns all parts, laid end to end along the dimension named above; an argument that names none is the same for every part. Nothing has to cross between parts.
Inputs may be any that keep to these rules, and one draw needn't show every extreme that they name: `block_dest`: in the blocks of one index of pool, at most 8 name the same owner index; some index receives exactly 8 from one sender. `cache_len`: every index of pool holds a request whose cache is full.
All inputs are finite; a program needn't handle non-finite values.
Results may differ from a plain program's by a relative error of at most 0.006.
Values may be sent and summed in bfloat16 or wider, within the bound.
No kernel may reach another device: no remote copies, remote signals or barrier semaphores. Data moves between devices by JAX's collectives and lax.ppermute only.
A program may use at most 128 MiB of HBM per device.

v0:
```python
import jax
import jax.numpy as jnp
from jax import lax
from jax.sharding import PartitionSpec as P

BLK = 8


def local(
    x_prompt, kv_weight, block_dest, block_row, block_fill, queries, kv_cache, cache_len, out_weight
):
    npool = lax.axis_size("pool")
    me_pool = lax.axis_index("pool")
    tok_rows = x_prompt.shape[0]
    kv_heads = kv_weight.shape[1]
    pair = kv_weight.shape[2]
    head_size = pair // 2
    width = kv_heads * pair
    blocks_dev = tok_rows // BLK
    capacity = max(2, 2 * blocks_dev // npool)
    piece = lax.all_gather(kv_weight, "pool", axis=0, tiled=True)
    projected = jnp.dot(
        x_prompt, piece.reshape(piece.shape[0], width), preferred_element_type=jnp.float32
    )
    prompt_kv = projected.astype(jnp.bfloat16).reshape(blocks_dev, BLK, kv_heads, pair)
    dests = block_dest[:, 0].reshape(npool, blocks_dev)
    owners = jnp.arange(npool, dtype=jnp.int32)
    slots = jnp.arange(capacity, dtype=jnp.int32)
    hits = (dests[:, :, None] == owners[None, None, :]).astype(jnp.int32)
    ranks = jnp.sum((jnp.cumsum(hits, 1) - hits) * hits, -1)
    match = ((dests == me_pool)[:, None, :] & (ranks[:, None, :] == slots[None, :, None])).astype(
        jnp.int32
    )
    slot_row = jnp.sum(match * block_row.reshape(npool, blocks_dev)[:, None, :], -1)
    slot_fill = jnp.sum(match * block_fill.reshape(npool, blocks_dev)[:, None, :], -1)
    everything = lax.all_gather(prompt_kv, "pool", axis=0, tiled=True)
    numbering = owners[:, None] * blocks_dev + jnp.arange(blocks_dev, dtype=jnp.int32)[None, :]
    slot_block = jnp.sum(match * numbering[:, None, :], -1)
    arrived = jnp.take(everything, slot_block.reshape(-1), axis=0)
    prompt = arrived.reshape(npool * capacity * BLK, kv_heads, pair)
    live_tok = (jnp.arange(BLK, dtype=jnp.int32)[None, None, :] < slot_fill[:, :, None]).reshape(-1)
    prompt_owner = jnp.broadcast_to(slot_row[:, :, None], (npool, capacity, BLK)).reshape(-1)
    rows_dev = queries.shape[0]
    heads = queries.shape[1]
    group = heads // kv_heads
    cache_slots = kv_cache.shape[1]
    query = queries.reshape(rows_dev, kv_heads, group, head_size)
    scale = 1.0 / head_size**0.5
    cache_scores = (
        jnp.einsum(
            "rkgd,rtkd->rkgt",
            query,
            kv_cache[:, :, :, :head_size],
            preferred_element_type=jnp.float32,
        )
        * scale
    )
    cache_live = jnp.arange(cache_slots, dtype=jnp.int32)[None, :] < cache_len[:, None]
    cache_scores = jnp.where(cache_live[:, None, None, :], cache_scores, -jnp.inf)
    prompt_scores = (
        jnp.einsum(
            "rkgd,pkd->rkgp", query, prompt[:, :, :head_size], preferred_element_type=jnp.float32
        )
        * scale
    )
    prompt_live = live_tok[None, :] & (
        prompt_owner[None, :] == jnp.arange(rows_dev, dtype=jnp.int32)[:, None]
    )
    prompt_scores = jnp.where(prompt_live[:, None, None, :], prompt_scores, -jnp.inf)
    top = jnp.maximum(jnp.max(cache_scores, -1), jnp.max(prompt_scores, -1))
    cache_exp = jnp.exp(cache_scores - top[..., None])
    prompt_exp = jnp.exp(prompt_scores - top[..., None])
    total = jnp.sum(cache_exp, -1) + jnp.sum(prompt_exp, -1)
    cache_w = (cache_exp / total[..., None]).astype(jnp.bfloat16)
    prompt_w = (prompt_exp / total[..., None]).astype(jnp.bfloat16)
    mixed = jnp.einsum(
        "rkgt,rtkd->rkgd",
        cache_w,
        kv_cache[:, :, :, head_size:],
        preferred_element_type=jnp.float32,
    )
    mixed = mixed + jnp.einsum(
        "rkgp,pkd->rkgd", prompt_w, prompt[:, :, head_size:], preferred_element_type=jnp.float32
    )
    attended = mixed.reshape(rows_dev, heads * head_size).astype(jnp.bfloat16)
    terms = jnp.dot(
        lax.all_gather(attended, "pool", axis=0, tiled=True),
        out_weight,
        preferred_element_type=jnp.float32,
    )
    return lax.psum_scatter(terms, "tp", scatter_dimension=1, tiled=True).astype(jnp.bfloat16)


def solution(mesh):
    in_specs = (
        P(("groups", "pool"), None),
        P("pool", "tp", None),
        P("groups", None),
        P("groups"),
        P("groups"),
        P(("groups", "pool"), "tp", None),
        P(("groups", "pool"), None, "tp", None),
        P(("groups", "pool")),
        P("tp", "pool"),
    )
    out_specs = P("groups", ("pool", "tp"))
    return jax.shard_map(local, mesh=mesh, in_specs=in_specs, out_specs=out_specs, check_vma=False)
```

profile of v0, /device:TPU:0, one launch (start us, length us, event | category | flops | bytes accessed | tf_op | source)
XLA Modules:
  0.0 384.8 jit_solution(7546964923599919707)
XLA Ops:
  6.5 0.0 copy-start
  6.5 0.0 all-gather.3.cloned.1.call-start
  6.5 0.7 all-gather.3.cloned.1.call-update
  7.3 0.0 all-gather.5.cloned.1.call-start
  7.3 232.5 %all-gather.3.cloned.1.call-done = bf16[8192,4,256]{2,1,0:T(4,128)(2,1)} async-done(((bf16[1024,4,256]{2,1,0:T(4,128)(2,1)}), bf16[8192,4,256]{2,1,0:T(4,128)(2,1)}) %all-gather.3.cloned.1.call-update) | async-done | bytes 16777232 | tf_op jit(solution)/shard_map/all_gather | solution.py:21
  239.8 0.0 copy-start.5
  239.8 11.7 %copy.71 = bf16[1024,8,4,256]{3,1,2,0:T(8,128)(2,1)S(1)} copy(bf16[1024,8,4,256]{3,2,1,0:T(4,128)(2,1)} %bitcast.48) | data formatting | bytes 33554432
  251.6 0.0 copy-done.5
  251.6 0.0 copy-start.3
  251.6 0.0 copy-start.1
  251.6 0.0 copy-start.2
  251.6 0.0 copy-start.4
  251.6 5.4 %convolution_convert_fusion = bf16[256,1024]{1,0:T(8,128)(2,1)} fusion(bf16[256,8192]{1,0:T(8,128)(2,1)S(1)} %copy-done.5, bf16[8192,1024]{1,0:T(8,128)(2,1)S(1)} %bitcast.49), kind=kOutput, calls=%fused_computation.5 | convolution fusion | flops 4295229440 | bytes 21495808 | tf_op jit(solution)/shard_map/dot_general | solution.py:22
  257.0 0.0 all-gather.5.cloned.1.call-update
  257.0 0.0 reduce-scatter.2.cloned.1.call-start
  257.1 0.5 broadcast.106
  257.6 0.0 copy-done.3
  257.6 0.7 reduce.3
  258.3 0.1 reshape_squeeze.3
  258.4 0.0 copy-done.1
  258.4 0.1 mul.60
  258.4 0.0 copy-done.2
  258.4 0.1 mul.57
  258.5 0.1 copy.58
  258.6 0.7 fusion.29
  259.3 0.1 copy.59
  259.4 0.1 iota_add_fusion
  259.5 0.5 select_reduce_fusion.2
  260.0 0.1 reshape.163
  260.1 0.1 reshape.160
  260.1 0.1 iota_compare_fusion.3
  260.2 0.1 lt.64
  260.3 0.1 broadcast_in_dim.66
  260.4 0.1 broadcast_in_dim.67
  260.5 0.1 broadcast_in_dim.42
  260.6 0.1 eq.63
  260.7 0.0 copy-done.4
  260.7 0.1 iota_compare_fusion.5
  260.8 3.1 fusion.28
  263.9 0.0 copy-done
  263.9 0.7 fusion.31
  264.6 64.1 %all-gather.5.cloned.1.call-done = bf16[256,8,4,256]{3,1,2,0:T(8,128)(2,1)} async-done(((bf16[32,8,4,256]{3,1,2,0:T(8,128)(2,1)}), bf16[256,8,4,256]{3,1,2,0:T(8,128)(2,1)}) %all-gather.5.cloned.1.call-update) | async-done | bytes 4194320 | tf_op jit(solution)/shard_map/all_gather | solution.py:36
  328.8 2.8 gather_fusion
  331.6 0.2 bitcast_select_fusion
  331.8 0.4 fusion.30
  332.2 0.2 fusion.16
  332.4 0.2 fusion.18
  332.7 0.4 fusion
  333.1 0.3 fusion.15
  333.5 31.3 %all_gather.11 = bf16[64,4096]{1,0:T(8,128)(2,1)S(1)} all-gather(bf16[8,4096]{1,0:T(8,128)(2,1)S(1)} %bitcast.51), channel_id=1, replica_groups=mesh['groups'=2,'pool'=8,'tp'=2] {'pool'}, dimensions={0}, use_global_device_ids=true | all-gather | bytes 589824 | tf_op jit(solution)/shard_map/all_gather | solution.py:87
  364.7 5.7 %fusion.32 = f32[64,1024]{1,0:T(8,128)} fusion(bf16[64,4096]{1,0:T(8,128)(2,1)S(1)} %all_gather.11, bf16[4096,1024]{1,0:T(8,128)(2,1)} %param.17), kind=kOutput, calls=%fused_computation.58 | convolution fusion | flops 536870912 | bytes 9175040 | tf_op jit(solution)/shard_map/dot_general | solution.py:86
  370.4 0.0 reduce-scatter.2.cloned.1.call-update
  370.4 6.3 %reduce-scatter.2.cloned.1.call-done = f32[64,512]{1,0:T(8,128)} async-done(((f32[64,1024]{1,0:T(8,128)}), f32[64,512]{1,0:T(8,128)}) %reduce-scatter.2.cloned.1.call-update) | async-done | bytes 131088 | tf_op jit(solution)/shard_map/reduce_scatter | solution.py:91
  376.7 1.5 convert_element_type.28
  (11 shorter events, 0.1 us)
Async XLA Ops:
  6.5 257.4 %copy-start = (bf16[8,32,128]{2,1,0:T(8,128)(2,1)S(1)}, bf16[8,32,128]{2,1,0:T(8,128)(2,1)}, u32[]{:S(2)}) copy-start(bf16[8,32,128]{2,1,0:T(8,128)(2,1)} %param.14) | copy-start | bytes 196612
  6.5 233.3 %all-gather.3.cloned.1.call-start = ((), (), s32[]{:S(2)}) async-start(), calls=%async_computation.1 | async-start | bytes 18874368 | tf_op jit(solution)/shard_map/all_gather | solution.py:21
  7.3 321.5 %all-gather.5.cloned.1.call-start = ((), (), s32[]{:S(2)}) async-start(), calls=%async_computation.2 | async-start | bytes 4718592 | tf_op jit(solution)/shard_map/all_gather | solution.py:36
  239.8 11.7 %copy-start.5 = (bf16[256,8192]{1,0:T(8,128)(2,1)S(1)}, bf16[256,8192]{1,0:T(8,128)(2,1)}, u32[]{:S(2)}) copy-start(bf16[256,8192]{1,0:T(8,128)(2,1)} %param.9) | copy-start | bytes 12582916
  251.6 6.0 %copy-start.3 = (s32[256,1]{0,1:T(1,128)S(1)}, s32[256,1]{0,1:T(1,128)}, u32[]{:S(2)}) copy-start(s32[256,1]{0,1:T(1,128)} %param.11) | copy-start | bytes 3076
  251.6 6.8 %copy-start.1 = (s32[256]{0:T(256)S(1)}, s32[256]{0:T(256)}, u32[]{:S(2)}) copy-start(s32[256]{0:T(256)} %param.12) | copy-start | bytes 3076
  251.6 6.8 %copy-start.2 = (s32[256]{0:T(256)S(1)}, s32[256]{0:T(256)}, u32[]{:S(2)}) copy-start(s32[256]{0:T(256)} %param.13) | copy-start | bytes 3076
  251.6 9.1 %copy-start.4 = (s32[8]{0:T(128)S(1)}, s32[8]{0:T(128)}, u32[]{:S(2)}) copy-start(s32[8]{0:T(128)} %param.16) | copy-start | bytes 100
  257.0 119.6 %reduce-scatter.2.cloned.1.call-start = ((), (), s32[]{:S(2)}) async-start(), calls=%async_computation.3 | async-start | bytes 393216 | tf_op jit(solution)/shard_map/reduce_scatter | solution.py:91
Sparse Core Ops, SparseCore 0:
  9.5 230.3 all-gather.2
  257.2 71.5 all-gather.4
  370.5 6.1 reduce-scatter.1
where the time goes:
time: 385 us
  waiting for transfers between devices  304 us (79%)
  blocking collectives  31.3 us (8%)
  local copies, waits for them, and re-layouts  19.2 us (5%)
  between operations  13.3 us (3%)
  matrix products  12.9 us (3%)
  other arithmetic  4.34 us (1%)
    all_gather x1, waiting for transfers between devices, local(): piece = lax.all_gather(kv_weight, 'pool', axis=0, tiled=True)  233 us
    all_gather x1, waiting for transfers between devices, local(): everything = lax.all_gather(prompt_kv, 'pool', axis=0, tiled=True)  64.1 us
    all_gather x1, blocking collectives, local(): lax.all_gather(attended, 'pool', axis=0, tiled=True)  31.3 us
    unnamed x15, local copies, waits for them, and re-layouts  12.3 us
  transfers between devices with their start and end apart: 3, of which 3 were waited for; matrix products, arithmetic and copies ran while one was open for 2% of the time, Pallas kernels for 0%

commit v1 on v0

v1 whole, which is shorter than its diff:
```python
import jax
import jax.numpy as jnp
from jax import lax
from jax.sharding import PartitionSpec as P

BLK = 8


def local(
    x_prompt, kv_weight, block_dest, block_row, block_fill, queries, kv_cache, cache_len, out_weight
):
    n = lax.axis_size("pool")
    ntp = lax.axis_size("tp")
    me = lax.axis_index("pool")
    core = lax.axis_index("tp")
    tokens, width = x_prompt.shape
    part = width // n
    kvh = kv_weight.shape[1]
    hd = kv_weight.shape[2] // 2
    rows, heads = queries.shape[0], queries.shape[1]
    group = heads // kvh
    cache_slots = kv_cache.shape[1]
    blocks = tokens // BLK
    cap = max(2, 2 * blocks // n)
    slots = cap * BLK
    scale = 1.0 / hd**0.5

    half = tokens // ntp
    first, second = [], []
    for k in range(1, n):
        sent = lax.dynamic_slice(x_prompt, (core * half, (me ^ k) * part), (half, part))
        first.append(lax.ppermute(sent, "pool", [(i, i ^ k) for i in range(n)]))
    for got in first:
        second.append(lax.ppermute(got, "tp", [(i, (i + 1) % ntp) for i in range(ntp)]))
    own = lax.dynamic_slice(x_prompt, (0, me * part), (tokens, part))
    chunks = [own]
    for a, b in zip(first, second):
        chunks.append(jnp.where(core == 0, jnp.concatenate([a, b]), jnp.concatenate([b, a])))
    arrived = jnp.stack(chunks)

    dests = block_dest[:, 0].reshape(n, blocks)
    owners = jnp.arange(n, dtype=jnp.int32)
    hits = (dests[:, :, None] == owners[None, None, :]).astype(jnp.int32)
    ranks = jnp.sum((jnp.cumsum(hits, 1) - hits) * hits, -1)
    match = (
        (dests[None, :, None, :] == owners[:, None, None, None])
        & (ranks[None, :, None, :] == jnp.arange(cap, dtype=jnp.int32)[None, None, :, None])
    ).astype(jnp.int32)
    slot_row = jnp.sum(match * block_row.reshape(1, n, 1, blocks), -1)
    slot_fill = jnp.sum(match * block_fill.reshape(1, n, 1, blocks), -1)
    live = jnp.arange(BLK, dtype=jnp.int32) < slot_fill[..., None]
    rowof = jnp.where(live, slot_row[..., None], -1).reshape(n, n * slots)
    rowmask = rowof[:, None, :] == jnp.arange(rows, dtype=jnp.int32)[None, :, None]

    place = (
        match.astype(jnp.bfloat16)[:, :, :, None, :, None]
        * jnp.eye(BLK, dtype=jnp.bfloat16)[None, None, None, :, None, :]
    ).reshape(n, n, slots, tokens)
    place = jnp.take(place, me ^ owners, axis=1)
    padded = jnp.einsum("qkst,ktp->qksp", place, arrived, preferred_element_type=jnp.bfloat16)
    padded = jnp.take(padded, me ^ owners, axis=1).reshape(n, n * slots, part)

    allq = lax.all_gather(queries, "pool", axis=0, tiled=True).reshape(n, rows, kvh, group, hd)
    keyed = jnp.einsum(
        "qrhgd,phd->qhrgp", allq, kv_weight[:, :, :hd], preferred_element_type=jnp.float32
    ).astype(jnp.bfloat16)
    raw = jnp.einsum("qhrgp,qtp->qhrgt", keyed, padded, preferred_element_type=jnp.float32)
    raw = jnp.sum(jnp.where(rowmask[:, None, :, None, :], raw, 0.0), 2)
    parts = lax.all_to_all(raw, "pool", split_axis=0, concat_axis=0, tiled=True)
    scores = jnp.sum(parts, 0) * scale

    mymask = lax.dynamic_index_in_dim(rowmask, me, 0, keepdims=False)
    prompt_scores = jnp.where(mymask[:, None, None, :], scores[None], -jnp.inf)
    query = queries.reshape(rows, kvh, group, hd)
    cache_scores = (
        jnp.einsum(
            "rhgd,rthd->rhgt", query, kv_cache[:, :, :, :hd], preferred_element_type=jnp.float32
        )
        * scale
    )
    cache_live = jnp.arange(cache_slots, dtype=jnp.int32)[None, :] < cache_len[:, None]
    cache_scores = jnp.where(cache_live[:, None, None, :], cache_scores, -jnp.inf)
    top = jnp.maximum(jnp.max(cache_scores, -1), jnp.max(prompt_scores, -1))
    cache_exp = jnp.exp(cache_scores - top[..., None])
    prompt_exp = jnp.exp(prompt_scores - top[..., None])
    total = jnp.sum(cache_exp, -1) + jnp.sum(prompt_exp, -1)
    cache_w = (cache_exp / total[..., None]).astype(jnp.bfloat16)
    prompt_w = jnp.sum(prompt_exp / total[..., None], 0).astype(jnp.bfloat16)
    cached = jnp.einsum(
        "rhgt,rthd->rhgd", cache_w, kv_cache[:, :, :, hd:], preferred_element_type=jnp.float32
    )

    allw = lax.all_gather(prompt_w, "pool", axis=0)
    spread = jnp.where(rowmask[:, None, :, None, :], allw[:, :, None], 0).astype(jnp.bfloat16)
    mixed = jnp.einsum(
        "qhrgt,qtp->qhrgp", spread, padded, preferred_element_type=jnp.float32
    ).astype(jnp.bfloat16)
    terms = jnp.einsum(
        "qhrgp,phd->qrhgd", mixed, kv_weight[:, :, hd:], preferred_element_type=jnp.float32
    ).astype(jnp.bfloat16)
    total_terms = cached
    for k in range(n):
        sent = lax.dynamic_index_in_dim(terms, me ^ k, 0, keepdims=False)
        if k:
            sent = lax.ppermute(sent, "pool", [(i, i ^ k) for i in range(n)])
        total_terms = total_terms + sent.astype(jnp.float32)
    attended = total_terms.reshape(rows, heads * hd).astype(jnp.bfloat16)

    cols = out_weight.shape[1] // ntp
    weights = []
    for j in range(ntp):
        piece = lax.dynamic_slice(
            out_weight, (0, ((core + j) % ntp) * cols), (out_weight.shape[0], cols)
        )
        if j:
            piece = lax.ppermute(piece, "tp", [(i, (i + j) % ntp) for i in range(ntp)])
        weights.append(piece)
    full = lax.all_gather(attended, ("tp", "pool"), axis=0).reshape(ntp, n * rows, heads * hd)
    out = jnp.zeros((n * rows, cols), jnp.float32)
    for j in range(ntp):
        out = out + jnp.dot(
            lax.dynamic_index_in_dim(full, (core - j) % ntp, 0, keepdims=False),
            weights[j],
            preferred_element_type=jnp.float32,
        )
    return out.astype(jnp.bfloat16)


def solution(mesh):
    in_specs = (
        P(("groups", "pool"), None),
        P("pool", "tp", None),
        P("groups", None),
        P("groups"),
        P("groups"),
        P(("groups", "pool"), "tp", None),
        P(("groups", "pool"), None, "tp", None),
        P(("groups", "pool")),
        P("tp", "pool"),
    )
    out_specs = P("groups", ("pool", "tp"))
    return jax.shard_map(local, mesh=mesh, in_specs=in_specs, out_specs=out_specs, check_vma=False)
```

time: 385 us -> 326 us (0.85)
  waiting for transfers between devices: 304 us -> 56.5 us
  local copies, waits for them, and re-layouts: 19.2 us -> 94.9 us
  starting transfers between devices: 0.08 us -> 37 us
  blocking collectives: 31.3 us -> 64.9 us
  other arithmetic: 4.34 us -> 29.2 us
  matrix products: 12.9 us -> 29.6 us
    all_gather x2 -> x1, waiting for transfers between devices: 297 us -> 37.8 us  [local(): lax.all_gather(attended, ('tp', 'pool'), axis=0)]
    mul x2 -> x6, local copies, waits for them, and re-layouts: 0.15 us -> 58.7 us  [the longest x4 58.6 us: local(): match.astype(jnp.bfloat16)[:, :, :, None, :, None]]
    all_gather x1 -> x2, blocking collectives: 31.3 us -> 64.9 us  [the longest x1 33.9 us: local(): lax.all_gather(queries, 'pool', axis=0, tiled=True)]
    ppermute x0 -> x22, starting transfers between devices: none -> 25.8 us  [the longest x7 12.7 us: local(): first.append(lax.ppermute(sent, 'pool', [(i, i ^ k) for i in range(n)]))]
    dot_general x6 -> x8, matrix products: 12.9 us -> 29.6 us  [the longest x1 7.79 us: local(): jnp.einsum('qkst,ktp->qksp', place, arrived, preferred_element_type=jnp.b...]
    gather x1 -> x3, local copies, waits for them, and re-layouts: 2.8 us -> 18.5 us  [the longest x2 16.5 us: local(): padded = jnp.take(padded, me ^ owners, axis=1).reshape(n, n * slots, part)]
    unnamed x1 -> x7, other arithmetic: 0.66 us -> 14.1 us
    all_to_all x0 -> x1, starting transfers between devices: none -> 11.2 us  [local(): parts = lax.all_to_all(raw, 'pool', split_axis=0, concat_axis=0, tiled=True)]
  transfers between devices with their start and end apart: 3 -> 24, of which waited for: 3 -> 8; matrix products, arithmetic and copies ran while one was open for 2% -> 45% of each run, Pallas kernels for 0% -> 0%
where the time goes in v1:
time: 326 us
  local copies, waits for them, and re-layouts  94.9 us (29%)
  blocking collectives  64.9 us (20%)
  waiting for transfers between devices  56.5 us (17%)
  starting transfers between devices  37 us (11%)
  matrix products  29.6 us (9%)
  other arithmetic  29.2 us (9%)
  between operations  13.8 us (4%)
    mul x4, local copies, waits for them, and re-layouts, local(): match.astype(jnp.bfloat16)[:, :, :, None, :, None]  58.6 us
    all_gather x1, waiting for transfers between devices, local(): lax.all_gather(attended, ('tp', 'pool'), axis=0)  37.8 us
    all_gather x1, blocking collectives, local(): lax.all_gather(queries, 'pool', axis=0, tiled=True)  33.9 us
    all_gather x1, blocking collectives, local(): allw = lax.all_gather(prompt_w, 'pool', axis=0)  31 us
    gather x2, local copies, waits for them, and re-layouts, local(): padded = jnp.take(padded, me ^ owners, axis=1).reshape(n, n * slots, part)  16.5 us
    unnamed x7, other arithmetic  14.1 us
    ppermute x7, starting transfers between devices, local(): first.append(lax.ppermute(sent, 'pool', [(i, i ^ k) for i in range(n)]))  12.7 us
    ppermute x7, starting transfers between devices, local(): sent = lax.ppermute(sent, 'pool', [(i, i ^ k) for i in range(n)])  11.3 us
  transfers between devices with their start and end apart: 24, of which 8 were waited for; matrix products, arithmetic and copies ran while one was open for 45% of the time, Pallas kernels for 0%

profile of v1, /device:TPU:0, one launch (start us, length us, event | category | flops | bytes accessed | tf_op | source)
XLA Modules:
  0.0 325.9 jit_solution(9129347744950304435)
XLA Ops:
  6.5 2.6 fusion.77
  9.1 3.0 collective-permute-start
  12.1 1.6 collective-permute-start.2
  13.7 3.0 collective-permute-start.6
  16.7 1.3 collective-permute-start.8
  18.0 0.5 broadcast.200
  18.5 1.3 reduce.3
  20.0 0.7 fusion.79
  20.9 11.2 %mul.116 = bf16[8,8,8,8,32,8]{5,4,3,2,1,0:T(8,128)(2,1)} broadcast(bf16[8,8,8,32]{3,2,1,0:T(8,128)(2,1)S(1)} %fusion.62), dimensions={0,1,2,4} | broadcast | bytes 2129920 | tf_op jit(solution)/shard_map/mul | solution.py:56
  32.1 46.6 %mul.117 = bf16[8,8,64,256]{3,2,1,0:T(8,128)(2,1)S(1)} reshape(bf16[8,8,8,8,32,8]{5,4,3,2,1,0:T(8,128)(2,1)} %mul.116) | data formatting | bytes 4194304 | tf_op jit(solution)/shard_map/mul | solution.py:56
  78.8 0.7 mul.119
  79.6 2.2 fusion.60
  82.0 0.2 broadcast_in_dim.127
  82.3 0.2 lt.153
  82.5 3.2 fusion.78
  85.8 33.9 %all_gather.11 = bf16[64,32,128]{2,1,0:T(8,128)(2,1)} all-gather(bf16[8,32,128]{2,1,0:T(8,128)(2,1)S(1)} %copy-done.5), channel_id=1, replica_groups=mesh['groups'=2,'pool'=8,'tp'=2] {'pool'}, dimensions={0}, use_global_device_ids=true | all-gather | bytes 589824 | tf_op jit(solution)/shard_map/all_gather | solution.py:63
  119.7 1.5 broadcast_multiply_fusion
  121.2 4.6 %constant_dynamic-slice_fusion = bf16[4096,512]{1,0:T(8,128)(2,1)} fusion(bf16[4096,1024]{1,0:T(8,128)(2,1)} %param.17, s32[]{:T(128)S(6)} %select_n.262), kind=kLoop, calls=%fused_computation.100 | loop fusion | bytes 8388612 | tf_op jit(solution)/shard_map/dynamic_slice | solution.py:112
  125.8 1.9 bitcast_dynamic-update-slice_fusion
  127.8 0.6 collective-permute-start.3
  128.3 0.6 collective-permute-start.10
  129.0 3.3 %collective-permute-start.12 = (bf16[128,1024]{1,0:T(8,128)(2,1)S(1)}, bf16[128,1024]{1,0:T(8,128)(2,1)}, u32[]{:S(2)}, u32[]{:S(2)}) collective-permute-start(bf16[128,1024]{1,0:T(8,128)(2,1)S(1)} %get-tuple-element.9), channel_id=1, source_target_pairs={{0,14},{2,12},{4,10},{6,8},{8,6},{10,4},{12,2},{14,0},{1,15},{3,13... | collective-permute-start | bytes 786440 | tf_op jit(solution)/shard_map/ppermute | solution.py:32
  132.4 2.0 gather_fusion
  134.4 0.5 collective-permute-start.7
  134.9 2.3 fusion.47
  137.3 2.2 fusion.48
  139.5 0.3 collective-permute-done.10
  139.8 0.2 collective-permute-start.21
  140.0 4.5 %collective-permute-done.12 = bf16[128,1024]{1,0:T(8,128)(2,1)} collective-permute-done((bf16[128,1024]{1,0:T(8,128)(2,1)S(1)}, bf16[128,1024]{1,0:T(8,128)(2,1)}, u32[]{:S(2)}, u32[]{:S(2)}) %collective-permute-start.12) | collective-permute-done | bytes 262176 | tf_op jit(solution)/shard_map/ppermute | solution.py:32
  144.5 0.5 collective-permute-start.13
  145.0 2.2 fusion.49
  147.2 2.0 fusion.50
  149.2 2.0 fusion.51
  151.2 2.0 fusion.52
  153.2 2.0 fusion.53
  155.2 7.8 %convolution_bitcast_fusion = bf16[8,8,64,1024]{3,2,0,1:T(8,128)(2,1)} fusion(bf16[8,256,1024]{2,1,0:T(8,128)(2,1)} %fusion.53, bf16[8,8,64,256]{3,2,1,0:T(8,128)(2,1)S(1)} %copy-done.1, pred[8]{0:T(512)(128)(4,1)S(1)} %compare_and_fusion), kind=kOutput, calls=%fused_computation.7 | convolution fusion | flops 2148532224 | bytes 14680072 | tf_op jit(solution)/shard_map/qkst,ktp->qksp/dot_general | solution.py:60
  163.0 8.1 %gather_fusion.1 = bf16[8,8,64,1024]{3,2,1,0:T(8,128)(2,1)} fusion(bf16[8,8,64,1024]{3,2,0,1:T(8,128)(2,1)} %convolution_bitcast_fusion, s32[1024]{0:T(1024)S(1)} %pad_clamp_fusion), kind=kCustom, calls=%fused_computation.1 | custom fusion | bytes 16777248 | tf_op jit(solution)/shard_map/jit(_take)/gather | solution.py:61
  171.1 8.4 %copy.45 = bf16[8,8,64,1024]{3,2,1,0:T(8,128)(2,1)} copy(bf16[8,8,64,1024]{3,2,0,1:T(8,128)(2,1)} %bitcast.122) | data formatting | bytes 16777216 | tf_op jit(solution)/shard_map/jit(_take)/gather | solution.py:61
  179.5 7.6 %bitcast_select_fusion = bf16[8,512,1024]{2,1,0:T(8,128)(2,1)} fusion(bf16[8,8,64,1024]{3,2,1,0:T(8,128)(2,1)} %copy.45, pred[512]{0:T(512)(128)(4,1)S(1)} %broadcast_in_dim.133), kind=kLoop, calls=%fused_computation.6 | loop fusion | flops 4194304 | bytes 16777728 | tf_op jit(solution)/shard_map/jit(_take)/select_n | solution.py:61
  187.1 6.7 %select_reduce_fusion = f32[8,4,8,512]{3,2,1,0:T(8,128)} fusion(pred[8,8,512]{2,1,0:T(8,128)(4,1)S(1)} %iota_compare_fusion, bf16[8,512,1024]{2,1,0:T(8,128)(2,1)} %bitcast_select_fusion, bf16[1024,4,128]{2,1,0:T(4,128)(2,1)S(1)} %get-tuple-element.17, bf16[8,8,4,8,128]{4,3,2,1,0:T(8,128)(2,1)S(1)} %bitcast.125), kind=kOutput, calls=%fused_computation.14 | convolution fusion | flops 2688417792 | bytes 10518528 | tf_op jit(solution)/shard_map/qhrgp,qtp->qhrgt/dot_general | solution.py:67
  193.8 11.2 %all-to-all-start = ((f32[8,4,8,512]{3,2,1,0:T(8,128)}), f32[8,4,8,512]{3,2,1,0:T(8,128)S(1)}, u32[]{:S(2)}, u32[]{:S(2)}) async-start(f32[8,4,8,512]{3,2,1,0:T(8,128)} %select_reduce_fusion), calls=%async_computation | async-start | bytes 1048576 | tf_op jit(solution)/shard_map/all_to_all | solution.py:69
  205.1 3.0 fusion.76
  208.2 0.7 fusion.80
  208.9 10.7 %all-to-all-done = f32[8,4,8,512]{3,2,1,0:T(8,128)S(1)} async-done(((f32[8,4,8,512]{3,2,1,0:T(8,128)}), f32[8,4,8,512]{3,2,1,0:T(8,128)S(1)}, u32[]{:S(2)}, u32[]{:S(2)}) %all-to-all-start) | async-done | bytes 524320 | tf_op jit(solution)/shard_map/all_to_all | solution.py:69
  219.8 0.3 fusion.45
  220.1 0.2 fusion.63
  220.3 0.2 fusion.46
  220.5 31.0 %all-gather = bf16[32,8,512]{2,1,0:T(8,128)(2,1)S(1)} all-gather(bf16[4,8,512]{2,1,0:T(8,128)(2,1)S(1)} %fusion.46), channel_id=2, replica_groups=mesh['groups'=2,'pool'=8,'tp'=2] {'pool'}, dimensions={0}, use_global_device_ids=true | all-gather | bytes 294912 | tf_op jit(solution)/shard_map/all_gather | solution.py:93
  251.5 5.8 %fusion.13 = bf16[8,4,8,8,1024]{4,3,2,0,1:T(8,128)(2,1)S(1)} fusion(bf16[8,512,1024]{2,1,0:T(8,128)(2,1)} %bitcast_select_fusion, pred[8,8,512]{2,1,0:T(8,128)(4,1)S(1)} %iota_compare_fusion, bf16[8,4,8,512]{3,2,1,0:T(8,128)(2,1)S(1)} %bitcast.126), kind=kOutput, calls=%fused_computation.17 | convolution fusion | flops 2150629376 | bytes 12877824 | tf_op jit(solution)/shard_map/qhrgt,qtp->qhrgp/dot_general | solution.py:95
  257.3 1.2 fusion.24
  258.6 2.5 collective-permute-start.20
  261.1 0.6 collective-permute-start.19
  261.7 4.6 %collective-permute-start.17 = (bf16[8,4,8,128]{3,2,1,0:T(8,128)(2,1)S(1)}, bf16[8,4,8,128]{3,2,1,0:T(8,128)(2,1)S(1)}, u32[]{:S(2)}, u32[]{:S(2)}) collective-permute-start(bf16[8,4,8,128]{3,2,1,0:T(8,128)(2,1)S(1)} %get-tuple-element.22), channel_id=1, source_target_pairs={{0,8},{2,10},{4,12},{6,14},{8,0},{10,2},{12,4},{14,6},{1,9},{3,11}... | collective-permute-start | bytes 196616 | tf_op jit(solution)/shard_map/ppermute | solution.py:105
  266.4 0.8 collective-permute-done.19
  267.2 0.4 collective-permute-start.15
  267.5 0.2 collective-permute-done.18
  267.7 3.1 collective-permute-start.14
  270.9 0.6 collective-permute-done.16
  271.5 1.6 collective-permute-done.14
  273.1 0.5 add_convert_fusion
  273.6 0.7 convert_element_type.123
  274.3 37.8 %all-gather.3.cloned.1.call-done = bf16[16,8,4096]{2,1,0:T(8,128)(2,1)} async-done(((bf16[1,8,4096]{2,1,0:T(8,128)(2,1)}), bf16[16,8,4096]{2,1,0:T(8,128)(2,1)}) %all-gather.3.cloned.1.call-update) | async-done | bytes 1048592 | tf_op jit(solution)/shard_map/all_gather | solution.py:118
  312.0 3.3 %fusion.8 = f32[64,512]{1,0:T(8,128)S(1)} fusion(bf16[4096,1024]{1,0:T(8,128)(2,1)} %param.17, s32[]{:T(128)S(6)} %select_n.258, bf16[2,64,4096]{2,1,0:T(8,128)(2,1)} %bitcast.123, s32[]{:T(128)S(6)} %select_n.257), kind=kOutput, calls=%fused_computation.12 | convolution fusion | flops 268435456 | bytes 4849672 | tf_op jit(solution)/shard_map/dot_general | solution.py:121
  315.3 3.7 %fusion.37 = bf16[64,512]{1,0:T(8,128)(2,1)} fusion(f32[64,512]{1,0:T(8,128)S(1)} %fusion.8, bf16[4096,512]{1,0:T(8,128)(2,1)} %collective-permute-done.21, bf16[2,64,4096]{2,1,0:T(8,128)(2,1)S(1)} %bitcast.124, s32[]{:T(128)S(6)} %select_n.260), kind=kOutput, calls=%fused_computation.34 | convolution fusion | flops 268500992 | bytes 4915204 | tf_op jit(solution)/shard_map/dot_general | solution.py:121
  (71 shorter events, 1.7 us)
Async XLA Ops:
  9.1 118.6 %collective-permute-start = (bf16[128,1024]{1,0:T(8,128)(2,1)}, bf16[128,1024]{1,0:T(8,128)(2,1)}, u32[]{:S(2)}, u32[]{:S(2)}) collective-permute-start(bf16[128,1024]{1,0:T(8,128)(2,1)} %get-tuple-element.14), channel_id=1, source_target_pairs={{0,2},{2,0},{4,6},{6,4},{8,10},{10,8},{12,14},{14,12},{1,3},{3,1},... | collective-permute-start | bytes 786440 | tf_op jit(solution)/shard_map/ppermute | solution.py:32
  12.1 115.6 %collective-permute-start.2 = (bf16[128,1024]{1,0:T(8,128)(2,1)}, bf16[128,1024]{1,0:T(8,128)(2,1)}, u32[]{:S(2)}, u32[]{:S(2)}) collective-permute-start(bf16[128,1024]{1,0:T(8,128)(2,1)} %get-tuple-element.13), channel_id=1, source_target_pairs={{0,4},{2,6},{4,0},{6,2},{8,12},{10,14},{12,8},{14,10},{1,5},{3,7},... | collective-permute-start | bytes 786440 | tf_op jit(solution)/shard_map/ppermute | solution.py:32
  13.7 114.6 %collective-permute-start.4 = (bf16[128,1024]{1,0:T(8,128)(2,1)}, bf16[128,1024]{1,0:T(8,128)(2,1)}, u32[]{:S(2)}, u32[]{:S(2)}) collective-permute-start(bf16[128,1024]{1,0:T(8,128)(2,1)} %get-tuple-element.12), channel_id=1, source_target_pairs={{0,6},{2,4},{4,2},{6,0},{8,14},{10,12},{12,10},{14,8},{1,7},{3,5},... | collective-permute-start | bytes 786440 | tf_op jit(solution)/shard_map/ppermute | solution.py:32
  13.7 115.3 %collective-permute-start.6 = (bf16[128,1024]{1,0:T(8,128)(2,1)}, bf16[128,1024]{1,0:T(8,128)(2,1)}, u32[]{:S(2)}, u32[]{:S(2)}) collective-permute-start(bf16[128,1024]{1,0:T(8,128)(2,1)} %get-tuple-element.11), channel_id=1, source_target_pairs={{0,8},{2,10},{4,12},{6,14},{8,0},{10,2},{12,4},{14,6},{1,9},{3,11}... | collective-permute-start | bytes 786440 | tf_op jit(solution)/shard_map/ppermute | solution.py:32
  16.7 115.6 %collective-permute-start.8 = (bf16[128,1024]{1,0:T(8,128)(2,1)}, bf16[128,1024]{1,0:T(8,128)(2,1)}, u32[]{:S(2)}, u32[]{:S(2)}) collective-permute-start(bf16[128,1024]{1,0:T(8,128)(2,1)} %get-tuple-element.10), channel_id=1, source_target_pairs={{0,10},{2,8},{4,14},{6,12},{8,2},{10,0},{12,6},{14,4},{1,11},{3,9}... | collective-permute-start | bytes 786440 | tf_op jit(solution)/shard_map/ppermute | solution.py:32
  32.1 47.4 %copy-start.6 = (s32[256]{0:T(256)S(1)}, s32[256]{0:T(256)}, u32[]{:S(2)}) copy-start(s32[256]{0:T(256)} %param.13) | copy-start | bytes 3076
  32.1 47.5 %copy-start.7 = (s32[256]{0:T(256)S(1)}, s32[256]{0:T(256)}, u32[]{:S(2)}) copy-start(s32[256]{0:T(256)} %param.12) | copy-start | bytes 3076
  78.6 7.1 %copy-start.5 = (bf16[8,32,128]{2,1,0:T(8,128)(2,1)S(1)}, bf16[8,32,128]{2,1,0:T(8,128)(2,1)}, u32[]{:S(2)}) copy-start(bf16[8,32,128]{2,1,0:T(8,128)(2,1)} %param.14) | copy-start | bytes 196612
  121.2 11.2 %copy-start = (bf16[8,8,64,256]{3,2,1,0:T(8,128)(2,1)S(1)}, bf16[8,8,64,256]{3,2,1,0:T(8,128)(2,1)}, u32[]{:S(2)}) copy-start(bf16[8,8,64,256]{3,2,1,0:T(8,128)(2,1)} %broadcast_multiply_fusion) | copy-start | bytes 6291460
  127.7 6.7 %collective-permute-start.1 = (bf16[128,1024]{1,0:T(8,128)(2,1)}, bf16[128,1024]{1,0:T(8,128)(2,1)}, u32[]{:S(2)}, u32[]{:S(2)}) collective-permute-start(bf16[128,1024]{1,0:T(8,128)(2,1)} %collective-permute-done), channel_id=1, source_target_pairs={{0,1},{1,0},{2,3},{3,2},{4,5},{5,4},{6,7},{7,6},{8,9},{9,8},{10,11... | collective-permute-start | bytes 786440 | tf_op jit(solution)/shard_map/ppermute | solution.py:34
  127.8 9.5 %collective-permute-start.3 = (bf16[128,1024]{1,0:T(8,128)(2,1)}, bf16[128,1024]{1,0:T(8,128)(2,1)}, u32[]{:S(2)}, u32[]{:S(2)}) collective-permute-start(bf16[128,1024]{1,0:T(8,128)(2,1)} %collective-permute-done.2), channel_id=1, source_target_pairs={{0,1},{1,0},{2,3},{3,2},{4,5},{5,4},{6,7},{7,6},{8,9},{9,8},{10,11... | collective-permute-start | bytes 786440 | tf_op jit(solution)/shard_map/ppermute | solution.py:34
  128.3 11.4 %collective-permute-start.10 = (bf16[128,1024]{1,0:T(8,128)(2,1)}, bf16[128,1024]{1,0:T(8,128)(2,1)}, u32[]{:S(2)}, u32[]{:S(2)}) collective-permute-start(bf16[128,1024]{1,0:T(8,128)(2,1)} %get-tuple-element.15), channel_id=1, source_target_pairs={{0,12},{2,14},{4,8},{6,10},{8,4},{10,6},{12,0},{14,2},{1,13},{3,15... | collective-permute-start | bytes 786440 | tf_op jit(solution)/shard_map/ppermute | solution.py:32
  129.0 15.5 %collective-permute-start.12 = (bf16[128,1024]{1,0:T(8,128)(2,1)S(1)}, bf16[128,1024]{1,0:T(8,128)(2,1)}, u32[]{:S(2)}, u32[]{:S(2)}) collective-permute-start(bf16[128,1024]{1,0:T(8,128)(2,1)S(1)} %get-tuple-element.9), channel_id=1, source_target_pairs={{0,14},{2,12},{4,10},{6,8},{8,6},{10,4},{12,2},{14,0},{1,15},{3,13... | collective-permute-start | bytes 786440 | tf_op jit(solution)/shard_map/ppermute | solution.py:32
  132.2 12.3 %collective-permute-start.5 = (bf16[128,1024]{1,0:T(8,128)(2,1)}, bf16[128,1024]{1,0:T(8,128)(2,1)}, u32[]{:S(2)}, u32[]{:S(2)}) collective-permute-start(bf16[128,1024]{1,0:T(8,128)(2,1)} %collective-permute-done.4), channel_id=1, source_target_pairs={{0,1},{1,0},{2,3},{3,2},{4,5},{5,4},{6,7},{7,6},{8,9},{9,8},{10,11... | collective-permute-start | bytes 786440 | tf_op jit(solution)/shard_map/ppermute | solution.py:34
  134.4 20.8 %copy-start.1 = (bf16[8,8,64,256]{3,2,1,0:T(8,128)(2,1)S(1)}, bf16[8,8,64,256]{3,2,1,0:T(8,128)(2,1)}, u32[]{:S(2)}) copy-start(bf16[8,8,64,256]{3,2,1,0:T(8,128)(2,1)} %gather_fusion) | copy-start | bytes 6291460
  134.4 12.7 %collective-permute-start.7 = (bf16[128,1024]{1,0:T(8,128)(2,1)}, bf16[128,1024]{1,0:T(8,128)(2,1)S(1)}, u32[]{:S(2)}, u32[]{:S(2)}) collective-permute-start(bf16[128,1024]{1,0:T(8,128)(2,1)} %collective-permute-done.6), channel_id=1, source_target_pairs={{0,1},{1,0},{2,3},{3,2},{4,5},{5,4},{6,7},{7,6},{8,9},{9,8},{10,11... | collective-permute-start | bytes 786440 | tf_op jit(solution)/shard_map/ppermute | solution.py:34
  137.3 11.9 %collective-permute-start.9 = (bf16[128,1024]{1,0:T(8,128)(2,1)}, bf16[128,1024]{1,0:T(8,128)(2,1)S(1)}, u32[]{:S(2)}, u32[]{:S(2)}) collective-permute-start(bf16[128,1024]{1,0:T(8,128)(2,1)} %collective-permute-done.8), channel_id=1, source_target_pairs={{0,1},{1,0},{2,3},{3,2},{4,5},{5,4},{6,7},{7,6},{8,9},{9,8},{10,11... | collective-permute-start | bytes 786440 | tf_op jit(solution)/shard_map/ppermute | solution.py:34
  139.8 175.6 %collective-permute-start.21 = (bf16[4096,512]{1,0:T(8,128)(2,1)}, bf16[4096,512]{1,0:T(8,128)(2,1)}, u32[]{:S(2)}, u32[]{:S(2)}) collective-permute-start(bf16[4096,512]{1,0:T(8,128)(2,1)} %constant_dynamic-slice_fusion), channel_id=1, source_target_pairs={{0,1},{1,0},{2,3},{3,2},{4,5},{5,4},{6,7},{7,6},{8,9},{9,8},{10,11... | collective-permute-start | bytes 12582920 | tf_op jit(solution)/shard_map/ppermute | solution.py:116
  144.5 6.8 %collective-permute-start.11 = (bf16[128,1024]{1,0:T(8,128)(2,1)}, bf16[128,1024]{1,0:T(8,128)(2,1)S(1)}, u32[]{:S(2)}, u32[]{:S(2)}) collective-permute-start(bf16[128,1024]{1,0:T(8,128)(2,1)} %collective-permute-done.10), channel_id=1, source_target_pairs={{0,1},{1,0},{2,3},{3,2},{4,5},{5,4},{6,7},{7,6},{8,9},{9,8},{10,11... | collective-permute-start | bytes 786440 | tf_op jit(solution)/shard_map/ppermute | solution.py:34
  144.5 8.7 %collective-permute-start.13 = (bf16[128,1024]{1,0:T(8,128)(2,1)}, bf16[128,1024]{1,0:T(8,128)(2,1)S(1)}, u32[]{:S(2)}, u32[]{:S(2)}) collective-permute-start(bf16[128,1024]{1,0:T(8,128)(2,1)} %collective-permute-done.12), channel_id=1, source_target_pairs={{0,1},{1,0},{2,3},{3,2},{4,5},{5,4},{6,7},{7,6},{8,9},{9,8},{10,11... | collective-permute-start | bytes 786440 | tf_op jit(solution)/shard_map/ppermute | solution.py:34
  179.5 7.6 %copy-start.4 = (bf16[64,32,128]{2,1,0:T(8,128)(2,1)S(1)}, bf16[64,32,128]{2,1,0:T(8,128)(2,1)}, u32[]{:S(2)}) copy-start(bf16[64,32,128]{2,1,0:T(8,128)(2,1)} %all_gather.11) | copy-start | bytes 1572868
  187.1 18.0 %copy-start.8 = (s32[8]{0:T(128)S(1)}, s32[8]{0:T(128)}, u32[]{:S(2)}) copy-start(s32[8]{0:T(128)} %param.16) | copy-start | bytes 100
  193.8 25.8 %all-to-all-start = ((f32[8,4,8,512]{3,2,1,0:T(8,128)}), f32[8,4,8,512]{3,2,1,0:T(8,128)S(1)}, u32[]{:S(2)}, u32[]{:S(2)}) async-start(f32[8,4,8,512]{3,2,1,0:T(8,128)} %select_reduce_fusion), calls=%async_computation | async-start | bytes 1048576 | tf_op jit(solution)/shard_map/all_to_all | solution.py:69
  204.9 107.1 %all-gather.3.cloned.1.call-start = ((), (), s32[]{:S(2)}) async-start(), calls=%async_computation.1 | async-start | bytes 1114112 | tf_op jit(solution)/shard_map/all_gather | solution.py:118
  251.5 5.8 %copy-start.2 = (bf16[1024,4,128]{2,1,0:T(4,128)(2,1)S(1)}, bf16[1024,4,128]{2,1,0:T(4,128)(2,1)}, u32[]{:S(2)}) copy-start(bf16[1024,4,128]{2,1,0:T(4,128)(2,1)} %get-tuple-element.16) | copy-start | bytes 3145732
  258.6 7.7 %collective-permute-start.20 = (bf16[8,4,8,128]{3,2,1,0:T(8,128)(2,1)S(1)}, bf16[8,4,8,128]{3,2,1,0:T(8,128)(2,1)S(1)}, u32[]{:S(2)}, u32[]{:S(2)}) collective-permute-start(bf16[8,4,8,128]{3,2,1,0:T(8,128)(2,1)S(1)} %get-tuple-element.19), channel_id=1, source_target_pairs={{0,14},{2,12},{4,10},{6,8},{8,6},{10,4},{12,2},{14,0},{1,15},{3,13... | collective-permute-start | bytes 196616 | tf_op jit(solution)/shard_map/ppermute | solution.py:105
  261.1 6.1 %collective-permute-start.19 = (bf16[8,4,8,128]{3,2,1,0:T(8,128)(2,1)S(1)}, bf16[8,4,8,128]{3,2,1,0:T(8,128)(2,1)S(1)}, u32[]{:S(2)}, u32[]{:S(2)}) collective-permute-start(bf16[8,4,8,128]{3,2,1,0:T(8,128)(2,1)S(1)} %get-tuple-element.20), channel_id=1, source_target_pairs={{0,12},{2,14},{4,8},{6,10},{8,4},{10,6},{12,0},{14,2},{1,13},{3,15... | collective-permute-start | bytes 196616 | tf_op jit(solution)/shard_map/ppermute | solution.py:105
  261.7 6.1 %collective-permute-start.18 = (bf16[8,4,8,128]{3,2,1,0:T(8,128)(2,1)S(1)}, bf16[8,4,8,128]{3,2,1,0:T(8,128)(2,1)S(1)}, u32[]{:S(2)}, u32[]{:S(2)}) collective-permute-start(bf16[8,4,8,128]{3,2,1,0:T(8,128)(2,1)S(1)} %get-tuple-element.21), channel_id=1, source_target_pairs={{0,10},{2,8},{4,14},{6,12},{8,2},{10,0},{12,6},{14,4},{1,11},{3,9}... | collective-permute-start | bytes 196616 | tf_op jit(solution)/shard_map/ppermute | solution.py:105
  261.7 9.2 %collective-permute-start.17 = (bf16[8,4,8,128]{3,2,1,0:T(8,128)(2,1)S(1)}, bf16[8,4,8,128]{3,2,1,0:T(8,128)(2,1)S(1)}, u32[]{:S(2)}, u32[]{:S(2)}) collective-permute-start(bf16[8,4,8,128]{3,2,1,0:T(8,128)(2,1)S(1)} %get-tuple-element.22), channel_id=1, source_target_pairs={{0,8},{2,10},{4,12},{6,14},{8,0},{10,2},{12,4},{14,6},{1,9},{3,11}... | collective-permute-start | bytes 196616 | tf_op jit(solution)/shard_map/ppermute | solution.py:105
  266.3 5.2 %collective-permute-start.16 = (bf16[8,4,8,128]{3,2,1,0:T(8,128)(2,1)S(1)}, bf16[8,4,8,128]{3,2,1,0:T(8,128)(2,1)S(1)}, u32[]{:S(2)}, u32[]{:S(2)}) collective-permute-start(bf16[8,4,8,128]{3,2,1,0:T(8,128)(2,1)S(1)} %get-tuple-element.23), channel_id=1, source_target_pairs={{0,6},{2,4},{4,2},{6,0},{8,14},{10,12},{12,10},{14,8},{1,7},{3,5},... | collective-permute-start | bytes 196616 | tf_op jit(solution)/shard_map/ppermute | solution.py:105
  267.2 4.3 %collective-permute-start.15 = (bf16[8,4,8,128]{3,2,1,0:T(8,128)(2,1)S(1)}, bf16[8,4,8,128]{3,2,1,0:T(8,128)(2,1)S(1)}, u32[]{:S(2)}, u32[]{:S(2)}) collective-permute-start(bf16[8,4,8,128]{3,2,1,0:T(8,128)(2,1)S(1)} %get-tuple-element.24), channel_id=1, source_target_pairs={{0,4},{2,6},{4,0},{6,2},{8,12},{10,14},{12,8},{14,10},{1,5},{3,7},... | collective-permute-start | bytes 196616 | tf_op jit(solution)/shard_map/ppermute | solution.py:105
  267.7 5.3 %collective-permute-start.14 = (bf16[8,4,8,128]{3,2,1,0:T(8,128)(2,1)S(1)}, bf16[8,4,8,128]{3,2,1,0:T(8,128)(2,1)S(1)}, u32[]{:S(2)}, u32[]{:S(2)}) collective-permute-start(bf16[8,4,8,128]{3,2,1,0:T(8,128)(2,1)S(1)} %get-tuple-element.18), channel_id=1, source_target_pairs={{0,2},{2,0},{4,6},{6,4},{8,10},{10,8},{12,14},{14,12},{1,3},{3,1},... | collective-permute-start | bytes 196616 | tf_op jit(solution)/shard_map/ppermute | solution.py:105
  312.0 3.3 %copy-start.3 = (bf16[16,8,4096]{2,1,0:T(8,128)(2,1)S(1)}, bf16[16,8,4096]{2,1,0:T(8,128)(2,1)}, u32[]{:S(2)}) copy-start(bf16[16,8,4096]{2,1,0:T(8,128)(2,1)} %all-gather.3.cloned.1.call-done) | copy-start | bytes 3145732
Sparse Core Ops, SparseCore 0:
  274.4 37.6 all-gather.2

commit v2 on v1

v2 whole, which is shorter than its diff:
```python
import functools

import jax
import jax.numpy as jnp
from jax import lax
from jax.experimental import pallas as pl
from jax.experimental.pallas import tpu as pltpu
from jax.sharding import PartitionSpec as P

BLK = 8
MIB = 1 << 20


def score_kernel(rows, src_ref, core_ref, mine_ref, other_ref, keyed_ref, row_ref, out_ref, slot_ref, wide):
    q = pl.program_id(0)
    held = mine_ref.shape[0]
    step = 256

    @pl.when(q == 0)
    def _():
        core = core_ref[0]
        for side, ref in ((core, mine_ref), (1 - core, other_ref)):
            for i in range(0, held, step):
                wide[pl.ds(pl.multiple_of(side * held + i, step), step), :] = ref[
                    i : i + step, :
                ].astype(jnp.float32)

    slots = slot_ref.shape[1]
    count = slots // BLK
    for i in range(0, count, 2):
        pair = [
            wide[pl.ds(pl.multiple_of(src_ref[q * count + i + j] * BLK, BLK), BLK), :]
            for j in range(2)
        ]
        slot_ref[0, i * BLK : (i + 2) * BLK, :] = jnp.concatenate(pair).astype(jnp.bfloat16)
    kvh, per, part = keyed_ref.shape
    raw = lax.dot_general(
        keyed_ref[...].reshape(kvh * per, part),
        slot_ref[0],
        (((1,), (1,)), ((), ())),
        preferred_element_type=jnp.float32,
    ).reshape(kvh, rows, per // rows, slots)
    owner_row = row_ref[0]
    picked = jnp.zeros((kvh, per // rows, slots), jnp.float32)
    for r in range(rows):
        picked = picked + jnp.where((owner_row == r)[None], raw[:, r], 0.0)
    out_ref[0] = picked.reshape(kvh * (per // rows), slots).astype(out_ref.dtype)


def weight_kernel(scale, parts_ref, row_ref, top_ref, sum_ref, cached_ref, w_ref, kept_ref):
    n = parts_ref.shape[0]
    scores = parts_ref[0].astype(jnp.float32)
    for i in range(1, n):
        scores = scores + parts_ref[i].astype(jnp.float32)
    scores = scores * scale
    owner_row = row_ref[...]
    weights = jnp.zeros(scores.shape, jnp.float32)
    for r in range(top_ref.shape[0]):
        own = jnp.where(owner_row == r, scores, -jnp.inf)
        cache_top = top_ref[r]
        top = jnp.maximum(jnp.max(own, 1, keepdims=True), cache_top)
        held = jnp.exp(own - top)
        fade = jnp.exp(cache_top - top)
        total = jnp.sum(held, 1, keepdims=True) + sum_ref[r] * fade
        weights = weights + held / total
        kept_ref[r] = cached_ref[r] * (fade / total)
    weights = weights.astype(w_ref.dtype)
    for i in range(n):
        w_ref[i] = weights


def value_kernel(rows, w_ref, row_ref, slot_ref, value_ref, out_ref, mixed):
    q = pl.program_id(0)
    kvh = value_ref.shape[0]
    heads, slots = w_ref.shape[1:]
    per = rows * heads // kvh
    weights = w_ref[0].astype(jnp.float32).reshape(kvh, 1, heads // kvh, slots)
    owner_row = row_ref[0]
    spread = jnp.concatenate(
        [jnp.where((owner_row == r)[None, None], weights, 0.0) for r in range(rows)], 1
    ).reshape(kvh * per, slots)
    got = jnp.dot(
        spread.astype(jnp.bfloat16), slot_ref[0], preferred_element_type=jnp.float32
    ).astype(jnp.bfloat16)
    for h in range(kvh):
        mixed[h, pl.ds(pl.multiple_of(q * per, per), per), :] = got[h * per : (h + 1) * per]

    @pl.when(q == pl.num_programs(0) - 1)
    def _():
        n = out_ref.shape[0]
        for h in range(kvh):
            done = jnp.dot(mixed[h], value_ref[h], preferred_element_type=jnp.float32)
            out_ref[:, h] = done.reshape(n, per, done.shape[1]).astype(out_ref.dtype)


def sum_kernel(parts_ref, kept_ref, out_ref, total):
    n, kvh, per, hd = parts_ref.shape
    rows, heads = kept_ref.shape[:2]
    group = heads // kvh
    for h in range(kvh):
        terms = parts_ref[0, h].astype(jnp.float32)
        for i in range(1, n):
            terms = terms + parts_ref[i, h].astype(jnp.float32)
        for r in range(rows):
            here = slice((h * rows + r) * group, (h * rows + r + 1) * group)
            total[here, :] = (
                terms[r * group : (r + 1) * group] + kept_ref[r, h * group : (h + 1) * group, :]
            )
    pieces = [
        total[pl.ds(h * per + g, rows, stride=group), :]
        for h in range(kvh)
        for g in range(group)
    ]
    attended = jnp.concatenate(pieces, 1).astype(out_ref.dtype)
    for i in range(n):
        out_ref[i] = attended


def everywhere(x, n):
    at = 0
    k = n // 2
    while k >= 1:
        got = lax.ppermute(x, "pool", [(i, i ^ k) for i in range(n)])
        low = (lax.axis_index("pool") & k) == 0
        x = jnp.where(low, jnp.stack([x, got], at), jnp.stack([got, x], at))
        at += 1
        k //= 2
    return x.reshape((n,) + x.shape[at:])


def local(
    x_prompt, kv_weight, block_dest, block_row, block_fill, queries, kv_cache, cache_len, out_weight
):
    n = lax.axis_size("pool")
    ntp = lax.axis_size("tp")
    me = lax.axis_index("pool")
    core = lax.axis_index("tp")
    tokens, width = x_prompt.shape
    part = width // n
    kvh = kv_weight.shape[1]
    hd = kv_weight.shape[2] // 2
    rows, heads = queries.shape[0], queries.shape[1]
    group = heads // kvh
    per = rows * group
    cache_slots = kv_cache.shape[1]
    blocks = tokens // BLK
    cap = max(2, 2 * blocks // n)
    count = n * cap
    slots = count * BLK
    half = tokens // ntp
    scale = 1.0 / hd**0.5
    swap = [(i, (i + 1) % ntp) for i in range(ntp)]

    sent = lax.dynamic_slice_in_dim(x_prompt, core * half, half, 0)
    sent = sent.reshape(half, n, part).transpose(1, 0, 2)
    mine = lax.all_to_all(sent, "pool", 0, 0, tiled=True).reshape(n * half, part)
    other = lax.ppermute(mine, "tp", swap)

    dest = block_dest[:, 0]
    index = jnp.arange(n * blocks, dtype=jnp.int32)
    sender = index // blocks
    key = dest * n + sender
    earlier = (key[:, None] == key[None, :]) & (index[None, :] < index[:, None])
    rank = jnp.sum(earlier.astype(jnp.int32), 1)
    hit = (
        jnp.arange(n * count, dtype=jnp.int32)[:, None] == (key * cap + rank)[None, :]
    ).astype(jnp.int32)
    inner = index % blocks
    held = half // BLK
    source = (inner // held) * (n * held) + sender * held + inner % held
    slot_src = jnp.sum(hit * source[None, :], 1)
    slot_row = jnp.sum(hit * (block_row + 1)[None, :], 1) - 1
    slot_fill = jnp.sum(hit * block_fill[None, :], 1)
    live = jnp.arange(BLK, dtype=jnp.int32)[None, :] < slot_fill[:, None]
    rowof = jnp.where(live, slot_row[:, None], -1).reshape(n, 1, slots)

    allq = everywhere(queries, n).reshape(n, rows, kvh, group, hd)
    keyed = jnp.einsum(
        "qrhgd,phd->hqrgp", allq, kv_weight[:, :, :hd], preferred_element_type=jnp.float32
    ).astype(jnp.bfloat16)
    keyed = keyed.reshape(kvh, n * per, part)
    values = kv_weight[:, :, hd:].transpose(1, 0, 2)

    query = queries.reshape(rows, kvh, group, hd)
    cache_scores = (
        jnp.einsum(
            "rhgd,rthd->rhgt", query, kv_cache[:, :, :, :hd], preferred_element_type=jnp.float32
        )
        * scale
    )
    cache_live = jnp.arange(cache_slots, dtype=jnp.int32)[None, :] < cache_len[:, None]
    cache_scores = jnp.where(cache_live[:, None, None, :], cache_scores, -jnp.inf)
    cache_top = jnp.max(cache_scores, -1, keepdims=True)
    cache_exp = jnp.exp(cache_scores - cache_top)
    cache_sum = jnp.sum(cache_exp, -1, keepdims=True)
    cached = jnp.einsum(
        "rhgt,rthd->rhgd",
        cache_exp.astype(jnp.bfloat16),
        kv_cache[:, :, :, hd:],
        preferred_element_type=jnp.float32,
    )

    partial_scores, slot_x = pl.pallas_call(
        functools.partial(score_kernel, rows),
        grid_spec=pltpu.PrefetchScalarGridSpec(
            num_scalar_prefetch=2,
            grid=(n,),
            in_specs=[
                pl.BlockSpec((n * half, part), lambda q, *_: (0, 0)),
                pl.BlockSpec((n * half, part), lambda q, *_: (0, 0)),
                pl.BlockSpec((kvh, per, part), lambda q, *_: (0, q, 0)),
                pl.BlockSpec((1, 1, slots), lambda q, *_: (q, 0, 0)),
            ],
            out_specs=[
                pl.BlockSpec((1, heads, slots), lambda q, *_: (q, 0, 0)),
                pl.BlockSpec((1, slots, part), lambda q, *_: (q, 0, 0)),
            ],
            scratch_shapes=[pltpu.VMEM((ntp * n * half, part), jnp.float32)],
        ),
        out_shape=[
            jax.ShapeDtypeStruct((n, heads, slots), jnp.bfloat16),
            jax.ShapeDtypeStruct((n, slots, part), jnp.bfloat16),
        ],
        compiler_params=pltpu.CompilerParams(vmem_limit_bytes=32 * MIB),
        name="prompt_scores",
    )(slot_src, core.astype(jnp.int32).reshape(1), mine, other, keyed, rowof)

    parts = lax.all_to_all(partial_scores, "pool", 0, 0, tiled=True)
    my_rows = lax.dynamic_index_in_dim(rowof, me, 0, keepdims=False)
    weights, kept = pl.pallas_call(
        functools.partial(weight_kernel, scale),
        out_shape=[
            jax.ShapeDtypeStruct((n, heads, slots), jnp.bfloat16),
            jax.ShapeDtypeStruct((rows, heads, hd), jnp.float32),
        ],
        compiler_params=pltpu.CompilerParams(vmem_limit_bytes=16 * MIB),
        name="softmax_weights",
    )(
        parts,
        my_rows,
        cache_top.reshape(rows, heads, 1),
        cache_sum.reshape(rows, heads, 1),
        cached.reshape(rows, heads, hd),
    )

    all_weights = lax.all_to_all(weights, "pool", 0, 0, tiled=True)
    terms = pl.pallas_call(
        functools.partial(value_kernel, rows),
        grid=(n,),
        in_specs=[
            pl.BlockSpec((1, heads, slots), lambda q: (q, 0, 0)),
            pl.BlockSpec((1, 1, slots), lambda q: (q, 0, 0)),
            pl.BlockSpec((1, slots, part), lambda q: (q, 0, 0)),
            pl.BlockSpec((kvh, part, hd), lambda q: (0, 0, 0)),
        ],
        out_specs=pl.BlockSpec((n, kvh, per, hd), lambda q: (0, 0, 0, 0)),
        out_shape=jax.ShapeDtypeStruct((n, kvh, per, hd), jnp.bfloat16),
        scratch_shapes=[pltpu.VMEM((kvh, n * per, part), jnp.bfloat16)],
        compiler_params=pltpu.CompilerParams(vmem_limit_bytes=24 * MIB),
        name="weighted_values",
    )(all_weights, rowof, slot_x, values)

    term_parts = lax.all_to_all(terms, "pool", 0, 0, tiled=True)
    attended = pl.pallas_call(
        sum_kernel,
        out_shape=jax.ShapeDtypeStruct((n, rows, heads * hd), jnp.bfloat16),
        scratch_shapes=[pltpu.VMEM((kvh * per, hd), jnp.float32)],
        compiler_params=pltpu.CompilerParams(vmem_limit_bytes=16 * MIB),
        name="attended_sum",
    )(term_parts, kept)

    everyone = lax.all_to_all(attended, "pool", 0, 0, tiled=True).reshape(n * rows, heads * hd)
    product = jnp.dot(everyone, out_weight, preferred_element_type=jnp.float32)
    cols = out_weight.shape[1] // ntp
    out = lax.dynamic_slice_in_dim(product, core * cols, cols, 1)
    for j in range(1, ntp):
        away = lax.dynamic_slice_in_dim(product, ((core + j) % ntp) * cols, cols, 1)
        out = out + lax.ppermute(away, "tp", [(i, (i + j) % ntp) for i in range(ntp)])
    return out.astype(jnp.bfloat16)


def solution(mesh):
    in_specs = (
        P(("groups", "pool"), None),
        P("pool", "tp", None),
        P("groups", None),
        P("groups"),
        P("groups"),
        P(("groups", "pool"), "tp", None),
        P(("groups", "pool"), None, "tp", None),
        P(("groups", "pool")),
        P("tp", "pool"),
    )
    out_specs = P("groups", ("pool", "tp"))
    return jax.shard_map(local, mesh=mesh, in_specs=in_specs, out_specs=out_specs, check_vma=False)
```

time: 326 us -> 174 us (0.53)
  local copies, waits for them, and re-layouts: 94.9 us -> 20.9 us
  blocking collectives: 64.9 us -> 17.2 us
  other arithmetic: 29.2 us -> 2.65 us
  waiting for transfers between devices: 56.5 us -> 81.8 us
  matrix products: 29.6 us -> 11.4 us
  Pallas kernels: 0 us -> 15.9 us
  starting transfers between devices: 37 us -> 22.5 us
  between operations: 13.8 us -> 0.34 us
    all_gather x2 -> x0, blocking collectives: 64.9 us -> none  [the longest x1 33.9 us: local(): lax.all_gather(queries, 'pool', axis=0, tiled=True)]
    mul x6 -> x0, local copies, waits for them, and re-layouts: 58.7 us -> none  [the longest x4 58.6 us: local(): match.astype(jnp.bfloat16)[:, :, :, None, :, None]]
    all_to_all x1 -> x4, waiting for transfers between devices: 10.7 us -> 68.5 us  [the longest x1 41.6 us: local(): lax.all_to_all(sent, 'pool', 0, 0, tiled=True).reshape(n * half, part)]
    all_gather x1 -> x0, waiting for transfers between devices: 37.8 us -> none  [local(): lax.all_gather(attended, ('tp', 'pool'), axis=0)]
    ppermute x22 -> x5, starting transfers between devices: 25.8 us -> 4.66 us  [the longest x3 4.52 us: everywhere(): got = lax.ppermute(x, 'pool', [(i, i ^ k) for i in range(n)])]
    dot_general x7 -> x3, matrix products: 28.9 us -> 8.33 us  [the longest x1 4.94 us: local(): product = jnp.dot(everyone, out_weight, preferred_element_type=jnp.float32)]
    gather x3 -> x0, local copies, waits for them, and re-layouts: 18.5 us -> none  [the longest x2 16.5 us: local(): padded = jnp.take(padded, me ^ owners, axis=1).reshape(n, n * slots, part)]
    all_to_all x0 -> x1, blocking collectives: none -> 17.2 us  [local(): term_parts = lax.all_to_all(terms, 'pool', 0, 0, tiled=True)]
  transfers between devices with their start and end apart: 24 -> 9, of which waited for: 8 -> 7; matrix products, arithmetic and copies ran while one was open for 45% -> 11% of each run, Pallas kernels for 0% -> 0%
where the time goes in v2:
time: 174 us; the launch traced here: 173 us
  waiting for transfers between devices  81.8 us (47%)
  starting transfers between devices  22.5 us (13%)
  local copies, waits for them, and re-layouts  20.9 us (12%)
  blocking collectives  17.2 us (10%)
  Pallas kernels  15.9 us (9%)
  matrix products  11.4 us (7%)
  other arithmetic  2.65 us (2%)
    all_to_all x1, waiting for transfers between devices, local(): lax.all_to_all(sent, 'pool', 0, 0, tiled=True).reshape(n * half, part)  41.6 us
    all_to_all x1, blocking collectives, local(): term_parts = lax.all_to_all(terms, 'pool', 0, 0, tiled=True)  17.2 us
    all_to_all x1, waiting for transfers between devices, local(): lax.all_to_all(attended, 'pool', 0, 0, tiled=True)  14 us
    ppermute x3, waiting for transfers between devices, everywhere(): got = lax.ppermute(x, 'pool', [(i, i ^ k) for i in range(n)])  11.9 us
    unnamed x20, local copies, waits for them, and re-layouts  9.22 us
    pallas_call x1, Pallas kernels, local(): pl.pallas_call(functools.partial(score_kernel, rows), grid_spec=pltpu.Pre...  8.22 us
    all_to_all x1, waiting for transfers between devices, local(): all_weights = lax.all_to_all(weights, 'pool', 0, 0, tiled=True)  8.1 us
    all_to_all x1, starting transfers between devices, local(): lax.all_to_all(sent, 'pool', 0, 0, tiled=True).reshape(n * half, part)  7.42 us
  transfers between devices with their start and end apart: 9, of which 7 were waited for; matrix products, arithmetic and copies ran while one was open for 11% of the time, Pallas kernels for 0%

profile of v2, /device:TPU:0, one launch (start us, length us, event | category | flops | bytes accessed | tf_op | source)
XLA Modules:
  0.0 172.7 jit_solution(14866840919515413184)
XLA Ops:
  0.0 1.7 constant_dynamic-slice_fusion
  1.7 2.4 %copy.41 = bf16[128,8192]{0,1:T(8,128)(2,1)} copy(bf16[128,8192]{1,0:T(8,128)(2,1)S(1)} %constant_dynamic-slice_fusion) | data formatting | bytes 4194304
  4.2 0.0 copy-start.4
  4.2 0.0 copy-start.5
  4.2 0.0 copy-start.6
  4.2 0.0 copy-start.8
  4.2 7.4 %all-to-all-start = ((bf16[8,128,1024]{1,2,0:T(8,128)(2,1)}), bf16[8,128,1024]{1,2,0:T(8,128)(2,1)}, u32[]{:S(2)}, u32[]{:S(2)}) async-start(bf16[8,128,1024]{1,2,0:T(8,128)(2,1)} %bitcast.4), calls=%async_computation | async-start | bytes 4194304 | tf_op jit(solution)/shard_map/all_to_all | solution.py:156
  11.6 0.0 copy-done.4
  11.6 2.9 %collective-permute-start.1 = (bf16[8,32,128]{2,1,0:T(8,128)(2,1)S(1)}, bf16[8,32,128]{2,1,0:T(8,128)(2,1)S(1)}, u32[]{:S(2)}, u32[]{:S(2)}) collective-permute-start(bf16[8,32,128]{2,1,0:T(8,128)(2,1)S(1)} %copy-done.4), channel_id=1, source_target_pairs={{0,8},{2,10},{4,12},{6,14},{8,0},{10,2},{12,4},{14,6},{1,9},{3,11}... | collective-permute-start | bytes 196616 | tf_op jit(solution)/shard_map/ppermute | solution.py:123
  14.5 0.0 copy-done.5
  14.6 0.2 convert_reduce_fusion
  14.8 0.0 copy-done.7
  14.8 0.0 copy-done.6
  14.8 0.3 select_reduce_fusion.1
  15.1 0.1 sub.32
  15.2 0.1 broadcast_in_dim.22
  15.4 0.2 broadcast_in_dim.31
  15.5 0.1 lt.96
  15.6 0.1 lt.97
  15.7 0.2 lt.107
  15.9 0.1 lt.94
  16.0 0.0 copy-done.8
  16.0 0.1 iota_compare_fusion.2
  16.1 4.3 %fusion.27 = (bf16[8,256,4,128]{3,2,1,0:T(4,128)(2,1)}, bf16[8,256,4,128]{3,2,1,0:T(4,128)(2,1)}) fusion(bf16[8,256,4,256]{3,2,1,0:T(4,128)(2,1)} %param.15), kind=kLoop, calls=%fused_computation.61 | loop fusion | bytes 8388608 | tf_op jit(solution)/shard_map/slice | solution.py:199
  20.4 41.6 %all-to-all-done = bf16[8,128,1024]{1,2,0:T(8,128)(2,1)} async-done(((bf16[8,128,1024]{1,2,0:T(8,128)(2,1)}), bf16[8,128,1024]{1,2,0:T(8,128)(2,1)}, u32[]{:S(2)}, u32[]{:S(2)}) %all-to-all-start) | async-done | bytes 2097184 | tf_op jit(solution)/shard_map/all_to_all | solution.py:156
  62.1 2.9 %copy.28 = bf16[8,128,1024]{2,1,0:T(8,128)(2,1)S(1)} copy(bf16[8,128,1024]{1,2,0:T(8,128)(2,1)} %all-to-all-done) | data formatting | bytes 4194304 | tf_op jit(solution)/shard_map/all_to_all | solution.py:156
  64.9 0.0 copy-start.3
  64.9 0.1 collective-permute-start
  65.0 3.1 %fusion.29 = (f32[8,4,8]{2,1,0:T(4,128)S(1)}, f32[8,4,8,256]{3,2,1,0:T(8,128)}) fusion(bf16[8,256,4,128]{3,2,1,0:T(4,128)(2,1)} %get-tuple-element.17, bf16[8,32,128]{2,1,0:T(8,128)(2,1)S(1)} %copy-done.4, pred[8,256]{1,0:T(8,128)(4,1)S(1)} %iota_compare_fusion.2), kind=kOutput, calls=%fused_computation.63 | convolution fusion | flops 16973568 | bytes 2427904 | tf_op jit(solution)/shard_map/rhgd,rthd->rhgt/dot_general | solution.py:186
  68.1 0.0 copy-done.3
  68.1 1.7 fusion.28
  69.9 0.1 reshape_broadcast_in_dim.8.top_ref
  70.0 0.0 copy-start.2
  70.0 0.0 collective-permute-done.1
  70.0 0.1 collective-permute-start.2
  70.1 5.7 %collective-permute-done.2 = bf16[2,8,32,128]{3,2,1,0:T(8,128)(2,1)S(1)} collective-permute-done((bf16[2,8,32,128]{3,2,1,0:T(8,128)(2,1)S(1)}, bf16[2,8,32,128]{3,2,1,0:T(8,128)(2,1)S(1)}, u32[]{:S(2)}, u32[]{:S(2)}) %collective-permute-start.2) | collective-permute-done | bytes 131104 | tf_op jit(solution)/shard_map/ppermute | solution.py:123
  75.9 1.5 collective-permute-start.3
  77.5 6.2 %collective-permute-done.3 = bf16[2,2,8,32,128]{4,3,2,1,0:T(8,128)(2,1)S(1)} collective-permute-done((bf16[2,2,8,32,128]{4,3,2,1,0:T(8,128)(2,1)S(1)}, bf16[2,2,8,32,128]{4,3,2,1,0:T(8,128)(2,1)S(1)}, u32[]{:S(2)}, u32[]{:S(2)}) %collective-permute-start.3) | collective-permute-done | bytes 262176 | tf_op jit(solution)/shard_map/ppermute | solution.py:123
  83.7 0.0 copy-done.2
  83.7 1.3 convolution_convert_fusion
  85.0 0.0 collective-permute-done.other_ref
  85.0 8.2 %prompt_scores.1 = (bf16[8,32,512]{2,1,0:T(8,128)(2,1)}, bf16[8,512,1024]{2,1,0:T(8,128)(2,1)S(1)}) custom-call(s32[512]{0:T(512)S(1)} %get-tuple-element.15.src_ref, s32[1]{0:T(128)} %bitcast.2.core_ref, bf16[1024,1024]{1,0:T(8,128)(2,1)S(1)} %bitcast.41, bf16[1024,1024]{1,0:T(8,128)(2,1)} %collective-permute-done.other_ref, ...), custom_call_target="tpu_custom_call" | custom-call | tf_op jit(solution)/shard_map/prompt_scores/pallas_call | solution.py:203
  93.2 0.0 copy-start
  93.2 3.2 %copy-done = bf16[8,512,1024]{2,1,0:T(8,128)(2,1)} copy-done((bf16[8,512,1024]{2,1,0:T(8,128)(2,1)}, bf16[8,512,1024]{2,1,0:T(8,128)(2,1)S(1)}, u32[]{:S(2)}) %copy-start) | copy-done | bytes 8388632
  96.5 3.4 %all-to-all-start.1 = ((bf16[8,32,512]{2,1,0:T(8,128)(2,1)}), bf16[8,32,512]{2,1,0:T(8,128)(2,1)S(1)}, u32[]{:S(2)}, u32[]{:S(2)}) async-start(bf16[8,32,512]{2,1,0:T(8,128)(2,1)} %get-tuple-element.9), calls=%async_computation.1 | async-start | bytes 524288 | tf_op jit(solution)/shard_map/all_to_all | solution.py:228
  99.9 1.2 fusion.18
  101.1 0.1 reshape_broadcast_in_dim.9.sum_ref
  101.2 2.1 %fusion.10.cached_ref = f32[8,32,128]{2,1,0:T(8,128)S(1)} fusion(bf16[8,256,4,128]{3,2,1,0:T(4,128)(2,1)} %get-tuple-element.16, f32[8,4,8,256]{3,2,1,0:T(8,128)} %get-tuple-element.25, f32[8,4,8]{2,1,0:T(4,128)S(1)} %get-tuple-element.24), kind=kOutput, calls=%fused_computation.7 | convolution fusion | flops 16908288 | bytes 2491392 | tf_op jit(solution)/shard_map/rhgt,rthd->rhgd/dot_general | solution.py:196
  103.3 4.7 %all-to-all-done.1.parts_ref = bf16[8,32,512]{2,1,0:T(8,128)(2,1)S(1)} async-done(((bf16[8,32,512]{2,1,0:T(8,128)(2,1)}), bf16[8,32,512]{2,1,0:T(8,128)(2,1)S(1)}, u32[]{:S(2)}, u32[]{:S(2)}) %all-to-all-start.1) | async-done | bytes 262176 | tf_op jit(solution)/shard_map/all_to_all | solution.py:228
  108.1 1.9 %softmax_weights.1 = (bf16[8,32,512]{2,1,0:T(8,128)(2,1)}, f32[8,32,128]{2,1,0:T(8,128)S(1)}) custom-call(bf16[8,32,512]{2,1,0:T(8,128)(2,1)S(1)} %all-to-all-done.1.parts_ref, s32[1,512]{1,0:T(1,128)S(1)} %dynamic-slice_bitcast_fusion.row_ref, f32[8,32,1]{2,1,0:T(8,128)S(1)} %reshape_broadcast_in_dim.8.top_ref, ...), custom_call_target="tpu_custom_call" | custom-call | tf_op jit(solution)/shard_map/softmax_weights/pallas_call | solution.py:230
  110.0 3.4 %all-to-all-start.2 = ((bf16[8,32,512]{2,1,0:T(8,128)(2,1)}), bf16[8,32,512]{2,1,0:T(8,128)(2,1)S(1)}, u32[]{:S(2)}, u32[]{:S(2)}) async-start(bf16[8,32,512]{2,1,0:T(8,128)(2,1)} %get-tuple-element.10), calls=%async_computation.2 | async-start | bytes 524288 | tf_op jit(solution)/shard_map/all_to_all | solution.py:246
  113.4 0.1 copy.65
  113.6 8.1 %all-to-all-done.2.w_ref = bf16[8,32,512]{2,1,0:T(8,128)(2,1)S(1)} async-done(((bf16[8,32,512]{2,1,0:T(8,128)(2,1)}), bf16[8,32,512]{2,1,0:T(8,128)(2,1)S(1)}, u32[]{:S(2)}, u32[]{:S(2)}) %all-to-all-start.2) | async-done | bytes 262176 | tf_op jit(solution)/shard_map/all_to_all | solution.py:246
  121.7 0.0 copy-start.1
  121.7 3.4 %copy-done.1 = bf16[8,512,1024]{2,1,0:T(8,128)(2,1)S(1)} copy-done((bf16[8,512,1024]{2,1,0:T(8,128)(2,1)S(1)}, bf16[8,512,1024]{2,1,0:T(8,128)(2,1)}, u32[]{:S(2)}) %copy-start.1) | copy-done | bytes 8388632
  125.0 4.8 %weighted_values.1 = bf16[8,4,64,128]{3,2,1,0:T(8,128)(2,1)S(1)} custom-call(bf16[8,32,512]{2,1,0:T(8,128)(2,1)S(1)} %all-to-all-done.2.w_ref, s32[8,1,512]{2,1,0:T(1,128)S(1)} %compare_select_fusion.row_ref, bf16[8,512,1024]{2,1,0:T(8,128)(2,1)S(1)} %copy-done.1, bf16[4,1024,128]{2,1,0:T(8,128)(2,1)S(1)} %bitcast.42), custom_call_target="tpu_custom_call" | custom-call | tf_op jit(solution)/shard_map/weighted_values/pallas_call | solution.py:247
  129.9 17.2 %all_to_all.25.parts_ref = bf16[8,4,64,128]{3,2,1,0:T(8,128)(2,1)S(1)} all-to-all(bf16[8,4,64,128]{3,2,1,0:T(8,128)(2,1)S(1)} %weighted_values.1), channel_id=1, replica_groups=mesh['groups'=2,'pool'=8,'tp'=2] {'pool'}, dimensions={0} | all-to-all | bytes 1048576 | tf_op jit(solution)/shard_map/all_to_all | solution.py:263
  147.1 0.9 attended_sum.1
  148.0 3.6 %all-to-all-start.4 = ((bf16[8,8,4096]{2,1,0:T(8,128)(2,1)}), bf16[8,8,4096]{2,1,0:T(8,128)(2,1)S(1)}, u32[]{:S(2)}, u32[]{:S(2)}) async-start(bf16[8,8,4096]{2,1,0:T(8,128)(2,1)} %attended_sum.1), calls=%async_computation.4 | async-start | bytes 1048576 | tf_op jit(solution)/shard_map/all_to_all | solution.py:272
  151.6 14.0 %all-to-all-done.4 = bf16[8,8,4096]{2,1,0:T(8,128)(2,1)S(1)} async-done(((bf16[8,8,4096]{2,1,0:T(8,128)(2,1)}), bf16[8,8,4096]{2,1,0:T(8,128)(2,1)S(1)}, u32[]{:S(2)}, u32[]{:S(2)}) %all-to-all-start.4) | async-done | bytes 524320 | tf_op jit(solution)/shard_map/all_to_all | solution.py:272
  165.7 4.9 %fusion.13 = f32[64,1024]{1,0:T(8,128)S(1)} fusion(bf16[4096,1024]{1,0:T(8,128)(2,1)} %param.17, bf16[8,8,4096]{2,1,0:T(8,128)(2,1)S(1)} %all-to-all-done.4), kind=kOutput, calls=%fused_computation.11 | convolution fusion | flops 536870912 | bytes 9175040 | tf_op jit(solution)/shard_map/dot_general | solution.py:273
  170.6 0.1 collective-permute-start.4
  170.7 1.3 collective-permute-done.4
  172.1 0.6 add_convert_fusion
  (17 shorter events, 0.3 us)
Async XLA Ops:
  4.2 7.5 %copy-start.4 = (bf16[8,32,128]{2,1,0:T(8,128)(2,1)S(1)}, bf16[8,32,128]{2,1,0:T(8,128)(2,1)}, u32[]{:S(2)}) copy-start(bf16[8,32,128]{2,1,0:T(8,128)(2,1)} %param.14) | copy-start | bytes 196612
  4.2 10.4 %copy-start.5 = (s32[256,1]{0,1:T(1,128)S(1)}, s32[256,1]{0,1:T(1,128)}, u32[]{:S(2)}) copy-start(s32[256,1]{0,1:T(1,128)} %param.11) | copy-start | bytes 3076
  4.2 10.6 %copy-start.7 = (s32[256]{0:T(256)S(1)}, s32[256]{0:T(256)}, u32[]{:S(2)}) copy-start(s32[256]{0:T(256)} %param.12) | copy-start | bytes 3076
  4.2 10.6 %copy-start.6 = (s32[256]{0:T(256)S(1)}, s32[256]{0:T(256)}, u32[]{:S(2)}) copy-start(s32[256]{0:T(256)} %param.13) | copy-start | bytes 3076
  4.2 11.8 %copy-start.8 = (s32[8]{0:T(128)S(1)}, s32[8]{0:T(128)}, u32[]{:S(2)}) copy-start(s32[8]{0:T(128)} %param.16) | copy-start | bytes 100
  4.2 57.9 %all-to-all-start = ((bf16[8,128,1024]{1,2,0:T(8,128)(2,1)}), bf16[8,128,1024]{1,2,0:T(8,128)(2,1)}, u32[]{:S(2)}, u32[]{:S(2)}) async-start(bf16[8,128,1024]{1,2,0:T(8,128)(2,1)} %bitcast.4), calls=%async_computation | async-start | bytes 4194304 | tf_op jit(solution)/shard_map/all_to_all | solution.py:156
  11.6 58.4 %collective-permute-start.1 = (bf16[8,32,128]{2,1,0:T(8,128)(2,1)S(1)}, bf16[8,32,128]{2,1,0:T(8,128)(2,1)S(1)}, u32[]{:S(2)}, u32[]{:S(2)}) collective-permute-start(bf16[8,32,128]{2,1,0:T(8,128)(2,1)S(1)} %copy-done.4), channel_id=1, source_target_pairs={{0,8},{2,10},{4,12},{6,14},{8,0},{10,2},{12,4},{14,6},{1,9},{3,11}... | collective-permute-start | bytes 196616 | tf_op jit(solution)/shard_map/ppermute | solution.py:123
  64.9 3.2 %copy-start.3 = (bf16[1024,4,256]{2,1,0:T(4,128)(2,1)S(1)}, bf16[1024,4,256]{2,1,0:T(4,128)(2,1)}, u32[]{:S(2)}) copy-start(bf16[1024,4,256]{2,1,0:T(4,128)(2,1)} %param.10) | copy-start | bytes 6291460
  64.9 20.1 %collective-permute-start = (bf16[1024,1024]{1,0:T(8,128)(2,1)S(1)}, bf16[1024,1024]{1,0:T(8,128)(2,1)}, u32[]{:S(2)}, u32[]{:S(2)}) collective-permute-start(bf16[1024,1024]{1,0:T(8,128)(2,1)S(1)} %bitcast.40), channel_id=1, source_target_pairs={{0,1},{1,0},{2,3},{3,2},{4,5},{5,4},{6,7},{7,6},{8,9},{9,8},{10,11... | collective-permute-start | bytes 6291464 | tf_op jit(solution)/shard_map/ppermute | solution.py:157
  70.0 13.8 %copy-start.2 = (bf16[1024,4,128]{2,1,0:T(4,128)(2,1)S(1)}, bf16[1024,4,128]{2,1,0:T(4,128)(2,1)}, u32[]{:S(2)}) copy-start(bf16[1024,4,128]{2,1,0:T(4,128)(2,1)} %get-tuple-element.19) | copy-start | bytes 3145732
  70.0 5.8 %collective-permute-start.2 = (bf16[2,8,32,128]{3,2,1,0:T(8,128)(2,1)S(1)}, bf16[2,8,32,128]{3,2,1,0:T(8,128)(2,1)S(1)}, u32[]{:S(2)}, u32[]{:S(2)}) collective-permute-start(bf16[2,8,32,128]{3,2,1,0:T(8,128)(2,1)S(1)} %maximum_select_fusion.3), channel_id=1, source_target_pairs={{0,4},{2,6},{4,0},{6,2},{8,12},{10,14},{12,8},{14,10},{1,5},{3,7},... | collective-permute-start | bytes 393224 | tf_op jit(solution)/shard_map/ppermute | solution.py:123
  75.9 7.8 %collective-permute-start.3 = (bf16[2,2,8,32,128]{4,3,2,1,0:T(8,128)(2,1)S(1)}, bf16[2,2,8,32,128]{4,3,2,1,0:T(8,128)(2,1)S(1)}, u32[]{:S(2)}, u32[]{:S(2)}) collective-permute-start(bf16[2,2,8,32,128]{4,3,2,1,0:T(8,128)(2,1)S(1)} %maximum_select_fusion.1), channel_id=1, source_target_pairs={{0,2},{2,0},{4,6},{6,4},{8,10},{10,8},{12,14},{14,12},{1,3},{3,1},... | collective-permute-start | bytes 786440 | tf_op jit(solution)/shard_map/ppermute | solution.py:123
  93.2 3.2 %copy-start = (bf16[8,512,1024]{2,1,0:T(8,128)(2,1)}, bf16[8,512,1024]{2,1,0:T(8,128)(2,1)S(1)}, u32[]{:S(2)}) copy-start(bf16[8,512,1024]{2,1,0:T(8,128)(2,1)S(1)} %get-tuple-element.11.slot_ref) | copy-start | bytes 25165828
  96.5 11.6 %all-to-all-start.1 = ((bf16[8,32,512]{2,1,0:T(8,128)(2,1)}), bf16[8,32,512]{2,1,0:T(8,128)(2,1)S(1)}, u32[]{:S(2)}, u32[]{:S(2)}) async-start(bf16[8,32,512]{2,1,0:T(8,128)(2,1)} %get-tuple-element.9), calls=%async_computation.1 | async-start | bytes 524288 | tf_op jit(solution)/shard_map/all_to_all | solution.py:228
  110.0 11.7 %all-to-all-start.2 = ((bf16[8,32,512]{2,1,0:T(8,128)(2,1)}), bf16[8,32,512]{2,1,0:T(8,128)(2,1)S(1)}, u32[]{:S(2)}, u32[]{:S(2)}) async-start(bf16[8,32,512]{2,1,0:T(8,128)(2,1)} %get-tuple-element.10), calls=%async_computation.2 | async-start | bytes 524288 | tf_op jit(solution)/shard_map/all_to_all | solution.py:246
  121.7 3.4 %copy-start.1 = (bf16[8,512,1024]{2,1,0:T(8,128)(2,1)S(1)}, bf16[8,512,1024]{2,1,0:T(8,128)(2,1)}, u32[]{:S(2)}) copy-start(bf16[8,512,1024]{2,1,0:T(8,128)(2,1)} %copy-done) | copy-start | bytes 25165828
  148.0 17.7 %all-to-all-start.4 = ((bf16[8,8,4096]{2,1,0:T(8,128)(2,1)}), bf16[8,8,4096]{2,1,0:T(8,128)(2,1)S(1)}, u32[]{:S(2)}, u32[]{:S(2)}) async-start(bf16[8,8,4096]{2,1,0:T(8,128)(2,1)} %attended_sum.1), calls=%async_computation.4 | async-start | bytes 1048576 | tf_op jit(solution)/shard_map/all_to_all | solution.py:272
  170.6 1.4 collective-permute-start.4

commit v3 on v2

--- a/solution.py
+++ b/solution.py
@@ -11,17 +11,20 @@
 MIB = 1 << 20
 
 
-def score_kernel(rows, src_ref, core_ref, mine_ref, other_ref, keyed_ref, row_ref, out_ref, slot_ref, wide):
+def score_kernel(rows, pieces, src_ref, core_ref, *refs):
+    keyed_ref, row_ref, out_ref, slot_ref, wide = refs[2 * pieces :]
     q = pl.program_id(0)
-    held = mine_ref.shape[0]
+    held = refs[0].shape[0]
     step = 256
 
     @pl.when(q == 0)
     def _():
         core = core_ref[0]
-        for side, ref in ((core, mine_ref), (1 - core, other_ref)):
+        for j in range(2 * pieces):
+            side = core if j < pieces else 1 - core
+            base = (side * pieces + j % pieces) * held
             for i in range(0, held, step):
-                wide[pl.ds(pl.multiple_of(side * held + i, step), step), :] = ref[
+                wide[pl.ds(pl.multiple_of(base + i, step), step), :] = refs[j][
                     i : i + step, :
                 ].astype(jnp.float32)
 
@@ -114,6 +117,12 @@
     attended = jnp.concatenate(pieces, 1).astype(out_ref.dtype)
     for i in range(n):
         out_ref[i] = attended
+
+
+def pack_kernel(core_ref, x_ref, *out_refs):
+    size = out_refs[0].shape[1]
+    for i, out_ref in enumerate(out_refs):
+        out_ref[0] = x_ref[i * size : (i + 1) * size, :]
 
 
 def everywhere(x, n):
@@ -151,10 +160,22 @@
     scale = 1.0 / hd**0.5
     swap = [(i, (i + 1) % ntp) for i in range(ntp)]
 
-    sent = lax.dynamic_slice_in_dim(x_prompt, core * half, half, 0)
-    sent = sent.reshape(half, n, part).transpose(1, 0, 2)
-    mine = lax.all_to_all(sent, "pool", 0, 0, tiled=True).reshape(n * half, part)
-    other = lax.ppermute(mine, "tp", swap)
+    pieces = 2
+    size = half // pieces
+    which = core.astype(jnp.int32).reshape(1)
+    packed = pl.pallas_call(
+        pack_kernel,
+        grid_spec=pltpu.PrefetchScalarGridSpec(
+            num_scalar_prefetch=1,
+            grid=(n,),
+            in_specs=[pl.BlockSpec((half, part), lambda q, c: (c[0], q))],
+            out_specs=[pl.BlockSpec((1, size, part), lambda q, c: (q, 0, 0))] * pieces,
+        ),
+        out_shape=[jax.ShapeDtypeStruct((n, size, part), jnp.bfloat16)] * pieces,
+        compiler_params=pltpu.CompilerParams(vmem_limit_bytes=16 * MIB),
+        name="pack_columns",
+    )(which, x_prompt)
+    mine = [lax.all_to_all(p, "pool", 0, 0, tiled=True).reshape(n * size, part) for p in packed]
 
     dest = block_dest[:, 0]
     index = jnp.arange(n * blocks, dtype=jnp.int32)
@@ -166,7 +187,7 @@
         jnp.arange(n * count, dtype=jnp.int32)[:, None] == (key * cap + rank)[None, :]
     ).astype(jnp.int32)
     inner = index % blocks
-    held = half // BLK
+    held = size // BLK
     source = (inner // held) * (n * held) + sender * held + inner % held
     slot_src = jnp.sum(hit * source[None, :], 1)
     slot_row = jnp.sum(hit * (block_row + 1)[None, :], 1) - 1
@@ -200,14 +221,20 @@
         preferred_element_type=jnp.float32,
     )
 
+    mine[-1], slot_src, rowof, keyed, values, cache_top, cache_sum, cached = (
+        lax.optimization_barrier(
+            (mine[-1], slot_src, rowof, keyed, values, cache_top, cache_sum, cached)
+        )
+    )
+    other = [lax.ppermute(m, "tp", swap) for m in mine]
+
     partial_scores, slot_x = pl.pallas_call(
-        functools.partial(score_kernel, rows),
+        functools.partial(score_kernel, rows, pieces),
         grid_spec=pltpu.PrefetchScalarGridSpec(
             num_scalar_prefetch=2,
             grid=(n,),
             in_specs=[
-                pl.BlockSpec((n * half, part), lambda q, *_: (0, 0)),
-                pl.BlockSpec((n * half, part), lambda q, *_: (0, 0)),
+                *[pl.BlockSpec((n * size, part), lambda q, *_: (0, 0))] * (2 * pieces),
                 pl.BlockSpec((kvh, per, part), lambda q, *_: (0, q, 0)),
                 pl.BlockSpec((1, 1, slots), lambda q, *_: (q, 0, 0)),
             ],
@@ -221,9 +248,9 @@
             jax.ShapeDtypeStruct((n, heads, slots), jnp.bfloat16),
             jax.ShapeDtypeStruct((n, slots, part), jnp.bfloat16),
         ],
-        compiler_params=pltpu.CompilerParams(vmem_limit_bytes=32 * MIB),
+        compiler_params=pltpu.CompilerParams(vmem_limit_bytes=56 * MIB),
         name="prompt_scores",
-    )(slot_src, core.astype(jnp.int32).reshape(1), mine, other, keyed, rowof)
+    )(slot_src, which, *mine, *other, keyed, rowof)
 
     parts = lax.all_to_all(partial_scores, "pool", 0, 0, tiled=True)
     my_rows = lax.dynamic_index_in_dim(rowof, me, 0, keepdims=False)
@@ -256,7 +283,7 @@
         out_specs=pl.BlockSpec((n, kvh, per, hd), lambda q: (0, 0, 0, 0)),
         out_shape=jax.ShapeDtypeStruct((n, kvh, per, hd), jnp.bfloat16),
         scratch_shapes=[pltpu.VMEM((kvh, n * per, part), jnp.bfloat16)],
-        compiler_params=pltpu.CompilerParams(vmem_limit_bytes=24 * MIB),
+        compiler_params=pltpu.CompilerParams(vmem_limit_bytes=56 * MIB),
         name="weighted_values",
     )(all_weights, rowof, slot_x, values)
 

time: 174 us -> 173 us (level)
  waiting for transfers between devices: 81.8 us -> 60.1 us
  blocking collectives: 17.2 us -> 29.6 us
  Pallas kernels: 15.9 us -> 26.3 us
  local copies, waits for them, and re-layouts: 20.9 us -> 14.1 us
  other arithmetic: 2.65 us -> 6.28 us
  starting transfers between devices: 22.5 us -> 25.4 us
  matrix products: 11.4 us -> 9.36 us
    all_to_all x2, waiting for transfers between devices: 49.7 us -> 17.5 us  [local(): lax.all_to_all(p, 'pool', 0, 0, tiled=True).reshape(n * size, part)]
    all_to_all x0 -> x1, blocking collectives: none -> 12.1 us  [local(): all_weights = lax.all_to_all(weights, 'pool', 0, 0, tiled=True)]
    pallas_call x1 -> x2, Pallas kernels: 8.22 us -> 14.2 us  [the longest x1 11.1 us: local(): pl.pallas_call(functools.partial(score_kernel, rows, pieces), grid_spec=p...]
    pallas_call x1, Pallas kernels: 4.82 us -> 9.98 us  [local(): pl.pallas_call(functools.partial(value_kernel, rows), grid=(n,), in_specs...]
    unnamed x20 -> x33, local copies, waits for them, and re-layouts: 9.22 us -> 4.38 us
    ppermute x1 -> x2, waiting for transfers between devices: 0.01 us -> 3.64 us  [local(): other = [lax.ppermute(m, 'tp', swap) for m in mine]]
    all_to_all x1, waiting for transfers between devices: 4.74 us -> 8.31 us  [local(): parts = lax.all_to_all(partial_scores, 'pool', 0, 0, tiled=True)]
    ppermute x3, waiting for transfers between devices: 11.9 us -> 15.3 us  [everywhere(): got = lax.ppermute(x, 'pool', [(i, i ^ k) for i in range(n)])]
  transfers between devices with their start and end apart: 9 -> 10, of which waited for: 7 -> 8; matrix products, arithmetic and copies ran while one was open for 11% -> 12% of each run, Pallas kernels for 0% -> 2%
where the time goes in v3:
time: 173 us; the launch traced here: 172 us
  waiting for transfers between devices  60.1 us (35%)
  blocking collectives  29.6 us (17%)
  Pallas kernels  26.3 us (15%)
  starting transfers between devices  25.4 us (15%)
  local copies, waits for them, and re-layouts  14.1 us (8%)
  matrix products  9.36 us (5%)
  other arithmetic  6.28 us (4%)
    all_to_all x1, blocking collectives, local(): term_parts = lax.all_to_all(terms, 'pool', 0, 0, tiled=True)  17.6 us
    all_to_all x2, waiting for transfers between devices, local(): lax.all_to_all(p, 'pool', 0, 0, tiled=True).reshape(n * size, part)  17.5 us
    ppermute x3, waiting for transfers between devices, everywhere(): got = lax.ppermute(x, 'pool', [(i, i ^ k) for i in range(n)])  15.3 us
    all_to_all x1, waiting for transfers between devices, local(): lax.all_to_all(attended, 'pool', 0, 0, tiled=True)  14 us
    all_to_all x1, blocking collectives, local(): all_weights = lax.all_to_all(weights, 'pool', 0, 0, tiled=True)  12.1 us
    pallas_call x1, Pallas kernels, local(): pl.pallas_call(functools.partial(score_kernel, rows, pieces), grid_spec=p...  11.1 us
    pallas_call x1, Pallas kernels, local(): pl.pallas_call(functools.partial(value_kernel, rows), grid=(n,), in_specs...  9.98 us
    all_to_all x1, waiting for transfers between devices, local(): parts = lax.all_to_all(partial_scores, 'pool', 0, 0, tiled=True)  8.31 us
  transfers between devices with their start and end apart: 10, of which 8 were waited for; matrix products, arithmetic and copies ran while one was open for 12% of the time, Pallas kernels for 2%

profile of v3, /device:TPU:0, one launch (start us, length us, event | category | flops | bytes accessed | tf_op | source)
XLA Modules:
  0.0 171.5 jit_solution(5479631825158245874)
XLA Ops:
  0.0 4.0 %collective-permute-start = (bf16[8,32,128]{2,1,0:T(8,128)(2,1)}, bf16[8,32,128]{2,1,0:T(8,128)(2,1)}, u32[]{:S(2)}, u32[]{:S(2)}) collective-permute-start(bf16[8,32,128]{2,1,0:T(8,128)(2,1)} %param.14), channel_id=1, source_target_pairs={{0,8},{2,10},{4,12},{6,14},{8,0},{10,2},{12,4},{14,6},{1,9},{3,11}... | collective-permute-start | bytes 196616 | tf_op jit(solution)/shard_map/ppermute | solution.py:132
  4.0 2.2 %copy-done = bf16[256,8192]{1,0:T(8,128)(2,1)S(1)} copy-done((bf16[256,8192]{1,0:T(8,128)(2,1)S(1)}, bf16[256,8192]{1,0:T(8,128)(2,1)}, u32[]{:S(2)}) %copy-start) | copy-done | bytes 4194328
  6.2 3.1 %pack_columns.1 = (bf16[8,64,1024]{2,1,0:T(8,128)(2,1)}, bf16[8,64,1024]{2,1,0:T(8,128)(2,1)}) custom-call(s32[1]{0:T(128)} %bitcast.core_ref, bf16[256,8192]{1,0:T(8,128)(2,1)S(1)} %copy-done), custom_call_target="tpu_custom_call" | custom-call | tf_op jit(solution)/shard_map/pack_columns/pallas_call | solution.py:166
  9.4 4.0 %all-to-all-start = ((bf16[8,64,1024]{2,1,0:T(8,128)(2,1)}), bf16[8,64,1024]{2,1,0:T(8,128)(2,1)S(1)}, u32[]{:S(2)}, u32[]{:S(2)}) async-start(bf16[8,64,1024]{2,1,0:T(8,128)(2,1)} %get-tuple-element.19), calls=%async_computation | async-start | bytes 2097152 | tf_op jit(solution)/shard_map/all_to_all | solution.py:178
  13.3 0.0 copy-done.12
  13.4 0.0 copy-done.14
  13.4 0.2 convert_reduce_fusion
  13.6 0.0 copy-done.13
  13.6 0.9 select_reduce_fusion.1
  14.5 0.1 sub.32
  14.6 0.1 broadcast_in_dim.26
  14.7 0.8 broadcast_in_dim.54
  15.5 0.1 lt.92
  15.6 0.1 lt.93
  15.7 0.8 lt.103
  16.5 0.6 lt.90
  17.1 0.0 copy-done.15
  17.1 0.1 iota_compare_fusion.2
  17.2 3.1 %fusion.24 = (bf16[8,256,4,128]{3,2,1,0:T(4,128)(2,1)S(1)}, bf16[8,256,4,128]{3,2,1,0:T(4,128)(2,1)S(1)}) fusion(bf16[8,256,4,256]{3,2,1,0:T(4,128)(2,1)} %param.15), kind=kLoop, calls=%fused_computation.59 | loop fusion | bytes 8388608 | tf_op jit(solution)/shard_map/slice | solution.py:220
  20.2 0.0 copy-done.6
  20.3 0.7 fusion.26
  21.0 0.4 fusion
  21.4 0.0 copy-start.11
  21.5 17.5 %all-to-all-done = bf16[8,64,1024]{2,1,0:T(8,128)(2,1)S(1)} async-done(((bf16[8,64,1024]{2,1,0:T(8,128)(2,1)}), bf16[8,64,1024]{2,1,0:T(8,128)(2,1)S(1)}, u32[]{:S(2)}, u32[]{:S(2)}) %all-to-all-start) | async-done | bytes 1048608 | tf_op jit(solution)/shard_map/all_to_all | solution.py:178
  39.0 3.6 %all-to-all-start.1 = ((bf16[8,64,1024]{2,1,0:T(8,128)(2,1)}), bf16[8,64,1024]{2,1,0:T(8,128)(2,1)S(1)}, u32[]{:S(2)}, u32[]{:S(2)}) async-start(bf16[8,64,1024]{2,1,0:T(8,128)(2,1)} %get-tuple-element.21), calls=%async_computation.1 | async-start | bytes 2097152 | tf_op jit(solution)/shard_map/all_to_all | solution.py:178
  42.5 0.0 copy-done.9
  42.5 0.0 copy-done.10
  42.6 0.6 compare_select_fusion.refs_5_.row_ref
  43.2 3.2 %fusion.25 = (bf16[1024,4,128]{2,1,0:T(4,128)(2,1)S(1)}, bf16[1024,4,128]{2,1,0:T(4,128)(2,1)}) fusion(bf16[1024,4,256]{2,1,0:T(4,128)(2,1)} %param.10), kind=kLoop, calls=%fused_computation.60 | loop fusion | bytes 4194304 | tf_op jit(solution)/shard_map/slice | solution.py:203
  46.4 0.8 fusion.15
  47.2 1.2 copy.58
  48.4 0.0 collective-permute-done
  48.4 1.0 maximum_select_fusion.3
  49.4 2.0 %collective-permute-start.1 = (bf16[2,8,32,128]{3,2,1,0:T(8,128)(2,1)S(1)}, bf16[2,8,32,128]{3,2,1,0:T(8,128)(2,1)S(1)}, u32[]{:S(2)}, u32[]{:S(2)}) collective-permute-start(bf16[2,8,32,128]{3,2,1,0:T(8,128)(2,1)S(1)} %maximum_select_fusion.3), channel_id=1, source_target_pairs={{0,4},{2,6},{4,0},{6,2},{8,12},{10,14},{12,8},{14,10},{1,5},{3,7},... | collective-permute-start | bytes 393224 | tf_op jit(solution)/shard_map/ppermute | solution.py:132
  51.4 0.9 fusion.28
  52.3 0.9 maximum_select_fusion.2
  53.3 9.5 %collective-permute-done.1 = bf16[2,8,32,128]{3,2,1,0:T(8,128)(2,1)S(1)} collective-permute-done((bf16[2,8,32,128]{3,2,1,0:T(8,128)(2,1)S(1)}, bf16[2,8,32,128]{3,2,1,0:T(8,128)(2,1)S(1)}, u32[]{:S(2)}, u32[]{:S(2)}) %collective-permute-start.1) | collective-permute-done | bytes 131104 | tf_op jit(solution)/shard_map/ppermute | solution.py:132
  62.8 1.5 collective-permute-start.2
  64.4 5.8 %collective-permute-done.2 = bf16[2,2,8,32,128]{4,3,2,1,0:T(8,128)(2,1)S(1)} collective-permute-done((bf16[2,2,8,32,128]{4,3,2,1,0:T(8,128)(2,1)S(1)}, bf16[2,2,8,32,128]{4,3,2,1,0:T(8,128)(2,1)S(1)}, u32[]{:S(2)}, u32[]{:S(2)}) %collective-permute-start.2) | collective-permute-done | bytes 262176 | tf_op jit(solution)/shard_map/ppermute | solution.py:132
  70.2 0.0 copy-done.3
  70.2 3.2 %convolution_convert_fusion = bf16[4,8,8,8,1024]{4,3,2,1,0:T(8,128)(2,1)} fusion(bf16[1024,4,128]{2,1,0:T(4,128)(2,1)S(1)} %copy-done.3, bf16[8,8,4,8,128]{4,3,2,1,0:T(8,128)(2,1)S(1)} %bitcast.49), kind=kOutput, calls=%fused_computation | convolution fusion | flops 538968064 | bytes 5767168 | tf_op jit(solution)/shard_map/qrhgd,phd->hqrgp/dot_general | solution.py:199
  73.5 0.0 collective-permute-start.4
  73.5 0.0 all-to-all-done.1
  73.5 0.5 collective-permute-start.3
  74.0 2.1 %collective-permute-done.4.refs_3_ = bf16[512,1024]{1,0:T(8,128)(2,1)S(1)} collective-permute-done((bf16[512,1024]{1,0:T(8,128)(2,1)S(1)}, bf16[512,1024]{1,0:T(8,128)(2,1)S(1)}, u32[]{:S(2)}, u32[]{:S(2)}) %collective-permute-start.4) | collective-permute-done | bytes 1048608 | tf_op jit(solution)/shard_map/ppermute | solution.py:229
  76.1 1.5 collective-permute-done.3.refs_2_
  77.6 1.0 copy-done.5
  78.6 11.1 %prompt_scores.1 = (bf16[8,32,512]{2,1,0:T(8,128)(2,1)}, bf16[8,512,1024]{2,1,0:T(8,128)(2,1)}) custom-call(s32[512]{0:T(512)} %get-tuple-element.20.src_ref, s32[1]{0:T(128)} %bitcast.core_ref, bf16[512,1024]{1,0:T(8,128)(2,1)} %bitcast.48, bf16[512,1024]{1,0:T(8,128)(2,1)} %bitcast.45, bf16[512,1024]{1,0:T(8,128)(2,1)} %copy-done.5, ...), custom_call_target="tpu_custom_call" | custom-call | tf_op jit(solution)/shard_map/prompt_scores/pallas_call | solution.py:231
  89.7 6.2 %all-to-all-start.2 = ((bf16[8,32,512]{2,1,0:T(8,128)(2,1)}), bf16[8,32,512]{2,1,0:T(8,128)(2,1)S(1)}, u32[]{:S(2)}, u32[]{:S(2)}) async-start(bf16[8,32,512]{2,1,0:T(8,128)(2,1)} %get-tuple-element.25), calls=%async_computation.2 | async-start | bytes 524288 | tf_op jit(solution)/shard_map/all_to_all | solution.py:255
  95.8 0.1 reshape.405.top_ref
  95.9 0.1 reshape.406.sum_ref
  96.1 0.7 dynamic-slice_bitcast_fusion.row_ref
  96.7 8.3 %all-to-all-done.2.parts_ref = bf16[8,32,512]{2,1,0:T(8,128)(2,1)S(1)} async-done(((bf16[8,32,512]{2,1,0:T(8,128)(2,1)}), bf16[8,32,512]{2,1,0:T(8,128)(2,1)S(1)}, u32[]{:S(2)}, u32[]{:S(2)}) %all-to-all-start.2) | async-done | bytes 262176 | tf_op jit(solution)/shard_map/all_to_all | solution.py:255
  105.0 1.2 softmax_weights.1
  106.3 12.1 %all_to_all.30.w_ref = bf16[8,32,512]{2,1,0:T(8,128)(2,1)} all-to-all(bf16[8,32,512]{2,1,0:T(8,128)(2,1)S(1)} %get-tuple-element.29), channel_id=1, replica_groups=mesh['groups'=2,'pool'=8,'tp'=2] {'pool'}, dimensions={0} | all-to-all | bytes 524288 | tf_op jit(solution)/shard_map/all_to_all | solution.py:273
  118.3 10.0 %weighted_values.1 = bf16[8,4,64,128]{3,2,1,0:T(8,128)(2,1)} custom-call(bf16[8,32,512]{2,1,0:T(8,128)(2,1)} %all_to_all.30.w_ref, s32[8,1,512]{2,1,0:T(1,128)} %compare_select_fusion.refs_5_.row_ref, bf16[8,512,1024]{2,1,0:T(8,128)(2,1)} %get-tuple-element.30.slot_ref, bf16[4,1024,128]{2,1,0:T(8,128)(2,1)} %bitcast.46), custom_call_target="tpu_custom_call" | custom-call | tf_op jit(solution)/shard_map/weighted_values/pallas_call | solution.py:274
  128.3 17.6 %all_to_all.31.parts_ref = bf16[8,4,64,128]{3,2,1,0:T(8,128)(2,1)S(1)} all-to-all(bf16[8,4,64,128]{3,2,1,0:T(8,128)(2,1)} %weighted_values.1), channel_id=1, replica_groups=mesh['groups'=2,'pool'=8,'tp'=2] {'pool'}, dimensions={0} | all-to-all | bytes 1048576 | tf_op jit(solution)/shard_map/all_to_all | solution.py:290
  145.9 0.9 attended_sum.1
  146.8 3.6 %all-to-all-start.5 = ((bf16[8,8,4096]{2,1,0:T(8,128)(2,1)}), bf16[8,8,4096]{2,1,0:T(8,128)(2,1)S(1)}, u32[]{:S(2)}, u32[]{:S(2)}) async-start(bf16[8,8,4096]{2,1,0:T(8,128)(2,1)} %attended_sum.1), calls=%async_computation.5 | async-start | bytes 1048576 | tf_op jit(solution)/shard_map/all_to_all | solution.py:299
  150.4 14.0 %all-to-all-done.5 = bf16[8,8,4096]{2,1,0:T(8,128)(2,1)S(1)} async-done(((bf16[8,8,4096]{2,1,0:T(8,128)(2,1)}), bf16[8,8,4096]{2,1,0:T(8,128)(2,1)S(1)}, u32[]{:S(2)}, u32[]{:S(2)}) %all-to-all-start.5) | async-done | bytes 524320 | tf_op jit(solution)/shard_map/all_to_all | solution.py:299
  164.5 4.9 %fusion.10 = f32[64,1024]{1,0:T(8,128)S(1)} fusion(bf16[4096,1024]{1,0:T(8,128)(2,1)} %param.17, bf16[8,8,4096]{2,1,0:T(8,128)(2,1)S(1)} %all-to-all-done.5), kind=kOutput, calls=%fused_computation.10 | convolution fusion | flops 536870912 | bytes 9175040 | tf_op jit(solution)/shard_map/dot_general | solution.py:300
  169.5 0.1 collective-permute-start.5
  169.5 1.3 collective-permute-done.5
  170.9 0.6 add_convert_fusion
  (32 shorter events, 0.2 us)
Async XLA Ops:
  0.0 48.4 %collective-permute-start = (bf16[8,32,128]{2,1,0:T(8,128)(2,1)}, bf16[8,32,128]{2,1,0:T(8,128)(2,1)}, u32[]{:S(2)}, u32[]{:S(2)}) collective-permute-start(bf16[8,32,128]{2,1,0:T(8,128)(2,1)} %param.14), channel_id=1, source_target_pairs={{0,8},{2,10},{4,12},{6,14},{8,0},{10,2},{12,4},{14,6},{1,9},{3,11}... | collective-permute-start | bytes 196616 | tf_op jit(solution)/shard_map/ppermute | solution.py:132
  4.0 2.2 %copy-start = (bf16[256,8192]{1,0:T(8,128)(2,1)S(1)}, bf16[256,8192]{1,0:T(8,128)(2,1)}, u32[]{:S(2)}) copy-start(bf16[256,8192]{1,0:T(8,128)(2,1)} %x_ref.1) | copy-start | bytes 12582916
  9.4 4.0 %copy-start.12 = (s32[256,1]{0,1:T(1,128)S(1)}, s32[256,1]{0,1:T(1,128)}, u32[]{:S(2)}) copy-start(s32[256,1]{0,1:T(1,128)} %param.11) | copy-start | bytes 3076
  9.4 4.0 %copy-start.14 = (s32[256]{0:T(256)S(1)}, s32[256]{0:T(256)}, u32[]{:S(2)}) copy-start(s32[256]{0:T(256)} %param.12) | copy-start | bytes 3076
  9.4 4.2 %copy-start.13 = (s32[256]{0:T(256)S(1)}, s32[256]{0:T(256)}, u32[]{:S(2)}) copy-start(s32[256]{0:T(256)} %param.13) | copy-start | bytes 3076
  9.4 7.7 %copy-start.15 = (s32[8]{0:T(128)S(1)}, s32[8]{0:T(128)}, u32[]{:S(2)}) copy-start(s32[8]{0:T(128)} %param.16) | copy-start | bytes 100
  9.4 29.6 %all-to-all-start = ((bf16[8,64,1024]{2,1,0:T(8,128)(2,1)}), bf16[8,64,1024]{2,1,0:T(8,128)(2,1)S(1)}, u32[]{:S(2)}, u32[]{:S(2)}) async-start(bf16[8,64,1024]{2,1,0:T(8,128)(2,1)} %get-tuple-element.19), calls=%async_computation | async-start | bytes 2097152 | tf_op jit(solution)/shard_map/all_to_all | solution.py:178
  17.2 3.1 %copy-start.6 = (bf16[8,32,128]{2,1,0:T(8,128)(2,1)S(1)}, bf16[8,32,128]{2,1,0:T(8,128)(2,1)}, u32[]{:S(2)}) copy-start(bf16[8,32,128]{2,1,0:T(8,128)(2,1)} %param.14) | copy-start | bytes 196612
  21.4 21.1 %copy-start.9 = (s32[8,1,512]{2,1,0:T(1,128)S(1)}, s32[8,1,512]{2,1,0:T(1,128)}, u32[]{:S(2)}) copy-start(s32[8,1,512]{2,1,0:T(1,128)} %broadcast_in_dim.54) | copy-start | bytes 49156
  21.4 21.1 %copy-start.10 = (s32[8,1,512]{2,1,0:T(1,128)S(1)}, s32[8,1,512]{2,1,0:T(1,128)}, u32[]{:S(2)}) copy-start(s32[8,1,512]{2,1,0:T(1,128)} %lt.103) | copy-start | bytes 49156
  21.4 21.1 %copy-start.11 = (s32[512]{0:T(512)S(1)}, s32[512]{0:T(512)}, u32[]{:S(2)}) copy-start(s32[512]{0:T(512)} %lt.90) | copy-start | bytes 6148
  39.0 34.5 %copy-start.1 = (bf16[8,64,1024]{2,1,0:T(8,128)(2,1)}, bf16[8,64,1024]{2,1,0:T(8,128)(2,1)S(1)}, u32[]{:S(2)}) copy-start(bf16[8,64,1024]{2,1,0:T(8,128)(2,1)S(1)} %all-to-all-done) | copy-start | bytes 3145732
  39.0 34.5 %all-to-all-start.1 = ((bf16[8,64,1024]{2,1,0:T(8,128)(2,1)}), bf16[8,64,1024]{2,1,0:T(8,128)(2,1)S(1)}, u32[]{:S(2)}, u32[]{:S(2)}) async-start(bf16[8,64,1024]{2,1,0:T(8,128)(2,1)} %get-tuple-element.21), calls=%async_computation.1 | async-start | bytes 2097152 | tf_op jit(solution)/shard_map/all_to_all | solution.py:178
  47.2 1.2 copy-start.7
  48.4 21.8 %copy-start.3 = (bf16[1024,4,128]{2,1,0:T(4,128)(2,1)S(1)}, bf16[1024,4,128]{2,1,0:T(4,128)(2,1)}, u32[]{:S(2)}) copy-start(bf16[1024,4,128]{2,1,0:T(4,128)(2,1)} %get-tuple-element.39) | copy-start | bytes 3145732
  49.4 13.4 %collective-permute-start.1 = (bf16[2,8,32,128]{3,2,1,0:T(8,128)(2,1)S(1)}, bf16[2,8,32,128]{3,2,1,0:T(8,128)(2,1)S(1)}, u32[]{:S(2)}, u32[]{:S(2)}) collective-permute-start(bf16[2,8,32,128]{3,2,1,0:T(8,128)(2,1)S(1)} %maximum_select_fusion.3), channel_id=1, source_target_pairs={{0,4},{2,6},{4,0},{6,2},{8,12},{10,14},{12,8},{14,10},{1,5},{3,7},... | collective-permute-start | bytes 393224 | tf_op jit(solution)/shard_map/ppermute | solution.py:132
  62.8 7.4 %collective-permute-start.2 = (bf16[2,2,8,32,128]{4,3,2,1,0:T(8,128)(2,1)S(1)}, bf16[2,2,8,32,128]{4,3,2,1,0:T(8,128)(2,1)S(1)}, u32[]{:S(2)}, u32[]{:S(2)}) collective-permute-start(bf16[2,2,8,32,128]{4,3,2,1,0:T(8,128)(2,1)S(1)} %maximum_select_fusion.1), channel_id=1, source_target_pairs={{0,2},{2,0},{4,6},{6,4},{8,10},{10,8},{12,14},{14,12},{1,3},{3,1},... | collective-permute-start | bytes 786440 | tf_op jit(solution)/shard_map/ppermute | solution.py:132
  73.5 2.7 %collective-permute-start.4 = (bf16[512,1024]{1,0:T(8,128)(2,1)S(1)}, bf16[512,1024]{1,0:T(8,128)(2,1)S(1)}, u32[]{:S(2)}, u32[]{:S(2)}) collective-permute-start(bf16[512,1024]{1,0:T(8,128)(2,1)S(1)} %bitcast.44), channel_id=1, source_target_pairs={{0,1},{1,0},{2,3},{3,2},{4,5},{5,4},{6,7},{7,6},{8,9},{9,8},{10,11... | collective-permute-start | bytes 3145736 | tf_op jit(solution)/shard_map/ppermute | solution.py:229
  73.5 4.2 %copy-start.2 = (bf16[8,64,1024]{2,1,0:T(8,128)(2,1)}, bf16[8,64,1024]{2,1,0:T(8,128)(2,1)S(1)}, u32[]{:S(2)}) copy-start(bf16[8,64,1024]{2,1,0:T(8,128)(2,1)S(1)} %all-to-all-done.1) | copy-start | bytes 3145732
  73.5 22.5 %copy-start.8 = (f32[8,4,8]{2,1,0:T(4,128)S(1)}, f32[8,4,8]{2,1,0:T(4,128)}, u32[]{:S(2)}) copy-start(f32[8,4,8]{2,1,0:T(4,128)} %fusion.15) | copy-start | bytes 3076
  73.5 4.1 %collective-permute-start.3 = (bf16[512,1024]{1,0:T(8,128)(2,1)S(1)}, bf16[512,1024]{1,0:T(8,128)(2,1)S(1)}, u32[]{:S(2)}, u32[]{:S(2)}) collective-permute-start(bf16[512,1024]{1,0:T(8,128)(2,1)S(1)} %bitcast.47), channel_id=1, source_target_pairs={{0,1},{1,0},{2,3},{3,2},{4,5},{5,4},{6,7},{7,6},{8,9},{9,8},{10,11... | collective-permute-start | bytes 3145736 | tf_op jit(solution)/shard_map/ppermute | solution.py:229
  76.1 1.5 copy-start.4
  77.6 1.0 copy-start.5
  89.7 15.4 %all-to-all-start.2 = ((bf16[8,32,512]{2,1,0:T(8,128)(2,1)}), bf16[8,32,512]{2,1,0:T(8,128)(2,1)S(1)}, u32[]{:S(2)}, u32[]{:S(2)}) async-start(bf16[8,32,512]{2,1,0:T(8,128)(2,1)} %get-tuple-element.25), calls=%async_computation.2 | async-start | bytes 524288 | tf_op jit(solution)/shard_map/all_to_all | solution.py:255
  146.8 17.7 %all-to-all-start.5 = ((bf16[8,8,4096]{2,1,0:T(8,128)(2,1)}), bf16[8,8,4096]{2,1,0:T(8,128)(2,1)S(1)}, u32[]{:S(2)}, u32[]{:S(2)}) async-start(bf16[8,8,4096]{2,1,0:T(8,128)(2,1)} %attended_sum.1), calls=%async_computation.5 | async-start | bytes 1048576 | tf_op jit(solution)/shard_map/all_to_all | solution.py:299
  169.5 1.4 collective-permute-start.5

commit v4 on v2

--- a/solution.py
+++ b/solution.py
@@ -11,40 +11,188 @@
 MIB = 1 << 20
 
 
-def score_kernel(rows, src_ref, core_ref, mine_ref, other_ref, keyed_ref, row_ref, out_ref, slot_ref, wide):
+def pack_kernel(base, at_ref, fill_ref, *refs):
+    *x_refs, out_ref, ranks, pick = refs
     q = pl.program_id(0)
-    held = mine_ref.shape[0]
-    step = 256
+    rows = out_ref.shape[1]
+    tokens = ranks.shape[1]
 
     @pl.when(q == 0)
     def _():
-        core = core_ref[0]
-        for side, ref in ((core, mine_ref), (1 - core, other_ref)):
-            for i in range(0, held, step):
-                wide[pl.ds(pl.multiple_of(side * held + i, step), step), :] = ref[
-                    i : i + step, :
-                ].astype(jnp.float32)
-
-    slots = slot_ref.shape[1]
-    count = slots // BLK
-    for i in range(0, count, 2):
-        pair = [
-            wide[pl.ds(pl.multiple_of(src_ref[q * count + i + j] * BLK, BLK), BLK), :]
-            for j in range(2)
+        fills = fill_ref[...].astype(jnp.float32)
+        blocks = fills.shape[1]
+        block = lax.broadcasted_iota(jnp.int32, (blocks, tokens), 0)
+        token = lax.broadcasted_iota(jnp.int32, (blocks, tokens), 1) // BLK
+        fill = jnp.dot(
+            fills, (block == token).astype(jnp.float32), preferred_element_type=jnp.float32
+        )
+        ahead = jnp.dot(
+            fills, (block < token).astype(jnp.float32), preferred_element_type=jnp.float32
+        )
+        place = lax.broadcasted_iota(jnp.int32, fill.shape, 1) % BLK
+        rank = ahead.astype(jnp.int32) + place
+        ranks[...] = jnp.where(place < fill.astype(jnp.int32), rank, -1)
+        wanted = (
+            base + at_ref[1] * rows + lax.broadcasted_iota(jnp.int32, (rows, tokens), 0)
+        )
+        pick[...] = (wanted == ranks[pl.ds(at_ref[0], 1), :]).astype(pick.dtype)
+
+    x = jnp.concatenate([ref[...] for ref in x_refs])
+    out_ref[0] = jnp.dot(pick[...], x, preferred_element_type=jnp.float32).astype(out_ref.dtype)
+
+
+def pack(x_prompt, fills, at, base, size):
+    tokens, width = x_prompt.shape
+    n = fills.shape[0]
+    part = width // n
+    cuts = 4
+    return pl.pallas_call(
+        functools.partial(pack_kernel, base),
+        grid_spec=pltpu.PrefetchScalarGridSpec(
+            num_scalar_prefetch=1,
+            grid=(n,),
+            in_specs=[pl.BlockSpec(fills.shape, lambda q, a: (0, 0))]
+            + [
+                pl.BlockSpec((tokens // cuts, part), functools.partial(lambda i, q, a: (i, q), i))
+                for i in range(cuts)
+            ],
+            out_specs=pl.BlockSpec((1, size, part), lambda q, a: (q, 0, 0)),
+            scratch_shapes=[
+                pltpu.VMEM((n, tokens), jnp.int32),
+                pltpu.VMEM((size, tokens), jnp.bfloat16),
+            ],
+        ),
+        out_shape=jax.ShapeDtypeStruct((n, size, part), jnp.bfloat16),
+        compiler_params=pltpu.CompilerParams(vmem_limit_bytes=56 * MIB),
+        name="pack_live_tokens",
+    )(at, fills, *([x_prompt] * cuts))
+
+
+def score_kernel(
+    rows, meta_ref, mine_ref, other_ref, more_mine_ref, more_other_ref, keyed_ref, row_ref,
+    out_ref, tile_ref, first, last, wide, line, tiles, in_sem, out_sem,
+):
+    q = pl.program_id(0)
+    n, count = tiles.shape[0], (meta_ref.shape[0] - 2) // (2 * tiles.shape[0]) - 1
+    size, extra = first.shape[1] // n, last.shape[1] // n
+    tokens = 2 * (size + extra)
+    tile, part = tile_ref.shape[2:]
+    lanes = wide.shape[1]
+    blocks_here = meta_ref[2 * n * count + q]
+    rows_here = meta_ref[2 * n * count + n + q]
+    core = meta_ref[2 * n * (count + 1)]
+    over = meta_ref[2 * n * (count + 1) + 1]
+    cuts = in_sem.shape[1]
+    span = n * size // cuts
+
+    @pl.when(q == 0)
+    def _():
+        copies = [
+            pltpu.make_async_copy(
+                ref.at[pl.ds(i * span, span)], first.at[j, pl.ds(i * span, span)], in_sem.at[j, i]
+            )
+            for i in range(cuts)
+            for j, ref in enumerate((mine_ref, other_ref))
         ]
-        slot_ref[0, i * BLK : (i + 2) * BLK, :] = jnp.concatenate(pair).astype(jnp.bfloat16)
-    kvh, per, part = keyed_ref.shape
-    raw = lax.dot_general(
-        keyed_ref[...].reshape(kvh * per, part),
-        slot_ref[0],
-        (((1,), (1,)), ((), ())),
-        preferred_element_type=jnp.float32,
-    ).reshape(kvh, rows, per // rows, slots)
-    owner_row = row_ref[0]
-    picked = jnp.zeros((kvh, per // rows, slots), jnp.float32)
-    for r in range(rows):
-        picked = picked + jnp.where((owner_row == r)[None], raw[:, r], 0.0)
-    out_ref[0] = picked.reshape(kvh * (per // rows), slots).astype(out_ref.dtype)
+        for copy in copies:
+            copy.start()
+
+        @pl.loop(0, line.shape[0] // (BLK * BLK))
+        def _(i):
+            line[pl.ds(pl.multiple_of(i * BLK * BLK, BLK), BLK * BLK), :] = jnp.zeros(
+                (BLK * BLK, lanes), line.dtype
+            )
+
+        wide[n * tokens * BLK :, :] = jnp.zeros((BLK * BLK, lanes), wide.dtype)
+        for copy in copies:
+            copy.wait()
+
+        def widen(held, j, s, at, length):
+            for k in range(part // lanes):
+                wide[pl.ds(at * BLK + k, length, stride=BLK), :] = held[
+                    j,
+                    pl.ds(pl.multiple_of(s * length, length), length),
+                    k * lanes : (k + 1) * lanes,
+                ].astype(wide.dtype)
+
+        @pl.loop(0, n)
+        def _(s):
+            for j in range(2):
+                side = core if j == 0 else 1 - core
+                widen(first, j, s, s * tokens + side * size, size)
+
+        @pl.when(over == 0)
+        def _():
+            @pl.loop(0, n)
+            def _(s):
+                at = pl.multiple_of((s * tokens + 2 * size) * BLK, BLK)
+                wide[pl.ds(at, 2 * extra * BLK), :] = jnp.zeros(
+                    (2 * extra * BLK, lanes), wide.dtype
+                )
+
+        @pl.when(over != 0)
+        def _():
+            rest = [
+                pltpu.make_async_copy(ref, last.at[j], in_sem.at[j, 0])
+                for j, ref in enumerate((more_mine_ref, more_other_ref))
+            ]
+            for copy in rest:
+                copy.start()
+            for copy in rest:
+                copy.wait()
+
+            @pl.loop(0, n)
+            def _(s):
+                for j in range(2):
+                    side = core if j == 0 else 1 - core
+                    widen(last, j, s, s * tokens + 2 * size + side * extra, extra)
+
+    @pl.loop(0, blocks_here)
+    def _(i):
+        source = pl.multiple_of(meta_ref[q * count + i] * BLK, BLK)
+        target = pl.multiple_of(meta_ref[n * count + q * count + i] * BLK, BLK)
+        line[pl.ds(target, BLK * BLK), :] = wide[pl.ds(source, BLK * BLK), :]
+
+    kvh, per, _ = keyed_ref.shape
+    group = per // rows
+
+    def one(t):
+        here = slice(t * tile, (t + 1) * tile)
+        for k in range(part // lanes):
+            tiles[q, t, :, k * lanes : (k + 1) * lanes] = line[
+                pl.ds(t * tile * BLK + k, tile, stride=BLK), :
+            ].astype(tiles.dtype)
+        pltpu.make_async_copy(tiles.at[q, t], tile_ref.at[q, t], out_sem.at[q, t]).start()
+        raw = lax.dot_general(
+            keyed_ref[...].reshape(kvh * per, part),
+            tiles[q, t],
+            (((1,), (1,)), ((), ())),
+            preferred_element_type=jnp.float32,
+        ).reshape(kvh, rows, group, tile)
+        owner_row = row_ref[0, :, here]
+        picked = jnp.zeros((kvh, group, tile), jnp.float32)
+        for r in range(rows):
+            picked = picked + jnp.where((owner_row == r)[None], raw[:, r], 0.0)
+        out_ref[0, :, here] = picked.reshape(kvh * group, tile).astype(out_ref.dtype)
+
+    one(0)
+    for t in range(1, tiles.shape[1]):
+        pl.when(rows_here > t * tile)(functools.partial(one, t))
+
+    @pl.when(q == n - 1)
+    def _():
+        for o in range(n):
+            for t in range(tiles.shape[1]):
+
+                def done(o=o, t=t):
+                    pltpu.make_async_copy(
+                        tiles.at[o, t], tile_ref.at[o, t], out_sem.at[o, t]
+                    ).wait()
+
+                if t:
+                    pl.when(meta_ref[2 * n * count + n + o] > t * tile)(done)
+                else:
+                    done()
 
 
 def weight_kernel(scale, parts_ref, row_ref, top_ref, sum_ref, cached_ref, w_ref, kept_ref):
@@ -69,25 +217,49 @@
         w_ref[i] = weights
 
 
-def value_kernel(rows, w_ref, row_ref, slot_ref, value_ref, out_ref, mixed):
+def value_kernel(rows, size_ref, w_ref, row_ref, tile_ref, value_ref, out_ref, tiles, acc, mixed, sem):
     q = pl.program_id(0)
+    n, cuts, tile, _ = tiles.shape
     kvh = value_ref.shape[0]
-    heads, slots = w_ref.shape[1:]
+    heads = w_ref.shape[1]
     per = rows * heads // kvh
-    weights = w_ref[0].astype(jnp.float32).reshape(kvh, 1, heads // kvh, slots)
-    owner_row = row_ref[0]
-    spread = jnp.concatenate(
-        [jnp.where((owner_row == r)[None, None], weights, 0.0) for r in range(rows)], 1
-    ).reshape(kvh * per, slots)
-    got = jnp.dot(
-        spread.astype(jnp.bfloat16), slot_ref[0], preferred_element_type=jnp.float32
-    ).astype(jnp.bfloat16)
+
+    def copy(o, t):
+        return pltpu.make_async_copy(tile_ref.at[o, t], tiles.at[o, t], sem.at[o, t])
+
+    @pl.when(q == 0)
+    def _():
+        for o in range(n):
+            copy(o, 0).start()
+            for t in range(1, cuts):
+                pl.when(size_ref[o] > t * tile)(lambda o=o, t=t: copy(o, t).start())
+
+    def one(t):
+        copy(q, t).wait()
+        here = slice(t * tile, (t + 1) * tile)
+        weights = w_ref[0, :, here].astype(jnp.float32).reshape(kvh, 1, heads // kvh, tile)
+        owner_row = row_ref[0, :, here]
+        spread = jnp.concatenate(
+            [jnp.where((owner_row == r)[None, None], weights, 0.0) for r in range(rows)], 1
+        ).reshape(kvh * per, tile)
+        got = jnp.dot(
+            spread.astype(jnp.bfloat16), tiles[q, t], preferred_element_type=jnp.float32
+        )
+        if t:
+            acc[...] += got
+        else:
+            acc[...] = got
+
+    one(0)
+    for t in range(1, cuts):
+        pl.when(size_ref[q] > t * tile)(functools.partial(one, t))
     for h in range(kvh):
-        mixed[h, pl.ds(pl.multiple_of(q * per, per), per), :] = got[h * per : (h + 1) * per]
-
-    @pl.when(q == pl.num_programs(0) - 1)
+        mixed[h, pl.ds(pl.multiple_of(q * per, per), per), :] = acc[
+            h * per : (h + 1) * per, :
+        ].astype(mixed.dtype)
+
+    @pl.when(q == n - 1)
     def _():
-        n = out_ref.shape[0]
         for h in range(kvh):
             done = jnp.dot(mixed[h], value_ref[h], preferred_element_type=jnp.float32)
             out_ref[:, h] = done.reshape(n, per, done.shape[1]).astype(out_ref.dtype)
@@ -151,28 +323,62 @@
     scale = 1.0 / hd**0.5
     swap = [(i, (i + 1) % ntp) for i in range(ntp)]
 
-    sent = lax.dynamic_slice_in_dim(x_prompt, core * half, half, 0)
-    sent = sent.reshape(half, n, part).transpose(1, 0, 2)
-    mine = lax.all_to_all(sent, "pool", 0, 0, tiled=True).reshape(n * half, part)
-    other = lax.ppermute(mine, "tp", swap)
+    size = half * 3 // 4
+    extra = half - size
+    at = jnp.stack([me, core]).astype(jnp.int32)
+    fills = block_fill.reshape(n, blocks)
+    mine = lax.all_to_all(pack(x_prompt, fills, at, 0, size), "pool", 0, 0, tiled=True)
+    mine = mine.reshape(n * size, part)
 
     dest = block_dest[:, 0]
     index = jnp.arange(n * blocks, dtype=jnp.int32)
     sender = index // blocks
-    key = dest * n + sender
-    earlier = (key[:, None] == key[None, :]) & (index[None, :] < index[:, None])
-    rank = jnp.sum(earlier.astype(jnp.int32), 1)
-    hit = (
-        jnp.arange(n * count, dtype=jnp.int32)[:, None] == (key * cap + rank)[None, :]
-    ).astype(jnp.int32)
-    inner = index % blocks
-    held = half // BLK
-    source = (inner // held) * (n * held) + sender * held + inner % held
-    slot_src = jnp.sum(hit * source[None, :], 1)
-    slot_row = jnp.sum(hit * (block_row + 1)[None, :], 1) - 1
-    slot_fill = jnp.sum(hit * block_fill[None, :], 1)
-    live = jnp.arange(BLK, dtype=jnp.int32)[None, :] < slot_fill[:, None]
-    rowof = jnp.where(live, slot_row[:, None], -1).reshape(n, 1, slots)
+    ahead = index[None, :] < index[:, None]
+    kin = ahead & (sender[None, :] == sender[:, None])
+    rival = ahead & (dest[None, :] == dest[:, None])
+    sent_at = jnp.sum(jnp.where(kin, block_fill[None, :], 0), 1)
+    list_at = jnp.sum(jnp.where(rival, block_fill[None, :], 0), 1)
+    rank = jnp.sum(rival.astype(jnp.int32), 1)
+    hit = jnp.arange(n * count, dtype=jnp.int32)[:, None] == (dest * count + rank)[None, :]
+    slot_src = jnp.sum(jnp.where(hit, (sender * tokens + sent_at)[None, :], 0), 1)
+    slot_dst = jnp.sum(jnp.where(hit, list_at[None, :], 0), 1)
+    owned = jnp.arange(n, dtype=jnp.int32)[:, None] == dest[None, :]
+    list_blocks = jnp.sum(owned.astype(jnp.int32), 1)
+    list_rows = jnp.sum(jnp.where(owned, block_fill[None, :], 0), 1)
+    spot = jnp.arange(n * slots, dtype=jnp.int32)[:, None]
+    start = (dest * slots + list_at)[None, :]
+    inside = (spot >= start) & (spot < start + block_fill[None, :])
+    rowof = jnp.sum(jnp.where(inside, (block_row + 1)[None, :], 0), 1) - 1
+    rowof = rowof.reshape(n, 1, slots)
+
+    most = jnp.max(jnp.sum(fills, 1))
+    groups = lax.axis_size("groups")
+    k = 1
+    while k < groups:
+        most = jnp.maximum(
+            most, lax.ppermute(most, "groups", [(i, i ^ k) for i in range(groups)])
+        )
+        k *= 2
+    over = most > ntp * size
+
+    def exchange_rest():
+        rest = pack(x_prompt, fills, at, ntp * size, extra)
+        rest = lax.all_to_all(rest, "pool", 0, 0, tiled=True).reshape(n * extra, part)
+        return rest, lax.ppermute(rest, "tp", swap)
+
+    def no_rest():
+        return (jnp.zeros((n * extra, part), jnp.bfloat16),) * 2
+
+    more_mine, more_other = lax.cond(over, exchange_rest, no_rest)
+    meta = jnp.concatenate(
+        [
+            slot_src,
+            slot_dst,
+            list_blocks,
+            list_rows,
+            jnp.stack([core.astype(jnp.int32), over.astype(jnp.int32)]),
+        ]
+    )
 
     allq = everywhere(queries, n).reshape(n, rows, kvh, group, hd)
     keyed = jnp.einsum(
@@ -200,30 +406,45 @@
         preferred_element_type=jnp.float32,
     )
 
-    partial_scores, slot_x = pl.pallas_call(
+    mine, meta, list_rows, rowof, keyed, values, cache_top, cache_sum, cached = (
+        lax.optimization_barrier(
+            (mine, meta, list_rows, rowof, keyed, values, cache_top, cache_sum, cached)
+        )
+    )
+    other = lax.ppermute(mine, "tp", swap)
+
+    tile = min(256, slots)
+    tiles = slots // tile
+    cuts = 4
+    anywhere = pl.BlockSpec(memory_space=pl.ANY)
+    partial_scores, listed = pl.pallas_call(
         functools.partial(score_kernel, rows),
         grid_spec=pltpu.PrefetchScalarGridSpec(
-            num_scalar_prefetch=2,
+            num_scalar_prefetch=1,
             grid=(n,),
             in_specs=[
-                pl.BlockSpec((n * half, part), lambda q, *_: (0, 0)),
-                pl.BlockSpec((n * half, part), lambda q, *_: (0, 0)),
+                *[anywhere] * 4,
                 pl.BlockSpec((kvh, per, part), lambda q, *_: (0, q, 0)),
                 pl.BlockSpec((1, 1, slots), lambda q, *_: (q, 0, 0)),
             ],
-            out_specs=[
-                pl.BlockSpec((1, heads, slots), lambda q, *_: (q, 0, 0)),
-                pl.BlockSpec((1, slots, part), lambda q, *_: (q, 0, 0)),
+            out_specs=[pl.BlockSpec((1, heads, slots), lambda q, *_: (q, 0, 0)), anywhere],
+            scratch_shapes=[
+                pltpu.VMEM((ntp, n * size, part), jnp.bfloat16),
+                pltpu.VMEM((ntp, n * extra, part), jnp.bfloat16),
+                pltpu.VMEM(((n * tokens + BLK) * BLK, 128), jnp.float32),
+                pltpu.VMEM(((slots + BLK) * BLK, 128), jnp.float32),
+                pltpu.VMEM((n, tiles, tile, part), jnp.bfloat16),
+                pltpu.SemaphoreType.DMA((ntp, cuts)),
+                pltpu.SemaphoreType.DMA((n, tiles)),
             ],
-            scratch_shapes=[pltpu.VMEM((ntp * n * half, part), jnp.float32)],
         ),
         out_shape=[
             jax.ShapeDtypeStruct((n, heads, slots), jnp.bfloat16),
-            jax.ShapeDtypeStruct((n, slots, part), jnp.bfloat16),
+            jax.ShapeDtypeStruct((n, tiles, tile, part), jnp.bfloat16),
         ],
-        compiler_params=pltpu.CompilerParams(vmem_limit_bytes=32 * MIB),
+        compiler_params=pltpu.CompilerParams(vmem_limit_bytes=56 * MIB),
         name="prompt_scores",
-    )(slot_src, core.astype(jnp.int32).reshape(1), mine, other, keyed, rowof)
+    )(meta, mine, other, more_mine, more_other, keyed, rowof)
 
     parts = lax.all_to_all(partial_scores, "pool", 0, 0, tiled=True)
     my_rows = lax.dynamic_index_in_dim(rowof, me, 0, keepdims=False)
@@ -246,19 +467,27 @@
     all_weights = lax.all_to_all(weights, "pool", 0, 0, tiled=True)
     terms = pl.pallas_call(
         functools.partial(value_kernel, rows),
-        grid=(n,),
-        in_specs=[
-            pl.BlockSpec((1, heads, slots), lambda q: (q, 0, 0)),
-            pl.BlockSpec((1, 1, slots), lambda q: (q, 0, 0)),
-            pl.BlockSpec((1, slots, part), lambda q: (q, 0, 0)),
-            pl.BlockSpec((kvh, part, hd), lambda q: (0, 0, 0)),
-        ],
-        out_specs=pl.BlockSpec((n, kvh, per, hd), lambda q: (0, 0, 0, 0)),
+        grid_spec=pltpu.PrefetchScalarGridSpec(
+            num_scalar_prefetch=1,
+            grid=(n,),
+            in_specs=[
+                pl.BlockSpec((1, heads, slots), lambda q, *_: (q, 0, 0)),
+                pl.BlockSpec((1, 1, slots), lambda q, *_: (q, 0, 0)),
+                anywhere,
+                pl.BlockSpec((kvh, part, hd), lambda q, *_: (0, 0, 0)),
+            ],
+            out_specs=pl.BlockSpec((n, kvh, per, hd), lambda q, *_: (0, 0, 0, 0)),
+            scratch_shapes=[
+                pltpu.VMEM((n, tiles, tile, part), jnp.bfloat16),
+                pltpu.VMEM((kvh * per, part), jnp.float32),
+                pltpu.VMEM((kvh, n * per, part), jnp.bfloat16),
+                pltpu.SemaphoreType.DMA((n, tiles)),
+            ],
+        ),
         out_shape=jax.ShapeDtypeStruct((n, kvh, per, hd), jnp.bfloat16),
-        scratch_shapes=[pltpu.VMEM((kvh, n * per, part), jnp.bfloat16)],
-        compiler_params=pltpu.CompilerParams(vmem_limit_bytes=24 * MIB),
+        compiler_params=pltpu.CompilerParams(vmem_limit_bytes=56 * MIB),
         name="weighted_values",
-    )(all_weights, rowof, slot_x, values)
+    )(list_rows, all_weights, rowof, listed, values)
 
     term_parts = lax.all_to_all(terms, "pool", 0, 0, tiled=True)
     attended = pl.pallas_call(

time: 174 us -> 161 us (0.925)
  waiting for transfers between devices: 81.8 us -> 38.8 us
  Pallas kernels: 15.9 us -> 33.3 us
  blocking collectives: 17.2 us -> 29.7 us
  other arithmetic: 2.65 us -> 12 us
  local copies, waits for them, and re-layouts: 20.9 us -> 11.6 us
  matrix products: 11.4 us -> 9.32 us
    all_to_all x2 -> x1, waiting for transfers between devices: 49.7 us -> 0.01 us  [local(): lax.all_to_all(pack(x_prompt, fills, at, 0, size), 'pool', 0, 0, tiled=True)]
    pallas_call x1 -> x2, Pallas kernels: 4.82 us -> 17.1 us  [the longest x1 9.56 us: local(): pl.pallas_call(functools.partial(value_kernel, rows), grid_spec=pltpu.Pre...]
    all_to_all x0 -> x1, blocking collectives: none -> 12.1 us  [local(): all_weights = lax.all_to_all(weights, 'pool', 0, 0, tiled=True)]
    all_to_all x2 -> x1, starting transfers between devices: 10.8 us -> 4.43 us  [local(): lax.all_to_all(pack(x_prompt, fills, at, 0, size), 'pool', 0, 0, tiled=True)]
    pallas_call x1, Pallas kernels: 8.22 us -> 14.1 us  [local(): pl.pallas_call(functools.partial(score_kernel, rows), grid_spec=pltpu.Pre...]
    unnamed x20 -> x31, local copies, waits for them, and re-layouts: 9.22 us -> 3.67 us
    reduce_sum x2 -> x5, other arithmetic: 0.52 us -> 4.27 us  [the longest x1 1.52 us: local(): slot_dst = jnp.sum(jnp.where(hit, list_at[None, :], 0), 1)]
    all_to_all x1, waiting for transfers between devices: 4.74 us -> 8.31 us  [local(): parts = lax.all_to_all(partial_scores, 'pool', 0, 0, tiled=True)]
  transfers between devices with their start and end apart: 9 -> 9, of which waited for: 7 -> 6; matrix products, arithmetic and copies ran while one was open for 11% -> 16% of each run, Pallas kernels for 0% -> 5%
where the time goes in v4:
time: 161 us; the launch traced here: 159 us
  waiting for transfers between devices  38.8 us (24%)
  Pallas kernels  33.3 us (21%)
  blocking collectives  29.7 us (18%)
  starting transfers between devices  22.7 us (14%)
  other arithmetic  12 us (7%)
  local copies, waits for them, and re-layouts  11.6 us (7%)
  matrix products  9.32 us (6%)
    all_to_all x1, blocking collectives, local(): term_parts = lax.all_to_all(terms, 'pool', 0, 0, tiled=True)  17.6 us
    pallas_call x1, Pallas kernels, local(): pl.pallas_call(functools.partial(score_kernel, rows), grid_spec=pltpu.Pre...  14.1 us
    all_to_all x1, waiting for transfers between devices, local(): lax.all_to_all(attended, 'pool', 0, 0, tiled=True)  14 us
    ppermute x3, waiting for transfers between devices, everywhere(): got = lax.ppermute(x, 'pool', [(i, i ^ k) for i in range(n)])  13.3 us
    all_to_all x1, blocking collectives, local(): all_weights = lax.all_to_all(weights, 'pool', 0, 0, tiled=True)  12.1 us
    pallas_call x1, Pallas kernels, local(): pl.pallas_call(functools.partial(value_kernel, rows), grid_spec=pltpu.Pre...  9.56 us
    all_to_all x1, waiting for transfers between devices, local(): parts = lax.all_to_all(partial_scores, 'pool', 0, 0, tiled=True)  8.31 us
    pallas_call x1, Pallas kernels, pack(): pl.pallas_call(functools.partial(pack_kernel, base), grid_spec=pltpu.Pref...  7.53 us
  transfers between devices with their start and end apart: 9, of which 6 were waited for; matrix products, arithmetic and copies ran while one was open for 16% of the time, Pallas kernels for 5%

profile of v4, /device:TPU:0, one launch (start us, length us, event | category | flops | bytes accessed | tf_op | source)
XLA Modules:
  0.0 159.0 jit_solution(12741701559361265511)
XLA Ops:
  0.0 4.0 %collective-permute-start.2 = (bf16[8,32,128]{2,1,0:T(8,128)(2,1)}, bf16[8,32,128]{2,1,0:T(8,128)(2,1)}, u32[]{:S(2)}, u32[]{:S(2)}) collective-permute-start(bf16[8,32,128]{2,1,0:T(8,128)(2,1)} %param.16), channel_id=1, source_target_pairs={{0,8},{2,10},{4,12},{6,14},{8,0},{10,2},{12,4},{14,6},{1,9},{3,11}... | collective-permute-start | bytes 196616 | tf_op jit(solution)/shard_map/ppermute | solution.py:295
  4.0 0.8 reshape.292.fill_ref
  4.8 0.1 reduce_sum.97
  4.9 0.7 reduce_max.18
  5.6 1.5 collective-permute-start.1
  7.1 0.1 pad_add_fusion.at_ref
  7.2 0.5 copy-done.12
  7.7 7.5 %pack_live_tokens.3 = bf16[8,96,1024]{2,1,0:T(8,128)(2,1)} custom-call(s32[2]{0:T(128)S(1)} %pad_add_fusion.at_ref, s32[8,32]{1,0:T(8,128)S(1)} %reshape.292.fill_ref, bf16[256,8192]{1,0:T(8,128)(2,1)} %refs_3_.1, bf16[256,8192]{1,0:T(8,128)(2,1)} %refs_3_.1, bf16[256,8192]{1,0:T(8,128)(2,1)} %refs_3_.1, bf16[256,8192]{1,0:T(8,128)(2,1)} %refs_3_.1), custom_call_target="tpu_custom_call" | custom-call | tf_op jit(solution)/shard_map/pack_live_tokens/pallas_call | solution.py:49
  15.2 4.4 %all-to-all-start.1 = ((bf16[8,96,1024]{2,1,0:T(8,128)(2,1)}), bf16[8,96,1024]{2,1,0:T(8,128)(2,1)}, u32[]{:S(2)}, u32[]{:S(2)}) async-start(bf16[8,96,1024]{2,1,0:T(8,128)(2,1)} %pack_live_tokens.3), calls=%async_computation.1 | async-start | bytes 3145728 | tf_op jit(solution)/shard_map/all_to_all | solution.py:330
  19.7 0.0 copy-start
  19.7 1.7 %fusion.23 = (bf16[1024,4,128]{2,1,0:T(4,128)(2,1)S(1)}, bf16[1024,4,128]{2,1,0:T(4,128)(2,1)}) fusion(bf16[1024,4,256]{2,1,0:T(4,128)(2,1)S(1)} %copy-done.2), kind=kLoop, calls=%fused_computation.56 | loop fusion | bytes 4194304 | tf_op jit(solution)/shard_map/slice | solution.py:388
  21.4 0.8 copy-done
  22.2 1.5 fusion.22
  23.7 0.0 copy-done.14
  23.8 0.1 iota_compare_fusion.4
  23.8 0.3 select_reduce_fusion.3
  24.1 0.6 fusion.21
  24.7 0.7 fusion.24
  25.5 0.6 multiply_add_fusion.1
  26.0 0.0 copy-done.10
  26.0 1.1 copy.54
  27.1 0.8 fusion.17
  27.9 1.5 select_reduce_fusion.1
  29.5 0.7 broadcast_add_fusion.1
  30.1 1.5 select_reduce_fusion
  31.6 0.6 broadcast_add_fusion
  32.3 0.4 fusion.1
  32.7 0.8 select_reduce_fusion.5
  33.6 0.0 collective-permute-done.1
  34.9 1.4 concatenate.49.meta_ref
  36.2 0.0 collective-permute-done.2
  36.2 1.0 maximum_select_fusion.3
  37.2 2.0 %collective-permute-start.3 = (bf16[2,8,32,128]{3,2,1,0:T(8,128)(2,1)S(1)}, bf16[2,8,32,128]{3,2,1,0:T(8,128)(2,1)S(1)}, u32[]{:S(2)}, u32[]{:S(2)}) collective-permute-start(bf16[2,8,32,128]{3,2,1,0:T(8,128)(2,1)S(1)} %maximum_select_fusion.3), channel_id=1, source_target_pairs={{0,4},{2,6},{4,0},{6,2},{8,12},{10,14},{12,8},{14,10},{1,5},{3,7},... | collective-permute-start | bytes 393224 | tf_op jit(solution)/shard_map/ppermute | solution.py:295
  39.1 1.0 fusion.26
  40.1 1.0 maximum_select_fusion.2
  41.1 6.9 %collective-permute-done.3 = bf16[2,8,32,128]{3,2,1,0:T(8,128)(2,1)S(1)} collective-permute-done((bf16[2,8,32,128]{3,2,1,0:T(8,128)(2,1)S(1)}, bf16[2,8,32,128]{3,2,1,0:T(8,128)(2,1)S(1)}, u32[]{:S(2)}, u32[]{:S(2)}) %collective-permute-start.3) | collective-permute-done | bytes 131104 | tf_op jit(solution)/shard_map/ppermute | solution.py:295
  48.0 1.4 collective-permute-start.4
  49.5 6.4 %collective-permute-done.4 = bf16[2,2,8,32,128]{4,3,2,1,0:T(8,128)(2,1)S(1)} collective-permute-done((bf16[2,2,8,32,128]{4,3,2,1,0:T(8,128)(2,1)S(1)}, bf16[2,2,8,32,128]{4,3,2,1,0:T(8,128)(2,1)S(1)}, u32[]{:S(2)}, u32[]{:S(2)}) %collective-permute-start.4) | collective-permute-done | bytes 262176 | tf_op jit(solution)/shard_map/ppermute | solution.py:295
  55.9 3.2 %convolution_convert_fusion = bf16[4,8,8,8,1024]{4,3,2,1,0:T(8,128)(2,1)} fusion(bf16[1024,4,128]{2,1,0:T(4,128)(2,1)S(1)} %copy-done.1, bf16[8,8,4,8,128]{4,3,2,1,0:T(8,128)(2,1)S(1)} %bitcast.47), kind=kOutput, calls=%fused_computation.4 | convolution fusion | flops 538968064 | bytes 5767168 | tf_op jit(solution)/shard_map/qrhgd,phd->hqrgp/dot_general | solution.py:384
  59.1 0.0 all-to-all-done.1
  59.1 0.0 collective-permute-start.5
  59.1 1.7 %conditional.1 = (bf16[256,1024]{1,0:T(8,128)(2,1)}, bf16[256,1024]{1,0:T(8,128)(2,1)}) conditional(s32[]{:T(128)} %convert_element_type.21, () %tuple.15, (s32[2]{0:T(128)S(1)}, s32[8,32]{1,0:T(8,128)S(1)}, bf16[256,8192]{1,0:T(8,128)(2,1)}) %tuple.30), branch_computations={%region_12.13_spmd, %region_13.14_spmd} | conditional | bytes 3145784 | solution.py:372
  59.2 0.9 broadcast.139
  60.0 0.9 broadcast.139.clone
  60.9 1.9 %collective-permute-done.5.other_ref = bf16[768,1024]{1,0:T(8,128)(2,1)S(1)} collective-permute-done((bf16[768,1024]{1,0:T(8,128)(2,1)}, bf16[768,1024]{1,0:T(8,128)(2,1)S(1)}, u32[]{:S(2)}, u32[]{:S(2)}) %collective-permute-start.5) | collective-permute-done | bytes 1572896 | tf_op jit(solution)/shard_map/ppermute | solution.py:414
  62.7 1.1 copy-done.3
  63.9 14.1 %prompt_scores.1 = (bf16[8,32,512]{2,1,0:T(8,128)(2,1)}, bf16[8,2,256,1024]{3,2,1,0:T(8,128)(2,1)}) custom-call(s32[1042]{0:T(1024)} %concatenate.49.meta_ref, bf16[768,1024]{1,0:T(8,128)(2,1)} %bitcast.3.mine_ref, bf16[768,1024]{1,0:T(8,128)(2,1)} %copy-done.3, bf16[256,1024]{1,0:T(8,128)(2,1)} %get-tuple-element.32.more_mine_ref, ...), custom_call_target="tpu_custom_call" | custom-call | tf_op jit(solution)/shard_map/prompt_scores/pallas_call | solution.py:420
  78.0 5.7 %all-to-all-start.2 = ((bf16[8,32,512]{2,1,0:T(8,128)(2,1)}), bf16[8,32,512]{2,1,0:T(8,128)(2,1)S(1)}, u32[]{:S(2)}, u32[]{:S(2)}) async-start(bf16[8,32,512]{2,1,0:T(8,128)(2,1)} %get-tuple-element.36), calls=%async_computation.2 | async-start | bytes 524288 | tf_op jit(solution)/shard_map/all_to_all | solution.py:449
  83.7 0.1 reshape.301.top_ref
  83.8 0.0 copy-done.5
  83.8 0.1 reshape.302.sum_ref
  83.9 0.7 dynamic-slice_bitcast_fusion.row_ref
  84.6 8.3 %all-to-all-done.2.parts_ref = bf16[8,32,512]{2,1,0:T(8,128)(2,1)S(1)} async-done(((bf16[8,32,512]{2,1,0:T(8,128)(2,1)}), bf16[8,32,512]{2,1,0:T(8,128)(2,1)S(1)}, u32[]{:S(2)}, u32[]{:S(2)}) %all-to-all-start.2) | async-done | bytes 262176 | tf_op jit(solution)/shard_map/all_to_all | solution.py:449
  92.9 1.2 softmax_weights.1
  94.1 12.1 %all_to_all.30.w_ref = bf16[8,32,512]{2,1,0:T(8,128)(2,1)} all-to-all(bf16[8,32,512]{2,1,0:T(8,128)(2,1)S(1)} %get-tuple-element.40), channel_id=1, replica_groups=mesh['groups'=2,'pool'=8,'tp'=2] {'pool'}, dimensions={0} | all-to-all | bytes 524288 | tf_op jit(solution)/shard_map/all_to_all | solution.py:467
  106.2 9.6 %weighted_values.1 = bf16[8,4,64,128]{3,2,1,0:T(8,128)(2,1)} custom-call(s32[8]{0:T(128)} %copy-done.11, bf16[8,32,512]{2,1,0:T(8,128)(2,1)} %all_to_all.30.w_ref, s32[8,1,512]{2,1,0:T(1,128)} %bitcast.57, bf16[8,2,256,1024]{3,2,1,0:T(8,128)(2,1)} %get-tuple-element.41.tile_ref, bf16[4,1024,128]{2,1,0:T(8,128)(2,1)} %bitcast.46), custom_call_target="tpu_custom_call" | custom-call | tf_op jit(solution)/shard_map/weighted_values/pallas_call | solution.py:468
  115.8 17.6 %all_to_all.31.parts_ref = bf16[8,4,64,128]{3,2,1,0:T(8,128)(2,1)S(1)} all-to-all(bf16[8,4,64,128]{3,2,1,0:T(8,128)(2,1)} %weighted_values.1), channel_id=1, replica_groups=mesh['groups'=2,'pool'=8,'tp'=2] {'pool'}, dimensions={0} | all-to-all | bytes 1048576 | tf_op jit(solution)/shard_map/all_to_all | solution.py:492
  133.3 0.9 attended_sum.1
  134.3 3.6 %all-to-all-start.5 = ((bf16[8,8,4096]{2,1,0:T(8,128)(2,1)}), bf16[8,8,4096]{2,1,0:T(8,128)(2,1)S(1)}, u32[]{:S(2)}, u32[]{:S(2)}) async-start(bf16[8,8,4096]{2,1,0:T(8,128)(2,1)} %attended_sum.1), calls=%async_computation.5 | async-start | bytes 1048576 | tf_op jit(solution)/shard_map/all_to_all | solution.py:501
  137.9 14.0 %all-to-all-done.5 = bf16[8,8,4096]{2,1,0:T(8,128)(2,1)S(1)} async-done(((bf16[8,8,4096]{2,1,0:T(8,128)(2,1)}), bf16[8,8,4096]{2,1,0:T(8,128)(2,1)S(1)}, u32[]{:S(2)}, u32[]{:S(2)}) %all-to-all-start.5) | async-done | bytes 524320 | tf_op jit(solution)/shard_map/all_to_all | solution.py:501
  151.9 4.9 %fusion.11 = f32[64,1024]{1,0:T(8,128)S(1)} fusion(bf16[4096,1024]{1,0:T(8,128)(2,1)} %param.19, bf16[8,8,4096]{2,1,0:T(8,128)(2,1)S(1)} %all-to-all-done.5), kind=kOutput, calls=%fused_computation.14 | convolution fusion | flops 536870912 | bytes 9175040 | tf_op jit(solution)/shard_map/dot_general | solution.py:502
  156.9 0.1 collective-permute-start.6
  157.0 1.3 collective-permute-done.6
  158.3 0.6 add_convert_fusion
  (29 shorter events, 0.2 us)
Async XLA Ops:
  0.0 36.2 %collective-permute-start.2 = (bf16[8,32,128]{2,1,0:T(8,128)(2,1)}, bf16[8,32,128]{2,1,0:T(8,128)(2,1)}, u32[]{:S(2)}, u32[]{:S(2)}) collective-permute-start(bf16[8,32,128]{2,1,0:T(8,128)(2,1)} %param.16), channel_id=1, source_target_pairs={{0,8},{2,10},{4,12},{6,14},{8,0},{10,2},{12,4},{14,6},{1,9},{3,11}... | collective-permute-start | bytes 196616 | tf_op jit(solution)/shard_map/ppermute | solution.py:295
  4.8 10.4 %copy-start.6 = (s32[8,32]{1,0:T(8,128)}, s32[8,32]{1,0:T(8,128)S(1)}, u32[]{:S(2)}) copy-start(s32[8,32]{1,0:T(8,128)S(1)} %reshape.292.fill_ref) | copy-start | bytes 3076
  5.6 27.9 %collective-permute-start.1 = (s32[]{:T(128)}, s32[]{:T(128)}, u32[]{:S(2)}, u32[]{:S(2)}) collective-permute-start(s32[]{:T(128)} %reduce_max.18), channel_id=1, source_target_pairs={{0,16},{16,0},{1,17},{17,1},{2,18},{18,2},{3,19},{19,3},{4,20},{20... | collective-permute-start | bytes 20 | tf_op jit(solution)/shard_map/ppermute | solution.py:359
  7.2 0.5 copy-start.12
  15.2 4.5 %copy-start.2 = (bf16[1024,4,256]{2,1,0:T(4,128)(2,1)S(1)}, bf16[1024,4,256]{2,1,0:T(4,128)(2,1)}, u32[]{:S(2)}) copy-start(bf16[1024,4,256]{2,1,0:T(4,128)(2,1)} %param.12) | copy-start | bytes 6291460
  15.2 43.9 %all-to-all-start.1 = ((bf16[8,96,1024]{2,1,0:T(8,128)(2,1)}), bf16[8,96,1024]{2,1,0:T(8,128)(2,1)}, u32[]{:S(2)}, u32[]{:S(2)}) async-start(bf16[8,96,1024]{2,1,0:T(8,128)(2,1)} %pack_live_tokens.3), calls=%async_computation.1 | async-start | bytes 3145728 | tf_op jit(solution)/shard_map/all_to_all | solution.py:330
  19.7 2.6 %copy-start = (bf16[8,256,4,256]{3,2,1,0:T(4,128)(2,1)S(1)}, bf16[8,256,4,256]{3,2,1,0:T(4,128)(2,1)}, u32[]{:S(2)}) copy-start(bf16[8,256,4,256]{3,2,1,0:T(4,128)(2,1)} %param.17) | copy-start | bytes 12582916
  22.2 1.5 copy-start.14
  22.2 1.6 %copy-start.8 = (s32[256]{0:T(256)S(1)}, s32[256]{0:T(256)}, u32[]{:S(2)}) copy-start(s32[256]{0:T(256)} %param.15) | copy-start | bytes 3076
  22.2 1.6 %copy-start.9 = (s32[256,1]{0,1:T(1,128)S(1)}, s32[256,1]{0,1:T(1,128)}, u32[]{:S(2)}) copy-start(s32[256,1]{0,1:T(1,128)} %param.13) | copy-start | bytes 3076
  22.2 2.5 %copy-start.4 = (bf16[8,32,128]{2,1,0:T(8,128)(2,1)S(1)}, bf16[8,32,128]{2,1,0:T(8,128)(2,1)}, u32[]{:S(2)}) copy-start(bf16[8,32,128]{2,1,0:T(8,128)(2,1)} %param.16) | copy-start | bytes 196612
  24.1 1.9 %copy-start.10 = (s32[256]{0:T(256)}, s32[256]{0:T(256)S(1)}, u32[]{:S(2)}) copy-start(s32[256]{0:T(256)S(1)} %get-tuple-element.48) | copy-start | bytes 3076
  27.1 28.8 %copy-start.1 = (bf16[1024,4,128]{2,1,0:T(4,128)(2,1)S(1)}, bf16[1024,4,128]{2,1,0:T(4,128)(2,1)}, u32[]{:S(2)}) copy-start(bf16[1024,4,128]{2,1,0:T(4,128)(2,1)} %get-tuple-element.56) | copy-start | bytes 3145732
  33.5 25.6 %copy-start.11 = (s32[8]{0:T(128)}, s32[8]{0:T(128)S(1)}, u32[]{:S(2)}) copy-start(s32[8]{0:T(128)S(1)} %get-tuple-element.29.size_ref) | copy-start | bytes 100
  37.2 10.8 %collective-permute-start.3 = (bf16[2,8,32,128]{3,2,1,0:T(8,128)(2,1)S(1)}, bf16[2,8,32,128]{3,2,1,0:T(8,128)(2,1)S(1)}, u32[]{:S(2)}, u32[]{:S(2)}) collective-permute-start(bf16[2,8,32,128]{3,2,1,0:T(8,128)(2,1)S(1)} %maximum_select_fusion.3), channel_id=1, source_target_pairs={{0,4},{2,6},{4,0},{6,2},{8,12},{10,14},{12,8},{14,10},{1,5},{3,7},... | collective-permute-start | bytes 393224 | tf_op jit(solution)/shard_map/ppermute | solution.py:295
  48.0 7.9 %collective-permute-start.4 = (bf16[2,2,8,32,128]{4,3,2,1,0:T(8,128)(2,1)S(1)}, bf16[2,2,8,32,128]{4,3,2,1,0:T(8,128)(2,1)S(1)}, u32[]{:S(2)}, u32[]{:S(2)}) collective-permute-start(bf16[2,2,8,32,128]{4,3,2,1,0:T(8,128)(2,1)S(1)} %maximum_select_fusion.1), channel_id=1, source_target_pairs={{0,2},{2,0},{4,6},{6,4},{8,10},{10,8},{12,14},{14,12},{1,3},{3,1},... | collective-permute-start | bytes 786440 | tf_op jit(solution)/shard_map/ppermute | solution.py:295
  49.4 9.7 %copy-start.7 = (s32[8,32]{1,0:T(8,128)S(1)}, s32[8,32]{1,0:T(8,128)}, u32[]{:S(2)}) copy-start(s32[8,32]{1,0:T(8,128)} %copy-done.6) | copy-start | bytes 3076
  49.4 9.7 %copy-start.13 = (s32[2]{0:T(128)S(1)}, s32[2]{0:T(128)}, u32[]{:S(2)}) copy-start(s32[2]{0:T(128)} %copy-done.12) | copy-start | bytes 28
  59.1 3.6 %collective-permute-start.5 = (bf16[768,1024]{1,0:T(8,128)(2,1)}, bf16[768,1024]{1,0:T(8,128)(2,1)S(1)}, u32[]{:S(2)}, u32[]{:S(2)}) collective-permute-start(bf16[768,1024]{1,0:T(8,128)(2,1)} %bitcast.3.mine_ref), channel_id=1, source_target_pairs={{0,1},{1,0},{2,3},{3,2},{4,5},{5,4},{6,7},{7,6},{8,9},{9,8},{10,11... | collective-permute-start | bytes 4718600 | tf_op jit(solution)/shard_map/ppermute | solution.py:414
  62.7 1.1 copy-start.3
  63.9 19.9 %copy-start.5 = (f32[8,4,8]{2,1,0:T(4,128)S(1)}, f32[8,4,8]{2,1,0:T(4,128)}, u32[]{:S(2)}) copy-start(f32[8,4,8]{2,1,0:T(4,128)} %fusion.17) | copy-start | bytes 3076
  78.0 14.9 %all-to-all-start.2 = ((bf16[8,32,512]{2,1,0:T(8,128)(2,1)}), bf16[8,32,512]{2,1,0:T(8,128)(2,1)S(1)}, u32[]{:S(2)}, u32[]{:S(2)}) async-start(bf16[8,32,512]{2,1,0:T(8,128)(2,1)} %get-tuple-element.36), calls=%async_computation.2 | async-start | bytes 524288 | tf_op jit(solution)/shard_map/all_to_all | solution.py:449
  134.3 17.7 %all-to-all-start.5 = ((bf16[8,8,4096]{2,1,0:T(8,128)(2,1)}), bf16[8,8,4096]{2,1,0:T(8,128)(2,1)S(1)}, u32[]{:S(2)}, u32[]{:S(2)}) async-start(bf16[8,8,4096]{2,1,0:T(8,128)(2,1)} %attended_sum.1), calls=%async_computation.5 | async-start | bytes 1048576 | tf_op jit(solution)/shard_map/all_to_all | solution.py:501
  156.9 1.4 collective-permute-start.6

commit v5 on v2

v5 whole, which is shorter than its diff:
```python
import functools

import jax
import jax.numpy as jnp
from jax import lax
from jax.experimental import pallas as pl
from jax.experimental.pallas import tpu as pltpu
from jax.sharding import PartitionSpec as P

BLK = 8
ROW = 16
MIB = 1 << 20


def pack_kernel(base, at_ref, fill_ref, dest_ref, x_ref, out_ref, held, packed, count, in_sem, out_sem):
    n, tokens, part = held.shape
    size = packed.shape[1]
    blocks = tokens // BLK

    def load(q):
        return pltpu.make_async_copy(
            x_ref.at[:, pl.ds(q * part, part)], held.at[q], in_sem.at[q]
        )

    def store(q):
        return pltpu.make_async_copy(packed.at[q], out_ref.at[q], out_sem.at[q])

    for q in range(n):
        load(q).start()
    first = at_ref[0] * blocks
    for q in range(n):
        count[q] = 0

    @pl.loop(0, blocks)
    def _(b):
        owner = dest_ref[first + b]
        count[owner] = count[owner] + fill_ref[first + b]

    def starts(q, total):
        here = count[q]
        count[q] = total
        return total + here

    lax.fori_loop(0, n, starts, jnp.int32(0))
    token = lax.broadcasted_iota(jnp.int32, (1, tokens), 1)

    def place(b, ranks):
        owner = dest_ref[first + b]
        fill = fill_ref[first + b]
        start = count[owner]
        count[owner] = start + fill
        inner = token - b * BLK
        return jnp.where((inner >= 0) & (inner < fill), start + inner, ranks)

    ranks = lax.fori_loop(0, blocks, place, jnp.full((1, tokens), -1, jnp.int32))
    wanted = base + at_ref[1] * size + lax.broadcasted_iota(jnp.int32, (size, tokens), 0)
    pick = (wanted == ranks).astype(jnp.bfloat16)
    for q in range(n):
        load(q).wait()
        packed[q] = jnp.dot(pick, held[q], preferred_element_type=jnp.float32).astype(
            packed.dtype
        )
        store(q).start()
    for q in range(n):
        store(q).wait()


def pack(x_prompt, fill, dest, at, n, base, size):
    tokens, width = x_prompt.shape
    part = width // n
    return pl.pallas_call(
        functools.partial(pack_kernel, base),
        grid_spec=pltpu.PrefetchScalarGridSpec(
            num_scalar_prefetch=3,
            grid=(1,),
            in_specs=[pl.BlockSpec(memory_space=pl.ANY)],
            out_specs=pl.BlockSpec(memory_space=pl.ANY),
            scratch_shapes=[
                pltpu.VMEM((n, tokens, part), jnp.bfloat16),
                pltpu.VMEM((n, size, part), jnp.bfloat16),
                pltpu.SMEM((n,), jnp.int32),
                pltpu.SemaphoreType.DMA((n,)),
                pltpu.SemaphoreType.DMA((n,)),
            ],
        ),
        out_shape=jax.ShapeDtypeStruct((n, size, part), jnp.bfloat16),
        compiler_params=pltpu.CompilerParams(vmem_limit_bytes=56 * MIB),
        name="pack_live_tokens",
    )(at, fill, dest, x_prompt)


def load_tokens(n, meta_ref, x_refs, x_all, sem):
    core, over = meta_ref[n * n + 1], meta_ref[n * n + 2]
    size, extra = x_refs[0].shape[0] // n, x_refs[2].shape[0] // n
    tokens = 2 * (size + extra)
    part = x_all.shape[1]

    def copies(refs, base, length):
        return [
            pltpu.make_async_copy(
                ref.at[pl.ds(s * length, length)],
                x_all.at[
                    pl.ds(
                        pl.multiple_of(
                            s * tokens + base + (core if j == 0 else 1 - core) * length, ROW
                        ),
                        length,
                    )
                ],
                sem.at[j, s],
            )
            for j, ref in enumerate(refs)
            for s in range(n)
        ]

    main = copies(x_refs[:2], 0, size)
    for copy in main:
        copy.start()
    x_all[n * tokens :, :] = jnp.zeros((x_all.shape[0] - n * tokens, part), x_all.dtype)

    @pl.when(over == 0)
    def _():
        for s in range(n):
            x_all[s * tokens + 2 * size : (s + 1) * tokens, :] = jnp.zeros(
                (2 * extra, part), x_all.dtype
            )

    for copy in main:
        copy.wait()

    @pl.when(over != 0)
    def _():
        rest = copies(x_refs[2:], 2 * size, extra)
        for copy in rest:
            copy.start()
        for copy in rest:
            copy.wait()


def cut_windows(n, q, window, meta_ref, x_all, stage):
    for s in range(n):
        start = pl.multiple_of(meta_ref[q * n + s], ROW)
        stage[s * window : (s + 1) * window, :] = x_all[pl.ds(start, window), :]


def score_kernel(n, rows, window, meta_ref, *refs):
    x_refs, (keyed_ref, row_ref), out_refs = refs[:4], refs[4:6], refs[6 : 6 + n]
    x_all, stage, sem = refs[6 + n :]
    k = pl.program_id(0)
    pl.when(k == 0)(lambda: load_tokens(n, meta_ref, x_refs, x_all, sem))
    cut_windows(n, meta_ref[n * n] ^ k, window, meta_ref, x_all, stage)
    kvh, per, part = keyed_ref.shape
    lanes = n * window
    raw = lax.dot_general(
        keyed_ref[...].reshape(kvh * per, part),
        stage[...],
        (((1,), (1,)), ((), ())),
        preferred_element_type=jnp.float32,
    ).reshape(kvh, rows, per // rows, lanes)
    owner_row = row_ref[0]
    picked = jnp.zeros((kvh, per // rows, lanes), jnp.float32)
    for r in range(rows):
        picked = picked + jnp.where((owner_row == r)[None], raw[:, r], 0.0)
    picked = picked.reshape(kvh * per // rows, lanes).astype(jnp.bfloat16)
    for j in range(n):

        @pl.when(k == j)
        def _(j=j):
            out_refs[j][...] = picked


def weight_kernel(n, scale, *refs):
    part_refs = refs[:n]
    row_ref, top_ref, sum_ref, cached_ref, w_ref, kept_ref = refs[n:]
    scores = part_refs[0][...].astype(jnp.float32)
    for ref in part_refs[1:]:
        scores = scores + ref[...].astype(jnp.float32)
    scores = scores * scale
    owner_row = row_ref[...]
    weights = jnp.zeros(scores.shape, jnp.float32)
    for r in range(top_ref.shape[0]):
        own = jnp.where(owner_row == r, scores, -jnp.inf)
        cache_top = top_ref[r]
        top = jnp.maximum(jnp.max(own, 1, keepdims=True), cache_top)
        held = jnp.exp(own - top)
        fade = jnp.exp(cache_top - top)
        total = jnp.sum(held, 1, keepdims=True) + sum_ref[r] * fade
        weights = weights + held / total
        kept_ref[r] = cached_ref[r] * (fade / total)
    w_ref[...] = weights.astype(w_ref.dtype)


def value_kernel(n, rows, window, meta_ref, *refs):
    x_refs, (row_ref, value_ref), w_refs = refs[:4], refs[4:6], refs[6 : 6 + n]
    out_refs = refs[6 + n : 6 + 2 * n]
    x_all, stage, chosen, mixed, sem = refs[6 + 2 * n :]
    k = pl.program_id(0)
    pl.when(k == 0)(lambda: load_tokens(n, meta_ref, x_refs, x_all, sem))
    for j in range(n):

        @pl.when(k == j)
        def _(j=j):
            chosen[...] = w_refs[j][...]

    cut_windows(n, meta_ref[n * n] ^ k, window, meta_ref, x_all, stage)
    kvh = value_ref.shape[0]
    heads, lanes = chosen.shape
    per = rows * heads // kvh
    weights = chosen[...].astype(jnp.float32).reshape(kvh, 1, heads // kvh, lanes)
    owner_row = row_ref[0]
    spread = jnp.concatenate(
        [jnp.where((owner_row == r)[None, None], weights, 0.0) for r in range(rows)], 1
    ).reshape(kvh * per, lanes)
    got = jnp.dot(
        spread.astype(jnp.bfloat16), stage[...], preferred_element_type=jnp.float32
    ).astype(jnp.bfloat16)
    for h in range(kvh):
        mixed[h, pl.ds(pl.multiple_of(k * per, per), per), :] = got[h * per : (h + 1) * per]

    @pl.when(k == n - 1)
    def _():
        for h in range(kvh):
            done = jnp.dot(mixed[h], value_ref[h], preferred_element_type=jnp.float32)
            done = done.astype(jnp.bfloat16)
            for j in range(n):
                out_refs[j][h] = done[j * per : (j + 1) * per]


def sum_kernel(n, *refs):
    part_refs = refs[:n]
    kept_ref, out_ref, total = refs[n:]
    kvh, per, hd = part_refs[0].shape
    rows, heads = kept_ref.shape[:2]
    group = heads // kvh
    for h in range(kvh):
        terms = part_refs[0][h].astype(jnp.float32)
        for ref in part_refs[1:]:
            terms = terms + ref[h].astype(jnp.float32)
        for r in range(rows):
            here = slice((h * rows + r) * group, (h * rows + r + 1) * group)
            total[here, :] = (
                terms[r * group : (r + 1) * group] + kept_ref[r, h * group : (h + 1) * group, :]
            )
    pieces = [
        total[pl.ds(h * per + g, rows, stride=group), :]
        for h in range(kvh)
        for g in range(group)
    ]
    out_ref[...] = jnp.concatenate(pieces, 1).astype(out_ref.dtype)


def order_kernel(n, me_ref, own_ref, got_ref, out_ref):
    rows = own_ref.shape[0] // n
    for q in range(0, n, 2):
        pair = []
        for j in range(2):
            here = pl.ds(pl.multiple_of((me_ref[0] ^ (q + j)) * rows, rows), rows)
            pair.append(own_ref[here, :] + got_ref[here, :])
        out_ref[q * rows : (q + 2) * rows, :] = jnp.concatenate(pair).astype(out_ref.dtype)


def with_partner(x, k, n):
    return lax.ppermute(x, "pool", [(i, i ^ k) for i in range(n)])


def from_all(x, n):
    order, held = [0], x[None]
    k = n // 2
    while k >= 1:
        held = jnp.concatenate([held, with_partner(held, k, n)])
        order = order + [i ^ k for i in order]
        k //= 2
    return [held[order.index(k)] for k in range(n)]


def far_first(n):
    return sorted(range(1, n), reverse=True)


def swap_parts(parts, n):
    got = [parts[0]] + [None] * (n - 1)
    for k in far_first(n):
        got[k] = with_partner(parts[k], k, n)
    return got


def local(
    x_prompt, kv_weight, block_dest, block_row, block_fill, queries, kv_cache, cache_len, out_weight
):
    n = lax.axis_size("pool")
    ntp = lax.axis_size("tp")
    me = lax.axis_index("pool").astype(jnp.int32)
    core = lax.axis_index("tp").astype(jnp.int32)
    tokens, width = x_prompt.shape
    part = width // n
    kvh = kv_weight.shape[1]
    hd = kv_weight.shape[2] // 2
    rows, heads = queries.shape[0], queries.shape[1]
    group = heads // kvh
    per = rows * group
    cache_slots = kv_cache.shape[1]
    blocks = tokens // BLK
    cap = max(2, 2 * blocks // n)
    window = cap * BLK + ROW
    lanes = n * window
    half = tokens // ntp
    scale = 1.0 / hd**0.5
    swap = [(i, (i + 1) % ntp) for i in range(ntp)]

    size = half * 3 // 4
    extra = half - size
    at = jnp.stack([me, core])
    dest = block_dest[:, 0]
    packed = pack(x_prompt, block_fill, dest, at, n, 0, size)
    mine = lax.all_to_all(packed, "pool", 0, 0, tiled=True).reshape(n * size, part)

    index = jnp.arange(n * blocks, dtype=jnp.int32)
    sender = index // blocks
    kin = sender[None, :] == sender[:, None]
    lower = kin & (dest[None, :] < dest[:, None])
    level = kin & (dest[None, :] == dest[:, None]) & (index[None, :] < index[:, None])
    before = jnp.sum(jnp.where(lower, block_fill[None, :], 0), 1)
    within = jnp.sum(jnp.where(level, block_fill[None, :], 0), 1)
    start = dest * lanes + sender * window + before % ROW + within
    spot = jnp.arange(n * lanes, dtype=jnp.int32)[:, None]
    inside = (spot >= start[None, :]) & (spot < (start + block_fill)[None, :])
    rowof = jnp.sum(jnp.where(inside, (block_row + 1)[None, :], 0), 1) - 1
    rowof = rowof.reshape(n, 1, lanes)
    pair = jnp.arange(n * n, dtype=jnp.int32)
    sooner = (sender[None, :] == (pair % n)[:, None]) & (dest[None, :] < (pair // n)[:, None])
    offset = jnp.sum(jnp.where(sooner, block_fill[None, :], 0), 1)
    starts = (pair % n) * tokens + offset // ROW * ROW

    most = jnp.max(jnp.sum(block_fill.reshape(n, blocks), 1))
    groups = lax.axis_size("groups")
    k = 1
    while k < groups:
        most = jnp.maximum(
            most, lax.ppermute(most, "groups", [(i, i ^ k) for i in range(groups)])
        )
        k *= 2
    over = most > ntp * size

    def exchange_rest():
        rest = pack(x_prompt, block_fill, dest, at, n, ntp * size, extra)
        rest = lax.all_to_all(rest, "pool", 0, 0, tiled=True).reshape(n * extra, part)
        return rest, lax.ppermute(rest, "tp", swap)

    def no_rest():
        return (jnp.zeros((n * extra, part), jnp.bfloat16),) * 2

    more_mine, more_other = lax.cond(over, exchange_rest, no_rest)
    meta = jnp.concatenate([starts, jnp.stack([me, core, over.astype(jnp.int32)])])

    allq = jnp.stack(from_all(queries, n)).reshape(n, rows, kvh, group, hd)
    keyed = jnp.einsum(
        "qrhgd,phd->hqrgp", allq, kv_weight[:, :, :hd], preferred_element_type=jnp.float32
    ).astype(jnp.bfloat16)
    keyed = keyed.reshape(kvh, n * per, part)
    values = kv_weight[:, :, hd:].transpose(1, 0, 2)

    query = queries.reshape(rows, kvh, group, hd)
    cache_scores = (
        jnp.einsum(
            "rhgd,rthd->rhgt", query, kv_cache[:, :, :, :hd], preferred_element_type=jnp.float32
        )
        * scale
    )
    cache_live = jnp.arange(cache_slots, dtype=jnp.int32)[None, :] < cache_len[:, None]
    cache_scores = jnp.where(cache_live[:, None, None, :], cache_scores, -jnp.inf)
    cache_top = jnp.max(cache_scores, -1, keepdims=True)
    cache_exp = jnp.exp(cache_scores - cache_top)
    cache_sum = jnp.sum(cache_exp, -1, keepdims=True)
    cached = jnp.einsum(
        "rhgt,rthd->rhgd",
        cache_exp.astype(jnp.bfloat16),
        kv_cache[:, :, :, hd:],
        preferred_element_type=jnp.float32,
    )
    cache_top = cache_top.reshape(rows, heads, 1)
    cache_sum = cache_sum.reshape(rows, heads, 1)
    cached = cached.reshape(rows, heads, hd)

    mine, meta, rowof, keyed, values, cache_top, cache_sum, cached = lax.optimization_barrier(
        (mine, meta, rowof, keyed, values, cache_top, cache_sum, cached)
    )
    other = lax.ppermute(mine, "tp", swap)

    anywhere = pl.BlockSpec(memory_space=pl.ANY)
    x_scratch = [
        pltpu.VMEM((n * tokens + window, part), jnp.bfloat16),
        pltpu.VMEM((lanes, part), jnp.bfloat16),
    ]
    x_parts = (mine, other, more_mine, more_other)
    row_spec = pl.BlockSpec((1, 1, lanes), lambda k, m: (m[n * n] ^ k, 0, 0))
    slot_spec = pl.BlockSpec((heads, lanes), lambda k, m: (0, 0))
    slot_shape = jax.ShapeDtypeStruct((heads, lanes), jnp.bfloat16)
    partial_scores = pl.pallas_call(
        functools.partial(score_kernel, n, rows, window),
        grid_spec=pltpu.PrefetchScalarGridSpec(
            num_scalar_prefetch=1,
            grid=(n,),
            in_specs=[
                *[anywhere] * 4,
                pl.BlockSpec((kvh, per, part), lambda k, m: (0, k, 0)),
                row_spec,
            ],
            out_specs=[slot_spec] * n,
            scratch_shapes=[*x_scratch, pltpu.SemaphoreType.DMA((ntp, n))],
        ),
        out_shape=[slot_shape] * n,
        compiler_params=pltpu.CompilerParams(vmem_limit_bytes=20 * MIB),
        name="prompt_scores",
    )(meta, *x_parts, keyed, rowof)

    parts = swap_parts(partial_scores, n)
    my_rows = lax.dynamic_index_in_dim(rowof, me, 0, keepdims=False)
    weights, kept = pl.pallas_call(
        functools.partial(weight_kernel, n, scale),
        out_shape=[slot_shape, jax.ShapeDtypeStruct((rows, heads, hd), jnp.float32)],
        compiler_params=pltpu.CompilerParams(vmem_limit_bytes=16 * MIB),
        name="softmax_weights",
    )(*parts, my_rows, cache_top, cache_sum, cached)

    all_weights = swap_parts([weights] * n, n)
    terms = pl.pallas_call(
        functools.partial(value_kernel, n, rows, window),
        grid_spec=pltpu.PrefetchScalarGridSpec(
            num_scalar_prefetch=1,
            grid=(n,),
            in_specs=[
                *[anywhere] * 4,
                row_spec,
                pl.BlockSpec((kvh, part, hd), lambda k, m: (0, 0, 0)),
                *[slot_spec] * n,
            ],
            out_specs=[pl.BlockSpec((kvh, per, hd), lambda k, m: (0, 0, 0))] * n,
            scratch_shapes=[
                *x_scratch,
                pltpu.VMEM((heads, lanes), jnp.bfloat16),
                pltpu.VMEM((kvh, n * per, part), jnp.bfloat16),
                pltpu.SemaphoreType.DMA((ntp, n)),
            ],
        ),
        out_shape=[jax.ShapeDtypeStruct((kvh, per, hd), jnp.bfloat16)] * n,
        compiler_params=pltpu.CompilerParams(vmem_limit_bytes=24 * MIB),
        name="weighted_values",
    )(meta, *x_parts, rowof, values, *all_weights)

    attended = pl.pallas_call(
        functools.partial(sum_kernel, n),
        out_shape=jax.ShapeDtypeStruct((rows, heads * hd), jnp.bfloat16),
        scratch_shapes=[pltpu.VMEM((kvh * per, hd), jnp.float32)],
        compiler_params=pltpu.CompilerParams(vmem_limit_bytes=16 * MIB),
        name="attended_sum",
    )(*swap_parts(terms, n), kept)

    everyone = jnp.concatenate(swap_parts([attended] * n, n))
    product = jnp.dot(everyone, out_weight, preferred_element_type=jnp.float32)
    cols = out_weight.shape[1] // ntp
    own = lax.dynamic_slice_in_dim(product, core * cols, cols, 1)
    away = lax.dynamic_slice_in_dim(product, (1 - core) * cols, cols, 1)
    got = lax.ppermute(away, "tp", swap)
    return pl.pallas_call(
        functools.partial(order_kernel, n),
        grid_spec=pltpu.PrefetchScalarGridSpec(
            num_scalar_prefetch=1,
            grid=(1,),
            in_specs=[pl.BlockSpec((n * rows, cols), lambda i, m: (0, 0))] * 2,
            out_specs=pl.BlockSpec((n * rows, cols), lambda i, m: (0, 0)),
        ),
        out_shape=jax.ShapeDtypeStruct((n * rows, cols), jnp.bfloat16),
        compiler_params=pltpu.CompilerParams(vmem_limit_bytes=16 * MIB),
        name="order_rows",
    )(me.reshape(1), own, got)


def solution(mesh):
    in_specs = (
        P(("groups", "pool"), None),
        P("pool", "tp", None),
        P("groups", None),
        P("groups"),
        P("groups"),
        P(("groups", "pool"), "tp", None),
        P(("groups", "pool"), None, "tp", None),
        P(("groups", "pool")),
        P("tp", "pool"),
    )
    out_specs = P("groups", ("pool", "tp"))
    return jax.shard_map(local, mesh=mesh, in_specs=in_specs, out_specs=out_specs, check_vma=False)
```

time: 174 us -> 183 us (1.052)
  starting transfers between devices: 22.5 us -> 58.1 us
  waiting for transfers between devices: 81.8 us -> 54.8 us
  blocking collectives: 17.2 us -> 0 us
  Pallas kernels: 15.9 us -> 31.1 us
    all_to_all x4 -> x1, waiting for transfers between devices: 68.5 us -> 0.01 us  [local(): lax.all_to_all(packed, 'pool', 0, 0, tiled=True).reshape(n * size, part)]
    ppermute x4 -> x33, starting transfers between devices: 4.59 us -> 50.7 us  [the longest x31 49.1 us: with_partner(): return lax.ppermute(x, 'pool', [(i, i ^ k) for i in range(n)])]
    ppermute x4 -> x33, waiting for transfers between devices: 13.3 us -> 53.2 us  [the longest x31 51.8 us: with_partner(): return lax.ppermute(x, 'pool', [(i, i ^ k) for i in range(n)])]
    all_to_all x1 -> x0, blocking collectives: 17.2 us -> none  [local(): term_parts = lax.all_to_all(terms, 'pool', 0, 0, tiled=True)]
    pallas_call x4 -> x6, Pallas kernels: 15.9 us -> 31.1 us  [the longest x1 12.7 us: local(): pl.pallas_call(functools.partial(value_kernel, n, rows, window), grid_spe...]
    all_to_all x4 -> x1, starting transfers between devices: 17.9 us -> 7.43 us  [local(): lax.all_to_all(packed, 'pool', 0, 0, tiled=True).reshape(n * size, part)]
    unnamed x20 -> x53, local copies, waits for them, and re-layouts: 9.22 us -> 14.5 us
    dot_general x1, matrix products: 1.25 us -> 4.27 us  [local(): jnp.einsum('qrhgd,phd->hqrgp', allq, kv_weight[:, :, :hd], preferred_elem...]
  transfers between devices with their start and end apart: 9 -> 35, of which waited for: 7 -> 14; matrix products, arithmetic and copies ran while one was open for 11% -> 12% of each run, Pallas kernels for 0% -> 0%
where the time goes in v5:
time: 183 us; the launch traced here: 182 us
  starting transfers between devices  58.1 us (32%)
  waiting for transfers between devices  54.8 us (30%)
  Pallas kernels  31.1 us (17%)
  local copies, waits for them, and re-layouts  22.3 us (12%)
  matrix products  10.4 us (6%)
  other arithmetic  3.49 us (2%)
    ppermute x31, waiting for transfers between devices, with_partner(): return lax.ppermute(x, 'pool', [(i, i ^ k) for i in range(n)])  51.8 us
    ppermute x31, starting transfers between devices, with_partner(): return lax.ppermute(x, 'pool', [(i, i ^ k) for i in range(n)])  49.1 us
    unnamed x53, local copies, waits for them, and re-layouts  14.5 us
    pallas_call x1, Pallas kernels, local(): pl.pallas_call(functools.partial(value_kernel, n, rows, window), grid_spe...  12.7 us
    pallas_call x1, Pallas kernels, local(): pl.pallas_call(functools.partial(score_kernel, n, rows, window), grid_spe...  11.3 us
    all_to_all x1, starting transfers between devices, local(): lax.all_to_all(packed, 'pool', 0, 0, tiled=True).reshape(n * size, part)  7.43 us
    dot_general x1, matrix products, local(): product = jnp.dot(everyone, out_weight, preferred_element_type=jnp.float32)  4.96 us
    pallas_call x1, Pallas kernels, pack(): pl.pallas_call(functools.partial(pack_kernel, base), grid_spec=pltpu.Pref...  4.38 us
  transfers between devices with their start and end apart: 35, of which 14 were waited for; matrix products, arithmetic and copies ran while one was open for 12% of the time, Pallas kernels for 0%

profile of v5, /device:TPU:0, one launch (start us, length us, event | category | flops | bytes accessed | tf_op | source)
XLA Modules:
  0.0 181.8 jit_solution(9390379119340175209)
XLA Ops:
  0.1 4.4 %pack_live_tokens.3 = bf16[8,96,1024]{2,1,0:T(8,128)(2,1)} custom-call(s32[2]{0:T(128)S(1)} %pad_add_fusion.at_ref, s32[256]{0:T(256)} %fill_ref.1, s32[256]{0:T(256)} %bitcast.67, bf16[256,8192]{1,0:T(8,128)(2,1)} %x_ref.1), custom_call_target="tpu_custom_call" | custom-call | tf_op jit(solution)/shard_map/pack_live_tokens/pallas_call | solution.py:71
  4.5 7.4 %all-to-all-start.1 = ((bf16[8,96,1024]{2,1,0:T(8,128)(2,1)}), bf16[8,96,1024]{2,1,0:T(8,128)(2,1)S(1)}, u32[]{:S(2)}, u32[]{:S(2)}) async-start(bf16[8,96,1024]{2,1,0:T(8,128)(2,1)} %pack_live_tokens.3), calls=%async_computation.1 | async-start | bytes 3145728 | tf_op jit(solution)/shard_map/all_to_all | solution.py:315
  12.1 0.6 reduce_max.18
  12.8 1.5 collective-permute-start.1
  14.3 2.9 %collective-permute-start.2 = (bf16[1,8,32,128]{3,2,1,0:T(8,128)(2,1)S(1)}, bf16[1,8,32,128]{3,2,1,0:T(8,128)(2,1)S(1)}, u32[]{:S(2)}, u32[]{:S(2)}) collective-permute-start(bf16[1,8,32,128]{3,2,1,0:T(8,128)(2,1)S(1)} %bitcast.64), channel_id=1, source_target_pairs={{0,8},{2,10},{4,12},{6,14},{8,0},{10,2},{12,4},{14,6},{1,9},{3,11}... | collective-permute-start | bytes 196616 | tf_op jit(solution)/shard_map/ppermute | solution.py:263
  18.1 1.0 select_reduce_fusion
  19.2 3.4 %fusion.33 = (bf16[1024,4,128]{2,1,0:T(4,128)(2,1)S(1)}, bf16[1024,4,128]{2,1,0:T(4,128)(2,1)}) fusion(bf16[1024,4,256]{2,1,0:T(4,128)(2,1)} %param.12), kind=kLoop, calls=%fused_computation.81 | loop fusion | bytes 4194304 | tf_op jit(solution)/shard_map/slice | solution.py:360
  22.6 1.5 fusion.32
  24.1 0.7 fusion.34
  25.6 26.2 %collective-permute-done.2 = bf16[1,8,32,128]{3,2,1,0:T(8,128)(2,1)S(1)} collective-permute-done((bf16[1,8,32,128]{3,2,1,0:T(8,128)(2,1)S(1)}, bf16[1,8,32,128]{3,2,1,0:T(8,128)(2,1)S(1)}, u32[]{:S(2)}, u32[]{:S(2)}) %collective-permute-start.2) | collective-permute-done | bytes 65568 | tf_op jit(solution)/shard_map/ppermute | solution.py:263
  51.9 1.1 copy.65
  53.3 3.5 %collective-permute-done.3 = bf16[2,8,32,128]{3,2,1,0:T(8,128)(2,1)S(1)} collective-permute-done((bf16[2,8,32,128]{3,2,1,0:T(8,128)(2,1)S(1)}, bf16[2,8,32,128]{3,2,1,0:T(8,128)(2,1)S(1)}, u32[]{:S(2)}, u32[]{:S(2)}) %collective-permute-start.3) | collective-permute-done | bytes 131104 | tf_op jit(solution)/shard_map/ppermute | solution.py:263
  56.8 0.7 pad_maximum_fusion
  57.5 1.4 collective-permute-start.4
  60.3 3.9 %collective-permute-done.4 = bf16[4,8,32,128]{3,2,1,0:T(8,128)(2,1)S(1)} collective-permute-done((bf16[4,8,32,128]{3,2,1,0:T(8,128)(2,1)}, bf16[4,8,32,128]{3,2,1,0:T(8,128)(2,1)S(1)}, u32[]{:S(2)}, u32[]{:S(2)}) %collective-permute-start.4) | collective-permute-done | bytes 262176 | tf_op jit(solution)/shard_map/ppermute | solution.py:263
  64.8 0.6 fusion.24
  65.4 0.6 fusion.23
  67.9 0.6 fusion.20
  68.5 4.3 %convolution_convert_fusion = bf16[4,8,8,8,1024]{4,3,2,1,0:T(8,128)(2,1)} fusion(bf16[1024,4,128]{2,1,0:T(4,128)(2,1)S(1)} %copy-done.13, bf16[8,8,4,8,128]{4,3,2,1,0:T(8,128)(2,1)} %fusion.20), kind=kOutput, calls=%fused_computation.4 | convolution fusion | flops 538968064 | bytes 5767168 | tf_op jit(solution)/shard_map/qrhgd,phd->hqrgp/dot_general | solution.py:356
  72.8 1.8 conditional.1
  72.8 0.9 broadcast.194
  73.7 0.9 broadcast.194.clone
  74.6 1.6 collective-permute-done.5.refs_1_
  76.2 2.2 %copy-done = bf16[4,8,8,8,1024]{4,3,2,1,0:T(8,128)(2,1)S(1)} copy-done((bf16[4,8,8,8,1024]{4,3,2,1,0:T(8,128)(2,1)S(1)}, bf16[4,8,8,8,1024]{4,3,2,1,0:T(8,128)(2,1)}, u32[]{:S(2)}) %copy-start) | copy-done | bytes 4194328
  78.4 11.3 %prompt_scores.1 = (bf16[32,640]{1,0:T(8,128)(2,1)S(1)}, bf16[32,640]{1,0:T(8,128)(2,1)S(1)}, bf16[32,640]{1,0:T(8,128)(2,1)S(1)}, bf16[32,640]{1,0:T(8,128)(2,1...) custom-call(s32[67]{0:T(128)S(1)} %pad_add_fusion.1.meta_ref, ...), custom_call_target="tpu_custom_call" | custom-call | tf_op jit(solution)/shard_map/prompt_scores/pallas_call | solution.py:398
  90.3 1.4 collective-permute-start.6
  91.7 2.0 %collective-permute-start.8 = (bf16[32,640]{1,0:T(8,128)(2,1)}, bf16[32,640]{1,0:T(8,128)(2,1)}, u32[]{:S(2)}, u32[]{:S(2)}) collective-permute-start(bf16[32,640]{1,0:T(8,128)(2,1)} %get-tuple-element.55), channel_id=1, source_target_pairs={{0,6},{2,4},{4,2},{6,0},{8,14},{10,12},{12,10},{14,8},{1,7},{3,5},... | collective-permute-start | bytes 122888 | tf_op jit(solution)/shard_map/ppermute | solution.py:263
  93.8 2.6 %collective-permute-start.9 = (bf16[32,640]{1,0:T(8,128)(2,1)}, bf16[32,640]{1,0:T(8,128)(2,1)}, u32[]{:S(2)}, u32[]{:S(2)}) collective-permute-start(bf16[32,640]{1,0:T(8,128)(2,1)} %get-tuple-element.56), channel_id=1, source_target_pairs={{0,8},{2,10},{4,12},{6,14},{8,0},{10,2},{12,4},{14,6},{1,9},{3,11}... | collective-permute-start | bytes 122888 | tf_op jit(solution)/shard_map/ppermute | solution.py:263
  96.4 1.2 collective-permute-start.10
  98.2 3.0 %collective-permute-start.11 = (bf16[32,640]{1,0:T(8,128)(2,1)}, bf16[32,640]{1,0:T(8,128)(2,1)}, u32[]{:S(2)}, u32[]{:S(2)}) collective-permute-start(bf16[32,640]{1,0:T(8,128)(2,1)} %get-tuple-element.58), channel_id=1, source_target_pairs={{0,12},{2,14},{4,8},{6,10},{8,4},{10,6},{12,0},{14,2},{1,13},{3,15... | collective-permute-start | bytes 122888 | tf_op jit(solution)/shard_map/ppermute | solution.py:263
  101.8 0.9 collective-permute-start.12
  102.9 1.4 collective-permute-done.11.refs_6_
  104.3 4.5 %collective-permute-done.12.refs_7_ = bf16[32,640]{1,0:T(8,128)(2,1)} collective-permute-done((bf16[32,640]{1,0:T(8,128)(2,1)}, bf16[32,640]{1,0:T(8,128)(2,1)}, u32[]{:S(2)}, u32[]{:S(2)}) %collective-permute-start.12) | collective-permute-done | bytes 40992 | tf_op jit(solution)/shard_map/ppermute | solution.py:263
  108.8 0.8 copy-done.7
  109.6 0.8 copy-done.9
  110.4 0.8 copy-done.11
  111.1 2.1 %softmax_weights.1 = (bf16[32,640]{1,0:T(8,128)(2,1)S(1)}, f32[8,32,128]{2,1,0:T(8,128)S(1)}) custom-call(bf16[32,640]{1,0:T(8,128)(2,1)S(1)} %copy-done.7, bf16[32,640]{1,0:T(8,128)(2,1)S(1)} %copy-done.9, bf16[32,640]{1,0:T(8,128)(2,1)S(1)} %copy-done.11, bf16[32,640]{1,0:T(8,128)(2,1)} %collective-permute-done.8.refs_3_, ...), custom_call_target="tpu_custom_call" | custom-call | tf_op jit(solution)/shard_map/softmax_weights/pallas_call | solution.py:418
  113.2 0.6 copy-done.4
  113.9 1.1 collective-permute-start.13
  115.0 2.4 %collective-permute-start.15 = (bf16[32,640]{1,0:T(8,128)(2,1)S(1)}, bf16[32,640]{1,0:T(8,128)(2,1)S(1)}, u32[]{:S(2)}, u32[]{:S(2)}) collective-permute-start(bf16[32,640]{1,0:T(8,128)(2,1)S(1)} %get-tuple-element.63.refs_6_), channel_id=1, source_target_pairs={{0,6},{2,4},{4,2},{6,0},{8,14},{10,12},{12,10},{14,8},{1,7},{3,5},... | collective-permute-start | bytes 122888 | tf_op jit(solution)/shard_map/ppermute | solution.py:263
  117.4 3.5 %collective-permute-start.17 = (bf16[32,640]{1,0:T(8,128)(2,1)S(1)}, bf16[32,640]{1,0:T(8,128)(2,1)S(1)}, u32[]{:S(2)}, u32[]{:S(2)}) collective-permute-start(bf16[32,640]{1,0:T(8,128)(2,1)S(1)} %get-tuple-element.63.refs_6_), channel_id=1, source_target_pairs={{0,10},{2,8},{4,14},{6,12},{8,2},{10,0},{12,6},{14,4},{1,11},{3,9}... | collective-permute-start | bytes 122888 | tf_op jit(solution)/shard_map/ppermute | solution.py:263
  121.2 3.8 %collective-permute-start.19 = (bf16[32,640]{1,0:T(8,128)(2,1)S(1)}, bf16[32,640]{1,0:T(8,128)(2,1)S(1)}, u32[]{:S(2)}, u32[]{:S(2)}) collective-permute-start(bf16[32,640]{1,0:T(8,128)(2,1)S(1)} %get-tuple-element.63.refs_6_), channel_id=1, source_target_pairs={{0,14},{2,12},{4,10},{6,8},{8,6},{10,4},{12,2},{14,0},{1,15},{3,13... | collective-permute-start | bytes 122888 | tf_op jit(solution)/shard_map/ppermute | solution.py:263
  125.0 1.6 collective-permute-done.18.refs_12_
  126.6 1.2 collective-permute-done.19.refs_13_
  127.9 1.2 copy-done.1
  129.1 0.7 copy-done.3
  129.8 12.7 %weighted_values.1 = (bf16[4,64,128]{2,1,0:T(8,128)(2,1)S(1)}, bf16[4,64,128]{2,1,0:T(8,128)(2,1)S(1)}, bf16[4,64,128]{2,1,0:T(8,128)(2,1)S(1)}, bf16[4,64,128]{...) custom-call(s32[67]{0:T(128)S(1)} %pad_add_fusion.1.meta_ref, ...), custom_call_target="tpu_custom_call" | custom-call | tf_op jit(solution)/shard_map/weighted_values/pallas_call | solution.py:426
  142.5 1.5 collective-permute-start.20
  144.0 2.0 %collective-permute-start.22 = (bf16[4,64,128]{2,1,0:T(8,128)(2,1)}, bf16[4,64,128]{2,1,0:T(8,128)(2,1)S(1)}, u32[]{:S(2)}, u32[]{:S(2)}) collective-permute-start(bf16[4,64,128]{2,1,0:T(8,128)(2,1)} %get-tuple-element.67), channel_id=1, source_target_pairs={{0,6},{2,4},{4,2},{6,0},{8,14},{10,12},{12,10},{14,8},{1,7},{3,5},... | collective-permute-start | bytes 196616 | tf_op jit(solution)/shard_map/ppermute | solution.py:263
  146.0 2.0 %collective-permute-start.23 = (bf16[4,64,128]{2,1,0:T(8,128)(2,1)}, bf16[4,64,128]{2,1,0:T(8,128)(2,1)S(1)}, u32[]{:S(2)}, u32[]{:S(2)}) collective-permute-start(bf16[4,64,128]{2,1,0:T(8,128)(2,1)} %get-tuple-element.68), channel_id=1, source_target_pairs={{0,8},{2,10},{4,12},{6,14},{8,0},{10,2},{12,4},{14,6},{1,9},{3,11}... | collective-permute-start | bytes 196616 | tf_op jit(solution)/shard_map/ppermute | solution.py:263
  148.1 1.8 collective-permute-start.24
  149.9 3.0 %collective-permute-start.25 = (bf16[4,64,128]{2,1,0:T(8,128)(2,1)S(1)}, bf16[4,64,128]{2,1,0:T(8,128)(2,1)S(1)}, u32[]{:S(2)}, u32[]{:S(2)}) collective-permute-start(bf16[4,64,128]{2,1,0:T(8,128)(2,1)S(1)} %get-tuple-element.70), channel_id=1, source_target_pairs={{0,12},{2,14},{4,8},{6,10},{8,4},{10,6},{12,0},{14,2},{1,13},{3,15... | collective-permute-start | bytes 196616 | tf_op jit(solution)/shard_map/ppermute | solution.py:263
  152.8 0.9 collective-permute-start.26
  154.1 2.5 %collective-permute-done.25.refs_6_ = bf16[4,64,128]{2,1,0:T(8,128)(2,1)S(1)} collective-permute-done((bf16[4,64,128]{2,1,0:T(8,128)(2,1)S(1)}, bf16[4,64,128]{2,1,0:T(8,128)(2,1)S(1)}, u32[]{:S(2)}, u32[]{:S(2)}) %collective-permute-start.25) | collective-permute-done | bytes 65568 | tf_op jit(solution)/shard_map/ppermute | solution.py:263
  156.6 3.8 %collective-permute-done.26.refs_7_ = bf16[4,64,128]{2,1,0:T(8,128)(2,1)S(1)} collective-permute-done((bf16[4,64,128]{2,1,0:T(8,128)(2,1)S(1)}, bf16[4,64,128]{2,1,0:T(8,128)(2,1)S(1)}, u32[]{:S(2)}, u32[]{:S(2)}) %collective-permute-start.26) | collective-permute-done | bytes 65568 | tf_op jit(solution)/shard_map/ppermute | solution.py:263
  160.5 1.0 collective-permute-start.27
  161.5 2.6 %collective-permute-start.29 = (bf16[8,4096]{1,0:T(8,128)(2,1)S(1)}, bf16[8,4096]{1,0:T(8,128)(2,1)S(1)}, u32[]{:S(2)}, u32[]{:S(2)}) collective-permute-start(bf16[8,4096]{1,0:T(8,128)(2,1)S(1)} %attended_sum.1), channel_id=1, source_target_pairs={{0,6},{2,4},{4,2},{6,0},{8,14},{10,12},{12,10},{14,8},{1,7},{3,5},... | collective-permute-start | bytes 196616 | tf_op jit(solution)/shard_map/ppermute | solution.py:263
  164.0 3.3 %collective-permute-start.31 = (bf16[8,4096]{1,0:T(8,128)(2,1)S(1)}, bf16[8,4096]{1,0:T(8,128)(2,1)S(1)}, u32[]{:S(2)}, u32[]{:S(2)}) collective-permute-start(bf16[8,4096]{1,0:T(8,128)(2,1)S(1)} %attended_sum.1), channel_id=1, source_target_pairs={{0,10},{2,8},{4,14},{6,12},{8,2},{10,0},{12,6},{14,4},{1,11},{3,9}... | collective-permute-start | bytes 196616 | tf_op jit(solution)/shard_map/ppermute | solution.py:263
  167.7 4.0 %collective-permute-start.33 = (bf16[8,4096]{1,0:T(8,128)(2,1)S(1)}, bf16[8,4096]{1,0:T(8,128)(2,1)S(1)}, u32[]{:S(2)}, u32[]{:S(2)}) collective-permute-start(bf16[8,4096]{1,0:T(8,128)(2,1)S(1)} %attended_sum.1), channel_id=1, source_target_pairs={{0,14},{2,12},{4,10},{6,8},{8,6},{10,4},{12,2},{14,0},{1,15},{3,13... | collective-permute-start | bytes 196616 | tf_op jit(solution)/shard_map/ppermute | solution.py:263
  171.8 1.5 collective-permute-done.32
  173.4 1.4 collective-permute-done.33
  174.8 5.0 %fusion.35 = f32[64,1024]{1,0:T(8,128)S(1)} fusion(bf16[64,4096]{1,0:T(8,128)(2,1)S(1)} %constant_dynamic-update-slice_fusion, bf16[4096,1024]{1,0:T(8,128)(2,1)} %param.19), kind=kOutput, calls=%fused_computation.83 | convolution fusion | flops 536870912 | bytes 9175040 | tf_op jit(solution)/shard_map/dot_general | solution.py:459
  179.8 1.3 collective-permute-done.34.got_ref
  181.2 0.6 order_rows.1
  (100 shorter events, 8.6 us)
Async XLA Ops:
  4.5 7.5 %copy-start.15 = (s32[256]{0:T(256)S(1)}, s32[256]{0:T(256)}, u32[]{:S(2)}) copy-start(s32[256]{0:T(256)} %fill_ref.1) | copy-start | bytes 3076
  4.5 9.8 %copy-start.14 = (bf16[8,32,128]{2,1,0:T(8,128)(2,1)S(1)}, bf16[8,32,128]{2,1,0:T(8,128)(2,1)}, u32[]{:S(2)}) copy-start(bf16[8,32,128]{2,1,0:T(8,128)(2,1)} %param.16) | copy-start | bytes 196612
  4.5 13.3 %copy-start.17 = (s32[256]{0:T(256)S(1)}, s32[256]{0:T(256)}, u32[]{:S(2)}) copy-start(s32[256]{0:T(256)} %param.14) | copy-start | bytes 3076
  4.5 13.3 %copy-start.16 = (s32[256,1]{0,1:T(1,128)S(1)}, s32[256,1]{0,1:T(1,128)}, u32[]{:S(2)}) copy-start(s32[256,1]{0,1:T(1,128)} %param.13) | copy-start | bytes 3076
  4.5 68.3 %all-to-all-start.1 = ((bf16[8,96,1024]{2,1,0:T(8,128)(2,1)}), bf16[8,96,1024]{2,1,0:T(8,128)(2,1)S(1)}, u32[]{:S(2)}, u32[]{:S(2)}) async-start(bf16[8,96,1024]{2,1,0:T(8,128)(2,1)} %pack_live_tokens.3), calls=%async_computation.1 | async-start | bytes 3145728 | tf_op jit(solution)/shard_map/all_to_all | solution.py:315
  12.8 46.2 %collective-permute-start.1 = (s32[]{:T(128)}, s32[]{:T(128)}, u32[]{:S(2)}, u32[]{:S(2)}) collective-permute-start(s32[]{:T(128)} %reduce_max.18), channel_id=1, source_target_pairs={{0,16},{16,0},{1,17},{17,1},{2,18},{18,2},{3,19},{19,3},{4,20},{20... | collective-permute-start | bytes 20 | tf_op jit(solution)/shard_map/ppermute | solution.py:339
  14.3 37.5 %collective-permute-start.2 = (bf16[1,8,32,128]{3,2,1,0:T(8,128)(2,1)S(1)}, bf16[1,8,32,128]{3,2,1,0:T(8,128)(2,1)S(1)}, u32[]{:S(2)}, u32[]{:S(2)}) collective-permute-start(bf16[1,8,32,128]{3,2,1,0:T(8,128)(2,1)S(1)} %bitcast.64), channel_id=1, source_target_pairs={{0,8},{2,10},{4,12},{6,14},{8,0},{10,2},{12,4},{14,6},{1,9},{3,11}... | collective-permute-start | bytes 196616 | tf_op jit(solution)/shard_map/ppermute | solution.py:263
  19.2 83.5 %copy-start.2 = (s32[5120]{0:T(1024)}, s32[5120]{0:T(1024)S(1)}, u32[]{:S(2)}) copy-start(s32[5120]{0:T(1024)S(1)} %broadcast_add_fusion) | copy-start | bytes 61444
  19.2 3.4 %copy-start.12 = (bf16[8,256,4,256]{3,2,1,0:T(4,128)(2,1)S(1)}, bf16[8,256,4,256]{3,2,1,0:T(4,128)(2,1)}, u32[]{:S(2)}) copy-start(bf16[8,256,4,256]{3,2,1,0:T(4,128)(2,1)} %param.17) | copy-start | bytes 12582916
  22.6 1.5 copy-start.18
  51.8 5.0 %collective-permute-start.3 = (bf16[2,8,32,128]{3,2,1,0:T(8,128)(2,1)S(1)}, bf16[2,8,32,128]{3,2,1,0:T(8,128)(2,1)S(1)}, u32[]{:S(2)}, u32[]{:S(2)}) collective-permute-start(bf16[2,8,32,128]{3,2,1,0:T(8,128)(2,1)S(1)} %pad_maximum_fusion.1), channel_id=1, source_target_pairs={{0,4},{2,6},{4,0},{6,2},{8,12},{10,14},{12,8},{14,10},{1,5},{3,7},... | collective-permute-start | bytes 393224 | tf_op jit(solution)/shard_map/ppermute | solution.py:263
  53.1 15.5 %copy-start.13 = (bf16[1024,4,128]{2,1,0:T(4,128)(2,1)S(1)}, bf16[1024,4,128]{2,1,0:T(4,128)(2,1)}, u32[]{:S(2)}) copy-start(bf16[1024,4,128]{2,1,0:T(4,128)(2,1)} %get-tuple-element.80) | copy-start | bytes 3145732
  57.5 6.6 %collective-permute-start.4 = (bf16[4,8,32,128]{3,2,1,0:T(8,128)(2,1)}, bf16[4,8,32,128]{3,2,1,0:T(8,128)(2,1)S(1)}, u32[]{:S(2)}, u32[]{:S(2)}) collective-permute-start(bf16[4,8,32,128]{3,2,1,0:T(8,128)(2,1)} %pad_maximum_fusion), channel_id=1, source_target_pairs={{0,2},{2,0},{4,6},{6,4},{8,10},{10,8},{12,14},{14,12},{1,3},{3,1},... | collective-permute-start | bytes 786440 | tf_op jit(solution)/shard_map/ppermute | solution.py:263
  72.8 3.4 %collective-permute-start.5 = (bf16[768,1024]{1,0:T(8,128)(2,1)S(1)}, bf16[768,1024]{1,0:T(8,128)(2,1)S(1)}, u32[]{:S(2)}, u32[]{:S(2)}) collective-permute-start(bf16[768,1024]{1,0:T(8,128)(2,1)S(1)} %bitcast.57), channel_id=1, source_target_pairs={{0,1},{1,0},{2,3},{3,2},{4,5},{5,4},{6,7},{7,6},{8,9},{9,8},{10,11... | collective-permute-start | bytes 4718600 | tf_op jit(solution)/shard_map/ppermute | solution.py:387
  76.2 2.2 %copy-start = (bf16[4,8,8,8,1024]{4,3,2,1,0:T(8,128)(2,1)S(1)}, bf16[4,8,8,8,1024]{4,3,2,1,0:T(8,128)(2,1)}, u32[]{:S(2)}) copy-start(bf16[4,8,8,8,1024]{4,3,2,1,0:T(8,128)(2,1)} %convolution_convert_fusion) | copy-start | bytes 12582916
  89.7 0.6 copy-start.6
  90.3 7.3 %collective-permute-start.6 = (bf16[32,640]{1,0:T(8,128)(2,1)S(1)}, bf16[32,640]{1,0:T(8,128)(2,1)S(1)}, u32[]{:S(2)}, u32[]{:S(2)}) collective-permute-start(bf16[32,640]{1,0:T(8,128)(2,1)S(1)} %get-tuple-element.53), channel_id=1, source_target_pairs={{0,2},{2,0},{4,6},{6,4},{8,10},{10,8},{12,14},{14,12},{1,3},{3,1},... | collective-permute-start | bytes 122888 | tf_op jit(solution)/shard_map/ppermute | solution.py:263
  91.7 9.4 %collective-permute-start.7 = (bf16[32,640]{1,0:T(8,128)(2,1)S(1)}, bf16[32,640]{1,0:T(8,128)(2,1)S(1)}, u32[]{:S(2)}, u32[]{:S(2)}) collective-permute-start(bf16[32,640]{1,0:T(8,128)(2,1)S(1)} %get-tuple-element.54), channel_id=1, source_target_pairs={{0,4},{2,6},{4,0},{6,2},{8,12},{10,14},{12,8},{14,10},{1,5},{3,7},... | collective-permute-start | bytes 122888 | tf_op jit(solution)/shard_map/ppermute | solution.py:263
  91.7 11.2 %collective-permute-start.8 = (bf16[32,640]{1,0:T(8,128)(2,1)}, bf16[32,640]{1,0:T(8,128)(2,1)}, u32[]{:S(2)}, u32[]{:S(2)}) collective-permute-start(bf16[32,640]{1,0:T(8,128)(2,1)} %get-tuple-element.55), channel_id=1, source_target_pairs={{0,6},{2,4},{4,2},{6,0},{8,14},{10,12},{12,10},{14,8},{1,7},{3,5},... | collective-permute-start | bytes 122888 | tf_op jit(solution)/shard_map/ppermute | solution.py:263
  93.8 9.2 %collective-permute-start.9 = (bf16[32,640]{1,0:T(8,128)(2,1)}, bf16[32,640]{1,0:T(8,128)(2,1)}, u32[]{:S(2)}, u32[]{:S(2)}) collective-permute-start(bf16[32,640]{1,0:T(8,128)(2,1)} %get-tuple-element.56), channel_id=1, source_target_pairs={{0,8},{2,10},{4,12},{6,14},{8,0},{10,2},{12,4},{14,6},{1,9},{3,11}... | collective-permute-start | bytes 122888 | tf_op jit(solution)/shard_map/ppermute | solution.py:263
  96.4 6.5 %collective-permute-start.10 = (bf16[32,640]{1,0:T(8,128)(2,1)}, bf16[32,640]{1,0:T(8,128)(2,1)}, u32[]{:S(2)}, u32[]{:S(2)}) collective-permute-start(bf16[32,640]{1,0:T(8,128)(2,1)} %get-tuple-element.57), channel_id=1, source_target_pairs={{0,10},{2,8},{4,14},{6,12},{8,2},{10,0},{12,6},{14,4},{1,11},{3,9}... | collective-permute-start | bytes 122888 | tf_op jit(solution)/shard_map/ppermute | solution.py:263
  97.6 0.6 copy-start.8
  98.2 6.1 %collective-permute-start.11 = (bf16[32,640]{1,0:T(8,128)(2,1)}, bf16[32,640]{1,0:T(8,128)(2,1)}, u32[]{:S(2)}, u32[]{:S(2)}) collective-permute-start(bf16[32,640]{1,0:T(8,128)(2,1)} %get-tuple-element.58), channel_id=1, source_target_pairs={{0,12},{2,14},{4,8},{6,10},{8,4},{10,6},{12,0},{14,2},{1,13},{3,15... | collective-permute-start | bytes 122888 | tf_op jit(solution)/shard_map/ppermute | solution.py:263
  101.2 0.6 copy-start.10
  101.8 7.0 %collective-permute-start.12 = (bf16[32,640]{1,0:T(8,128)(2,1)}, bf16[32,640]{1,0:T(8,128)(2,1)}, u32[]{:S(2)}, u32[]{:S(2)}) collective-permute-start(bf16[32,640]{1,0:T(8,128)(2,1)} %get-tuple-element.59), channel_id=1, source_target_pairs={{0,14},{2,12},{4,10},{6,8},{8,6},{10,4},{12,2},{14,0},{1,15},{3,13... | collective-permute-start | bytes 122888 | tf_op jit(solution)/shard_map/ppermute | solution.py:263
  108.8 0.8 copy-start.7
  109.6 0.8 copy-start.9
  110.4 0.8 copy-start.11
  113.2 0.7 copy-start.4
  113.9 7.0 %collective-permute-start.13 = (bf16[32,640]{1,0:T(8,128)(2,1)S(1)}, bf16[32,640]{1,0:T(8,128)(2,1)S(1)}, u32[]{:S(2)}, u32[]{:S(2)}) collective-permute-start(bf16[32,640]{1,0:T(8,128)(2,1)S(1)} %get-tuple-element.63.refs_6_), channel_id=1, source_target_pairs={{0,2},{2,0},{4,6},{6,4},{8,10},{10,8},{12,14},{14,12},{1,3},{3,1},... | collective-permute-start | bytes 122888 | tf_op jit(solution)/shard_map/ppermute | solution.py:263
  115.0 6.2 %collective-permute-start.14 = (bf16[32,640]{1,0:T(8,128)(2,1)S(1)}, bf16[32,640]{1,0:T(8,128)(2,1)S(1)}, u32[]{:S(2)}, u32[]{:S(2)}) collective-permute-start(bf16[32,640]{1,0:T(8,128)(2,1)S(1)} %get-tuple-element.63.refs_6_), channel_id=1, source_target_pairs={{0,4},{2,6},{4,0},{6,2},{8,12},{10,14},{12,8},{14,10},{1,5},{3,7},... | collective-permute-start | bytes 122888 | tf_op jit(solution)/shard_map/ppermute | solution.py:263
  115.0 10.0 %collective-permute-start.15 = (bf16[32,640]{1,0:T(8,128)(2,1)S(1)}, bf16[32,640]{1,0:T(8,128)(2,1)S(1)}, u32[]{:S(2)}, u32[]{:S(2)}) collective-permute-start(bf16[32,640]{1,0:T(8,128)(2,1)S(1)} %get-tuple-element.63.refs_6_), channel_id=1, source_target_pairs={{0,6},{2,4},{4,2},{6,0},{8,14},{10,12},{12,10},{14,8},{1,7},{3,5},... | collective-permute-start | bytes 122888 | tf_op jit(solution)/shard_map/ppermute | solution.py:263
  117.4 7.7 %collective-permute-start.16 = (bf16[32,640]{1,0:T(8,128)(2,1)S(1)}, bf16[32,640]{1,0:T(8,128)(2,1)S(1)}, u32[]{:S(2)}, u32[]{:S(2)}) collective-permute-start(bf16[32,640]{1,0:T(8,128)(2,1)S(1)} %get-tuple-element.63.refs_6_), channel_id=1, source_target_pairs={{0,8},{2,10},{4,12},{6,14},{8,0},{10,2},{12,4},{14,6},{1,9},{3,11}... | collective-permute-start | bytes 122888 | tf_op jit(solution)/shard_map/ppermute | solution.py:263
  117.4 7.7 %collective-permute-start.17 = (bf16[32,640]{1,0:T(8,128)(2,1)S(1)}, bf16[32,640]{1,0:T(8,128)(2,1)S(1)}, u32[]{:S(2)}, u32[]{:S(2)}) collective-permute-start(bf16[32,640]{1,0:T(8,128)(2,1)S(1)} %get-tuple-element.63.refs_6_), channel_id=1, source_target_pairs={{0,10},{2,8},{4,14},{6,12},{8,2},{10,0},{12,6},{14,4},{1,11},{3,9}... | collective-permute-start | bytes 122888 | tf_op jit(solution)/shard_map/ppermute | solution.py:263
  120.8 5.8 %collective-permute-start.18 = (bf16[32,640]{1,0:T(8,128)(2,1)S(1)}, bf16[32,640]{1,0:T(8,128)(2,1)S(1)}, u32[]{:S(2)}, u32[]{:S(2)}) collective-permute-start(bf16[32,640]{1,0:T(8,128)(2,1)S(1)} %get-tuple-element.63.refs_6_), channel_id=1, source_target_pairs={{0,12},{2,14},{4,8},{6,10},{8,4},{10,6},{12,0},{14,2},{1,13},{3,15... | collective-permute-start | bytes 122888 | tf_op jit(solution)/shard_map/ppermute | solution.py:263
  121.2 6.7 %collective-permute-start.19 = (bf16[32,640]{1,0:T(8,128)(2,1)S(1)}, bf16[32,640]{1,0:T(8,128)(2,1)S(1)}, u32[]{:S(2)}, u32[]{:S(2)}) collective-permute-start(bf16[32,640]{1,0:T(8,128)(2,1)S(1)} %get-tuple-element.63.refs_6_), channel_id=1, source_target_pairs={{0,14},{2,12},{4,10},{6,8},{8,6},{10,4},{12,2},{14,0},{1,15},{3,13... | collective-permute-start | bytes 122888 | tf_op jit(solution)/shard_map/ppermute | solution.py:263
  127.9 1.2 copy-start.1
  129.1 0.7 copy-start.3
  129.8 30.6 %copy-start.5 = (f32[8,32,128]{2,1,0:T(8,128)S(1)}, f32[8,32,128]{2,1,0:T(8,128)}, u32[]{:S(2)}) copy-start(f32[8,32,128]{2,1,0:T(8,128)} %copy-done.4) | copy-start | bytes 393220
  142.5 7.4 %collective-permute-start.20 = (bf16[4,64,128]{2,1,0:T(8,128)(2,1)S(1)}, bf16[4,64,128]{2,1,0:T(8,128)(2,1)S(1)}, u32[]{:S(2)}, u32[]{:S(2)}) collective-permute-start(bf16[4,64,128]{2,1,0:T(8,128)(2,1)S(1)} %get-tuple-element.65), channel_id=1, source_target_pairs={{0,2},{2,0},{4,6},{6,4},{8,10},{10,8},{12,14},{14,12},{1,3},{3,1},... | collective-permute-start | bytes 196616 | tf_op jit(solution)/shard_map/ppermute | solution.py:263
  144.0 8.8 %collective-permute-start.21 = (bf16[4,64,128]{2,1,0:T(8,128)(2,1)S(1)}, bf16[4,64,128]{2,1,0:T(8,128)(2,1)S(1)}, u32[]{:S(2)}, u32[]{:S(2)}) collective-permute-start(bf16[4,64,128]{2,1,0:T(8,128)(2,1)S(1)} %get-tuple-element.66), channel_id=1, source_target_pairs={{0,4},{2,6},{4,0},{6,2},{8,12},{10,14},{12,8},{14,10},{1,5},{3,7},... | collective-permute-start | bytes 196616 | tf_op jit(solution)/shard_map/ppermute | solution.py:263
  144.0 9.7 %collective-permute-start.22 = (bf16[4,64,128]{2,1,0:T(8,128)(2,1)}, bf16[4,64,128]{2,1,0:T(8,128)(2,1)S(1)}, u32[]{:S(2)}, u32[]{:S(2)}) collective-permute-start(bf16[4,64,128]{2,1,0:T(8,128)(2,1)} %get-tuple-element.67), channel_id=1, source_target_pairs={{0,6},{2,4},{4,2},{6,0},{8,14},{10,12},{12,10},{14,8},{1,7},{3,5},... | collective-permute-start | bytes 196616 | tf_op jit(solution)/shard_map/ppermute | solution.py:263
  146.0 7.7 %collective-permute-start.23 = (bf16[4,64,128]{2,1,0:T(8,128)(2,1)}, bf16[4,64,128]{2,1,0:T(8,128)(2,1)S(1)}, u32[]{:S(2)}, u32[]{:S(2)}) collective-permute-start(bf16[4,64,128]{2,1,0:T(8,128)(2,1)} %get-tuple-element.68), channel_id=1, source_target_pairs={{0,8},{2,10},{4,12},{6,14},{8,0},{10,2},{12,4},{14,6},{1,9},{3,11}... | collective-permute-start | bytes 196616 | tf_op jit(solution)/shard_map/ppermute | solution.py:263
  148.1 6.1 %collective-permute-start.24 = (bf16[4,64,128]{2,1,0:T(8,128)(2,1)S(1)}, bf16[4,64,128]{2,1,0:T(8,128)(2,1)S(1)}, u32[]{:S(2)}, u32[]{:S(2)}) collective-permute-start(bf16[4,64,128]{2,1,0:T(8,128)(2,1)S(1)} %get-tuple-element.69), channel_id=1, source_target_pairs={{0,10},{2,8},{4,14},{6,12},{8,2},{10,0},{12,6},{14,4},{1,11},{3,9}... | collective-permute-start | bytes 196616 | tf_op jit(solution)/shard_map/ppermute | solution.py:263
  149.9 6.8 %collective-permute-start.25 = (bf16[4,64,128]{2,1,0:T(8,128)(2,1)S(1)}, bf16[4,64,128]{2,1,0:T(8,128)(2,1)S(1)}, u32[]{:S(2)}, u32[]{:S(2)}) collective-permute-start(bf16[4,64,128]{2,1,0:T(8,128)(2,1)S(1)} %get-tuple-element.70), channel_id=1, source_target_pairs={{0,12},{2,14},{4,8},{6,10},{8,4},{10,6},{12,0},{14,2},{1,13},{3,15... | collective-permute-start | bytes 196616 | tf_op jit(solution)/shard_map/ppermute | solution.py:263
  152.8 7.6 %collective-permute-start.26 = (bf16[4,64,128]{2,1,0:T(8,128)(2,1)S(1)}, bf16[4,64,128]{2,1,0:T(8,128)(2,1)S(1)}, u32[]{:S(2)}, u32[]{:S(2)}) collective-permute-start(bf16[4,64,128]{2,1,0:T(8,128)(2,1)S(1)} %get-tuple-element.71), channel_id=1, source_target_pairs={{0,14},{2,12},{4,10},{6,8},{8,6},{10,4},{12,2},{14,0},{1,15},{3,13... | collective-permute-start | bytes 196616 | tf_op jit(solution)/shard_map/ppermute | solution.py:263
  160.5 6.8 %collective-permute-start.27 = (bf16[8,4096]{1,0:T(8,128)(2,1)S(1)}, bf16[8,4096]{1,0:T(8,128)(2,1)S(1)}, u32[]{:S(2)}, u32[]{:S(2)}) collective-permute-start(bf16[8,4096]{1,0:T(8,128)(2,1)S(1)} %attended_sum.1), channel_id=1, source_target_pairs={{0,2},{2,0},{4,6},{6,4},{8,10},{10,8},{12,14},{14,12},{1,3},{3,1},... | collective-permute-start | bytes 196616 | tf_op jit(solution)/shard_map/ppermute | solution.py:263
  161.5 6.3 %collective-permute-start.28 = (bf16[8,4096]{1,0:T(8,128)(2,1)S(1)}, bf16[8,4096]{1,0:T(8,128)(2,1)S(1)}, u32[]{:S(2)}, u32[]{:S(2)}) collective-permute-start(bf16[8,4096]{1,0:T(8,128)(2,1)S(1)} %attended_sum.1), channel_id=1, source_target_pairs={{0,4},{2,6},{4,0},{6,2},{8,12},{10,14},{12,8},{14,10},{1,5},{3,7},... | collective-permute-start | bytes 196616 | tf_op jit(solution)/shard_map/ppermute | solution.py:263
  161.5 10.3 %collective-permute-start.29 = (bf16[8,4096]{1,0:T(8,128)(2,1)S(1)}, bf16[8,4096]{1,0:T(8,128)(2,1)S(1)}, u32[]{:S(2)}, u32[]{:S(2)}) collective-permute-start(bf16[8,4096]{1,0:T(8,128)(2,1)S(1)} %attended_sum.1), channel_id=1, source_target_pairs={{0,6},{2,4},{4,2},{6,0},{8,14},{10,12},{12,10},{14,8},{1,7},{3,5},... | collective-permute-start | bytes 196616 | tf_op jit(solution)/shard_map/ppermute | solution.py:263
  164.0 7.8 %collective-permute-start.30 = (bf16[8,4096]{1,0:T(8,128)(2,1)S(1)}, bf16[8,4096]{1,0:T(8,128)(2,1)S(1)}, u32[]{:S(2)}, u32[]{:S(2)}) collective-permute-start(bf16[8,4096]{1,0:T(8,128)(2,1)S(1)} %attended_sum.1), channel_id=1, source_target_pairs={{0,8},{2,10},{4,12},{6,14},{8,0},{10,2},{12,4},{14,6},{1,9},{3,11}... | collective-permute-start | bytes 196616 | tf_op jit(solution)/shard_map/ppermute | solution.py:263
  164.0 7.8 %collective-permute-start.31 = (bf16[8,4096]{1,0:T(8,128)(2,1)S(1)}, bf16[8,4096]{1,0:T(8,128)(2,1)S(1)}, u32[]{:S(2)}, u32[]{:S(2)}) collective-permute-start(bf16[8,4096]{1,0:T(8,128)(2,1)S(1)} %attended_sum.1), channel_id=1, source_target_pairs={{0,10},{2,8},{4,14},{6,12},{8,2},{10,0},{12,6},{14,4},{1,11},{3,9}... | collective-permute-start | bytes 196616 | tf_op jit(solution)/shard_map/ppermute | solution.py:263
  167.3 6.1 %collective-permute-start.32 = (bf16[8,4096]{1,0:T(8,128)(2,1)S(1)}, bf16[8,4096]{1,0:T(8,128)(2,1)S(1)}, u32[]{:S(2)}, u32[]{:S(2)}) collective-permute-start(bf16[8,4096]{1,0:T(8,128)(2,1)S(1)} %attended_sum.1), channel_id=1, source_target_pairs={{0,12},{2,14},{4,8},{6,10},{8,4},{10,6},{12,0},{14,2},{1,13},{3,15... | collective-permute-start | bytes 196616 | tf_op jit(solution)/shard_map/ppermute | solution.py:263
  167.7 7.0 %collective-permute-start.33 = (bf16[8,4096]{1,0:T(8,128)(2,1)S(1)}, bf16[8,4096]{1,0:T(8,128)(2,1)S(1)}, u32[]{:S(2)}, u32[]{:S(2)}) collective-permute-start(bf16[8,4096]{1,0:T(8,128)(2,1)S(1)} %attended_sum.1), channel_id=1, source_target_pairs={{0,14},{2,12},{4,10},{6,8},{8,6},{10,4},{12,2},{14,0},{1,15},{3,13... | collective-permute-start | bytes 196616 | tf_op jit(solution)/shard_map/ppermute | solution.py:263
  179.8 1.4 collective-permute-start.34

commit v6 on v5

v6 whole, which is shorter than its diff:
```python
import functools

import jax
import jax.numpy as jnp
from jax import lax
from jax.experimental import pallas as pl
from jax.experimental.pallas import tpu as pltpu
from jax.sharding import PartitionSpec as P

BLK = 8
MIB = 1 << 20


def pack_kernel(base, at_ref, fill_ref, dest_ref, x_ref, out_ref, held, packed, count, in_sem, out_sem):
    n, tokens, part = held.shape
    size = packed.shape[1]
    blocks = tokens // BLK

    def load(q):
        return pltpu.make_async_copy(
            x_ref.at[:, pl.ds(q * part, part)], held.at[q], in_sem.at[q]
        )

    def store(q):
        return pltpu.make_async_copy(packed.at[q], out_ref.at[q], out_sem.at[q])

    for q in range(n):
        load(q).start()
    first = at_ref[0] * blocks
    for q in range(n):
        count[q] = 0

    @pl.loop(0, blocks)
    def _(b):
        owner = dest_ref[first + b]
        count[owner] = count[owner] + fill_ref[first + b]

    def starts(q, total):
        here = count[q]
        count[q] = total
        return total + here

    lax.fori_loop(0, n, starts, jnp.int32(0))
    token = lax.broadcasted_iota(jnp.int32, (1, tokens), 1)

    def place(b, ranks):
        owner = dest_ref[first + b]
        fill = fill_ref[first + b]
        start = count[owner]
        count[owner] = start + fill
        inner = token - b * BLK
        return jnp.where((inner >= 0) & (inner < fill), start + inner, ranks)

    ranks = lax.fori_loop(0, blocks, place, jnp.full((1, tokens), -1, jnp.int32))
    wanted = base + at_ref[1] * size + lax.broadcasted_iota(jnp.int32, (size, tokens), 0)
    pick = (wanted == ranks).astype(jnp.bfloat16)
    for q in range(n):
        load(q).wait()
        packed[q] = jnp.dot(pick, held[q], preferred_element_type=jnp.float32).astype(
            packed.dtype
        )
        store(q).start()
    for q in range(n):
        store(q).wait()


def pack(x_prompt, fill, dest, at, n, base, size):
    tokens, width = x_prompt.shape
    part = width // n
    return pl.pallas_call(
        functools.partial(pack_kernel, base),
        grid_spec=pltpu.PrefetchScalarGridSpec(
            num_scalar_prefetch=3,
            grid=(1,),
            in_specs=[pl.BlockSpec(memory_space=pl.ANY)],
            out_specs=pl.BlockSpec(memory_space=pl.ANY),
            scratch_shapes=[
                pltpu.VMEM((n, tokens, part), jnp.bfloat16),
                pltpu.VMEM((n, size, part), jnp.bfloat16),
                pltpu.SMEM((n,), jnp.int32),
                pltpu.SemaphoreType.DMA((n,)),
                pltpu.SemaphoreType.DMA((n,)),
            ],
        ),
        out_shape=jax.ShapeDtypeStruct((n, size, part), jnp.bfloat16),
        compiler_params=pltpu.CompilerParams(vmem_limit_bytes=56 * MIB),
        name="pack_live_tokens",
    )(at, fill, dest, x_prompt)


def tile_cuts(lanes):
    return [0] + list(range(min(256, lanes), lanes, 128)) + [lanes]


def load_tokens(n, core, over, x_refs, held, more, wide, sem):
    size, extra = held.shape[1] // n, more.shape[1] // n
    tokens = 2 * (size + extra)
    part = wide.shape[1]
    cuts = sem.shape[1]

    def copies(refs, buffer):
        span = buffer.shape[1] // cuts
        return [
            [
                pltpu.make_async_copy(
                    ref.at[pl.ds(i * span, span)], buffer.at[j, pl.ds(i * span, span)], sem.at[j, i]
                )
                for j, ref in enumerate(refs)
            ]
            for i in range(cuts)
        ]

    def widen(buffer, base, first, last):
        length = buffer.shape[1] // n

        @pl.loop(first, last)
        def _(s):
            for j in range(2):
                side = core if j == 0 else 1 - core
                to = pl.multiple_of(s * tokens + base + side * length, BLK)
                wide[pl.ds(to, length), :] = buffer[
                    j, pl.ds(pl.multiple_of(s * length, length), length), :
                ].astype(wide.dtype)

    main = copies(x_refs[:2], held)
    for pair in main:
        for copy in pair:
            copy.start()

    @pl.loop(0, n)
    def _(s):
        at = pl.multiple_of(s * tokens + 2 * size, BLK)
        wide[pl.ds(at, 2 * extra), :] = jnp.zeros((2 * extra, part), wide.dtype)

    wide[n * tokens :, :] = jnp.zeros((wide.shape[0] - n * tokens, part), wide.dtype)
    for i, pair in enumerate(main):
        for copy in pair:
            copy.wait()
        widen(held, 0, i * n // cuts, (i + 1) * n // cuts)

    @pl.when(over != 0)
    def _():
        rest = copies(x_refs[2:], more)
        for pair in rest:
            for copy in pair:
                copy.start()
        for pair in rest:
            for copy in pair:
                copy.wait()
        widen(more, 2 * size, 0, n)


def score_kernel(n, rows, window, meta_ref, *refs):
    x_refs, (keyed_ref, row_ref), (out_ref, low_ref, high_ref) = refs[:4], refs[4:6], refs[6:9]
    held, more, wide, line, low, high, in_sem, out_sem = refs[9:]
    q = pl.program_id(0)
    pairs = n * n
    part = wide.shape[1]
    lanes = out_ref.shape[2]
    cuts = tile_cuts(lanes)

    @pl.when(q == 0)
    def _():
        load_tokens(
            n, meta_ref[3 * pairs + n + 1], meta_ref[3 * pairs + n + 2], x_refs, held, more, wide, in_sem
        )

        @pl.loop(0, line.shape[0] // BLK)
        def _(i):
            line[pl.ds(pl.multiple_of(i * BLK, BLK), BLK), :] = jnp.zeros((BLK, part), line.dtype)

    usual = min(32, window)
    for s in range(n):
        source = pl.multiple_of(meta_ref[q * n + s], BLK)
        target = pl.multiple_of(meta_ref[pairs + q * n + s], BLK)
        line[pl.ds(target, usual), :] = wide[pl.ds(source, usual), :]
        if window > usual:

            @pl.when(meta_ref[2 * pairs + q * n + s] > usual)
            def _(source=source, target=target):
                line[pl.ds(target + usual, window - usual), :] = wide[
                    pl.ds(source + usual, window - usual), :
                ]

    kvh, per, _ = keyed_ref.shape
    group = per // rows

    def copy(o, t):
        if t == 0:
            return pltpu.make_async_copy(low.at[o], low_ref.at[o], out_sem.at[o, 0])
        here = pl.ds(cuts[t] - cuts[1], cuts[t + 1] - cuts[t])
        return pltpu.make_async_copy(
            high.at[o, here], high_ref.at[o, here], out_sem.at[o, t]
        )

    def one(t):
        here = slice(cuts[t], cuts[t + 1])
        tile = line[here, :].astype(low.dtype)
        if t == 0:
            low[q] = tile
        else:
            high[q, cuts[t] - cuts[1] : cuts[t + 1] - cuts[1], :] = tile
        copy(q, t).start()
        raw = lax.dot_general(
            keyed_ref[...].reshape(kvh * per, part),
            tile,
            (((1,), (1,)), ((), ())),
            preferred_element_type=jnp.float32,
        ).reshape(kvh, rows, group, cuts[t + 1] - cuts[t])
        owner_row = row_ref[0, :, here]
        picked = jnp.zeros((kvh, group, cuts[t + 1] - cuts[t]), jnp.float32)
        for r in range(rows):
            picked = picked + jnp.where((owner_row == r)[None], raw[:, r], 0.0)
        out_ref[0, :, here] = picked.reshape(kvh * group, -1).astype(out_ref.dtype)

    one(0)
    for t in range(1, len(cuts) - 1):
        pl.when(meta_ref[3 * pairs + q] > cuts[t])(functools.partial(one, t))

    @pl.when(q == n - 1)
    def _():
        for o in range(n):
            copy(o, 0).wait()
            for t in range(1, len(cuts) - 1):
                pl.when(meta_ref[3 * pairs + o] > cuts[t])(lambda o=o, t=t: copy(o, t).wait())


def weight_kernel(scale, parts_ref, row_ref, top_ref, sum_ref, cached_ref, w_ref, kept_ref):
    n = parts_ref.shape[0]
    scores = parts_ref[0].astype(jnp.float32)
    for i in range(1, n):
        scores = scores + parts_ref[i].astype(jnp.float32)
    scores = scores * scale
    owner_row = row_ref[...]
    weights = jnp.zeros(scores.shape, jnp.float32)
    for r in range(top_ref.shape[0]):
        own = jnp.where(owner_row == r, scores, -jnp.inf)
        cache_top = top_ref[r]
        top = jnp.maximum(jnp.max(own, 1, keepdims=True), cache_top)
        held = jnp.exp(own - top)
        fade = jnp.exp(cache_top - top)
        total = jnp.sum(held, 1, keepdims=True) + sum_ref[r] * fade
        weights = weights + held / total
        kept_ref[r] = cached_ref[r] * (fade / total)
    weights = weights.astype(w_ref.dtype)
    for i in range(n):
        w_ref[i] = weights


def value_kernel(
    rows, size_ref, w_ref, row_ref, low_ref, high_ref, value_ref, out_ref, low, high, acc, mixed, sem
):
    q = pl.program_id(0)
    n = low.shape[0]
    kvh = value_ref.shape[0]
    _, heads, lanes = w_ref.shape
    per = rows * heads // kvh
    cuts = tile_cuts(lanes)

    def copy(o, t):
        if t == 0:
            return pltpu.make_async_copy(low_ref.at[o], low.at[o], sem.at[o, 0])
        here = pl.ds(cuts[t] - cuts[1], cuts[t + 1] - cuts[t])
        return pltpu.make_async_copy(high_ref.at[o, here], high.at[o, here], sem.at[o, t])

    @pl.when(q == 0)
    def _():
        for o in range(n):
            copy(o, 0).start()
            for t in range(1, len(cuts) - 1):
                pl.when(size_ref[o] > cuts[t])(lambda o=o, t=t: copy(o, t).start())

    def one(t):
        copy(q, t).wait()
        here = slice(cuts[t], cuts[t + 1])
        width = cuts[t + 1] - cuts[t]
        weights = w_ref[0, :, here].astype(jnp.float32).reshape(kvh, 1, heads // kvh, width)
        owner_row = row_ref[0, :, here]
        spread = jnp.concatenate(
            [jnp.where((owner_row == r)[None, None], weights, 0.0) for r in range(rows)], 1
        ).reshape(kvh * per, width)
        tile = low[q] if t == 0 else high[q, cuts[t] - cuts[1] : cuts[t + 1] - cuts[1], :]
        got = jnp.dot(spread.astype(jnp.bfloat16), tile, preferred_element_type=jnp.float32)
        if t:
            acc[...] += got
        else:
            acc[...] = got

    one(0)
    for t in range(1, len(cuts) - 1):
        pl.when(size_ref[q] > cuts[t])(functools.partial(one, t))
    for h in range(kvh):
        mixed[h, pl.ds(pl.multiple_of(q * per, per), per), :] = acc[
            h * per : (h + 1) * per, :
        ].astype(mixed.dtype)

    @pl.when(q == n - 1)
    def _():
        for h in range(kvh):
            done = jnp.dot(mixed[h], value_ref[h], preferred_element_type=jnp.float32)
            out_ref[:, h] = done.reshape(n, per, done.shape[1]).astype(out_ref.dtype)


def sum_kernel(parts_ref, kept_ref, out_ref, total):
    n, kvh, per, hd = parts_ref.shape
    rows, heads = kept_ref.shape[:2]
    group = heads // kvh
    for h in range(kvh):
        terms = parts_ref[0, h].astype(jnp.float32)
        for i in range(1, n):
            terms = terms + parts_ref[i, h].astype(jnp.float32)
        for r in range(rows):
            here = slice((h * rows + r) * group, (h * rows + r + 1) * group)
            total[here, :] = (
                terms[r * group : (r + 1) * group] + kept_ref[r, h * group : (h + 1) * group, :]
            )
    pieces = [
        total[pl.ds(h * per + g, rows, stride=group), :]
        for h in range(kvh)
        for g in range(group)
    ]
    out_ref[...] = jnp.concatenate(pieces, 1).astype(out_ref.dtype)


def project_kernel(n, core_ref, *refs):
    row_refs, (weight_ref, own_ref, away_ref, gathered) = refs[:n], refs[n:]
    rows = row_refs[0].shape[0]
    cols = own_ref.shape[1]
    for k in range(0, n, 2):
        pair = [row_refs[k + j][...].astype(jnp.float32) for j in range(2)]
        gathered[k * rows : (k + 2) * rows, :] = jnp.concatenate(pair).astype(gathered.dtype)
    step = min(256, cols)
    for i in range(0, 2 * cols, step):
        done = jnp.dot(
            gathered[...], weight_ref[:, i : i + step], preferred_element_type=jnp.float32
        )
        here = slice(i % cols, i % cols + step)

        @pl.when(core_ref[0] == i // cols)
        def _(done=done, here=here):
            own_ref[:, here] = done

        @pl.when(core_ref[0] != i // cols)
        def _(done=done, here=here):
            away_ref[:, here] = done


def order_kernel(n, me_ref, own_ref, got_ref, out_ref):
    rows = own_ref.shape[0] // n
    for q in range(0, n, 2):
        pair = []
        for j in range(2):
            here = pl.ds(pl.multiple_of((me_ref[0] ^ (q + j)) * rows, rows), rows)
            pair.append(own_ref[here, :] + got_ref[here, :])
        out_ref[q * rows : (q + 2) * rows, :] = jnp.concatenate(pair).astype(out_ref.dtype)


def with_partner(x, k, n):
    return lax.ppermute(x, "pool", [(i, i ^ k) for i in range(n)])


def from_rest(held, n):
    k = n // 4
    while k >= 1:
        held = jnp.concatenate([held, with_partner(held, k, n)])
        k //= 2
    return held


def reversed_bits(k, n):
    out, bit = 0, 1
    while bit < n:
        out = out + (k // bit) % 2 * (n // 2 // bit)
        bit *= 2
    return out


def far_first(n):
    return sorted(range(1, n), reverse=True)


def swap_parts(parts, n):
    got = [parts[0]] + [None] * (n - 1)
    for k in far_first(n):
        got[k] = with_partner(parts[k], k, n)
    return got


def local(
    x_prompt, kv_weight, block_dest, block_row, block_fill, queries, kv_cache, cache_len, out_weight
):
    n = lax.axis_size("pool")
    ntp = lax.axis_size("tp")
    me = lax.axis_index("pool").astype(jnp.int32)
    core = lax.axis_index("tp").astype(jnp.int32)
    tokens, width = x_prompt.shape
    part = width // n
    kvh = kv_weight.shape[1]
    hd = kv_weight.shape[2] // 2
    rows, heads = queries.shape[0], queries.shape[1]
    group = heads // kvh
    per = rows * group
    cache_slots = kv_cache.shape[1]
    blocks = tokens // BLK
    cap = max(2, 2 * blocks // n)
    window = cap * BLK + BLK
    lanes = -(-n * window // 128) * 128
    half = tokens // ntp
    scale = 1.0 / hd**0.5
    swap = [(i, (i + 1) % ntp) for i in range(ntp)]

    size = half * 3 // 4
    extra = half - size
    at = jnp.stack([me, core])
    dest = block_dest[:, 0]
    packed = pack(x_prompt, block_fill, dest, at, n, 0, size)
    far = with_partner(queries, n // 2, n)
    packed, far = lax.optimization_barrier((packed, far))
    mine = lax.all_to_all(packed, "pool", 0, 0, tiled=True).reshape(n * size, part)

    index = jnp.arange(n * blocks, dtype=jnp.int32)
    sender = index // blocks
    kin = sender[None, :] == sender[:, None]
    lower = kin & (dest[None, :] < dest[:, None])
    level = kin & (dest[None, :] == dest[:, None]) & (index[None, :] < index[:, None])
    before = jnp.sum(jnp.where(lower, block_fill[None, :], 0), 1)
    within = jnp.sum(jnp.where(level, block_fill[None, :], 0), 1)
    pair = jnp.arange(n * n, dtype=jnp.int32)
    to, by = pair // n, pair % n
    owned = dest[None, :] == to[:, None]
    sent = sender[None, :] == by[:, None]
    earlier = sent & (dest[None, :] < to[:, None])
    offset = jnp.sum(jnp.where(earlier, block_fill[None, :], 0), 1)
    amount = jnp.sum(jnp.where(sent & owned, block_fill[None, :], 0), 1)
    runs = jnp.where(amount > 0, (offset % BLK + amount + BLK - 1) // BLK * BLK, 0)
    runs_by = runs.reshape(n, n)
    prior = jnp.arange(n)[:, None] < jnp.arange(n)[None, :]
    targets = jnp.sum(jnp.where(prior[None], runs_by[:, :, None], 0), 1)
    list_rows = jnp.sum(runs_by, 1)
    targets = targets.reshape(-1)
    mine_pair = (dest * n + sender)[:, None] == pair[None, :]
    start = (
        dest * lanes
        + jnp.sum(jnp.where(mine_pair, targets[None, :], 0), 1)
        + before % BLK
        + within
    )
    spot = jnp.arange(n * lanes, dtype=jnp.int32)[:, None]
    inside = (spot >= start[None, :]) & (spot < (start + block_fill)[None, :])
    rowof = jnp.sum(jnp.where(inside, (block_row + 1)[None, :], 0), 1) - 1
    rowof = rowof.reshape(n, 1, lanes)
    sources = by * tokens + offset // BLK * BLK

    most = jnp.max(jnp.sum(block_fill.reshape(n, blocks), 1))
    groups = lax.axis_size("groups")
    k = 1
    while k < groups:
        most = jnp.maximum(
            most, lax.ppermute(most, "groups", [(i, i ^ k) for i in range(groups)])
        )
        k *= 2
    over = most > ntp * size

    def exchange_rest():
        rest = pack(x_prompt, block_fill, dest, at, n, ntp * size, extra)
        rest = lax.all_to_all(rest, "pool", 0, 0, tiled=True).reshape(n * extra, part)
        return rest, lax.ppermute(rest, "tp", swap)

    def no_rest():
        return (jnp.zeros((n * extra, part), jnp.bfloat16),) * 2

    more_mine, more_other = lax.cond(over, exchange_rest, no_rest)
    meta = jnp.concatenate(
        [sources, targets, runs, list_rows, jnp.stack([me, core, over.astype(jnp.int32)])]
    )

    allq = from_rest(jnp.stack([queries, far]), n).reshape(n, rows, kvh, group, hd)
    keyed = jnp.einsum(
        "qrhgd,phd->hqrgp", allq, kv_weight[:, :, :hd], preferred_element_type=jnp.float32
    ).astype(jnp.bfloat16)
    keyed = keyed.reshape(kvh, n * per, part)
    values = kv_weight[:, :, hd:].transpose(1, 0, 2)

    query = queries.reshape(rows, kvh, group, hd)
    cache_scores = (
        jnp.einsum(
            "rhgd,rthd->rhgt", query, kv_cache[:, :, :, :hd], preferred_element_type=jnp.float32
        )
        * scale
    )
    cache_live = jnp.arange(cache_slots, dtype=jnp.int32)[None, :] < cache_len[:, None]
    cache_scores = jnp.where(cache_live[:, None, None, :], cache_scores, -jnp.inf)
    cache_top = jnp.max(cache_scores, -1, keepdims=True)
    cache_exp = jnp.exp(cache_scores - cache_top)
    cache_sum = jnp.sum(cache_exp, -1, keepdims=True)
    cached = jnp.einsum(
        "rhgt,rthd->rhgd",
        cache_exp.astype(jnp.bfloat16),
        kv_cache[:, :, :, hd:],
        preferred_element_type=jnp.float32,
    )
    cache_top = cache_top.reshape(rows, heads, 1)
    cache_sum = cache_sum.reshape(rows, heads, 1)
    cached = cached.reshape(rows, heads, hd)

    mine, meta, list_rows, rowof, keyed, values, cache_top, cache_sum, cached = (
        lax.optimization_barrier(
            (mine, meta, list_rows, rowof, keyed, values, cache_top, cache_sum, cached)
        )
    )
    other = lax.ppermute(mine, "tp", swap)

    anywhere = pl.BlockSpec(memory_space=pl.ANY)
    row_spec = pl.BlockSpec((1, 1, lanes), lambda q, m: (q, 0, 0))
    slot_spec = pl.BlockSpec((1, heads, lanes), lambda q, m: (q, 0, 0))
    slot_shape = jax.ShapeDtypeStruct((n, heads, lanes), jnp.bfloat16)
    cuts = tile_cuts(lanes)
    list_shapes = [(n, cuts[1], part), (n, lanes - cuts[1], part)]
    list_scratch = [pltpu.VMEM(shape, jnp.bfloat16) for shape in list_shapes]
    at_me = 3 * n * n + n
    partial_scores, low, high = pl.pallas_call(
        functools.partial(score_kernel, n, rows, window),
        grid_spec=pltpu.PrefetchScalarGridSpec(
            num_scalar_prefetch=1,
            grid=(n,),
            in_specs=[
                *[anywhere] * 4,
                pl.BlockSpec(
                    (kvh, per, part), lambda q, m: (0, reversed_bits(m[at_me] ^ q, n), 0)
                ),
                row_spec,
            ],
            out_specs=[slot_spec, anywhere, anywhere],
            scratch_shapes=[
                pltpu.VMEM((ntp, n * size, part), jnp.bfloat16),
                pltpu.VMEM((ntp, n * extra, part), jnp.bfloat16),
                pltpu.VMEM((n * tokens + window, part), jnp.float32),
                pltpu.VMEM((lanes + window, part), jnp.float32),
                *list_scratch,
                pltpu.SemaphoreType.DMA((ntp, 4)),
                pltpu.SemaphoreType.DMA((n, len(cuts) - 1)),
            ],
        ),
        out_shape=[
            slot_shape,
            *[jax.ShapeDtypeStruct(shape, jnp.bfloat16) for shape in list_shapes],
        ],
        compiler_params=pltpu.CompilerParams(vmem_limit_bytes=34 * MIB),
        name="prompt_scores",
    )(meta, mine, other, more_mine, more_other, keyed, rowof)

    parts = lax.all_to_all(partial_scores, "pool", 0, 0, tiled=True)
    my_rows = lax.dynamic_index_in_dim(rowof, me, 0, keepdims=False)
    weights, kept = pl.pallas_call(
        functools.partial(weight_kernel, scale),
        out_shape=[slot_shape, jax.ShapeDtypeStruct((rows, heads, hd), jnp.float32)],
        compiler_params=pltpu.CompilerParams(vmem_limit_bytes=8 * MIB),
        name="softmax_weights",
    )(parts, my_rows, cache_top, cache_sum, cached)

    all_weights = lax.all_to_all(weights, "pool", 0, 0, tiled=True)
    terms = pl.pallas_call(
        functools.partial(value_kernel, rows),
        grid_spec=pltpu.PrefetchScalarGridSpec(
            num_scalar_prefetch=1,
            grid=(n,),
            in_specs=[
                slot_spec,
                row_spec,
                anywhere,
                anywhere,
                pl.BlockSpec((kvh, part, hd), lambda q, m: (0, 0, 0)),
            ],
            out_specs=pl.BlockSpec((n, kvh, per, hd), lambda q, m: (0, 0, 0, 0)),
            scratch_shapes=[
                *list_scratch,
                pltpu.VMEM((kvh * per, part), jnp.float32),
                pltpu.VMEM((kvh, n * per, part), jnp.bfloat16),
                pltpu.SemaphoreType.DMA((n, len(cuts) - 1)),
            ],
        ),
        out_shape=jax.ShapeDtypeStruct((n, kvh, per, hd), jnp.bfloat16),
        compiler_params=pltpu.CompilerParams(vmem_limit_bytes=24 * MIB),
        name="weighted_values",
    )(list_rows, all_weights, rowof, low, high, values)

    term_parts = lax.all_to_all(terms, "pool", 0, 0, tiled=True)
    attended = pl.pallas_call(
        sum_kernel,
        out_shape=jax.ShapeDtypeStruct((rows, heads * hd), jnp.bfloat16),
        scratch_shapes=[pltpu.VMEM((kvh * per, hd), jnp.float32)],
        compiler_params=pltpu.CompilerParams(vmem_limit_bytes=8 * MIB),
        name="attended_sum",
    )(term_parts, kept)

    cols = out_weight.shape[1] // ntp
    half_shape = jax.ShapeDtypeStruct((n * rows, cols), jnp.float32)
    half_spec = pl.BlockSpec((n * rows, cols), lambda i, m: (0, 0))
    own, away = pl.pallas_call(
        functools.partial(project_kernel, n),
        grid_spec=pltpu.PrefetchScalarGridSpec(
            num_scalar_prefetch=1,
            grid=(1,),
            in_specs=[
                *[pl.BlockSpec((rows, heads * hd), lambda i, m: (0, 0))] * n,
                pl.BlockSpec(out_weight.shape, lambda i, m: (0, 0)),
            ],
            out_specs=[half_spec] * 2,
            scratch_shapes=[pltpu.VMEM((n * rows, heads * hd), jnp.bfloat16)],
        ),
        out_shape=[half_shape] * 2,
        compiler_params=pltpu.CompilerParams(vmem_limit_bytes=26 * MIB),
        name="output_projection",
    )(core.reshape(1), *swap_parts([attended] * n, n), out_weight)
    got = lax.ppermute(away, "tp", swap)
    return pl.pallas_call(
        functools.partial(order_kernel, n),
        grid_spec=pltpu.PrefetchScalarGridSpec(
            num_scalar_prefetch=1,
            grid=(1,),
            in_specs=[half_spec] * 2,
            out_specs=half_spec,
        ),
        out_shape=jax.ShapeDtypeStruct((n * rows, cols), jnp.bfloat16),
        compiler_params=pltpu.CompilerParams(vmem_limit_bytes=4 * MIB),
        name="order_rows",
    )(me.reshape(1), own, got)


def solution(mesh):
    in_specs = (
        P(("groups", "pool"), None),
        P("pool", "tp", None),
        P("groups", None),
        P("groups"),
        P("groups"),
        P(("groups", "pool"), "tp", None),
        P(("groups", "pool"), None, "tp", None),
        P(("groups", "pool")),
        P("tp", "pool"),
    )
    out_specs = P("groups", ("pool", "tp"))
    return jax.shard_map(local, mesh=mesh, in_specs=in_specs, out_specs=out_specs, check_vma=False)
```

time: 183 us -> 164 us (0.90)
  starting transfers between devices: 58.1 us -> 26.4 us
  blocking collectives: 0 us -> 31.6 us
  waiting for transfers between devices: 54.8 us -> 39.8 us
  matrix products: 10.4 us -> 5.72 us
  Pallas kernels: 31.1 us -> 26.8 us
  other arithmetic: 3.49 us -> 7.26 us
    ppermute x31 -> x10, starting transfers between devices: 49.1 us -> 13.9 us  [with_partner(): return lax.ppermute(x, 'pool', [(i, i ^ k) for i in range(n)])]
    all_to_all x0 -> x2, blocking collectives: none -> 31.6 us  [the longest x1 17.2 us: local(): term_parts = lax.all_to_all(terms, 'pool', 0, 0, tiled=True)]
    ppermute x31 -> x10, waiting for transfers between devices: 51.8 us -> 26.4 us  [with_partner(): return lax.ppermute(x, 'pool', [(i, i ^ k) for i in range(n)])]
    all_to_all x0 -> x1, waiting for transfers between devices: none -> 10.3 us  [local(): parts = lax.all_to_all(partial_scores, 'pool', 0, 0, tiled=True)]
    all_to_all x0 -> x1, starting transfers between devices: none -> 5.58 us  [local(): parts = lax.all_to_all(partial_scores, 'pool', 0, 0, tiled=True)]
    dot_general x1 -> x0, matrix products: 4.96 us -> none  [local(): product = jnp.dot(everyone, out_weight, preferred_element_type=jnp.float32)]
    pallas_call x3 -> x4, Pallas kernels: 14.8 us -> 10.5 us  [the longest x1 6.22 us: local(): pl.pallas_call(functools.partial(value_kernel, rows), grid_spec=pltpu.Pre...]
    all_to_all x1, starting transfers between devices: 7.43 us -> 3.82 us  [local(): lax.all_to_all(packed, 'pool', 0, 0, tiled=True).reshape(n * size, part)]
  transfers between devices with their start and end apart: 35 -> 15, of which waited for: 14 -> 9; matrix products, arithmetic and copies ran while one was open for 12% -> 14% of each run, Pallas kernels for 0% -> 3%
where the time goes in v6:
time: 164 us; the launch traced here: 163 us
  waiting for transfers between devices  39.8 us (24%)
  blocking collectives  31.6 us (19%)
  Pallas kernels  26.8 us (16%)
  starting transfers between devices  26.4 us (16%)
  local copies, waits for them, and re-layouts  24 us (15%)
  other arithmetic  7.26 us (4%)
  matrix products  5.72 us (3%)
    ppermute x10, waiting for transfers between devices, with_partner(): return lax.ppermute(x, 'pool', [(i, i ^ k) for i in range(n)])  26.4 us
    all_to_all x1, blocking collectives, local(): term_parts = lax.all_to_all(terms, 'pool', 0, 0, tiled=True)  17.2 us
    unnamed x27, local copies, waits for them, and re-layouts  14.6 us
    all_to_all x1, blocking collectives, local(): all_weights = lax.all_to_all(weights, 'pool', 0, 0, tiled=True)  14.4 us
    ppermute x10, starting transfers between devices, with_partner(): return lax.ppermute(x, 'pool', [(i, i ^ k) for i in range(n)])  13.9 us
    pallas_call x1, Pallas kernels, local(): pl.pallas_call(functools.partial(score_kernel, n, rows, window), grid_spe...  11.3 us
    all_to_all x1, waiting for transfers between devices, local(): parts = lax.all_to_all(partial_scores, 'pool', 0, 0, tiled=True)  10.3 us
    pallas_call x1, Pallas kernels, local(): pl.pallas_call(functools.partial(value_kernel, rows), grid_spec=pltpu.Pre...  6.22 us
  transfers between devices with their start and end apart: 15, of which 9 were waited for; matrix products, arithmetic and copies ran while one was open for 14% of the time, Pallas kernels for 3%

profile of v6, /device:TPU:0, one launch (start us, length us, event | category | flops | bytes accessed | tf_op | source)
XLA Modules:
  0.0 162.9 jit_solution(1690555920443005422)
XLA Ops:
  0.0 0.8 reshape.233
  0.8 0.1 reduce_sum.100
  0.9 0.6 reduce_max.18
  1.5 2.9 %collective-permute-start.2 = (s32[]{:T(128)}, s32[]{:T(128)}, u32[]{:S(2)}, u32[]{:S(2)}) collective-permute-start(s32[]{:T(128)} %reduce_max.18), channel_id=1, source_target_pairs={{0,16},{16,0},{1,17},{17,1},{2,18},{18,2},{3,19},{19,3},{4,20},{20... | collective-permute-start | bytes 20 | tf_op jit(solution)/shard_map/ppermute | solution.py:459
  4.5 2.6 %collective-permute-start.1 = (bf16[8,32,128]{2,1,0:T(8,128)(2,1)}, bf16[8,32,128]{2,1,0:T(8,128)(2,1)S(1)}, u32[]{:S(2)}, u32[]{:S(2)}) collective-permute-start(bf16[8,32,128]{2,1,0:T(8,128)(2,1)} %param.16), channel_id=1, source_target_pairs={{0,8},{2,10},{4,12},{6,14},{8,0},{10,2},{12,4},{14,6},{1,9},{3,11}... | collective-permute-start | bytes 196616 | tf_op jit(solution)/shard_map/ppermute | solution.py:359
  7.1 0.7 fusion.30
  7.8 1.0 select_reduce_fusion.2
  8.8 0.9 select_reduce_fusion.4
  9.8 0.1 fusion.35
  10.0 0.1 select_reduce_fusion.6
  10.2 0.7 iota_compare_fusion.4
  10.9 0.1 select_reduce_fusion.3
  11.0 0.7 fusion.33
  11.8 4.4 %pack_live_tokens.3 = bf16[8,96,1024]{2,1,0:T(8,128)(2,1)} custom-call(s32[2]{0:T(128)S(1)} %pad_add_fusion.at_ref, s32[256]{0:T(256)} %fill_ref.1, s32[256]{0:T(256)} %bitcast.51, bf16[256,8192]{1,0:T(8,128)(2,1)} %x_ref.1), custom_call_target="tpu_custom_call" | custom-call | tf_op jit(solution)/shard_map/pack_live_tokens/pallas_call | solution.py:70
  16.2 3.8 %all-to-all-start.1 = ((bf16[8,96,1024]{2,1,0:T(8,128)(2,1)}), bf16[8,96,1024]{2,1,0:T(8,128)(2,1)S(1)}, u32[]{:S(2)}, u32[]{:S(2)}) async-start(bf16[8,96,1024]{2,1,0:T(8,128)(2,1)} %pack_live_tokens.3), calls=%async_computation.1 | async-start | bytes 3145728 | tf_op jit(solution)/shard_map/all_to_all | solution.py:419
  20.0 1.0 select_reduce_fusion
  21.1 4.0 %fusion.37 = (bf16[8,256,4,128]{3,2,1,0:T(4,128)(2,1)}, bf16[8,256,4,128]{3,2,1,0:T(4,128)(2,1)S(1)}) fusion(bf16[8,256,4,256]{3,2,1,0:T(4,128)(2,1)} %param.17), kind=kLoop, calls=%fused_computation.91 | loop fusion | bytes 8388608 | tf_op jit(solution)/shard_map/slice | solution.py:499
  25.1 0.7 fusion.39
  25.9 0.9 copy-done.6
  26.7 2.1 %fusion.38 = (bf16[1024,4,128]{2,1,0:T(4,128)(2,1)}, bf16[1024,4,128]{2,1,0:T(4,128)(2,1)}) fusion(bf16[1024,4,256]{2,1,0:T(4,128)(2,1)S(1)} %copy-done.6), kind=kLoop, calls=%fused_computation.92 | loop fusion | bytes 4194304 | tf_op jit(solution)/shard_map/slice | solution.py:482
  28.8 2.1 %collective-permute-start.3 = (bf16[2,8,32,128]{3,2,1,0:T(8,128)(2,1)S(1)}, bf16[2,8,32,128]{3,2,1,0:T(8,128)(2,1)S(1)}, u32[]{:S(2)}, u32[]{:S(2)}) collective-permute-start(bf16[2,8,32,128]{3,2,1,0:T(8,128)(2,1)S(1)} %pad_maximum_fusion.2), channel_id=1, source_target_pairs={{0,4},{2,6},{4,0},{6,2},{8,12},{10,14},{12,8},{14,10},{1,5},{3,7},... | collective-permute-start | bytes 393224 | tf_op jit(solution)/shard_map/ppermute | solution.py:359
  30.9 16.9 %collective-permute-done.3 = bf16[2,8,32,128]{3,2,1,0:T(8,128)(2,1)S(1)} collective-permute-done((bf16[2,8,32,128]{3,2,1,0:T(8,128)(2,1)S(1)}, bf16[2,8,32,128]{3,2,1,0:T(8,128)(2,1)S(1)}, u32[]{:S(2)}, u32[]{:S(2)}) %collective-permute-start.3) | collective-permute-done | bytes 131104 | tf_op jit(solution)/shard_map/ppermute | solution.py:359
  47.8 0.7 pad_maximum_fusion.1
  48.5 1.7 %collective-permute-start.4 = (bf16[4,8,32,128]{3,2,1,0:T(8,128)(2,1)}, bf16[4,8,32,128]{3,2,1,0:T(8,128)(2,1)}, u32[]{:S(2)}, u32[]{:S(2)}) collective-permute-start(bf16[4,8,32,128]{3,2,1,0:T(8,128)(2,1)} %pad_maximum_fusion.1), channel_id=1, source_target_pairs={{0,2},{2,0},{4,6},{6,4},{8,10},{10,8},{12,14},{14,12},{1,3},{3,1},... | collective-permute-start | bytes 786440 | tf_op jit(solution)/shard_map/ppermute | solution.py:359
  50.2 0.2 fusion.17
  50.6 1.5 copy.57
  52.1 0.4 copy-done.5
  52.5 0.4 fusion.11.cached_ref
  54.2 0.1 concatenate.20.meta_ref
  54.3 2.0 %collective-permute-done.4 = bf16[4,8,32,128]{3,2,1,0:T(8,128)(2,1)} collective-permute-done((bf16[4,8,32,128]{3,2,1,0:T(8,128)(2,1)}, bf16[4,8,32,128]{3,2,1,0:T(8,128)(2,1)}, u32[]{:S(2)}, u32[]{:S(2)}) %collective-permute-start.4) | collective-permute-done | bytes 262176 | tf_op jit(solution)/shard_map/ppermute | solution.py:359
  56.4 4.5 %convolution_convert_fusion = bf16[4,8,8,8,1024]{4,3,2,1,0:T(8,128)(2,1)} fusion(bf16[1024,4,128]{2,1,0:T(4,128)(2,1)} %get-tuple-element.68, bf16[4,8,4,8,128]{4,3,2,1,0:T(8,128)(2,1)} %bitcast.13, bf16[2,8,4,8,128]{4,3,2,1,0:T(8,128)(2,1)S(1)} %bitcast.47, bf16[1,8,4,8,128]{4,3,2,1,0:T(8,128)(2,1)S(1)} %bitcast.46, bf16[1,8,4,8,128]{4,3,2,1,0:T(8,128)(2,1)S(1)} %bitcast.43), kind=kOutput, calls=%fused_computation.4 | convolution fusion | flops 539754496 | bytes 5767168 | tf_op jit(solution)/shard_map/qrhgd,phd->hqrgp/dot_general | solution.py:478
  60.9 1.7 %conditional.1 = (bf16[256,1024]{1,0:T(8,128)(2,1)}, bf16[256,1024]{1,0:T(8,128)(2,1)}) conditional(s32[]{:T(128)} %convert_element_type.10, () %tuple.17, (s32[2]{0:T(128)S(1)}, s32[256]{0:T(256)S(1)}, s32[256]{0:T(256)S(1)}, bf16[256,8192]{1,0:T(8,128)(2,1)}) %tuple.31), branch_computations={%region_12.13_spmd, %region_13.14_spmd} | conditional | bytes 3145784 | solution.py:472
  60.9 0.8 broadcast.299
  61.8 0.9 broadcast.299.clone
  62.7 1.8 %collective-permute-done.5.refs_1_ = bf16[768,1024]{1,0:T(8,128)(2,1)} collective-permute-done((bf16[768,1024]{1,0:T(8,128)(2,1)S(1)}, bf16[768,1024]{1,0:T(8,128)(2,1)}, u32[]{:S(2)}, u32[]{:S(2)}) %collective-permute-start.5) | collective-permute-done | bytes 1572896 | tf_op jit(solution)/shard_map/ppermute | solution.py:511
  64.5 2.2 %copy-done = bf16[4,8,8,8,1024]{4,3,2,1,0:T(8,128)(2,1)S(1)} copy-done((bf16[4,8,8,8,1024]{4,3,2,1,0:T(8,128)(2,1)S(1)}, bf16[4,8,8,8,1024]{4,3,2,1,0:T(8,128)(2,1)}, u32[]{:S(2)}) %copy-start) | copy-done | bytes 4194328
  66.6 11.3 %prompt_scores.1 = (bf16[8,32,640]{2,1,0:T(8,128)(2,1)}, bf16[8,256,1024]{2,1,0:T(8,128)(2,1)S(1)}, bf16[8,384,1024]{2,1,0:T(8,128)(2,1)S(1)}) custom-call(s32[203]{0:T(256)S(1)} %concatenate.20.meta_ref, bf16[768,1024]{1,0:T(8,128)(2,1)S(1)} %bitcast.36, bf16[768,1024]{1,0:T(8,128)(2,1)} %collective-permute-done.5.refs_1_, ...), custom_call_target="tpu_custom_call" | custom-call | tf_op jit(solution)/shard_map/prompt_scores/pallas_call | solution.py:521
  77.9 2.6 %copy-done.1 = bf16[8,384,1024]{2,1,0:T(8,128)(2,1)} copy-done((bf16[8,384,1024]{2,1,0:T(8,128)(2,1)}, bf16[8,384,1024]{2,1,0:T(8,128)(2,1)S(1)}, u32[]{:S(2)}) %copy-start.1) | copy-done | bytes 6291480
  80.6 2.0 %copy-done.3 = bf16[8,256,1024]{2,1,0:T(8,128)(2,1)} copy-done((bf16[8,256,1024]{2,1,0:T(8,128)(2,1)}, bf16[8,256,1024]{2,1,0:T(8,128)(2,1)S(1)}, u32[]{:S(2)}) %copy-start.3) | copy-done | bytes 4194328
  82.6 5.6 %all-to-all-start.2 = ((bf16[8,32,640]{2,1,0:T(8,128)(2,1)}), bf16[8,32,640]{2,1,0:T(8,128)(2,1)S(1)}, u32[]{:S(2)}, u32[]{:S(2)}) async-start(bf16[8,32,640]{2,1,0:T(8,128)(2,1)} %get-tuple-element.46), calls=%async_computation.2 | async-start | bytes 655360 | tf_op jit(solution)/shard_map/all_to_all | solution.py:552
  88.2 0.1 copy.32.top_ref
  88.3 0.1 copy.33.sum_ref
  88.5 10.3 %all-to-all-done.2.parts_ref = bf16[8,32,640]{2,1,0:T(8,128)(2,1)S(1)} async-done(((bf16[8,32,640]{2,1,0:T(8,128)(2,1)}), bf16[8,32,640]{2,1,0:T(8,128)(2,1)S(1)}, u32[]{:S(2)}, u32[]{:S(2)}) %all-to-all-start.2) | async-done | bytes 327712 | tf_op jit(solution)/shard_map/all_to_all | solution.py:552
  98.8 1.2 softmax_weights.1
  100.0 14.4 %all_to_all.25.w_ref = bf16[8,32,640]{2,1,0:T(8,128)(2,1)S(1)} all-to-all(bf16[8,32,640]{2,1,0:T(8,128)(2,1)S(1)} %get-tuple-element.50), channel_id=1, replica_groups=mesh['groups'=2,'pool'=8,'tp'=2] {'pool'}, dimensions={0} | all-to-all | bytes 655360 | tf_op jit(solution)/shard_map/all_to_all | solution.py:561
  114.4 2.8 %copy-done.2 = bf16[8,384,1024]{2,1,0:T(8,128)(2,1)S(1)} copy-done((bf16[8,384,1024]{2,1,0:T(8,128)(2,1)S(1)}, bf16[8,384,1024]{2,1,0:T(8,128)(2,1)}, u32[]{:S(2)}) %copy-start.2) | copy-done | bytes 6291480
  117.2 2.2 %copy-done.4 = bf16[8,256,1024]{2,1,0:T(8,128)(2,1)S(1)} copy-done((bf16[8,256,1024]{2,1,0:T(8,128)(2,1)S(1)}, bf16[8,256,1024]{2,1,0:T(8,128)(2,1)}, u32[]{:S(2)}) %copy-start.4) | copy-done | bytes 4194328
  119.4 6.2 %weighted_values.1 = bf16[8,4,64,128]{3,2,1,0:T(8,128)(2,1)S(1)} custom-call(s32[8]{0:T(128)S(1)} %get-tuple-element.39.size_ref, bf16[8,32,640]{2,1,0:T(8,128)(2,1)S(1)} %all_to_all.25.w_ref, s32[8,1,640]{2,1,0:T(1,128)S(1)} %bitcast.40, bf16[8,256,1024]{2,1,0:T(8,128)(2,1)S(1)} %copy-done.4, bf16[8,384,1024]{2,1,0:T(8,128)(2,1)S(1)} %copy-done.2, ...), custom_call_target="tpu_custom_call" | custom-call | tf_op jit(solution)/shard_map/weighted_values/pallas_call | solution.py:562
  125.6 17.2 %all_to_all.26.parts_ref = bf16[8,4,64,128]{3,2,1,0:T(8,128)(2,1)S(1)} all-to-all(bf16[8,4,64,128]{3,2,1,0:T(8,128)(2,1)S(1)} %weighted_values.1), channel_id=1, replica_groups=mesh['groups'=2,'pool'=8,'tp'=2] {'pool'}, dimensions={0} | all-to-all | bytes 1048576 | tf_op jit(solution)/shard_map/all_to_all | solution.py:587
  142.8 0.1 attended_sum.1.refs_0_
  142.9 0.6 collective-permute-start.10
  143.5 2.5 %collective-permute-start.11 = (bf16[8,4096]{1,0:T(8,128)(2,1)S(1)}, bf16[8,4096]{1,0:T(8,128)(2,1)S(1)}, u32[]{:S(2)}, u32[]{:S(2)}) collective-permute-start(bf16[8,4096]{1,0:T(8,128)(2,1)S(1)} %attended_sum.1.refs_0_), channel_id=1, source_target_pairs={{0,12},{2,14},{4,8},{6,10},{8,4},{10,6},{12,0},{14,2},{1,13},{3,15... | collective-permute-start | bytes 196616 | tf_op jit(solution)/shard_map/ppermute | solution.py:359
  146.1 2.7 %collective-permute-start.12 = (bf16[8,4096]{1,0:T(8,128)(2,1)S(1)}, bf16[8,4096]{1,0:T(8,128)(2,1)S(1)}, u32[]{:S(2)}, u32[]{:S(2)}) collective-permute-start(bf16[8,4096]{1,0:T(8,128)(2,1)S(1)} %attended_sum.1.refs_0_), channel_id=1, source_target_pairs={{0,14},{2,12},{4,10},{6,8},{8,6},{10,4},{12,2},{14,0},{1,15},{3,13... | collective-permute-start | bytes 196616 | tf_op jit(solution)/shard_map/ppermute | solution.py:359
  148.7 0.1 collective-permute-start.6
  148.8 0.5 collective-permute-start.7
  149.3 2.8 %collective-permute-done.10.refs_5_ = bf16[8,4096]{1,0:T(8,128)(2,1)S(1)} collective-permute-done((bf16[8,4096]{1,0:T(8,128)(2,1)S(1)}, bf16[8,4096]{1,0:T(8,128)(2,1)S(1)}, u32[]{:S(2)}, u32[]{:S(2)}) %collective-permute-start.10) | collective-permute-done | bytes 65568 | tf_op jit(solution)/shard_map/ppermute | solution.py:359
  152.1 0.1 collective-permute-start.8
  152.2 1.1 collective-permute-start.9
  153.3 0.2 collective-permute-done.12.refs_7_
  153.5 0.9 collective-permute-done.6.refs_1_
  154.4 3.5 %collective-permute-done.8.refs_3_ = bf16[8,4096]{1,0:T(8,128)(2,1)S(1)} collective-permute-done((bf16[8,4096]{1,0:T(8,128)(2,1)S(1)}, bf16[8,4096]{1,0:T(8,128)(2,1)S(1)}, u32[]{:S(2)}, u32[]{:S(2)}) %collective-permute-start.8) | collective-permute-done | bytes 65568 | tf_op jit(solution)/shard_map/ppermute | solution.py:359
  158.0 2.9 %output_projection.1 = (f32[64,512]{1,0:T(8,128)S(1)}, f32[64,512]{1,0:T(8,128)S(1)}) custom-call(s32[1]{0:T(128)} %bitcast.2.core_ref, bf16[8,4096]{1,0:T(8,128)(2,1)S(1)} %attended_sum.1.refs_0_, bf16[8,4096]{1,0:T(8,128)(2,1)S(1)} %collective-permute-done.6.refs_1_, bf16[8,4096]{1,0:T(8,128)(2,1)S(1)} %collective-permute-done.7.refs_2_, ...), custom_call_target="tpu_custom_call" | custom-call | tf_op jit(solution)/shard_map/output_projection/pallas_call | solution.py:599
  160.9 1.3 collective-permute-done.13.got_ref
  162.3 0.6 order_rows.1
  (42 shorter events, 0.7 us)
Async XLA Ops:
  1.5 51.5 %collective-permute-start.2 = (s32[]{:T(128)}, s32[]{:T(128)}, u32[]{:S(2)}, u32[]{:S(2)}) collective-permute-start(s32[]{:T(128)} %reduce_max.18), channel_id=1, source_target_pairs={{0,16},{16,0},{1,17},{17,1},{2,18},{18,2},{3,19},{19,3},{4,20},{20... | collective-permute-start | bytes 20 | tf_op jit(solution)/shard_map/ppermute | solution.py:459
  4.5 11.7 %collective-permute-start.1 = (bf16[8,32,128]{2,1,0:T(8,128)(2,1)}, bf16[8,32,128]{2,1,0:T(8,128)(2,1)S(1)}, u32[]{:S(2)}, u32[]{:S(2)}) collective-permute-start(bf16[8,32,128]{2,1,0:T(8,128)(2,1)} %param.16), channel_id=1, source_target_pairs={{0,8},{2,10},{4,12},{6,14},{8,0},{10,2},{12,4},{14,6},{1,9},{3,11}... | collective-permute-start | bytes 196616 | tf_op jit(solution)/shard_map/ppermute | solution.py:359
  16.2 3.8 %copy-start.10 = (s32[256]{0:T(256)S(1)}, s32[256]{0:T(256)}, u32[]{:S(2)}) copy-start(s32[256]{0:T(256)} %param.14) | copy-start | bytes 3076
  16.2 44.7 %all-to-all-start.1 = ((bf16[8,96,1024]{2,1,0:T(8,128)(2,1)}), bf16[8,96,1024]{2,1,0:T(8,128)(2,1)S(1)}, u32[]{:S(2)}, u32[]{:S(2)}) async-start(bf16[8,96,1024]{2,1,0:T(8,128)(2,1)} %pack_live_tokens.3), calls=%async_computation.1 | async-start | bytes 3145728 | tf_op jit(solution)/shard_map/all_to_all | solution.py:419
  21.1 4.1 %copy-start.7 = (bf16[8,32,128]{2,1,0:T(8,128)(2,1)S(1)}, bf16[8,32,128]{2,1,0:T(8,128)(2,1)}, u32[]{:S(2)}) copy-start(bf16[8,32,128]{2,1,0:T(8,128)(2,1)} %param.16) | copy-start | bytes 196612
  25.1 1.6 copy-start.6
  28.8 19.0 %collective-permute-start.3 = (bf16[2,8,32,128]{3,2,1,0:T(8,128)(2,1)S(1)}, bf16[2,8,32,128]{3,2,1,0:T(8,128)(2,1)S(1)}, u32[]{:S(2)}, u32[]{:S(2)}) collective-permute-start(bf16[2,8,32,128]{3,2,1,0:T(8,128)(2,1)S(1)} %pad_maximum_fusion.2), channel_id=1, source_target_pairs={{0,4},{2,6},{4,0},{6,2},{8,12},{10,14},{12,8},{14,10},{1,5},{3,7},... | collective-permute-start | bytes 393224 | tf_op jit(solution)/shard_map/ppermute | solution.py:359
  48.5 7.8 %collective-permute-start.4 = (bf16[4,8,32,128]{3,2,1,0:T(8,128)(2,1)}, bf16[4,8,32,128]{3,2,1,0:T(8,128)(2,1)}, u32[]{:S(2)}, u32[]{:S(2)}) collective-permute-start(bf16[4,8,32,128]{3,2,1,0:T(8,128)(2,1)} %pad_maximum_fusion.1), channel_id=1, source_target_pairs={{0,2},{2,0},{4,6},{6,4},{8,10},{10,8},{12,14},{14,12},{1,3},{3,1},... | collective-permute-start | bytes 786440 | tf_op jit(solution)/shard_map/ppermute | solution.py:359
  50.6 1.9 %copy-start.5 = (bf16[8,256,4,128]{3,2,1,0:T(4,128)(2,1)S(1)}, bf16[8,256,4,128]{3,2,1,0:T(4,128)(2,1)}, u32[]{:S(2)}) copy-start(bf16[8,256,4,128]{3,2,1,0:T(4,128)(2,1)} %get-tuple-element.65) | copy-start | bytes 6291460
  56.4 4.6 %copy-start.8 = (s32[256,1]{0,1:T(1,128)S(1)}, s32[256,1]{0,1:T(1,128)}, u32[]{:S(2)}) copy-start(s32[256,1]{0,1:T(1,128)} %param.13) | copy-start | bytes 3076
  56.4 4.6 %copy-start.9 = (s32[256]{0:T(256)S(1)}, s32[256]{0:T(256)}, u32[]{:S(2)}) copy-start(s32[256]{0:T(256)} %fill_ref.1) | copy-start | bytes 3076
  60.9 3.5 %collective-permute-start.5 = (bf16[768,1024]{1,0:T(8,128)(2,1)S(1)}, bf16[768,1024]{1,0:T(8,128)(2,1)}, u32[]{:S(2)}, u32[]{:S(2)}) collective-permute-start(bf16[768,1024]{1,0:T(8,128)(2,1)S(1)} %bitcast.35), channel_id=1, source_target_pairs={{0,1},{1,0},{2,3},{3,2},{4,5},{5,4},{6,7},{7,6},{8,9},{9,8},{10,11... | collective-permute-start | bytes 4718600 | tf_op jit(solution)/shard_map/ppermute | solution.py:511
  64.5 2.2 %copy-start = (bf16[4,8,8,8,1024]{4,3,2,1,0:T(8,128)(2,1)S(1)}, bf16[4,8,8,8,1024]{4,3,2,1,0:T(8,128)(2,1)}, u32[]{:S(2)}) copy-start(bf16[4,8,8,8,1024]{4,3,2,1,0:T(8,128)(2,1)} %convolution_convert_fusion) | copy-start | bytes 12582916
  77.9 2.7 %copy-start.1 = (bf16[8,384,1024]{2,1,0:T(8,128)(2,1)}, bf16[8,384,1024]{2,1,0:T(8,128)(2,1)S(1)}, u32[]{:S(2)}) copy-start(bf16[8,384,1024]{2,1,0:T(8,128)(2,1)S(1)} %get-tuple-element.52.high_ref) | copy-start | bytes 18874372
  80.6 2.0 %copy-start.3 = (bf16[8,256,1024]{2,1,0:T(8,128)(2,1)}, bf16[8,256,1024]{2,1,0:T(8,128)(2,1)S(1)}, u32[]{:S(2)}) copy-start(bf16[8,256,1024]{2,1,0:T(8,128)(2,1)S(1)} %get-tuple-element.51.low_ref) | copy-start | bytes 12582916
  82.6 16.2 %all-to-all-start.2 = ((bf16[8,32,640]{2,1,0:T(8,128)(2,1)}), bf16[8,32,640]{2,1,0:T(8,128)(2,1)S(1)}, u32[]{:S(2)}, u32[]{:S(2)}) async-start(bf16[8,32,640]{2,1,0:T(8,128)(2,1)} %get-tuple-element.46), calls=%async_computation.2 | async-start | bytes 655360 | tf_op jit(solution)/shard_map/all_to_all | solution.py:552
  98.8 59.2 %slice-start = ((s8[8388608]{0:T(1024)(128)(4,1)}), s8[4194304]{0:T(1024)(128)(4,1)S(1)}, s32[]{:S(2)}) async-start(s8[8388608]{0:T(1024)(128)(4,1)} %bitcast.33), calls=%async_computation.5 | async-start | bytes 8388608
  114.4 2.8 %copy-start.2 = (bf16[8,384,1024]{2,1,0:T(8,128)(2,1)S(1)}, bf16[8,384,1024]{2,1,0:T(8,128)(2,1)}, u32[]{:S(2)}) copy-start(bf16[8,384,1024]{2,1,0:T(8,128)(2,1)} %copy-done.1) | copy-start | bytes 18874372
  117.2 2.2 %copy-start.4 = (bf16[8,256,1024]{2,1,0:T(8,128)(2,1)S(1)}, bf16[8,256,1024]{2,1,0:T(8,128)(2,1)}, u32[]{:S(2)}) copy-start(bf16[8,256,1024]{2,1,0:T(8,128)(2,1)} %copy-done.3) | copy-start | bytes 12582916
  119.4 38.6 %slice-start.1 = ((s8[8388608]{0:T(1024)(128)(4,1)}), s8[4194304]{0:T(1024)(128)(4,1)S(1)}, s32[]{:S(2)}) async-start(s8[8388608]{0:T(1024)(128)(4,1)} %bitcast.33), calls=%async_computation.6 | async-start | bytes 8388608
  142.9 9.2 %collective-permute-start.10 = (bf16[8,4096]{1,0:T(8,128)(2,1)S(1)}, bf16[8,4096]{1,0:T(8,128)(2,1)S(1)}, u32[]{:S(2)}, u32[]{:S(2)}) collective-permute-start(bf16[8,4096]{1,0:T(8,128)(2,1)S(1)} %attended_sum.1.refs_0_), channel_id=1, source_target_pairs={{0,10},{2,8},{4,14},{6,12},{8,2},{10,0},{12,6},{14,4},{1,11},{3,9}... | collective-permute-start | bytes 196616 | tf_op jit(solution)/shard_map/ppermute | solution.py:359
  143.5 8.7 %collective-permute-start.11 = (bf16[8,4096]{1,0:T(8,128)(2,1)S(1)}, bf16[8,4096]{1,0:T(8,128)(2,1)S(1)}, u32[]{:S(2)}, u32[]{:S(2)}) collective-permute-start(bf16[8,4096]{1,0:T(8,128)(2,1)S(1)} %attended_sum.1.refs_0_), channel_id=1, source_target_pairs={{0,12},{2,14},{4,8},{6,10},{8,4},{10,6},{12,0},{14,2},{1,13},{3,15... | collective-permute-start | bytes 196616 | tf_op jit(solution)/shard_map/ppermute | solution.py:359
  146.1 7.4 %collective-permute-start.12 = (bf16[8,4096]{1,0:T(8,128)(2,1)S(1)}, bf16[8,4096]{1,0:T(8,128)(2,1)S(1)}, u32[]{:S(2)}, u32[]{:S(2)}) collective-permute-start(bf16[8,4096]{1,0:T(8,128)(2,1)S(1)} %attended_sum.1.refs_0_), channel_id=1, source_target_pairs={{0,14},{2,12},{4,10},{6,8},{8,6},{10,4},{12,2},{14,0},{1,15},{3,13... | collective-permute-start | bytes 196616 | tf_op jit(solution)/shard_map/ppermute | solution.py:359
  148.7 5.7 %collective-permute-start.6 = (bf16[8,4096]{1,0:T(8,128)(2,1)S(1)}, bf16[8,4096]{1,0:T(8,128)(2,1)S(1)}, u32[]{:S(2)}, u32[]{:S(2)}) collective-permute-start(bf16[8,4096]{1,0:T(8,128)(2,1)S(1)} %attended_sum.1.refs_0_), channel_id=1, source_target_pairs={{0,2},{2,0},{4,6},{6,4},{8,10},{10,8},{12,14},{14,12},{1,3},{3,1},... | collective-permute-start | bytes 196616 | tf_op jit(solution)/shard_map/ppermute | solution.py:359
  148.8 5.6 %collective-permute-start.7 = (bf16[8,4096]{1,0:T(8,128)(2,1)S(1)}, bf16[8,4096]{1,0:T(8,128)(2,1)S(1)}, u32[]{:S(2)}, u32[]{:S(2)}) collective-permute-start(bf16[8,4096]{1,0:T(8,128)(2,1)S(1)} %attended_sum.1.refs_0_), channel_id=1, source_target_pairs={{0,4},{2,6},{4,0},{6,2},{8,12},{10,14},{12,8},{14,10},{1,5},{3,7},... | collective-permute-start | bytes 196616 | tf_op jit(solution)/shard_map/ppermute | solution.py:359
  152.1 5.8 %collective-permute-start.8 = (bf16[8,4096]{1,0:T(8,128)(2,1)S(1)}, bf16[8,4096]{1,0:T(8,128)(2,1)S(1)}, u32[]{:S(2)}, u32[]{:S(2)}) collective-permute-start(bf16[8,4096]{1,0:T(8,128)(2,1)S(1)} %attended_sum.1.refs_0_), channel_id=1, source_target_pairs={{0,6},{2,4},{4,2},{6,0},{8,14},{10,12},{12,10},{14,8},{1,7},{3,5},... | collective-permute-start | bytes 196616 | tf_op jit(solution)/shard_map/ppermute | solution.py:359
  152.2 5.7 %collective-permute-start.9 = (bf16[8,4096]{1,0:T(8,128)(2,1)S(1)}, bf16[8,4096]{1,0:T(8,128)(2,1)S(1)}, u32[]{:S(2)}, u32[]{:S(2)}) collective-permute-start(bf16[8,4096]{1,0:T(8,128)(2,1)S(1)} %attended_sum.1.refs_0_), channel_id=1, source_target_pairs={{0,8},{2,10},{4,12},{6,14},{8,0},{10,2},{12,4},{14,6},{1,9},{3,11}... | collective-permute-start | bytes 196616 | tf_op jit(solution)/shard_map/ppermute | solution.py:359
  160.9 1.4 collective-permute-start.13

commit v7 on v6

--- a/solution.py
+++ b/solution.py
@@ -126,13 +126,6 @@
     for pair in main:
         for copy in pair:
             copy.start()
-
-    @pl.loop(0, n)
-    def _(s):
-        at = pl.multiple_of(s * tokens + 2 * size, BLK)
-        wide[pl.ds(at, 2 * extra), :] = jnp.zeros((2 * extra, part), wide.dtype)
-
-    wide[n * tokens :, :] = jnp.zeros((wide.shape[0] - n * tokens, part), wide.dtype)
     for i, pair in enumerate(main):
         for copy in pair:
             copy.wait()
@@ -150,40 +143,26 @@
         widen(more, 2 * size, 0, n)
 
 
-def score_kernel(n, rows, window, meta_ref, *refs):
-    x_refs, (keyed_ref, row_ref), (out_ref, low_ref, high_ref) = refs[:4], refs[4:6], refs[6:9]
-    held, more, wide, line, low, high, in_sem, out_sem = refs[9:]
-    q = pl.program_id(0)
-    pairs = n * n
+def score_kernel(n, rows, meta_ref, *refs):
+    x_refs, (near_ref, far_ref, row_ref), (out_ref, low_ref, high_ref) = refs[:4], refs[4:7], refs[7:10]
+    held, more, wide, low, high, in_sem, out_sem = refs[10:]
+    step = pl.program_id(0)
     part = wide.shape[1]
     lanes = out_ref.shape[2]
     cuts = tile_cuts(lanes)
-
-    @pl.when(q == 0)
+    groups = lanes // BLK
+    at_size = n * groups
+    q = meta_ref[at_size + n] ^ reversed_bits(step, n)
+
+    @pl.when(step == 0)
     def _():
         load_tokens(
-            n, meta_ref[3 * pairs + n + 1], meta_ref[3 * pairs + n + 2], x_refs, held, more, wide, in_sem
-        )
-
-        @pl.loop(0, line.shape[0] // BLK)
-        def _(i):
-            line[pl.ds(pl.multiple_of(i * BLK, BLK), BLK), :] = jnp.zeros((BLK, part), line.dtype)
-
-    usual = min(32, window)
-    for s in range(n):
-        source = pl.multiple_of(meta_ref[q * n + s], BLK)
-        target = pl.multiple_of(meta_ref[pairs + q * n + s], BLK)
-        line[pl.ds(target, usual), :] = wide[pl.ds(source, usual), :]
-        if window > usual:
-
-            @pl.when(meta_ref[2 * pairs + q * n + s] > usual)
-            def _(source=source, target=target):
-                line[pl.ds(target + usual, window - usual), :] = wide[
-                    pl.ds(source + usual, window - usual), :
-                ]
-
-    kvh, per, _ = keyed_ref.shape
+            n, meta_ref[at_size + n + 1], meta_ref[at_size + n + 2], x_refs, held, more, wide, in_sem
+        )
+
+    kvh, per, _ = near_ref.shape
     group = per // rows
+    keyed = jnp.where(step < n // 2, near_ref[...], far_ref[...]).reshape(kvh * per, part)
 
     def copy(o, t):
         if t == 0:
@@ -195,15 +174,17 @@
 
     def one(t):
         here = slice(cuts[t], cuts[t + 1])
-        tile = line[here, :].astype(low.dtype)
-        if t == 0:
-            low[q] = tile
-        else:
-            high[q, cuts[t] - cuts[1] : cuts[t + 1] - cuts[1], :] = tile
+        buffer, base = (low, 0) if t == 0 else (high, cuts[1])
+        for i in range(cuts[t], cuts[t + 1], 2 * BLK):
+            pair = [
+                wide[pl.ds(pl.multiple_of(meta_ref[q * groups + i // BLK + j], BLK), BLK), :]
+                for j in range(2)
+            ]
+            buffer[q, i - base : i - base + 2 * BLK, :] = jnp.concatenate(pair).astype(low.dtype)
         copy(q, t).start()
         raw = lax.dot_general(
-            keyed_ref[...].reshape(kvh * per, part),
-            tile,
+            keyed,
+            buffer[q, cuts[t] - base : cuts[t + 1] - base, :],
             (((1,), (1,)), ((), ())),
             preferred_element_type=jnp.float32,
         ).reshape(kvh, rows, group, cuts[t + 1] - cuts[t])
@@ -215,14 +196,14 @@
 
     one(0)
     for t in range(1, len(cuts) - 1):
-        pl.when(meta_ref[3 * pairs + q] > cuts[t])(functools.partial(one, t))
-
-    @pl.when(q == n - 1)
+        pl.when(meta_ref[at_size + q] > cuts[t])(functools.partial(one, t))
+
+    @pl.when(step == n - 1)
     def _():
         for o in range(n):
             copy(o, 0).wait()
             for t in range(1, len(cuts) - 1):
-                pl.when(meta_ref[3 * pairs + o] > cuts[t])(lambda o=o, t=t: copy(o, t).wait())
+                pl.when(meta_ref[at_size + o] > cuts[t])(lambda o=o, t=t: copy(o, t).wait())
 
 
 def weight_kernel(scale, parts_ref, row_ref, top_ref, sum_ref, cached_ref, w_ref, kept_ref):
@@ -361,7 +342,7 @@
 
 def from_rest(held, n):
     k = n // 4
-    while k >= 1:
+    while k >= 2:
         held = jnp.concatenate([held, with_partner(held, k, n)])
         k //= 2
     return held
@@ -412,10 +393,15 @@
     size = half * 3 // 4
     extra = half - size
     at = jnp.stack([me, core])
-    dest = block_dest[:, 0]
-    packed = pack(x_prompt, block_fill, dest, at, n, 0, size)
+    pack_fill, pack_dest = block_fill, block_dest[:, 0]
+    packed = pack(x_prompt, pack_fill, pack_dest, at, n, 0, size)
+    dest = pack_dest
     far = with_partner(queries, n // 2, n)
-    packed, far = lax.optimization_barrier((packed, far))
+    packed, far, dest, block_row, block_fill, query, kv_cache, kv_weight = (
+        lax.optimization_barrier(
+            (packed, far, dest, block_row, block_fill, queries, kv_cache, kv_weight)
+        )
+    )
     mine = lax.all_to_all(packed, "pool", 0, 0, tiled=True).reshape(n * size, part)
 
     index = jnp.arange(n * blocks, dtype=jnp.int32)
@@ -438,6 +424,12 @@
     targets = jnp.sum(jnp.where(prior[None], runs_by[:, :, None], 0), 1)
     list_rows = jnp.sum(runs_by, 1)
     targets = targets.reshape(-1)
+    sources = by * tokens + offset // BLK * BLK
+    group_at = jnp.arange(n * lanes // BLK, dtype=jnp.int32) * BLK
+    skip = group_at[:, None] - (to * lanes + targets)[None, :]
+    group_rows = jnp.sum(
+        jnp.where((skip >= 0) & (skip < runs[None, :]), sources[None, :] + skip, 0), 1
+    )
     mine_pair = (dest * n + sender)[:, None] == pair[None, :]
     start = (
         dest * lanes
@@ -449,7 +441,6 @@
     inside = (spot >= start[None, :]) & (spot < (start + block_fill)[None, :])
     rowof = jnp.sum(jnp.where(inside, (block_row + 1)[None, :], 0), 1) - 1
     rowof = rowof.reshape(n, 1, lanes)
-    sources = by * tokens + offset // BLK * BLK
 
     most = jnp.max(jnp.sum(block_fill.reshape(n, blocks), 1))
     groups = lax.axis_size("groups")
@@ -462,7 +453,7 @@
     over = most > ntp * size
 
     def exchange_rest():
-        rest = pack(x_prompt, block_fill, dest, at, n, ntp * size, extra)
+        rest = pack(x_prompt, pack_fill, pack_dest, at, n, ntp * size, extra)
         rest = lax.all_to_all(rest, "pool", 0, 0, tiled=True).reshape(n * extra, part)
         return rest, lax.ppermute(rest, "tp", swap)
 
@@ -471,17 +462,25 @@
 
     more_mine, more_other = lax.cond(over, exchange_rest, no_rest)
     meta = jnp.concatenate(
-        [sources, targets, runs, list_rows, jnp.stack([me, core, over.astype(jnp.int32)])]
-    )
-
-    allq = from_rest(jnp.stack([queries, far]), n).reshape(n, rows, kvh, group, hd)
-    keyed = jnp.einsum(
-        "qrhgd,phd->hqrgp", allq, kv_weight[:, :, :hd], preferred_element_type=jnp.float32
-    ).astype(jnp.bfloat16)
-    keyed = keyed.reshape(kvh, n * per, part)
+        [group_rows, list_rows, jnp.stack([me, core, over.astype(jnp.int32)])]
+    )
+
+    keys = kv_weight[:, :, :hd]
+
+    def through_keys(held):
+        held = held.reshape(n // 2, rows, kvh, group, hd)
+        return (
+            jnp.einsum("qrhgd,phd->hqrgp", held, keys, preferred_element_type=jnp.float32)
+            .astype(jnp.bfloat16)
+            .reshape(kvh, n // 2 * per, part)
+        )
+
+    even = from_rest(jnp.stack([queries, far]), n)
+    keyed_even = through_keys(even)
+    keyed_odd = through_keys(with_partner(even, 1, n))
     values = kv_weight[:, :, hd:].transpose(1, 0, 2)
 
-    query = queries.reshape(rows, kvh, group, hd)
+    query = query.reshape(rows, kvh, group, hd)
     cache_scores = (
         jnp.einsum(
             "rhgd,rthd->rhgt", query, kv_cache[:, :, :, :hd], preferred_element_type=jnp.float32
@@ -503,39 +502,45 @@
     cache_sum = cache_sum.reshape(rows, heads, 1)
     cached = cached.reshape(rows, heads, hd)
 
-    mine, meta, list_rows, rowof, keyed, values, cache_top, cache_sum, cached = (
+    mine, meta, list_rows, rowof, keyed_even, values, cache_top, cache_sum, cached = (
         lax.optimization_barrier(
-            (mine, meta, list_rows, rowof, keyed, values, cache_top, cache_sum, cached)
+            (mine, meta, list_rows, rowof, keyed_even, values, cache_top, cache_sum, cached)
         )
     )
     other = lax.ppermute(mine, "tp", swap)
 
-    anywhere = pl.BlockSpec(memory_space=pl.ANY)
+    in_hbm = pl.BlockSpec(memory_space=pltpu.HBM)
     row_spec = pl.BlockSpec((1, 1, lanes), lambda q, m: (q, 0, 0))
     slot_spec = pl.BlockSpec((1, heads, lanes), lambda q, m: (q, 0, 0))
     slot_shape = jax.ShapeDtypeStruct((n, heads, lanes), jnp.bfloat16)
     cuts = tile_cuts(lanes)
     list_shapes = [(n, cuts[1], part), (n, lanes - cuts[1], part)]
     list_scratch = [pltpu.VMEM(shape, jnp.bfloat16) for shape in list_shapes]
-    at_me = 3 * n * n + n
+    at_me = n * lanes // BLK + n
+
+    def owner(i, m):
+        return m[at_me] ^ reversed_bits(i, n)
+
     partial_scores, low, high = pl.pallas_call(
-        functools.partial(score_kernel, n, rows, window),
+        functools.partial(score_kernel, n, rows),
         grid_spec=pltpu.PrefetchScalarGridSpec(
             num_scalar_prefetch=1,
             grid=(n,),
             in_specs=[
-                *[anywhere] * 4,
-                pl.BlockSpec(
-                    (kvh, per, part), lambda q, m: (0, reversed_bits(m[at_me] ^ q, n), 0)
-                ),
-                row_spec,
+                *[in_hbm] * 4,
+                pl.BlockSpec((kvh, per, part), lambda i, m: (0, jnp.minimum(i, n // 2 - 1), 0)),
+                pl.BlockSpec((kvh, per, part), lambda i, m: (0, jnp.maximum(i - n // 2, 0), 0)),
+                pl.BlockSpec((1, 1, lanes), lambda i, m: (owner(i, m), 0, 0)),
             ],
-            out_specs=[slot_spec, anywhere, anywhere],
+            out_specs=[
+                pl.BlockSpec((1, heads, lanes), lambda i, m: (owner(i, m), 0, 0)),
+                in_hbm,
+                in_hbm,
+            ],
             scratch_shapes=[
                 pltpu.VMEM((ntp, n * size, part), jnp.bfloat16),
                 pltpu.VMEM((ntp, n * extra, part), jnp.bfloat16),
-                pltpu.VMEM((n * tokens + window, part), jnp.float32),
-                pltpu.VMEM((lanes + window, part), jnp.float32),
+                pltpu.VMEM((n * tokens, part), jnp.float32),
                 *list_scratch,
                 pltpu.SemaphoreType.DMA((ntp, 4)),
                 pltpu.SemaphoreType.DMA((n, len(cuts) - 1)),
@@ -545,9 +550,9 @@
             slot_shape,
             *[jax.ShapeDtypeStruct(shape, jnp.bfloat16) for shape in list_shapes],
         ],
-        compiler_params=pltpu.CompilerParams(vmem_limit_bytes=34 * MIB),
+        compiler_params=pltpu.CompilerParams(vmem_limit_bytes=32 * MIB),
         name="prompt_scores",
-    )(meta, mine, other, more_mine, more_other, keyed, rowof)
+    )(meta, mine, other, more_mine, more_other, keyed_even, keyed_odd, rowof)
 
     parts = lax.all_to_all(partial_scores, "pool", 0, 0, tiled=True)
     my_rows = lax.dynamic_index_in_dim(rowof, me, 0, keepdims=False)
@@ -567,8 +572,8 @@
             in_specs=[
                 slot_spec,
                 row_spec,
-                anywhere,
-                anywhere,
+                in_hbm,
+                in_hbm,
                 pl.BlockSpec((kvh, part, hd), lambda q, m: (0, 0, 0)),
             ],
             out_specs=pl.BlockSpec((n, kvh, per, hd), lambda q, m: (0, 0, 0, 0)),

time: 164 us -> 163 us (level)
  waiting for transfers between devices: 39.8 us -> 48.9 us
  local copies, waits for them, and re-layouts: 24 us -> 18.5 us
  matrix products: 5.72 us -> 8.39 us
  starting transfers between devices: 26.4 us -> 24.3 us
  Pallas kernels: 26.8 us -> 24.9 us
    all_to_all x1, waiting for transfers between devices: 0.01 us -> 22.4 us  [local(): lax.all_to_all(packed, 'pool', 0, 0, tiled=True).reshape(n * size, part)]
    ppermute x10, waiting for transfers between devices: 26.4 us -> 13.1 us  [with_partner(): return lax.ppermute(x, 'pool', [(i, i ^ k) for i in range(n)])]
    slice x2 -> x0, local copies, waits for them, and re-layouts: 6.12 us -> none  [the longest x1 4.04 us: local(): kv_cache[:, :, :, hd:]]
    optimization_barrier x2 -> x4, local copies, waits for them, and re-layouts: 0.26 us -> 5.61 us  [the longest x2 5.35 us: local(): lax.optimization_barrier((packed, far, dest, block_row, block_fill, queri...]
    unnamed x27 -> x26, local copies, waits for them, and re-layouts: 14.6 us -> 10.4 us
    ppermute x1, waiting for transfers between devices: 0.01 us -> 2.16 us  [local(): lax.ppermute(most, 'groups', [(i, i ^ k) for i in range(groups)])]
    pallas_call x1, Pallas kernels: 11.3 us -> 9.25 us  [local(): pl.pallas_call(functools.partial(score_kernel, n, rows), grid_spec=pltpu....]
    all_to_all x1, starting transfers between devices: 5.58 us -> 3.62 us  [local(): parts = lax.all_to_all(partial_scores, 'pool', 0, 0, tiled=True)]
  transfers between devices with their start and end apart: 15 -> 15, of which waited for: 9 -> 9; matrix products, arithmetic and copies ran while one was open for 14% -> 10% of each run, Pallas kernels for 3% -> 3%
where the time goes in v7:
time: 163 us
  waiting for transfers between devices  48.9 us (30%)
  blocking collectives  30.7 us (19%)
  Pallas kernels  24.9 us (15%)
  starting transfers between devices  24.3 us (15%)
  local copies, waits for them, and re-layouts  18.5 us (11%)
  matrix products  8.39 us (5%)
  other arithmetic  6.09 us (4%)
    all_to_all x1, waiting for transfers between devices, local(): lax.all_to_all(packed, 'pool', 0, 0, tiled=True).reshape(n * size, part)  22.4 us
    all_to_all x1, blocking collectives, local(): term_parts = lax.all_to_all(terms, 'pool', 0, 0, tiled=True)  16.8 us
    ppermute x10, starting transfers between devices, with_partner(): return lax.ppermute(x, 'pool', [(i, i ^ k) for i in range(n)])  14.8 us
    all_to_all x1, blocking collectives, local(): all_weights = lax.all_to_all(weights, 'pool', 0, 0, tiled=True)  13.9 us
    ppermute x10, waiting for transfers between devices, with_partner(): return lax.ppermute(x, 'pool', [(i, i ^ k) for i in range(n)])  13.1 us
    unnamed x26, local copies, waits for them, and re-layouts  10.4 us
    all_to_all x1, waiting for transfers between devices, local(): parts = lax.all_to_all(partial_scores, 'pool', 0, 0, tiled=True)  9.93 us
    pallas_call x1, Pallas kernels, local(): pl.pallas_call(functools.partial(score_kernel, n, rows), grid_spec=pltpu....  9.25 us
  transfers between devices with their start and end apart: 15, of which 9 were waited for; matrix products, arithmetic and copies ran while one was open for 10% of the time, Pallas kernels for 3%

profile of v7, /device:TPU:0, one launch (start us, length us, event | category | flops | bytes accessed | tf_op | source)
XLA Modules:
  0.0 163.1 jit_solution(2237110436340812317)
XLA Ops:
  0.0 4.0 %collective-permute-start.1 = (bf16[8,32,128]{2,1,0:T(8,128)(2,1)}, bf16[8,32,128]{2,1,0:T(8,128)(2,1)S(1)}, u32[]{:S(2)}, u32[]{:S(2)}) collective-permute-start(bf16[8,32,128]{2,1,0:T(8,128)(2,1)} %param.16), channel_id=1, source_target_pairs={{0,8},{2,10},{4,12},{6,14},{8,0},{10,2},{12,4},{14,6},{1,9},{3,11}... | collective-permute-start | bytes 196616 | tf_op jit(solution)/shard_map/ppermute | solution.py:340
  4.0 0.7 iota_compare_fusion.4
  4.9 4.5 %pack_live_tokens.3 = bf16[8,96,1024]{2,1,0:T(8,128)(2,1)} custom-call(s32[2]{0:T(128)S(1)} %pad_add_fusion.at_ref, s32[256]{0:T(256)} %fill_ref.1, s32[256]{0:T(256)} %bitcast.48, bf16[256,8192]{1,0:T(8,128)(2,1)} %x_ref.1), custom_call_target="tpu_custom_call" | custom-call | tf_op jit(solution)/shard_map/pack_live_tokens/pallas_call | solution.py:70
  9.4 0.2 select_reduce_fusion.5
  9.6 0.1 reduce_sum.104
  9.8 0.1 fusion.38
  9.9 0.1 select_reduce_fusion.6
  10.1 5.1 %copy.29 = bf16[8,256,4,256]{3,1,2,0:T(8,128)(2,1)} copy(bf16[8,256,4,256]{3,2,1,0:T(4,128)(2,1)} %param.17) | data formatting | bytes 8388608 | tf_op jit(solution)/shard_map/optimization_barrier | solution.py:401
  15.2 0.7 pad_maximum_fusion.2
  15.9 1.6 collective-permute-start.3
  17.4 0.3 copy.27
  17.7 4.3 %all-to-all-start.1 = ((bf16[8,96,1024]{2,1,0:T(8,128)(2,1)}), bf16[8,96,1024]{2,1,0:T(8,128)(2,1)}, u32[]{:S(2)}, u32[]{:S(2)}) async-start(bf16[8,96,1024]{2,1,0:T(8,128)(2,1)} %pack_live_tokens.3), calls=%async_computation.1 | async-start | bytes 3145728 | tf_op jit(solution)/shard_map/all_to_all | solution.py:405
  22.0 0.1 select_reduce_fusion.3
  22.1 0.3 select_reduce_fusion.2
  22.5 1.0 select_reduce_fusion
  23.5 2.3 %fusion.40 = (f32[8,4,8]{2,1,0:T(4,128)S(1)}, f32[8,4,8,256]{3,2,1,0:T(8,128)S(1)}) fusion(bf16[8,256,4,256]{3,1,2,0:T(8,128)(2,1)} %copy.29, bf16[8,32,128]{2,1,0:T(8,128)(2,1)S(1)} %copy-done.7, pred[8,256]{1,0:T(8,128)(4,1)S(1)} %iota_compare_fusion.4), kind=kOutput, calls=%fused_computation.97 | convolution fusion | flops 16973568 | bytes 2427904 | tf_op jit(solution)/shard_map/rhgd,rthd->rhgt/dot_general | solution.py:485
  25.8 2.0 %fusion.11.cached_ref = f32[8,32,128]{2,1,0:T(8,128)S(1)} fusion(bf16[8,256,4,256]{3,1,2,0:T(8,128)(2,1)} %copy.29, f32[8,4,8,256]{3,2,1,0:T(8,128)S(1)} %get-tuple-element.80, f32[8,4,8]{2,1,0:T(4,128)S(1)} %get-tuple-element.79), kind=kOutput, calls=%fused_computation.12 | convolution fusion | flops 16908288 | bytes 2491392 | tf_op jit(solution)/shard_map/rhgt,rthd->rhgd/dot_general | solution.py:495
  27.9 0.2 slice_bitcast_fusion.value_ref
  28.1 0.2 fusion.18
  28.4 0.1 reshape_broadcast_in_dim.6
  28.4 0.1 reduce_sum.110
  28.6 0.7 reduce_max.18
  29.2 1.5 collective-permute-start.2
  30.8 0.1 fusion.20
  30.9 2.2 %collective-permute-done.2 = s32[]{:T(128)} collective-permute-done((s32[]{:T(128)}, s32[]{:T(128)}, u32[]{:S(2)}, u32[]{:S(2)}) %collective-permute-start.2) | collective-permute-done | bytes 36 | tf_op jit(solution)/shard_map/ppermute | solution.py:450
  34.3 0.1 concatenate.16.meta_ref
  34.4 2.0 %convolution_convert_fusion.1 = bf16[4,4,8,8,1024]{4,3,2,1,0:T(8,128)(2,1)S(1)} fusion(bf16[1024,4,256]{2,0,1:T(8,128)(2,1)} %copy-done.5, bf16[2,8,4,8,128]{4,3,2,1,0:T(8,128)(2,1)} %bitcast.11, bf16[1,8,4,8,128]{4,3,2,1,0:T(8,128)(2,1)S(1)} %bitcast.46, bf16[1,8,4,8,128]{4,3,2,1,0:T(8,128)(2,1)S(1)} %bitcast.43), kind=kOutput, calls=%fused_computation.9 | convolution fusion | flops 269746176 | bytes 3407872 | tf_op jit(solution)/shard_map/qrhgd,phd->hqrgp/dot_general | solution.py:473
  36.4 22.4 %all-to-all-done.1 = bf16[8,96,1024]{2,1,0:T(8,128)(2,1)} async-done(((bf16[8,96,1024]{2,1,0:T(8,128)(2,1)}), bf16[8,96,1024]{2,1,0:T(8,128)(2,1)}, u32[]{:S(2)}, u32[]{:S(2)}) %all-to-all-start.1) | async-done | bytes 1572896 | tf_op jit(solution)/shard_map/all_to_all | solution.py:405
  58.8 1.6 %pad_maximum_fusion.1 = bf16[4,8,32,128]{3,2,1,0:T(8,128)(2,1)} fusion(bf16[2,8,32,128]{3,2,1,0:T(8,128)(2,1)} %collective-permute-done.3, bf16[1,8,32,128]{3,2,1,0:T(8,128)(2,1)S(1)} %bitcast.47, bf16[1,8,32,128]{3,2,1,0:T(8,128)(2,1)S(1)} %bitcast.44), kind=kLoop, calls=%fused_computation.21 | loop fusion | flops 262144 | bytes 524288 | tf_op jit(solution)/shard_map/concatenate | solution.py:346
  60.4 1.4 collective-permute-start.5
  61.8 1.7 %conditional.1 = (bf16[256,1024]{1,0:T(8,128)(2,1)}, bf16[256,1024]{1,0:T(8,128)(2,1)}) conditional(s32[]{:T(128)} %convert_element_type.13, () %tuple.17, (s32[2]{0:T(128)S(1)}, s32[256]{0:T(256)S(1)}, s32[256]{0:T(256)S(1)}, bf16[256,8192]{1,0:T(8,128)(2,1)}) %tuple.30), branch_computations={%region_13.14_spmd, %region_14.15_spmd} | conditional | bytes 3145784 | solution.py:463
  61.8 0.9 broadcast.391
  62.7 0.9 broadcast.391.clone
  63.5 5.9 %collective-permute-done.5 = bf16[4,8,32,128]{3,2,1,0:T(8,128)(2,1)} collective-permute-done((bf16[4,8,32,128]{3,2,1,0:T(8,128)(2,1)}, bf16[4,8,32,128]{3,2,1,0:T(8,128)(2,1)}, u32[]{:S(2)}, u32[]{:S(2)}) %collective-permute-start.5) | collective-permute-done | bytes 262176 | tf_op jit(solution)/shard_map/ppermute | solution.py:340
  69.4 2.0 %convolution_convert_fusion = bf16[4,4,8,8,1024]{4,3,2,1,0:T(8,128)(2,1)S(1)} fusion(bf16[1024,4,256]{2,0,1:T(8,128)(2,1)} %copy-done.5, bf16[4,8,32,128]{3,2,1,0:T(8,128)(2,1)} %collective-permute-done.5), kind=kOutput, calls=%fused_computation.8 | convolution fusion | flops 269484032 | bytes 3407872 | tf_op jit(solution)/shard_map/qrhgd,phd->hqrgp/dot_general | solution.py:473
  71.5 9.3 %prompt_scores.1 = (bf16[8,32,640]{2,1,0:T(8,128)(2,1)S(1)}, bf16[8,256,1024]{2,1,0:T(8,128)(2,1)S(1)}, bf16[8,384,1024]{2,1,0:T(8,128)(2,1)S(1)}) custom-call(s32[651]{0:T(1024)S(1)} %concatenate.16.meta_ref, bf16[768,1024]{1,0:T(8,128)(2,1)} %bitcast.4.refs_0_, bf16[768,1024]{1,0:T(8,128)(2,1)} %collective-permute-done.4.refs_1_, ...), custom_call_target="tpu_custom_call" | custom-call | tf_op jit(solution)/shard_map/prompt_scores/pallas_call | solution.py:524
  80.7 2.6 %copy-done = bf16[8,384,1024]{2,1,0:T(8,128)(2,1)} copy-done((bf16[8,384,1024]{2,1,0:T(8,128)(2,1)}, bf16[8,384,1024]{2,1,0:T(8,128)(2,1)S(1)}, u32[]{:S(2)}) %copy-start) | copy-done | bytes 6291480
  83.4 2.0 %copy-done.2 = bf16[8,256,1024]{2,1,0:T(8,128)(2,1)} copy-done((bf16[8,256,1024]{2,1,0:T(8,128)(2,1)}, bf16[8,256,1024]{2,1,0:T(8,128)(2,1)S(1)}, u32[]{:S(2)}) %copy-start.2) | copy-done | bytes 4194328
  85.4 0.7 copy-done.4
  86.1 3.6 %all-to-all-start.2 = ((bf16[8,32,640]{2,1,0:T(8,128)(2,1)}), bf16[8,32,640]{2,1,0:T(8,128)(2,1)S(1)}, u32[]{:S(2)}, u32[]{:S(2)}) async-start(bf16[8,32,640]{2,1,0:T(8,128)(2,1)} %copy-done.4), calls=%async_computation.2 | async-start | bytes 655360 | tf_op jit(solution)/shard_map/all_to_all | solution.py:557
  89.8 0.1 copy.32.top_ref
  89.9 0.1 copy.33.sum_ref
  90.0 9.9 %all-to-all-done.2.parts_ref = bf16[8,32,640]{2,1,0:T(8,128)(2,1)S(1)} async-done(((bf16[8,32,640]{2,1,0:T(8,128)(2,1)}), bf16[8,32,640]{2,1,0:T(8,128)(2,1)S(1)}, u32[]{:S(2)}, u32[]{:S(2)}) %all-to-all-start.2) | async-done | bytes 327712 | tf_op jit(solution)/shard_map/all_to_all | solution.py:557
  100.0 1.2 softmax_weights.1
  101.2 13.9 %all_to_all.25.w_ref = bf16[8,32,640]{2,1,0:T(8,128)(2,1)S(1)} all-to-all(bf16[8,32,640]{2,1,0:T(8,128)(2,1)S(1)} %get-tuple-element.62), channel_id=1, replica_groups=mesh['groups'=2,'pool'=8,'tp'=2] {'pool'}, dimensions={0} | all-to-all | bytes 655360 | tf_op jit(solution)/shard_map/all_to_all | solution.py:566
  115.2 2.8 %copy-done.1 = bf16[8,384,1024]{2,1,0:T(8,128)(2,1)S(1)} copy-done((bf16[8,384,1024]{2,1,0:T(8,128)(2,1)S(1)}, bf16[8,384,1024]{2,1,0:T(8,128)(2,1)}, u32[]{:S(2)}) %copy-start.1) | copy-done | bytes 6291480
  117.9 2.2 %copy-done.3 = bf16[8,256,1024]{2,1,0:T(8,128)(2,1)S(1)} copy-done((bf16[8,256,1024]{2,1,0:T(8,128)(2,1)S(1)}, bf16[8,256,1024]{2,1,0:T(8,128)(2,1)}, u32[]{:S(2)}) %copy-start.3) | copy-done | bytes 4194328
  120.1 6.2 %weighted_values.1 = bf16[8,4,64,128]{3,2,1,0:T(8,128)(2,1)S(1)} custom-call(s32[8]{0:T(128)S(1)} %get-tuple-element.51.size_ref, bf16[8,32,640]{2,1,0:T(8,128)(2,1)S(1)} %all_to_all.25.w_ref, s32[8,1,640]{2,1,0:T(1,128)S(1)} %bitcast.41, bf16[8,256,1024]{2,1,0:T(8,128)(2,1)S(1)} %copy-done.3, bf16[8,384,1024]{2,1,0:T(8,128)(2,1)S(1)} %copy-done.1, ...), custom_call_target="tpu_custom_call" | custom-call | tf_op jit(solution)/shard_map/weighted_values/pallas_call | solution.py:567
  126.4 16.8 %all_to_all.26.parts_ref = bf16[8,4,64,128]{3,2,1,0:T(8,128)(2,1)S(1)} all-to-all(bf16[8,4,64,128]{3,2,1,0:T(8,128)(2,1)S(1)} %weighted_values.1), channel_id=1, replica_groups=mesh['groups'=2,'pool'=8,'tp'=2] {'pool'}, dimensions={0} | all-to-all | bytes 1048576 | tf_op jit(solution)/shard_map/all_to_all | solution.py:592
  143.1 0.1 attended_sum.1.refs_0_
  143.2 0.8 collective-permute-start.10
  144.0 2.4 %collective-permute-start.11 = (bf16[8,4096]{1,0:T(8,128)(2,1)S(1)}, bf16[8,4096]{1,0:T(8,128)(2,1)S(1)}, u32[]{:S(2)}, u32[]{:S(2)}) collective-permute-start(bf16[8,4096]{1,0:T(8,128)(2,1)S(1)} %attended_sum.1.refs_0_), channel_id=1, source_target_pairs={{0,12},{2,14},{4,8},{6,10},{8,4},{10,6},{12,0},{14,2},{1,13},{3,15... | collective-permute-start | bytes 196616 | tf_op jit(solution)/shard_map/ppermute | solution.py:340
  146.4 2.7 %collective-permute-start.12 = (bf16[8,4096]{1,0:T(8,128)(2,1)S(1)}, bf16[8,4096]{1,0:T(8,128)(2,1)S(1)}, u32[]{:S(2)}, u32[]{:S(2)}) collective-permute-start(bf16[8,4096]{1,0:T(8,128)(2,1)S(1)} %attended_sum.1.refs_0_), channel_id=1, source_target_pairs={{0,14},{2,12},{4,10},{6,8},{8,6},{10,4},{12,2},{14,0},{1,15},{3,13... | collective-permute-start | bytes 196616 | tf_op jit(solution)/shard_map/ppermute | solution.py:340
  149.1 0.2 collective-permute-start.6
  149.3 0.4 collective-permute-start.7
  149.7 2.6 %collective-permute-done.10.refs_5_ = bf16[8,4096]{1,0:T(8,128)(2,1)S(1)} collective-permute-done((bf16[8,4096]{1,0:T(8,128)(2,1)S(1)}, bf16[8,4096]{1,0:T(8,128)(2,1)S(1)}, u32[]{:S(2)}, u32[]{:S(2)}) %collective-permute-start.10) | collective-permute-done | bytes 65568 | tf_op jit(solution)/shard_map/ppermute | solution.py:340
  152.3 0.3 collective-permute-start.8
  152.6 1.0 collective-permute-start.9
  153.6 0.3 collective-permute-done.12.refs_7_
  153.9 0.7 collective-permute-done.6.refs_1_
  154.7 3.5 %collective-permute-done.8.refs_3_ = bf16[8,4096]{1,0:T(8,128)(2,1)S(1)} collective-permute-done((bf16[8,4096]{1,0:T(8,128)(2,1)S(1)}, bf16[8,4096]{1,0:T(8,128)(2,1)S(1)}, u32[]{:S(2)}, u32[]{:S(2)}) %collective-permute-start.8) | collective-permute-done | bytes 65568 | tf_op jit(solution)/shard_map/ppermute | solution.py:340
  158.2 2.9 %output_projection.1 = (f32[64,512]{1,0:T(8,128)S(1)}, f32[64,512]{1,0:T(8,128)S(1)}) custom-call(s32[1]{0:T(128)} %bitcast.2.core_ref, bf16[8,4096]{1,0:T(8,128)(2,1)S(1)} %attended_sum.1.refs_0_, bf16[8,4096]{1,0:T(8,128)(2,1)S(1)} %collective-permute-done.6.refs_1_, bf16[8,4096]{1,0:T(8,128)(2,1)S(1)} %collective-permute-done.7.refs_2_, ...), custom_call_target="tpu_custom_call" | custom-call | tf_op jit(solution)/shard_map/output_projection/pallas_call | solution.py:604
  161.2 1.3 collective-permute-done.13.got_ref
  162.5 0.6 order_rows.1
  (45 shorter events, 0.6 us)
Async XLA Ops:
  0.0 9.4 %collective-permute-start.1 = (bf16[8,32,128]{2,1,0:T(8,128)(2,1)}, bf16[8,32,128]{2,1,0:T(8,128)(2,1)S(1)}, u32[]{:S(2)}, u32[]{:S(2)}) collective-permute-start(bf16[8,32,128]{2,1,0:T(8,128)(2,1)} %param.16), channel_id=1, source_target_pairs={{0,8},{2,10},{4,12},{6,14},{8,0},{10,2},{12,4},{14,6},{1,9},{3,11}... | collective-permute-start | bytes 196616 | tf_op jit(solution)/shard_map/ppermute | solution.py:340
  4.9 4.6 %copy-start.8 = (s32[256,1]{0,1:T(1,128)S(1)}, s32[256,1]{0,1:T(1,128)}, u32[]{:S(2)}) copy-start(s32[256,1]{0,1:T(1,128)} %param.13) | copy-start | bytes 3076
  4.9 4.6 %copy-start.9 = (s32[256]{0:T(256)S(1)}, s32[256]{0:T(256)}, u32[]{:S(2)}) copy-start(s32[256]{0:T(256)} %fill_ref.1) | copy-start | bytes 3076
  4.9 5.3 %copy-start.10 = (s32[256]{0:T(256)S(1)}, s32[256]{0:T(256)}, u32[]{:S(2)}) copy-start(s32[256]{0:T(256)} %param.14) | copy-start | bytes 3076
  10.1 5.1 %copy-start.7 = (bf16[8,32,128]{2,1,0:T(8,128)(2,1)S(1)}, bf16[8,32,128]{2,1,0:T(8,128)(2,1)}, u32[]{:S(2)}) copy-start(bf16[8,32,128]{2,1,0:T(8,128)(2,1)} %param.16) | copy-start | bytes 196612
  10.1 7.3 %copy-start.6 = (bf16[1024,4,256]{2,1,0:T(4,128)(2,1)S(1)}, bf16[1024,4,256]{2,1,0:T(4,128)(2,1)}, u32[]{:S(2)}) copy-start(bf16[1024,4,256]{2,1,0:T(4,128)(2,1)} %param.12) | copy-start | bytes 6291460
  15.9 18.5 %collective-permute-start.3 = (bf16[2,8,32,128]{3,2,1,0:T(8,128)(2,1)}, bf16[2,8,32,128]{3,2,1,0:T(8,128)(2,1)}, u32[]{:S(2)}, u32[]{:S(2)}) collective-permute-start(bf16[2,8,32,128]{3,2,1,0:T(8,128)(2,1)} %pad_maximum_fusion.2), channel_id=1, source_target_pairs={{0,4},{2,6},{4,0},{6,2},{8,12},{10,14},{12,8},{14,10},{1,5},{3,7},... | collective-permute-start | bytes 393224 | tf_op jit(solution)/shard_map/ppermute | solution.py:340
  17.7 10.1 %copy-start.5 = (bf16[1024,4,256]{2,0,1:T(8,128)(2,1)}, bf16[1024,4,256]{2,0,1:T(8,128)(2,1)S(1)}, u32[]{:S(2)}) copy-start(bf16[1024,4,256]{2,0,1:T(8,128)(2,1)S(1)} %copy.27) | copy-start | bytes 6291460
  17.7 41.0 %all-to-all-start.1 = ((bf16[8,96,1024]{2,1,0:T(8,128)(2,1)}), bf16[8,96,1024]{2,1,0:T(8,128)(2,1)}, u32[]{:S(2)}, u32[]{:S(2)}) async-start(bf16[8,96,1024]{2,1,0:T(8,128)(2,1)} %pack_live_tokens.3), calls=%async_computation.1 | async-start | bytes 3145728 | tf_op jit(solution)/shard_map/all_to_all | solution.py:405
  29.2 3.9 %collective-permute-start.2 = (s32[]{:T(128)}, s32[]{:T(128)}, u32[]{:S(2)}, u32[]{:S(2)}) collective-permute-start(s32[]{:T(128)} %reduce_max.18), channel_id=1, source_target_pairs={{0,16},{16,0},{1,17},{17,1},{2,18},{18,2},{3,19},{19,3},{4,20},{20... | collective-permute-start | bytes 20 | tf_op jit(solution)/shard_map/ppermute | solution.py:450
  58.8 12.7 %collective-permute-start.4 = (bf16[768,1024]{1,0:T(8,128)(2,1)}, bf16[768,1024]{1,0:T(8,128)(2,1)}, u32[]{:S(2)}, u32[]{:S(2)}) collective-permute-start(bf16[768,1024]{1,0:T(8,128)(2,1)} %bitcast.4.refs_0_), channel_id=1, source_target_pairs={{0,1},{1,0},{2,3},{3,2},{4,5},{5,4},{6,7},{7,6},{8,9},{9,8},{10,11... | collective-permute-start | bytes 4718600 | tf_op jit(solution)/shard_map/ppermute | solution.py:510
  60.4 9.0 %collective-permute-start.5 = (bf16[4,8,32,128]{3,2,1,0:T(8,128)(2,1)}, bf16[4,8,32,128]{3,2,1,0:T(8,128)(2,1)}, u32[]{:S(2)}, u32[]{:S(2)}) collective-permute-start(bf16[4,8,32,128]{3,2,1,0:T(8,128)(2,1)} %pad_maximum_fusion.1), channel_id=1, source_target_pairs={{0,2},{2,0},{4,6},{6,4},{8,10},{10,8},{12,14},{14,12},{1,3},{3,1},... | collective-permute-start | bytes 786440 | tf_op jit(solution)/shard_map/ppermute | solution.py:340
  80.7 2.7 %copy-start = (bf16[8,384,1024]{2,1,0:T(8,128)(2,1)}, bf16[8,384,1024]{2,1,0:T(8,128)(2,1)S(1)}, u32[]{:S(2)}) copy-start(bf16[8,384,1024]{2,1,0:T(8,128)(2,1)S(1)} %get-tuple-element.64.high_ref) | copy-start | bytes 18874372
  83.4 2.0 %copy-start.2 = (bf16[8,256,1024]{2,1,0:T(8,128)(2,1)}, bf16[8,256,1024]{2,1,0:T(8,128)(2,1)S(1)}, u32[]{:S(2)}) copy-start(bf16[8,256,1024]{2,1,0:T(8,128)(2,1)S(1)} %get-tuple-element.63.low_ref) | copy-start | bytes 12582916
  85.4 0.7 copy-start.4
  86.1 13.8 %all-to-all-start.2 = ((bf16[8,32,640]{2,1,0:T(8,128)(2,1)}), bf16[8,32,640]{2,1,0:T(8,128)(2,1)S(1)}, u32[]{:S(2)}, u32[]{:S(2)}) async-start(bf16[8,32,640]{2,1,0:T(8,128)(2,1)} %copy-done.4), calls=%async_computation.2 | async-start | bytes 655360 | tf_op jit(solution)/shard_map/all_to_all | solution.py:557
  100.0 58.2 %slice-start = ((s8[8388608]{0:T(1024)(128)(4,1)}), s8[4194304]{0:T(1024)(128)(4,1)S(1)}, s32[]{:S(2)}) async-start(s8[8388608]{0:T(1024)(128)(4,1)} %bitcast.37), calls=%async_computation.5 | async-start | bytes 8388608
  115.2 2.8 %copy-start.1 = (bf16[8,384,1024]{2,1,0:T(8,128)(2,1)S(1)}, bf16[8,384,1024]{2,1,0:T(8,128)(2,1)}, u32[]{:S(2)}) copy-start(bf16[8,384,1024]{2,1,0:T(8,128)(2,1)} %copy-done) | copy-start | bytes 18874372
  117.9 2.2 %copy-start.3 = (bf16[8,256,1024]{2,1,0:T(8,128)(2,1)S(1)}, bf16[8,256,1024]{2,1,0:T(8,128)(2,1)}, u32[]{:S(2)}) copy-start(bf16[8,256,1024]{2,1,0:T(8,128)(2,1)} %copy-done.2) | copy-start | bytes 12582916
  120.1 38.0 %slice-start.1 = ((s8[8388608]{0:T(1024)(128)(4,1)}), s8[4194304]{0:T(1024)(128)(4,1)S(1)}, s32[]{:S(2)}) async-start(s8[8388608]{0:T(1024)(128)(4,1)} %bitcast.37), calls=%async_computation.6 | async-start | bytes 8388608
  143.2 9.1 %collective-permute-start.10 = (bf16[8,4096]{1,0:T(8,128)(2,1)S(1)}, bf16[8,4096]{1,0:T(8,128)(2,1)S(1)}, u32[]{:S(2)}, u32[]{:S(2)}) collective-permute-start(bf16[8,4096]{1,0:T(8,128)(2,1)S(1)} %attended_sum.1.refs_0_), channel_id=1, source_target_pairs={{0,10},{2,8},{4,14},{6,12},{8,2},{10,0},{12,6},{14,4},{1,11},{3,9}... | collective-permute-start | bytes 196616 | tf_op jit(solution)/shard_map/ppermute | solution.py:340
  144.0 8.6 %collective-permute-start.11 = (bf16[8,4096]{1,0:T(8,128)(2,1)S(1)}, bf16[8,4096]{1,0:T(8,128)(2,1)S(1)}, u32[]{:S(2)}, u32[]{:S(2)}) collective-permute-start(bf16[8,4096]{1,0:T(8,128)(2,1)S(1)} %attended_sum.1.refs_0_), channel_id=1, source_target_pairs={{0,12},{2,14},{4,8},{6,10},{8,4},{10,6},{12,0},{14,2},{1,13},{3,15... | collective-permute-start | bytes 196616 | tf_op jit(solution)/shard_map/ppermute | solution.py:340
  146.4 7.5 %collective-permute-start.12 = (bf16[8,4096]{1,0:T(8,128)(2,1)S(1)}, bf16[8,4096]{1,0:T(8,128)(2,1)S(1)}, u32[]{:S(2)}, u32[]{:S(2)}) collective-permute-start(bf16[8,4096]{1,0:T(8,128)(2,1)S(1)} %attended_sum.1.refs_0_), channel_id=1, source_target_pairs={{0,14},{2,12},{4,10},{6,8},{8,6},{10,4},{12,2},{14,0},{1,15},{3,13... | collective-permute-start | bytes 196616 | tf_op jit(solution)/shard_map/ppermute | solution.py:340
  149.1 5.6 %collective-permute-start.6 = (bf16[8,4096]{1,0:T(8,128)(2,1)S(1)}, bf16[8,4096]{1,0:T(8,128)(2,1)S(1)}, u32[]{:S(2)}, u32[]{:S(2)}) collective-permute-start(bf16[8,4096]{1,0:T(8,128)(2,1)S(1)} %attended_sum.1.refs_0_), channel_id=1, source_target_pairs={{0,2},{2,0},{4,6},{6,4},{8,10},{10,8},{12,14},{14,12},{1,3},{3,1},... | collective-permute-start | bytes 196616 | tf_op jit(solution)/shard_map/ppermute | solution.py:340
  149.3 5.4 %collective-permute-start.7 = (bf16[8,4096]{1,0:T(8,128)(2,1)S(1)}, bf16[8,4096]{1,0:T(8,128)(2,1)S(1)}, u32[]{:S(2)}, u32[]{:S(2)}) collective-permute-start(bf16[8,4096]{1,0:T(8,128)(2,1)S(1)} %attended_sum.1.refs_0_), channel_id=1, source_target_pairs={{0,4},{2,6},{4,0},{6,2},{8,12},{10,14},{12,8},{14,10},{1,5},{3,7},... | collective-permute-start | bytes 196616 | tf_op jit(solution)/shard_map/ppermute | solution.py:340
  152.3 5.9 %collective-permute-start.8 = (bf16[8,4096]{1,0:T(8,128)(2,1)S(1)}, bf16[8,4096]{1,0:T(8,128)(2,1)S(1)}, u32[]{:S(2)}, u32[]{:S(2)}) collective-permute-start(bf16[8,4096]{1,0:T(8,128)(2,1)S(1)} %attended_sum.1.refs_0_), channel_id=1, source_target_pairs={{0,6},{2,4},{4,2},{6,0},{8,14},{10,12},{12,10},{14,8},{1,7},{3,5},... | collective-permute-start | bytes 196616 | tf_op jit(solution)/shard_map/ppermute | solution.py:340
  152.6 5.6 %collective-permute-start.9 = (bf16[8,4096]{1,0:T(8,128)(2,1)S(1)}, bf16[8,4096]{1,0:T(8,128)(2,1)S(1)}, u32[]{:S(2)}, u32[]{:S(2)}) collective-permute-start(bf16[8,4096]{1,0:T(8,128)(2,1)S(1)} %attended_sum.1.refs_0_), channel_id=1, source_target_pairs={{0,8},{2,10},{4,12},{6,14},{8,0},{10,2},{12,4},{14,6},{1,9},{3,11}... | collective-permute-start | bytes 196616 | tf_op jit(solution)/shard_map/ppermute | solution.py:340
  161.1 1.4 collective-permute-start.13

commit v8 on v7

--- a/solution.py
+++ b/solution.py
@@ -397,10 +397,8 @@
     packed = pack(x_prompt, pack_fill, pack_dest, at, n, 0, size)
     dest = pack_dest
     far = with_partner(queries, n // 2, n)
-    packed, far, dest, block_row, block_fill, query, kv_cache, kv_weight = (
-        lax.optimization_barrier(
-            (packed, far, dest, block_row, block_fill, queries, kv_cache, kv_weight)
-        )
+    packed, far, dest, block_row, block_fill, query = lax.optimization_barrier(
+        (packed, far, dest, block_row, block_fill, queries)
     )
     mine = lax.all_to_all(packed, "pool", 0, 0, tiled=True).reshape(n * size, part)
 
@@ -477,7 +475,7 @@
 
     even = from_rest(jnp.stack([queries, far]), n)
     keyed_even = through_keys(even)
-    keyed_odd = through_keys(with_partner(even, 1, n))
+    odd = with_partner(even, 1, n)
     values = kv_weight[:, :, hd:].transpose(1, 0, 2)
 
     query = query.reshape(rows, kvh, group, hd)
@@ -502,12 +500,13 @@
     cache_sum = cache_sum.reshape(rows, heads, 1)
     cached = cached.reshape(rows, heads, hd)
 
-    mine, meta, list_rows, rowof, keyed_even, values, cache_top, cache_sum, cached = (
+    mine, odd, meta, list_rows, rowof, keyed_even, values, cache_top, cache_sum, cached = (
         lax.optimization_barrier(
-            (mine, meta, list_rows, rowof, keyed_even, values, cache_top, cache_sum, cached)
+            (mine, odd, meta, list_rows, rowof, keyed_even, values, cache_top, cache_sum, cached)
         )
     )
     other = lax.ppermute(mine, "tp", swap)
+    keyed_odd = through_keys(odd)
 
     in_hbm = pl.BlockSpec(memory_space=pltpu.HBM)
     row_spec = pl.BlockSpec((1, 1, lanes), lambda q, m: (q, 0, 0))
@@ -550,7 +549,7 @@
             slot_shape,
             *[jax.ShapeDtypeStruct(shape, jnp.bfloat16) for shape in list_shapes],
         ],
-        compiler_params=pltpu.CompilerParams(vmem_limit_bytes=32 * MIB),
+        compiler_params=pltpu.CompilerParams(vmem_limit_bytes=56 * MIB),
         name="prompt_scores",
     )(meta, mine, other, more_mine, more_other, keyed_even, keyed_odd, rowof)
 
@@ -585,7 +584,7 @@
             ],
         ),
         out_shape=jax.ShapeDtypeStruct((n, kvh, per, hd), jnp.bfloat16),
-        compiler_params=pltpu.CompilerParams(vmem_limit_bytes=24 * MIB),
+        compiler_params=pltpu.CompilerParams(vmem_limit_bytes=56 * MIB),
         name="weighted_values",
     )(list_rows, all_weights, rowof, low, high, values)
 

time: 163 us -> 160 us (0.982); the launches traced: 163 us -> 158 us
  waiting for transfers between devices: 48.9 us -> 38.2 us
  Pallas kernels: 24.9 us -> 30.5 us
  local copies, waits for them, and re-layouts: 18.5 us -> 16.3 us
    all_to_all x1, waiting for transfers between devices: 22.4 us -> 9.21 us  [local(): lax.all_to_all(packed, 'pool', 0, 0, tiled=True).reshape(n * size, part)]
    optimization_barrier x4 -> x2, local copies, waits for them, and re-layouts: 5.61 us -> 0.26 us  [local(): lax.optimization_barrier((mine, odd, meta, list_rows, rowof, keyed_even,...]
    slice x0 -> x2, local copies, waits for them, and re-layouts: none -> 4.9 us  [the longest x1 4.18 us: local(): kv_cache[:, :, :, hd:]]
    unnamed x26 -> x27, local copies, waits for them, and re-layouts: 10.4 us -> 6.3 us
    pallas_call x1, Pallas kernels: 6.21 us -> 10.1 us  [local(): pl.pallas_call(functools.partial(value_kernel, rows), grid_spec=pltpu.Pre...]
    ppermute x10, waiting for transfers between devices: 13.1 us -> 16.5 us  [with_partner(): return lax.ppermute(x, 'pool', [(i, i ^ k) for i in range(n)])]
    pallas_call x1, Pallas kernels: 9.25 us -> 11.3 us  [local(): pl.pallas_call(functools.partial(score_kernel, n, rows), grid_spec=pltpu....]
  transfers between devices with their start and end apart: 15 -> 15, of which waited for: 9 -> 9; matrix products, arithmetic and copies ran while one was open for 10% -> 15% of each run, Pallas kernels for 3% -> 3%
where the time goes in v8:
time: 160 us; the launch traced here: 158 us
  waiting for transfers between devices  38.2 us (24%)
  blocking collectives  32 us (20%)
  Pallas kernels  30.5 us (19%)
  starting transfers between devices  25.2 us (16%)
  local copies, waits for them, and re-layouts  16.3 us (10%)
  other arithmetic  7.45 us (5%)
  matrix products  6.85 us (4%)
    all_to_all x1, blocking collectives, local(): term_parts = lax.all_to_all(terms, 'pool', 0, 0, tiled=True)  17.4 us
    ppermute x10, waiting for transfers between devices, with_partner(): return lax.ppermute(x, 'pool', [(i, i ^ k) for i in range(n)])  16.5 us
    ppermute x10, starting transfers between devices, with_partner(): return lax.ppermute(x, 'pool', [(i, i ^ k) for i in range(n)])  15.4 us
    all_to_all x1, blocking collectives, local(): all_weights = lax.all_to_all(weights, 'pool', 0, 0, tiled=True)  14.7 us
    pallas_call x1, Pallas kernels, local(): pl.pallas_call(functools.partial(score_kernel, n, rows), grid_spec=pltpu....  11.3 us
    pallas_call x1, Pallas kernels, local(): pl.pallas_call(functools.partial(value_kernel, rows), grid_spec=pltpu.Pre...  10.1 us
    all_to_all x1, waiting for transfers between devices, local(): parts = lax.all_to_all(partial_scores, 'pool', 0, 0, tiled=True)  9.99 us
    all_to_all x1, waiting for transfers between devices, local(): lax.all_to_all(packed, 'pool', 0, 0, tiled=True).reshape(n * size, part)  9.21 us
  transfers between devices with their start and end apart: 15, of which 9 were waited for; matrix products, arithmetic and copies ran while one was open for 15% of the time, Pallas kernels for 3%

profile of v8, /device:TPU:0, one launch (start us, length us, event | category | flops | bytes accessed | tf_op | source)
XLA Modules:
  0.0 158.2 jit_solution(2903578958223876810)
XLA Ops:
  0.0 4.0 %collective-permute-start.1 = (bf16[8,32,128]{2,1,0:T(8,128)(2,1)}, bf16[8,32,128]{2,1,0:T(8,128)(2,1)S(1)}, u32[]{:S(2)}, u32[]{:S(2)}) collective-permute-start(bf16[8,32,128]{2,1,0:T(8,128)(2,1)} %param.16), channel_id=1, source_target_pairs={{0,8},{2,10},{4,12},{6,14},{8,0},{10,2},{12,4},{14,6},{1,9},{3,11}... | collective-permute-start | bytes 196616 | tf_op jit(solution)/shard_map/ppermute | solution.py:340
  4.0 0.6 iota_multiply_fusion
  4.6 4.2 %fusion.40 = (bf16[8,256,4,128]{3,2,1,0:T(4,128)(2,1)S(1)}, bf16[8,256,4,128]{3,2,1,0:T(4,128)(2,1)}) fusion(bf16[8,256,4,256]{3,2,1,0:T(4,128)(2,1)} %param.17), kind=kLoop, calls=%fused_computation.97 | loop fusion | bytes 8388608 | tf_op jit(solution)/shard_map/slice | solution.py:496
  8.9 0.7 fusion.41
  9.7 1.2 copy.61
  10.9 0.6 copy-done.1
  11.5 4.2 %pack_live_tokens.3 = bf16[8,96,1024]{2,1,0:T(8,128)(2,1)} custom-call(s32[2]{0:T(128)S(1)} %pad_add_fusion.at_ref, s32[256]{0:T(256)S(1)} %copy-done.7, s32[256]{0:T(256)S(1)} %bitcast.49, bf16[256,8192]{1,0:T(8,128)(2,1)S(1)} %copy-done.1), custom_call_target="tpu_custom_call" | custom-call | tf_op jit(solution)/shard_map/pack_live_tokens/pallas_call | solution.py:70
  15.8 0.2 select_reduce_fusion.5
  16.1 0.7 fusion.38
  16.8 0.1 select_reduce_fusion.6
  17.0 0.7 pad_maximum_fusion.2
  17.6 1.6 collective-permute-start.2
  19.2 4.3 %all-to-all-start.1 = ((bf16[8,96,1024]{2,1,0:T(8,128)(2,1)}), bf16[8,96,1024]{2,1,0:T(8,128)(2,1)}, u32[]{:S(2)}, u32[]{:S(2)}) async-start(bf16[8,96,1024]{2,1,0:T(8,128)(2,1)} %pack_live_tokens.3), calls=%async_computation.1 | async-start | bytes 3145728 | tf_op jit(solution)/shard_map/all_to_all | solution.py:403
  23.5 0.1 select_reduce_fusion.3
  23.6 0.3 select_reduce_fusion.2
  23.9 0.6 multiply_add_fusion.2
  24.5 0.6 compare_select_fusion.2
  25.1 1.0 select_reduce_fusion
  26.1 0.6 broadcast_add_fusion
  26.7 2.3 %fusion.42 = (f32[8,4,8]{2,1,0:T(4,128)S(1)}, f32[8,4,8,256]{3,2,1,0:T(8,128)S(1)}) fusion(bf16[8,256,4,128]{3,2,1,0:T(4,128)(2,1)} %get-tuple-element.76, bf16[8,32,128]{2,1,0:T(8,128)(2,1)S(1)} %copy-done.4, pred[8,256]{1,0:T(8,128)(4,1)S(1)} %iota_compare_fusion.4), kind=kOutput, calls=%fused_computation.99 | convolution fusion | flops 16973568 | bytes 2427904 | tf_op jit(solution)/shard_map/rhgd,rthd->rhgt/dot_general | solution.py:483
  29.1 0.5 fusion.11.cached_ref
  29.5 0.2 fusion.18
  29.7 0.8 reshape.280
  30.6 0.1 reduce_sum.110
  30.7 0.7 reduce_max.18
  31.4 1.5 collective-permute-start.4
  33.0 0.8 fusion.20
  33.8 1.2 collective-permute-done.4
  36.3 1.3 concatenate.17.meta_ref
  37.6 1.9 %collective-permute-start.3 = (bf16[4,8,32,128]{3,2,1,0:T(8,128)(2,1)S(1)}, bf16[4,8,32,128]{3,2,1,0:T(8,128)(2,1)S(1)}, u32[]{:S(2)}, u32[]{:S(2)}) collective-permute-start(bf16[4,8,32,128]{3,2,1,0:T(8,128)(2,1)S(1)} %pad_maximum_fusion), channel_id=1, source_target_pairs={{0,2},{2,0},{4,6},{6,4},{8,10},{10,8},{12,14},{14,12},{1,3},{3,1},... | collective-permute-start | bytes 786440 | tf_op jit(solution)/shard_map/ppermute | solution.py:340
  39.6 2.0 %convolution_convert_fusion.1 = bf16[4,4,8,8,1024]{4,3,2,1,0:T(8,128)(2,1)} fusion(bf16[1024,4,128]{2,1,0:T(4,128)(2,1)S(1)} %get-tuple-element.78, bf16[2,8,4,8,128]{4,3,2,1,0:T(8,128)(2,1)S(1)} %bitcast.45, bf16[1,8,4,8,128]{4,3,2,1,0:T(8,128)(2,1)S(1)} %bitcast.44, bf16[1,8,4,8,128]{4,3,2,1,0:T(8,128)(2,1)S(1)} %bitcast.41), kind=kOutput, calls=%fused_computation.9 | convolution fusion | flops 269746176 | bytes 3407872 | tf_op jit(solution)/shard_map/qrhgd,phd->hqrgp/dot_general | solution.py:471
  41.6 9.4 %collective-permute-done.3 = bf16[4,8,32,128]{3,2,1,0:T(8,128)(2,1)S(1)} collective-permute-done((bf16[4,8,32,128]{3,2,1,0:T(8,128)(2,1)S(1)}, bf16[4,8,32,128]{3,2,1,0:T(8,128)(2,1)S(1)}, u32[]{:S(2)}, u32[]{:S(2)}) %collective-permute-start.3) | collective-permute-done | bytes 262176 | tf_op jit(solution)/shard_map/ppermute | solution.py:340
  51.0 9.2 %all-to-all-done.1 = bf16[8,96,1024]{2,1,0:T(8,128)(2,1)} async-done(((bf16[8,96,1024]{2,1,0:T(8,128)(2,1)}), bf16[8,96,1024]{2,1,0:T(8,128)(2,1)}, u32[]{:S(2)}, u32[]{:S(2)}) %all-to-all-start.1) | async-done | bytes 1572896 | tf_op jit(solution)/shard_map/all_to_all | solution.py:403
  60.2 1.7 %conditional.1 = (bf16[256,1024]{1,0:T(8,128)(2,1)}, bf16[256,1024]{1,0:T(8,128)(2,1)}) conditional(s32[]{:T(128)} %convert_element_type.13, () %tuple.17, (s32[2]{0:T(128)S(1)}, s32[256]{0:T(256)S(1)}, s32[256]{0:T(256)S(1)}, bf16[256,8192]{1,0:T(8,128)(2,1)}) %tuple.33), branch_computations={%region_13.14_spmd, %region_14.15_spmd} | conditional | bytes 3145784 | solution.py:461
  60.3 0.9 broadcast.391
  61.1 0.9 broadcast.391.clone
  62.0 2.0 %convolution_convert_fusion = bf16[4,4,8,8,1024]{4,3,2,1,0:T(8,128)(2,1)} fusion(bf16[1024,4,128]{2,1,0:T(4,128)(2,1)S(1)} %get-tuple-element.78, bf16[4,8,32,128]{3,2,1,0:T(8,128)(2,1)S(1)} %collective-permute-done.3), kind=kOutput, calls=%fused_computation.8 | convolution fusion | flops 269484032 | bytes 3407872 | tf_op jit(solution)/shard_map/qrhgd,phd->hqrgp/dot_general | solution.py:471
  64.0 1.1 copy-done.3
  65.2 11.3 %prompt_scores.1 = (bf16[8,32,640]{2,1,0:T(8,128)(2,1)}, bf16[8,256,1024]{2,1,0:T(8,128)(2,1)}, bf16[8,384,1024]{2,1,0:T(8,128)(2,1)}) custom-call(s32[651]{0:T(1024)} %concatenate.17.meta_ref, bf16[768,1024]{1,0:T(8,128)(2,1)} %bitcast.4.refs_0_, bf16[768,1024]{1,0:T(8,128)(2,1)} %copy-done.3, bf16[256,1024]{1,0:T(8,128)(2,1)} %get-tuple-element.51.refs_2_, ...), custom_call_target="tpu_custom_call" | custom-call | tf_op jit(solution)/shard_map/prompt_scores/pallas_call | solution.py:523
  76.5 4.0 %all-to-all-start.2 = ((bf16[8,32,640]{2,1,0:T(8,128)(2,1)}), bf16[8,32,640]{2,1,0:T(8,128)(2,1)S(1)}, u32[]{:S(2)}, u32[]{:S(2)}) async-start(bf16[8,32,640]{2,1,0:T(8,128)(2,1)} %get-tuple-element.56), calls=%async_computation.2 | async-start | bytes 655360 | tf_op jit(solution)/shard_map/all_to_all | solution.py:556
  80.5 0.1 copy.33.top_ref
  80.6 0.1 copy.34.sum_ref
  80.8 0.7 dynamic-slice_bitcast_fusion.row_ref
  81.4 10.0 %all-to-all-done.2.parts_ref = bf16[8,32,640]{2,1,0:T(8,128)(2,1)S(1)} async-done(((bf16[8,32,640]{2,1,0:T(8,128)(2,1)}), bf16[8,32,640]{2,1,0:T(8,128)(2,1)S(1)}, u32[]{:S(2)}, u32[]{:S(2)}) %all-to-all-start.2) | async-done | bytes 327712 | tf_op jit(solution)/shard_map/all_to_all | solution.py:556
  91.4 1.2 softmax_weights.1
  92.7 14.7 %all_to_all.25.w_ref = bf16[8,32,640]{2,1,0:T(8,128)(2,1)} all-to-all(bf16[8,32,640]{2,1,0:T(8,128)(2,1)S(1)} %get-tuple-element.60), channel_id=1, replica_groups=mesh['groups'=2,'pool'=8,'tp'=2] {'pool'}, dimensions={0} | all-to-all | bytes 655360 | tf_op jit(solution)/shard_map/all_to_all | solution.py:565
  107.3 10.1 %weighted_values.1 = bf16[8,4,64,128]{3,2,1,0:T(8,128)(2,1)} custom-call(s32[8]{0:T(128)} %get-tuple-element.48.size_ref, bf16[8,32,640]{2,1,0:T(8,128)(2,1)} %all_to_all.25.w_ref, s32[8,1,640]{2,1,0:T(1,128)} %bitcast.48, bf16[8,256,1024]{2,1,0:T(8,128)(2,1)} %get-tuple-element.61.low_ref, bf16[8,384,1024]{2,1,0:T(8,128)(2,1)} %get-tuple-element.62.high_ref, ...), custom_call_target="tpu_custom_call" | custom-call | tf_op jit(solution)/shard_map/weighted_values/pallas_call | solution.py:566
  117.4 17.4 %all_to_all.26.parts_ref = bf16[8,4,64,128]{3,2,1,0:T(8,128)(2,1)S(1)} all-to-all(bf16[8,4,64,128]{3,2,1,0:T(8,128)(2,1)} %weighted_values.1), channel_id=1, replica_groups=mesh['groups'=2,'pool'=8,'tp'=2] {'pool'}, dimensions={0} | all-to-all | bytes 1048576 | tf_op jit(solution)/shard_map/all_to_all | solution.py:591
  134.8 0.1 attended_sum.1.refs_0_
  134.9 0.8 collective-permute-start.10
  135.7 2.4 %collective-permute-start.11 = (bf16[8,4096]{1,0:T(8,128)(2,1)S(1)}, bf16[8,4096]{1,0:T(8,128)(2,1)S(1)}, u32[]{:S(2)}, u32[]{:S(2)}) collective-permute-start(bf16[8,4096]{1,0:T(8,128)(2,1)S(1)} %attended_sum.1.refs_0_), channel_id=1, source_target_pairs={{0,12},{2,14},{4,8},{6,10},{8,4},{10,6},{12,0},{14,2},{1,13},{3,15... | collective-permute-start | bytes 196616 | tf_op jit(solution)/shard_map/ppermute | solution.py:340
  138.1 2.7 %collective-permute-start.12 = (bf16[8,4096]{1,0:T(8,128)(2,1)S(1)}, bf16[8,4096]{1,0:T(8,128)(2,1)S(1)}, u32[]{:S(2)}, u32[]{:S(2)}) collective-permute-start(bf16[8,4096]{1,0:T(8,128)(2,1)S(1)} %attended_sum.1.refs_0_), channel_id=1, source_target_pairs={{0,14},{2,12},{4,10},{6,8},{8,6},{10,4},{12,2},{14,0},{1,15},{3,13... | collective-permute-start | bytes 196616 | tf_op jit(solution)/shard_map/ppermute | solution.py:340
  140.8 0.2 collective-permute-start.6
  141.0 0.4 collective-permute-start.7
  141.4 2.6 %collective-permute-done.10.refs_5_ = bf16[8,4096]{1,0:T(8,128)(2,1)S(1)} collective-permute-done((bf16[8,4096]{1,0:T(8,128)(2,1)S(1)}, bf16[8,4096]{1,0:T(8,128)(2,1)S(1)}, u32[]{:S(2)}, u32[]{:S(2)}) %collective-permute-start.10) | collective-permute-done | bytes 65568 | tf_op jit(solution)/shard_map/ppermute | solution.py:340
  144.0 0.3 collective-permute-start.8
  144.3 1.1 collective-permute-start.9
  145.4 0.4 collective-permute-done.12.refs_7_
  145.8 0.6 collective-permute-done.6.refs_1_
  146.4 3.5 %collective-permute-done.8.refs_3_ = bf16[8,4096]{1,0:T(8,128)(2,1)S(1)} collective-permute-done((bf16[8,4096]{1,0:T(8,128)(2,1)S(1)}, bf16[8,4096]{1,0:T(8,128)(2,1)S(1)}, u32[]{:S(2)}, u32[]{:S(2)}) %collective-permute-start.8) | collective-permute-done | bytes 65568 | tf_op jit(solution)/shard_map/ppermute | solution.py:340
  149.9 3.4 %copy-done = bf16[4096,1024]{1,0:T(8,128)(2,1)S(1)} copy-done((bf16[4096,1024]{1,0:T(8,128)(2,1)S(1)}, bf16[4096,1024]{1,0:T(8,128)(2,1)}, u32[]{:S(2)}) %copy-start) | copy-done | bytes 8388632
  153.2 2.9 %output_projection.1 = (f32[64,512]{1,0:T(8,128)S(1)}, f32[64,512]{1,0:T(8,128)S(1)}) custom-call(s32[1]{0:T(128)} %bitcast.2.core_ref, bf16[8,4096]{1,0:T(8,128)(2,1)S(1)} %attended_sum.1.refs_0_, bf16[8,4096]{1,0:T(8,128)(2,1)S(1)} %collective-permute-done.6.refs_1_, bf16[8,4096]{1,0:T(8,128)(2,1)S(1)} %collective-permute-done.7.refs_2_, ...), custom_call_target="tpu_custom_call" | custom-call | tf_op jit(solution)/shard_map/output_projection/pallas_call | solution.py:603
  156.2 1.3 collective-permute-done.13.got_ref
  157.5 0.6 order_rows.1
  (44 shorter events, 0.7 us)
Async XLA Ops:
  0.0 15.8 %collective-permute-start.1 = (bf16[8,32,128]{2,1,0:T(8,128)(2,1)}, bf16[8,32,128]{2,1,0:T(8,128)(2,1)S(1)}, u32[]{:S(2)}, u32[]{:S(2)}) collective-permute-start(bf16[8,32,128]{2,1,0:T(8,128)(2,1)} %param.16), channel_id=1, source_target_pairs={{0,8},{2,10},{4,12},{6,14},{8,0},{10,2},{12,4},{14,6},{1,9},{3,11}... | collective-permute-start | bytes 196616 | tf_op jit(solution)/shard_map/ppermute | solution.py:340
  4.6 4.2 %copy-start.12 = (s32[8]{0:T(128)S(1)}, s32[8]{0:T(128)}, u32[]{:S(2)}) copy-start(s32[8]{0:T(128)} %param.18) | copy-start | bytes 100
  4.6 4.3 %copy-start.2 = (bf16[1024,4,256]{2,1,0:T(4,128)(2,1)S(1)}, bf16[1024,4,256]{2,1,0:T(4,128)(2,1)}, u32[]{:S(2)}) copy-start(bf16[1024,4,256]{2,1,0:T(4,128)(2,1)} %param.12) | copy-start | bytes 6291460
  8.9 2.6 %copy-start.1 = (bf16[256,8192]{1,0:T(8,128)(2,1)S(1)}, bf16[256,8192]{1,0:T(8,128)(2,1)}, u32[]{:S(2)}) copy-start(bf16[256,8192]{1,0:T(8,128)(2,1)} %x_ref.1) | copy-start | bytes 12582916
  9.6 1.8 %copy-start.5 = (s32[256,1]{0,1:T(1,128)S(1)}, s32[256,1]{0,1:T(1,128)}, u32[]{:S(2)}) copy-start(s32[256,1]{0,1:T(1,128)} %param.13) | copy-start | bytes 3076
  9.6 1.8 %copy-start.7 = (s32[256]{0:T(256)S(1)}, s32[256]{0:T(256)}, u32[]{:S(2)}) copy-start(s32[256]{0:T(256)} %fill_ref.1) | copy-start | bytes 3076
  10.9 4.8 %copy-start.9 = (s32[2]{0:T(128)}, s32[2]{0:T(128)S(1)}, u32[]{:S(2)}) copy-start(s32[2]{0:T(128)S(1)} %pad_add_fusion.at_ref) | copy-start | bytes 28
  11.5 5.5 %copy-start.4 = (bf16[8,32,128]{2,1,0:T(8,128)(2,1)S(1)}, bf16[8,32,128]{2,1,0:T(8,128)(2,1)}, u32[]{:S(2)}) copy-start(bf16[8,32,128]{2,1,0:T(8,128)(2,1)} %param.16) | copy-start | bytes 196612
  15.7 7.8 %copy-start.11 = (s32[256]{0:T(256)S(1)}, s32[256]{0:T(256)}, u32[]{:S(2)}) copy-start(s32[256]{0:T(256)} %param.14) | copy-start | bytes 3076
  17.6 20.0 %collective-permute-start.2 = (bf16[2,8,32,128]{3,2,1,0:T(8,128)(2,1)}, bf16[2,8,32,128]{3,2,1,0:T(8,128)(2,1)S(1)}, u32[]{:S(2)}, u32[]{:S(2)}) collective-permute-start(bf16[2,8,32,128]{3,2,1,0:T(8,128)(2,1)} %pad_maximum_fusion.2), channel_id=1, source_target_pairs={{0,4},{2,6},{4,0},{6,2},{8,12},{10,14},{12,8},{14,10},{1,5},{3,7},... | collective-permute-start | bytes 393224 | tf_op jit(solution)/shard_map/ppermute | solution.py:340
  19.2 41.0 %all-to-all-start.1 = ((bf16[8,96,1024]{2,1,0:T(8,128)(2,1)}), bf16[8,96,1024]{2,1,0:T(8,128)(2,1)}, u32[]{:S(2)}, u32[]{:S(2)}) async-start(bf16[8,96,1024]{2,1,0:T(8,128)(2,1)} %pack_live_tokens.3), calls=%async_computation.1 | async-start | bytes 3145728 | tf_op jit(solution)/shard_map/all_to_all | solution.py:403
  29.5 30.7 %copy-start.6 = (s32[256,1]{0,1:T(1,128)S(1)}, s32[256,1]{0,1:T(1,128)}, u32[]{:S(2)}) copy-start(s32[256,1]{0,1:T(1,128)} %param.13) | copy-start | bytes 3076
  29.5 30.7 %copy-start.8 = (s32[256]{0:T(256)S(1)}, s32[256]{0:T(256)}, u32[]{:S(2)}) copy-start(s32[256]{0:T(256)} %fill_ref.1) | copy-start | bytes 3076
  29.5 30.7 %copy-start.10 = (s32[2]{0:T(128)S(1)}, s32[2]{0:T(128)}, u32[]{:S(2)}) copy-start(s32[2]{0:T(128)} %copy-done.9) | copy-start | bytes 28
  31.4 3.6 %collective-permute-start.4 = (s32[]{:T(128)}, s32[]{:T(128)}, u32[]{:S(2)}, u32[]{:S(2)}) collective-permute-start(s32[]{:T(128)} %reduce_max.18), channel_id=1, source_target_pairs={{0,16},{16,0},{1,17},{17,1},{2,18},{18,2},{3,19},{19,3},{4,20},{20... | collective-permute-start | bytes 20 | tf_op jit(solution)/shard_map/ppermute | solution.py:448
  37.6 13.4 %collective-permute-start.3 = (bf16[4,8,32,128]{3,2,1,0:T(8,128)(2,1)S(1)}, bf16[4,8,32,128]{3,2,1,0:T(8,128)(2,1)S(1)}, u32[]{:S(2)}, u32[]{:S(2)}) collective-permute-start(bf16[4,8,32,128]{3,2,1,0:T(8,128)(2,1)S(1)} %pad_maximum_fusion), channel_id=1, source_target_pairs={{0,2},{2,0},{4,6},{6,4},{8,10},{10,8},{12,14},{14,12},{1,3},{3,1},... | collective-permute-start | bytes 786440 | tf_op jit(solution)/shard_map/ppermute | solution.py:340
  60.2 3.8 %collective-permute-start.5 = (bf16[768,1024]{1,0:T(8,128)(2,1)}, bf16[768,1024]{1,0:T(8,128)(2,1)S(1)}, u32[]{:S(2)}, u32[]{:S(2)}) collective-permute-start(bf16[768,1024]{1,0:T(8,128)(2,1)} %bitcast.4.refs_0_), channel_id=1, source_target_pairs={{0,1},{1,0},{2,3},{3,2},{4,5},{5,4},{6,7},{7,6},{8,9},{9,8},{10,11... | collective-permute-start | bytes 4718600 | tf_op jit(solution)/shard_map/ppermute | solution.py:508
  64.0 1.1 copy-start.3
  76.5 14.9 %all-to-all-start.2 = ((bf16[8,32,640]{2,1,0:T(8,128)(2,1)}), bf16[8,32,640]{2,1,0:T(8,128)(2,1)S(1)}, u32[]{:S(2)}, u32[]{:S(2)}) async-start(bf16[8,32,640]{2,1,0:T(8,128)(2,1)} %get-tuple-element.56), calls=%async_computation.2 | async-start | bytes 655360 | tf_op jit(solution)/shard_map/all_to_all | solution.py:556
  134.9 9.1 %collective-permute-start.10 = (bf16[8,4096]{1,0:T(8,128)(2,1)S(1)}, bf16[8,4096]{1,0:T(8,128)(2,1)S(1)}, u32[]{:S(2)}, u32[]{:S(2)}) collective-permute-start(bf16[8,4096]{1,0:T(8,128)(2,1)S(1)} %attended_sum.1.refs_0_), channel_id=1, source_target_pairs={{0,10},{2,8},{4,14},{6,12},{8,2},{10,0},{12,6},{14,4},{1,11},{3,9}... | collective-permute-start | bytes 196616 | tf_op jit(solution)/shard_map/ppermute | solution.py:340
  135.7 8.6 %collective-permute-start.11 = (bf16[8,4096]{1,0:T(8,128)(2,1)S(1)}, bf16[8,4096]{1,0:T(8,128)(2,1)S(1)}, u32[]{:S(2)}, u32[]{:S(2)}) collective-permute-start(bf16[8,4096]{1,0:T(8,128)(2,1)S(1)} %attended_sum.1.refs_0_), channel_id=1, source_target_pairs={{0,12},{2,14},{4,8},{6,10},{8,4},{10,6},{12,0},{14,2},{1,13},{3,15... | collective-permute-start | bytes 196616 | tf_op jit(solution)/shard_map/ppermute | solution.py:340
  138.1 7.7 %collective-permute-start.12 = (bf16[8,4096]{1,0:T(8,128)(2,1)S(1)}, bf16[8,4096]{1,0:T(8,128)(2,1)S(1)}, u32[]{:S(2)}, u32[]{:S(2)}) collective-permute-start(bf16[8,4096]{1,0:T(8,128)(2,1)S(1)} %attended_sum.1.refs_0_), channel_id=1, source_target_pairs={{0,14},{2,12},{4,10},{6,8},{8,6},{10,4},{12,2},{14,0},{1,15},{3,13... | collective-permute-start | bytes 196616 | tf_op jit(solution)/shard_map/ppermute | solution.py:340
  140.8 5.6 %collective-permute-start.6 = (bf16[8,4096]{1,0:T(8,128)(2,1)S(1)}, bf16[8,4096]{1,0:T(8,128)(2,1)S(1)}, u32[]{:S(2)}, u32[]{:S(2)}) collective-permute-start(bf16[8,4096]{1,0:T(8,128)(2,1)S(1)} %attended_sum.1.refs_0_), channel_id=1, source_target_pairs={{0,2},{2,0},{4,6},{6,4},{8,10},{10,8},{12,14},{14,12},{1,3},{3,1},... | collective-permute-start | bytes 196616 | tf_op jit(solution)/shard_map/ppermute | solution.py:340
  141.0 5.4 %collective-permute-start.7 = (bf16[8,4096]{1,0:T(8,128)(2,1)S(1)}, bf16[8,4096]{1,0:T(8,128)(2,1)S(1)}, u32[]{:S(2)}, u32[]{:S(2)}) collective-permute-start(bf16[8,4096]{1,0:T(8,128)(2,1)S(1)} %attended_sum.1.refs_0_), channel_id=1, source_target_pairs={{0,4},{2,6},{4,0},{6,2},{8,12},{10,14},{12,8},{14,10},{1,5},{3,7},... | collective-permute-start | bytes 196616 | tf_op jit(solution)/shard_map/ppermute | solution.py:340
  144.0 5.9 %collective-permute-start.8 = (bf16[8,4096]{1,0:T(8,128)(2,1)S(1)}, bf16[8,4096]{1,0:T(8,128)(2,1)S(1)}, u32[]{:S(2)}, u32[]{:S(2)}) collective-permute-start(bf16[8,4096]{1,0:T(8,128)(2,1)S(1)} %attended_sum.1.refs_0_), channel_id=1, source_target_pairs={{0,6},{2,4},{4,2},{6,0},{8,14},{10,12},{12,10},{14,8},{1,7},{3,5},... | collective-permute-start | bytes 196616 | tf_op jit(solution)/shard_map/ppermute | solution.py:340
  144.3 5.6 %collective-permute-start.9 = (bf16[8,4096]{1,0:T(8,128)(2,1)S(1)}, bf16[8,4096]{1,0:T(8,128)(2,1)S(1)}, u32[]{:S(2)}, u32[]{:S(2)}) collective-permute-start(bf16[8,4096]{1,0:T(8,128)(2,1)S(1)} %attended_sum.1.refs_0_), channel_id=1, source_target_pairs={{0,8},{2,10},{4,12},{6,14},{8,0},{10,2},{12,4},{14,6},{1,9},{3,11}... | collective-permute-start | bytes 196616 | tf_op jit(solution)/shard_map/ppermute | solution.py:340
  149.9 3.4 %copy-start = (bf16[4096,1024]{1,0:T(8,128)(2,1)S(1)}, bf16[4096,1024]{1,0:T(8,128)(2,1)}, u32[]{:S(2)}) copy-start(bf16[4096,1024]{1,0:T(8,128)(2,1)} %refs_8_.1) | copy-start | bytes 25165828
  156.1 1.4 collective-permute-start.13

commit v9 on v8

--- a/solution.py
+++ b/solution.py
@@ -84,6 +84,9 @@
         ),
         out_shape=jax.ShapeDtypeStruct((n, size, part), jnp.bfloat16),
         compiler_params=pltpu.CompilerParams(vmem_limit_bytes=56 * MIB),
+        cost_estimate=pl.CostEstimate(
+            flops=2 * size * tokens * width, bytes_accessed=64 * MIB, transcendentals=0
+        ),
         name="pack_live_tokens",
     )(at, fill, dest, x_prompt)
 
@@ -92,7 +95,11 @@
     return [0] + list(range(min(256, lanes), lanes, 128)) + [lanes]
 
 
-def load_tokens(n, core, over, x_refs, held, more, wide, sem):
+def near_lanes(lanes):
+    return min(lanes, -(-lanes * 3 // 5 // 128) * 128)
+
+
+def load_tokens(n, core, over, x_refs, held, more, wide, sem, others):
     size, extra = held.shape[1] // n, more.shape[1] // n
     tokens = 2 * (size + extra)
     part = wide.shape[1]
@@ -126,6 +133,8 @@
     for pair in main:
         for copy in pair:
             copy.start()
+    for copy in others:
+        copy.start()
     for i, pair in enumerate(main):
         for copy in pair:
             copy.wait()
@@ -144,25 +153,43 @@
 
 
 def score_kernel(n, rows, meta_ref, *refs):
-    x_refs, (near_ref, far_ref, row_ref), (out_ref, low_ref, high_ref) = refs[:4], refs[4:7], refs[7:10]
-    held, more, wide, low, high, in_sem, out_sem = refs[10:]
+    x_refs, keyed_refs, (row_ref, near_ref, rest_ref, low_ref, high_ref) = (
+        refs[:4], refs[4:6], refs[6:11]
+    )
+    held, more, wide, keyed, low, high, in_sem, keyed_sem, out_sem = refs[11:]
     step = pl.program_id(0)
     part = wide.shape[1]
-    lanes = out_ref.shape[2]
+    near = near_ref.shape[2]
+    lanes = near + rest_ref.shape[2]
     cuts = tile_cuts(lanes)
     groups = lanes // BLK
     at_size = n * groups
     q = meta_ref[at_size + n] ^ reversed_bits(step, n)
+    kvh, per = keyed.shape[0], keyed.shape[1] // n
+    group = per // rows
 
     @pl.when(step == 0)
     def _():
+        loads = [
+            pltpu.make_async_copy(
+                ref.at[h], keyed.at[h, pl.ds(i * n // 2 * per, n // 2 * per)], keyed_sem.at[i, h]
+            )
+            for i, ref in enumerate(keyed_refs)
+            for h in range(kvh)
+        ]
         load_tokens(
-            n, meta_ref[at_size + n + 1], meta_ref[at_size + n + 2], x_refs, held, more, wide, in_sem
-        )
-
-    kvh, per, _ = near_ref.shape
-    group = per // rows
-    keyed = jnp.where(step < n // 2, near_ref[...], far_ref[...]).reshape(kvh * per, part)
+            n,
+            meta_ref[at_size + n + 1],
+            meta_ref[at_size + n + 2],
+            x_refs,
+            held,
+            more,
+            wide,
+            in_sem,
+            loads,
+        )
+        for load in loads:
+            load.wait()
 
     def copy(o, t):
         if t == 0:
@@ -183,7 +210,7 @@
             buffer[q, i - base : i - base + 2 * BLK, :] = jnp.concatenate(pair).astype(low.dtype)
         copy(q, t).start()
         raw = lax.dot_general(
-            keyed,
+            keyed[:, pl.ds(pl.multiple_of(step * per, per), per), :].reshape(kvh * per, part),
             buffer[q, cuts[t] - base : cuts[t + 1] - base, :],
             (((1,), (1,)), ((), ())),
             preferred_element_type=jnp.float32,
@@ -192,7 +219,11 @@
         picked = jnp.zeros((kvh, group, cuts[t + 1] - cuts[t]), jnp.float32)
         for r in range(rows):
             picked = picked + jnp.where((owner_row == r)[None], raw[:, r], 0.0)
-        out_ref[0, :, here] = picked.reshape(kvh * group, -1).astype(out_ref.dtype)
+        picked = picked.reshape(kvh * group, -1).astype(near_ref.dtype)
+        if cuts[t] < near:
+            near_ref[0, :, here] = picked
+        else:
+            rest_ref[0, :, cuts[t] - near : cuts[t + 1] - near] = picked
 
     one(0)
     for t in range(1, len(cuts) - 1):
@@ -206,37 +237,49 @@
                 pl.when(meta_ref[at_size + o] > cuts[t])(lambda o=o, t=t: copy(o, t).wait())
 
 
-def weight_kernel(scale, parts_ref, row_ref, top_ref, sum_ref, cached_ref, w_ref, kept_ref):
-    n = parts_ref.shape[0]
-    scores = parts_ref[0].astype(jnp.float32)
-    for i in range(1, n):
-        scores = scores + parts_ref[i].astype(jnp.float32)
-    scores = scores * scale
-    owner_row = row_ref[...]
-    weights = jnp.zeros(scores.shape, jnp.float32)
+def weight_kernel(scale, count, *refs):
+    part_refs, row_refs = refs[:count], refs[count : 2 * count]
+    top_ref, sum_ref, cached_ref = refs[2 * count : 2 * count + 3]
+    w_refs, kept_ref = refs[2 * count + 3 : -1], refs[-1]
+    n = part_refs[0].shape[0]
+    scores, owner_rows = [], []
+    for part_ref, row_ref in zip(part_refs, row_refs):
+        got = part_ref[0].astype(jnp.float32)
+        for i in range(1, n):
+            got = got + part_ref[i].astype(jnp.float32)
+        scores.append(got * scale)
+        owner_rows.append(row_ref[...])
+    weights = [jnp.zeros(s.shape, jnp.float32) for s in scores]
     for r in range(top_ref.shape[0]):
-        own = jnp.where(owner_row == r, scores, -jnp.inf)
+        own = [jnp.where(o == r, s, -jnp.inf) for o, s in zip(owner_rows, scores)]
         cache_top = top_ref[r]
-        top = jnp.maximum(jnp.max(own, 1, keepdims=True), cache_top)
-        held = jnp.exp(own - top)
+        top = cache_top
+        for o in own:
+            top = jnp.maximum(top, jnp.max(o, 1, keepdims=True))
+        held = [jnp.exp(o - top) for o in own]
         fade = jnp.exp(cache_top - top)
-        total = jnp.sum(held, 1, keepdims=True) + sum_ref[r] * fade
-        weights = weights + held / total
+        total = sum_ref[r] * fade
+        for h in held:
+            total = total + jnp.sum(h, 1, keepdims=True)
+        weights = [w + h / total for w, h in zip(weights, held)]
         kept_ref[r] = cached_ref[r] * (fade / total)
-    weights = weights.astype(w_ref.dtype)
-    for i in range(n):
-        w_ref[i] = weights
+    for w, w_ref in zip(weights, w_refs):
+        for i in range(n):
+            w_ref[i] = w.astype(w_ref.dtype)
 
 
 def value_kernel(
-    rows, size_ref, w_ref, row_ref, low_ref, high_ref, value_ref, out_ref, low, high, acc, mixed, sem
+    rows, size_ref, near_ref, rest_ref, row_ref, low_ref, high_ref, value_ref, out_ref,
+    low, high, values, acc, mixed, sem, value_sem,
 ):
     q = pl.program_id(0)
     n = low.shape[0]
-    kvh = value_ref.shape[0]
-    _, heads, lanes = w_ref.shape
+    kvh = values.shape[0]
+    _, heads, near = near_ref.shape
+    lanes = near + rest_ref.shape[2]
     per = rows * heads // kvh
     cuts = tile_cuts(lanes)
+    load_values = pltpu.make_async_copy(value_ref, values, value_sem)
 
     def copy(o, t):
         if t == 0:
@@ -250,12 +293,17 @@
             copy(o, 0).start()
             for t in range(1, len(cuts) - 1):
                 pl.when(size_ref[o] > cuts[t])(lambda o=o, t=t: copy(o, t).start())
+        load_values.start()
 
     def one(t):
         copy(q, t).wait()
         here = slice(cuts[t], cuts[t + 1])
         width = cuts[t + 1] - cuts[t]
-        weights = w_ref[0, :, here].astype(jnp.float32).reshape(kvh, 1, heads // kvh, width)
+        if cuts[t] < near:
+            weights = near_ref[0, :, here]
+        else:
+            weights = rest_ref[0, :, cuts[t] - near : cuts[t + 1] - near]
+        weights = weights.astype(jnp.float32).reshape(kvh, 1, heads // kvh, width)
         owner_row = row_ref[0, :, here]
         spread = jnp.concatenate(
             [jnp.where((owner_row == r)[None, None], weights, 0.0) for r in range(rows)], 1
@@ -277,8 +325,9 @@
 
     @pl.when(q == n - 1)
     def _():
+        load_values.wait()
         for h in range(kvh):
-            done = jnp.dot(mixed[h], value_ref[h], preferred_element_type=jnp.float32)
+            done = jnp.dot(mixed[h], values[h], preferred_element_type=jnp.float32)
             out_ref[:, h] = done.reshape(n, per, done.shape[1]).astype(out_ref.dtype)
 
 
@@ -304,26 +353,31 @@
 
 
 def project_kernel(n, core_ref, *refs):
-    row_refs, (weight_ref, own_ref, away_ref, gathered) = refs[:n], refs[n:]
-    rows = row_refs[0].shape[0]
-    cols = own_ref.shape[1]
+    row_refs, (weight_ref, own_ref, away_ref, gathered, weight, sem) = refs[:n], refs[n:]
+    rows, cols = row_refs[0].shape[0], own_ref.shape[1]
+    cuts = sem.shape[0]
+    span = weight.shape[0] // cuts
+    loads = [
+        pltpu.make_async_copy(
+            weight_ref.at[pl.ds(i * span, span)], weight.at[pl.ds(i * span, span)], sem.at[i]
+        )
+        for i in range(cuts)
+    ]
+    for load in loads:
+        load.start()
     for k in range(0, n, 2):
         pair = [row_refs[k + j][...].astype(jnp.float32) for j in range(2)]
         gathered[k * rows : (k + 2) * rows, :] = jnp.concatenate(pair).astype(gathered.dtype)
-    step = min(256, cols)
-    for i in range(0, 2 * cols, step):
-        done = jnp.dot(
-            gathered[...], weight_ref[:, i : i + step], preferred_element_type=jnp.float32
-        )
-        here = slice(i % cols, i % cols + step)
-
-        @pl.when(core_ref[0] == i // cols)
-        def _(done=done, here=here):
-            own_ref[:, here] = done
-
-        @pl.when(core_ref[0] != i // cols)
-        def _(done=done, here=here):
-            away_ref[:, here] = done
+    done = jnp.zeros((n * rows, 2 * cols), jnp.float32)
+    for i, load in enumerate(loads):
+        load.wait()
+        here = slice(i * span, (i + 1) * span)
+        done = done + jnp.dot(
+            gathered[:, here], weight[here, :], preferred_element_type=jnp.float32
+        )
+    first = core_ref[0] == 0
+    own_ref[...] = jnp.where(first, done[:, :cols], done[:, cols:])
+    away_ref[...] = jnp.where(first, done[:, cols:], done[:, :cols])
 
 
 def order_kernel(n, me_ref, own_ref, got_ref, out_ref):
@@ -440,7 +494,8 @@
     rowof = jnp.sum(jnp.where(inside, (block_row + 1)[None, :], 0), 1) - 1
     rowof = rowof.reshape(n, 1, lanes)
 
-    most = jnp.max(jnp.sum(block_fill.reshape(n, blocks), 1))
+    near = near_lanes(lanes)
+    most = jnp.stack([jnp.max(jnp.sum(block_fill.reshape(n, blocks), 1)), jnp.max(list_rows)])
     groups = lax.axis_size("groups")
     k = 1
     while k < groups:
@@ -448,7 +503,7 @@
             most, lax.ppermute(most, "groups", [(i, i ^ k) for i in range(groups)])
         )
         k *= 2
-    over = most > ntp * size
+    over, longer = most[0] > ntp * size, most[1] > near
 
     def exchange_rest():
         rest = pack(x_prompt, pack_fill, pack_dest, at, n, ntp * size, extra)
@@ -475,7 +530,7 @@
 
     even = from_rest(jnp.stack([queries, far]), n)
     keyed_even = through_keys(even)
-    odd = with_partner(even, 1, n)
+    keyed_odd = through_keys(with_partner(even, 1, n))
     values = kv_weight[:, :, hd:].transpose(1, 0, 2)
 
     query = query.reshape(rows, kvh, group, hd)
@@ -500,18 +555,24 @@
     cache_sum = cache_sum.reshape(rows, heads, 1)
     cached = cached.reshape(rows, heads, hd)
 
-    mine, odd, meta, list_rows, rowof, keyed_even, values, cache_top, cache_sum, cached = (
+    mine, meta, list_rows, rowof, keyed_even, keyed_odd, values, cache_top, cache_sum, cached = (
         lax.optimization_barrier(
-            (mine, odd, meta, list_rows, rowof, keyed_even, values, cache_top, cache_sum, cached)
+            (
+                mine, meta, list_rows, rowof, keyed_even, keyed_odd, values,
+                cache_top, cache_sum, cached,
+            )
         )
     )
     other = lax.ppermute(mine, "tp", swap)
-    keyed_odd = through_keys(odd)
 
     in_hbm = pl.BlockSpec(memory_space=pltpu.HBM)
     row_spec = pl.BlockSpec((1, 1, lanes), lambda q, m: (q, 0, 0))
-    slot_spec = pl.BlockSpec((1, heads, lanes), lambda q, m: (q, 0, 0))
-    slot_shape = jax.ShapeDtypeStruct((n, heads, lanes), jnp.bfloat16)
+    slot_specs = [
+        pl.BlockSpec((1, heads, length), lambda q, m: (q, 0, 0)) for length in (near, lanes - near)
+    ]
+    slot_shapes = [
+        jax.ShapeDtypeStruct((n, heads, length), jnp.bfloat16) for length in (near, lanes - near)
+    ]
     cuts = tile_cuts(lanes)
     list_shapes = [(n, cuts[1], part), (n, lanes - cuts[1], part)]
     list_scratch = [pltpu.VMEM(shape, jnp.bfloat16) for shape in list_shapes]
@@ -520,19 +581,20 @@
     def owner(i, m):
         return m[at_me] ^ reversed_bits(i, n)
 
-    partial_scores, low, high = pl.pallas_call(
+    score_near, score_rest, low, high = pl.pallas_call(
         functools.partial(score_kernel, n, rows),
         grid_spec=pltpu.PrefetchScalarGridSpec(
             num_scalar_prefetch=1,
             grid=(n,),
             in_specs=[
-                *[in_hbm] * 4,
-                pl.BlockSpec((kvh, per, part), lambda i, m: (0, jnp.minimum(i, n // 2 - 1), 0)),
-                pl.BlockSpec((kvh, per, part), lambda i, m: (0, jnp.maximum(i - n // 2, 0), 0)),
+                *[in_hbm] * 6,
                 pl.BlockSpec((1, 1, lanes), lambda i, m: (owner(i, m), 0, 0)),
             ],
             out_specs=[
-                pl.BlockSpec((1, heads, lanes), lambda i, m: (owner(i, m), 0, 0)),
+                *[
+                    pl.BlockSpec((1, heads, length), lambda i, m: (owner(i, m), 0, 0))
+                    for length in (near, lanes - near)
+                ],
                 in_hbm,
                 in_hbm,
             ],
@@ -540,53 +602,62 @@
                 pltpu.VMEM((ntp, n * size, part), jnp.bfloat16),
                 pltpu.VMEM((ntp, n * extra, part), jnp.bfloat16),
                 pltpu.VMEM((n * tokens, part), jnp.float32),
+                pltpu.VMEM((kvh, n * per, part), jnp.bfloat16),
                 *list_scratch,
                 pltpu.SemaphoreType.DMA((ntp, 4)),
+                pltpu.SemaphoreType.DMA((2, kvh)),
                 pltpu.SemaphoreType.DMA((n, len(cuts) - 1)),
             ],
         ),
         out_shape=[
-            slot_shape,
+            *slot_shapes,
             *[jax.ShapeDtypeStruct(shape, jnp.bfloat16) for shape in list_shapes],
         ],
         compiler_params=pltpu.CompilerParams(vmem_limit_bytes=56 * MIB),
         name="prompt_scores",
     )(meta, mine, other, more_mine, more_other, keyed_even, keyed_odd, rowof)
 
-    parts = lax.all_to_all(partial_scores, "pool", 0, 0, tiled=True)
     my_rows = lax.dynamic_index_in_dim(rowof, me, 0, keepdims=False)
-    weights, kept = pl.pallas_call(
-        functools.partial(weight_kernel, scale),
-        out_shape=[slot_shape, jax.ShapeDtypeStruct((rows, heads, hd), jnp.float32)],
-        compiler_params=pltpu.CompilerParams(vmem_limit_bytes=8 * MIB),
-        name="softmax_weights",
-    )(parts, my_rows, cache_top, cache_sum, cached)
-
-    all_weights = lax.all_to_all(weights, "pool", 0, 0, tiled=True)
+
+    def exchange_weights(*scores):
+        count = len(scores)
+        parts = [lax.all_to_all(s, "pool", 0, 0, tiled=True) for s in scores]
+        row_parts = [my_rows[:, :near], my_rows[:, near:]][:count]
+        *weights, kept = pl.pallas_call(
+            functools.partial(weight_kernel, scale, count),
+            out_shape=[*slot_shapes[:count], jax.ShapeDtypeStruct((rows, heads, hd), jnp.float32)],
+            compiler_params=pltpu.CompilerParams(vmem_limit_bytes=8 * MIB),
+            name="softmax_weights",
+        )(*parts, *row_parts, cache_top, cache_sum, cached)
+        return *[lax.all_to_all(w, "pool", 0, 0, tiled=True) for w in weights], kept
+
+    def near_only():
+        weights, kept = exchange_weights(score_near)
+        return weights, jnp.zeros(slot_shapes[1].shape, jnp.bfloat16), kept
+
+    weight_near, weight_rest, kept = lax.cond(
+        longer, lambda: exchange_weights(score_near, score_rest), near_only
+    )
     terms = pl.pallas_call(
         functools.partial(value_kernel, rows),
         grid_spec=pltpu.PrefetchScalarGridSpec(
             num_scalar_prefetch=1,
             grid=(n,),
-            in_specs=[
-                slot_spec,
-                row_spec,
-                in_hbm,
-                in_hbm,
-                pl.BlockSpec((kvh, part, hd), lambda q, m: (0, 0, 0)),
-            ],
+            in_specs=[*slot_specs, row_spec, in_hbm, in_hbm, in_hbm],
             out_specs=pl.BlockSpec((n, kvh, per, hd), lambda q, m: (0, 0, 0, 0)),
             scratch_shapes=[
                 *list_scratch,
+                pltpu.VMEM((kvh, part, hd), jnp.bfloat16),
                 pltpu.VMEM((kvh * per, part), jnp.float32),
                 pltpu.VMEM((kvh, n * per, part), jnp.bfloat16),
                 pltpu.SemaphoreType.DMA((n, len(cuts) - 1)),
+                pltpu.SemaphoreType.DMA,
             ],
         ),
         out_shape=jax.ShapeDtypeStruct((n, kvh, per, hd), jnp.bfloat16),
         compiler_params=pltpu.CompilerParams(vmem_limit_bytes=56 * MIB),
         name="weighted_values",
-    )(list_rows, all_weights, rowof, low, high, values)
+    )(list_rows, weight_near, weight_rest, rowof, low, high, values)
 
     term_parts = lax.all_to_all(terms, "pool", 0, 0, tiled=True)
     attended = pl.pallas_call(
@@ -607,13 +678,17 @@
             grid=(1,),
             in_specs=[
                 *[pl.BlockSpec((rows, heads * hd), lambda i, m: (0, 0))] * n,
-                pl.BlockSpec(out_weight.shape, lambda i, m: (0, 0)),
+                in_hbm,
             ],
             out_specs=[half_spec] * 2,
-            scratch_shapes=[pltpu.VMEM((n * rows, heads * hd), jnp.bfloat16)],
+            scratch_shapes=[
+                pltpu.VMEM((n * rows, heads * hd), jnp.bfloat16),
+                pltpu.VMEM(out_weight.shape, jnp.bfloat16),
+                pltpu.SemaphoreType.DMA((8,)),
+            ],
         ),
         out_shape=[half_shape] * 2,
-        compiler_params=pltpu.CompilerParams(vmem_limit_bytes=26 * MIB),
+        compiler_params=pltpu.CompilerParams(vmem_limit_bytes=56 * MIB),
         name="output_projection",
     )(core.reshape(1), *swap_parts([attended] * n, n), out_weight)
     got = lax.ppermute(away, "tp", swap)

time: 160 us -> 153 us (0.956)
  waiting for transfers between devices: 38.2 us -> 27.3 us
  starting transfers between devices: 25.2 us -> 29.6 us
  blocking collectives: 32 us -> 27.9 us
  other arithmetic: 7.45 us -> 10.4 us
  Pallas kernels: 30.5 us -> 32.4 us
    all_to_all x1, waiting for transfers between devices: 9.21 us -> 0.01 us  [local(): lax.all_to_all(packed, 'pool', 0, 0, tiled=True).reshape(n * size, part)]
    all_to_all x1, blocking collectives: 14.7 us -> 10.7 us  [exchange_weights(): lax.all_to_all(w, 'pool', 0, 0, tiled=True)]
    ppermute x10, starting transfers between devices: 15.4 us -> 18.3 us  [with_partner(): return lax.ppermute(x, 'pool', [(i, i ^ k) for i in range(n)])]
    pallas_call x1, Pallas kernels: 2.88 us -> 5.54 us  [local(): pl.pallas_call(functools.partial(project_kernel, n), grid_spec=pltpu.Pref...]
    unnamed x27 -> x51, local copies, waits for them, and re-layouts: 6.3 us -> 4.26 us
    all_to_all x1, waiting for transfers between devices: 9.99 us -> 7.99 us  [exchange_weights(): parts = [lax.all_to_all(s, 'pool', 0, 0, tiled=True) for s in scores]]
    max x0 -> x1, other arithmetic: none -> 1.95 us  [local(): jnp.maximum(most, lax.ppermute(most, 'groups', [(i, i ^ k) for i in range...]
    another operation x0 -> x1, other arithmetic: none -> 1.83 us  [local(): jnp.stack([jnp.max(jnp.sum(block_fill.reshape(n, blocks), 1)), jnp.max(li...]
  transfers between devices with their start and end apart: 15 -> 15, of which waited for: 9 -> 8; matrix products, arithmetic and copies ran while one was open for 15% -> 20% of each run, Pallas kernels for 3% -> 3%
where the time goes in v9:
time: 153 us
  Pallas kernels  32.4 us (21%)
  starting transfers between devices  29.6 us (19%)
  blocking collectives  27.9 us (18%)
  waiting for transfers between devices  27.3 us (18%)
  local copies, waits for them, and re-layouts  15.4 us (10%)
  other arithmetic  10.4 us (7%)
  matrix products  7.79 us (5%)
    ppermute x10, starting transfers between devices, with_partner(): return lax.ppermute(x, 'pool', [(i, i ^ k) for i in range(n)])  18.3 us
    ppermute x10, waiting for transfers between devices, with_partner(): return lax.ppermute(x, 'pool', [(i, i ^ k) for i in range(n)])  17.2 us
    all_to_all x1, blocking collectives, local(): term_parts = lax.all_to_all(terms, 'pool', 0, 0, tiled=True)  17.2 us
    pallas_call x1, Pallas kernels, local(): pl.pallas_call(functools.partial(score_kernel, n, rows), grid_spec=pltpu....  11.3 us
    all_to_all x1, blocking collectives, exchange_weights(): lax.all_to_all(w, 'pool', 0, 0, tiled=True)  10.7 us
    pallas_call x1, Pallas kernels, local(): pl.pallas_call(functools.partial(value_kernel, rows), grid_spec=pltpu.Pre...  9.42 us
    all_to_all x1, waiting for transfers between devices, exchange_weights(): parts = [lax.all_to_all(s, 'pool', 0, 0, tiled=True) for s in scores]  7.99 us
    pallas_call x1, Pallas kernels, local(): pl.pallas_call(functools.partial(project_kernel, n), grid_spec=pltpu.Pref...  5.54 us
  transfers between devices with their start and end apart: 15, of which 8 were waited for; matrix products, arithmetic and copies ran while one was open for 20% of the time, Pallas kernels for 3%

profile of v9, /device:TPU:0, one launch (start us, length us, event | category | flops | bytes accessed | tf_op | source)
XLA Modules:
  0.0 152.5 jit_solution(2730991858632410054)
XLA Ops:
  0.0 4.0 %collective-permute-start.1 = (bf16[8,32,128]{2,1,0:T(8,128)(2,1)}, bf16[8,32,128]{2,1,0:T(8,128)(2,1)S(1)}, u32[]{:S(2)}, u32[]{:S(2)}) collective-permute-start(bf16[8,32,128]{2,1,0:T(8,128)(2,1)} %param.18), channel_id=1, source_target_pairs={{0,8},{2,10},{4,12},{6,14},{8,0},{10,2},{12,4},{14,6},{1,9},{3,11}... | collective-permute-start | bytes 196616 | tf_op jit(solution)/shard_map/ppermute | solution.py:394
  4.1 2.4 %fusion.41 = (bf16[1024,4,128]{2,1,0:T(4,128)(2,1)S(1)}, bf16[1024,4,128]{2,1,0:T(4,128)(2,1)S(1)}) fusion(bf16[1024,4,256]{2,1,0:T(4,128)(2,1)} %param.14), kind=kLoop, calls=%fused_computation.99 | loop fusion | bytes 4194304 | tf_op jit(solution)/shard_map/slice | solution.py:534
  6.5 0.4 copy-done.3
  6.9 2.4 %fusion.40 = (bf16[8,256,4,128]{3,2,1,0:T(4,128)(2,1)S(1)}, bf16[8,256,4,128]{3,2,1,0:T(4,128)(2,1)}) fusion(bf16[8,256,4,256]{3,2,1,0:T(4,128)(2,1)S(1)} %copy-done.3), kind=kLoop, calls=%fused_computation.98 | loop fusion | bytes 8388608 | tf_op jit(solution)/shard_map/slice | solution.py:551
  9.5 1.1 copy.64
  10.6 4.2 %pack_live_tokens.3 = bf16[8,96,1024]{2,1,0:T(8,128)(2,1)} custom-call(s32[2]{0:T(128)S(1)} %pad_add_fusion.at_ref, s32[256]{0:T(256)S(1)} %copy-done.18, s32[256]{0:T(256)S(1)} %bitcast.51, bf16[256,8192]{1,0:T(8,128)(2,1)S(1)} %copy-done.2), custom_call_target="tpu_custom_call" | custom-call | flops 402653184 | bytes 67108864 | tf_op jit(solution)/shard_map/pack_live_tokens/pallas_call | solution.py:70
  14.9 4.3 %all-to-all-start.7 = ((bf16[8,96,1024]{2,1,0:T(8,128)(2,1)}), bf16[8,96,1024]{2,1,0:T(8,128)(2,1)}, u32[]{:S(2)}, u32[]{:S(2)}) async-start(bf16[8,96,1024]{2,1,0:T(8,128)(2,1)} %pack_live_tokens.3), calls=%async_computation.7 | async-start | bytes 3145728 | tf_op jit(solution)/shard_map/all_to_all | solution.py:457
  19.3 0.2 select_reduce_fusion.5
  19.6 0.1 fusion.38
  19.9 0.6 reduce_max.28
  20.6 0.1 reduce_sum.110
  20.7 0.7 reduce_max.27
  21.4 1.8 %pad_add_fusion.1 = s32[2]{0:T(128)} fusion(s32[1]{0:T(128)} %bitcast.6, s32[1]{0:T(128)} %bitcast.5), kind=kLoop, calls=%fused_computation.92 | loop fusion | flops 2 | bytes 16 | tf_op jit(solution)/shard_map/stack | solution.py:498
  23.2 1.5 collective-permute-start.2
  24.7 0.7 pad_maximum_fusion.2
  25.3 1.9 %collective-permute-start.3 = (bf16[2,8,32,128]{3,2,1,0:T(8,128)(2,1)}, bf16[2,8,32,128]{3,2,1,0:T(8,128)(2,1)}, u32[]{:S(2)}, u32[]{:S(2)}) collective-permute-start(bf16[2,8,32,128]{3,2,1,0:T(8,128)(2,1)} %pad_maximum_fusion.2), channel_id=1, source_target_pairs={{0,4},{2,6},{4,0},{6,2},{8,12},{10,14},{12,8},{14,10},{1,5},{3,7},... | collective-permute-start | bytes 393224 | tf_op jit(solution)/shard_map/ppermute | solution.py:394
  27.2 2.3 %fusion.43 = (f32[8,4,8]{2,1,0:T(4,128)S(1)}, f32[8,4,8,256]{3,2,1,0:T(8,128)S(1)}) fusion(bf16[8,256,4,128]{3,2,1,0:T(4,128)(2,1)} %get-tuple-element.140, bf16[8,32,128]{2,1,0:T(8,128)(2,1)S(1)} %copy-done.5, pred[8,256]{1,0:T(8,128)(4,1)S(1)} %iota_compare_fusion.4), kind=kOutput, calls=%fused_computation.101 | convolution fusion | flops 16973568 | bytes 2427904 | tf_op jit(solution)/shard_map/rhgd,rthd->rhgt/dot_general | solution.py:538
  29.6 0.7 reshape_broadcast_in_dim.6
  30.3 0.2 fusion.18
  30.5 0.7 reshape_broadcast_in_dim.7
  31.3 0.7 fusion.20
  32.0 0.3 select_reduce_fusion.2
  32.3 1.0 select_reduce_fusion
  33.3 0.6 broadcast_add_fusion
  33.9 0.4 fusion.11
  34.4 1.9 %fusion.44 = s32[2]{0:T(128)S(1)} fusion(s32[2]{0:T(128)} %collective-permute-done.2, s32[1]{0:T(128)} %bitcast.6, s32[1]{0:T(128)} %bitcast.5), kind=kLoop, calls=%fused_computation.102 | loop fusion | flops 4 | bytes 24 | tf_op jit(solution)/shard_map/max | solution.py:502
  36.3 0.6 fusion.42
  37.5 1.3 concatenate.16.meta_ref
  38.9 9.4 %collective-permute-done.3 = bf16[2,8,32,128]{3,2,1,0:T(8,128)(2,1)} collective-permute-done((bf16[2,8,32,128]{3,2,1,0:T(8,128)(2,1)}, bf16[2,8,32,128]{3,2,1,0:T(8,128)(2,1)}, u32[]{:S(2)}, u32[]{:S(2)}) %collective-permute-start.3) | collective-permute-done | bytes 131104 | tf_op jit(solution)/shard_map/ppermute | solution.py:394
  48.2 1.0 pad_maximum_fusion.1
  49.2 1.1 collective-permute-start.4
  50.3 3.0 %convolution_convert_fusion.1 = bf16[4,4,8,8,1024]{4,3,2,1,0:T(8,128)(2,1)} fusion(bf16[1024,4,128]{2,1,0:T(4,128)(2,1)S(1)} %get-tuple-element.142, bf16[2,8,4,8,128]{4,3,2,1,0:T(8,128)(2,1)} %bitcast.12, bf16[1,8,4,8,128]{4,3,2,1,0:T(8,128)(2,1)} %bitcast.47, bf16[1,8,4,8,128]{4,3,2,1,0:T(8,128)(2,1)} %bitcast.43), kind=kOutput, calls=%fused_computation.9 | convolution fusion | flops 269746176 | bytes 3407872 | tf_op jit(solution)/shard_map/qrhgd,phd->hqrgp/dot_general | solution.py:526
  53.3 3.1 %collective-permute-done.4 = bf16[4,8,32,128]{3,2,1,0:T(8,128)(2,1)S(1)} collective-permute-done((bf16[4,8,32,128]{3,2,1,0:T(8,128)(2,1)S(1)}, bf16[4,8,32,128]{3,2,1,0:T(8,128)(2,1)S(1)}, u32[]{:S(2)}, u32[]{:S(2)}) %collective-permute-start.4) | collective-permute-done | bytes 262176 | tf_op jit(solution)/shard_map/ppermute | solution.py:394
  56.5 2.0 %convolution_convert_fusion = bf16[4,4,8,8,1024]{4,3,2,1,0:T(8,128)(2,1)} fusion(bf16[1024,4,128]{2,1,0:T(4,128)(2,1)S(1)} %get-tuple-element.142, bf16[4,8,32,128]{3,2,1,0:T(8,128)(2,1)S(1)} %collective-permute-done.4), kind=kOutput, calls=%fused_computation.8 | convolution fusion | flops 269484032 | bytes 3407872 | tf_op jit(solution)/shard_map/qrhgd,phd->hqrgp/dot_general | solution.py:526
  59.1 1.7 %conditional.2 = (bf16[256,1024]{1,0:T(8,128)(2,1)}, bf16[256,1024]{1,0:T(8,128)(2,1)}) conditional(s32[]{:T(128)} %bitcast.23, () %tuple.25, (s32[2]{0:T(128)S(1)}, s32[256]{0:T(256)S(1)}, s32[256]{0:T(256)S(1)}, bf16[256,8192]{1,0:T(8,128)(2,1)}) %tuple.54), branch_computations={%region_14.15_spmd, %region_15.16_spmd} | conditional | flops 134217728 | bytes 70254648 | solution.py:516
  59.1 0.9 broadcast.393
  60.0 0.9 broadcast.393.clone
  60.8 0.7 dynamic-slice_bitcast_fusion
  61.5 0.6 collective-permute-done.5.refs_1_
  62.1 1.2 copy-done.4
  63.3 11.3 %prompt_scores.1 = (bf16[8,32,384]{2,1,0:T(8,128)(2,1)}, bf16[8,32,256]{2,1,0:T(8,128)(2,1)S(1)}, bf16[8,256,1024]{2,1,0:T(8,128)(2,1)}, bf16[8,384,1024]{2,1,0:T(8,128)(2,1)}) custom-call(s32[651]{0:T(1024)} %concatenate.16.meta_ref, bf16[768,1024]{1,0:T(8,128)(2,1)} %bitcast.4.refs_0_, bf16[768,1024]{1,0:T(8,128)(2,1)} %copy-done.4, ...), custom_call_target="tpu_custom_call" | custom-call | tf_op jit(solution)/shard_map/prompt_scores/pallas_call | solution.py:584
  74.6 25.9 %conditional.3 = (bf16[8,32,384]{2,1,0:T(8,128)(2,1)S(1)}, bf16[8,32,256]{2,1,0:T(8,128)(2,1)S(1)}, f32[8,32,128]{2,1,0:T(8,128)S(1)}) conditional(s32[]{:T(128)} %bitcast.22, (bf16[8,32,384]{2,1,0:T(8,128)(2,1)}, s32[1,640]{1,0:T(1,128)S(1)}, f32[8,32,1]{1,0,2:T(8,128)S(1)}, f32[8,32,1]{1,0,2:T(8,128)S(1)}, ...), branch_computations={%region_16.17_spmd, %region_17.18_spmd} | conditional | bytes 1516600 | solution.py:638
  74.6 5.5 %all-to-all-start.1 = ((bf16[8,32,384]{2,1,0:T(8,128)(2,1)}), bf16[8,32,384]{2,1,0:T(8,128)(2,1)S(1)}, u32[]{:S(2)}, u32[]{:S(2)}) async-start(bf16[8,32,384]{2,1,0:T(8,128)(2,1)} %get-tuple-element.39), calls=%async_computation.1 | async-start | bytes 393216 | tf_op jit(solution)/shard_map/cond/branch_0_fun/all_to_all | solution.py:624
  80.1 0.1 copy.34.refs_2_
  80.2 0.1 copy.35.refs_3_
  80.4 8.0 %all-to-all-done.1.refs_0_ = bf16[8,32,384]{2,1,0:T(8,128)(2,1)S(1)} async-done(((bf16[8,32,384]{2,1,0:T(8,128)(2,1)}), bf16[8,32,384]{2,1,0:T(8,128)(2,1)S(1)}, u32[]{:S(2)}, u32[]{:S(2)}) %all-to-all-start.1) | async-done | bytes 196640 | tf_op jit(solution)/shard_map/cond/branch_0_fun/all_to_all | solution.py:624
  88.4 1.2 softmax_weights.2
  89.6 10.7 %all_to_all.39 = bf16[8,32,384]{2,1,0:T(8,128)(2,1)S(1)} all-to-all(bf16[8,32,384]{2,1,0:T(8,128)(2,1)S(1)} %get-tuple-element.44), channel_id=1, replica_groups=mesh['groups'=2,'pool'=8,'tp'=2] {'pool'}, dimensions={0} | all-to-all | bytes 393216 | tf_op jit(solution)/shard_map/cond/branch_0_fun/all_to_all | solution.py:632
  100.5 9.4 %weighted_values.1 = bf16[8,4,64,128]{3,2,1,0:T(8,128)(2,1)} custom-call(s32[8]{0:T(128)} %copy-done.20, bf16[8,32,384]{2,1,0:T(8,128)(2,1)S(1)} %get-tuple-element.101.near_ref, bf16[8,32,256]{2,1,0:T(8,128)(2,1)S(1)} %get-tuple-element.102.rest_ref, s32[8,1,640]{2,1,0:T(1,128)} %bitcast.50, bf16[8,256,1024]{2,1,0:T(8,128)(2,1)} %get-tuple-element.103.low_ref, ...), custom_call_target="tpu_custom_call" | custom-call | tf_op jit(solution)/shard_map/weighted_values/pallas_call | solution.py:641
  109.9 17.2 %all_to_all.43.parts_ref = bf16[8,4,64,128]{3,2,1,0:T(8,128)(2,1)S(1)} all-to-all(bf16[8,4,64,128]{3,2,1,0:T(8,128)(2,1)} %weighted_values.1), channel_id=1, replica_groups=mesh['groups'=2,'pool'=8,'tp'=2] {'pool'}, dimensions={0} | all-to-all | bytes 1048576 | tf_op jit(solution)/shard_map/all_to_all | solution.py:662
  127.2 1.6 %collective-permute-start.6 = (bf16[8,4096]{1,0:T(8,128)(2,1)S(1)}, bf16[8,4096]{1,0:T(8,128)(2,1)S(1)}, u32[]{:S(2)}, u32[]{:S(2)}) collective-permute-start(bf16[8,4096]{1,0:T(8,128)(2,1)S(1)} %attended_sum.1.refs_0_), channel_id=1, source_target_pairs={{0,2},{2,0},{4,6},{6,4},{8,10},{10,8},{12,14},{14,12},{1,3},{3,1},... | collective-permute-start | bytes 196616 | tf_op jit(solution)/shard_map/ppermute | solution.py:394
  128.8 2.0 %collective-permute-start.8 = (bf16[8,4096]{1,0:T(8,128)(2,1)S(1)}, bf16[8,4096]{1,0:T(8,128)(2,1)S(1)}, u32[]{:S(2)}, u32[]{:S(2)}) collective-permute-start(bf16[8,4096]{1,0:T(8,128)(2,1)S(1)} %attended_sum.1.refs_0_), channel_id=1, source_target_pairs={{0,6},{2,4},{4,2},{6,0},{8,14},{10,12},{12,10},{14,8},{1,7},{3,5},... | collective-permute-start | bytes 196616 | tf_op jit(solution)/shard_map/ppermute | solution.py:394
  130.7 1.1 collective-permute-start.9
  131.9 2.8 %collective-permute-start.10 = (bf16[8,4096]{1,0:T(8,128)(2,1)S(1)}, bf16[8,4096]{1,0:T(8,128)(2,1)S(1)}, u32[]{:S(2)}, u32[]{:S(2)}) collective-permute-start(bf16[8,4096]{1,0:T(8,128)(2,1)S(1)} %attended_sum.1.refs_0_), channel_id=1, source_target_pairs={{0,10},{2,8},{4,14},{6,12},{8,2},{10,0},{12,6},{14,4},{1,11},{3,9}... | collective-permute-start | bytes 196616 | tf_op jit(solution)/shard_map/ppermute | solution.py:394
  134.6 1.4 collective-permute-start.11
  136.0 2.4 %collective-permute-start.12 = (bf16[8,4096]{1,0:T(8,128)(2,1)S(1)}, bf16[8,4096]{1,0:T(8,128)(2,1)S(1)}, u32[]{:S(2)}, u32[]{:S(2)}) collective-permute-start(bf16[8,4096]{1,0:T(8,128)(2,1)S(1)} %attended_sum.1.refs_0_), channel_id=1, source_target_pairs={{0,14},{2,12},{4,10},{6,8},{8,6},{10,4},{12,2},{14,0},{1,15},{3,13... | collective-permute-start | bytes 196616 | tf_op jit(solution)/shard_map/ppermute | solution.py:394
  138.4 1.5 collective-permute-done.9.refs_4_
  139.9 2.2 %collective-permute-done.10.refs_5_ = bf16[8,4096]{1,0:T(8,128)(2,1)S(1)} collective-permute-done((bf16[8,4096]{1,0:T(8,128)(2,1)S(1)}, bf16[8,4096]{1,0:T(8,128)(2,1)S(1)}, u32[]{:S(2)}, u32[]{:S(2)}) %collective-permute-start.10) | collective-permute-done | bytes 65568 | tf_op jit(solution)/shard_map/ppermute | solution.py:394
  142.1 1.0 collective-permute-done.12.refs_7_
  143.2 0.6 copy-done.13
  143.8 5.5 %output_projection.1 = (f32[64,512]{1,0:T(8,128)}, f32[64,512]{1,0:T(8,128)}) custom-call(s32[1]{0:T(128)} %bitcast.2.core_ref, bf16[8,4096]{1,0:T(8,128)(2,1)} %copy-done, bf16[8,4096]{1,0:T(8,128)(2,1)} %copy-done.7, bf16[8,4096]{1,0:T(8,128)(2,1)} %copy-done.8, bf16[8,4096]{1,0:T(8,128)(2,1)} %copy-done.9, bf16[8,4096]{1,0:T(8,128)(2,1)} %copy-done.10, ...), custom_call_target="tpu_custom_call" | custom-call | tf_op jit(solution)/shard_map/output_projection/pallas_call | solution.py:674
  149.4 1.5 %collective-permute-done.13.got_ref = f32[64,512]{1,0:T(8,128)S(1)} collective-permute-done((f32[64,512]{1,0:T(8,128)}, f32[64,512]{1,0:T(8,128)S(1)}, u32[]{:S(2)}, u32[]{:S(2)}) %collective-permute-start.13) | collective-permute-done | bytes 131104 | tf_op jit(solution)/shard_map/ppermute | solution.py:694
  151.0 0.9 copy-done.1
  151.9 0.6 order_rows.1
  (75 shorter events, 1.0 us)
Async XLA Ops:
  0.0 14.9 %collective-permute-start.1 = (bf16[8,32,128]{2,1,0:T(8,128)(2,1)}, bf16[8,32,128]{2,1,0:T(8,128)(2,1)S(1)}, u32[]{:S(2)}, u32[]{:S(2)}) collective-permute-start(bf16[8,32,128]{2,1,0:T(8,128)(2,1)} %param.18), channel_id=1, source_target_pairs={{0,8},{2,10},{4,12},{6,14},{8,0},{10,2},{12,4},{14,6},{1,9},{3,11}... | collective-permute-start | bytes 196616 | tf_op jit(solution)/shard_map/ppermute | solution.py:394
  4.1 2.8 %copy-start.3 = (bf16[8,256,4,256]{3,2,1,0:T(4,128)(2,1)S(1)}, bf16[8,256,4,256]{3,2,1,0:T(4,128)(2,1)}, u32[]{:S(2)}) copy-start(bf16[8,256,4,256]{3,2,1,0:T(4,128)(2,1)} %param.19) | copy-start | bytes 12582916
  6.9 2.4 %copy-start.24 = (s32[8]{0:T(128)S(1)}, s32[8]{0:T(128)}, u32[]{:S(2)}) copy-start(s32[8]{0:T(128)} %param.20) | copy-start | bytes 100
  6.9 3.7 %copy-start.2 = (bf16[256,8192]{1,0:T(8,128)(2,1)S(1)}, bf16[256,8192]{1,0:T(8,128)(2,1)}, u32[]{:S(2)}) copy-start(bf16[256,8192]{1,0:T(8,128)(2,1)} %x_ref.1) | copy-start | bytes 12582916
  9.3 1.3 copy-start.14
  9.3 1.3 copy-start.18
  9.5 5.4 %copy-start.21 = (s32[2]{0:T(128)}, s32[2]{0:T(128)S(1)}, u32[]{:S(2)}) copy-start(s32[2]{0:T(128)S(1)} %pad_add_fusion.at_ref) | copy-start | bytes 28
  14.8 9.9 %copy-start.23 = (s32[256]{0:T(256)S(1)}, s32[256]{0:T(256)}, u32[]{:S(2)}) copy-start(s32[256]{0:T(256)} %param.16) | copy-start | bytes 3076
  14.8 9.8 %copy-start.5 = (bf16[8,32,128]{2,1,0:T(8,128)(2,1)S(1)}, bf16[8,32,128]{2,1,0:T(8,128)(2,1)}, u32[]{:S(2)}) copy-start(bf16[8,32,128]{2,1,0:T(8,128)(2,1)} %param.18) | copy-start | bytes 196612
  14.9 12.4 %copy-start.6 = (bf16[8,32,128]{2,1,0:T(8,128)(2,1)}, bf16[8,32,128]{2,1,0:T(8,128)(2,1)S(1)}, u32[]{:S(2)}) copy-start(bf16[8,32,128]{2,1,0:T(8,128)(2,1)S(1)} %collective-permute-done.1) | copy-start | bytes 196612
  14.9 43.6 %all-to-all-start.7 = ((bf16[8,96,1024]{2,1,0:T(8,128)(2,1)}), bf16[8,96,1024]{2,1,0:T(8,128)(2,1)}, u32[]{:S(2)}, u32[]{:S(2)}) async-start(bf16[8,96,1024]{2,1,0:T(8,128)(2,1)} %pack_live_tokens.3), calls=%async_computation.7 | async-start | bytes 3145728 | tf_op jit(solution)/shard_map/all_to_all | solution.py:457
  19.8 7.5 %copy-start.20 = (s32[8]{0:T(128)}, s32[8]{0:T(128)S(1)}, u32[]{:S(2)}) copy-start(s32[8]{0:T(128)S(1)} %get-tuple-element.88.size_ref) | copy-start | bytes 100
  23.2 11.2 %collective-permute-start.2 = (s32[2]{0:T(128)}, s32[2]{0:T(128)}, u32[]{:S(2)}, u32[]{:S(2)}) collective-permute-start(s32[2]{0:T(128)} %pad_add_fusion.1), channel_id=1, source_target_pairs={{0,16},{16,0},{1,17},{17,1},{2,18},{18,2},{3,19},{19,3},{4,20},{20... | collective-permute-start | bytes 32 | tf_op jit(solution)/shard_map/ppermute | solution.py:503
  25.3 22.9 %collective-permute-start.3 = (bf16[2,8,32,128]{3,2,1,0:T(8,128)(2,1)}, bf16[2,8,32,128]{3,2,1,0:T(8,128)(2,1)}, u32[]{:S(2)}, u32[]{:S(2)}) collective-permute-start(bf16[2,8,32,128]{3,2,1,0:T(8,128)(2,1)} %pad_maximum_fusion.2), channel_id=1, source_target_pairs={{0,4},{2,6},{4,0},{6,2},{8,12},{10,14},{12,8},{14,10},{1,5},{3,7},... | collective-permute-start | bytes 393224 | tf_op jit(solution)/shard_map/ppermute | solution.py:394
  49.2 7.3 %collective-permute-start.4 = (bf16[4,8,32,128]{3,2,1,0:T(8,128)(2,1)S(1)}, bf16[4,8,32,128]{3,2,1,0:T(8,128)(2,1)S(1)}, u32[]{:S(2)}, u32[]{:S(2)}) collective-permute-start(bf16[4,8,32,128]{3,2,1,0:T(8,128)(2,1)S(1)} %pad_maximum_fusion.1), channel_id=1, source_target_pairs={{0,2},{2,0},{4,6},{6,4},{8,10},{10,8},{12,14},{14,12},{1,3},{3,1},... | collective-permute-start | bytes 786440 | tf_op jit(solution)/shard_map/ppermute | solution.py:394
  53.3 5.7 %copy-start.15 = (s32[256,1]{0,1:T(1,128)S(1)}, s32[256,1]{0,1:T(1,128)}, u32[]{:S(2)}) copy-start(s32[256,1]{0,1:T(1,128)} %param.15) | copy-start | bytes 3076
  53.3 5.7 %copy-start.19 = (s32[256]{0:T(256)S(1)}, s32[256]{0:T(256)}, u32[]{:S(2)}) copy-start(s32[256]{0:T(256)} %fill_ref.1) | copy-start | bytes 3076
  53.3 5.8 %copy-start.22 = (s32[2]{0:T(128)S(1)}, s32[2]{0:T(128)}, u32[]{:S(2)}) copy-start(s32[2]{0:T(128)} %copy-done.21) | copy-start | bytes 28
  58.5 3.6 %collective-permute-start.5 = (bf16[768,1024]{1,0:T(8,128)(2,1)}, bf16[768,1024]{1,0:T(8,128)(2,1)S(1)}, u32[]{:S(2)}, u32[]{:S(2)}) collective-permute-start(bf16[768,1024]{1,0:T(8,128)(2,1)} %bitcast.4.refs_0_), channel_id=1, source_target_pairs={{0,1},{1,0},{2,3},{3,2},{4,5},{5,4},{6,7},{7,6},{8,9},{9,8},{10,11... | collective-permute-start | bytes 4718600 | tf_op jit(solution)/shard_map/ppermute | solution.py:566
  62.1 1.2 copy-start.4
  63.3 11.3 %copy-start.16 = (f32[8,32,1]{1,0,2:T(8,128)S(1)}, f32[8,32,1]{1,0,2:T(8,128)}, u32[]{:S(2)}) copy-start(f32[8,32,1]{1,0,2:T(8,128)} %reshape_broadcast_in_dim.6) | copy-start | bytes 3076
  63.3 11.3 %copy-start.17 = (f32[8,32,1]{1,0,2:T(8,128)S(1)}, f32[8,32,1]{1,0,2:T(8,128)}, u32[]{:S(2)}) copy-start(f32[8,32,1]{1,0,2:T(8,128)} %reshape_broadcast_in_dim.7) | copy-start | bytes 3076
  74.6 13.7 %all-to-all-start.1 = ((bf16[8,32,384]{2,1,0:T(8,128)(2,1)}), bf16[8,32,384]{2,1,0:T(8,128)(2,1)S(1)}, u32[]{:S(2)}, u32[]{:S(2)}) async-start(bf16[8,32,384]{2,1,0:T(8,128)(2,1)} %get-tuple-element.39), calls=%async_computation.1 | async-start | bytes 393216 | tf_op jit(solution)/shard_map/cond/branch_0_fun/all_to_all | solution.py:624
  127.2 15.9 %copy-start = (bf16[8,4096]{1,0:T(8,128)(2,1)}, bf16[8,4096]{1,0:T(8,128)(2,1)S(1)}, u32[]{:S(2)}) copy-start(bf16[8,4096]{1,0:T(8,128)(2,1)S(1)} %attended_sum.1.refs_0_) | copy-start | bytes 196612
  127.2 7.4 %collective-permute-start.6 = (bf16[8,4096]{1,0:T(8,128)(2,1)S(1)}, bf16[8,4096]{1,0:T(8,128)(2,1)S(1)}, u32[]{:S(2)}, u32[]{:S(2)}) collective-permute-start(bf16[8,4096]{1,0:T(8,128)(2,1)S(1)} %attended_sum.1.refs_0_), channel_id=1, source_target_pairs={{0,2},{2,0},{4,6},{6,4},{8,10},{10,8},{12,14},{14,12},{1,3},{3,1},... | collective-permute-start | bytes 196616 | tf_op jit(solution)/shard_map/ppermute | solution.py:394
  128.8 7.3 %collective-permute-start.7 = (bf16[8,4096]{1,0:T(8,128)(2,1)S(1)}, bf16[8,4096]{1,0:T(8,128)(2,1)S(1)}, u32[]{:S(2)}, u32[]{:S(2)}) collective-permute-start(bf16[8,4096]{1,0:T(8,128)(2,1)S(1)} %attended_sum.1.refs_0_), channel_id=1, source_target_pairs={{0,4},{2,6},{4,0},{6,2},{8,12},{10,14},{12,8},{14,10},{1,5},{3,7},... | collective-permute-start | bytes 196616 | tf_op jit(solution)/shard_map/ppermute | solution.py:394
  128.8 9.6 %collective-permute-start.8 = (bf16[8,4096]{1,0:T(8,128)(2,1)S(1)}, bf16[8,4096]{1,0:T(8,128)(2,1)S(1)}, u32[]{:S(2)}, u32[]{:S(2)}) collective-permute-start(bf16[8,4096]{1,0:T(8,128)(2,1)S(1)} %attended_sum.1.refs_0_), channel_id=1, source_target_pairs={{0,6},{2,4},{4,2},{6,0},{8,14},{10,12},{12,10},{14,8},{1,7},{3,5},... | collective-permute-start | bytes 196616 | tf_op jit(solution)/shard_map/ppermute | solution.py:394
  130.7 9.2 %collective-permute-start.9 = (bf16[8,4096]{1,0:T(8,128)(2,1)S(1)}, bf16[8,4096]{1,0:T(8,128)(2,1)S(1)}, u32[]{:S(2)}, u32[]{:S(2)}) collective-permute-start(bf16[8,4096]{1,0:T(8,128)(2,1)S(1)} %attended_sum.1.refs_0_), channel_id=1, source_target_pairs={{0,8},{2,10},{4,12},{6,14},{8,0},{10,2},{12,4},{14,6},{1,9},{3,11}... | collective-permute-start | bytes 196616 | tf_op jit(solution)/shard_map/ppermute | solution.py:394
  131.9 10.3 %collective-permute-start.10 = (bf16[8,4096]{1,0:T(8,128)(2,1)S(1)}, bf16[8,4096]{1,0:T(8,128)(2,1)S(1)}, u32[]{:S(2)}, u32[]{:S(2)}) collective-permute-start(bf16[8,4096]{1,0:T(8,128)(2,1)S(1)} %attended_sum.1.refs_0_), channel_id=1, source_target_pairs={{0,10},{2,8},{4,14},{6,12},{8,2},{10,0},{12,6},{14,4},{1,11},{3,9}... | collective-permute-start | bytes 196616 | tf_op jit(solution)/shard_map/ppermute | solution.py:394
  134.6 8.5 %copy-start.7 = (bf16[8,4096]{1,0:T(8,128)(2,1)}, bf16[8,4096]{1,0:T(8,128)(2,1)S(1)}, u32[]{:S(2)}) copy-start(bf16[8,4096]{1,0:T(8,128)(2,1)S(1)} %collective-permute-done.6.refs_1_) | copy-start | bytes 196612
  134.6 7.5 %collective-permute-start.11 = (bf16[8,4096]{1,0:T(8,128)(2,1)S(1)}, bf16[8,4096]{1,0:T(8,128)(2,1)S(1)}, u32[]{:S(2)}, u32[]{:S(2)}) collective-permute-start(bf16[8,4096]{1,0:T(8,128)(2,1)S(1)} %attended_sum.1.refs_0_), channel_id=1, source_target_pairs={{0,12},{2,14},{4,8},{6,10},{8,4},{10,6},{12,0},{14,2},{1,13},{3,15... | collective-permute-start | bytes 196616 | tf_op jit(solution)/shard_map/ppermute | solution.py:394
  136.0 7.1 %copy-start.8 = (bf16[8,4096]{1,0:T(8,128)(2,1)}, bf16[8,4096]{1,0:T(8,128)(2,1)S(1)}, u32[]{:S(2)}) copy-start(bf16[8,4096]{1,0:T(8,128)(2,1)S(1)} %collective-permute-done.7.refs_2_) | copy-start | bytes 196612
  136.0 7.1 %collective-permute-start.12 = (bf16[8,4096]{1,0:T(8,128)(2,1)S(1)}, bf16[8,4096]{1,0:T(8,128)(2,1)S(1)}, u32[]{:S(2)}, u32[]{:S(2)}) collective-permute-start(bf16[8,4096]{1,0:T(8,128)(2,1)S(1)} %attended_sum.1.refs_0_), channel_id=1, source_target_pairs={{0,14},{2,12},{4,10},{6,8},{8,6},{10,4},{12,2},{14,0},{1,15},{3,13... | collective-permute-start | bytes 196616 | tf_op jit(solution)/shard_map/ppermute | solution.py:394
  138.4 4.7 %copy-start.9 = (bf16[8,4096]{1,0:T(8,128)(2,1)}, bf16[8,4096]{1,0:T(8,128)(2,1)S(1)}, u32[]{:S(2)}) copy-start(bf16[8,4096]{1,0:T(8,128)(2,1)S(1)} %collective-permute-done.8.refs_3_) | copy-start | bytes 196612
  139.9 3.2 %copy-start.10 = (bf16[8,4096]{1,0:T(8,128)(2,1)}, bf16[8,4096]{1,0:T(8,128)(2,1)S(1)}, u32[]{:S(2)}) copy-start(bf16[8,4096]{1,0:T(8,128)(2,1)S(1)} %collective-permute-done.9.refs_4_) | copy-start | bytes 196612
  142.1 1.0 copy-start.11
  142.1 1.0 copy-start.12
  143.2 0.6 copy-start.13
  149.3 1.6 %collective-permute-start.13 = (f32[64,512]{1,0:T(8,128)}, f32[64,512]{1,0:T(8,128)S(1)}, u32[]{:S(2)}, u32[]{:S(2)}) collective-permute-start(f32[64,512]{1,0:T(8,128)} %get-tuple-element.108), channel_id=1, source_target_pairs={{0,1},{1,0},{2,3},{3,2},{4,5},{5,4},{6,7},{7,6},{8,9},{9,8},{10,11... | collective-permute-start | bytes 393224 | tf_op jit(solution)/shard_map/ppermute | solution.py:694
  150.9 0.9 copy-start.1

commit v10 on v9

--- a/solution.py
+++ b/solution.py
@@ -99,10 +99,9 @@
     return min(lanes, -(-lanes * 3 // 5 // 128) * 128)
 
 
-def load_tokens(n, core, over, x_refs, held, more, wide, sem, others):
+def load_tokens(n, core, over, x_refs, held, more, wide, sem):
     size, extra = held.shape[1] // n, more.shape[1] // n
     tokens = 2 * (size + extra)
-    part = wide.shape[1]
     cuts = sem.shape[1]
 
     def copies(refs, buffer):
@@ -133,8 +132,6 @@
     for pair in main:
         for copy in pair:
             copy.start()
-    for copy in others:
-        copy.start()
     for i, pair in enumerate(main):
         for copy in pair:
             copy.wait()
@@ -152,11 +149,18 @@
         widen(more, 2 * size, 0, n)
 
 
+def list_tile(meta_ref, first, count, wide, tile):
+    for i in range(0, count, 2):
+        pair = [
+            wide[pl.ds(pl.multiple_of(meta_ref[first + i + j], BLK), BLK), :] for j in range(2)
+        ]
+        tile[i * BLK : (i + 2) * BLK, :] = jnp.concatenate(pair).astype(tile.dtype)
+    return tile[: count * BLK, :]
+
+
 def score_kernel(n, rows, meta_ref, *refs):
-    x_refs, keyed_refs, (row_ref, near_ref, rest_ref, low_ref, high_ref) = (
-        refs[:4], refs[4:6], refs[6:11]
-    )
-    held, more, wide, keyed, low, high, in_sem, keyed_sem, out_sem = refs[11:]
+    x_refs, (even_ref, odd_ref, row_ref), (near_ref, rest_ref) = refs[:4], refs[4:7], refs[7:9]
+    held, more, wide, tile, sem = refs[9:]
     step = pl.program_id(0)
     part = wide.shape[1]
     near = near_ref.shape[2]
@@ -165,58 +169,26 @@
     groups = lanes // BLK
     at_size = n * groups
     q = meta_ref[at_size + n] ^ reversed_bits(step, n)
-    kvh, per = keyed.shape[0], keyed.shape[1] // n
+    kvh, per = even_ref.shape[0], even_ref.shape[1] * 2 // n
     group = per // rows
 
     @pl.when(step == 0)
     def _():
-        loads = [
-            pltpu.make_async_copy(
-                ref.at[h], keyed.at[h, pl.ds(i * n // 2 * per, n // 2 * per)], keyed_sem.at[i, h]
-            )
-            for i, ref in enumerate(keyed_refs)
-            for h in range(kvh)
-        ]
         load_tokens(
-            n,
-            meta_ref[at_size + n + 1],
-            meta_ref[at_size + n + 2],
-            x_refs,
-            held,
-            more,
-            wide,
-            in_sem,
-            loads,
-        )
-        for load in loads:
-            load.wait()
-
-    def copy(o, t):
-        if t == 0:
-            return pltpu.make_async_copy(low.at[o], low_ref.at[o], out_sem.at[o, 0])
-        here = pl.ds(cuts[t] - cuts[1], cuts[t + 1] - cuts[t])
-        return pltpu.make_async_copy(
-            high.at[o, here], high_ref.at[o, here], out_sem.at[o, t]
-        )
-
-    def one(t):
+            n, meta_ref[at_size + n + 1], meta_ref[at_size + n + 2], x_refs, held, more, wide, sem
+        )
+
+    def one(keyed_ref, at, t):
         here = slice(cuts[t], cuts[t + 1])
-        buffer, base = (low, 0) if t == 0 else (high, cuts[1])
-        for i in range(cuts[t], cuts[t + 1], 2 * BLK):
-            pair = [
-                wide[pl.ds(pl.multiple_of(meta_ref[q * groups + i // BLK + j], BLK), BLK), :]
-                for j in range(2)
-            ]
-            buffer[q, i - base : i - base + 2 * BLK, :] = jnp.concatenate(pair).astype(low.dtype)
-        copy(q, t).start()
+        count = (cuts[t + 1] - cuts[t]) // BLK
         raw = lax.dot_general(
-            keyed[:, pl.ds(pl.multiple_of(step * per, per), per), :].reshape(kvh * per, part),
-            buffer[q, cuts[t] - base : cuts[t + 1] - base, :],
+            keyed_ref[:, pl.ds(pl.multiple_of(at * per, per), per), :].reshape(kvh * per, part),
+            list_tile(meta_ref, q * groups + cuts[t] // BLK, count, wide, tile),
             (((1,), (1,)), ((), ())),
             preferred_element_type=jnp.float32,
-        ).reshape(kvh, rows, group, cuts[t + 1] - cuts[t])
+        ).reshape(kvh, rows, group, count * BLK)
         owner_row = row_ref[0, :, here]
-        picked = jnp.zeros((kvh, group, cuts[t + 1] - cuts[t]), jnp.float32)
+        picked = jnp.zeros((kvh, group, count * BLK), jnp.float32)
         for r in range(rows):
             picked = picked + jnp.where((owner_row == r)[None], raw[:, r], 0.0)
         picked = picked.reshape(kvh * group, -1).astype(near_ref.dtype)
@@ -225,16 +197,13 @@
         else:
             rest_ref[0, :, cuts[t] - near : cuts[t + 1] - near] = picked
 
-    one(0)
-    for t in range(1, len(cuts) - 1):
-        pl.when(meta_ref[at_size + q] > cuts[t])(functools.partial(one, t))
-
-    @pl.when(step == n - 1)
-    def _():
-        for o in range(n):
-            copy(o, 0).wait()
-            for t in range(1, len(cuts) - 1):
-                pl.when(meta_ref[at_size + o] > cuts[t])(lambda o=o, t=t: copy(o, t).wait())
+    def whole(keyed_ref, at):
+        one(keyed_ref, at, 0)
+        for t in range(1, len(cuts) - 1):
+            pl.when(meta_ref[at_size + q] > cuts[t])(functools.partial(one, keyed_ref, at, t))
+
+    pl.when(step < n // 2)(lambda: whole(even_ref, step))
+    pl.when(step >= n // 2)(lambda: whole(odd_ref, step - n // 2))
 
 
 def weight_kernel(scale, count, *refs):
@@ -268,35 +237,25 @@
             w_ref[i] = w.astype(w_ref.dtype)
 
 
-def value_kernel(
-    rows, size_ref, near_ref, rest_ref, row_ref, low_ref, high_ref, value_ref, out_ref,
-    low, high, values, acc, mixed, sem, value_sem,
-):
+def value_kernel(n, rows, meta_ref, *refs):
+    x_refs, (near_ref, rest_ref, row_ref, value_ref, out_ref) = refs[:4], refs[4:9]
+    held, more, wide, tile, acc, mixed, sem = refs[9:]
     q = pl.program_id(0)
-    n = low.shape[0]
-    kvh = values.shape[0]
+    kvh = value_ref.shape[0]
     _, heads, near = near_ref.shape
     lanes = near + rest_ref.shape[2]
     per = rows * heads // kvh
     cuts = tile_cuts(lanes)
-    load_values = pltpu.make_async_copy(value_ref, values, value_sem)
-
-    def copy(o, t):
-        if t == 0:
-            return pltpu.make_async_copy(low_ref.at[o], low.at[o], sem.at[o, 0])
-        here = pl.ds(cuts[t] - cuts[1], cuts[t + 1] - cuts[t])
-        return pltpu.make_async_copy(high_ref.at[o, here], high.at[o, here], sem.at[o, t])
+    groups = lanes // BLK
+    at_size = n * groups
 
     @pl.when(q == 0)
     def _():
-        for o in range(n):
-            copy(o, 0).start()
-            for t in range(1, len(cuts) - 1):
-                pl.when(size_ref[o] > cuts[t])(lambda o=o, t=t: copy(o, t).start())
-        load_values.start()
+        load_tokens(
+            n, meta_ref[at_size + n + 1], meta_ref[at_size + n + 2], x_refs, held, more, wide, sem
+        )
 
     def one(t):
-        copy(q, t).wait()
         here = slice(cuts[t], cuts[t + 1])
         width = cuts[t + 1] - cuts[t]
         if cuts[t] < near:
@@ -308,8 +267,11 @@
         spread = jnp.concatenate(
             [jnp.where((owner_row == r)[None, None], weights, 0.0) for r in range(rows)], 1
         ).reshape(kvh * per, width)
-        tile = low[q] if t == 0 else high[q, cuts[t] - cuts[1] : cuts[t + 1] - cuts[1], :]
-        got = jnp.dot(spread.astype(jnp.bfloat16), tile, preferred_element_type=jnp.float32)
+        got = jnp.dot(
+            spread.astype(jnp.bfloat16),
+            list_tile(meta_ref, q * groups + cuts[t] // BLK, width // BLK, wide, tile),
+            preferred_element_type=jnp.float32,
+        )
         if t:
             acc[...] += got
         else:
@@ -317,7 +279,7 @@
 
     one(0)
     for t in range(1, len(cuts) - 1):
-        pl.when(size_ref[q] > cuts[t])(functools.partial(one, t))
+        pl.when(meta_ref[at_size + q] > cuts[t])(functools.partial(one, t))
     for h in range(kvh):
         mixed[h, pl.ds(pl.multiple_of(q * per, per), per), :] = acc[
             h * per : (h + 1) * per, :
@@ -325,9 +287,8 @@
 
     @pl.when(q == n - 1)
     def _():
-        load_values.wait()
         for h in range(kvh):
-            done = jnp.dot(mixed[h], values[h], preferred_element_type=jnp.float32)
+            done = jnp.dot(mixed[h], value_ref[h], preferred_element_type=jnp.float32)
             out_ref[:, h] = done.reshape(n, per, done.shape[1]).astype(out_ref.dtype)
 
 
@@ -353,31 +314,26 @@
 
 
 def project_kernel(n, core_ref, *refs):
-    row_refs, (weight_ref, own_ref, away_ref, gathered, weight, sem) = refs[:n], refs[n:]
-    rows, cols = row_refs[0].shape[0], own_ref.shape[1]
-    cuts = sem.shape[0]
-    span = weight.shape[0] // cuts
-    loads = [
-        pltpu.make_async_copy(
-            weight_ref.at[pl.ds(i * span, span)], weight.at[pl.ds(i * span, span)], sem.at[i]
-        )
-        for i in range(cuts)
-    ]
-    for load in loads:
-        load.start()
+    row_refs, (weight_ref, own_ref, away_ref, gathered) = refs[:n], refs[n:]
+    rows = row_refs[0].shape[0]
+    cols = own_ref.shape[1]
     for k in range(0, n, 2):
         pair = [row_refs[k + j][...].astype(jnp.float32) for j in range(2)]
         gathered[k * rows : (k + 2) * rows, :] = jnp.concatenate(pair).astype(gathered.dtype)
-    done = jnp.zeros((n * rows, 2 * cols), jnp.float32)
-    for i, load in enumerate(loads):
-        load.wait()
-        here = slice(i * span, (i + 1) * span)
-        done = done + jnp.dot(
-            gathered[:, here], weight[here, :], preferred_element_type=jnp.float32
-        )
-    first = core_ref[0] == 0
-    own_ref[...] = jnp.where(first, done[:, :cols], done[:, cols:])
-    away_ref[...] = jnp.where(first, done[:, cols:], done[:, :cols])
+    step = min(256, cols)
+    for i in range(0, 2 * cols, step):
+        done = jnp.dot(
+            gathered[...], weight_ref[:, i : i + step], preferred_element_type=jnp.float32
+        )
+        here = slice(i % cols, i % cols + step)
+
+        @pl.when(core_ref[0] == i // cols)
+        def _(done=done, here=here):
+            own_ref[:, here] = done
+
+        @pl.when(core_ref[0] != i // cols)
+        def _(done=done, here=here):
+            away_ref[:, here] = done
 
 
 def order_kernel(n, me_ref, own_ref, got_ref, out_ref):
@@ -451,8 +407,10 @@
     packed = pack(x_prompt, pack_fill, pack_dest, at, n, 0, size)
     dest = pack_dest
     far = with_partner(queries, n // 2, n)
-    packed, far, dest, block_row, block_fill, query = lax.optimization_barrier(
-        (packed, far, dest, block_row, block_fill, queries)
+    packed, far, dest, block_row, block_fill, query, cache_len, kv_weight = (
+        lax.optimization_barrier(
+            (packed, far, dest, block_row, block_fill, queries, cache_len, kv_weight)
+        )
     )
     mine = lax.all_to_all(packed, "pool", 0, 0, tiled=True).reshape(n * size, part)
 
@@ -534,13 +492,15 @@
     values = kv_weight[:, :, hd:].transpose(1, 0, 2)
 
     query = query.reshape(rows, kvh, group, hd)
+    cache_live = jnp.arange(cache_slots, dtype=jnp.int32)[None, :] < cache_len[:, None]
+    cached_keys, cached_values = (
+        jnp.where(cache_live[:, :, None, None], kv_cache[:, :, :, at : at + hd], 0)
+        for at in (0, hd)
+    )
     cache_scores = (
-        jnp.einsum(
-            "rhgd,rthd->rhgt", query, kv_cache[:, :, :, :hd], preferred_element_type=jnp.float32
-        )
+        jnp.einsum("rhgd,rthd->rhgt", query, cached_keys, preferred_element_type=jnp.float32)
         * scale
     )
-    cache_live = jnp.arange(cache_slots, dtype=jnp.int32)[None, :] < cache_len[:, None]
     cache_scores = jnp.where(cache_live[:, None, None, :], cache_scores, -jnp.inf)
     cache_top = jnp.max(cache_scores, -1, keepdims=True)
     cache_exp = jnp.exp(cache_scores - cache_top)
@@ -548,19 +508,16 @@
     cached = jnp.einsum(
         "rhgt,rthd->rhgd",
         cache_exp.astype(jnp.bfloat16),
-        kv_cache[:, :, :, hd:],
+        cached_values,
         preferred_element_type=jnp.float32,
     )
     cache_top = cache_top.reshape(rows, heads, 1)
     cache_sum = cache_sum.reshape(rows, heads, 1)
     cached = cached.reshape(rows, heads, hd)
 
-    mine, meta, list_rows, rowof, keyed_even, keyed_odd, values, cache_top, cache_sum, cached = (
+    mine, meta, rowof, keyed_even, keyed_odd, values, cache_top, cache_sum, cached = (
         lax.optimization_barrier(
-            (
-                mine, meta, list_rows, rowof, keyed_even, keyed_odd, values,
-                cache_top, cache_sum, cached,
-            )
+            (mine, meta, rowof, keyed_even, keyed_odd, values, cache_top, cache_sum, cached)
         )
     )
     other = lax.ppermute(mine, "tp", swap)
@@ -573,49 +530,40 @@
     slot_shapes = [
         jax.ShapeDtypeStruct((n, heads, length), jnp.bfloat16) for length in (near, lanes - near)
     ]
-    cuts = tile_cuts(lanes)
-    list_shapes = [(n, cuts[1], part), (n, lanes - cuts[1], part)]
-    list_scratch = [pltpu.VMEM(shape, jnp.bfloat16) for shape in list_shapes]
+    in_vmem = pl.BlockSpec(memory_space=pltpu.VMEM)
+    x_parts = (mine, other, more_mine, more_other)
+    x_scratch = [
+        pltpu.VMEM((ntp, n * size, part), jnp.bfloat16),
+        pltpu.VMEM((ntp, n * extra, part), jnp.bfloat16),
+        pltpu.VMEM((n * tokens, part), jnp.float32),
+        pltpu.VMEM((tile_cuts(lanes)[1], part), jnp.bfloat16),
+    ]
     at_me = n * lanes // BLK + n
 
     def owner(i, m):
         return m[at_me] ^ reversed_bits(i, n)
 
-    score_near, score_rest, low, high = pl.pallas_call(
+    score_near, score_rest = pl.pallas_call(
         functools.partial(score_kernel, n, rows),
         grid_spec=pltpu.PrefetchScalarGridSpec(
             num_scalar_prefetch=1,
             grid=(n,),
             in_specs=[
-                *[in_hbm] * 6,
+                *[in_hbm] * 4,
+                in_vmem,
+                in_vmem,
                 pl.BlockSpec((1, 1, lanes), lambda i, m: (owner(i, m), 0, 0)),
             ],
             out_specs=[
-                *[
-                    pl.BlockSpec((1, heads, length), lambda i, m: (owner(i, m), 0, 0))
-                    for length in (near, lanes - near)
-                ],
-                in_hbm,
-                in_hbm,
+                pl.BlockSpec((1, heads, length), lambda i, m: (owner(i, m), 0, 0))
+                for length in (near, lanes - near)
             ],
-            scratch_shapes=[
-                pltpu.VMEM((ntp, n * size, part), jnp.bfloat16),
-                pltpu.VMEM((ntp, n * extra, part), jnp.bfloat16),
-                pltpu.VMEM((n * tokens, part), jnp.float32),
-                pltpu.VMEM((kvh, n * per, part), jnp.bfloat16),
-                *list_scratch,
-                pltpu.SemaphoreType.DMA((ntp, 4)),
-                pltpu.SemaphoreType.DMA((2, kvh)),
-                pltpu.SemaphoreType.DMA((n, len(cuts) - 1)),
-            ],
+            scratch_shapes=[*x_scratch, pltpu.SemaphoreType.DMA((ntp, 4))],
         ),
-        out_shape=[
-            *slot_shapes,
-            *[jax.ShapeDtypeStruct(shape, jnp.bfloat16) for shape in list_shapes],
-        ],
-        compiler_params=pltpu.CompilerParams(vmem_limit_bytes=56 * MIB),
+        out_shape=slot_shapes,
+        compiler_params=pltpu.CompilerParams(vmem_limit_bytes=20 * MIB),
         name="prompt_scores",
-    )(meta, mine, other, more_mine, more_other, keyed_even, keyed_odd, rowof)
+    )(meta, *x_parts, keyed_even, keyed_odd, rowof)
 
     my_rows = lax.dynamic_index_in_dim(rowof, me, 0, keepdims=False)
 
@@ -639,25 +587,23 @@
         longer, lambda: exchange_weights(score_near, score_rest), near_only
     )
     terms = pl.pallas_call(
-        functools.partial(value_kernel, rows),
+        functools.partial(value_kernel, n, rows),
         grid_spec=pltpu.PrefetchScalarGridSpec(
             num_scalar_prefetch=1,
             grid=(n,),
-            in_specs=[*slot_specs, row_spec, in_hbm, in_hbm, in_hbm],
+            in_specs=[*[in_hbm] * 4, *slot_specs, row_spec, in_vmem],
             out_specs=pl.BlockSpec((n, kvh, per, hd), lambda q, m: (0, 0, 0, 0)),
             scratch_shapes=[
-                *list_scratch,
-                pltpu.VMEM((kvh, part, hd), jnp.bfloat16),
+                *x_scratch,
                 pltpu.VMEM((kvh * per, part), jnp.float32),
                 pltpu.VMEM((kvh, n * per, part), jnp.bfloat16),
-                pltpu.SemaphoreType.DMA((n, len(cuts) - 1)),
-                pltpu.SemaphoreType.DMA,
+                pltpu.SemaphoreType.DMA((ntp, 4)),
             ],
         ),
         out_shape=jax.ShapeDtypeStruct((n, kvh, per, hd), jnp.bfloat16),
-        compiler_params=pltpu.CompilerParams(vmem_limit_bytes=56 * MIB),
+        compiler_params=pltpu.CompilerParams(vmem_limit_bytes=26 * MIB),
         name="weighted_values",
-    )(list_rows, weight_near, weight_rest, rowof, low, high, values)
+    )(meta, *x_parts, weight_near, weight_rest, rowof, values)
 
     term_parts = lax.all_to_all(terms, "pool", 0, 0, tiled=True)
     attended = pl.pallas_call(
@@ -678,17 +624,13 @@
             grid=(1,),
             in_specs=[
                 *[pl.BlockSpec((rows, heads * hd), lambda i, m: (0, 0))] * n,
-                in_hbm,
+                pl.BlockSpec(out_weight.shape, lambda i, m: (0, 0)),
             ],
             out_specs=[half_spec] * 2,
-            scratch_shapes=[
-                pltpu.VMEM((n * rows, heads * hd), jnp.bfloat16),
-                pltpu.VMEM(out_weight.shape, jnp.bfloat16),
-                pltpu.SemaphoreType.DMA((8,)),
-            ],
+            scratch_shapes=[pltpu.VMEM((n * rows, heads * hd), jnp.bfloat16)],
         ),
         out_shape=[half_shape] * 2,
-        compiler_params=pltpu.CompilerParams(vmem_limit_bytes=56 * MIB),
+        compiler_params=pltpu.CompilerParams(vmem_limit_bytes=26 * MIB),
         name="output_projection",
     )(core.reshape(1), *swap_parts([attended] * n, n), out_weight)
     got = lax.ppermute(away, "tp", swap)

time: 153 us -> 161 us (1.052)
  waiting for transfers between devices: 27.3 us -> 37.1 us
  Pallas kernels: 32.4 us -> 28.5 us
  other arithmetic: 10.4 us -> 13.9 us
  starting transfers between devices: 29.6 us -> 27.4 us
    ppermute x10, waiting for transfers between devices: 17.2 us -> 27.4 us  [with_partner(): return lax.ppermute(x, 'pool', [(i, i ^ k) for i in range(n)])]
    select_n x0 -> x1, other arithmetic: none -> 7.32 us  [local(): jnp.where(cache_live[:, :, None, None], kv_cache[:, :, :, at:at + hd], 0)]
    slice x2 -> x0, local copies, waits for them, and re-layouts: 4.84 us -> none  [the longest x1 2.42 us: local(): kv_cache[:, :, :, hd:]]
    unnamed x51 -> x30, local copies, waits for them, and re-layouts: 4.26 us -> 8.56 us
    pallas_call x1, Pallas kernels: 11.3 us -> 7.95 us  [local(): pl.pallas_call(functools.partial(score_kernel, n, rows), grid_spec=pltpu....]
    ppermute x10, starting transfers between devices: 18.3 us -> 15.5 us  [with_partner(): return lax.ppermute(x, 'pool', [(i, i ^ k) for i in range(n)])]
    pallas_call x1, Pallas kernels: 5.54 us -> 2.88 us  [local(): pl.pallas_call(functools.partial(project_kernel, n), grid_spec=pltpu.Pref...]
    optimization_barrier x0 -> x1, local copies, waits for them, and re-layouts: none -> 1.86 us  [local(): lax.optimization_barrier((packed, far, dest, block_row, block_fill, queri...]
  transfers between devices with their start and end apart: 15 -> 15, of which waited for: 8 -> 9; matrix products, arithmetic and copies ran while one was open for 20% -> 15% of each run, Pallas kernels for 3% -> 3%
where the time goes in v10:
time: 161 us; the launch traced here: 160 us
  waiting for transfers between devices  37.1 us (23%)
  Pallas kernels  28.5 us (18%)
  blocking collectives  27.7 us (17%)
  starting transfers between devices  27.4 us (17%)
  local copies, waits for them, and re-layouts  16.3 us (10%)
  other arithmetic  13.9 us (9%)
  matrix products  7.14 us (4%)
    ppermute x10, waiting for transfers between devices, with_partner(): return lax.ppermute(x, 'pool', [(i, i ^ k) for i in range(n)])  27.4 us
    all_to_all x1, blocking collectives, local(): term_parts = lax.all_to_all(terms, 'pool', 0, 0, tiled=True)  17 us
    ppermute x10, starting transfers between devices, with_partner(): return lax.ppermute(x, 'pool', [(i, i ^ k) for i in range(n)])  15.5 us
    all_to_all x1, blocking collectives, exchange_weights(): lax.all_to_all(w, 'pool', 0, 0, tiled=True)  10.7 us
    pallas_call x1, Pallas kernels, local(): pl.pallas_call(functools.partial(value_kernel, n, rows), grid_spec=pltpu....  9.67 us
    unnamed x30, local copies, waits for them, and re-layouts  8.56 us
    pallas_call x1, Pallas kernels, local(): pl.pallas_call(functools.partial(score_kernel, n, rows), grid_spec=pltpu....  7.95 us
    all_to_all x1, waiting for transfers between devices, exchange_weights(): parts = [lax.all_to_all(s, 'pool', 0, 0, tiled=True) for s in scores]  7.34 us
  transfers between devices with their start and end apart: 15, of which 9 were waited for; matrix products, arithmetic and copies ran while one was open for 15% of the time, Pallas kernels for 3%

profile of v10, /device:TPU:0, one launch (start us, length us, event | category | flops | bytes accessed | tf_op | source)
XLA Modules:
  0.0 159.8 jit_solution(7298557987858986026)
XLA Ops:
  0.0 4.0 %collective-permute-start.1 = (bf16[8,32,128]{2,1,0:T(8,128)(2,1)}, bf16[8,32,128]{2,1,0:T(8,128)(2,1)S(1)}, u32[]{:S(2)}, u32[]{:S(2)}) collective-permute-start(bf16[8,32,128]{2,1,0:T(8,128)(2,1)} %param.18), channel_id=1, source_target_pairs={{0,8},{2,10},{4,12},{6,14},{8,0},{10,2},{12,4},{14,6},{1,9},{3,11}... | collective-permute-start | bytes 196616 | tf_op jit(solution)/shard_map/ppermute | solution.py:350
  4.2 4.5 %pack_live_tokens.3 = bf16[8,96,1024]{2,1,0:T(8,128)(2,1)} custom-call(s32[2]{0:T(128)S(1)} %pad_add_fusion.at_ref, s32[256]{0:T(256)} %fill_ref.1, s32[256]{0:T(256)} %bitcast.53, bf16[256,8192]{1,0:T(8,128)(2,1)} %x_ref.1), custom_call_target="tpu_custom_call" | custom-call | flops 402653184 | bytes 67108864 | tf_op jit(solution)/shard_map/pack_live_tokens/pallas_call | solution.py:70
  8.8 0.2 select_reduce_fusion.5
  9.2 0.1 fusion.38
  9.3 0.1 select_reduce_fusion.6
  9.5 0.7 reduce_max.28
  10.2 0.1 reduce_sum.110
  10.3 0.7 reduce_max.27
  11.0 1.4 pad_add_fusion.1
  12.3 1.5 collective-permute-start.2
  13.9 7.3 %slice_select_fusion = (bf16[8,256,4,128]{3,2,1,0:T(4,128)(2,1)}, bf16[8,256,4,128]{3,2,1,0:T(4,128)(2,1)S(1)}) fusion(bf16[8,256,4,256]{3,2,1,0:T(4,128)(2,1)} %param.19, pred[8,256]{1,0:T(8,128)(4,1)S(1)} %iota_compare_fusion.4), kind=kLoop, calls=%fused_computation.8 | loop fusion | flops 2097152 | bytes 8390656 | tf_op jit(solution)/shard_map/jit(_where)/select_n | solution.py:497
  21.2 0.7 fusion.41
  22.1 4.8 %all-to-all-start.7 = ((bf16[8,96,1024]{2,1,0:T(8,128)(2,1)}), bf16[8,96,1024]{2,1,0:T(8,128)(2,1)S(1)}, u32[]{:S(2)}, u32[]{:S(2)}) async-start(bf16[8,96,1024]{2,1,0:T(8,128)(2,1)} %pack_live_tokens.3), calls=%async_computation.7 | async-start | bytes 3145728 | tf_op jit(solution)/shard_map/all_to_all | solution.py:415
  26.9 0.2 fusion.18
  27.2 2.0 %collective-permute-start.3 = (bf16[2,8,32,128]{3,2,1,0:T(8,128)(2,1)S(1)}, bf16[2,8,32,128]{3,2,1,0:T(8,128)(2,1)S(1)}, u32[]{:S(2)}, u32[]{:S(2)}) collective-permute-start(bf16[2,8,32,128]{3,2,1,0:T(8,128)(2,1)S(1)} %pad_maximum_fusion.2), channel_id=1, source_target_pairs={{0,4},{2,6},{4,0},{6,2},{8,12},{10,14},{12,8},{14,10},{1,5},{3,7},... | collective-permute-start | bytes 393224 | tf_op jit(solution)/shard_map/ppermute | solution.py:350
  29.2 1.9 %copy.29 = bf16[1024,4,256]{2,0,1:T(8,128)(2,1)S(1)} copy(bf16[1024,4,256]{2,1,0:T(4,128)(2,1)} %param.14) | data formatting | bytes 4194304 | tf_op jit(solution)/shard_map/optimization_barrier | solution.py:411
  31.1 0.1 select_reduce_fusion.3
  31.2 0.1 fusion.20
  31.3 0.3 select_reduce_fusion.2
  31.6 1.0 select_reduce_fusion
  32.7 1.1 fusion.11
  33.8 1.2 slice_bitcast_fusion.refs_7_
  34.9 1.4 fusion.42
  36.3 0.6 fusion.40
  37.7 17.2 %collective-permute-done.3 = bf16[2,8,32,128]{3,2,1,0:T(8,128)(2,1)S(1)} collective-permute-done((bf16[2,8,32,128]{3,2,1,0:T(8,128)(2,1)S(1)}, bf16[2,8,32,128]{3,2,1,0:T(8,128)(2,1)S(1)}, u32[]{:S(2)}, u32[]{:S(2)}) %collective-permute-start.3) | collective-permute-done | bytes 131104 | tf_op jit(solution)/shard_map/ppermute | solution.py:350
  54.9 1.7 %collective-permute-start.4 = (bf16[4,8,32,128]{3,2,1,0:T(8,128)(2,1)S(1)}, bf16[4,8,32,128]{3,2,1,0:T(8,128)(2,1)S(1)}, u32[]{:S(2)}, u32[]{:S(2)}) collective-permute-start(bf16[4,8,32,128]{3,2,1,0:T(8,128)(2,1)S(1)} %pad_maximum_fusion.1), channel_id=1, source_target_pairs={{0,2},{2,0},{4,6},{6,4},{8,10},{10,8},{12,14},{14,12},{1,3},{3,1},... | collective-permute-start | bytes 786440 | tf_op jit(solution)/shard_map/ppermute | solution.py:350
  56.5 3.3 %convolution_convert_fusion.1 = bf16[4,4,8,8,1024]{4,3,2,1,0:T(8,128)(2,1)} fusion(bf16[1024,4,256]{2,0,1:T(8,128)(2,1)} %copy-done.7, bf16[2,8,4,8,128]{4,3,2,1,0:T(8,128)(2,1)S(1)} %bitcast.52, bf16[1,8,4,8,128]{4,3,2,1,0:T(8,128)(2,1)S(1)} %bitcast.51, bf16[1,8,4,8,128]{4,3,2,1,0:T(8,128)(2,1)S(1)} %bitcast.48), kind=kOutput, calls=%fused_computation.11 | convolution fusion | flops 269746176 | bytes 3407872 | tf_op jit(solution)/shard_map/qrhgd,phd->hqrgp/dot_general | solution.py:484
  59.8 3.0 %collective-permute-done.4 = bf16[4,8,32,128]{3,2,1,0:T(8,128)(2,1)S(1)} collective-permute-done((bf16[4,8,32,128]{3,2,1,0:T(8,128)(2,1)S(1)}, bf16[4,8,32,128]{3,2,1,0:T(8,128)(2,1)S(1)}, u32[]{:S(2)}, u32[]{:S(2)}) %collective-permute-start.4) | collective-permute-done | bytes 262176 | tf_op jit(solution)/shard_map/ppermute | solution.py:350
  62.8 2.0 %convolution_convert_fusion = bf16[4,4,8,8,1024]{4,3,2,1,0:T(8,128)(2,1)} fusion(bf16[1024,4,256]{2,0,1:T(8,128)(2,1)S(1)} %copy-done.8, bf16[4,8,32,128]{3,2,1,0:T(8,128)(2,1)S(1)} %collective-permute-done.4), kind=kOutput, calls=%fused_computation.10 | convolution fusion | flops 269484032 | bytes 3407872 | tf_op jit(solution)/shard_map/qrhgd,phd->hqrgp/dot_general | solution.py:484
  65.5 1.7 %conditional.2 = (bf16[256,1024]{1,0:T(8,128)(2,1)}, bf16[256,1024]{1,0:T(8,128)(2,1)}) conditional(s32[]{:T(128)} %bitcast.22, () %tuple.25, (s32[2]{0:T(128)S(1)}, s32[256]{0:T(256)S(1)}, s32[256]{0:T(256)S(1)}, bf16[256,8192]{1,0:T(8,128)(2,1)}) %tuple.48), branch_computations={%region_14.15_spmd, %region_15.16_spmd} | conditional | flops 134217728 | bytes 70254648 | solution.py:474
  65.5 0.9 broadcast.407
  66.4 0.9 broadcast.407.clone
  67.2 1.1 collective-permute-done.5.refs_1_
  68.3 1.6 copy-done
  69.9 1.6 copy-done.1
  71.5 8.0 %prompt_scores.1 = (bf16[8,32,384]{2,1,0:T(8,128)(2,1)}, bf16[8,32,256]{2,1,0:T(8,128)(2,1)}) custom-call(s32[651]{0:T(1024)S(1)} %concatenate.16.meta_ref, bf16[768,1024]{1,0:T(8,128)(2,1)S(1)} %bitcast.39, bf16[768,1024]{1,0:T(8,128)(2,1)S(1)} %collective-permute-done.5.refs_1_, bf16[256,1024]{1,0:T(8,128)(2,1)} %get-tuple-element.91.refs_2_, ...), custom_call_target="tpu_custom_call" | custom-call | tf_op jit(solution)/shard_map/prompt_scores/pallas_call | solution.py:546
  79.4 28.4 %conditional.3 = (bf16[8,32,384]{2,1,0:T(8,128)(2,1)S(1)}, bf16[8,32,256]{2,1,0:T(8,128)(2,1)S(1)}, f32[8,32,128]{2,1,0:T(8,128)}) conditional(s32[]{:T(128)} %bitcast.23, (bf16[8,32,384]{2,1,0:T(8,128)(2,1)}, s32[1,640]{1,0:T(1,128)S(1)}, f32[8,32,1]{1,0,2:T(8,128)S(1)}, f32[8,32,1]{1,0,2:T(8,128)S(1)}, f32[8,32,128]{2,1,0:T(8,128)}) %tuple.27, ...), branch_computations={%region_16.17_spmd, %region_17.18_spmd} | conditional | bytes 1524848 | solution.py:586
  79.4 5.6 %all-to-all-start.1 = ((bf16[8,32,384]{2,1,0:T(8,128)(2,1)}), bf16[8,32,384]{2,1,0:T(8,128)(2,1)S(1)}, u32[]{:S(2)}, u32[]{:S(2)}) async-start(bf16[8,32,384]{2,1,0:T(8,128)(2,1)} %get-tuple-element.39), calls=%async_computation.1 | async-start | bytes 393216 | tf_op jit(solution)/shard_map/cond/branch_0_fun/all_to_all | solution.py:572
  85.0 0.1 copy.34.refs_2_
  85.1 0.8 copy.35.refs_3_
  85.9 7.3 %all-to-all-done.1.refs_0_ = bf16[8,32,384]{2,1,0:T(8,128)(2,1)S(1)} async-done(((bf16[8,32,384]{2,1,0:T(8,128)(2,1)}), bf16[8,32,384]{2,1,0:T(8,128)(2,1)S(1)}, u32[]{:S(2)}, u32[]{:S(2)}) %all-to-all-start.1) | async-done | bytes 196640 | tf_op jit(solution)/shard_map/cond/branch_0_fun/all_to_all | solution.py:572
  93.3 0.9 copy-done.6
  94.2 2.7 %softmax_weights.2 = (bf16[8,32,384]{2,1,0:T(8,128)(2,1)S(1)}, f32[8,32,128]{2,1,0:T(8,128)}) custom-call(bf16[8,32,384]{2,1,0:T(8,128)(2,1)S(1)} %all-to-all-done.1.refs_0_, s32[1,384]{1,0:T(1,128)S(1)} %slice.18.refs_1_, f32[8,32,1]{2,1,0:T(8,128)S(1)} %copy.34.refs_2_, f32[8,32,1]{2,1,0:T(8,128)S(1)} %copy-done.6, f32[8,32,128]{2,1,0:T(8,128)} %get-tuple-element.43.refs_4_), custom_call_target="tpu_custom_call" | custom-call | tf_op jit(solution)/shard_map/cond/branch_0_fun/softmax_weights/pallas_call | solution.py:574
  96.9 10.7 %all_to_all.39 = bf16[8,32,384]{2,1,0:T(8,128)(2,1)S(1)} all-to-all(bf16[8,32,384]{2,1,0:T(8,128)(2,1)S(1)} %get-tuple-element.44), channel_id=1, replica_groups=mesh['groups'=2,'pool'=8,'tp'=2] {'pool'}, dimensions={0} | all-to-all | bytes 393216 | tf_op jit(solution)/shard_map/cond/branch_0_fun/all_to_all | solution.py:580
  107.8 0.7 copy-done.11
  108.6 1.2 copy-done.3
  109.8 9.7 %weighted_values.1 = bf16[8,4,64,128]{3,2,1,0:T(8,128)(2,1)S(1)} custom-call(s32[651]{0:T(1024)S(1)} %concatenate.16.meta_ref, bf16[768,1024]{1,0:T(8,128)(2,1)S(1)} %bitcast.40, bf16[768,1024]{1,0:T(8,128)(2,1)S(1)} %collective-permute-done.5.refs_1_, bf16[256,1024]{1,0:T(8,128)(2,1)} %get-tuple-element.91.refs_2_, ...), custom_call_target="tpu_custom_call" | custom-call | tf_op jit(solution)/shard_map/weighted_values/pallas_call | solution.py:589
  119.5 17.0 %all_to_all.43.parts_ref = bf16[8,4,64,128]{3,2,1,0:T(8,128)(2,1)S(1)} all-to-all(bf16[8,4,64,128]{3,2,1,0:T(8,128)(2,1)S(1)} %weighted_values.1), channel_id=1, replica_groups=mesh['groups'=2,'pool'=8,'tp'=2] {'pool'}, dimensions={0} | all-to-all | bytes 1048576 | tf_op jit(solution)/shard_map/all_to_all | solution.py:608
  136.4 0.1 attended_sum.1.refs_0_
  136.5 0.8 collective-permute-start.10
  137.3 2.4 %collective-permute-start.11 = (bf16[8,4096]{1,0:T(8,128)(2,1)S(1)}, bf16[8,4096]{1,0:T(8,128)(2,1)S(1)}, u32[]{:S(2)}, u32[]{:S(2)}) collective-permute-start(bf16[8,4096]{1,0:T(8,128)(2,1)S(1)} %attended_sum.1.refs_0_), channel_id=1, source_target_pairs={{0,12},{2,14},{4,8},{6,10},{8,4},{10,6},{12,0},{14,2},{1,13},{3,15... | collective-permute-start | bytes 196616 | tf_op jit(solution)/shard_map/ppermute | solution.py:350
  139.8 2.7 %collective-permute-start.12 = (bf16[8,4096]{1,0:T(8,128)(2,1)S(1)}, bf16[8,4096]{1,0:T(8,128)(2,1)S(1)}, u32[]{:S(2)}, u32[]{:S(2)}) collective-permute-start(bf16[8,4096]{1,0:T(8,128)(2,1)S(1)} %attended_sum.1.refs_0_), channel_id=1, source_target_pairs={{0,14},{2,12},{4,10},{6,8},{8,6},{10,4},{12,2},{14,0},{1,15},{3,13... | collective-permute-start | bytes 196616 | tf_op jit(solution)/shard_map/ppermute | solution.py:350
  142.4 0.2 collective-permute-start.6
  142.6 0.4 collective-permute-start.7
  143.0 2.6 %collective-permute-done.10.refs_5_ = bf16[8,4096]{1,0:T(8,128)(2,1)S(1)} collective-permute-done((bf16[8,4096]{1,0:T(8,128)(2,1)S(1)}, bf16[8,4096]{1,0:T(8,128)(2,1)S(1)}, u32[]{:S(2)}, u32[]{:S(2)}) %collective-permute-start.10) | collective-permute-done | bytes 65568 | tf_op jit(solution)/shard_map/ppermute | solution.py:350
  145.6 0.3 collective-permute-start.8
  145.9 1.0 collective-permute-start.9
  146.9 0.3 collective-permute-done.12.refs_7_
  147.2 0.7 collective-permute-done.6.refs_1_
  148.0 3.5 %collective-permute-done.8.refs_3_ = bf16[8,4096]{1,0:T(8,128)(2,1)S(1)} collective-permute-done((bf16[8,4096]{1,0:T(8,128)(2,1)S(1)}, bf16[8,4096]{1,0:T(8,128)(2,1)S(1)}, u32[]{:S(2)}, u32[]{:S(2)}) %collective-permute-start.8) | collective-permute-done | bytes 65568 | tf_op jit(solution)/shard_map/ppermute | solution.py:350
  151.5 3.4 %copy-done.2 = bf16[4096,1024]{1,0:T(8,128)(2,1)S(1)} copy-done((bf16[4096,1024]{1,0:T(8,128)(2,1)S(1)}, bf16[4096,1024]{1,0:T(8,128)(2,1)}, u32[]{:S(2)}) %copy-start.2) | copy-done | bytes 8388632
  154.9 2.9 %output_projection.1 = (f32[64,512]{1,0:T(8,128)S(1)}, f32[64,512]{1,0:T(8,128)S(1)}) custom-call(s32[1]{0:T(128)} %bitcast.2.core_ref, bf16[8,4096]{1,0:T(8,128)(2,1)S(1)} %attended_sum.1.refs_0_, bf16[8,4096]{1,0:T(8,128)(2,1)S(1)} %collective-permute-done.6.refs_1_, bf16[8,4096]{1,0:T(8,128)(2,1)S(1)} %collective-permute-done.7.refs_2_, ...), custom_call_target="tpu_custom_call" | custom-call | tf_op jit(solution)/shard_map/output_projection/pallas_call | solution.py:620
  157.8 1.3 collective-permute-done.13.got_ref
  159.2 0.6 order_rows.1
  (57 shorter events, 1.1 us)
Async XLA Ops:
  0.0 8.7 %collective-permute-start.1 = (bf16[8,32,128]{2,1,0:T(8,128)(2,1)}, bf16[8,32,128]{2,1,0:T(8,128)(2,1)S(1)}, u32[]{:S(2)}, u32[]{:S(2)}) collective-permute-start(bf16[8,32,128]{2,1,0:T(8,128)(2,1)} %param.18), channel_id=1, source_target_pairs={{0,8},{2,10},{4,12},{6,14},{8,0},{10,2},{12,4},{14,6},{1,9},{3,11}... | collective-permute-start | bytes 196616 | tf_op jit(solution)/shard_map/ppermute | solution.py:350
  4.1 4.6 %copy-start.15 = (s32[256]{0:T(256)S(1)}, s32[256]{0:T(256)}, u32[]{:S(2)}) copy-start(s32[256]{0:T(256)} %fill_ref.1) | copy-start | bytes 3076
  4.1 4.6 %copy-start.14 = (s32[256,1]{0,1:T(1,128)S(1)}, s32[256,1]{0,1:T(1,128)}, u32[]{:S(2)}) copy-start(s32[256,1]{0,1:T(1,128)} %param.15) | copy-start | bytes 3076
  4.1 5.3 %copy-start.16 = (s32[256]{0:T(256)S(1)}, s32[256]{0:T(256)}, u32[]{:S(2)}) copy-start(s32[256]{0:T(256)} %param.16) | copy-start | bytes 3076
  4.1 9.7 %copy-start.17 = (s32[8]{0:T(128)S(1)}, s32[8]{0:T(128)}, u32[]{:S(2)}) copy-start(s32[8]{0:T(128)} %param.20) | copy-start | bytes 100
  12.3 22.6 %collective-permute-start.2 = (s32[2]{0:T(128)S(1)}, s32[2]{0:T(128)S(1)}, u32[]{:S(2)}, u32[]{:S(2)}) collective-permute-start(s32[2]{0:T(128)S(1)} %pad_add_fusion.1), channel_id=1, source_target_pairs={{0,16},{16,0},{1,17},{17,1},{2,18},{18,2},{3,19},{19,3},{4,20},{20... | collective-permute-start | bytes 32 | tf_op jit(solution)/shard_map/ppermute | solution.py:461
  13.9 7.3 %copy-start.10 = (bf16[8,32,128]{2,1,0:T(8,128)(2,1)S(1)}, bf16[8,32,128]{2,1,0:T(8,128)(2,1)}, u32[]{:S(2)}) copy-start(bf16[8,32,128]{2,1,0:T(8,128)(2,1)} %param.18) | copy-start | bytes 196612
  22.1 42.8 %all-to-all-start.7 = ((bf16[8,96,1024]{2,1,0:T(8,128)(2,1)}), bf16[8,96,1024]{2,1,0:T(8,128)(2,1)S(1)}, u32[]{:S(2)}, u32[]{:S(2)}) async-start(bf16[8,96,1024]{2,1,0:T(8,128)(2,1)} %pack_live_tokens.3), calls=%async_computation.7 | async-start | bytes 3145728 | tf_op jit(solution)/shard_map/all_to_all | solution.py:415
  27.2 5.5 %copy-start.9 = (bf16[8,256,4,128]{3,2,1,0:T(4,128)(2,1)S(1)}, bf16[8,256,4,128]{3,2,1,0:T(4,128)(2,1)}, u32[]{:S(2)}) copy-start(bf16[8,256,4,128]{3,2,1,0:T(4,128)(2,1)} %get-tuple-element.137) | copy-start | bytes 6291460
  27.2 27.7 %collective-permute-start.3 = (bf16[2,8,32,128]{3,2,1,0:T(8,128)(2,1)S(1)}, bf16[2,8,32,128]{3,2,1,0:T(8,128)(2,1)S(1)}, u32[]{:S(2)}, u32[]{:S(2)}) collective-permute-start(bf16[2,8,32,128]{3,2,1,0:T(8,128)(2,1)S(1)} %pad_maximum_fusion.2), channel_id=1, source_target_pairs={{0,4},{2,6},{4,0},{6,2},{8,12},{10,14},{12,8},{14,10},{1,5},{3,7},... | collective-permute-start | bytes 393224 | tf_op jit(solution)/shard_map/ppermute | solution.py:350
  31.1 3.8 %copy-start.7 = (bf16[1024,4,256]{2,0,1:T(8,128)(2,1)}, bf16[1024,4,256]{2,0,1:T(8,128)(2,1)S(1)}, u32[]{:S(2)}) copy-start(bf16[1024,4,256]{2,0,1:T(8,128)(2,1)S(1)} %copy.29) | copy-start | bytes 6291460
  37.7 25.2 %copy-start.8 = (bf16[1024,4,256]{2,0,1:T(8,128)(2,1)S(1)}, bf16[1024,4,256]{2,0,1:T(8,128)(2,1)}, u32[]{:S(2)}) copy-start(bf16[1024,4,256]{2,0,1:T(8,128)(2,1)} %copy-done.7) | copy-start | bytes 6291460
  54.9 8.0 %collective-permute-start.4 = (bf16[4,8,32,128]{3,2,1,0:T(8,128)(2,1)S(1)}, bf16[4,8,32,128]{3,2,1,0:T(8,128)(2,1)S(1)}, u32[]{:S(2)}, u32[]{:S(2)}) collective-permute-start(bf16[4,8,32,128]{3,2,1,0:T(8,128)(2,1)S(1)} %pad_maximum_fusion.1), channel_id=1, source_target_pairs={{0,2},{2,0},{4,6},{6,4},{8,10},{10,8},{12,14},{14,12},{1,3},{3,1},... | collective-permute-start | bytes 786440 | tf_op jit(solution)/shard_map/ppermute | solution.py:350
  64.9 3.4 %collective-permute-start.5 = (bf16[768,1024]{1,0:T(8,128)(2,1)S(1)}, bf16[768,1024]{1,0:T(8,128)(2,1)S(1)}, u32[]{:S(2)}, u32[]{:S(2)}) collective-permute-start(bf16[768,1024]{1,0:T(8,128)(2,1)S(1)} %bitcast.38), channel_id=1, source_target_pairs={{0,1},{1,0},{2,3},{3,2},{4,5},{5,4},{6,7},{7,6},{8,9},{9,8},{10,11... | collective-permute-start | bytes 4718600 | tf_op jit(solution)/shard_map/ppermute | solution.py:523
  68.3 1.6 copy-start
  69.9 1.6 copy-start.1
  79.4 13.8 %all-to-all-start.1 = ((bf16[8,32,384]{2,1,0:T(8,128)(2,1)}), bf16[8,32,384]{2,1,0:T(8,128)(2,1)S(1)}, u32[]{:S(2)}, u32[]{:S(2)}) async-start(bf16[8,32,384]{2,1,0:T(8,128)(2,1)} %get-tuple-element.39), calls=%async_computation.1 | async-start | bytes 393216 | tf_op jit(solution)/shard_map/cond/branch_0_fun/all_to_all | solution.py:572
  93.3 0.9 copy-start.6
  107.8 0.7 copy-start.11
  107.8 0.7 copy-start.12
  108.6 1.2 copy-start.3
  109.8 26.6 %copy-start.13 = (f32[8,32,128]{2,1,0:T(8,128)S(1)}, f32[8,32,128]{2,1,0:T(8,128)}, u32[]{:S(2)}) copy-start(f32[8,32,128]{2,1,0:T(8,128)} %get-tuple-element.104.kept_ref) | copy-start | bytes 393220
  136.5 9.1 %collective-permute-start.10 = (bf16[8,4096]{1,0:T(8,128)(2,1)S(1)}, bf16[8,4096]{1,0:T(8,128)(2,1)S(1)}, u32[]{:S(2)}, u32[]{:S(2)}) collective-permute-start(bf16[8,4096]{1,0:T(8,128)(2,1)S(1)} %attended_sum.1.refs_0_), channel_id=1, source_target_pairs={{0,10},{2,8},{4,14},{6,12},{8,2},{10,0},{12,6},{14,4},{1,11},{3,9}... | collective-permute-start | bytes 196616 | tf_op jit(solution)/shard_map/ppermute | solution.py:350
  137.3 8.6 %collective-permute-start.11 = (bf16[8,4096]{1,0:T(8,128)(2,1)S(1)}, bf16[8,4096]{1,0:T(8,128)(2,1)S(1)}, u32[]{:S(2)}, u32[]{:S(2)}) collective-permute-start(bf16[8,4096]{1,0:T(8,128)(2,1)S(1)} %attended_sum.1.refs_0_), channel_id=1, source_target_pairs={{0,12},{2,14},{4,8},{6,10},{8,4},{10,6},{12,0},{14,2},{1,13},{3,15... | collective-permute-start | bytes 196616 | tf_op jit(solution)/shard_map/ppermute | solution.py:350
  139.8 7.5 %collective-permute-start.12 = (bf16[8,4096]{1,0:T(8,128)(2,1)S(1)}, bf16[8,4096]{1,0:T(8,128)(2,1)S(1)}, u32[]{:S(2)}, u32[]{:S(2)}) collective-permute-start(bf16[8,4096]{1,0:T(8,128)(2,1)S(1)} %attended_sum.1.refs_0_), channel_id=1, source_target_pairs={{0,14},{2,12},{4,10},{6,8},{8,6},{10,4},{12,2},{14,0},{1,15},{3,13... | collective-permute-start | bytes 196616 | tf_op jit(solution)/shard_map/ppermute | solution.py:350
  142.4 5.6 %collective-permute-start.6 = (bf16[8,4096]{1,0:T(8,128)(2,1)S(1)}, bf16[8,4096]{1,0:T(8,128)(2,1)S(1)}, u32[]{:S(2)}, u32[]{:S(2)}) collective-permute-start(bf16[8,4096]{1,0:T(8,128)(2,1)S(1)} %attended_sum.1.refs_0_), channel_id=1, source_target_pairs={{0,2},{2,0},{4,6},{6,4},{8,10},{10,8},{12,14},{14,12},{1,3},{3,1},... | collective-permute-start | bytes 196616 | tf_op jit(solution)/shard_map/ppermute | solution.py:350
  142.6 5.4 %collective-permute-start.7 = (bf16[8,4096]{1,0:T(8,128)(2,1)S(1)}, bf16[8,4096]{1,0:T(8,128)(2,1)S(1)}, u32[]{:S(2)}, u32[]{:S(2)}) collective-permute-start(bf16[8,4096]{1,0:T(8,128)(2,1)S(1)} %attended_sum.1.refs_0_), channel_id=1, source_target_pairs={{0,4},{2,6},{4,0},{6,2},{8,12},{10,14},{12,8},{14,10},{1,5},{3,7},... | collective-permute-start | bytes 196616 | tf_op jit(solution)/shard_map/ppermute | solution.py:350
  145.6 5.9 %collective-permute-start.8 = (bf16[8,4096]{1,0:T(8,128)(2,1)S(1)}, bf16[8,4096]{1,0:T(8,128)(2,1)S(1)}, u32[]{:S(2)}, u32[]{:S(2)}) collective-permute-start(bf16[8,4096]{1,0:T(8,128)(2,1)S(1)} %attended_sum.1.refs_0_), channel_id=1, source_target_pairs={{0,6},{2,4},{4,2},{6,0},{8,14},{10,12},{12,10},{14,8},{1,7},{3,5},... | collective-permute-start | bytes 196616 | tf_op jit(solution)/shard_map/ppermute | solution.py:350
  145.9 5.6 %collective-permute-start.9 = (bf16[8,4096]{1,0:T(8,128)(2,1)S(1)}, bf16[8,4096]{1,0:T(8,128)(2,1)S(1)}, u32[]{:S(2)}, u32[]{:S(2)}) collective-permute-start(bf16[8,4096]{1,0:T(8,128)(2,1)S(1)} %attended_sum.1.refs_0_), channel_id=1, source_target_pairs={{0,8},{2,10},{4,12},{6,14},{8,0},{10,2},{12,4},{14,6},{1,9},{3,11}... | collective-permute-start | bytes 196616 | tf_op jit(solution)/shard_map/ppermute | solution.py:350
  151.5 3.4 %copy-start.2 = (bf16[4096,1024]{1,0:T(8,128)(2,1)S(1)}, bf16[4096,1024]{1,0:T(8,128)(2,1)}, u32[]{:S(2)}) copy-start(bf16[4096,1024]{1,0:T(8,128)(2,1)} %refs_8_.1) | copy-start | bytes 25165828
  157.8 1.4 collective-permute-start.13

commit v11 on v10

--- a/solution.py
+++ b/solution.py
@@ -99,7 +99,7 @@
     return min(lanes, -(-lanes * 3 // 5 // 128) * 128)
 
 
-def load_tokens(n, core, over, x_refs, held, more, wide, sem):
+def load_tokens(n, core, over, x_refs, held, more, wide, sem, others=()):
     size, extra = held.shape[1] // n, more.shape[1] // n
     tokens = 2 * (size + extra)
     cuts = sem.shape[1]
@@ -132,6 +132,8 @@
     for pair in main:
         for copy in pair:
             copy.start()
+    for copy in others:
+        copy.start()
     for i, pair in enumerate(main):
         for copy in pair:
             copy.wait()
@@ -159,8 +161,8 @@
 
 
 def score_kernel(n, rows, meta_ref, *refs):
-    x_refs, (even_ref, odd_ref, row_ref), (near_ref, rest_ref) = refs[:4], refs[4:7], refs[7:9]
-    held, more, wide, tile, sem = refs[9:]
+    x_refs, keyed_refs, (row_ref, near_ref, rest_ref) = refs[:4], refs[4:6], refs[6:9]
+    held, more, wide, tile, keyed, sem, keyed_sem = refs[9:]
     step = pl.program_id(0)
     part = wide.shape[1]
     near = near_ref.shape[2]
@@ -169,20 +171,31 @@
     groups = lanes // BLK
     at_size = n * groups
     q = meta_ref[at_size + n] ^ reversed_bits(step, n)
-    kvh, per = even_ref.shape[0], even_ref.shape[1] * 2 // n
+    kvh, per = keyed.shape[0], keyed.shape[1] // n
     group = per // rows
 
     @pl.when(step == 0)
     def _():
+        span = n // 2 * per
+        loads = [
+            pltpu.make_async_copy(
+                ref.at[h], keyed.at[h, pl.ds(i * span, span)], keyed_sem.at[i, h]
+            )
+            for i, ref in enumerate(keyed_refs)
+            for h in range(kvh)
+        ]
         load_tokens(
-            n, meta_ref[at_size + n + 1], meta_ref[at_size + n + 2], x_refs, held, more, wide, sem
-        )
-
-    def one(keyed_ref, at, t):
+            n, meta_ref[at_size + n + 1], meta_ref[at_size + n + 2], x_refs, held, more, wide, sem,
+            loads,
+        )
+        for load in loads:
+            load.wait()
+
+    def one(t):
         here = slice(cuts[t], cuts[t + 1])
         count = (cuts[t + 1] - cuts[t]) // BLK
         raw = lax.dot_general(
-            keyed_ref[:, pl.ds(pl.multiple_of(at * per, per), per), :].reshape(kvh * per, part),
+            keyed[:, pl.ds(pl.multiple_of(step * per, per), per), :].reshape(kvh * per, part),
             list_tile(meta_ref, q * groups + cuts[t] // BLK, count, wide, tile),
             (((1,), (1,)), ((), ())),
             preferred_element_type=jnp.float32,
@@ -197,13 +210,9 @@
         else:
             rest_ref[0, :, cuts[t] - near : cuts[t + 1] - near] = picked
 
-    def whole(keyed_ref, at):
-        one(keyed_ref, at, 0)
-        for t in range(1, len(cuts) - 1):
-            pl.when(meta_ref[at_size + q] > cuts[t])(functools.partial(one, keyed_ref, at, t))
-
-    pl.when(step < n // 2)(lambda: whole(even_ref, step))
-    pl.when(step >= n // 2)(lambda: whole(odd_ref, step - n // 2))
+    one(0)
+    for t in range(1, len(cuts) - 1):
+        pl.when(meta_ref[at_size + q] > cuts[t])(functools.partial(one, t))
 
 
 def weight_kernel(scale, count, *refs):
@@ -239,9 +248,10 @@
 
 def value_kernel(n, rows, meta_ref, *refs):
     x_refs, (near_ref, rest_ref, row_ref, value_ref, out_ref) = refs[:4], refs[4:9]
-    held, more, wide, tile, acc, mixed, sem = refs[9:]
+    held, more, wide, tile, values, acc, mixed, sem, value_sem = refs[9:]
     q = pl.program_id(0)
-    kvh = value_ref.shape[0]
+    kvh = values.shape[0]
+    load_values = pltpu.make_async_copy(value_ref, values, value_sem)
     _, heads, near = near_ref.shape
     lanes = near + rest_ref.shape[2]
     per = rows * heads // kvh
@@ -252,7 +262,8 @@
     @pl.when(q == 0)
     def _():
         load_tokens(
-            n, meta_ref[at_size + n + 1], meta_ref[at_size + n + 2], x_refs, held, more, wide, sem
+            n, meta_ref[at_size + n + 1], meta_ref[at_size + n + 2], x_refs, held, more, wide, sem,
+            [load_values],
         )
 
     def one(t):
@@ -287,61 +298,57 @@
 
     @pl.when(q == n - 1)
     def _():
+        load_values.wait()
         for h in range(kvh):
-            done = jnp.dot(mixed[h], value_ref[h], preferred_element_type=jnp.float32)
-            out_ref[:, h] = done.reshape(n, per, done.shape[1]).astype(out_ref.dtype)
-
-
-def sum_kernel(parts_ref, kept_ref, out_ref, total):
-    n, kvh, per, hd = parts_ref.shape
+            done = jnp.dot(mixed[h], values[h], preferred_element_type=jnp.float32)
+            done = done.reshape(2, n // 2, per, done.shape[1]).astype(out_ref.dtype)
+            for side in range(2):
+                out_ref[:, side, h] = done[side]
+
+
+def half_sum_kernel(side_ref, parts_ref, kept_ref, send_ref, mine_ref):
+    half, sides, kvh, per, hd = parts_ref.shape
     rows, heads = kept_ref.shape[:2]
     group = heads // kvh
+    for side in range(sides):
+        own = side_ref[0] == side
+        for h in range(kvh):
+            terms = parts_ref[0, side, h].astype(jnp.float32)
+            for i in range(1, half):
+                terms = terms + parts_ref[i, side, h].astype(jnp.float32)
+            kept = jnp.concatenate(
+                [kept_ref[r, h * group : (h + 1) * group, :] for r in range(rows)]
+            )
+            terms = terms + jnp.where(own, kept, 0.0)
+            mine_ref[side, h] = terms
+            send_ref[side, h] = terms.astype(send_ref.dtype)
+
+
+def whole_sum_kernel(mine_ref, got_ref, out_ref, total):
+    sides, kvh, per, _ = mine_ref.shape
+    rows = out_ref.shape[0] // sides
+    group = per // rows
+    total[...] = mine_ref[...] + got_ref[...].astype(jnp.float32)
     for h in range(kvh):
-        terms = parts_ref[0, h].astype(jnp.float32)
-        for i in range(1, n):
-            terms = terms + parts_ref[i, h].astype(jnp.float32)
-        for r in range(rows):
-            here = slice((h * rows + r) * group, (h * rows + r + 1) * group)
-            total[here, :] = (
-                terms[r * group : (r + 1) * group] + kept_ref[r, h * group : (h + 1) * group, :]
+        for g in range(group):
+            column = [
+                total[side, h, pl.ds(g, rows, stride=group), :] for side in range(sides)
+            ]
+            head = h * group + g
+            hd = column[0].shape[1]
+            out_ref[:, head * hd : (head + 1) * hd] = jnp.concatenate(column).astype(
+                out_ref.dtype
             )
-    pieces = [
-        total[pl.ds(h * per + g, rows, stride=group), :]
-        for h in range(kvh)
-        for g in range(group)
-    ]
-    out_ref[...] = jnp.concatenate(pieces, 1).astype(out_ref.dtype)
-
-
-def project_kernel(n, core_ref, *refs):
-    row_refs, (weight_ref, own_ref, away_ref, gathered) = refs[:n], refs[n:]
-    rows = row_refs[0].shape[0]
-    cols = own_ref.shape[1]
-    for k in range(0, n, 2):
-        pair = [row_refs[k + j][...].astype(jnp.float32) for j in range(2)]
-        gathered[k * rows : (k + 2) * rows, :] = jnp.concatenate(pair).astype(gathered.dtype)
-    step = min(256, cols)
-    for i in range(0, 2 * cols, step):
-        done = jnp.dot(
-            gathered[...], weight_ref[:, i : i + step], preferred_element_type=jnp.float32
-        )
-        here = slice(i % cols, i % cols + step)
-
-        @pl.when(core_ref[0] == i // cols)
-        def _(done=done, here=here):
-            own_ref[:, here] = done
-
-        @pl.when(core_ref[0] != i // cols)
-        def _(done=done, here=here):
-            away_ref[:, here] = done
 
 
 def order_kernel(n, me_ref, own_ref, got_ref, out_ref):
+    half = n // 2
     rows = own_ref.shape[0] // n
     for q in range(0, n, 2):
         pair = []
-        for j in range(2):
-            here = pl.ds(pl.multiple_of((me_ref[0] ^ (q + j)) * rows, rows), rows)
+        for owner in (q, q + 1):
+            block = ((me_ref[0] % half) ^ (owner % half)) * 2 + owner // half
+            here = pl.ds(pl.multiple_of(block * rows, rows), rows)
             pair.append(own_ref[here, :] + got_ref[here, :])
         out_ref[q * rows : (q + 2) * rows, :] = jnp.concatenate(pair).astype(out_ref.dtype)
 
@@ -364,17 +371,6 @@
         out = out + (k // bit) % 2 * (n // 2 // bit)
         bit *= 2
     return out
-
-
-def far_first(n):
-    return sorted(range(1, n), reverse=True)
-
-
-def swap_parts(parts, n):
-    got = [parts[0]] + [None] * (n - 1)
-    for k in far_first(n):
-        got[k] = with_partner(parts[k], k, n)
-    return got
 
 
 def local(
@@ -406,10 +402,13 @@
     pack_fill, pack_dest = block_fill, block_dest[:, 0]
     packed = pack(x_prompt, pack_fill, pack_dest, at, n, 0, size)
     dest = pack_dest
-    far = with_partner(queries, n // 2, n)
-    packed, far, dest, block_row, block_fill, query, cache_len, kv_weight = (
+    even = from_rest(jnp.stack([queries, with_partner(queries, n // 2, n)]), n)
+    packed, even, dest, block_row, block_fill, query, kv_weight, ready = (
         lax.optimization_barrier(
-            (packed, far, dest, block_row, block_fill, queries, cache_len, kv_weight)
+            (
+                packed, even, dest, block_row, block_fill, queries, kv_weight,
+                jnp.ones((), jnp.bool_),
+            )
         )
     )
     mine = lax.all_to_all(packed, "pool", 0, 0, tiled=True).reshape(n * size, part)
@@ -486,7 +485,6 @@
             .reshape(kvh, n // 2 * per, part)
         )
 
-    even = from_rest(jnp.stack([queries, far]), n)
     keyed_even = through_keys(even)
     keyed_odd = through_keys(with_partner(even, 1, n))
     values = kv_weight[:, :, hd:].transpose(1, 0, 2)
@@ -494,7 +492,7 @@
     query = query.reshape(rows, kvh, group, hd)
     cache_live = jnp.arange(cache_slots, dtype=jnp.int32)[None, :] < cache_len[:, None]
     cached_keys, cached_values = (
-        jnp.where(cache_live[:, :, None, None], kv_cache[:, :, :, at : at + hd], 0)
+        jnp.where(ready, kv_cache[:, :, :, at : at + hd], 0)
         for at in (0, hd)
     )
     cache_scores = (
@@ -549,19 +547,22 @@
             num_scalar_prefetch=1,
             grid=(n,),
             in_specs=[
-                *[in_hbm] * 4,
-                in_vmem,
-                in_vmem,
+                *[in_hbm] * 6,
                 pl.BlockSpec((1, 1, lanes), lambda i, m: (owner(i, m), 0, 0)),
             ],
             out_specs=[
                 pl.BlockSpec((1, heads, length), lambda i, m: (owner(i, m), 0, 0))
                 for length in (near, lanes - near)
             ],
-            scratch_shapes=[*x_scratch, pltpu.SemaphoreType.DMA((ntp, 4))],
+            scratch_shapes=[
+                *x_scratch,
+                pltpu.VMEM((kvh, n * per, part), jnp.bfloat16),
+                pltpu.SemaphoreType.DMA((ntp, 4)),
+                pltpu.SemaphoreType.DMA((2, kvh)),
+            ],
         ),
         out_shape=slot_shapes,
-        compiler_params=pltpu.CompilerParams(vmem_limit_bytes=20 * MIB),
+        compiler_params=pltpu.CompilerParams(vmem_limit_bytes=56 * MIB),
         name="prompt_scores",
     )(meta, *x_parts, keyed_even, keyed_odd, rowof)
 
@@ -591,48 +592,53 @@
         grid_spec=pltpu.PrefetchScalarGridSpec(
             num_scalar_prefetch=1,
             grid=(n,),
-            in_specs=[*[in_hbm] * 4, *slot_specs, row_spec, in_vmem],
-            out_specs=pl.BlockSpec((n, kvh, per, hd), lambda q, m: (0, 0, 0, 0)),
+            in_specs=[*[in_hbm] * 4, *slot_specs, row_spec, in_hbm],
+            out_specs=pl.BlockSpec((n // 2, 2, kvh, per, hd), lambda q, m: (0, 0, 0, 0, 0)),
             scratch_shapes=[
                 *x_scratch,
+                pltpu.VMEM((kvh, part, hd), jnp.bfloat16),
                 pltpu.VMEM((kvh * per, part), jnp.float32),
                 pltpu.VMEM((kvh, n * per, part), jnp.bfloat16),
                 pltpu.SemaphoreType.DMA((ntp, 4)),
+                pltpu.SemaphoreType.DMA,
             ],
         ),
-        out_shape=jax.ShapeDtypeStruct((n, kvh, per, hd), jnp.bfloat16),
-        compiler_params=pltpu.CompilerParams(vmem_limit_bytes=26 * MIB),
+        out_shape=jax.ShapeDtypeStruct((n // 2, 2, kvh, per, hd), jnp.bfloat16),
+        compiler_params=pltpu.CompilerParams(vmem_limit_bytes=56 * MIB),
         name="weighted_values",
     )(meta, *x_parts, weight_near, weight_rest, rowof, values)
 
-    term_parts = lax.all_to_all(terms, "pool", 0, 0, tiled=True)
+    halves = [list(range(n // 2)), list(range(n // 2, n))]
+    term_parts = lax.all_to_all(
+        terms, "pool", 0, 0, axis_index_groups=halves, tiled=True
+    )
+    pair_shape = (2, kvh, per, hd)
+    send, held = pl.pallas_call(
+        half_sum_kernel,
+        in_specs=[pl.BlockSpec(memory_space=pltpu.SMEM), in_vmem, in_vmem],
+        out_shape=[
+            jax.ShapeDtypeStruct(pair_shape, jnp.bfloat16),
+            jax.ShapeDtypeStruct(pair_shape, jnp.float32),
+        ],
+        compiler_params=pltpu.CompilerParams(vmem_limit_bytes=8 * MIB),
+        name="half_pool_sum",
+    )((me // (n // 2)).reshape(1), term_parts, kept)
     attended = pl.pallas_call(
-        sum_kernel,
-        out_shape=jax.ShapeDtypeStruct((rows, heads * hd), jnp.bfloat16),
-        scratch_shapes=[pltpu.VMEM((kvh * per, hd), jnp.float32)],
+        whole_sum_kernel,
+        out_shape=jax.ShapeDtypeStruct((2 * rows, heads * hd), jnp.bfloat16),
+        scratch_shapes=[pltpu.VMEM(pair_shape, jnp.float32)],
         compiler_params=pltpu.CompilerParams(vmem_limit_bytes=8 * MIB),
         name="attended_sum",
-    )(term_parts, kept)
-
+    )(held, with_partner(send, n // 2, n))
+
+    everyone = [attended] + [with_partner(attended, k, n) for k in range(1, n // 2)]
+    product = jnp.dot(
+        jnp.concatenate(everyone), out_weight, preferred_element_type=jnp.float32
+    )
     cols = out_weight.shape[1] // ntp
-    half_shape = jax.ShapeDtypeStruct((n * rows, cols), jnp.float32)
     half_spec = pl.BlockSpec((n * rows, cols), lambda i, m: (0, 0))
-    own, away = pl.pallas_call(
-        functools.partial(project_kernel, n),
-        grid_spec=pltpu.PrefetchScalarGridSpec(
-            num_scalar_prefetch=1,
-            grid=(1,),
-            in_specs=[
-                *[pl.BlockSpec((rows, heads * hd), lambda i, m: (0, 0))] * n,
-                pl.BlockSpec(out_weight.shape, lambda i, m: (0, 0)),
-            ],
-            out_specs=[half_spec] * 2,
-            scratch_shapes=[pltpu.VMEM((n * rows, heads * hd), jnp.bfloat16)],
-        ),
-        out_shape=[half_shape] * 2,
-        compiler_params=pltpu.CompilerParams(vmem_limit_bytes=26 * MIB),
-        name="output_projection",
-    )(core.reshape(1), *swap_parts([attended] * n, n), out_weight)
+    own = lax.dynamic_slice_in_dim(product, core * cols, cols, 1)
+    away = lax.dynamic_slice_in_dim(product, (1 - core) * cols, cols, 1)
     got = lax.ppermute(away, "tp", swap)
     return pl.pallas_call(
         functools.partial(order_kernel, n),

time: 161 us -> 143 us (0.89)
  blocking collectives: 27.7 us -> 10.7 us
  waiting for transfers between devices: 37.1 us -> 46.8 us
  other arithmetic: 13.9 us -> 6.52 us
  matrix products: 7.14 us -> 13 us
  starting transfers between devices: 27.4 us -> 24.1 us
  local copies, waits for them, and re-layouts: 16.3 us -> 13.1 us
  Pallas kernels: 28.5 us -> 25.7 us
    all_to_all x1, waiting for transfers between devices: 0.01 us -> 19.7 us  [local(): lax.all_to_all(packed, 'pool', 0, 0, tiled=True).reshape(n * size, part)]
    all_to_all x1 -> x0, blocking collectives: 17 us -> none  [local(): term_parts = lax.all_to_all(terms, 'pool', 0, 0, tiled=True)]
    ppermute x10 -> x7, waiting for transfers between devices: 27.4 us -> 10.5 us  [with_partner(): return lax.ppermute(x, 'pool', [(i, i ^ k) for i in range(n)])]
    select_n x1 -> x0, other arithmetic: 7.32 us -> none  [local(): jnp.where(cache_live[:, :, None, None], kv_cache[:, :, :, at:at + hd], 0)]
    unnamed x30 -> x22, local copies, waits for them, and re-layouts: 8.56 us -> 1.69 us
    all_to_all x0 -> x1, waiting for transfers between devices: none -> 6.68 us  [local(): lax.all_to_all(terms, 'pool', 0, 0, axis_index_groups=halves, tiled=True)]
    dot_general x0 -> x1, matrix products: none -> 4.94 us  [local(): jnp.dot(jnp.concatenate(everyone), out_weight, preferred_element_type=jnp...]
    slice x0 -> x1, local copies, waits for them, and re-layouts: none -> 4.46 us  [local(): kv_cache[:, :, :, at:at + hd]]
  transfers between devices with their start and end apart: 15 -> 13, of which waited for: 9 -> 9; matrix products, arithmetic and copies ran while one was open for 15% -> 16% of each run, Pallas kernels for 3% -> 3%
where the time goes in v11:
time: 143 us; the launch traced here: 142 us
  waiting for transfers between devices  46.8 us (33%)
  Pallas kernels  25.7 us (18%)
  starting transfers between devices  24.1 us (17%)
  local copies, waits for them, and re-layouts  13.1 us (9%)
  matrix products  13 us (9%)
  blocking collectives  10.7 us (7%)
  other arithmetic  6.52 us (5%)
  between operations  1.52 us (1%)
    all_to_all x1, waiting for transfers between devices, local(): lax.all_to_all(packed, 'pool', 0, 0, tiled=True).reshape(n * size, part)  19.7 us
    ppermute x7, starting transfers between devices, with_partner(): return lax.ppermute(x, 'pool', [(i, i ^ k) for i in range(n)])  12 us
    all_to_all x1, blocking collectives, exchange_weights(): lax.all_to_all(w, 'pool', 0, 0, tiled=True)  10.7 us
    ppermute x7, waiting for transfers between devices, with_partner(): return lax.ppermute(x, 'pool', [(i, i ^ k) for i in range(n)])  10.5 us
    pallas_call x1, Pallas kernels, local(): pl.pallas_call(functools.partial(value_kernel, n, rows), grid_spec=pltpu....  9.78 us
    pallas_call x1, Pallas kernels, local(): pl.pallas_call(functools.partial(score_kernel, n, rows), grid_spec=pltpu....  9.72 us
    all_to_all x1, waiting for transfers between devices, exchange_weights(): parts = [lax.all_to_all(s, 'pool', 0, 0, tiled=True) for s in scores]  8.1 us
    all_to_all x1, waiting for transfers between devices, local(): lax.all_to_all(terms, 'pool', 0, 0, axis_index_groups=halves, tiled=True)  6.68 us
  transfers between devices with their start and end apart: 13, of which 9 were waited for; matrix products, arithmetic and copies ran while one was open for 16% of the time, Pallas kernels for 3%

profile of v11, /device:TPU:0, one launch (start us, length us, event | category | flops | bytes accessed | tf_op | source)
XLA Modules:
  0.0 141.7 jit_solution(4688202944355331140)
XLA Ops:
  0.0 4.0 %collective-permute-start.1 = (bf16[8,32,128]{2,1,0:T(8,128)(2,1)}, bf16[8,32,128]{2,1,0:T(8,128)(2,1)S(1)}, u32[]{:S(2)}, u32[]{:S(2)}) collective-permute-start(bf16[8,32,128]{2,1,0:T(8,128)(2,1)} %param.18), channel_id=1, source_target_pairs={{0,8},{2,10},{4,12},{6,14},{8,0},{10,2},{12,4},{14,6},{1,9},{3,11}... | collective-permute-start | bytes 196616 | tf_op jit(solution)/shard_map/ppermute | solution.py:357
  4.1 4.5 %fusion.47 = (bf16[8,256,4,128]{3,2,1,0:T(4,128)(2,1)}, bf16[8,256,4,128]{3,2,1,0:T(4,128)(2,1)}) fusion(bf16[8,256,4,256]{3,2,1,0:T(4,128)(2,1)} %param.19), kind=kLoop, calls=%fused_computation.114 | loop fusion | bytes 8388608 | tf_op jit(solution)/shard_map/slice | solution.py:495
  8.8 1.6 %collective-permute-start.2 = (bf16[2,8,32,128]{3,2,1,0:T(8,128)(2,1)S(1)}, bf16[2,8,32,128]{3,2,1,0:T(8,128)(2,1)S(1)}, u32[]{:S(2)}, u32[]{:S(2)}) collective-permute-start(bf16[2,8,32,128]{3,2,1,0:T(8,128)(2,1)S(1)} %pad_maximum_fusion.1), channel_id=1, source_target_pairs={{0,4},{2,6},{4,0},{6,2},{8,12},{10,14},{12,8},{14,10},{1,5},{3,7},... | collective-permute-start | bytes 393224 | tf_op jit(solution)/shard_map/ppermute | solution.py:357
  10.4 4.2 %pack_live_tokens.3 = bf16[8,96,1024]{2,1,0:T(8,128)(2,1)} custom-call(s32[2]{0:T(128)S(1)} %pad_add_fusion.at_ref, s32[256]{0:T(256)S(1)} %copy-done.8, s32[256]{0:T(256)S(1)} %bitcast.53, bf16[256,8192]{1,0:T(8,128)(2,1)S(1)} %copy-done), custom_call_target="tpu_custom_call" | custom-call | flops 402653184 | bytes 67108864 | tf_op jit(solution)/shard_map/pack_live_tokens/pallas_call | solution.py:70
  14.7 0.1 reshape.285
  14.8 0.2 select_reduce_fusion.5
  15.0 0.1 reduce_sum.104
  15.1 0.1 reduce_sum.106
  15.1 0.1 fusion.45
  15.3 0.1 select_reduce_fusion.6
  15.4 0.1 reshape.284
  15.5 0.7 reduce_max.28
  16.2 0.1 reduce_sum.110
  16.3 0.6 reduce_max.27
  16.9 1.3 pad_add_fusion.1
  18.2 1.5 %collective-permute-start.3 = (s32[2]{0:T(128)S(1)}, s32[2]{0:T(128)S(1)}, u32[]{:S(2)}, u32[]{:S(2)}) collective-permute-start(s32[2]{0:T(128)S(1)} %pad_add_fusion.1), channel_id=1, source_target_pairs={{0,16},{16,0},{1,17},{17,1},{2,18},{18,2},{3,19},{19,3},{4,20},{20... | collective-permute-start | bytes 32 | tf_op jit(solution)/shard_map/ppermute | solution.py:460
  19.7 1.5 %collective-permute-start.4 = (bf16[4,8,32,128]{3,2,1,0:T(8,128)(2,1)S(1)}, bf16[4,8,32,128]{3,2,1,0:T(8,128)(2,1)S(1)}, u32[]{:S(2)}, u32[]{:S(2)}) collective-permute-start(bf16[4,8,32,128]{3,2,1,0:T(8,128)(2,1)S(1)} %pad_maximum_fusion), channel_id=1, source_target_pairs={{0,2},{2,0},{4,6},{6,4},{8,10},{10,8},{12,14},{14,12},{1,3},{3,1},... | collective-permute-start | bytes 786440 | tf_op jit(solution)/shard_map/ppermute | solution.py:357
  21.3 3.6 %all-to-all-start.7 = ((bf16[8,96,1024]{2,1,0:T(8,128)(2,1)}), bf16[8,96,1024]{2,1,0:T(8,128)(2,1)S(1)}, u32[]{:S(2)}, u32[]{:S(2)}) async-start(bf16[8,96,1024]{2,1,0:T(8,128)(2,1)} %pack_live_tokens.3), calls=%async_computation.7 | async-start | bytes 3145728 | tf_op jit(solution)/shard_map/all_to_all | solution.py:414
  24.8 2.3 %fusion.49 = (f32[8,4,8]{2,1,0:T(4,128)S(1)}, f32[8,4,8,256]{3,2,1,0:T(8,128)S(1)}) fusion(bf16[8,256,4,128]{3,2,1,0:T(4,128)(2,1)} %get-tuple-element.138, pred[]{:T(512)} %constant.140.clone.1, bf16[8,32,128]{2,1,0:T(8,128)(2,1)S(1)} %copy-done.5, pred[8,256]{1,0:T(8,128)(4,1)S(1)} %iota_compare_fusion.4), kind=kOutput, calls=%fused_computation.116 | convolution fusion | flops 18022144 | bytes 2427905 | tf_op jit(solution)/shard_map/rhgd,rthd->rhgt/dot_general | solution.py:499
  27.2 0.2 fusion.22
  27.4 0.1 select_reduce_fusion.3
  27.5 0.1 reshape_broadcast_in_dim.6
  27.6 0.1 reshape_broadcast_in_dim.7
  27.7 1.9 %copy.25 = bf16[1024,4,256]{2,0,1:T(8,128)(2,1)S(1)} copy(bf16[1024,4,256]{2,1,0:T(4,128)(2,1)} %param.14) | data formatting | bytes 4194304 | tf_op jit(solution)/shard_map/optimization_barrier | solution.py:407
  29.6 0.1 fusion.24
  29.7 0.3 select_reduce_fusion.2
  30.0 1.0 select_reduce_fusion
  31.0 1.3 slice_bitcast_fusion.refs_7_
  32.3 0.5 fusion.7
  32.8 2.1 %convolution_convert_fusion.1 = bf16[4,4,8,8,1024]{4,3,2,1,0:T(8,128)(2,1)} fusion(bf16[1024,4,256]{2,0,1:T(8,128)(2,1)S(1)} %copy.25, bf16[4,8,32,128]{3,2,1,0:T(8,128)(2,1)S(1)} %pad_maximum_fusion), kind=kOutput, calls=%fused_computation.11 | convolution fusion | flops 269484032 | bytes 3407872 | tf_op jit(solution)/shard_map/qrhgd,phd->hqrgp/dot_general | solution.py:483
  34.8 1.3 fusion.51
  36.2 0.7 fusion.48
  37.4 0.7 concatenate.11.meta_ref
  38.1 3.2 %convolution_convert_fusion = bf16[4,4,8,8,1024]{4,3,2,1,0:T(8,128)(2,1)} fusion(bf16[1024,4,256]{2,0,1:T(8,128)(2,1)} %copy-done.2, bf16[4,8,32,128]{3,2,1,0:T(8,128)(2,1)S(1)} %collective-permute-done.4), kind=kOutput, calls=%fused_computation.10 | convolution fusion | flops 269484032 | bytes 3407872 | tf_op jit(solution)/shard_map/qrhgd,phd->hqrgp/dot_general | solution.py:483
  41.3 19.7 %all-to-all-done.7 = bf16[8,96,1024]{2,1,0:T(8,128)(2,1)S(1)} async-done(((bf16[8,96,1024]{2,1,0:T(8,128)(2,1)}), bf16[8,96,1024]{2,1,0:T(8,128)(2,1)S(1)}, u32[]{:S(2)}, u32[]{:S(2)}) %all-to-all-start.7) | async-done | bytes 1572896 | tf_op jit(solution)/shard_map/all_to_all | solution.py:414
  61.7 0.5 copy-done.1
  62.2 1.7 %conditional.2 = (bf16[256,1024]{1,0:T(8,128)(2,1)}, bf16[256,1024]{1,0:T(8,128)(2,1)}) conditional(s32[]{:T(128)} %bitcast.21, () %tuple.25, (s32[2]{0:T(128)S(1)}, s32[256]{0:T(256)S(1)}, s32[256]{0:T(256)S(1)}, bf16[256,8192]{1,0:T(8,128)(2,1)}) %tuple.49), branch_computations={%region_14.15_spmd, %region_15.16_spmd} | conditional | flops 134217728 | bytes 70254648 | solution.py:473
  62.2 0.9 broadcast.394
  63.0 0.9 broadcast.394.clone
  63.9 0.5 collective-permute-done.5.refs_1_
  64.4 1.2 copy-done.3
  65.6 9.7 %prompt_scores.1 = (bf16[8,32,384]{2,1,0:T(8,128)(2,1)}, bf16[8,32,256]{2,1,0:T(8,128)(2,1)S(1)}) custom-call(s32[651]{0:T(1024)} %concatenate.11.meta_ref, bf16[768,1024]{1,0:T(8,128)(2,1)} %bitcast.42, bf16[768,1024]{1,0:T(8,128)(2,1)} %copy-done.3, bf16[256,1024]{1,0:T(8,128)(2,1)} %get-tuple-element.91.refs_2_, ...), custom_call_target="tpu_custom_call" | custom-call | tf_op jit(solution)/shard_map/prompt_scores/pallas_call | solution.py:544
  75.3 24.0 %conditional.3 = (bf16[8,32,384]{2,1,0:T(8,128)(2,1)S(1)}, bf16[8,32,256]{2,1,0:T(8,128)(2,1)S(1)}, f32[8,32,128]{2,1,0:T(8,128)S(1)}) conditional(s32[]{:T(128)} %bitcast.22, (bf16[8,32,384]{2,1,0:T(8,128)(2,1)}, s32[1,640]{1,0:T(1,128)S(1)}, f32[8,32,1]{1,0,2:T(8,128)S(1)}, f32[8,32,1]{1,0,2:T(8,128)S(1)}, ...), branch_computations={%region_16.17_spmd, %region_17.18_spmd} | conditional | bytes 1516600 | solution.py:587
  75.3 3.5 %all-to-all-start.1 = ((bf16[8,32,384]{2,1,0:T(8,128)(2,1)}), bf16[8,32,384]{2,1,0:T(8,128)(2,1)S(1)}, u32[]{:S(2)}, u32[]{:S(2)}) async-start(bf16[8,32,384]{2,1,0:T(8,128)(2,1)} %get-tuple-element.39), calls=%async_computation.1 | async-start | bytes 393216 | tf_op jit(solution)/shard_map/cond/branch_0_fun/all_to_all | solution.py:573
  78.8 0.1 copy.31.refs_2_
  79.0 0.1 copy.32.refs_3_
  79.1 8.1 %all-to-all-done.1.refs_0_ = bf16[8,32,384]{2,1,0:T(8,128)(2,1)S(1)} async-done(((bf16[8,32,384]{2,1,0:T(8,128)(2,1)}), bf16[8,32,384]{2,1,0:T(8,128)(2,1)S(1)}, u32[]{:S(2)}, u32[]{:S(2)}) %all-to-all-start.1) | async-done | bytes 196640 | tf_op jit(solution)/shard_map/cond/branch_0_fun/all_to_all | solution.py:573
  87.2 1.2 softmax_weights.2
  88.4 10.7 %all_to_all.39 = bf16[8,32,384]{2,1,0:T(8,128)(2,1)S(1)} all-to-all(bf16[8,32,384]{2,1,0:T(8,128)(2,1)S(1)} %get-tuple-element.44), channel_id=1, replica_groups=mesh['groups'=2,'pool'=8,'tp'=2] {'pool'}, dimensions={0} | all-to-all | bytes 393216 | tf_op jit(solution)/shard_map/cond/branch_0_fun/all_to_all | solution.py:581
  99.3 9.8 %weighted_values.1 = bf16[4,2,4,64,128]{4,3,2,1,0:T(8,128)(2,1)} custom-call(s32[651]{0:T(1024)} %concatenate.11.meta_ref, bf16[768,1024]{1,0:T(8,128)(2,1)} %bitcast.43, bf16[768,1024]{1,0:T(8,128)(2,1)} %copy-done.3, bf16[256,1024]{1,0:T(8,128)(2,1)} %get-tuple-element.91.refs_2_, bf16[256,1024]{1,0:T(8,128)(2,1)} %get-tuple-element.92.refs_3_, ...), custom_call_target="tpu_custom_call" | custom-call | tf_op jit(solution)/shard_map/weighted_values/pallas_call | solution.py:590
  109.1 3.5 %all-to-all-start.8 = ((bf16[4,2,4,64,128]{4,3,2,1,0:T(8,128)(2,1)}), bf16[4,2,4,64,128]{4,3,2,1,0:T(8,128)(2,1)S(1)}, u32[]{:S(2)}, u32[]{:S(2)}) async-start(bf16[4,2,4,64,128]{4,3,2,1,0:T(8,128)(2,1)} %weighted_values.1), calls=%async_computation.8 | async-start | bytes 1048576 | tf_op jit(solution)/shard_map/all_to_all | solution.py:612
  112.6 6.7 %all-to-all-done.8.parts_ref = bf16[4,2,4,64,128]{4,3,2,1,0:T(8,128)(2,1)S(1)} async-done(((bf16[4,2,4,64,128]{4,3,2,1,0:T(8,128)(2,1)}), bf16[4,2,4,64,128]{4,3,2,1,0:T(8,128)(2,1)S(1)}, u32[]{:S(2)}, u32[]{:S(2)}) %all-to-all-start.8) | async-done | bytes 524320 | tf_op jit(solution)/shard_map/all_to_all | solution.py:612
  119.2 0.1 half_pool_sum.1
  119.3 1.2 collective-permute-start.6
  120.6 6.1 %collective-permute-done.6.got_ref = bf16[2,4,64,128]{3,2,1,0:T(8,128)(2,1)S(1)} collective-permute-done((bf16[2,4,64,128]{3,2,1,0:T(8,128)(2,1)S(1)}, bf16[2,4,64,128]{3,2,1,0:T(8,128)(2,1)S(1)}, u32[]{:S(2)}, u32[]{:S(2)}) %collective-permute-start.6) | collective-permute-done | bytes 131104 | tf_op jit(solution)/shard_map/ppermute | solution.py:357
  126.7 0.1 attended_sum.1
  126.8 1.5 %collective-permute-start.7 = (bf16[16,4096]{1,0:T(8,128)(2,1)S(1)}, bf16[16,4096]{1,0:T(8,128)(2,1)S(1)}, u32[]{:S(2)}, u32[]{:S(2)}) collective-permute-start(bf16[16,4096]{1,0:T(8,128)(2,1)S(1)} %attended_sum.1), channel_id=1, source_target_pairs={{0,2},{2,0},{4,6},{6,4},{8,10},{10,8},{12,14},{14,12},{1,3},{3,1},... | collective-permute-start | bytes 393224 | tf_op jit(solution)/shard_map/ppermute | solution.py:357
  128.3 2.0 %collective-permute-start.9 = (bf16[16,4096]{1,0:T(8,128)(2,1)S(1)}, bf16[16,4096]{1,0:T(8,128)(2,1)S(1)}, u32[]{:S(2)}, u32[]{:S(2)}) collective-permute-start(bf16[16,4096]{1,0:T(8,128)(2,1)S(1)} %attended_sum.1), channel_id=1, source_target_pairs={{0,6},{2,4},{4,2},{6,0},{8,14},{10,12},{12,10},{14,8},{1,7},{3,5},... | collective-permute-start | bytes 393224 | tf_op jit(solution)/shard_map/ppermute | solution.py:357
  130.3 1.5 %collective-permute-done.7 = bf16[16,4096]{1,0:T(8,128)(2,1)S(1)} collective-permute-done((bf16[16,4096]{1,0:T(8,128)(2,1)S(1)}, bf16[16,4096]{1,0:T(8,128)(2,1)S(1)}, u32[]{:S(2)}, u32[]{:S(2)}) %collective-permute-start.7) | collective-permute-done | bytes 131104 | tf_op jit(solution)/shard_map/ppermute | solution.py:357
  131.8 1.4 %collective-permute-done.8 = bf16[16,4096]{1,0:T(8,128)(2,1)S(1)} collective-permute-done((bf16[16,4096]{1,0:T(8,128)(2,1)S(1)}, bf16[16,4096]{1,0:T(8,128)(2,1)S(1)}, u32[]{:S(2)}, u32[]{:S(2)}) %collective-permute-start.8) | collective-permute-done | bytes 131104 | tf_op jit(solution)/shard_map/ppermute | solution.py:357
  133.2 1.4 %collective-permute-done.9 = bf16[16,4096]{1,0:T(8,128)(2,1)S(1)} collective-permute-done((bf16[16,4096]{1,0:T(8,128)(2,1)S(1)}, bf16[16,4096]{1,0:T(8,128)(2,1)S(1)}, u32[]{:S(2)}, u32[]{:S(2)}) %collective-permute-start.9) | collective-permute-done | bytes 131104 | tf_op jit(solution)/shard_map/ppermute | solution.py:357
  134.7 4.9 %fusion.10 = f32[64,1024]{1,0:T(8,128)S(1)} fusion(bf16[4096,1024]{1,0:T(8,128)(2,1)} %param.21, bf16[16,4096]{1,0:T(8,128)(2,1)S(1)} %collective-permute-done.9, bf16[16,4096]{1,0:T(8,128)(2,1)S(1)} %collective-permute-done.8, bf16[16,4096]{1,0:T(8,128)(2,1)S(1)} %collective-permute-done.7, bf16[16,4096]{1,0:T(8,128)(2,1)S(1)} %attended_sum.1), kind=kOutput, calls=%fused_computation.19 | convolution fusion | flops 538968064 | bytes 9175040 | tf_op jit(solution)/shard_map/dot_general | solution.py:635
  139.7 1.3 collective-permute-done.10.got_ref
  141.1 0.6 order_rows.1
  (44 shorter events, 0.4 us)
Async XLA Ops:
  0.0 8.7 %collective-permute-start.1 = (bf16[8,32,128]{2,1,0:T(8,128)(2,1)}, bf16[8,32,128]{2,1,0:T(8,128)(2,1)S(1)}, u32[]{:S(2)}, u32[]{:S(2)}) collective-permute-start(bf16[8,32,128]{2,1,0:T(8,128)(2,1)} %param.18), channel_id=1, source_target_pairs={{0,8},{2,10},{4,12},{6,14},{8,0},{10,2},{12,4},{14,6},{1,9},{3,11}... | collective-permute-start | bytes 196616 | tf_op jit(solution)/shard_map/ppermute | solution.py:357
  4.1 4.5 %copy-start.10 = (s32[8]{0:T(128)S(1)}, s32[8]{0:T(128)}, u32[]{:S(2)}) copy-start(s32[8]{0:T(128)} %param.20) | copy-start | bytes 100
  4.1 4.7 %copy-start.5 = (bf16[8,32,128]{2,1,0:T(8,128)(2,1)S(1)}, bf16[8,32,128]{2,1,0:T(8,128)(2,1)}, u32[]{:S(2)}) copy-start(bf16[8,32,128]{2,1,0:T(8,128)(2,1)} %param.18) | copy-start | bytes 196612
  4.1 6.3 %copy-start = (bf16[256,8192]{1,0:T(8,128)(2,1)S(1)}, bf16[256,8192]{1,0:T(8,128)(2,1)}, u32[]{:S(2)}) copy-start(bf16[256,8192]{1,0:T(8,128)(2,1)} %x_ref.1) | copy-start | bytes 12582916
  4.1 6.3 %copy-start.7 = (s32[256,1]{0,1:T(1,128)S(1)}, s32[256,1]{0,1:T(1,128)}, u32[]{:S(2)}) copy-start(s32[256,1]{0,1:T(1,128)} %param.15) | copy-start | bytes 3076
  4.1 6.3 %copy-start.8 = (s32[256]{0:T(256)S(1)}, s32[256]{0:T(256)}, u32[]{:S(2)}) copy-start(s32[256]{0:T(256)} %fill_ref.1) | copy-start | bytes 3076
  8.8 5.9 %collective-permute-start.2 = (bf16[2,8,32,128]{3,2,1,0:T(8,128)(2,1)S(1)}, bf16[2,8,32,128]{3,2,1,0:T(8,128)(2,1)S(1)}, u32[]{:S(2)}, u32[]{:S(2)}) collective-permute-start(bf16[2,8,32,128]{3,2,1,0:T(8,128)(2,1)S(1)} %pad_maximum_fusion.1), channel_id=1, source_target_pairs={{0,4},{2,6},{4,0},{6,2},{8,12},{10,14},{12,8},{14,10},{1,5},{3,7},... | collective-permute-start | bytes 393224 | tf_op jit(solution)/shard_map/ppermute | solution.py:357
  10.4 5.0 %copy-start.9 = (s32[256]{0:T(256)S(1)}, s32[256]{0:T(256)}, u32[]{:S(2)}) copy-start(s32[256]{0:T(256)} %param.16) | copy-start | bytes 3076
  18.2 16.6 %collective-permute-start.3 = (s32[2]{0:T(128)S(1)}, s32[2]{0:T(128)S(1)}, u32[]{:S(2)}, u32[]{:S(2)}) collective-permute-start(s32[2]{0:T(128)S(1)} %pad_add_fusion.1), channel_id=1, source_target_pairs={{0,16},{16,0},{1,17},{17,1},{2,18},{18,2},{3,19},{19,3},{4,20},{20... | collective-permute-start | bytes 32 | tf_op jit(solution)/shard_map/ppermute | solution.py:460
  19.7 18.3 %collective-permute-start.4 = (bf16[4,8,32,128]{3,2,1,0:T(8,128)(2,1)S(1)}, bf16[4,8,32,128]{3,2,1,0:T(8,128)(2,1)S(1)}, u32[]{:S(2)}, u32[]{:S(2)}) collective-permute-start(bf16[4,8,32,128]{3,2,1,0:T(8,128)(2,1)S(1)} %pad_maximum_fusion), channel_id=1, source_target_pairs={{0,2},{2,0},{4,6},{6,4},{8,10},{10,8},{12,14},{14,12},{1,3},{3,1},... | collective-permute-start | bytes 786440 | tf_op jit(solution)/shard_map/ppermute | solution.py:357
  21.3 39.7 %all-to-all-start.7 = ((bf16[8,96,1024]{2,1,0:T(8,128)(2,1)}), bf16[8,96,1024]{2,1,0:T(8,128)(2,1)S(1)}, u32[]{:S(2)}, u32[]{:S(2)}) async-start(bf16[8,96,1024]{2,1,0:T(8,128)(2,1)} %pack_live_tokens.3), calls=%async_computation.7 | async-start | bytes 3145728 | tf_op jit(solution)/shard_map/all_to_all | solution.py:414
  29.5 3.2 %copy-start.2 = (bf16[1024,4,256]{2,0,1:T(8,128)(2,1)}, bf16[1024,4,256]{2,0,1:T(8,128)(2,1)S(1)}, u32[]{:S(2)}) copy-start(bf16[1024,4,256]{2,0,1:T(8,128)(2,1)S(1)} %copy.25) | copy-start | bytes 6291460
  29.5 2.8 %copy-start.4 = (bf16[8,256,4,128]{3,2,1,0:T(4,128)(2,1)S(1)}, bf16[8,256,4,128]{3,2,1,0:T(4,128)(2,1)}, u32[]{:S(2)}) copy-start(bf16[8,256,4,128]{3,2,1,0:T(4,128)(2,1)} %get-tuple-element.137) | copy-start | bytes 6291460
  31.0 32.9 %copy-start.6 = (s32[5120]{0:T(1024)}, s32[5120]{0:T(1024)S(1)}, u32[]{:S(2)}) copy-start(s32[5120]{0:T(1024)S(1)} %broadcast_add_fusion) | copy-start | bytes 61444
  61.0 1.2 copy-start.1
  61.0 3.4 %collective-permute-start.5 = (bf16[768,1024]{1,0:T(8,128)(2,1)S(1)}, bf16[768,1024]{1,0:T(8,128)(2,1)S(1)}, u32[]{:S(2)}, u32[]{:S(2)}) collective-permute-start(bf16[768,1024]{1,0:T(8,128)(2,1)S(1)} %bitcast.41), channel_id=1, source_target_pairs={{0,1},{1,0},{2,3},{3,2},{4,5},{5,4},{6,7},{7,6},{8,9},{9,8},{10,11... | collective-permute-start | bytes 4718600 | tf_op jit(solution)/shard_map/ppermute | solution.py:521
  64.4 1.2 copy-start.3
  75.3 11.9 %all-to-all-start.1 = ((bf16[8,32,384]{2,1,0:T(8,128)(2,1)}), bf16[8,32,384]{2,1,0:T(8,128)(2,1)S(1)}, u32[]{:S(2)}, u32[]{:S(2)}) async-start(bf16[8,32,384]{2,1,0:T(8,128)(2,1)} %get-tuple-element.39), calls=%async_computation.1 | async-start | bytes 393216 | tf_op jit(solution)/shard_map/cond/branch_0_fun/all_to_all | solution.py:573
  109.1 10.2 %all-to-all-start.8 = ((bf16[4,2,4,64,128]{4,3,2,1,0:T(8,128)(2,1)}), bf16[4,2,4,64,128]{4,3,2,1,0:T(8,128)(2,1)S(1)}, u32[]{:S(2)}, u32[]{:S(2)}) async-start(bf16[4,2,4,64,128]{4,3,2,1,0:T(8,128)(2,1)} %weighted_values.1), calls=%async_computation.8 | async-start | bytes 1048576 | tf_op jit(solution)/shard_map/all_to_all | solution.py:612
  119.3 7.3 %collective-permute-start.6 = (bf16[2,4,64,128]{3,2,1,0:T(8,128)(2,1)S(1)}, bf16[2,4,64,128]{3,2,1,0:T(8,128)(2,1)S(1)}, u32[]{:S(2)}, u32[]{:S(2)}) collective-permute-start(bf16[2,4,64,128]{3,2,1,0:T(8,128)(2,1)S(1)} %get-tuple-element.106), channel_id=1, source_target_pairs={{0,8},{2,10},{4,12},{6,14},{8,0},{10,2},{12,4},{14,6},{1,9},{3,11}... | collective-permute-start | bytes 393224 | tf_op jit(solution)/shard_map/ppermute | solution.py:357
  126.8 5.0 %collective-permute-start.7 = (bf16[16,4096]{1,0:T(8,128)(2,1)S(1)}, bf16[16,4096]{1,0:T(8,128)(2,1)S(1)}, u32[]{:S(2)}, u32[]{:S(2)}) collective-permute-start(bf16[16,4096]{1,0:T(8,128)(2,1)S(1)} %attended_sum.1), channel_id=1, source_target_pairs={{0,2},{2,0},{4,6},{6,4},{8,10},{10,8},{12,14},{14,12},{1,3},{3,1},... | collective-permute-start | bytes 393224 | tf_op jit(solution)/shard_map/ppermute | solution.py:357
  128.3 5.0 %collective-permute-start.8 = (bf16[16,4096]{1,0:T(8,128)(2,1)S(1)}, bf16[16,4096]{1,0:T(8,128)(2,1)S(1)}, u32[]{:S(2)}, u32[]{:S(2)}) collective-permute-start(bf16[16,4096]{1,0:T(8,128)(2,1)S(1)} %attended_sum.1), channel_id=1, source_target_pairs={{0,4},{2,6},{4,0},{6,2},{8,12},{10,14},{12,8},{14,10},{1,5},{3,7},... | collective-permute-start | bytes 393224 | tf_op jit(solution)/shard_map/ppermute | solution.py:357
  128.3 6.4 %collective-permute-start.9 = (bf16[16,4096]{1,0:T(8,128)(2,1)S(1)}, bf16[16,4096]{1,0:T(8,128)(2,1)S(1)}, u32[]{:S(2)}, u32[]{:S(2)}) collective-permute-start(bf16[16,4096]{1,0:T(8,128)(2,1)S(1)} %attended_sum.1), channel_id=1, source_target_pairs={{0,6},{2,4},{4,2},{6,0},{8,14},{10,12},{12,10},{14,8},{1,7},{3,5},... | collective-permute-start | bytes 393224 | tf_op jit(solution)/shard_map/ppermute | solution.py:357
  139.6 1.4 collective-permute-start.10

commit v12 on v11

--- a/solution.py
+++ b/solution.py
@@ -11,21 +11,14 @@
 MIB = 1 << 20
 
 
-def pack_kernel(base, at_ref, fill_ref, dest_ref, x_ref, out_ref, held, packed, count, in_sem, out_sem):
-    n, tokens, part = held.shape
-    size = packed.shape[1]
+def pack_kernel(base, at_ref, fill_ref, dest_ref, x_ref, out_ref, packed, count, out_sem):
+    n, size, part = packed.shape
+    tokens = x_ref.shape[0]
     blocks = tokens // BLK
-
-    def load(q):
-        return pltpu.make_async_copy(
-            x_ref.at[:, pl.ds(q * part, part)], held.at[q], in_sem.at[q]
-        )
 
     def store(q):
         return pltpu.make_async_copy(packed.at[q], out_ref.at[q], out_sem.at[q])
 
-    for q in range(n):
-        load(q).start()
     first = at_ref[0] * blocks
     for q in range(n):
         count[q] = 0
@@ -55,10 +48,9 @@
     wanted = base + at_ref[1] * size + lax.broadcasted_iota(jnp.int32, (size, tokens), 0)
     pick = (wanted == ranks).astype(jnp.bfloat16)
     for q in range(n):
-        load(q).wait()
-        packed[q] = jnp.dot(pick, held[q], preferred_element_type=jnp.float32).astype(
-            packed.dtype
-        )
+        packed[q] = jnp.dot(
+            pick, x_ref[:, q * part : (q + 1) * part], preferred_element_type=jnp.float32
+        ).astype(packed.dtype)
         store(q).start()
     for q in range(n):
         store(q).wait()
@@ -72,18 +64,16 @@
         grid_spec=pltpu.PrefetchScalarGridSpec(
             num_scalar_prefetch=3,
             grid=(1,),
-            in_specs=[pl.BlockSpec(memory_space=pl.ANY)],
+            in_specs=[pl.BlockSpec(memory_space=pltpu.VMEM)],
             out_specs=pl.BlockSpec(memory_space=pl.ANY),
             scratch_shapes=[
-                pltpu.VMEM((n, tokens, part), jnp.bfloat16),
                 pltpu.VMEM((n, size, part), jnp.bfloat16),
                 pltpu.SMEM((n,), jnp.int32),
-                pltpu.SemaphoreType.DMA((n,)),
                 pltpu.SemaphoreType.DMA((n,)),
             ],
         ),
         out_shape=jax.ShapeDtypeStruct((n, size, part), jnp.bfloat16),
-        compiler_params=pltpu.CompilerParams(vmem_limit_bytes=56 * MIB),
+        compiler_params=pltpu.CompilerParams(vmem_limit_bytes=16 * MIB),
         cost_estimate=pl.CostEstimate(
             flops=2 * size * tokens * width, bytes_accessed=64 * MIB, transcendentals=0
         ),
@@ -99,56 +89,46 @@
     return min(lanes, -(-lanes * 3 // 5 // 128) * 128)
 
 
-def load_tokens(n, core, over, x_refs, held, more, wide, sem, others=()):
-    size, extra = held.shape[1] // n, more.shape[1] // n
-    tokens = 2 * (size + extra)
+def widen(core, n, refs, wide, base, first, last):
+    length = refs[0].shape[0] // n
+    tokens = wide.shape[0] // n
+
+    @pl.loop(first, last)
+    def _(s):
+        for j, ref in enumerate(refs):
+            side = core if j == 0 else 1 - core
+            to = pl.multiple_of(s * tokens + base + side * length, BLK)
+            wide[pl.ds(to, length), :] = ref[
+                pl.ds(pl.multiple_of(s * length, length), length), :
+            ].astype(wide.dtype)
+
+
+def span_copies(refs, buffer, sem):
     cuts = sem.shape[1]
-
-    def copies(refs, buffer):
-        span = buffer.shape[1] // cuts
-        return [
-            [
-                pltpu.make_async_copy(
-                    ref.at[pl.ds(i * span, span)], buffer.at[j, pl.ds(i * span, span)], sem.at[j, i]
-                )
-                for j, ref in enumerate(refs)
-            ]
-            for i in range(cuts)
+    span = buffer.shape[1] // cuts
+    return [
+        [
+            pltpu.make_async_copy(
+                ref.at[pl.ds(i * span, span)], buffer.at[j, pl.ds(i * span, span)], sem.at[j, i]
+            )
+            for j, ref in enumerate(refs)
         ]
-
-    def widen(buffer, base, first, last):
-        length = buffer.shape[1] // n
-
-        @pl.loop(first, last)
-        def _(s):
-            for j in range(2):
-                side = core if j == 0 else 1 - core
-                to = pl.multiple_of(s * tokens + base + side * length, BLK)
-                wide[pl.ds(to, length), :] = buffer[
-                    j, pl.ds(pl.multiple_of(s * length, length), length), :
-                ].astype(wide.dtype)
-
-    main = copies(x_refs[:2], held)
-    for pair in main:
-        for copy in pair:
-            copy.start()
-    for copy in others:
-        copy.start()
-    for i, pair in enumerate(main):
-        for copy in pair:
-            copy.wait()
-        widen(held, 0, i * n // cuts, (i + 1) * n // cuts)
-
+        for i in range(cuts)
+    ]
+
+
+def widen_rest(core, over, n, refs, more, wide, sem):
     @pl.when(over != 0)
     def _():
-        rest = copies(x_refs[2:], more)
+        rest = span_copies(refs, more, sem)
         for pair in rest:
             for copy in pair:
                 copy.start()
         for pair in rest:
             for copy in pair:
                 copy.wait()
-        widen(more, 2 * size, 0, n)
+        base = wide.shape[0] // n - 2 * more.shape[1] // n
+        widen(core, n, [more.at[0], more.at[1]], wide, base, 0, n)
 
 
 def list_tile(meta_ref, first, count, wide, tile):
@@ -162,7 +142,7 @@
 
 def score_kernel(n, rows, meta_ref, *refs):
     x_refs, keyed_refs, (row_ref, near_ref, rest_ref) = refs[:4], refs[4:6], refs[6:9]
-    held, more, wide, tile, keyed, sem, keyed_sem = refs[9:]
+    more, wide, tile, keyed, sem, keyed_sem = refs[9:]
     step = pl.program_id(0)
     part = wide.shape[1]
     near = near_ref.shape[2]
@@ -174,22 +154,30 @@
     kvh, per = keyed.shape[0], keyed.shape[1] // n
     group = per // rows
 
+    def load(i):
+        span = n // 2 * per
+        return [
+            pltpu.make_async_copy(
+                keyed_refs[i].at[h], keyed.at[h, pl.ds(i * span, span)], keyed_sem.at[i, h]
+            )
+            for h in range(kvh)
+        ]
+
     @pl.when(step == 0)
     def _():
-        span = n // 2 * per
-        loads = [
-            pltpu.make_async_copy(
-                ref.at[h], keyed.at[h, pl.ds(i * span, span)], keyed_sem.at[i, h]
-            )
-            for i, ref in enumerate(keyed_refs)
-            for h in range(kvh)
-        ]
-        load_tokens(
-            n, meta_ref[at_size + n + 1], meta_ref[at_size + n + 2], x_refs, held, more, wide, sem,
-            loads,
-        )
-        for load in loads:
-            load.wait()
+        for i in range(2):
+            for copy in load(i):
+                copy.start()
+        core = meta_ref[at_size + n + 1]
+        widen(core, n, x_refs[:2], wide, 0, 0, n)
+        widen_rest(core, meta_ref[at_size + n + 2], n, x_refs[2:], more, wide, sem)
+
+    for i in range(2):
+
+        @pl.when(step == i * (n // 2))
+        def _(i=i):
+            for copy in load(i):
+                copy.wait()
 
     def one(t):
         here = slice(cuts[t], cuts[t + 1])
@@ -217,8 +205,8 @@
 
 def weight_kernel(scale, count, *refs):
     part_refs, row_refs = refs[:count], refs[count : 2 * count]
-    top_ref, sum_ref, cached_ref = refs[2 * count : 2 * count + 3]
-    w_refs, kept_ref = refs[2 * count + 3 : -1], refs[-1]
+    top_ref, sum_ref = refs[2 * count : 2 * count + 2]
+    w_refs, share_ref = refs[2 * count + 2 : -1], refs[-1]
     n = part_refs[0].shape[0]
     scores, owner_rows = [], []
     for part_ref, row_ref in zip(part_refs, row_refs):
@@ -240,7 +228,7 @@
         for h in held:
             total = total + jnp.sum(h, 1, keepdims=True)
         weights = [w + h / total for w, h in zip(weights, held)]
-        kept_ref[r] = cached_ref[r] * (fade / total)
+        share_ref[r] = fade / total
     for w, w_ref in zip(weights, w_refs):
         for i in range(n):
             w_ref[i] = w.astype(w_ref.dtype)
@@ -261,10 +249,18 @@
 
     @pl.when(q == 0)
     def _():
-        load_tokens(
-            n, meta_ref[at_size + n + 1], meta_ref[at_size + n + 2], x_refs, held, more, wide, sem,
-            [load_values],
-        )
+        core = meta_ref[at_size + n + 1]
+        main = span_copies(x_refs[:2], held, sem)
+        for pair in main:
+            for copy in pair:
+                copy.start()
+        load_values.start()
+        for i, pair in enumerate(main):
+            for copy in pair:
+                copy.wait()
+            parts = [held.at[0], held.at[1]]
+            widen(core, n, parts, wide, 0, i * n // len(main), (i + 1) * n // len(main))
+        widen_rest(core, meta_ref[at_size + n + 2], n, x_refs[2:], more, wide, sem)
 
     def one(t):
         here = slice(cuts[t], cuts[t + 1])
@@ -403,13 +399,8 @@
     packed = pack(x_prompt, pack_fill, pack_dest, at, n, 0, size)
     dest = pack_dest
     even = from_rest(jnp.stack([queries, with_partner(queries, n // 2, n)]), n)
-    packed, even, dest, block_row, block_fill, query, kv_weight, ready = (
-        lax.optimization_barrier(
-            (
-                packed, even, dest, block_row, block_fill, queries, kv_weight,
-                jnp.ones((), jnp.bool_),
-            )
-        )
+    packed, even, dest, block_row, block_fill, kv_weight = lax.optimization_barrier(
+        (packed, even, dest, block_row, block_fill, kv_weight)
     )
     mine = lax.all_to_all(packed, "pool", 0, 0, tiled=True).reshape(n * size, part)
 
@@ -489,34 +480,8 @@
     keyed_odd = through_keys(with_partner(even, 1, n))
     values = kv_weight[:, :, hd:].transpose(1, 0, 2)
 
-    query = query.reshape(rows, kvh, group, hd)
-    cache_live = jnp.arange(cache_slots, dtype=jnp.int32)[None, :] < cache_len[:, None]
-    cached_keys, cached_values = (
-        jnp.where(ready, kv_cache[:, :, :, at : at + hd], 0)
-        for at in (0, hd)
-    )
-    cache_scores = (
-        jnp.einsum("rhgd,rthd->rhgt", query, cached_keys, preferred_element_type=jnp.float32)
-        * scale
-    )
-    cache_scores = jnp.where(cache_live[:, None, None, :], cache_scores, -jnp.inf)
-    cache_top = jnp.max(cache_scores, -1, keepdims=True)
-    cache_exp = jnp.exp(cache_scores - cache_top)
-    cache_sum = jnp.sum(cache_exp, -1, keepdims=True)
-    cached = jnp.einsum(
-        "rhgt,rthd->rhgd",
-        cache_exp.astype(jnp.bfloat16),
-        cached_values,
-        preferred_element_type=jnp.float32,
-    )
-    cache_top = cache_top.reshape(rows, heads, 1)
-    cache_sum = cache_sum.reshape(rows, heads, 1)
-    cached = cached.reshape(rows, heads, hd)
-
-    mine, meta, rowof, keyed_even, keyed_odd, values, cache_top, cache_sum, cached = (
-        lax.optimization_barrier(
-            (mine, meta, rowof, keyed_even, keyed_odd, values, cache_top, cache_sum, cached)
-        )
+    mine, meta, rowof, keyed_even, keyed_odd, values = lax.optimization_barrier(
+        (mine, meta, rowof, keyed_even, keyed_odd, values)
     )
     other = lax.ppermute(mine, "tp", swap)
 
@@ -531,7 +496,6 @@
     in_vmem = pl.BlockSpec(memory_space=pltpu.VMEM)
     x_parts = (mine, other, more_mine, more_other)
     x_scratch = [
-        pltpu.VMEM((ntp, n * size, part), jnp.bfloat16),
         pltpu.VMEM((ntp, n * extra, part), jnp.bfloat16),
         pltpu.VMEM((n * tokens, part), jnp.float32),
         pltpu.VMEM((tile_cuts(lanes)[1], part), jnp.bfloat16),
@@ -547,7 +511,8 @@
             num_scalar_prefetch=1,
             grid=(n,),
             in_specs=[
-                *[in_hbm] * 6,
+                *[in_vmem] * 2,
+                *[in_hbm] * 4,
                 pl.BlockSpec((1, 1, lanes), lambda i, m: (owner(i, m), 0, 0)),
             ],
             out_specs=[
@@ -562,7 +527,7 @@
             ],
         ),
         out_shape=slot_shapes,
-        compiler_params=pltpu.CompilerParams(vmem_limit_bytes=56 * MIB),
+        compiler_params=pltpu.CompilerParams(vmem_limit_bytes=20 * MIB),
         name="prompt_scores",
     )(meta, *x_parts, keyed_even, keyed_odd, rowof)
 
@@ -571,14 +536,38 @@
     def exchange_weights(*scores):
         count = len(scores)
         parts = [lax.all_to_all(s, "pool", 0, 0, tiled=True) for s in scores]
+        query = queries.reshape(rows, kvh, group, hd)
+        cache_scores = (
+            jnp.einsum(
+                "rhgd,rthd->rhgt", query, kv_cache[:, :, :, :hd], preferred_element_type=jnp.float32
+            )
+            * scale
+        )
+        cache_live = jnp.arange(cache_slots, dtype=jnp.int32)[None, :] < cache_len[:, None]
+        cache_scores = jnp.where(cache_live[:, None, None, :], cache_scores, -jnp.inf)
+        cache_top = jnp.max(cache_scores, -1, keepdims=True)
+        cache_exp = jnp.exp(cache_scores - cache_top)
+        cache_sum = jnp.sum(cache_exp, -1, keepdims=True)
         row_parts = [my_rows[:, :near], my_rows[:, near:]][:count]
-        *weights, kept = pl.pallas_call(
+        *weights, share = pl.pallas_call(
             functools.partial(weight_kernel, scale, count),
-            out_shape=[*slot_shapes[:count], jax.ShapeDtypeStruct((rows, heads, hd), jnp.float32)],
+            out_shape=[*slot_shapes[:count], jax.ShapeDtypeStruct((rows, heads, 1), jnp.float32)],
             compiler_params=pltpu.CompilerParams(vmem_limit_bytes=8 * MIB),
             name="softmax_weights",
-        )(*parts, *row_parts, cache_top, cache_sum, cached)
-        return *[lax.all_to_all(w, "pool", 0, 0, tiled=True) for w in weights], kept
+        )(
+            *parts,
+            *row_parts,
+            cache_top.reshape(rows, heads, 1),
+            cache_sum.reshape(rows, heads, 1),
+        )
+        weights = [lax.all_to_all(w, "pool", 0, 0, tiled=True) for w in weights]
+        cached = jnp.einsum(
+            "rhgt,rthd->rhgd",
+            cache_exp.astype(jnp.bfloat16),
+            kv_cache[:, :, :, hd:],
+            preferred_element_type=jnp.float32,
+        )
+        return *weights, cached.reshape(rows, heads, hd) * share
 
     def near_only():
         weights, kept = exchange_weights(score_near)
@@ -595,6 +584,7 @@
             in_specs=[*[in_hbm] * 4, *slot_specs, row_spec, in_hbm],
             out_specs=pl.BlockSpec((n // 2, 2, kvh, per, hd), lambda q, m: (0, 0, 0, 0, 0)),
             scratch_shapes=[
+                pltpu.VMEM((ntp, n * size, part), jnp.bfloat16),
                 *x_scratch,
                 pltpu.VMEM((kvh, part, hd), jnp.bfloat16),
                 pltpu.VMEM((kvh * per, part), jnp.float32),

time: 143 us -> 147 us (1.028)
  blocking collectives: 10.7 us -> 0 us
  waiting for transfers between devices: 46.8 us -> 56.3 us
  starting transfers between devices: 24.1 us -> 27.5 us
  Pallas kernels: 25.7 us -> 23.9 us
  local copies, waits for them, and re-layouts: 13.1 us -> 14.9 us
    all_to_all x1 -> x0, blocking collectives: 10.7 us -> none  [exchange_weights(): lax.all_to_all(w, 'pool', 0, 0, tiled=True)]
    all_to_all x0 -> x1, waiting for transfers between devices: none -> 5.66 us  [exchange_weights(): weights = [lax.all_to_all(w, 'pool', 0, 0, tiled=True) for w in weights]]
    ppermute x7, waiting for transfers between devices: 10.5 us -> 15.7 us  [with_partner(): return lax.ppermute(x, 'pool', [(i, i ^ k) for i in range(n)])]
    all_to_all x1, waiting for transfers between devices: 8.1 us -> 3.06 us  [exchange_weights(): parts = [lax.all_to_all(s, 'pool', 0, 0, tiled=True) for s in scores]]
    slice x1 -> x0, local copies, waits for them, and re-layouts: 4.46 us -> none  [local(): kv_cache[:, :, :, at:at + hd]]
    all_to_all x0 -> x1, starting transfers between devices: none -> 4.01 us  [exchange_weights(): weights = [lax.all_to_all(w, 'pool', 0, 0, tiled=True) for w in weights]]
    all_to_all x1, waiting for transfers between devices: 19.7 us -> 23.1 us  [local(): lax.all_to_all(packed, 'pool', 0, 0, tiled=True).reshape(n * size, part)]
    pallas_call x1, Pallas kernels: 9.72 us -> 6.56 us  [local(): pl.pallas_call(functools.partial(score_kernel, n, rows), grid_spec=pltpu....]
  transfers between devices with their start and end apart: 13 -> 14, of which waited for: 9 -> 11; matrix products, arithmetic and copies ran while one was open for 16% -> 15% of each run, Pallas kernels for 3% -> 3%
where the time goes in v12:
time: 147 us; the launch traced here: 146 us
  waiting for transfers between devices  56.3 us (38%)
  starting transfers between devices  27.5 us (19%)
  Pallas kernels  23.9 us (16%)
  local copies, waits for them, and re-layouts  14.9 us (10%)
  matrix products  14.2 us (10%)
  other arithmetic  7.24 us (5%)
    all_to_all x1, waiting for transfers between devices, local(): lax.all_to_all(packed, 'pool', 0, 0, tiled=True).reshape(n * size, part)  23.1 us
    ppermute x7, waiting for transfers between devices, with_partner(): return lax.ppermute(x, 'pool', [(i, i ^ k) for i in range(n)])  15.7 us
    ppermute x7, starting transfers between devices, with_partner(): return lax.ppermute(x, 'pool', [(i, i ^ k) for i in range(n)])  10.4 us
    pallas_call x1, Pallas kernels, local(): pl.pallas_call(functools.partial(value_kernel, n, rows), grid_spec=pltpu....  10 us
    pallas_call x1, Pallas kernels, local(): pl.pallas_call(functools.partial(score_kernel, n, rows), grid_spec=pltpu....  6.56 us
    all_to_all x1, waiting for transfers between devices, local(): lax.all_to_all(terms, 'pool', 0, 0, axis_index_groups=halves, tiled=True)  6.53 us
    dot_general x2, matrix products, through_keys(): jnp.einsum('qrhgd,phd->hqrgp', held, keys, preferred_element_type=jnp.flo...  6.52 us
    all_to_all x1, waiting for transfers between devices, exchange_weights(): weights = [lax.all_to_all(w, 'pool', 0, 0, tiled=True) for w in weights]  5.66 us
  transfers between devices with their start and end apart: 14, of which 11 were waited for; matrix products, arithmetic and copies ran while one was open for 15% of the time, Pallas kernels for 3%

profile of v12, /device:TPU:0, one launch (start us, length us, event | category | flops | bytes accessed | tf_op | source)
XLA Modules:
  0.0 145.7 jit_solution(13167026805242371054)
XLA Ops:
  0.0 4.1 %collective-permute-start.1 = (bf16[8,32,128]{2,1,0:T(8,128)(2,1)}, bf16[8,32,128]{2,1,0:T(8,128)(2,1)S(1)}, u32[]{:S(2)}, u32[]{:S(2)}) collective-permute-start(bf16[8,32,128]{2,1,0:T(8,128)(2,1)} %param.18), channel_id=1, source_target_pairs={{0,8},{2,10},{4,12},{6,14},{8,0},{10,2},{12,4},{14,6},{1,9},{3,11}... | collective-permute-start | bytes 196616 | tf_op jit(solution)/shard_map/ppermute | solution.py:353
  4.2 3.8 %collective-permute-done.1 = bf16[8,32,128]{2,1,0:T(8,128)(2,1)S(1)} collective-permute-done((bf16[8,32,128]{2,1,0:T(8,128)(2,1)}, bf16[8,32,128]{2,1,0:T(8,128)(2,1)S(1)}, u32[]{:S(2)}, u32[]{:S(2)}) %collective-permute-start.1) | collective-permute-done | bytes 65568 | tf_op jit(solution)/shard_map/ppermute | solution.py:353
  8.0 0.9 pad_maximum_fusion.1
  8.8 0.7 collective-permute-start.2
  9.6 4.8 %pack_live_tokens.3 = bf16[8,96,1024]{2,1,0:T(8,128)(2,1)} custom-call(s32[2]{0:T(128)S(1)} %pad_add_fusion.at_ref, s32[256]{0:T(256)} %fill_ref.1, s32[256]{0:T(256)} %bitcast.64, bf16[256,8192]{1,0:T(8,128)(2,1)} %x_ref.1), custom_call_target="tpu_custom_call" | custom-call | flops 402653184 | bytes 67108864 | tf_op jit(solution)/shard_map/pack_live_tokens/pallas_call | solution.py:62
  14.5 0.2 select_reduce_fusion.5
  14.7 0.1 reduce_sum.113
  14.9 0.1 fusion.71
  15.0 0.1 select_reduce_fusion.6
  15.2 0.7 reduce_max.37
  15.9 0.1 reduce_sum.119
  16.0 0.6 reduce_max.36
  16.6 1.3 pad_add_fusion.1
  17.8 1.5 %collective-permute-start.3 = (s32[2]{0:T(128)S(1)}, s32[2]{0:T(128)S(1)}, u32[]{:S(2)}, u32[]{:S(2)}) collective-permute-start(s32[2]{0:T(128)S(1)} %pad_add_fusion.1), channel_id=1, source_target_pairs={{0,16},{16,0},{1,17},{17,1},{2,18},{18,2},{3,19},{19,3},{4,20},{20... | collective-permute-start | bytes 32 | tf_op jit(solution)/shard_map/ppermute | solution.py:451
  19.3 1.6 %copy.29 = bf16[1024,4,256]{2,0,1:T(8,128)(2,1)} copy(bf16[1024,4,256]{2,1,0:T(4,128)(2,1)S(1)} %copy-done.7) | data formatting | bytes 4194304 | tf_op jit(solution)/shard_map/optimization_barrier | solution.py:402
  20.9 1.5 %collective-permute-start.4 = (bf16[4,8,32,128]{3,2,1,0:T(8,128)(2,1)S(1)}, bf16[4,8,32,128]{3,2,1,0:T(8,128)(2,1)S(1)}, u32[]{:S(2)}, u32[]{:S(2)}) collective-permute-start(bf16[4,8,32,128]{3,2,1,0:T(8,128)(2,1)S(1)} %pad_maximum_fusion), channel_id=1, source_target_pairs={{0,2},{2,0},{4,6},{6,4},{8,10},{10,8},{12,14},{14,12},{1,3},{3,1},... | collective-permute-start | bytes 786440 | tf_op jit(solution)/shard_map/ppermute | solution.py:353
  22.4 4.6 %all-to-all-start.7 = ((bf16[8,96,1024]{2,1,0:T(8,128)(2,1)}), bf16[8,96,1024]{2,1,0:T(8,128)(2,1)S(1)}, u32[]{:S(2)}, u32[]{:S(2)}) async-start(bf16[8,96,1024]{2,1,0:T(8,128)(2,1)} %pack_live_tokens.3), calls=%async_computation.7 | async-start | bytes 3145728 | tf_op jit(solution)/shard_map/all_to_all | solution.py:405
  27.0 0.1 select_reduce_fusion.3
  27.1 0.1 fusion.55
  27.3 0.3 select_reduce_fusion.2
  27.6 1.0 select_reduce_fusion
  28.6 2.4 %slice_bitcast_fusion.refs_7_ = bf16[4,1024,128]{2,1,0:T(8,128)(2,1)} fusion(bf16[1024,4,256]{2,0,1:T(8,128)(2,1)} %copy.29), kind=kLoop, calls=%fused_computation.34 | loop fusion | bytes 2097152 | tf_op jit(solution)/shard_map/transpose | solution.py:481
  31.0 3.3 %convolution_convert_fusion.1 = bf16[4,4,8,8,1024]{4,3,2,1,0:T(8,128)(2,1)} fusion(bf16[1024,4,256]{2,0,1:T(8,128)(2,1)} %copy.29, bf16[4,8,32,128]{3,2,1,0:T(8,128)(2,1)S(1)} %pad_maximum_fusion), kind=kOutput, calls=%fused_computation.33 | convolution fusion | flops 269484032 | bytes 3407872 | tf_op jit(solution)/shard_map/qrhgd,phd->hqrgp/dot_general | solution.py:474
  34.2 1.3 fusion.77
  35.5 0.7 fusion.75
  36.7 0.1 concatenate.11.meta_ref
  36.8 3.2 %convolution_convert_fusion = bf16[4,4,8,8,1024]{4,3,2,1,0:T(8,128)(2,1)} fusion(bf16[1024,4,256]{2,0,1:T(8,128)(2,1)} %copy.29, bf16[4,8,32,128]{3,2,1,0:T(8,128)(2,1)S(1)} %collective-permute-done.4), kind=kOutput, calls=%fused_computation.32 | convolution fusion | flops 269484032 | bytes 3407872 | tf_op jit(solution)/shard_map/qrhgd,phd->hqrgp/dot_general | solution.py:474
  40.1 23.1 %all-to-all-done.7 = bf16[8,96,1024]{2,1,0:T(8,128)(2,1)S(1)} async-done(((bf16[8,96,1024]{2,1,0:T(8,128)(2,1)}), bf16[8,96,1024]{2,1,0:T(8,128)(2,1)S(1)}, u32[]{:S(2)}, u32[]{:S(2)}) %all-to-all-start.7) | async-done | bytes 1572896 | tf_op jit(solution)/shard_map/all_to_all | solution.py:405
  63.8 1.8 %conditional.2 = (bf16[256,1024]{1,0:T(8,128)(2,1)}, bf16[256,1024]{1,0:T(8,128)(2,1)}) conditional(s32[]{:T(128)} %bitcast.23, () %tuple.25, (s32[2]{0:T(128)S(1)}, s32[256]{0:T(256)S(1)}, s32[256]{0:T(256)S(1)}, bf16[256,8192]{1,0:T(8,128)(2,1)}) %tuple.53), branch_computations={%region_12.13_spmd, %region_13.14_spmd} | conditional | flops 134217728 | bytes 70254648 | solution.py:464
  63.8 0.9 broadcast.408
  64.7 0.8 broadcast.408.clone
  65.6 1.0 collective-permute-done.5.refs_1_
  66.6 2.2 %copy-done.1 = bf16[4,4,8,8,1024]{4,3,2,1,0:T(8,128)(2,1)S(1)} copy-done((bf16[4,4,8,8,1024]{4,3,2,1,0:T(8,128)(2,1)S(1)}, bf16[4,4,8,8,1024]{4,3,2,1,0:T(8,128)(2,1)}, u32[]{:S(2)}) %copy-start.1) | copy-done | bytes 2097176
  68.7 1.6 %copy-done.2 = bf16[4,4,8,8,1024]{4,3,2,1,0:T(8,128)(2,1)S(1)} copy-done((bf16[4,4,8,8,1024]{4,3,2,1,0:T(8,128)(2,1)S(1)}, bf16[4,4,8,8,1024]{4,3,2,1,0:T(8,128)(2,1)}, u32[]{:S(2)}) %copy-start.2) | copy-done | bytes 2097176
  70.3 6.6 %prompt_scores.1 = (bf16[8,32,384]{2,1,0:T(8,128)(2,1)}, bf16[8,32,256]{2,1,0:T(8,128)(2,1)}) custom-call(s32[651]{0:T(1024)S(1)} %concatenate.11.meta_ref, bf16[768,1024]{1,0:T(8,128)(2,1)S(1)} %bitcast.53, bf16[768,1024]{1,0:T(8,128)(2,1)S(1)} %collective-permute-done.5.refs_1_, bf16[256,1024]{1,0:T(8,128)(2,1)} %get-tuple-element.84.refs_2_, ...), custom_call_target="tpu_custom_call" | custom-call | tf_op jit(solution)/shard_map/prompt_scores/pallas_call | solution.py:508
  76.9 25.6 %conditional.3 = (bf16[8,32,384]{2,1,0:T(8,128)(2,1)}, bf16[8,32,256]{2,1,0:T(8,128)(2,1)S(1)}, f32[8,32,128]{2,1,0:T(8,128)S(1)}) conditional(s32[]{:T(128)} %bitcast.24, (bf16[8,32,384]{2,1,0:T(8,128)(2,1)}, s32[1,640]{1,0:T(1,128)S(1)}, s32[8]{0:T(128)S(1)}, bf16[8,32,128]{2,1,0:T(8,128)(2,1)S(1)}, ...), branch_computations={%region_14.17_spmd, %region_17.20_spmd} | conditional | flops 34047488 | bytes 31672474 | solution.py:576
  76.9 3.4 %all-to-all-start.1 = ((bf16[8,32,384]{2,1,0:T(8,128)(2,1)}), bf16[8,32,384]{2,1,0:T(8,128)(2,1)S(1)}, u32[]{:S(2)}, u32[]{:S(2)}) async-start(bf16[8,32,384]{2,1,0:T(8,128)(2,1)} %get-tuple-element.39), calls=%async_computation.1 | async-start | bytes 393216 | tf_op jit(solution)/shard_map/cond/branch_0_fun/all_to_all | solution.py:538
  80.4 3.0 %copy.33 = bf16[8,256,4,256]{3,1,2,0:T(8,128)(2,1)S(1)} copy(bf16[8,256,4,256]{3,2,1,0:T(4,128)(2,1)} %get-tuple-element.123) | data formatting | bytes 8388608 | tf_op jit(solution)/shard_map
  83.4 0.7 fusion.73
  84.2 1.1 copy-done.6
  85.3 0.1 broadcast_in_dim.162.refs_2_
  85.4 0.2 fusion.17
  85.6 0.1 broadcast_in_dim.163.refs_3_
  85.7 3.1 %all-to-all-done.1.refs_0_ = bf16[8,32,384]{2,1,0:T(8,128)(2,1)S(1)} async-done(((bf16[8,32,384]{2,1,0:T(8,128)(2,1)}), bf16[8,32,384]{2,1,0:T(8,128)(2,1)S(1)}, u32[]{:S(2)}, u32[]{:S(2)}) %all-to-all-start.1) | async-done | bytes 196640 | tf_op jit(solution)/shard_map/cond/branch_0_fun/all_to_all | solution.py:538
  88.8 1.7 %softmax_weights.2 = (bf16[8,32,384]{2,1,0:T(8,128)(2,1)}, f32[8,32,1]{2,1,0:T(8,128)S(1)}) custom-call(bf16[8,32,384]{2,1,0:T(8,128)(2,1)S(1)} %all-to-all-done.1.refs_0_, s32[1,384]{1,0:T(1,128)S(1)} %slice.22.refs_1_, f32[8,32,1]{2,1,0:T(8,128)S(1)} %broadcast_in_dim.162.refs_2_, f32[8,32,1]{2,1,0:T(8,128)S(1)} %broadcast_in_dim.163.refs_3_), custom_call_target="tpu_custom_call" | custom-call | tf_op jit(solution)/shard_map/cond/branch_0_fun/softmax_weights/pallas_call | solution.py:552
  90.5 4.0 %all-to-all-start.2 = ((bf16[8,32,384]{2,1,0:T(8,128)(2,1)}), bf16[8,32,384]{2,1,0:T(8,128)(2,1)}, u32[]{:S(2)}, u32[]{:S(2)}) async-start(bf16[8,32,384]{2,1,0:T(8,128)(2,1)} %get-tuple-element.44), calls=%async_computation.2 | async-start | bytes 393216 | tf_op jit(solution)/shard_map/cond/branch_0_fun/all_to_all | solution.py:563
  94.5 0.1 reduce
  94.6 2.0 %fusion.13 = f32[8,32,128]{2,1,0:T(8,128)S(1)} fusion(bf16[8,256,4,256]{3,1,2,0:T(8,128)(2,1)} %copy-done.6, f32[8,4,8,256]{3,2,1,0:T(8,128)S(1)} %get-tuple-element.139, f32[8,4,8]{2,1,0:T(4,128)S(1)} %get-tuple-element.138, f32[8,32]{1,0:T(8,128)S(1)} %reduce), kind=kOutput, calls=%fused_computation.7 | convolution fusion | flops 16941056 | bytes 2492416 | tf_op jit(solution)/shard_map/cond/branch_0_fun/rhgt,rthd->rhgd/dot_general | solution.py:564
  96.7 5.7 %all-to-all-done.2 = bf16[8,32,384]{2,1,0:T(8,128)(2,1)} async-done(((bf16[8,32,384]{2,1,0:T(8,128)(2,1)}), bf16[8,32,384]{2,1,0:T(8,128)(2,1)}, u32[]{:S(2)}, u32[]{:S(2)}) %all-to-all-start.2) | async-done | bytes 196640 | tf_op jit(solution)/shard_map/cond/branch_0_fun/all_to_all | solution.py:563
  102.5 10.0 %weighted_values.1 = bf16[4,2,4,64,128]{4,3,2,1,0:T(8,128)(2,1)} custom-call(s32[651]{0:T(1024)} %copy-done.5, bf16[768,1024]{1,0:T(8,128)(2,1)} %bitcast.54, bf16[768,1024]{1,0:T(8,128)(2,1)} %copy-done.3, bf16[256,1024]{1,0:T(8,128)(2,1)} %get-tuple-element.84.refs_2_, bf16[256,1024]{1,0:T(8,128)(2,1)} %get-tuple-element.85.refs_3_, ...), custom_call_target="tpu_custom_call" | custom-call | tf_op jit(solution)/shard_map/weighted_values/pallas_call | solution.py:579
  112.6 3.5 %all-to-all-start.8 = ((bf16[4,2,4,64,128]{4,3,2,1,0:T(8,128)(2,1)}), bf16[4,2,4,64,128]{4,3,2,1,0:T(8,128)(2,1)S(1)}, u32[]{:S(2)}, u32[]{:S(2)}) async-start(bf16[4,2,4,64,128]{4,3,2,1,0:T(8,128)(2,1)} %weighted_values.1), calls=%async_computation.8 | async-start | bytes 1048576 | tf_op jit(solution)/shard_map/all_to_all | solution.py:602
  116.1 6.5 %all-to-all-done.8.parts_ref = bf16[4,2,4,64,128]{4,3,2,1,0:T(8,128)(2,1)S(1)} async-done(((bf16[4,2,4,64,128]{4,3,2,1,0:T(8,128)(2,1)}), bf16[4,2,4,64,128]{4,3,2,1,0:T(8,128)(2,1)S(1)}, u32[]{:S(2)}, u32[]{:S(2)}) %all-to-all-start.8) | async-done | bytes 524320 | tf_op jit(solution)/shard_map/all_to_all | solution.py:602
  122.6 0.1 half_pool_sum.1
  122.7 0.5 collective-permute-start.6
  123.2 6.4 %collective-permute-done.6.got_ref = bf16[2,4,64,128]{3,2,1,0:T(8,128)(2,1)S(1)} collective-permute-done((bf16[2,4,64,128]{3,2,1,0:T(8,128)(2,1)S(1)}, bf16[2,4,64,128]{3,2,1,0:T(8,128)(2,1)S(1)}, u32[]{:S(2)}, u32[]{:S(2)}) %collective-permute-start.6) | collective-permute-done | bytes 131104 | tf_op jit(solution)/shard_map/ppermute | solution.py:353
  129.6 1.4 collective-permute-start.7
  131.1 1.8 %collective-permute-start.8 = (bf16[16,4096]{1,0:T(8,128)(2,1)S(1)}, bf16[16,4096]{1,0:T(8,128)(2,1)S(1)}, u32[]{:S(2)}, u32[]{:S(2)}) collective-permute-start(bf16[16,4096]{1,0:T(8,128)(2,1)S(1)} %attended_sum.1), channel_id=1, source_target_pairs={{0,4},{2,6},{4,0},{6,2},{8,12},{10,14},{12,8},{14,10},{1,5},{3,7},... | collective-permute-start | bytes 393224 | tf_op jit(solution)/shard_map/ppermute | solution.py:353
  132.8 0.4 collective-permute-start.9
  133.2 1.5 %collective-permute-done.7 = bf16[16,4096]{1,0:T(8,128)(2,1)S(1)} collective-permute-done((bf16[16,4096]{1,0:T(8,128)(2,1)S(1)}, bf16[16,4096]{1,0:T(8,128)(2,1)S(1)}, u32[]{:S(2)}, u32[]{:S(2)}) %collective-permute-start.7) | collective-permute-done | bytes 131104 | tf_op jit(solution)/shard_map/ppermute | solution.py:353
  134.7 1.4 collective-permute-done.8
  136.0 2.7 %collective-permute-done.9 = bf16[16,4096]{1,0:T(8,128)(2,1)S(1)} collective-permute-done((bf16[16,4096]{1,0:T(8,128)(2,1)S(1)}, bf16[16,4096]{1,0:T(8,128)(2,1)S(1)}, u32[]{:S(2)}, u32[]{:S(2)}) %collective-permute-start.9) | collective-permute-done | bytes 131104 | tf_op jit(solution)/shard_map/ppermute | solution.py:353
  138.7 4.9 %fusion.43 = f32[64,1024]{1,0:T(8,128)S(1)} fusion(bf16[4096,1024]{1,0:T(8,128)(2,1)} %param.21, bf16[16,4096]{1,0:T(8,128)(2,1)S(1)} %collective-permute-done.9, bf16[16,4096]{1,0:T(8,128)(2,1)S(1)} %collective-permute-done.8, bf16[16,4096]{1,0:T(8,128)(2,1)S(1)} %collective-permute-done.7, bf16[16,4096]{1,0:T(8,128)(2,1)S(1)} %attended_sum.1), kind=kOutput, calls=%fused_computation.36 | convolution fusion | flops 538968064 | bytes 9175040 | tf_op jit(solution)/shard_map/dot_general | solution.py:625
  143.8 1.3 collective-permute-done.10.got_ref
  145.1 0.6 order_rows.1
  (48 shorter events, 0.7 us)
Async XLA Ops:
  0.0 14.4 %copy-start.8 = (bf16[8,32,128]{2,1,0:T(8,128)(2,1)S(1)}, bf16[8,32,128]{2,1,0:T(8,128)(2,1)}, u32[]{:S(2)}) copy-start(bf16[8,32,128]{2,1,0:T(8,128)(2,1)} %param.18) | copy-start | bytes 196612
  0.0 14.5 %copy-start.9 = (s32[256,1]{0,1:T(1,128)S(1)}, s32[256,1]{0,1:T(1,128)}, u32[]{:S(2)}) copy-start(s32[256,1]{0,1:T(1,128)} %param.15) | copy-start | bytes 3076
  0.0 14.4 %copy-start.10 = (s32[256]{0:T(256)S(1)}, s32[256]{0:T(256)}, u32[]{:S(2)}) copy-start(s32[256]{0:T(256)} %fill_ref.1) | copy-start | bytes 3076
  0.0 19.3 %copy-start.7 = (bf16[1024,4,256]{2,1,0:T(4,128)(2,1)S(1)}, bf16[1024,4,256]{2,1,0:T(4,128)(2,1)}, u32[]{:S(2)}) copy-start(bf16[1024,4,256]{2,1,0:T(4,128)(2,1)} %param.14) | copy-start | bytes 6291460
  0.0 8.0 %collective-permute-start.1 = (bf16[8,32,128]{2,1,0:T(8,128)(2,1)}, bf16[8,32,128]{2,1,0:T(8,128)(2,1)S(1)}, u32[]{:S(2)}, u32[]{:S(2)}) collective-permute-start(bf16[8,32,128]{2,1,0:T(8,128)(2,1)} %param.18), channel_id=1, source_target_pairs={{0,8},{2,10},{4,12},{6,14},{8,0},{10,2},{12,4},{14,6},{1,9},{3,11}... | collective-permute-start | bytes 196616 | tf_op jit(solution)/shard_map/ppermute | solution.py:353
  8.8 5.5 %collective-permute-start.2 = (bf16[2,8,32,128]{3,2,1,0:T(8,128)(2,1)S(1)}, bf16[2,8,32,128]{3,2,1,0:T(8,128)(2,1)S(1)}, u32[]{:S(2)}, u32[]{:S(2)}) collective-permute-start(bf16[2,8,32,128]{3,2,1,0:T(8,128)(2,1)S(1)} %pad_maximum_fusion.1), channel_id=1, source_target_pairs={{0,4},{2,6},{4,0},{6,2},{8,12},{10,14},{12,8},{14,10},{1,5},{3,7},... | collective-permute-start | bytes 393224 | tf_op jit(solution)/shard_map/ppermute | solution.py:353
  14.4 12.6 %copy-start.12 = (s32[256]{0:T(256)S(1)}, s32[256]{0:T(256)}, u32[]{:S(2)}) copy-start(s32[256]{0:T(256)} %param.16) | copy-start | bytes 3076
  17.8 16.4 %collective-permute-start.3 = (s32[2]{0:T(128)S(1)}, s32[2]{0:T(128)S(1)}, u32[]{:S(2)}, u32[]{:S(2)}) collective-permute-start(s32[2]{0:T(128)S(1)} %pad_add_fusion.1), channel_id=1, source_target_pairs={{0,16},{16,0},{1,17},{17,1},{2,18},{18,2},{3,19},{19,3},{4,20},{20... | collective-permute-start | bytes 32 | tf_op jit(solution)/shard_map/ppermute | solution.py:451
  20.9 15.9 %collective-permute-start.4 = (bf16[4,8,32,128]{3,2,1,0:T(8,128)(2,1)S(1)}, bf16[4,8,32,128]{3,2,1,0:T(8,128)(2,1)S(1)}, u32[]{:S(2)}, u32[]{:S(2)}) collective-permute-start(bf16[4,8,32,128]{3,2,1,0:T(8,128)(2,1)S(1)} %pad_maximum_fusion), channel_id=1, source_target_pairs={{0,2},{2,0},{4,6},{6,4},{8,10},{10,8},{12,14},{14,12},{1,3},{3,1},... | collective-permute-start | bytes 786440 | tf_op jit(solution)/shard_map/ppermute | solution.py:353
  22.4 40.7 %all-to-all-start.7 = ((bf16[8,96,1024]{2,1,0:T(8,128)(2,1)}), bf16[8,96,1024]{2,1,0:T(8,128)(2,1)S(1)}, u32[]{:S(2)}, u32[]{:S(2)}) async-start(bf16[8,96,1024]{2,1,0:T(8,128)(2,1)} %pack_live_tokens.3), calls=%async_computation.7 | async-start | bytes 3145728 | tf_op jit(solution)/shard_map/all_to_all | solution.py:405
  28.6 38.0 %copy-start.4 = (s32[5120]{0:T(1024)}, s32[5120]{0:T(1024)S(1)}, u32[]{:S(2)}) copy-start(s32[5120]{0:T(1024)S(1)} %broadcast_add_fusion) | copy-start | bytes 61444
  36.8 29.8 %copy-start.5 = (s32[651]{0:T(1024)}, s32[651]{0:T(1024)S(1)}, u32[]{:S(2)}) copy-start(s32[651]{0:T(1024)S(1)} %concatenate.11.meta_ref) | copy-start | bytes 7816
  63.1 13.8 %copy-start = (bf16[8,96,1024]{2,1,0:T(8,128)(2,1)}, bf16[8,96,1024]{2,1,0:T(8,128)(2,1)S(1)}, u32[]{:S(2)}) copy-start(bf16[8,96,1024]{2,1,0:T(8,128)(2,1)S(1)} %all-to-all-done.7) | copy-start | bytes 4718596
  63.1 3.4 %collective-permute-start.5 = (bf16[768,1024]{1,0:T(8,128)(2,1)S(1)}, bf16[768,1024]{1,0:T(8,128)(2,1)S(1)}, u32[]{:S(2)}, u32[]{:S(2)}) collective-permute-start(bf16[768,1024]{1,0:T(8,128)(2,1)S(1)} %bitcast.52), channel_id=1, source_target_pairs={{0,1},{1,0},{2,3},{3,2},{4,5},{5,4},{6,7},{7,6},{8,9},{9,8},{10,11... | collective-permute-start | bytes 4718600 | tf_op jit(solution)/shard_map/ppermute | solution.py:486
  66.5 10.3 %copy-start.3 = (bf16[768,1024]{1,0:T(8,128)(2,1)}, bf16[768,1024]{1,0:T(8,128)(2,1)S(1)}, u32[]{:S(2)}) copy-start(bf16[768,1024]{1,0:T(8,128)(2,1)S(1)} %collective-permute-done.5.refs_1_) | copy-start | bytes 4718596
  66.6 2.2 %copy-start.1 = (bf16[4,4,8,8,1024]{4,3,2,1,0:T(8,128)(2,1)S(1)}, bf16[4,4,8,8,1024]{4,3,2,1,0:T(8,128)(2,1)}, u32[]{:S(2)}) copy-start(bf16[4,4,8,8,1024]{4,3,2,1,0:T(8,128)(2,1)} %convolution_convert_fusion.1) | copy-start | bytes 6291460
  68.7 1.6 %copy-start.2 = (bf16[4,4,8,8,1024]{4,3,2,1,0:T(8,128)(2,1)S(1)}, bf16[4,4,8,8,1024]{4,3,2,1,0:T(8,128)(2,1)}, u32[]{:S(2)}) copy-start(bf16[4,4,8,8,1024]{4,3,2,1,0:T(8,128)(2,1)} %convolution_convert_fusion) | copy-start | bytes 6291460
  70.3 6.6 %copy-start.11 = (s32[8]{0:T(128)S(1)}, s32[8]{0:T(128)}, u32[]{:S(2)}) copy-start(s32[8]{0:T(128)} %param.20) | copy-start | bytes 100
  76.9 11.9 %all-to-all-start.1 = ((bf16[8,32,384]{2,1,0:T(8,128)(2,1)}), bf16[8,32,384]{2,1,0:T(8,128)(2,1)S(1)}, u32[]{:S(2)}, u32[]{:S(2)}) async-start(bf16[8,32,384]{2,1,0:T(8,128)(2,1)} %get-tuple-element.39), calls=%async_computation.1 | async-start | bytes 393216 | tf_op jit(solution)/shard_map/cond/branch_0_fun/all_to_all | solution.py:538
  83.3 1.9 %copy-start.6 = (bf16[8,256,4,256]{3,1,2,0:T(8,128)(2,1)}, bf16[8,256,4,256]{3,1,2,0:T(8,128)(2,1)S(1)}, u32[]{:S(2)}) copy-start(bf16[8,256,4,256]{3,1,2,0:T(8,128)(2,1)S(1)} %copy.33) | copy-start | bytes 12582916 | tf_op jit(solution)/shard_map/cond
  90.5 11.8 %all-to-all-start.2 = ((bf16[8,32,384]{2,1,0:T(8,128)(2,1)}), bf16[8,32,384]{2,1,0:T(8,128)(2,1)}, u32[]{:S(2)}, u32[]{:S(2)}) async-start(bf16[8,32,384]{2,1,0:T(8,128)(2,1)} %get-tuple-element.44), calls=%async_computation.2 | async-start | bytes 393216 | tf_op jit(solution)/shard_map/cond/branch_0_fun/all_to_all | solution.py:563
  112.6 10.0 %all-to-all-start.8 = ((bf16[4,2,4,64,128]{4,3,2,1,0:T(8,128)(2,1)}), bf16[4,2,4,64,128]{4,3,2,1,0:T(8,128)(2,1)S(1)}, u32[]{:S(2)}, u32[]{:S(2)}) async-start(bf16[4,2,4,64,128]{4,3,2,1,0:T(8,128)(2,1)} %weighted_values.1), calls=%async_computation.8 | async-start | bytes 1048576 | tf_op jit(solution)/shard_map/all_to_all | solution.py:602
  122.7 6.9 %collective-permute-start.6 = (bf16[2,4,64,128]{3,2,1,0:T(8,128)(2,1)S(1)}, bf16[2,4,64,128]{3,2,1,0:T(8,128)(2,1)S(1)}, u32[]{:S(2)}, u32[]{:S(2)}) collective-permute-start(bf16[2,4,64,128]{3,2,1,0:T(8,128)(2,1)S(1)} %get-tuple-element.96), channel_id=1, source_target_pairs={{0,8},{2,10},{4,12},{6,14},{8,0},{10,2},{12,4},{14,6},{1,9},{3,11}... | collective-permute-start | bytes 393224 | tf_op jit(solution)/shard_map/ppermute | solution.py:353
  129.6 5.0 %collective-permute-start.7 = (bf16[16,4096]{1,0:T(8,128)(2,1)S(1)}, bf16[16,4096]{1,0:T(8,128)(2,1)S(1)}, u32[]{:S(2)}, u32[]{:S(2)}) collective-permute-start(bf16[16,4096]{1,0:T(8,128)(2,1)S(1)} %attended_sum.1), channel_id=1, source_target_pairs={{0,2},{2,0},{4,6},{6,4},{8,10},{10,8},{12,14},{14,12},{1,3},{3,1},... | collective-permute-start | bytes 393224 | tf_op jit(solution)/shard_map/ppermute | solution.py:353
  131.1 5.0 %collective-permute-start.8 = (bf16[16,4096]{1,0:T(8,128)(2,1)S(1)}, bf16[16,4096]{1,0:T(8,128)(2,1)S(1)}, u32[]{:S(2)}, u32[]{:S(2)}) collective-permute-start(bf16[16,4096]{1,0:T(8,128)(2,1)S(1)} %attended_sum.1), channel_id=1, source_target_pairs={{0,4},{2,6},{4,0},{6,2},{8,12},{10,14},{12,8},{14,10},{1,5},{3,7},... | collective-permute-start | bytes 393224 | tf_op jit(solution)/shard_map/ppermute | solution.py:353
  132.8 5.9 %collective-permute-start.9 = (bf16[16,4096]{1,0:T(8,128)(2,1)S(1)}, bf16[16,4096]{1,0:T(8,128)(2,1)S(1)}, u32[]{:S(2)}, u32[]{:S(2)}) collective-permute-start(bf16[16,4096]{1,0:T(8,128)(2,1)S(1)} %attended_sum.1), channel_id=1, source_target_pairs={{0,6},{2,4},{4,2},{6,0},{8,14},{10,12},{12,10},{14,8},{1,7},{3,5},... | collective-permute-start | bytes 393224 | tf_op jit(solution)/shard_map/ppermute | solution.py:353
  143.7 1.4 collective-permute-start.10

commit v13 on v12

--- a/solution.py
+++ b/solution.py
@@ -117,10 +117,22 @@
     ]
 
 
-def widen_rest(core, over, n, refs, more, wide, sem):
+def load_tokens(n, core, over, x_refs, held, more, wide, sem, others):
+    main = span_copies(x_refs[:2], held, sem)
+    for pair in main:
+        for copy in pair:
+            copy.start()
+    for copy in others:
+        copy.start()
+    for i, pair in enumerate(main):
+        for copy in pair:
+            copy.wait()
+        parts = [held.at[0], held.at[1]]
+        widen(core, n, parts, wide, 0, i * n // len(main), (i + 1) * n // len(main))
+
     @pl.when(over != 0)
     def _():
-        rest = span_copies(refs, more, sem)
+        rest = span_copies(x_refs[2:], more, sem)
         for pair in rest:
             for copy in pair:
                 copy.start()
@@ -140,9 +152,26 @@
     return tile[: count * BLK, :]
 
 
+def key_kernel(query_ref, weight_ref, out_ref):
+    group = out_ref.shape[1] // query_ref.shape[0]
+    hd = query_ref.shape[2]
+    h = pl.program_id(0)
+    for i in range(query_ref.shape[1] // group):
+
+        @pl.when(h == i)
+        def _(i=i):
+            query = query_ref[:, i * group : (i + 1) * group, :].astype(jnp.float32)
+            out_ref[0] = lax.dot_general(
+                query.reshape(-1, hd).astype(jnp.bfloat16),
+                weight_ref[0, :, :hd],
+                (((1,), (1,)), ((), ())),
+                preferred_element_type=jnp.float32,
+            ).astype(out_ref.dtype)
+
+
 def score_kernel(n, rows, meta_ref, *refs):
     x_refs, keyed_refs, (row_ref, near_ref, rest_ref) = refs[:4], refs[4:6], refs[6:9]
-    more, wide, tile, keyed, sem, keyed_sem = refs[9:]
+    held, more, wide, tile, keyed, sem, keyed_sem = refs[9:]
     step = pl.program_id(0)
     part = wide.shape[1]
     near = near_ref.shape[2]
@@ -165,12 +194,10 @@
 
     @pl.when(step == 0)
     def _():
-        for i in range(2):
-            for copy in load(i):
-                copy.start()
-        core = meta_ref[at_size + n + 1]
-        widen(core, n, x_refs[:2], wide, 0, 0, n)
-        widen_rest(core, meta_ref[at_size + n + 2], n, x_refs[2:], more, wide, sem)
+        load_tokens(
+            n, meta_ref[at_size + n + 1], meta_ref[at_size + n + 2], x_refs, held, more, wide, sem,
+            load(0) + load(1),
+        )
 
     for i in range(2):
 
@@ -235,11 +262,17 @@
 
 
 def value_kernel(n, rows, meta_ref, *refs):
-    x_refs, (near_ref, rest_ref, row_ref, value_ref, out_ref) = refs[:4], refs[4:9]
+    x_refs, (near_ref, rest_ref, row_ref, weight_ref, out_ref) = refs[:4], refs[4:9]
     held, more, wide, tile, values, acc, mixed, sem, value_sem = refs[9:]
     q = pl.program_id(0)
     kvh = values.shape[0]
-    load_values = pltpu.make_async_copy(value_ref, values, value_sem)
+    hd = values.shape[2]
+    load_values = [
+        pltpu.make_async_copy(
+            weight_ref.at[h, :, pl.ds(hd, hd)], values.at[h], value_sem.at[h]
+        )
+        for h in range(kvh)
+    ]
     _, heads, near = near_ref.shape
     lanes = near + rest_ref.shape[2]
     per = rows * heads // kvh
@@ -249,18 +282,10 @@
 
     @pl.when(q == 0)
     def _():
-        core = meta_ref[at_size + n + 1]
-        main = span_copies(x_refs[:2], held, sem)
-        for pair in main:
-            for copy in pair:
-                copy.start()
-        load_values.start()
-        for i, pair in enumerate(main):
-            for copy in pair:
-                copy.wait()
-            parts = [held.at[0], held.at[1]]
-            widen(core, n, parts, wide, 0, i * n // len(main), (i + 1) * n // len(main))
-        widen_rest(core, meta_ref[at_size + n + 2], n, x_refs[2:], more, wide, sem)
+        load_tokens(
+            n, meta_ref[at_size + n + 1], meta_ref[at_size + n + 2], x_refs, held, more, wide, sem,
+            load_values,
+        )
 
     def one(t):
         here = slice(cuts[t], cuts[t + 1])
@@ -294,7 +319,8 @@
 
     @pl.when(q == n - 1)
     def _():
-        load_values.wait()
+        for load in load_values:
+            load.wait()
         for h in range(kvh):
             done = jnp.dot(mixed[h], values[h], preferred_element_type=jnp.float32)
             done = done.reshape(2, n // 2, per, done.shape[1]).astype(out_ref.dtype)
@@ -398,10 +424,13 @@
     pack_fill, pack_dest = block_fill, block_dest[:, 0]
     packed = pack(x_prompt, pack_fill, pack_dest, at, n, 0, size)
     dest = pack_dest
-    even = from_rest(jnp.stack([queries, with_partner(queries, n // 2, n)]), n)
-    packed, even, dest, block_row, block_fill, kv_weight = lax.optimization_barrier(
-        (packed, even, dest, block_row, block_fill, kv_weight)
-    )
+    far = with_partner(queries, n // 2, n)
+    packed, far, dest, block_row, block_fill, kv_weight = lax.optimization_barrier(
+        (packed, far, dest, block_row, block_fill, kv_weight)
+    )
+    kv_weight = kv_weight.transpose(1, 0, 2)
+    even = from_rest(jnp.stack([queries, far]), n)
+    packed, even = lax.optimization_barrier((packed, even))
     mine = lax.all_to_all(packed, "pool", 0, 0, tiled=True).reshape(n * size, part)
 
     index = jnp.arange(n * blocks, dtype=jnp.int32)
@@ -466,22 +495,27 @@
         [group_rows, list_rows, jnp.stack([me, core, over.astype(jnp.int32)])]
     )
 
-    keys = kv_weight[:, :, :hd]
-
     def through_keys(held):
-        held = held.reshape(n // 2, rows, kvh, group, hd)
-        return (
-            jnp.einsum("qrhgd,phd->hqrgp", held, keys, preferred_element_type=jnp.float32)
-            .astype(jnp.bfloat16)
-            .reshape(kvh, n // 2 * per, part)
-        )
+        held = held.reshape(n // 2 * rows, heads, hd)
+        return pl.pallas_call(
+            key_kernel,
+            grid=(kvh,),
+            in_specs=[
+                pl.BlockSpec(held.shape, lambda h: (0, 0, 0)),
+                pl.BlockSpec((1, part, 2 * hd), lambda h: (h, 0, 0)),
+            ],
+            out_specs=pl.BlockSpec((1, n // 2 * per, part), lambda h: (h, 0, 0)),
+            out_shape=jax.ShapeDtypeStruct((kvh, n // 2 * per, part), jnp.bfloat16),
+            compiler_params=pltpu.CompilerParams(vmem_limit_bytes=16 * MIB),
+            cost_estimate=pl.CostEstimate(flops=0, bytes_accessed=1024, transcendentals=0),
+            name="key_projection",
+        )(held, kv_weight)
 
     keyed_even = through_keys(even)
     keyed_odd = through_keys(with_partner(even, 1, n))
-    values = kv_weight[:, :, hd:].transpose(1, 0, 2)
-
-    mine, meta, rowof, keyed_even, keyed_odd, values = lax.optimization_barrier(
-        (mine, meta, rowof, keyed_even, keyed_odd, values)
+
+    mine, meta, rowof, keyed_even, keyed_odd = lax.optimization_barrier(
+        (mine, meta, rowof, keyed_even, keyed_odd)
     )
     other = lax.ppermute(mine, "tp", swap)
 
@@ -496,6 +530,7 @@
     in_vmem = pl.BlockSpec(memory_space=pltpu.VMEM)
     x_parts = (mine, other, more_mine, more_other)
     x_scratch = [
+        pltpu.VMEM((ntp, n * size, part), jnp.bfloat16),
         pltpu.VMEM((ntp, n * extra, part), jnp.bfloat16),
         pltpu.VMEM((n * tokens, part), jnp.float32),
         pltpu.VMEM((tile_cuts(lanes)[1], part), jnp.bfloat16),
@@ -511,8 +546,7 @@
             num_scalar_prefetch=1,
             grid=(n,),
             in_specs=[
-                *[in_vmem] * 2,
-                *[in_hbm] * 4,
+                *[in_hbm] * 6,
                 pl.BlockSpec((1, 1, lanes), lambda i, m: (owner(i, m), 0, 0)),
             ],
             out_specs=[
@@ -527,7 +561,7 @@
             ],
         ),
         out_shape=slot_shapes,
-        compiler_params=pltpu.CompilerParams(vmem_limit_bytes=20 * MIB),
+        compiler_params=pltpu.CompilerParams(vmem_limit_bytes=24 * MIB),
         name="prompt_scores",
     )(meta, *x_parts, keyed_even, keyed_odd, rowof)
 
@@ -584,19 +618,18 @@
             in_specs=[*[in_hbm] * 4, *slot_specs, row_spec, in_hbm],
             out_specs=pl.BlockSpec((n // 2, 2, kvh, per, hd), lambda q, m: (0, 0, 0, 0, 0)),
             scratch_shapes=[
-                pltpu.VMEM((ntp, n * size, part), jnp.bfloat16),
                 *x_scratch,
                 pltpu.VMEM((kvh, part, hd), jnp.bfloat16),
                 pltpu.VMEM((kvh * per, part), jnp.float32),
                 pltpu.VMEM((kvh, n * per, part), jnp.bfloat16),
                 pltpu.SemaphoreType.DMA((ntp, 4)),
-                pltpu.SemaphoreType.DMA,
+                pltpu.SemaphoreType.DMA((kvh,)),
             ],
         ),
         out_shape=jax.ShapeDtypeStruct((n // 2, 2, kvh, per, hd), jnp.bfloat16),
         compiler_params=pltpu.CompilerParams(vmem_limit_bytes=56 * MIB),
         name="weighted_values",
-    )(meta, *x_parts, weight_near, weight_rest, rowof, values)
+    )(meta, *x_parts, weight_near, weight_rest, rowof, kv_weight)
 
     halves = [list(range(n // 2)), list(range(n // 2, n))]
     term_parts = lax.all_to_all(

time: 147 us -> 138 us (0.939)
  matrix products: 14.2 us -> 7.7 us
  waiting for transfers between devices: 56.3 us -> 51 us
  Pallas kernels: 23.9 us -> 27.8 us
  local copies, waits for them, and re-layouts: 14.9 us -> 13.1 us
    all_to_all x1, waiting for transfers between devices: 23.1 us -> 12.4 us  [local(): lax.all_to_all(packed, 'pool', 0, 0, tiled=True).reshape(n * size, part)]
    dot_general x2 -> x0, matrix products: 6.52 us -> none  [through_keys(): jnp.einsum('qrhgd,phd->hqrgp', held, keys, preferred_element_type=jnp.flo...]
    ppermute x7, waiting for transfers between devices: 15.7 us -> 20.6 us  [with_partner(): return lax.ppermute(x, 'pool', [(i, i ^ k) for i in range(n)])]
    pallas_call x0 -> x2, Pallas kernels: none -> 2.56 us  [through_keys(): pl.pallas_call(key_kernel, grid=(kvh,), in_specs=[pl.BlockSpec(held.shape...]
    transpose x1 -> x0, local copies, waits for them, and re-layouts: 2.37 us -> none  [local(): values = kv_weight[:, :, hd:].transpose(1, 0, 2)]
  transfers between devices with their start and end apart: 14 -> 14, of which waited for: 11 -> 12; matrix products, arithmetic and copies ran while one was open for 15% -> 12% of each run, Pallas kernels for 3% -> 6%
where the time goes in v13:
time: 138 us; the launch traced here: 137 us
  waiting for transfers between devices  51 us (37%)
  starting transfers between devices  28.8 us (21%)
  Pallas kernels  27.8 us (20%)
  local copies, waits for them, and re-layouts  13.1 us (9%)
  matrix products  7.7 us (6%)
  other arithmetic  6.6 us (5%)
  between operations  1.63 us (1%)
    ppermute x7, waiting for transfers between devices, with_partner(): return lax.ppermute(x, 'pool', [(i, i ^ k) for i in range(n)])  20.6 us
    all_to_all x1, waiting for transfers between devices, local(): lax.all_to_all(packed, 'pool', 0, 0, tiled=True).reshape(n * size, part)  12.4 us
    ppermute x7, starting transfers between devices, with_partner(): return lax.ppermute(x, 'pool', [(i, i ^ k) for i in range(n)])  11.8 us
    pallas_call x1, Pallas kernels, local(): pl.pallas_call(functools.partial(value_kernel, n, rows), grid_spec=pltpu....  10.3 us
    pallas_call x1, Pallas kernels, local(): pl.pallas_call(functools.partial(score_kernel, n, rows), grid_spec=pltpu....  7.41 us
    all_to_all x1, waiting for transfers between devices, local(): lax.all_to_all(terms, 'pool', 0, 0, axis_index_groups=halves, tiled=True)  6.53 us
    all_to_all x1, waiting for transfers between devices, exchange_weights(): weights = [lax.all_to_all(w, 'pool', 0, 0, tiled=True) for w in weights]  5.66 us
    pallas_call x1, Pallas kernels, pack(): pl.pallas_call(functools.partial(pack_kernel, base), grid_spec=pltpu.Pref...  4.99 us
  transfers between devices with their start and end apart: 14, of which 12 were waited for; matrix products, arithmetic and copies ran while one was open for 12% of the time, Pallas kernels for 6%

profile of v13, /device:TPU:0, one launch (start us, length us, event | category | flops | bytes accessed | tf_op | source)
XLA Modules:
  0.0 136.8 jit_solution(11555712970174598994)
XLA Ops:
  0.0 4.0 %collective-permute-start.1 = (bf16[8,32,128]{2,1,0:T(8,128)(2,1)}, bf16[8,32,128]{2,1,0:T(8,128)(2,1)S(1)}, u32[]{:S(2)}, u32[]{:S(2)}) collective-permute-start(bf16[8,32,128]{2,1,0:T(8,128)(2,1)} %param.18), channel_id=1, source_target_pairs={{0,8},{2,10},{4,12},{6,14},{8,0},{10,2},{12,4},{14,6},{1,9},{3,11}... | collective-permute-start | bytes 196616 | tf_op jit(solution)/shard_map/ppermute | solution.py:379
  4.1 5.0 %pack_live_tokens.3 = bf16[8,96,1024]{2,1,0:T(8,128)(2,1)} custom-call(s32[2]{0:T(128)S(1)} %pad_add_fusion.at_ref, s32[256]{0:T(256)} %fill_ref.1, s32[256]{0:T(256)} %bitcast.51, bf16[256,8192]{1,0:T(8,128)(2,1)} %x_ref.1), custom_call_target="tpu_custom_call" | custom-call | flops 402653184 | bytes 67108864 | tf_op jit(solution)/shard_map/pack_live_tokens/pallas_call | solution.py:62
  9.2 1.6 %collective-permute-start.2 = (bf16[2,8,32,128]{3,2,1,0:T(8,128)(2,1)S(1)}, bf16[2,8,32,128]{3,2,1,0:T(8,128)(2,1)S(1)}, u32[]{:S(2)}, u32[]{:S(2)}) collective-permute-start(bf16[2,8,32,128]{3,2,1,0:T(8,128)(2,1)S(1)} %pad_maximum_fusion.1), channel_id=1, source_target_pairs={{0,4},{2,6},{4,0},{6,2},{8,12},{10,14},{12,8},{14,10},{1,5},{3,7},... | collective-permute-start | bytes 393224 | tf_op jit(solution)/shard_map/ppermute | solution.py:379
  10.8 3.4 %collective-permute-done.2 = bf16[2,8,32,128]{3,2,1,0:T(8,128)(2,1)S(1)} collective-permute-done((bf16[2,8,32,128]{3,2,1,0:T(8,128)(2,1)S(1)}, bf16[2,8,32,128]{3,2,1,0:T(8,128)(2,1)S(1)}, u32[]{:S(2)}, u32[]{:S(2)}) %collective-permute-start.2) | collective-permute-done | bytes 131104 | tf_op jit(solution)/shard_map/ppermute | solution.py:379
  14.2 4.5 %all-to-all-start.7 = ((bf16[8,96,1024]{2,1,0:T(8,128)(2,1)}), bf16[8,96,1024]{2,1,0:T(8,128)(2,1)}, u32[]{:S(2)}, u32[]{:S(2)}) async-start(bf16[8,96,1024]{2,1,0:T(8,128)(2,1)} %pack_live_tokens.3), calls=%async_computation.7 | async-start | bytes 3145728 | tf_op jit(solution)/shard_map/all_to_all | solution.py:434
  18.8 0.2 select_reduce_fusion.5
  19.0 0.1 reduce_sum.113
  19.2 0.1 fusion.69
  19.3 0.1 select_reduce_fusion.6
  19.5 0.7 reduce_max.37
  20.2 0.1 reduce_sum.119
  20.3 0.6 reduce_max.36
  21.0 1.3 pad_add_fusion.1
  22.3 1.5 %collective-permute-start.3 = (s32[2]{0:T(128)S(1)}, s32[2]{0:T(128)S(1)}, u32[]{:S(2)}, u32[]{:S(2)}) collective-permute-start(s32[2]{0:T(128)S(1)} %pad_add_fusion.1), channel_id=1, source_target_pairs={{0,16},{16,0},{1,17},{17,1},{2,18},{18,2},{3,19},{19,3},{4,20},{20... | collective-permute-start | bytes 32 | tf_op jit(solution)/shard_map/ppermute | solution.py:480
  23.8 1.9 %copy.28 = bf16[1024,4,256]{2,0,1:T(8,128)(2,1)S(1)} copy(bf16[1024,4,256]{2,1,0:T(4,128)(2,1)} %param.14) | data formatting | bytes 4194304 | tf_op jit(solution)/shard_map/optimization_barrier | solution.py:428
  25.7 0.1 select_reduce_fusion.3
  25.8 0.1 fusion.53
  25.9 0.3 select_reduce_fusion.2
  26.2 1.0 select_reduce_fusion
  27.3 2.1 %collective-permute-start.4 = (bf16[4,8,32,128]{3,2,1,0:T(8,128)(2,1)S(1)}, bf16[4,8,32,128]{3,2,1,0:T(8,128)(2,1)S(1)}, u32[]{:S(2)}, u32[]{:S(2)}) collective-permute-start(bf16[4,8,32,128]{3,2,1,0:T(8,128)(2,1)S(1)} %pad_maximum_fusion), channel_id=1, source_target_pairs={{0,2},{2,0},{4,6},{6,4},{8,10},{10,8},{12,14},{14,12},{1,3},{3,1},... | collective-permute-start | bytes 786440 | tf_op jit(solution)/shard_map/ppermute | solution.py:379
  29.3 1.3 fusion.75
  30.7 0.6 fusion.73
  31.9 0.1 concatenate.11.meta_ref
  31.9 1.3 key_projection.2.refs_4_
  33.2 1.3 copy-done.1
  34.6 5.3 %collective-permute-done.4 = bf16[4,8,32,128]{3,2,1,0:T(8,128)(2,1)S(1)} collective-permute-done((bf16[4,8,32,128]{3,2,1,0:T(8,128)(2,1)S(1)}, bf16[4,8,32,128]{3,2,1,0:T(8,128)(2,1)S(1)}, u32[]{:S(2)}, u32[]{:S(2)}) %collective-permute-start.4) | collective-permute-done | bytes 262176 | tf_op jit(solution)/shard_map/ppermute | solution.py:379
  39.9 1.3 key_projection.3.refs_5_
  41.2 1.3 copy-done.3
  42.5 12.4 %all-to-all-done.7 = bf16[8,96,1024]{2,1,0:T(8,128)(2,1)} async-done(((bf16[8,96,1024]{2,1,0:T(8,128)(2,1)}), bf16[8,96,1024]{2,1,0:T(8,128)(2,1)}, u32[]{:S(2)}, u32[]{:S(2)}) %all-to-all-start.7) | async-done | bytes 1572896 | tf_op jit(solution)/shard_map/all_to_all | solution.py:434
  55.7 1.7 %conditional.2 = (bf16[256,1024]{1,0:T(8,128)(2,1)}, bf16[256,1024]{1,0:T(8,128)(2,1)}) conditional(s32[]{:T(128)} %bitcast.18, () %tuple.27, (s32[2]{0:T(128)S(1)}, s32[256]{0:T(256)S(1)}, s32[256]{0:T(256)S(1)}, bf16[256,8192]{1,0:T(8,128)(2,1)}) %tuple.55), branch_computations={%region_12.13_spmd, %region_13.14_spmd} | conditional | flops 134217728 | bytes 70254648 | solution.py:493
  55.7 0.8 broadcast.408
  56.5 0.8 broadcast.408.clone
  57.4 1.3 collective-permute-done.5.refs_1_
  58.7 1.6 %copy-done.4 = bf16[4,256,1024]{2,1,0:T(8,128)(2,1)S(1)} copy-done((bf16[4,256,1024]{2,1,0:T(8,128)(2,1)S(1)}, bf16[4,256,1024]{2,1,0:T(8,128)(2,1)}, u32[]{:S(2)}) %copy-start.4) | copy-done | bytes 2097176
  60.3 7.4 %prompt_scores.1 = (bf16[8,32,384]{2,1,0:T(8,128)(2,1)}, bf16[8,32,256]{2,1,0:T(8,128)(2,1)}) custom-call(s32[651]{0:T(1024)S(1)} %concatenate.11.meta_ref, bf16[768,1024]{1,0:T(8,128)(2,1)} %bitcast.11.refs_0_, bf16[768,1024]{1,0:T(8,128)(2,1)} %collective-permute-done.5.refs_1_, bf16[256,1024]{1,0:T(8,128)(2,1)} %get-tuple-element.87.refs_2_, ...), custom_call_target="tpu_custom_call" | custom-call | tf_op jit(solution)/shard_map/prompt_scores/pallas_call | solution.py:543
  67.7 25.6 %conditional.3 = (bf16[8,32,384]{2,1,0:T(8,128)(2,1)}, bf16[8,32,256]{2,1,0:T(8,128)(2,1)S(1)}, f32[8,32,128]{2,1,0:T(8,128)S(1)}) conditional(s32[]{:T(128)} %bitcast.19, (bf16[8,32,384]{2,1,0:T(8,128)(2,1)}, s32[1,640]{1,0:T(1,128)S(1)}, s32[8]{0:T(128)S(1)}, bf16[8,32,128]{2,1,0:T(8,128)(2,1)S(1)}, ...), branch_computations={%region_14.17_spmd, %region_17.20_spmd} | conditional | flops 34047488 | bytes 31672474 | solution.py:610
  67.7 3.4 %all-to-all-start.1 = ((bf16[8,32,384]{2,1,0:T(8,128)(2,1)}), bf16[8,32,384]{2,1,0:T(8,128)(2,1)S(1)}, u32[]{:S(2)}, u32[]{:S(2)}) async-start(bf16[8,32,384]{2,1,0:T(8,128)(2,1)} %get-tuple-element.39), calls=%async_computation.1 | async-start | bytes 393216 | tf_op jit(solution)/shard_map/cond/branch_0_fun/all_to_all | solution.py:572
  71.2 3.0 %copy.25 = bf16[8,256,4,256]{3,1,2,0:T(8,128)(2,1)S(1)} copy(bf16[8,256,4,256]{3,2,1,0:T(4,128)(2,1)} %get-tuple-element.125) | data formatting | bytes 8388608 | tf_op jit(solution)/shard_map
  74.2 0.7 fusion.71
  75.0 1.1 copy-done.7
  76.1 0.1 broadcast_in_dim.162.refs_2_
  76.2 0.2 fusion.17
  76.4 0.1 broadcast_in_dim.163.refs_3_
  76.5 3.1 %all-to-all-done.1.refs_0_ = bf16[8,32,384]{2,1,0:T(8,128)(2,1)S(1)} async-done(((bf16[8,32,384]{2,1,0:T(8,128)(2,1)}), bf16[8,32,384]{2,1,0:T(8,128)(2,1)S(1)}, u32[]{:S(2)}, u32[]{:S(2)}) %all-to-all-start.1) | async-done | bytes 196640 | tf_op jit(solution)/shard_map/cond/branch_0_fun/all_to_all | solution.py:572
  79.6 1.7 %softmax_weights.2 = (bf16[8,32,384]{2,1,0:T(8,128)(2,1)}, f32[8,32,1]{2,1,0:T(8,128)S(1)}) custom-call(bf16[8,32,384]{2,1,0:T(8,128)(2,1)S(1)} %all-to-all-done.1.refs_0_, s32[1,384]{1,0:T(1,128)S(1)} %slice.18.refs_1_, f32[8,32,1]{2,1,0:T(8,128)S(1)} %broadcast_in_dim.162.refs_2_, f32[8,32,1]{2,1,0:T(8,128)S(1)} %broadcast_in_dim.163.refs_3_), custom_call_target="tpu_custom_call" | custom-call | tf_op jit(solution)/shard_map/cond/branch_0_fun/softmax_weights/pallas_call | solution.py:586
  81.3 4.0 %all-to-all-start.2 = ((bf16[8,32,384]{2,1,0:T(8,128)(2,1)}), bf16[8,32,384]{2,1,0:T(8,128)(2,1)}, u32[]{:S(2)}, u32[]{:S(2)}) async-start(bf16[8,32,384]{2,1,0:T(8,128)(2,1)} %get-tuple-element.44), calls=%async_computation.2 | async-start | bytes 393216 | tf_op jit(solution)/shard_map/cond/branch_0_fun/all_to_all | solution.py:597
  85.4 0.1 reduce
  85.5 2.0 %fusion.13 = f32[8,32,128]{2,1,0:T(8,128)S(1)} fusion(bf16[8,256,4,256]{3,1,2,0:T(8,128)(2,1)} %copy-done.7, f32[8,4,8,256]{3,2,1,0:T(8,128)S(1)} %get-tuple-element.141, f32[8,4,8]{2,1,0:T(4,128)S(1)} %get-tuple-element.140, f32[8,32]{1,0:T(8,128)S(1)} %reduce), kind=kOutput, calls=%fused_computation.7 | convolution fusion | flops 16941056 | bytes 2492416 | tf_op jit(solution)/shard_map/cond/branch_0_fun/rhgt,rthd->rhgd/dot_general | solution.py:598
  87.5 5.7 %all-to-all-done.2 = bf16[8,32,384]{2,1,0:T(8,128)(2,1)} async-done(((bf16[8,32,384]{2,1,0:T(8,128)(2,1)}), bf16[8,32,384]{2,1,0:T(8,128)(2,1)}, u32[]{:S(2)}, u32[]{:S(2)}) %all-to-all-start.2) | async-done | bytes 196640 | tf_op jit(solution)/shard_map/cond/branch_0_fun/all_to_all | solution.py:597
  93.4 10.3 %weighted_values.1 = bf16[4,2,4,64,128]{4,3,2,1,0:T(8,128)(2,1)} custom-call(s32[651]{0:T(1024)} %copy-done.6, bf16[768,1024]{1,0:T(8,128)(2,1)} %bitcast.11.refs_0_, bf16[768,1024]{1,0:T(8,128)(2,1)} %collective-permute-done.5.refs_1_, bf16[256,1024]{1,0:T(8,128)(2,1)} %get-tuple-element.87.refs_2_, bf16[256,1024]{1,0:T(8,128)(2,1)} %get-tuple-element.88.refs_3_, ...), custom_call_target="tpu_custom_call" | custom-call | tf_op jit(solution)/shard_map/weighted_values/pallas_call | solution.py:613
  103.7 3.5 %all-to-all-start.8 = ((bf16[4,2,4,64,128]{4,3,2,1,0:T(8,128)(2,1)}), bf16[4,2,4,64,128]{4,3,2,1,0:T(8,128)(2,1)S(1)}, u32[]{:S(2)}, u32[]{:S(2)}) async-start(bf16[4,2,4,64,128]{4,3,2,1,0:T(8,128)(2,1)} %weighted_values.1), calls=%async_computation.8 | async-start | bytes 1048576 | tf_op jit(solution)/shard_map/all_to_all | solution.py:635
  107.2 6.5 %all-to-all-done.8.parts_ref = bf16[4,2,4,64,128]{4,3,2,1,0:T(8,128)(2,1)S(1)} async-done(((bf16[4,2,4,64,128]{4,3,2,1,0:T(8,128)(2,1)}), bf16[4,2,4,64,128]{4,3,2,1,0:T(8,128)(2,1)S(1)}, u32[]{:S(2)}, u32[]{:S(2)}) %all-to-all-start.8) | async-done | bytes 524320 | tf_op jit(solution)/shard_map/all_to_all | solution.py:635
  113.7 0.1 half_pool_sum.1
  113.8 0.5 collective-permute-start.6
  114.3 6.4 %collective-permute-done.6.got_ref = bf16[2,4,64,128]{3,2,1,0:T(8,128)(2,1)S(1)} collective-permute-done((bf16[2,4,64,128]{3,2,1,0:T(8,128)(2,1)S(1)}, bf16[2,4,64,128]{3,2,1,0:T(8,128)(2,1)S(1)}, u32[]{:S(2)}, u32[]{:S(2)}) %collective-permute-start.6) | collective-permute-done | bytes 131104 | tf_op jit(solution)/shard_map/ppermute | solution.py:379
  120.7 1.4 %collective-permute-start.7 = (bf16[16,4096]{1,0:T(8,128)(2,1)S(1)}, bf16[16,4096]{1,0:T(8,128)(2,1)S(1)}, u32[]{:S(2)}, u32[]{:S(2)}) collective-permute-start(bf16[16,4096]{1,0:T(8,128)(2,1)S(1)} %attended_sum.1), channel_id=1, source_target_pairs={{0,2},{2,0},{4,6},{6,4},{8,10},{10,8},{12,14},{14,12},{1,3},{3,1},... | collective-permute-start | bytes 393224 | tf_op jit(solution)/shard_map/ppermute | solution.py:379
  122.2 1.7 %collective-permute-start.8 = (bf16[16,4096]{1,0:T(8,128)(2,1)S(1)}, bf16[16,4096]{1,0:T(8,128)(2,1)S(1)}, u32[]{:S(2)}, u32[]{:S(2)}) collective-permute-start(bf16[16,4096]{1,0:T(8,128)(2,1)S(1)} %attended_sum.1), channel_id=1, source_target_pairs={{0,4},{2,6},{4,0},{6,2},{8,12},{10,14},{12,8},{14,10},{1,5},{3,7},... | collective-permute-start | bytes 393224 | tf_op jit(solution)/shard_map/ppermute | solution.py:379
  123.9 0.4 collective-permute-start.9
  124.3 1.5 %collective-permute-done.7 = bf16[16,4096]{1,0:T(8,128)(2,1)S(1)} collective-permute-done((bf16[16,4096]{1,0:T(8,128)(2,1)S(1)}, bf16[16,4096]{1,0:T(8,128)(2,1)S(1)}, u32[]{:S(2)}, u32[]{:S(2)}) %collective-permute-start.7) | collective-permute-done | bytes 131104 | tf_op jit(solution)/shard_map/ppermute | solution.py:379
  125.8 1.4 collective-permute-done.8
  127.1 2.6 %collective-permute-done.9 = bf16[16,4096]{1,0:T(8,128)(2,1)S(1)} collective-permute-done((bf16[16,4096]{1,0:T(8,128)(2,1)S(1)}, bf16[16,4096]{1,0:T(8,128)(2,1)S(1)}, u32[]{:S(2)}, u32[]{:S(2)}) %collective-permute-start.9) | collective-permute-done | bytes 131104 | tf_op jit(solution)/shard_map/ppermute | solution.py:379
  129.8 4.9 %fusion.43 = f32[64,1024]{1,0:T(8,128)S(1)} fusion(bf16[4096,1024]{1,0:T(8,128)(2,1)} %param.21, bf16[16,4096]{1,0:T(8,128)(2,1)S(1)} %collective-permute-done.9, bf16[16,4096]{1,0:T(8,128)(2,1)S(1)} %collective-permute-done.8, bf16[16,4096]{1,0:T(8,128)(2,1)S(1)} %collective-permute-done.7, bf16[16,4096]{1,0:T(8,128)(2,1)S(1)} %attended_sum.1), kind=kOutput, calls=%fused_computation.33 | convolution fusion | flops 538968064 | bytes 9175040 | tf_op jit(solution)/shard_map/dot_general | solution.py:658
  134.8 1.3 collective-permute-done.10.got_ref
  136.2 0.6 order_rows.1
  (47 shorter events, 0.7 us)
Async XLA Ops:
  0.0 9.1 %copy-start.8 = (bf16[8,32,128]{2,1,0:T(8,128)(2,1)S(1)}, bf16[8,32,128]{2,1,0:T(8,128)(2,1)}, u32[]{:S(2)}) copy-start(bf16[8,32,128]{2,1,0:T(8,128)(2,1)} %param.18) | copy-start | bytes 196612
  0.0 9.1 %collective-permute-start.1 = (bf16[8,32,128]{2,1,0:T(8,128)(2,1)}, bf16[8,32,128]{2,1,0:T(8,128)(2,1)S(1)}, u32[]{:S(2)}, u32[]{:S(2)}) collective-permute-start(bf16[8,32,128]{2,1,0:T(8,128)(2,1)} %param.18), channel_id=1, source_target_pairs={{0,8},{2,10},{4,12},{6,14},{8,0},{10,2},{12,4},{14,6},{1,9},{3,11}... | collective-permute-start | bytes 196616 | tf_op jit(solution)/shard_map/ppermute | solution.py:379
  4.1 14.6 %copy-start.10 = (s32[256]{0:T(256)S(1)}, s32[256]{0:T(256)}, u32[]{:S(2)}) copy-start(s32[256]{0:T(256)} %fill_ref.1) | copy-start | bytes 3076
  4.1 14.7 %copy-start.9 = (s32[256,1]{0,1:T(1,128)S(1)}, s32[256,1]{0,1:T(1,128)}, u32[]{:S(2)}) copy-start(s32[256,1]{0,1:T(1,128)} %param.15) | copy-start | bytes 3076
  9.1 16.5 %copy-start.12 = (s32[256]{0:T(256)S(1)}, s32[256]{0:T(256)}, u32[]{:S(2)}) copy-start(s32[256]{0:T(256)} %param.16) | copy-start | bytes 3076
  9.2 5.0 %collective-permute-start.2 = (bf16[2,8,32,128]{3,2,1,0:T(8,128)(2,1)S(1)}, bf16[2,8,32,128]{3,2,1,0:T(8,128)(2,1)S(1)}, u32[]{:S(2)}, u32[]{:S(2)}) collective-permute-start(bf16[2,8,32,128]{3,2,1,0:T(8,128)(2,1)S(1)} %pad_maximum_fusion.1), channel_id=1, source_target_pairs={{0,4},{2,6},{4,0},{6,2},{8,12},{10,14},{12,8},{14,10},{1,5},{3,7},... | collective-permute-start | bytes 393224 | tf_op jit(solution)/shard_map/ppermute | solution.py:379
  14.2 40.7 %all-to-all-start.7 = ((bf16[8,96,1024]{2,1,0:T(8,128)(2,1)}), bf16[8,96,1024]{2,1,0:T(8,128)(2,1)}, u32[]{:S(2)}, u32[]{:S(2)}) async-start(bf16[8,96,1024]{2,1,0:T(8,128)(2,1)} %pack_live_tokens.3), calls=%async_computation.7 | async-start | bytes 3145728 | tf_op jit(solution)/shard_map/all_to_all | solution.py:434
  22.3 7.1 %collective-permute-start.3 = (s32[2]{0:T(128)S(1)}, s32[2]{0:T(128)S(1)}, u32[]{:S(2)}, u32[]{:S(2)}) collective-permute-start(s32[2]{0:T(128)S(1)} %pad_add_fusion.1), channel_id=1, source_target_pairs={{0,16},{16,0},{1,17},{17,1},{2,18},{18,2},{3,19},{19,3},{4,20},{20... | collective-permute-start | bytes 32 | tf_op jit(solution)/shard_map/ppermute | solution.py:480
  25.6 15.5 %copy-start = (bf16[1024,4,256]{2,0,1:T(8,128)(2,1)}, bf16[1024,4,256]{2,0,1:T(8,128)(2,1)S(1)}, u32[]{:S(2)}) copy-start(bf16[1024,4,256]{2,0,1:T(8,128)(2,1)S(1)} %copy.28) | copy-start | bytes 6291460
  27.2 31.4 %copy-start.5 = (s32[5120]{0:T(1024)}, s32[5120]{0:T(1024)S(1)}, u32[]{:S(2)}) copy-start(s32[5120]{0:T(1024)S(1)} %broadcast_add_fusion) | copy-start | bytes 61444
  27.3 12.6 %collective-permute-start.4 = (bf16[4,8,32,128]{3,2,1,0:T(8,128)(2,1)S(1)}, bf16[4,8,32,128]{3,2,1,0:T(8,128)(2,1)S(1)}, u32[]{:S(2)}, u32[]{:S(2)}) collective-permute-start(bf16[4,8,32,128]{3,2,1,0:T(8,128)(2,1)S(1)} %pad_maximum_fusion), channel_id=1, source_target_pairs={{0,2},{2,0},{4,6},{6,4},{8,10},{10,8},{12,14},{14,12},{1,3},{3,1},... | collective-permute-start | bytes 786440 | tf_op jit(solution)/shard_map/ppermute | solution.py:379
  31.9 26.7 %copy-start.6 = (s32[651]{0:T(1024)}, s32[651]{0:T(1024)S(1)}, u32[]{:S(2)}) copy-start(s32[651]{0:T(1024)S(1)} %concatenate.11.meta_ref) | copy-start | bytes 7816
  33.2 1.3 copy-start.1
  41.2 1.3 copy-start.3
  54.9 3.8 %copy-start.2 = (bf16[4,256,1024]{2,1,0:T(8,128)(2,1)S(1)}, bf16[4,256,1024]{2,1,0:T(8,128)(2,1)}, u32[]{:S(2)}) copy-start(bf16[4,256,1024]{2,1,0:T(8,128)(2,1)} %copy-done.1) | copy-start | bytes 6291460
  54.9 3.8 %collective-permute-start.5 = (bf16[768,1024]{1,0:T(8,128)(2,1)}, bf16[768,1024]{1,0:T(8,128)(2,1)}, u32[]{:S(2)}, u32[]{:S(2)}) collective-permute-start(bf16[768,1024]{1,0:T(8,128)(2,1)} %bitcast.11.refs_0_), channel_id=1, source_target_pairs={{0,1},{1,0},{2,3},{3,2},{4,5},{5,4},{6,7},{7,6},{8,9},{9,8},{10,11... | collective-permute-start | bytes 4718600 | tf_op jit(solution)/shard_map/ppermute | solution.py:520
  58.7 1.6 %copy-start.4 = (bf16[4,256,1024]{2,1,0:T(8,128)(2,1)S(1)}, bf16[4,256,1024]{2,1,0:T(8,128)(2,1)}, u32[]{:S(2)}) copy-start(bf16[4,256,1024]{2,1,0:T(8,128)(2,1)} %copy-done.3) | copy-start | bytes 6291460
  60.3 7.4 %copy-start.11 = (s32[8]{0:T(128)S(1)}, s32[8]{0:T(128)}, u32[]{:S(2)}) copy-start(s32[8]{0:T(128)} %param.20) | copy-start | bytes 100
  67.7 11.9 %all-to-all-start.1 = ((bf16[8,32,384]{2,1,0:T(8,128)(2,1)}), bf16[8,32,384]{2,1,0:T(8,128)(2,1)S(1)}, u32[]{:S(2)}, u32[]{:S(2)}) async-start(bf16[8,32,384]{2,1,0:T(8,128)(2,1)} %get-tuple-element.39), calls=%async_computation.1 | async-start | bytes 393216 | tf_op jit(solution)/shard_map/cond/branch_0_fun/all_to_all | solution.py:572
  74.1 1.9 %copy-start.7 = (bf16[8,256,4,256]{3,1,2,0:T(8,128)(2,1)}, bf16[8,256,4,256]{3,1,2,0:T(8,128)(2,1)S(1)}, u32[]{:S(2)}) copy-start(bf16[8,256,4,256]{3,1,2,0:T(8,128)(2,1)S(1)} %copy.25) | copy-start | bytes 12582916 | tf_op jit(solution)/shard_map/cond
  81.3 11.8 %all-to-all-start.2 = ((bf16[8,32,384]{2,1,0:T(8,128)(2,1)}), bf16[8,32,384]{2,1,0:T(8,128)(2,1)}, u32[]{:S(2)}, u32[]{:S(2)}) async-start(bf16[8,32,384]{2,1,0:T(8,128)(2,1)} %get-tuple-element.44), calls=%async_computation.2 | async-start | bytes 393216 | tf_op jit(solution)/shard_map/cond/branch_0_fun/all_to_all | solution.py:597
  103.7 10.0 %all-to-all-start.8 = ((bf16[4,2,4,64,128]{4,3,2,1,0:T(8,128)(2,1)}), bf16[4,2,4,64,128]{4,3,2,1,0:T(8,128)(2,1)S(1)}, u32[]{:S(2)}, u32[]{:S(2)}) async-start(bf16[4,2,4,64,128]{4,3,2,1,0:T(8,128)(2,1)} %weighted_values.1), calls=%async_computation.8 | async-start | bytes 1048576 | tf_op jit(solution)/shard_map/all_to_all | solution.py:635
  113.8 6.9 %collective-permute-start.6 = (bf16[2,4,64,128]{3,2,1,0:T(8,128)(2,1)S(1)}, bf16[2,4,64,128]{3,2,1,0:T(8,128)(2,1)S(1)}, u32[]{:S(2)}, u32[]{:S(2)}) collective-permute-start(bf16[2,4,64,128]{3,2,1,0:T(8,128)(2,1)S(1)} %get-tuple-element.98), channel_id=1, source_target_pairs={{0,8},{2,10},{4,12},{6,14},{8,0},{10,2},{12,4},{14,6},{1,9},{3,11}... | collective-permute-start | bytes 393224 | tf_op jit(solution)/shard_map/ppermute | solution.py:379
  120.7 5.0 %collective-permute-start.7 = (bf16[16,4096]{1,0:T(8,128)(2,1)S(1)}, bf16[16,4096]{1,0:T(8,128)(2,1)S(1)}, u32[]{:S(2)}, u32[]{:S(2)}) collective-permute-start(bf16[16,4096]{1,0:T(8,128)(2,1)S(1)} %attended_sum.1), channel_id=1, source_target_pairs={{0,2},{2,0},{4,6},{6,4},{8,10},{10,8},{12,14},{14,12},{1,3},{3,1},... | collective-permute-start | bytes 393224 | tf_op jit(solution)/shard_map/ppermute | solution.py:379
  122.2 5.0 %collective-permute-start.8 = (bf16[16,4096]{1,0:T(8,128)(2,1)S(1)}, bf16[16,4096]{1,0:T(8,128)(2,1)S(1)}, u32[]{:S(2)}, u32[]{:S(2)}) collective-permute-start(bf16[16,4096]{1,0:T(8,128)(2,1)S(1)} %attended_sum.1), channel_id=1, source_target_pairs={{0,4},{2,6},{4,0},{6,2},{8,12},{10,14},{12,8},{14,10},{1,5},{3,7},... | collective-permute-start | bytes 393224 | tf_op jit(solution)/shard_map/ppermute | solution.py:379
  123.9 5.9 %collective-permute-start.9 = (bf16[16,4096]{1,0:T(8,128)(2,1)S(1)}, bf16[16,4096]{1,0:T(8,128)(2,1)S(1)}, u32[]{:S(2)}, u32[]{:S(2)}) collective-permute-start(bf16[16,4096]{1,0:T(8,128)(2,1)S(1)} %attended_sum.1), channel_id=1, source_target_pairs={{0,6},{2,4},{4,2},{6,0},{8,14},{10,12},{12,10},{14,8},{1,7},{3,5},... | collective-permute-start | bytes 393224 | tf_op jit(solution)/shard_map/ppermute | solution.py:379
  134.8 1.4 %collective-permute-start.10 = (f32[64,512]{1,0:T(8,128)S(1)}, f32[64,512]{1,0:T(8,128)S(1)}, u32[]{:S(2)}, u32[]{:S(2)}) collective-permute-start(f32[64,512]{1,0:T(8,128)S(1)} %get-tuple-element.144), channel_id=1, source_target_pairs={{0,1},{1,0},{2,3},{3,2},{4,5},{5,4},{6,7},{7,6},{8,9},{9,8},{10,11... | collective-permute-start | bytes 393224 | tf_op jit(solution)/shard_map/ppermute | solution.py:665

commit v14 on v13

--- a/solution.py
+++ b/solution.py
@@ -304,18 +304,29 @@
             list_tile(meta_ref, q * groups + cuts[t] // BLK, width // BLK, wide, tile),
             preferred_element_type=jnp.float32,
         )
-        if t:
+        if t == 0:
+            first = got
+            pl.when(size <= cuts[1])(lambda: keep(first))
+
+            @pl.when(size > cuts[1])
+            def _():
+                acc[...] = first
+
+        else:
             acc[...] += got
-        else:
-            acc[...] = got
+
+    size = meta_ref[at_size + q]
+
+    def keep(sums):
+        for h in range(kvh):
+            mixed[h, pl.ds(pl.multiple_of(q * per, per), per), :] = sums[
+                h * per : (h + 1) * per
+            ].astype(mixed.dtype)
 
     one(0)
     for t in range(1, len(cuts) - 1):
-        pl.when(meta_ref[at_size + q] > cuts[t])(functools.partial(one, t))
-    for h in range(kvh):
-        mixed[h, pl.ds(pl.multiple_of(q * per, per), per), :] = acc[
-            h * per : (h + 1) * per, :
-        ].astype(mixed.dtype)
+        pl.when(size > cuts[t])(functools.partial(one, t))
+    pl.when(size > cuts[1])(lambda: keep(acc[...]))
 
     @pl.when(q == n - 1)
     def _():
@@ -361,6 +372,21 @@
             out_ref[:, head * hd : (head + 1) * hd] = jnp.concatenate(column).astype(
                 out_ref.dtype
             )
+
+
+def stage_kernel(after_ref, weight_ref, out_ref, sem):
+    cuts = sem.shape[0]
+    span = out_ref.shape[0] // cuts
+    copies = [
+        pltpu.make_async_copy(
+            weight_ref.at[pl.ds(i * span, span)], out_ref.at[pl.ds(i * span, span)], sem.at[i]
+        )
+        for i in range(cuts)
+    ]
+    for copy in copies:
+        copy.start()
+    for copy in copies:
+        copy.wait()
 
 
 def order_kernel(n, me_ref, own_ref, got_ref, out_ref):
@@ -430,7 +456,6 @@
     )
     kv_weight = kv_weight.transpose(1, 0, 2)
     even = from_rest(jnp.stack([queries, far]), n)
-    packed, even = lax.optimization_barrier((packed, even))
     mine = lax.all_to_all(packed, "pool", 0, 0, tiled=True).reshape(n * size, part)
 
     index = jnp.arange(n * blocks, dtype=jnp.int32)
@@ -519,7 +544,7 @@
     )
     other = lax.ppermute(mine, "tp", swap)
 
-    in_hbm = pl.BlockSpec(memory_space=pltpu.HBM)
+    anywhere = pl.BlockSpec(memory_space=pl.ANY)
     row_spec = pl.BlockSpec((1, 1, lanes), lambda q, m: (q, 0, 0))
     slot_specs = [
         pl.BlockSpec((1, heads, length), lambda q, m: (q, 0, 0)) for length in (near, lanes - near)
@@ -546,7 +571,7 @@
             num_scalar_prefetch=1,
             grid=(n,),
             in_specs=[
-                *[in_hbm] * 6,
+                *[anywhere] * 6,
                 pl.BlockSpec((1, 1, lanes), lambda i, m: (owner(i, m), 0, 0)),
             ],
             out_specs=[
@@ -615,7 +640,7 @@
         grid_spec=pltpu.PrefetchScalarGridSpec(
             num_scalar_prefetch=1,
             grid=(n,),
-            in_specs=[*[in_hbm] * 4, *slot_specs, row_spec, in_hbm],
+            in_specs=[*[anywhere] * 4, *slot_specs, row_spec, anywhere],
             out_specs=pl.BlockSpec((n // 2, 2, kvh, per, hd), lambda q, m: (0, 0, 0, 0, 0)),
             scratch_shapes=[
                 *x_scratch,
@@ -654,9 +679,22 @@
         name="attended_sum",
     )(held, with_partner(send, n // 2, n))
 
+    staged = pl.pallas_call(
+        stage_kernel,
+        in_specs=[anywhere, pl.BlockSpec(memory_space=pltpu.HBM)],
+        out_specs=in_vmem,
+        out_shape=jax.ShapeDtypeStruct(out_weight.shape, jnp.bfloat16),
+        scratch_shapes=[pltpu.SemaphoreType.DMA((8,))],
+        compiler_params=pltpu.CompilerParams(vmem_limit_bytes=16 * MIB),
+        cost_estimate=pl.CostEstimate(
+            flops=0, bytes_accessed=2 * out_weight.size * 2, transcendentals=0
+        ),
+        name="stage_out_weight",
+    )(send, out_weight)
+
     everyone = [attended] + [with_partner(attended, k, n) for k in range(1, n // 2)]
     product = jnp.dot(
-        jnp.concatenate(everyone), out_weight, preferred_element_type=jnp.float32
+        jnp.concatenate(everyone), staged, preferred_element_type=jnp.float32
     )
     cols = out_weight.shape[1] // ntp
     half_spec = pl.BlockSpec((n * rows, cols), lambda i, m: (0, 0))

time: 138 us -> 135 us (0.978)
  waiting for transfers between devices: 51 us -> 45.3 us
  local copies, waits for them, and re-layouts: 13.1 us -> 16.5 us
  matrix products: 7.7 us -> 4.36 us
  starting transfers between devices: 28.8 us -> 30.5 us
    all_to_all x1, waiting for transfers between devices: 12.4 us -> 0.01 us  [local(): lax.all_to_all(packed, 'pool', 0, 0, tiled=True).reshape(n * size, part)]
    ppermute x7, waiting for transfers between devices: 20.6 us -> 27.6 us  [with_partner(): return lax.ppermute(x, 'pool', [(i, i ^ k) for i in range(n)])]
    unnamed x24 -> x26, local copies, waits for them, and re-layouts: 4.25 us -> 7.62 us
    dot_general x1, matrix products: 4.94 us -> 1.6 us  [local(): jnp.dot(jnp.concatenate(everyone), staged, preferred_element_type=jnp.flo...]
    all_to_all x1, starting transfers between devices: 3.43 us -> 5.68 us  [exchange_weights(): parts = [lax.all_to_all(s, 'pool', 0, 0, tiled=True) for s in scores]]
  transfers between devices with their start and end apart: 14 -> 14, of which waited for: 12 -> 9; matrix products, arithmetic and copies ran while one was open for 12% -> 13% of each run, Pallas kernels for 6% -> 6%
where the time goes in v14:
time: 135 us; the launch traced here: 134 us
  waiting for transfers between devices  45.3 us (34%)
  starting transfers between devices  30.5 us (23%)
  Pallas kernels  29.1 us (22%)
  local copies, waits for them, and re-layouts  16.5 us (12%)
  other arithmetic  6.44 us (5%)
  matrix products  4.36 us (3%)
  between operations  1.62 us (1%)
    ppermute x7, waiting for transfers between devices, with_partner(): return lax.ppermute(x, 'pool', [(i, i ^ k) for i in range(n)])  27.6 us
    ppermute x7, starting transfers between devices, with_partner(): return lax.ppermute(x, 'pool', [(i, i ^ k) for i in range(n)])  11.4 us
    pallas_call x1, Pallas kernels, local(): pl.pallas_call(functools.partial(value_kernel, n, rows), grid_spec=pltpu....  10.7 us
    pallas_call x1, Pallas kernels, local(): pl.pallas_call(functools.partial(score_kernel, n, rows), grid_spec=pltpu....  7.72 us
    unnamed x26, local copies, waits for them, and re-layouts  7.62 us
    all_to_all x1, waiting for transfers between devices, local(): lax.all_to_all(terms, 'pool', 0, 0, axis_index_groups=halves, tiled=True)  6.54 us
    all_to_all x1, starting transfers between devices, exchange_weights(): parts = [lax.all_to_all(s, 'pool', 0, 0, tiled=True) for s in scores]  5.68 us
    all_to_all x1, waiting for transfers between devices, exchange_weights(): weights = [lax.all_to_all(w, 'pool', 0, 0, tiled=True) for w in weights]  5.66 us
  transfers between devices with their start and end apart: 14, of which 9 were waited for; matrix products, arithmetic and copies ran while one was open for 13% of the time, Pallas kernels for 6%

profile of v14, /device:TPU:0, one launch (start us, length us, event | category | flops | bytes accessed | tf_op | source)
XLA Modules:
  0.0 134.1 jit_solution(9945018500507233633)
XLA Ops:
  0.0 4.0 %collective-permute-start.1 = (bf16[8,32,128]{2,1,0:T(8,128)(2,1)}, bf16[8,32,128]{2,1,0:T(8,128)(2,1)S(1)}, u32[]{:S(2)}, u32[]{:S(2)}) collective-permute-start(bf16[8,32,128]{2,1,0:T(8,128)(2,1)} %param.18), channel_id=1, source_target_pairs={{0,8},{2,10},{4,12},{6,14},{8,0},{10,2},{12,4},{14,6},{1,9},{3,11}... | collective-permute-start | bytes 196616 | tf_op jit(solution)/shard_map/ppermute | solution.py:405
  4.2 5.0 %pack_live_tokens.3 = bf16[8,96,1024]{2,1,0:T(8,128)(2,1)} custom-call(s32[2]{0:T(128)S(1)} %pad_add_fusion.at_ref, s32[256]{0:T(256)} %fill_ref.1, s32[256]{0:T(256)} %bitcast.51, bf16[256,8192]{1,0:T(8,128)(2,1)} %x_ref.1), custom_call_target="tpu_custom_call" | custom-call | flops 402653184 | bytes 67108864 | tf_op jit(solution)/shard_map/pack_live_tokens/pallas_call | solution.py:62
  9.2 4.4 %all-to-all-start.7 = ((bf16[8,96,1024]{2,1,0:T(8,128)(2,1)}), bf16[8,96,1024]{2,1,0:T(8,128)(2,1)}, u32[]{:S(2)}, u32[]{:S(2)}) async-start(bf16[8,96,1024]{2,1,0:T(8,128)(2,1)} %pack_live_tokens.3), calls=%async_computation.7 | async-start | bytes 3145728 | tf_op jit(solution)/shard_map/all_to_all | solution.py:459
  13.6 0.2 select_reduce_fusion.5
  13.8 0.1 reduce_sum.113
  14.0 0.1 fusion.69
  14.1 0.1 select_reduce_fusion.6
  14.2 0.1 reshape.302
  14.3 0.6 reduce_max.37
  14.9 0.1 reduce_sum.119
  15.0 0.6 reduce_max.36
  15.7 2.1 %collective-permute-start.3 = (bf16[2,8,32,128]{3,2,1,0:T(8,128)(2,1)S(1)}, bf16[2,8,32,128]{3,2,1,0:T(8,128)(2,1)S(1)}, u32[]{:S(2)}, u32[]{:S(2)}) collective-permute-start(bf16[2,8,32,128]{3,2,1,0:T(8,128)(2,1)S(1)} %pad_maximum_fusion.1), channel_id=1, source_target_pairs={{0,4},{2,6},{4,0},{6,2},{8,12},{10,14},{12,8},{14,10},{1,5},{3,7},... | collective-permute-start | bytes 393224 | tf_op jit(solution)/shard_map/ppermute | solution.py:405
  17.8 0.1 select_reduce_fusion.3
  17.9 0.3 select_reduce_fusion.2
  18.2 1.0 select_reduce_fusion
  19.3 1.3 pad_add_fusion.1
  20.5 1.5 %collective-permute-start.2 = (s32[2]{0:T(128)S(1)}, s32[2]{0:T(128)S(1)}, u32[]{:S(2)}, u32[]{:S(2)}) collective-permute-start(s32[2]{0:T(128)S(1)} %pad_add_fusion.1), channel_id=1, source_target_pairs={{0,16},{16,0},{1,17},{17,1},{2,18},{18,2},{3,19},{19,3},{4,20},{20... | collective-permute-start | bytes 32 | tf_op jit(solution)/shard_map/ppermute | solution.py:505
  22.0 1.9 %copy.28 = bf16[1024,4,256]{2,0,1:T(8,128)(2,1)S(1)} copy(bf16[1024,4,256]{2,1,0:T(4,128)(2,1)} %param.14) | data formatting | bytes 4194304 | tf_op jit(solution)/shard_map/optimization_barrier | solution.py:454
  23.9 0.1 fusion.53
  24.0 18.2 %collective-permute-done.3 = bf16[2,8,32,128]{3,2,1,0:T(8,128)(2,1)S(1)} collective-permute-done((bf16[2,8,32,128]{3,2,1,0:T(8,128)(2,1)S(1)}, bf16[2,8,32,128]{3,2,1,0:T(8,128)(2,1)S(1)}, u32[]{:S(2)}, u32[]{:S(2)}) %collective-permute-start.3) | collective-permute-done | bytes 131104 | tf_op jit(solution)/shard_map/ppermute | solution.py:405
  42.3 1.3 collective-permute-start.4
  43.5 1.3 fusion.75
  44.8 0.6 fusion.73
  46.0 0.1 concatenate.10.meta_ref
  46.0 1.3 key_projection.2.refs_4_
  47.3 1.3 copy-done.1
  48.7 1.4 %collective-permute-done.4 = bf16[4,8,32,128]{3,2,1,0:T(8,128)(2,1)S(1)} collective-permute-done((bf16[4,8,32,128]{3,2,1,0:T(8,128)(2,1)S(1)}, bf16[4,8,32,128]{3,2,1,0:T(8,128)(2,1)S(1)}, u32[]{:S(2)}, u32[]{:S(2)}) %collective-permute-start.4) | collective-permute-done | bytes 262176 | tf_op jit(solution)/shard_map/ppermute | solution.py:405
  50.1 1.3 key_projection.3.refs_5_
  51.4 1.3 copy-done.3
  53.5 1.7 %conditional.2 = (bf16[256,1024]{1,0:T(8,128)(2,1)}, bf16[256,1024]{1,0:T(8,128)(2,1)}) conditional(s32[]{:T(128)} %bitcast.18, () %tuple.25, (s32[2]{0:T(128)S(1)}, s32[256]{0:T(256)S(1)}, s32[256]{0:T(256)S(1)}, bf16[256,8192]{1,0:T(8,128)(2,1)}) %tuple.53), branch_computations={%region_12.13_spmd, %region_13.14_spmd} | conditional | flops 134217728 | bytes 70254648 | solution.py:518
  53.5 0.8 broadcast.408
  54.3 0.8 broadcast.408.clone
  55.2 1.3 collective-permute-done.5.refs_1_
  56.5 1.6 %copy-done.4 = bf16[4,256,1024]{2,1,0:T(8,128)(2,1)S(1)} copy-done((bf16[4,256,1024]{2,1,0:T(8,128)(2,1)S(1)}, bf16[4,256,1024]{2,1,0:T(8,128)(2,1)}, u32[]{:S(2)}) %copy-start.4) | copy-done | bytes 2097176
  58.1 7.7 %prompt_scores.1 = (bf16[8,32,384]{2,1,0:T(8,128)(2,1)}, bf16[8,32,256]{2,1,0:T(8,128)(2,1)}) custom-call(s32[651]{0:T(1024)S(1)} %concatenate.10.meta_ref, bf16[768,1024]{1,0:T(8,128)(2,1)} %bitcast.9.refs_0_, bf16[768,1024]{1,0:T(8,128)(2,1)} %collective-permute-done.5.refs_1_, bf16[256,1024]{1,0:T(8,128)(2,1)} %get-tuple-element.83.refs_2_, ...), custom_call_target="tpu_custom_call" | custom-call | tf_op jit(solution)/shard_map/prompt_scores/pallas_call | solution.py:568
  65.8 27.7 %conditional.3 = (bf16[8,32,384]{2,1,0:T(8,128)(2,1)}, bf16[8,32,256]{2,1,0:T(8,128)(2,1)S(1)}, f32[8,32,128]{2,1,0:T(8,128)S(1)}) conditional(s32[]{:T(128)} %bitcast.19, (bf16[8,32,384]{2,1,0:T(8,128)(2,1)}, s32[1,640]{1,0:T(1,128)S(1)}, s32[8]{0:T(128)S(1)}, bf16[8,32,128]{2,1,0:T(8,128)(2,1)S(1)}, ...), branch_computations={%region_14.17_spmd, %region_17.20_spmd} | conditional | flops 34047488 | bytes 31672474 | solution.py:635
  65.8 5.7 %all-to-all-start.1 = ((bf16[8,32,384]{2,1,0:T(8,128)(2,1)}), bf16[8,32,384]{2,1,0:T(8,128)(2,1)S(1)}, u32[]{:S(2)}, u32[]{:S(2)}) async-start(bf16[8,32,384]{2,1,0:T(8,128)(2,1)} %get-tuple-element.39), calls=%async_computation.1 | async-start | bytes 393216 | tf_op jit(solution)/shard_map/cond/branch_0_fun/all_to_all | solution.py:597
  71.5 3.0 %copy.25 = bf16[8,256,4,256]{3,1,2,0:T(8,128)(2,1)S(1)} copy(bf16[8,256,4,256]{3,2,1,0:T(4,128)(2,1)} %get-tuple-element.121) | data formatting | bytes 8388608 | tf_op jit(solution)/shard_map
  74.5 0.7 fusion.71
  75.3 1.1 copy-done.8
  76.4 0.1 broadcast_in_dim.162.refs_2_
  76.5 0.2 fusion.17
  76.7 0.1 broadcast_in_dim.163.refs_3_
  76.9 2.9 %all-to-all-done.1.refs_0_ = bf16[8,32,384]{2,1,0:T(8,128)(2,1)S(1)} async-done(((bf16[8,32,384]{2,1,0:T(8,128)(2,1)}), bf16[8,32,384]{2,1,0:T(8,128)(2,1)S(1)}, u32[]{:S(2)}, u32[]{:S(2)}) %all-to-all-start.1) | async-done | bytes 196640 | tf_op jit(solution)/shard_map/cond/branch_0_fun/all_to_all | solution.py:597
  79.7 1.7 %softmax_weights.2 = (bf16[8,32,384]{2,1,0:T(8,128)(2,1)}, f32[8,32,1]{2,1,0:T(8,128)S(1)}) custom-call(bf16[8,32,384]{2,1,0:T(8,128)(2,1)S(1)} %all-to-all-done.1.refs_0_, s32[1,384]{1,0:T(1,128)S(1)} %slice.18.refs_1_, f32[8,32,1]{2,1,0:T(8,128)S(1)} %broadcast_in_dim.162.refs_2_, f32[8,32,1]{2,1,0:T(8,128)S(1)} %broadcast_in_dim.163.refs_3_), custom_call_target="tpu_custom_call" | custom-call | tf_op jit(solution)/shard_map/cond/branch_0_fun/softmax_weights/pallas_call | solution.py:611
  81.4 4.0 %all-to-all-start.2 = ((bf16[8,32,384]{2,1,0:T(8,128)(2,1)}), bf16[8,32,384]{2,1,0:T(8,128)(2,1)}, u32[]{:S(2)}, u32[]{:S(2)}) async-start(bf16[8,32,384]{2,1,0:T(8,128)(2,1)} %get-tuple-element.44), calls=%async_computation.2 | async-start | bytes 393216 | tf_op jit(solution)/shard_map/cond/branch_0_fun/all_to_all | solution.py:622
  85.5 0.1 reduce
  85.6 2.0 %fusion.13 = f32[8,32,128]{2,1,0:T(8,128)S(1)} fusion(bf16[8,256,4,256]{3,1,2,0:T(8,128)(2,1)} %copy-done.8, f32[8,4,8,256]{3,2,1,0:T(8,128)S(1)} %get-tuple-element.137, f32[8,4,8]{2,1,0:T(4,128)S(1)} %get-tuple-element.136, f32[8,32]{1,0:T(8,128)S(1)} %reduce), kind=kOutput, calls=%fused_computation.7 | convolution fusion | flops 16941056 | bytes 2492416 | tf_op jit(solution)/shard_map/cond/branch_0_fun/rhgt,rthd->rhgd/dot_general | solution.py:623
  87.6 5.7 %all-to-all-done.2 = bf16[8,32,384]{2,1,0:T(8,128)(2,1)} async-done(((bf16[8,32,384]{2,1,0:T(8,128)(2,1)}), bf16[8,32,384]{2,1,0:T(8,128)(2,1)}, u32[]{:S(2)}, u32[]{:S(2)}) %all-to-all-start.2) | async-done | bytes 196640 | tf_op jit(solution)/shard_map/cond/branch_0_fun/all_to_all | solution.py:622
  93.5 10.7 %weighted_values.1 = bf16[4,2,4,64,128]{4,3,2,1,0:T(8,128)(2,1)} custom-call(s32[651]{0:T(1024)} %copy-done.7, bf16[768,1024]{1,0:T(8,128)(2,1)} %bitcast.9.refs_0_, bf16[768,1024]{1,0:T(8,128)(2,1)} %collective-permute-done.5.refs_1_, bf16[256,1024]{1,0:T(8,128)(2,1)} %get-tuple-element.83.refs_2_, bf16[256,1024]{1,0:T(8,128)(2,1)} %get-tuple-element.84.refs_3_, ...), custom_call_target="tpu_custom_call" | custom-call | tf_op jit(solution)/shard_map/weighted_values/pallas_call | solution.py:638
  104.2 3.5 %all-to-all-start.8 = ((bf16[4,2,4,64,128]{4,3,2,1,0:T(8,128)(2,1)}), bf16[4,2,4,64,128]{4,3,2,1,0:T(8,128)(2,1)S(1)}, u32[]{:S(2)}, u32[]{:S(2)}) async-start(bf16[4,2,4,64,128]{4,3,2,1,0:T(8,128)(2,1)} %weighted_values.1), calls=%async_computation.8 | async-start | bytes 1048576 | tf_op jit(solution)/shard_map/all_to_all | solution.py:660
  107.7 6.5 %all-to-all-done.8.parts_ref = bf16[4,2,4,64,128]{4,3,2,1,0:T(8,128)(2,1)S(1)} async-done(((bf16[4,2,4,64,128]{4,3,2,1,0:T(8,128)(2,1)}), bf16[4,2,4,64,128]{4,3,2,1,0:T(8,128)(2,1)S(1)}, u32[]{:S(2)}, u32[]{:S(2)}) %all-to-all-start.8) | async-done | bytes 524320 | tf_op jit(solution)/shard_map/all_to_all | solution.py:660
  114.2 0.1 half_pool_sum.1
  114.3 0.5 collective-permute-start.6
  114.8 6.4 %collective-permute-done.6.got_ref = bf16[2,4,64,128]{3,2,1,0:T(8,128)(2,1)S(1)} collective-permute-done((bf16[2,4,64,128]{3,2,1,0:T(8,128)(2,1)S(1)}, bf16[2,4,64,128]{3,2,1,0:T(8,128)(2,1)S(1)}, u32[]{:S(2)}, u32[]{:S(2)}) %collective-permute-start.6) | collective-permute-done | bytes 131104 | tf_op jit(solution)/shard_map/ppermute | solution.py:405
  121.3 1.3 collective-permute-start.7
  122.6 1.9 %collective-permute-start.8 = (bf16[16,4096]{1,0:T(8,128)(2,1)S(1)}, bf16[16,4096]{1,0:T(8,128)(2,1)S(1)}, u32[]{:S(2)}, u32[]{:S(2)}) collective-permute-start(bf16[16,4096]{1,0:T(8,128)(2,1)S(1)} %attended_sum.1), channel_id=1, source_target_pairs={{0,4},{2,6},{4,0},{6,2},{8,12},{10,14},{12,8},{14,10},{1,5},{3,7},... | collective-permute-start | bytes 393224 | tf_op jit(solution)/shard_map/ppermute | solution.py:405
  124.5 0.3 collective-permute-start.9
  124.8 3.4 %copy-done.5 = bf16[4096,1024]{1,0:T(8,128)(2,1)S(1)} copy-done((bf16[4096,1024]{1,0:T(8,128)(2,1)S(1)}, bf16[4096,1024]{1,0:T(8,128)(2,1)}, u32[]{:S(2)}) %copy-start.5) | copy-done | bytes 8388632
  128.2 0.6 stage_out_weight.1
  128.9 1.5 %collective-permute-done.9 = bf16[16,4096]{1,0:T(8,128)(2,1)S(1)} collective-permute-done((bf16[16,4096]{1,0:T(8,128)(2,1)S(1)}, bf16[16,4096]{1,0:T(8,128)(2,1)S(1)}, u32[]{:S(2)}, u32[]{:S(2)}) %collective-permute-start.9) | collective-permute-done | bytes 131104 | tf_op jit(solution)/shard_map/ppermute | solution.py:405
  130.4 1.6 %fusion.43 = f32[64,1024]{1,0:T(8,128)S(1)} fusion(bf16[4096,1024]{1,0:T(8,128)(2,1)S(1)} %stage_out_weight.1, bf16[16,4096]{1,0:T(8,128)(2,1)S(1)} %collective-permute-done.9, bf16[16,4096]{1,0:T(8,128)(2,1)S(1)} %collective-permute-done.8, bf16[16,4096]{1,0:T(8,128)(2,1)S(1)} %collective-permute-done.7, bf16[16,4096]{1,0:T(8,128)(2,1)S(1)} %attended_sum.1), kind=kOutput, calls=%fused_computation.33 | convolution fusion | flops 538968064 | bytes 9175040 | tf_op jit(solution)/shard_map/dot_general | solution.py:696
  132.1 1.3 collective-permute-done.10.got_ref
  133.5 0.6 order_rows.1
  (50 shorter events, 0.7 us)
Async XLA Ops:
  0.0 9.1 %collective-permute-start.1 = (bf16[8,32,128]{2,1,0:T(8,128)(2,1)}, bf16[8,32,128]{2,1,0:T(8,128)(2,1)S(1)}, u32[]{:S(2)}, u32[]{:S(2)}) collective-permute-start(bf16[8,32,128]{2,1,0:T(8,128)(2,1)} %param.18), channel_id=1, source_target_pairs={{0,8},{2,10},{4,12},{6,14},{8,0},{10,2},{12,4},{14,6},{1,9},{3,11}... | collective-permute-start | bytes 196616 | tf_op jit(solution)/shard_map/ppermute | solution.py:405
  4.1 9.4 %copy-start.11 = (s32[256]{0:T(256)S(1)}, s32[256]{0:T(256)}, u32[]{:S(2)}) copy-start(s32[256]{0:T(256)} %fill_ref.1) | copy-start | bytes 3076
  4.1 9.5 %copy-start.10 = (s32[256,1]{0,1:T(1,128)S(1)}, s32[256,1]{0,1:T(1,128)}, u32[]{:S(2)}) copy-start(s32[256,1]{0,1:T(1,128)} %param.15) | copy-start | bytes 3076
  4.1 11.5 %copy-start.9 = (bf16[8,32,128]{2,1,0:T(8,128)(2,1)S(1)}, bf16[8,32,128]{2,1,0:T(8,128)(2,1)}, u32[]{:S(2)}) copy-start(bf16[8,32,128]{2,1,0:T(8,128)(2,1)} %param.18) | copy-start | bytes 196612
  4.1 13.6 %copy-start.13 = (s32[256]{0:T(256)S(1)}, s32[256]{0:T(256)}, u32[]{:S(2)}) copy-start(s32[256]{0:T(256)} %param.16) | copy-start | bytes 3076
  9.2 43.5 %all-to-all-start.7 = ((bf16[8,96,1024]{2,1,0:T(8,128)(2,1)}), bf16[8,96,1024]{2,1,0:T(8,128)(2,1)}, u32[]{:S(2)}, u32[]{:S(2)}) async-start(bf16[8,96,1024]{2,1,0:T(8,128)(2,1)} %pack_live_tokens.3), calls=%async_computation.7 | async-start | bytes 3145728 | tf_op jit(solution)/shard_map/all_to_all | solution.py:459
  15.7 26.5 %collective-permute-start.3 = (bf16[2,8,32,128]{3,2,1,0:T(8,128)(2,1)S(1)}, bf16[2,8,32,128]{3,2,1,0:T(8,128)(2,1)S(1)}, u32[]{:S(2)}, u32[]{:S(2)}) collective-permute-start(bf16[2,8,32,128]{3,2,1,0:T(8,128)(2,1)S(1)} %pad_maximum_fusion.1), channel_id=1, source_target_pairs={{0,4},{2,6},{4,0},{6,2},{8,12},{10,14},{12,8},{14,10},{1,5},{3,7},... | collective-permute-start | bytes 393224 | tf_op jit(solution)/shard_map/ppermute | solution.py:405
  19.2 37.2 %copy-start.6 = (s32[5120]{0:T(1024)}, s32[5120]{0:T(1024)S(1)}, u32[]{:S(2)}) copy-start(s32[5120]{0:T(1024)S(1)} %broadcast_add_fusion) | copy-start | bytes 61444
  20.5 23.0 %collective-permute-start.2 = (s32[2]{0:T(128)S(1)}, s32[2]{0:T(128)S(1)}, u32[]{:S(2)}, u32[]{:S(2)}) collective-permute-start(s32[2]{0:T(128)S(1)} %pad_add_fusion.1), channel_id=1, source_target_pairs={{0,16},{16,0},{1,17},{17,1},{2,18},{18,2},{3,19},{19,3},{4,20},{20... | collective-permute-start | bytes 32 | tf_op jit(solution)/shard_map/ppermute | solution.py:505
  23.9 27.5 %copy-start = (bf16[1024,4,256]{2,0,1:T(8,128)(2,1)}, bf16[1024,4,256]{2,0,1:T(8,128)(2,1)S(1)}, u32[]{:S(2)}) copy-start(bf16[1024,4,256]{2,0,1:T(8,128)(2,1)S(1)} %copy.28) | copy-start | bytes 6291460
  42.3 7.8 %collective-permute-start.4 = (bf16[4,8,32,128]{3,2,1,0:T(8,128)(2,1)S(1)}, bf16[4,8,32,128]{3,2,1,0:T(8,128)(2,1)S(1)}, u32[]{:S(2)}, u32[]{:S(2)}) collective-permute-start(bf16[4,8,32,128]{3,2,1,0:T(8,128)(2,1)S(1)} %pad_maximum_fusion), channel_id=1, source_target_pairs={{0,2},{2,0},{4,6},{6,4},{8,10},{10,8},{12,14},{14,12},{1,3},{3,1},... | collective-permute-start | bytes 786440 | tf_op jit(solution)/shard_map/ppermute | solution.py:405
  46.0 10.4 %copy-start.7 = (s32[651]{0:T(1024)}, s32[651]{0:T(1024)S(1)}, u32[]{:S(2)}) copy-start(s32[651]{0:T(1024)S(1)} %concatenate.10.meta_ref) | copy-start | bytes 7816
  47.3 1.3 copy-start.1
  51.4 1.3 copy-start.3
  52.7 3.8 %copy-start.2 = (bf16[4,256,1024]{2,1,0:T(8,128)(2,1)S(1)}, bf16[4,256,1024]{2,1,0:T(8,128)(2,1)}, u32[]{:S(2)}) copy-start(bf16[4,256,1024]{2,1,0:T(8,128)(2,1)} %copy-done.1) | copy-start | bytes 6291460
  52.7 3.8 %collective-permute-start.5 = (bf16[768,1024]{1,0:T(8,128)(2,1)}, bf16[768,1024]{1,0:T(8,128)(2,1)}, u32[]{:S(2)}, u32[]{:S(2)}) collective-permute-start(bf16[768,1024]{1,0:T(8,128)(2,1)} %bitcast.9.refs_0_), channel_id=1, source_target_pairs={{0,1},{1,0},{2,3},{3,2},{4,5},{5,4},{6,7},{7,6},{8,9},{9,8},{10,11... | collective-permute-start | bytes 4718600 | tf_op jit(solution)/shard_map/ppermute | solution.py:545
  56.5 1.6 %copy-start.4 = (bf16[4,256,1024]{2,1,0:T(8,128)(2,1)S(1)}, bf16[4,256,1024]{2,1,0:T(8,128)(2,1)}, u32[]{:S(2)}) copy-start(bf16[4,256,1024]{2,1,0:T(8,128)(2,1)} %copy-done.3) | copy-start | bytes 6291460
  58.0 7.7 %copy-start.12 = (s32[8]{0:T(128)S(1)}, s32[8]{0:T(128)}, u32[]{:S(2)}) copy-start(s32[8]{0:T(128)} %param.20) | copy-start | bytes 100
  65.8 13.9 %all-to-all-start.1 = ((bf16[8,32,384]{2,1,0:T(8,128)(2,1)}), bf16[8,32,384]{2,1,0:T(8,128)(2,1)S(1)}, u32[]{:S(2)}, u32[]{:S(2)}) async-start(bf16[8,32,384]{2,1,0:T(8,128)(2,1)} %get-tuple-element.39), calls=%async_computation.1 | async-start | bytes 393216 | tf_op jit(solution)/shard_map/cond/branch_0_fun/all_to_all | solution.py:597
  74.5 1.9 %copy-start.8 = (bf16[8,256,4,256]{3,1,2,0:T(8,128)(2,1)}, bf16[8,256,4,256]{3,1,2,0:T(8,128)(2,1)S(1)}, u32[]{:S(2)}) copy-start(bf16[8,256,4,256]{3,1,2,0:T(8,128)(2,1)S(1)} %copy.25) | copy-start | bytes 12582916 | tf_op jit(solution)/shard_map/cond
  81.4 11.8 %all-to-all-start.2 = ((bf16[8,32,384]{2,1,0:T(8,128)(2,1)}), bf16[8,32,384]{2,1,0:T(8,128)(2,1)}, u32[]{:S(2)}, u32[]{:S(2)}) async-start(bf16[8,32,384]{2,1,0:T(8,128)(2,1)} %get-tuple-element.44), calls=%async_computation.2 | async-start | bytes 393216 | tf_op jit(solution)/shard_map/cond/branch_0_fun/all_to_all | solution.py:622
  104.2 10.0 %all-to-all-start.8 = ((bf16[4,2,4,64,128]{4,3,2,1,0:T(8,128)(2,1)}), bf16[4,2,4,64,128]{4,3,2,1,0:T(8,128)(2,1)S(1)}, u32[]{:S(2)}, u32[]{:S(2)}) async-start(bf16[4,2,4,64,128]{4,3,2,1,0:T(8,128)(2,1)} %weighted_values.1), calls=%async_computation.8 | async-start | bytes 1048576 | tf_op jit(solution)/shard_map/all_to_all | solution.py:660
  114.3 6.9 %collective-permute-start.6 = (bf16[2,4,64,128]{3,2,1,0:T(8,128)(2,1)S(1)}, bf16[2,4,64,128]{3,2,1,0:T(8,128)(2,1)S(1)}, u32[]{:S(2)}, u32[]{:S(2)}) collective-permute-start(bf16[2,4,64,128]{3,2,1,0:T(8,128)(2,1)S(1)} %get-tuple-element.94.after_ref), channel_id=1, source_target_pairs={{0,8},{2,10},{4,12},{6,14},{8,0},{10,2},{12,4},{14,6},{1,9},{3,11}... | collective-permute-start | bytes 393224 | tf_op jit(solution)/shard_map/ppermute | solution.py:405
  121.3 7.6 %collective-permute-start.7 = (bf16[16,4096]{1,0:T(8,128)(2,1)S(1)}, bf16[16,4096]{1,0:T(8,128)(2,1)S(1)}, u32[]{:S(2)}, u32[]{:S(2)}) collective-permute-start(bf16[16,4096]{1,0:T(8,128)(2,1)S(1)} %attended_sum.1), channel_id=1, source_target_pairs={{0,2},{2,0},{4,6},{6,4},{8,10},{10,8},{12,14},{14,12},{1,3},{3,1},... | collective-permute-start | bytes 393224 | tf_op jit(solution)/shard_map/ppermute | solution.py:405
  122.6 6.3 %collective-permute-start.8 = (bf16[16,4096]{1,0:T(8,128)(2,1)S(1)}, bf16[16,4096]{1,0:T(8,128)(2,1)S(1)}, u32[]{:S(2)}, u32[]{:S(2)}) collective-permute-start(bf16[16,4096]{1,0:T(8,128)(2,1)S(1)} %attended_sum.1), channel_id=1, source_target_pairs={{0,4},{2,6},{4,0},{6,2},{8,12},{10,14},{12,8},{14,10},{1,5},{3,7},... | collective-permute-start | bytes 393224 | tf_op jit(solution)/shard_map/ppermute | solution.py:405
  124.5 5.9 %collective-permute-start.9 = (bf16[16,4096]{1,0:T(8,128)(2,1)S(1)}, bf16[16,4096]{1,0:T(8,128)(2,1)S(1)}, u32[]{:S(2)}, u32[]{:S(2)}) collective-permute-start(bf16[16,4096]{1,0:T(8,128)(2,1)S(1)} %attended_sum.1), channel_id=1, source_target_pairs={{0,6},{2,4},{4,2},{6,0},{8,14},{10,12},{12,10},{14,8},{1,7},{3,5},... | collective-permute-start | bytes 393224 | tf_op jit(solution)/shard_map/ppermute | solution.py:405
  124.8 3.4 %copy-start.5 = (bf16[4096,1024]{1,0:T(8,128)(2,1)S(1)}, bf16[4096,1024]{1,0:T(8,128)(2,1)}, u32[]{:S(2)}) copy-start(bf16[4096,1024]{1,0:T(8,128)(2,1)} %weight_ref.1) | copy-start | bytes 25165828
  132.0 1.4 %collective-permute-start.10 = (f32[64,512]{1,0:T(8,128)S(1)}, f32[64,512]{1,0:T(8,128)S(1)}, u32[]{:S(2)}, u32[]{:S(2)}) collective-permute-start(f32[64,512]{1,0:T(8,128)S(1)} %get-tuple-element.140), channel_id=1, source_target_pairs={{0,1},{1,0},{2,3},{3,2},{4,5},{5,4},{6,7},{7,6},{8,9},{9,8},{10,11... | collective-permute-start | bytes 393224 | tf_op jit(solution)/shard_map/ppermute | solution.py:703

commit v15 on v14

--- a/solution.py
+++ b/solution.py
@@ -117,8 +117,8 @@
     ]
 
 
-def load_tokens(n, core, over, x_refs, held, more, wide, sem, others):
-    main = span_copies(x_refs[:2], held, sem)
+def load_tokens(n, core, over, x_refs, there, held, more, wide, sem, others):
+    main = span_copies(x_refs[: 2 - len(there)], held, sem)
     for pair in main:
         for copy in pair:
             copy.start()
@@ -127,7 +127,7 @@
     for i, pair in enumerate(main):
         for copy in pair:
             copy.wait()
-        parts = [held.at[0], held.at[1]]
+        parts = [held.at[j] for j in range(2 - len(there))] + there
         widen(core, n, parts, wide, 0, i * n // len(main), (i + 1) * n // len(main))
 
     @pl.when(over != 0)
@@ -180,37 +180,31 @@
     groups = lanes // BLK
     at_size = n * groups
     q = meta_ref[at_size + n] ^ reversed_bits(step, n)
-    kvh, per = keyed.shape[0], keyed.shape[1] // n
+    kvh, per = keyed.shape[0], keyed.shape[1] * 2 // n
     group = per // rows
 
-    def load(i):
-        span = n // 2 * per
-        return [
-            pltpu.make_async_copy(
-                keyed_refs[i].at[h], keyed.at[h, pl.ds(i * span, span)], keyed_sem.at[i, h]
-            )
-            for h in range(kvh)
-        ]
+    even_ref, odd_ref = keyed_refs
+    load = [
+        pltpu.make_async_copy(even_ref.at[h], keyed.at[h], keyed_sem.at[h]) for h in range(kvh)
+    ]
 
     @pl.when(step == 0)
     def _():
         load_tokens(
-            n, meta_ref[at_size + n + 1], meta_ref[at_size + n + 2], x_refs, held, more, wide, sem,
-            load(0) + load(1),
-        )
-
-    for i in range(2):
-
-        @pl.when(step == i * (n // 2))
-        def _(i=i):
-            for copy in load(i):
-                copy.wait()
+            n, meta_ref[at_size + n + 1], meta_ref[at_size + n + 2], x_refs, [x_refs[1]], held, more,
+            wide, sem, load,
+        )
+        for copy in load:
+            copy.wait()
+
+    at = pl.ds(pl.multiple_of(step % (n // 2) * per, per), per)
+    query = jnp.where(step < n // 2, keyed[:, at, :], odd_ref[:, at, :])
 
     def one(t):
         here = slice(cuts[t], cuts[t + 1])
         count = (cuts[t + 1] - cuts[t]) // BLK
         raw = lax.dot_general(
-            keyed[:, pl.ds(pl.multiple_of(step * per, per), per), :].reshape(kvh * per, part),
+            query.reshape(kvh * per, part),
             list_tile(meta_ref, q * groups + cuts[t] // BLK, count, wide, tile),
             (((1,), (1,)), ((), ())),
             preferred_element_type=jnp.float32,
@@ -261,61 +255,76 @@
             w_ref[i] = w.astype(w_ref.dtype)
 
 
-def value_kernel(n, rows, meta_ref, *refs):
-    x_refs, (near_ref, rest_ref, row_ref, weight_ref, out_ref) = refs[:4], refs[4:9]
-    held, more, wide, tile, values, acc, mixed, sem, value_sem = refs[9:]
+def list_kernel(n, meta_ref, *refs):
+    x_refs, (_, out_ref, held, more, wide, sem) = refs[:4], refs[4:]
     q = pl.program_id(0)
-    kvh = values.shape[0]
-    hd = values.shape[2]
+    lanes = out_ref.shape[1]
+    cuts = tile_cuts(lanes)
+    groups = lanes // BLK
+    at_size = n * groups
+
+    @pl.when(q == 0)
+    def _():
+        load_tokens(
+            n, meta_ref[at_size + n + 1], meta_ref[at_size + n + 2], x_refs, [], held, more, wide,
+            sem, [],
+        )
+
+    def one(t):
+        list_tile(
+            meta_ref, q * groups + cuts[t] // BLK, (cuts[t + 1] - cuts[t]) // BLK, wide,
+            out_ref.at[q, cuts[t] : cuts[t + 1]],
+        )
+
+    one(0)
+    for t in range(1, len(cuts) - 1):
+        pl.when(meta_ref[at_size + q] > cuts[t])(functools.partial(one, t))
+
+
+def value_kernel(n, rows, count, meta_ref, *refs):
+    w_refs, (row_ref, list_ref, weight_ref, out_ref) = refs[:count], refs[count : count + 4]
+    values, acc, mixed, value_sem = refs[count + 4 :]
+    q = pl.program_id(0)
+    kvh, _, hd = values.shape
     load_values = [
         pltpu.make_async_copy(
             weight_ref.at[h, :, pl.ds(hd, hd)], values.at[h], value_sem.at[h]
         )
         for h in range(kvh)
     ]
-    _, heads, near = near_ref.shape
-    lanes = near + rest_ref.shape[2]
+    _, heads, near = w_refs[0].shape
+    lanes = list_ref.shape[1]
     per = rows * heads // kvh
     cuts = tile_cuts(lanes)
-    groups = lanes // BLK
-    at_size = n * groups
+    size = meta_ref[n * lanes // BLK + q]
 
     @pl.when(q == 0)
     def _():
-        load_tokens(
-            n, meta_ref[at_size + n + 1], meta_ref[at_size + n + 2], x_refs, held, more, wide, sem,
-            load_values,
-        )
+        for load in load_values:
+            load.start()
 
     def one(t):
         here = slice(cuts[t], cuts[t + 1])
         width = cuts[t + 1] - cuts[t]
-        if cuts[t] < near:
-            weights = near_ref[0, :, here]
-        else:
-            weights = rest_ref[0, :, cuts[t] - near : cuts[t + 1] - near]
+        piece = 0 if cuts[t] < near else 1
+        weights = w_refs[piece][0, :, cuts[t] - piece * near : cuts[t + 1] - piece * near]
         weights = weights.astype(jnp.float32).reshape(kvh, 1, heads // kvh, width)
         owner_row = row_ref[0, :, here]
         spread = jnp.concatenate(
             [jnp.where((owner_row == r)[None, None], weights, 0.0) for r in range(rows)], 1
         ).reshape(kvh * per, width)
         got = jnp.dot(
-            spread.astype(jnp.bfloat16),
-            list_tile(meta_ref, q * groups + cuts[t] // BLK, width // BLK, wide, tile),
-            preferred_element_type=jnp.float32,
+            spread.astype(jnp.bfloat16), list_ref[q, here, :], preferred_element_type=jnp.float32
         )
         if t == 0:
-            first = got
-            pl.when(size <= cuts[1])(lambda: keep(first))
+            pl.when(size <= cuts[1])(lambda: keep(got))
 
             @pl.when(size > cuts[1])
             def _():
-                acc[...] = first
+                acc[...] = got
 
         else:
             acc[...] += got
-
-    size = meta_ref[at_size + q]
 
     def keep(sums):
         for h in range(kvh):
@@ -325,7 +334,8 @@
 
     one(0)
     for t in range(1, len(cuts) - 1):
-        pl.when(size > cuts[t])(functools.partial(one, t))
+        if cuts[t] < near or count > 1:
+            pl.when(size > cuts[t])(functools.partial(one, t))
     pl.when(size > cuts[1])(lambda: keep(acc[...]))
 
     @pl.when(q == n - 1)
@@ -555,10 +565,8 @@
     in_vmem = pl.BlockSpec(memory_space=pltpu.VMEM)
     x_parts = (mine, other, more_mine, more_other)
     x_scratch = [
-        pltpu.VMEM((ntp, n * size, part), jnp.bfloat16),
         pltpu.VMEM((ntp, n * extra, part), jnp.bfloat16),
         pltpu.VMEM((n * tokens, part), jnp.float32),
-        pltpu.VMEM((tile_cuts(lanes)[1], part), jnp.bfloat16),
     ]
     at_me = n * lanes // BLK + n
 
@@ -571,7 +579,12 @@
             num_scalar_prefetch=1,
             grid=(n,),
             in_specs=[
-                *[anywhere] * 6,
+                anywhere,
+                in_vmem,
+                anywhere,
+                anywhere,
+                anywhere,
+                in_vmem,
                 pl.BlockSpec((1, 1, lanes), lambda i, m: (owner(i, m), 0, 0)),
             ],
             out_specs=[
@@ -579,10 +592,12 @@
                 for length in (near, lanes - near)
             ],
             scratch_shapes=[
+                pltpu.VMEM((1, n * size, part), jnp.bfloat16),
                 *x_scratch,
-                pltpu.VMEM((kvh, n * per, part), jnp.bfloat16),
+                pltpu.VMEM((tile_cuts(lanes)[1], part), jnp.bfloat16),
+                pltpu.VMEM((kvh, n // 2 * per, part), jnp.bfloat16),
                 pltpu.SemaphoreType.DMA((ntp, 4)),
-                pltpu.SemaphoreType.DMA((2, kvh)),
+                pltpu.SemaphoreType.DMA((kvh,)),
             ],
         ),
         out_shape=slot_shapes,
@@ -619,6 +634,26 @@
             cache_top.reshape(rows, heads, 1),
             cache_sum.reshape(rows, heads, 1),
         )
+        lists = pl.pallas_call(
+            functools.partial(list_kernel, n),
+            grid_spec=pltpu.PrefetchScalarGridSpec(
+                num_scalar_prefetch=1,
+                grid=(n,),
+                in_specs=[anywhere] * 5,
+                out_specs=in_vmem,
+                scratch_shapes=[
+                    pltpu.VMEM((ntp, n * size, part), jnp.bfloat16),
+                    *x_scratch,
+                    pltpu.SemaphoreType.DMA((ntp, 4)),
+                ],
+            ),
+            out_shape=jax.ShapeDtypeStruct((n, lanes, part), jnp.bfloat16),
+            compiler_params=pltpu.CompilerParams(vmem_limit_bytes=28 * MIB),
+            cost_estimate=pl.CostEstimate(
+                flops=0, bytes_accessed=16 * MIB, transcendentals=0
+            ),
+            name="owner_lists",
+        )(meta, *x_parts, weights[0])
         weights = [lax.all_to_all(w, "pool", 0, 0, tiled=True) for w in weights]
         cached = jnp.einsum(
             "rhgt,rthd->rhgd",
@@ -626,35 +661,31 @@
             kv_cache[:, :, :, hd:],
             preferred_element_type=jnp.float32,
         )
-        return *weights, cached.reshape(rows, heads, hd) * share
-
-    def near_only():
-        weights, kept = exchange_weights(score_near)
-        return weights, jnp.zeros(slot_shapes[1].shape, jnp.bfloat16), kept
-
-    weight_near, weight_rest, kept = lax.cond(
-        longer, lambda: exchange_weights(score_near, score_rest), near_only
-    )
-    terms = pl.pallas_call(
-        functools.partial(value_kernel, n, rows),
-        grid_spec=pltpu.PrefetchScalarGridSpec(
-            num_scalar_prefetch=1,
-            grid=(n,),
-            in_specs=[*[anywhere] * 4, *slot_specs, row_spec, anywhere],
-            out_specs=pl.BlockSpec((n // 2, 2, kvh, per, hd), lambda q, m: (0, 0, 0, 0, 0)),
-            scratch_shapes=[
-                *x_scratch,
-                pltpu.VMEM((kvh, part, hd), jnp.bfloat16),
-                pltpu.VMEM((kvh * per, part), jnp.float32),
-                pltpu.VMEM((kvh, n * per, part), jnp.bfloat16),
-                pltpu.SemaphoreType.DMA((ntp, 4)),
-                pltpu.SemaphoreType.DMA((kvh,)),
-            ],
-        ),
-        out_shape=jax.ShapeDtypeStruct((n // 2, 2, kvh, per, hd), jnp.bfloat16),
-        compiler_params=pltpu.CompilerParams(vmem_limit_bytes=56 * MIB),
-        name="weighted_values",
-    )(meta, *x_parts, weight_near, weight_rest, rowof, kv_weight)
+        terms = pl.pallas_call(
+            functools.partial(value_kernel, n, rows, count),
+            grid_spec=pltpu.PrefetchScalarGridSpec(
+                num_scalar_prefetch=1,
+                grid=(n,),
+                in_specs=[*slot_specs[:count], row_spec, in_vmem, anywhere],
+                out_specs=pl.BlockSpec((n // 2, 2, kvh, per, hd), lambda q, m: (0, 0, 0, 0, 0)),
+                scratch_shapes=[
+                    pltpu.VMEM((kvh, part, hd), jnp.bfloat16),
+                    pltpu.VMEM((kvh * per, part), jnp.float32),
+                    pltpu.VMEM((kvh, n * per, part), jnp.bfloat16),
+                    pltpu.SemaphoreType.DMA((kvh,)),
+                ],
+            ),
+            out_shape=jax.ShapeDtypeStruct((n // 2, 2, kvh, per, hd), jnp.bfloat16),
+            compiler_params=pltpu.CompilerParams(vmem_limit_bytes=16 * MIB),
+            name="weighted_values",
+        )(meta, *weights, rowof, lists, kv_weight)
+        return terms, cached.reshape(rows, heads, hd) * share
+
+    terms, kept = lax.cond(
+        longer,
+        lambda: exchange_weights(score_near, score_rest),
+        lambda: exchange_weights(score_near),
+    )
 
     halves = [list(range(n // 2)), list(range(n // 2, n))]
     term_parts = lax.all_to_all(

time: 135 us -> 135 us (level)
  waiting for transfers between devices: 45.3 us -> 37 us
  local copies, waits for them, and re-layouts: 16.5 us -> 23 us
  starting transfers between devices: 30.5 us -> 32.7 us
  matrix products: 4.36 us -> 2.76 us
  Pallas kernels: 29.1 us -> 30.6 us
    cond x2 -> x10, local copies, waits for them, and re-layouts: 1.12 us -> 9.27 us
    all_to_all x1, waiting for transfers between devices: 5.66 us -> 0.01 us  [exchange_weights(): weights = [lax.all_to_all(w, 'pool', 0, 0, tiled=True) for w in weights]]
    ppermute x7, waiting for transfers between devices: 27.6 us -> 24.3 us  [with_partner(): return lax.ppermute(x, 'pool', [(i, i ^ k) for i in range(n)])]
    ppermute x7, starting transfers between devices: 11.4 us -> 13.5 us  [with_partner(): return lax.ppermute(x, 'pool', [(i, i ^ k) for i in range(n)])]
    pallas_call x2, Pallas kernels: 2.56 us -> 4.51 us  [through_keys(): pl.pallas_call(key_kernel, grid=(kvh,), in_specs=[pl.BlockSpec(held.shape...]
    dot_general x1, matrix products: 2.03 us -> 0.43 us  [exchange_weights(): jnp.einsum('rhgt,rthd->rhgd', cache_exp.astype(jnp.bfloat16), kv_cache[:,...]
    unnamed x26 -> x20, local copies, waits for them, and re-layouts: 7.62 us -> 6.33 us
    pallas_call x1 -> x2, Pallas kernels: 10.7 us -> 9.67 us  [the longest x1 6.07 us: exchange_weights(): pl.pallas_call(functools.partial(value_kernel, n, rows, count), grid_spec...]
  transfers between devices with their start and end apart: 14 -> 14, of which waited for: 9 -> 7; matrix products, arithmetic and copies ran while one was open for 13% -> 11% of each run, Pallas kernels for 6% -> 10%
where the time goes in v15:
time: 135 us; the launch traced here: 134 us
  waiting for transfers between devices  37 us (27%)
  starting transfers between devices  32.7 us (24%)
  Pallas kernels  30.6 us (23%)
  local copies, waits for them, and re-layouts  23 us (17%)
  other arithmetic  6.64 us (5%)
  matrix products  2.76 us (2%)
  between operations  1.46 us (1%)
    ppermute x7, waiting for transfers between devices, with_partner(): return lax.ppermute(x, 'pool', [(i, i ^ k) for i in range(n)])  24.3 us
    ppermute x7, starting transfers between devices, with_partner(): return lax.ppermute(x, 'pool', [(i, i ^ k) for i in range(n)])  13.5 us
    cond x10, local copies, waits for them, and re-layouts  9.27 us
    pallas_call x1, Pallas kernels, local(): pl.pallas_call(functools.partial(score_kernel, n, rows), grid_spec=pltpu....  8.31 us
    all_to_all x1, waiting for transfers between devices, local(): lax.all_to_all(terms, 'pool', 0, 0, axis_index_groups=halves, tiled=True)  7.21 us
    unnamed x20, local copies, waits for them, and re-layouts  6.33 us
    pallas_call x1, Pallas kernels, exchange_weights(): pl.pallas_call(functools.partial(value_kernel, n, rows, count), grid_spec...  6.07 us
    all_to_all x1, starting transfers between devices, exchange_weights(): parts = [lax.all_to_all(s, 'pool', 0, 0, tiled=True) for s in scores]  5.65 us
  transfers between devices with their start and end apart: 14, of which 7 were waited for; matrix products, arithmetic and copies ran while one was open for 11% of the time, Pallas kernels for 10%

profile of v15, /device:TPU:0, one launch (start us, length us, event | category | flops | bytes accessed | tf_op | source)
XLA Modules:
  0.0 134.5 jit_solution(10455080059175809603)
XLA Ops:
  0.0 4.0 %collective-permute-start.1 = (bf16[8,32,128]{2,1,0:T(8,128)(2,1)}, bf16[8,32,128]{2,1,0:T(8,128)(2,1)S(1)}, u32[]{:S(2)}, u32[]{:S(2)}) collective-permute-start(bf16[8,32,128]{2,1,0:T(8,128)(2,1)} %param.18), channel_id=1, source_target_pairs={{0,8},{2,10},{4,12},{6,14},{8,0},{10,2},{12,4},{14,6},{1,9},{3,11}... | collective-permute-start | bytes 196616 | tf_op jit(solution)/shard_map/ppermute | solution.py:415
  4.2 4.9 %pack_live_tokens.3 = bf16[8,96,1024]{2,1,0:T(8,128)(2,1)} custom-call(s32[2]{0:T(128)S(1)} %pad_add_fusion.at_ref, s32[256]{0:T(256)} %fill_ref.1, s32[256]{0:T(256)} %bitcast.53, bf16[256,8192]{1,0:T(8,128)(2,1)} %x_ref.1), custom_call_target="tpu_custom_call" | custom-call | flops 402653184 | bytes 67108864 | tf_op jit(solution)/shard_map/pack_live_tokens/pallas_call | solution.py:62
  9.1 4.4 %all-to-all-start.7 = ((bf16[8,96,1024]{2,1,0:T(8,128)(2,1)}), bf16[8,96,1024]{2,1,0:T(8,128)(2,1)}, u32[]{:S(2)}, u32[]{:S(2)}) async-start(bf16[8,96,1024]{2,1,0:T(8,128)(2,1)} %pack_live_tokens.3), calls=%async_computation.7 | async-start | bytes 3145728 | tf_op jit(solution)/shard_map/all_to_all | solution.py:469
  13.6 0.2 select_reduce_fusion.4
  13.8 0.1 reduce_sum.116
  14.0 0.1 fusion.69
  14.1 0.1 select_reduce_fusion.6
  14.2 0.1 reshape.303
  14.3 0.6 reduce_max.37
  14.9 0.1 reduce_sum.112
  15.0 0.7 reduce_max.36
  15.7 1.3 pad_add_fusion.1
  17.1 1.5 %collective-permute-start.2 = (s32[2]{0:T(128)S(1)}, s32[2]{0:T(128)S(1)}, u32[]{:S(2)}, u32[]{:S(2)}) collective-permute-start(s32[2]{0:T(128)S(1)} %pad_add_fusion.1), channel_id=1, source_target_pairs={{0,16},{16,0},{1,17},{17,1},{2,18},{18,2},{3,19},{19,3},{4,20},{20... | collective-permute-start | bytes 32 | tf_op jit(solution)/shard_map/ppermute | solution.py:515
  18.6 2.1 %collective-permute-start.3 = (bf16[2,8,32,128]{3,2,1,0:T(8,128)(2,1)S(1)}, bf16[2,8,32,128]{3,2,1,0:T(8,128)(2,1)S(1)}, u32[]{:S(2)}, u32[]{:S(2)}) collective-permute-start(bf16[2,8,32,128]{3,2,1,0:T(8,128)(2,1)S(1)} %pad_maximum_fusion.1), channel_id=1, source_target_pairs={{0,4},{2,6},{4,0},{6,2},{8,12},{10,14},{12,8},{14,10},{1,5},{3,7},... | collective-permute-start | bytes 393224 | tf_op jit(solution)/shard_map/ppermute | solution.py:415
  20.7 0.1 select_reduce_fusion.3
  20.8 0.3 select_reduce_fusion.2
  21.1 1.0 select_reduce_fusion
  22.1 1.6 %copy.28 = bf16[1024,4,256]{2,0,1:T(8,128)(2,1)} copy(bf16[1024,4,256]{2,1,0:T(4,128)(2,1)S(1)} %copy-done.13) | data formatting | bytes 4194304 | tf_op jit(solution)/shard_map/optimization_barrier | solution.py:464
  23.7 0.1 fusion.53
  23.8 18.3 %collective-permute-done.3 = bf16[2,8,32,128]{3,2,1,0:T(8,128)(2,1)S(1)} collective-permute-done((bf16[2,8,32,128]{3,2,1,0:T(8,128)(2,1)S(1)}, bf16[2,8,32,128]{3,2,1,0:T(8,128)(2,1)S(1)}, u32[]{:S(2)}, u32[]{:S(2)}) %collective-permute-start.3) | collective-permute-done | bytes 131104 | tf_op jit(solution)/shard_map/ppermute | solution.py:415
  42.2 1.3 %collective-permute-start.4 = (bf16[4,8,32,128]{3,2,1,0:T(8,128)(2,1)S(1)}, bf16[4,8,32,128]{3,2,1,0:T(8,128)(2,1)S(1)}, u32[]{:S(2)}, u32[]{:S(2)}) collective-permute-start(bf16[4,8,32,128]{3,2,1,0:T(8,128)(2,1)S(1)} %pad_maximum_fusion), channel_id=1, source_target_pairs={{0,2},{2,0},{4,6},{6,4},{8,10},{10,8},{12,14},{14,12},{1,3},{3,1},... | collective-permute-start | bytes 786440 | tf_op jit(solution)/shard_map/ppermute | solution.py:415
  43.5 1.3 %fusion.75 = s32[2]{0:T(128)S(1)} fusion(s32[2]{0:T(128)S(1)} %collective-permute-done.2, s32[1]{0:T(128)} %bitcast.10, s32[1]{0:T(128)} %bitcast.9), kind=kLoop, calls=%fused_computation.121 | loop fusion | flops 4 | bytes 24 | tf_op jit(solution)/shard_map/max | solution.py:514
  44.9 0.6 fusion.73
  46.1 0.1 concatenate.10.meta_ref
  46.2 3.2 %key_projection.2.refs_4_ = bf16[4,256,1024]{2,1,0:T(8,128)(2,1)S(1)} custom-call(bf16[32,32,128]{2,1,0:T(8,128)(2,1)S(1)} %bitcast.39, bf16[4,1024,256]{2,1,0:T(8,128)(2,1)} %bitcast.41), custom_call_target="tpu_custom_call" | custom-call | bytes 1024 | tf_op jit(solution)/shard_map/key_projection/pallas_call | solution.py:535
  49.4 0.6 collective-permute-done.4
  50.0 1.3 key_projection.3.refs_5_
  51.3 1.3 copy-done.4
  53.2 1.7 %conditional.2 = (bf16[256,1024]{1,0:T(8,128)(2,1)}, bf16[256,1024]{1,0:T(8,128)(2,1)}) conditional(s32[]{:T(128)} %bitcast.19, () %tuple.25, (s32[2]{0:T(128)S(1)}, s32[256]{0:T(256)S(1)}, s32[256]{0:T(256)S(1)}, bf16[256,8192]{1,0:T(8,128)(2,1)}) %tuple.57), branch_computations={%region_12.13_spmd, %region_13.14_spmd} | conditional | flops 134217728 | bytes 70254648 | solution.py:528
  53.3 0.9 broadcast.406.clone
  54.1 0.9 broadcast.406
  55.0 1.4 %collective-permute-done.5.refs_1_ = bf16[768,1024]{1,0:T(8,128)(2,1)} collective-permute-done((bf16[768,1024]{1,0:T(8,128)(2,1)}, bf16[768,1024]{1,0:T(8,128)(2,1)}, u32[]{:S(2)}, u32[]{:S(2)}) %collective-permute-start.5) | collective-permute-done | bytes 1572896 | tf_op jit(solution)/shard_map/ppermute | solution.py:555
  56.4 1.6 %copy-done.5 = bf16[4,256,1024]{2,1,0:T(8,128)(2,1)S(1)} copy-done((bf16[4,256,1024]{2,1,0:T(8,128)(2,1)S(1)}, bf16[4,256,1024]{2,1,0:T(8,128)(2,1)}, u32[]{:S(2)}) %copy-start.5) | copy-done | bytes 2097176
  58.0 8.3 %prompt_scores.1 = (bf16[8,32,384]{2,1,0:T(8,128)(2,1)}, bf16[8,32,256]{2,1,0:T(8,128)(2,1)}) custom-call(s32[651]{0:T(1024)S(1)} %concatenate.10.meta_ref, bf16[768,1024]{1,0:T(8,128)(2,1)} %bitcast.12.refs_0_, bf16[768,1024]{1,0:T(8,128)(2,1)} %collective-permute-done.5.refs_1_, bf16[256,1024]{1,0:T(8,128)(2,1)} %get-tuple-element.124.refs_2_, ...), custom_call_target="tpu_custom_call" | custom-call | tf_op jit(solution)/shard_map/prompt_scores/pallas_call | solution.py:576
  66.3 37.4 %conditional.3 = (bf16[4,2,4,64,128]{4,3,2,1,0:T(8,128)(2,1)}, f32[8,32,128]{2,1,0:T(8,128)S(1)}) conditional(s32[]{:T(128)} %bitcast.11, (bf16[8,32,384]{2,1,0:T(8,128)(2,1)}, s32[1,640]{1,0:T(1,128)S(1)}, s32[8]{0:T(128)S(1)}, bf16[8,32,128]{2,1,0:T(8,128)(2,1)S(1)}, bf16[8,256,4,256]{3,2,1,0:T(4,128)(2,1)}, /*index=5*/s32[651]{0:T(1024)S(1)}, ...), branch_computations={%region_14.17_spmd, %region_17.20_spmd} | conditional | flops 34047488 | bytes 157389072 | solution.py:684
  66.4 5.7 %all-to-all-start.1 = ((bf16[8,32,384]{2,1,0:T(8,128)(2,1)}), bf16[8,32,384]{2,1,0:T(8,128)(2,1)S(1)}, u32[]{:S(2)}, u32[]{:S(2)}) async-start(bf16[8,32,384]{2,1,0:T(8,128)(2,1)} %get-tuple-element.68), calls=%async_computation.1 | async-start | bytes 393216 | tf_op jit(solution)/shard_map/cond/branch_0_fun/all_to_all | solution.py:612
  72.1 3.0 %copy.25 = bf16[8,256,4,256]{3,1,2,0:T(8,128)(2,1)S(1)} copy(bf16[8,256,4,256]{3,2,1,0:T(4,128)(2,1)} %get-tuple-element.189) | data formatting | bytes 8388608 | tf_op jit(solution)/shard_map
  75.1 0.7 fusion.71
  75.8 1.3 copy-done.11
  77.1 0.1 broadcast_in_dim.162.refs_2_
  77.2 0.2 fusion.17
  77.5 0.1 broadcast_in_dim.163.refs_3_
  77.6 2.7 %all-to-all-done.1.refs_0_ = bf16[8,32,384]{2,1,0:T(8,128)(2,1)S(1)} async-done(((bf16[8,32,384]{2,1,0:T(8,128)(2,1)}), bf16[8,32,384]{2,1,0:T(8,128)(2,1)S(1)}, u32[]{:S(2)}, u32[]{:S(2)}) %all-to-all-start.1) | async-done | bytes 196640 | tf_op jit(solution)/shard_map/cond/branch_0_fun/all_to_all | solution.py:612
  80.3 1.7 %softmax_weights.2 = (bf16[8,32,384]{2,1,0:T(8,128)(2,1)}, f32[8,32,1]{2,1,0:T(8,128)S(1)}) custom-call(bf16[8,32,384]{2,1,0:T(8,128)(2,1)S(1)} %all-to-all-done.1.refs_0_, s32[1,384]{1,0:T(1,128)S(1)} %slice.18.refs_1_, f32[8,32,1]{2,1,0:T(8,128)S(1)} %broadcast_in_dim.162.refs_2_, f32[8,32,1]{2,1,0:T(8,128)S(1)} %broadcast_in_dim.163.refs_3_), custom_call_target="tpu_custom_call" | custom-call | tf_op jit(solution)/shard_map/cond/branch_0_fun/softmax_weights/pallas_call | solution.py:626
  82.0 3.4 %all-to-all-start.2 = ((bf16[8,32,384]{2,1,0:T(8,128)(2,1)}), bf16[8,32,384]{2,1,0:T(8,128)(2,1)S(1)}, u32[]{:S(2)}, u32[]{:S(2)}) async-start(bf16[8,32,384]{2,1,0:T(8,128)(2,1)} %get-tuple-element.73.refs_4_), calls=%async_computation.2 | async-start | bytes 393216 | tf_op jit(solution)/shard_map/cond/branch_0_fun/all_to_all | solution.py:657
  85.4 0.1 reduce
  85.5 3.6 %owner_lists.2.refs_2_ = bf16[8,640,1024]{2,1,0:T(8,128)(2,1)S(1)} custom-call(s32[651]{0:T(1024)S(1)} %get-tuple-element.67.meta_ref, bf16[768,1024]{1,0:T(8,128)(2,1)} %get-tuple-element.75.refs_0_, bf16[768,1024]{1,0:T(8,128)(2,1)} %get-tuple-element.76.refs_1_, bf16[256,1024]{1,0:T(8,128)(2,1)} %get-tuple-element.77.refs_2_, ...), custom_call_target="tpu_custom_call" | custom-call | bytes 16777216 | tf_op jit(solution)/shard_map/cond/branch_0_fun/owner_lists/pallas_call | solution.py:637
  89.1 4.0 %copy-done.2 = bf16[8,640,1024]{2,1,0:T(8,128)(2,1)} copy-done((bf16[8,640,1024]{2,1,0:T(8,128)(2,1)}, bf16[8,640,1024]{2,1,0:T(8,128)(2,1)S(1)}, u32[]{:S(2)}) %copy-start.2) | copy-done | bytes 10485784 | tf_op jit(solution)/shard_map/cond
  93.1 0.4 fusion.13
  93.6 4.0 %copy-done.3 = bf16[8,640,1024]{2,1,0:T(8,128)(2,1)S(1)} copy-done((bf16[8,640,1024]{2,1,0:T(8,128)(2,1)S(1)}, bf16[8,640,1024]{2,1,0:T(8,128)(2,1)}, u32[]{:S(2)}) %copy-start.3) | copy-done | bytes 10485784 | tf_op jit(solution)/shard_map/cond
  97.5 6.1 %weighted_values.2 = bf16[4,2,4,64,128]{4,3,2,1,0:T(8,128)(2,1)} custom-call(s32[651]{0:T(1024)S(1)} %get-tuple-element.67.meta_ref, bf16[8,32,384]{2,1,0:T(8,128)(2,1)S(1)} %all-to-all-done.2.refs_0_, s32[8,1,640]{2,1,0:T(1,128)S(1)} %get-tuple-element.74.refs_1_, bf16[8,640,1024]{2,1,0:T(8,128)(2,1)S(1)} %copy-done.3, bf16[4,1024,256]{2,1,0:T(8,128)(2,1)S(1)} %copy-done.8), custom_call_target="tpu_custom_call" | custom-call | tf_op jit(solution)/shard_map/cond/branch_0_fun/weighted_values/pallas_call | solution.py:664
  103.8 4.1 %all-to-all-start.8 = ((bf16[4,2,4,64,128]{4,3,2,1,0:T(8,128)(2,1)}), bf16[4,2,4,64,128]{4,3,2,1,0:T(8,128)(2,1)S(1)}, u32[]{:S(2)}, u32[]{:S(2)}) async-start(bf16[4,2,4,64,128]{4,3,2,1,0:T(8,128)(2,1)} %get-tuple-element.131), calls=%async_computation.8 | async-start | bytes 1048576 | tf_op jit(solution)/shard_map/all_to_all | solution.py:691
  107.9 7.2 %all-to-all-done.8.parts_ref = bf16[4,2,4,64,128]{4,3,2,1,0:T(8,128)(2,1)S(1)} async-done(((bf16[4,2,4,64,128]{4,3,2,1,0:T(8,128)(2,1)}), bf16[4,2,4,64,128]{4,3,2,1,0:T(8,128)(2,1)S(1)}, u32[]{:S(2)}, u32[]{:S(2)}) %all-to-all-start.8) | async-done | bytes 524320 | tf_op jit(solution)/shard_map/all_to_all | solution.py:691
  115.1 0.1 half_pool_sum.1
  115.2 2.5 %collective-permute-start.6 = (bf16[2,4,64,128]{3,2,1,0:T(8,128)(2,1)S(1)}, bf16[2,4,64,128]{3,2,1,0:T(8,128)(2,1)S(1)}, u32[]{:S(2)}, u32[]{:S(2)}) collective-permute-start(bf16[2,4,64,128]{3,2,1,0:T(8,128)(2,1)S(1)} %get-tuple-element.134.after_ref), channel_id=1, source_target_pairs={{0,8},{2,10},{4,12},{6,14},{8,0},{10,2},{12,4},{14,6},{1,9},{3,11}... | collective-permute-start | bytes 393224 | tf_op jit(solution)/shard_map/ppermute | solution.py:415
  117.7 5.3 %collective-permute-done.6.got_ref = bf16[2,4,64,128]{3,2,1,0:T(8,128)(2,1)S(1)} collective-permute-done((bf16[2,4,64,128]{3,2,1,0:T(8,128)(2,1)S(1)}, bf16[2,4,64,128]{3,2,1,0:T(8,128)(2,1)S(1)}, u32[]{:S(2)}, u32[]{:S(2)}) %collective-permute-start.6) | collective-permute-done | bytes 131104 | tf_op jit(solution)/shard_map/ppermute | solution.py:415
  123.1 0.7 collective-permute-start.9
  123.9 1.8 %collective-permute-start.8 = (bf16[16,4096]{1,0:T(8,128)(2,1)S(1)}, bf16[16,4096]{1,0:T(8,128)(2,1)S(1)}, u32[]{:S(2)}, u32[]{:S(2)}) collective-permute-start(bf16[16,4096]{1,0:T(8,128)(2,1)S(1)} %attended_sum.1), channel_id=1, source_target_pairs={{0,4},{2,6},{4,0},{6,2},{8,12},{10,14},{12,8},{14,10},{1,5},{3,7},... | collective-permute-start | bytes 393224 | tf_op jit(solution)/shard_map/ppermute | solution.py:415
  125.7 1.0 collective-permute-start.7
  126.7 3.4 %copy-done.6 = bf16[4096,1024]{1,0:T(8,128)(2,1)S(1)} copy-done((bf16[4096,1024]{1,0:T(8,128)(2,1)S(1)}, bf16[4096,1024]{1,0:T(8,128)(2,1)}, u32[]{:S(2)}) %copy-start.6) | copy-done | bytes 8388632
  130.1 0.6 stage_out_weight.1
  130.8 1.6 %fusion.43 = f32[64,1024]{1,0:T(8,128)S(1)} fusion(bf16[4096,1024]{1,0:T(8,128)(2,1)S(1)} %stage_out_weight.1, bf16[16,4096]{1,0:T(8,128)(2,1)S(1)} %collective-permute-done.9, bf16[16,4096]{1,0:T(8,128)(2,1)S(1)} %collective-permute-done.8, bf16[16,4096]{1,0:T(8,128)(2,1)S(1)} %collective-permute-done.7, bf16[16,4096]{1,0:T(8,128)(2,1)S(1)} %attended_sum.1), kind=kOutput, calls=%fused_computation.33 | convolution fusion | flops 538968064 | bytes 9175040 | tf_op jit(solution)/shard_map/dot_general | solution.py:727
  132.5 1.3 collective-permute-done.10.got_ref
  133.8 0.6 order_rows.1
  (52 shorter events, 0.7 us)
Async XLA Ops:
  0.0 9.1 %collective-permute-start.1 = (bf16[8,32,128]{2,1,0:T(8,128)(2,1)}, bf16[8,32,128]{2,1,0:T(8,128)(2,1)S(1)}, u32[]{:S(2)}, u32[]{:S(2)}) collective-permute-start(bf16[8,32,128]{2,1,0:T(8,128)(2,1)} %param.18), channel_id=1, source_target_pairs={{0,8},{2,10},{4,12},{6,14},{8,0},{10,2},{12,4},{14,6},{1,9},{3,11}... | collective-permute-start | bytes 196616 | tf_op jit(solution)/shard_map/ppermute | solution.py:415
  4.1 9.4 %copy-start.16 = (s32[256]{0:T(256)S(1)}, s32[256]{0:T(256)}, u32[]{:S(2)}) copy-start(s32[256]{0:T(256)} %fill_ref.1) | copy-start | bytes 3076
  4.1 9.5 %copy-start.15 = (s32[256,1]{0,1:T(1,128)S(1)}, s32[256,1]{0,1:T(1,128)}, u32[]{:S(2)}) copy-start(s32[256,1]{0,1:T(1,128)} %param.15) | copy-start | bytes 3076
  4.1 14.4 %copy-start.14 = (bf16[8,32,128]{2,1,0:T(8,128)(2,1)S(1)}, bf16[8,32,128]{2,1,0:T(8,128)(2,1)}, u32[]{:S(2)}) copy-start(bf16[8,32,128]{2,1,0:T(8,128)(2,1)} %param.18) | copy-start | bytes 196612
  4.1 16.5 %copy-start.18 = (s32[256]{0:T(256)S(1)}, s32[256]{0:T(256)}, u32[]{:S(2)}) copy-start(s32[256]{0:T(256)} %param.16) | copy-start | bytes 3076
  4.2 18.0 %copy-start.13 = (bf16[1024,4,256]{2,1,0:T(4,128)(2,1)S(1)}, bf16[1024,4,256]{2,1,0:T(4,128)(2,1)}, u32[]{:S(2)}) copy-start(bf16[1024,4,256]{2,1,0:T(4,128)(2,1)} %param.14) | copy-start | bytes 6291460
  9.1 43.6 %all-to-all-start.7 = ((bf16[8,96,1024]{2,1,0:T(8,128)(2,1)}), bf16[8,96,1024]{2,1,0:T(8,128)(2,1)}, u32[]{:S(2)}, u32[]{:S(2)}) async-start(bf16[8,96,1024]{2,1,0:T(8,128)(2,1)} %pack_live_tokens.3), calls=%async_computation.7 | async-start | bytes 3145728 | tf_op jit(solution)/shard_map/all_to_all | solution.py:469
  17.1 26.4 %collective-permute-start.2 = (s32[2]{0:T(128)S(1)}, s32[2]{0:T(128)S(1)}, u32[]{:S(2)}, u32[]{:S(2)}) collective-permute-start(s32[2]{0:T(128)S(1)} %pad_add_fusion.1), channel_id=1, source_target_pairs={{0,16},{16,0},{1,17},{17,1},{2,18},{18,2},{3,19},{19,3},{4,20},{20... | collective-permute-start | bytes 32 | tf_op jit(solution)/shard_map/ppermute | solution.py:515
  18.6 23.5 %collective-permute-start.3 = (bf16[2,8,32,128]{3,2,1,0:T(8,128)(2,1)S(1)}, bf16[2,8,32,128]{3,2,1,0:T(8,128)(2,1)S(1)}, u32[]{:S(2)}, u32[]{:S(2)}) collective-permute-start(bf16[2,8,32,128]{3,2,1,0:T(8,128)(2,1)S(1)} %pad_maximum_fusion.1), channel_id=1, source_target_pairs={{0,4},{2,6},{4,0},{6,2},{8,12},{10,14},{12,8},{14,10},{1,5},{3,7},... | collective-permute-start | bytes 393224 | tf_op jit(solution)/shard_map/ppermute | solution.py:415
  42.2 7.9 %collective-permute-start.4 = (bf16[4,8,32,128]{3,2,1,0:T(8,128)(2,1)S(1)}, bf16[4,8,32,128]{3,2,1,0:T(8,128)(2,1)S(1)}, u32[]{:S(2)}, u32[]{:S(2)}) collective-permute-start(bf16[4,8,32,128]{3,2,1,0:T(8,128)(2,1)S(1)} %pad_maximum_fusion), channel_id=1, source_target_pairs={{0,2},{2,0},{4,6},{6,4},{8,10},{10,8},{12,14},{14,12},{1,3},{3,1},... | collective-permute-start | bytes 786440 | tf_op jit(solution)/shard_map/ppermute | solution.py:415
  46.2 3.9 %copy-start.7 = (bf16[1024,4,256]{2,0,1:T(8,128)(2,1)S(1)}, bf16[1024,4,256]{2,0,1:T(8,128)(2,1)}, u32[]{:S(2)}) copy-start(bf16[1024,4,256]{2,0,1:T(8,128)(2,1)} %copy.28) | copy-start | bytes 6291460
  51.3 1.3 copy-start.4
  52.7 3.8 %collective-permute-start.5 = (bf16[768,1024]{1,0:T(8,128)(2,1)}, bf16[768,1024]{1,0:T(8,128)(2,1)}, u32[]{:S(2)}, u32[]{:S(2)}) collective-permute-start(bf16[768,1024]{1,0:T(8,128)(2,1)} %bitcast.12.refs_0_), channel_id=1, source_target_pairs={{0,1},{1,0},{2,3},{3,2},{4,5},{5,4},{6,7},{7,6},{8,9},{9,8},{10,11... | collective-permute-start | bytes 4718600 | tf_op jit(solution)/shard_map/ppermute | solution.py:555
  56.4 1.6 %copy-start.5 = (bf16[4,256,1024]{2,1,0:T(8,128)(2,1)S(1)}, bf16[4,256,1024]{2,1,0:T(8,128)(2,1)}, u32[]{:S(2)}) copy-start(bf16[4,256,1024]{2,1,0:T(8,128)(2,1)} %copy-done.4) | copy-start | bytes 6291460
  58.0 8.3 %copy-start.17 = (s32[8]{0:T(128)S(1)}, s32[8]{0:T(128)}, u32[]{:S(2)}) copy-start(s32[8]{0:T(128)} %param.20) | copy-start | bytes 100
  66.4 13.9 %all-to-all-start.1 = ((bf16[8,32,384]{2,1,0:T(8,128)(2,1)}), bf16[8,32,384]{2,1,0:T(8,128)(2,1)S(1)}, u32[]{:S(2)}, u32[]{:S(2)}) async-start(bf16[8,32,384]{2,1,0:T(8,128)(2,1)} %get-tuple-element.68), calls=%async_computation.1 | async-start | bytes 393216 | tf_op jit(solution)/shard_map/cond/branch_0_fun/all_to_all | solution.py:612
  75.1 2.1 %copy-start.11 = (bf16[8,256,4,256]{3,1,2,0:T(8,128)(2,1)}, bf16[8,256,4,256]{3,1,2,0:T(8,128)(2,1)S(1)}, u32[]{:S(2)}) copy-start(bf16[8,256,4,256]{3,1,2,0:T(8,128)(2,1)S(1)} %copy.25) | copy-start | bytes 12582916 | tf_op jit(solution)/shard_map/cond
  82.0 11.5 %all-to-all-start.2 = ((bf16[8,32,384]{2,1,0:T(8,128)(2,1)}), bf16[8,32,384]{2,1,0:T(8,128)(2,1)S(1)}, u32[]{:S(2)}, u32[]{:S(2)}) async-start(bf16[8,32,384]{2,1,0:T(8,128)(2,1)} %get-tuple-element.73.refs_4_), calls=%async_computation.2 | async-start | bytes 393216 | tf_op jit(solution)/shard_map/cond/branch_0_fun/all_to_all | solution.py:657
  85.5 7.6 %copy-start.12 = (bf16[8,256,4,256]{3,1,2,0:T(8,128)(2,1)S(1)}, bf16[8,256,4,256]{3,1,2,0:T(8,128)(2,1)}, u32[]{:S(2)}) copy-start(bf16[8,256,4,256]{3,1,2,0:T(8,128)(2,1)} %copy-done.11) | copy-start | bytes 12582916 | tf_op jit(solution)/shard_map/cond
  85.5 8.0 %copy-start.8 = (bf16[4,1024,256]{2,1,0:T(8,128)(2,1)S(1)}, bf16[4,1024,256]{2,1,0:T(8,128)(2,1)}, u32[]{:S(2)}) copy-start(bf16[4,1024,256]{2,1,0:T(8,128)(2,1)} %get-tuple-element.79.refs_3_) | copy-start | bytes 6291460 | tf_op jit(solution)/shard_map/cond
  89.1 4.0 %copy-start.2 = (bf16[8,640,1024]{2,1,0:T(8,128)(2,1)}, bf16[8,640,1024]{2,1,0:T(8,128)(2,1)S(1)}, u32[]{:S(2)}) copy-start(bf16[8,640,1024]{2,1,0:T(8,128)(2,1)S(1)} %owner_lists.2.refs_2_) | copy-start | bytes 31457284 | tf_op jit(solution)/shard_map/cond
  93.5 4.0 %copy-start.3 = (bf16[8,640,1024]{2,1,0:T(8,128)(2,1)S(1)}, bf16[8,640,1024]{2,1,0:T(8,128)(2,1)}, u32[]{:S(2)}) copy-start(bf16[8,640,1024]{2,1,0:T(8,128)(2,1)} %copy-done.2) | copy-start | bytes 31457284 | tf_op jit(solution)/shard_map/cond
  103.8 11.3 %all-to-all-start.8 = ((bf16[4,2,4,64,128]{4,3,2,1,0:T(8,128)(2,1)}), bf16[4,2,4,64,128]{4,3,2,1,0:T(8,128)(2,1)S(1)}, u32[]{:S(2)}, u32[]{:S(2)}) async-start(bf16[4,2,4,64,128]{4,3,2,1,0:T(8,128)(2,1)} %get-tuple-element.131), calls=%async_computation.8 | async-start | bytes 1048576 | tf_op jit(solution)/shard_map/all_to_all | solution.py:691
  115.2 7.9 %collective-permute-start.6 = (bf16[2,4,64,128]{3,2,1,0:T(8,128)(2,1)S(1)}, bf16[2,4,64,128]{3,2,1,0:T(8,128)(2,1)S(1)}, u32[]{:S(2)}, u32[]{:S(2)}) collective-permute-start(bf16[2,4,64,128]{3,2,1,0:T(8,128)(2,1)S(1)} %get-tuple-element.134.after_ref), channel_id=1, source_target_pairs={{0,8},{2,10},{4,12},{6,14},{8,0},{10,2},{12,4},{14,6},{1,9},{3,11}... | collective-permute-start | bytes 393224 | tf_op jit(solution)/shard_map/ppermute | solution.py:415
  123.1 7.6 %collective-permute-start.9 = (bf16[16,4096]{1,0:T(8,128)(2,1)S(1)}, bf16[16,4096]{1,0:T(8,128)(2,1)S(1)}, u32[]{:S(2)}, u32[]{:S(2)}) collective-permute-start(bf16[16,4096]{1,0:T(8,128)(2,1)S(1)} %attended_sum.1), channel_id=1, source_target_pairs={{0,6},{2,4},{4,2},{6,0},{8,14},{10,12},{12,10},{14,8},{1,7},{3,5},... | collective-permute-start | bytes 393224 | tf_op jit(solution)/shard_map/ppermute | solution.py:415
  123.9 6.9 %collective-permute-start.8 = (bf16[16,4096]{1,0:T(8,128)(2,1)S(1)}, bf16[16,4096]{1,0:T(8,128)(2,1)S(1)}, u32[]{:S(2)}, u32[]{:S(2)}) collective-permute-start(bf16[16,4096]{1,0:T(8,128)(2,1)S(1)} %attended_sum.1), channel_id=1, source_target_pairs={{0,4},{2,6},{4,0},{6,2},{8,12},{10,14},{12,8},{14,10},{1,5},{3,7},... | collective-permute-start | bytes 393224 | tf_op jit(solution)/shard_map/ppermute | solution.py:415
  125.7 5.1 %collective-permute-start.7 = (bf16[16,4096]{1,0:T(8,128)(2,1)S(1)}, bf16[16,4096]{1,0:T(8,128)(2,1)S(1)}, u32[]{:S(2)}, u32[]{:S(2)}) collective-permute-start(bf16[16,4096]{1,0:T(8,128)(2,1)S(1)} %attended_sum.1), channel_id=1, source_target_pairs={{0,2},{2,0},{4,6},{6,4},{8,10},{10,8},{12,14},{14,12},{1,3},{3,1},... | collective-permute-start | bytes 393224 | tf_op jit(solution)/shard_map/ppermute | solution.py:415
  126.7 3.4 %copy-start.6 = (bf16[4096,1024]{1,0:T(8,128)(2,1)S(1)}, bf16[4096,1024]{1,0:T(8,128)(2,1)}, u32[]{:S(2)}) copy-start(bf16[4096,1024]{1,0:T(8,128)(2,1)} %weight_ref.1) | copy-start | bytes 25165828
  132.4 1.4 %collective-permute-start.10 = (f32[64,512]{1,0:T(8,128)S(1)}, f32[64,512]{1,0:T(8,128)S(1)}, u32[]{:S(2)}, u32[]{:S(2)}) collective-permute-start(f32[64,512]{1,0:T(8,128)S(1)} %get-tuple-element.222), channel_id=1, source_target_pairs={{0,1},{1,0},{2,3},{3,2},{4,5},{5,4},{6,7},{7,6},{8,9},{9,8},{10,11... | collective-permute-start | bytes 393224 | tf_op jit(solution)/shard_map/ppermute | solution.py:734

commit v16 on v15

--- a/solution.py
+++ b/solution.py
@@ -180,31 +180,37 @@
     groups = lanes // BLK
     at_size = n * groups
     q = meta_ref[at_size + n] ^ reversed_bits(step, n)
-    kvh, per = keyed.shape[0], keyed.shape[1] * 2 // n
+    kvh, per = keyed.shape[0], keyed.shape[1] // n
     group = per // rows
 
-    even_ref, odd_ref = keyed_refs
-    load = [
-        pltpu.make_async_copy(even_ref.at[h], keyed.at[h], keyed_sem.at[h]) for h in range(kvh)
-    ]
+    def load(i):
+        span = n // 2 * per
+        return [
+            pltpu.make_async_copy(
+                keyed_refs[i].at[h], keyed.at[h, pl.ds(i * span, span)], keyed_sem.at[i, h]
+            )
+            for h in range(kvh)
+        ]
 
     @pl.when(step == 0)
     def _():
         load_tokens(
-            n, meta_ref[at_size + n + 1], meta_ref[at_size + n + 2], x_refs, [x_refs[1]], held, more,
-            wide, sem, load,
+            n, meta_ref[at_size + n + 1], meta_ref[at_size + n + 2], x_refs, [], held, more, wide, sem,
+            load(0) + load(1),
         )
-        for copy in load:
-            copy.wait()
-
-    at = pl.ds(pl.multiple_of(step % (n // 2) * per, per), per)
-    query = jnp.where(step < n // 2, keyed[:, at, :], odd_ref[:, at, :])
+
+    for i in range(2):
+
+        @pl.when(step == i * (n // 2))
+        def _(i=i):
+            for copy in load(i):
+                copy.wait()
 
     def one(t):
         here = slice(cuts[t], cuts[t + 1])
         count = (cuts[t + 1] - cuts[t]) // BLK
         raw = lax.dot_general(
-            query.reshape(kvh * per, part),
+            keyed[:, pl.ds(pl.multiple_of(step * per, per), per), :].reshape(kvh * per, part),
             list_tile(meta_ref, q * groups + cuts[t] // BLK, count, wide, tile),
             (((1,), (1,)), ((), ())),
             preferred_element_type=jnp.float32,
@@ -255,13 +261,26 @@
             w_ref[i] = w.astype(w_ref.dtype)
 
 
+def list_copies(n, lanes, sizes, source, target, sem):
+    cuts = tile_cuts(lanes)
+
+    def copies(o):
+        for t in range(len(cuts) - 1):
+            here = pl.ds(cuts[t], cuts[t + 1] - cuts[t])
+            copy = pltpu.make_async_copy(source.at[o, here], target.at[o, here], sem.at[o, t])
+            yield (True if t == 0 else sizes(o) > cuts[t]), copy
+
+    return copies
+
+
 def list_kernel(n, meta_ref, *refs):
-    x_refs, (_, out_ref, held, more, wide, sem) = refs[:4], refs[4:]
+    x_refs, (_, out_ref, held, more, wide, lists, sem, out_sem) = refs[:4], refs[4:]
     q = pl.program_id(0)
-    lanes = out_ref.shape[1]
+    lanes = lists.shape[1]
     cuts = tile_cuts(lanes)
     groups = lanes // BLK
     at_size = n * groups
+    copies = list_copies(n, lanes, lambda o: meta_ref[at_size + o], lists, out_ref, out_sem)
 
     @pl.when(q == 0)
     def _():
@@ -270,20 +289,26 @@
             sem, [],
         )
 
-    def one(t):
-        list_tile(
-            meta_ref, q * groups + cuts[t] // BLK, (cuts[t + 1] - cuts[t]) // BLK, wide,
-            out_ref.at[q, cuts[t] : cuts[t + 1]],
-        )
-
-    one(0)
-    for t in range(1, len(cuts) - 1):
-        pl.when(meta_ref[at_size + q] > cuts[t])(functools.partial(one, t))
+    for t, (used, copy) in enumerate(copies(q)):
+
+        @pl.when(used)
+        def _(t=t, copy=copy):
+            list_tile(
+                meta_ref, q * groups + cuts[t] // BLK, (cuts[t + 1] - cuts[t]) // BLK, wide,
+                lists.at[q, cuts[t] : cuts[t + 1]],
+            )
+            copy.start()
+
+    @pl.when(q == n - 1)
+    def _():
+        for o in range(n):
+            for used, copy in copies(o):
+                pl.when(used)(copy.wait)
 
 
 def value_kernel(n, rows, count, meta_ref, *refs):
     w_refs, (row_ref, list_ref, weight_ref, out_ref) = refs[:count], refs[count : count + 4]
-    values, acc, mixed, value_sem = refs[count + 4 :]
+    values, lists, acc, mixed, value_sem, sem = refs[count + 4 :]
     q = pl.program_id(0)
     kvh, _, hd = values.shape
     load_values = [
@@ -293,15 +318,32 @@
         for h in range(kvh)
     ]
     _, heads, near = w_refs[0].shape
-    lanes = list_ref.shape[1]
+    lanes = lists.shape[1]
     per = rows * heads // kvh
     cuts = tile_cuts(lanes)
-    size = meta_ref[n * lanes // BLK + q]
+    at_size = n * lanes // BLK
+    size = meta_ref[at_size + q]
+    copies = list_copies(n, lanes, lambda o: meta_ref[at_size + o], list_ref, lists, sem)
+    ahead = min(3, n)
+
+    def fetch(o):
+        for used, copy in copies(o):
+            pl.when(used)(copy.start)
 
     @pl.when(q == 0)
+    def _():
+        for o in range(ahead):
+            fetch(o)
+
+    pl.when(q + ahead < n)(lambda: fetch(jnp.minimum(q + ahead, n - 1)))
+
+    @pl.when(q == n // 2)
     def _():
         for load in load_values:
             load.start()
+
+    for used, copy in copies(q):
+        pl.when(used)(copy.wait)
 
     def one(t):
         here = slice(cuts[t], cuts[t + 1])
@@ -314,7 +356,7 @@
             [jnp.where((owner_row == r)[None, None], weights, 0.0) for r in range(rows)], 1
         ).reshape(kvh * per, width)
         got = jnp.dot(
-            spread.astype(jnp.bfloat16), list_ref[q, here, :], preferred_element_type=jnp.float32
+            spread.astype(jnp.bfloat16), lists[q, here, :], preferred_element_type=jnp.float32
         )
         if t == 0:
             pl.when(size <= cuts[1])(lambda: keep(got))
@@ -565,6 +607,7 @@
     in_vmem = pl.BlockSpec(memory_space=pltpu.VMEM)
     x_parts = (mine, other, more_mine, more_other)
     x_scratch = [
+        pltpu.VMEM((ntp, n * size, part), jnp.bfloat16),
         pltpu.VMEM((ntp, n * extra, part), jnp.bfloat16),
         pltpu.VMEM((n * tokens, part), jnp.float32),
     ]
@@ -579,12 +622,7 @@
             num_scalar_prefetch=1,
             grid=(n,),
             in_specs=[
-                anywhere,
-                in_vmem,
-                anywhere,
-                anywhere,
-                anywhere,
-                in_vmem,
+                *[anywhere] * 6,
                 pl.BlockSpec((1, 1, lanes), lambda i, m: (owner(i, m), 0, 0)),
             ],
             out_specs=[
@@ -592,12 +630,11 @@
                 for length in (near, lanes - near)
             ],
             scratch_shapes=[
-                pltpu.VMEM((1, n * size, part), jnp.bfloat16),
                 *x_scratch,
                 pltpu.VMEM((tile_cuts(lanes)[1], part), jnp.bfloat16),
-                pltpu.VMEM((kvh, n // 2 * per, part), jnp.bfloat16),
+                pltpu.VMEM((kvh, n * per, part), jnp.bfloat16),
                 pltpu.SemaphoreType.DMA((ntp, 4)),
-                pltpu.SemaphoreType.DMA((kvh,)),
+                pltpu.SemaphoreType.DMA((2, kvh)),
             ],
         ),
         out_shape=slot_shapes,
@@ -640,15 +677,16 @@
                 num_scalar_prefetch=1,
                 grid=(n,),
                 in_specs=[anywhere] * 5,
-                out_specs=in_vmem,
+                out_specs=anywhere,
                 scratch_shapes=[
-                    pltpu.VMEM((ntp, n * size, part), jnp.bfloat16),
                     *x_scratch,
+                    pltpu.VMEM((n, lanes, part), jnp.bfloat16),
                     pltpu.SemaphoreType.DMA((ntp, 4)),
+                    pltpu.SemaphoreType.DMA((n, len(tile_cuts(lanes)) - 1)),
                 ],
             ),
             out_shape=jax.ShapeDtypeStruct((n, lanes, part), jnp.bfloat16),
-            compiler_params=pltpu.CompilerParams(vmem_limit_bytes=28 * MIB),
+            compiler_params=pltpu.CompilerParams(vmem_limit_bytes=56 * MIB),
             cost_estimate=pl.CostEstimate(
                 flops=0, bytes_accessed=16 * MIB, transcendentals=0
             ),
@@ -666,17 +704,19 @@
             grid_spec=pltpu.PrefetchScalarGridSpec(
                 num_scalar_prefetch=1,
                 grid=(n,),
-                in_specs=[*slot_specs[:count], row_spec, in_vmem, anywhere],
+                in_specs=[*slot_specs[:count], row_spec, anywhere, anywhere],
                 out_specs=pl.BlockSpec((n // 2, 2, kvh, per, hd), lambda q, m: (0, 0, 0, 0, 0)),
                 scratch_shapes=[
                     pltpu.VMEM((kvh, part, hd), jnp.bfloat16),
+                    pltpu.VMEM((n, lanes, part), jnp.bfloat16),
                     pltpu.VMEM((kvh * per, part), jnp.float32),
                     pltpu.VMEM((kvh, n * per, part), jnp.bfloat16),
                     pltpu.SemaphoreType.DMA((kvh,)),
+                    pltpu.SemaphoreType.DMA((n, len(tile_cuts(lanes)) - 1)),
                 ],
             ),
             out_shape=jax.ShapeDtypeStruct((n // 2, 2, kvh, per, hd), jnp.bfloat16),
-            compiler_params=pltpu.CompilerParams(vmem_limit_bytes=16 * MIB),
+            compiler_params=pltpu.CompilerParams(vmem_limit_bytes=56 * MIB),
             name="weighted_values",
         )(meta, *weights, rowof, lists, kv_weight)
         return terms, cached.reshape(rows, heads, hd) * share

time: 135 us -> 133 us (0.985)
  local copies, waits for them, and re-layouts: 23 us -> 15.9 us
  Pallas kernels: 30.6 us -> 34.9 us
    cond x10 -> x8, local copies, waits for them, and re-layouts: 9.27 us -> 2 us
    pallas_call x1, Pallas kernels: 6.07 us -> 9.37 us  [exchange_weights(): pl.pallas_call(functools.partial(value_kernel, n, rows, count), grid_spec...]
    pallas_call x1, Pallas kernels: 3.6 us -> 5.54 us  [exchange_weights(): pl.pallas_call(functools.partial(list_kernel, n), grid_spec=pltpu.Prefetc...]
    all_to_all x1, waiting for transfers between devices: 0.01 us -> 1.43 us  [exchange_weights(): weights = [lax.all_to_all(w, 'pool', 0, 0, tiled=True) for w in weights]]
  transfers between devices with their start and end apart: 14 -> 14, of which waited for: 7 -> 9; matrix products, arithmetic and copies ran while one was open for 11% -> 11% of each run, Pallas kernels for 10% -> 12%
where the time goes in v16:
time: 133 us; the launch traced here: 132 us
  waiting for transfers between devices  38.1 us (29%)
  Pallas kernels  34.9 us (26%)
  starting transfers between devices  31.8 us (24%)
  local copies, waits for them, and re-layouts  15.9 us (12%)
  other arithmetic  6.45 us (5%)
  matrix products  2.77 us (2%)
  between operations  1.54 us (1%)
    ppermute x7, waiting for transfers between devices, with_partner(): return lax.ppermute(x, 'pool', [(i, i ^ k) for i in range(n)])  24.6 us
    ppermute x7, starting transfers between devices, with_partner(): return lax.ppermute(x, 'pool', [(i, i ^ k) for i in range(n)])  13.2 us
    pallas_call x1, Pallas kernels, exchange_weights(): pl.pallas_call(functools.partial(value_kernel, n, rows, count), grid_spec...  9.37 us
    pallas_call x1, Pallas kernels, local(): pl.pallas_call(functools.partial(score_kernel, n, rows), grid_spec=pltpu....  7.44 us
    all_to_all x1, waiting for transfers between devices, local(): lax.all_to_all(terms, 'pool', 0, 0, axis_index_groups=halves, tiled=True)  6.61 us
    unnamed x20, local copies, waits for them, and re-layouts  6.34 us
    all_to_all x1, starting transfers between devices, exchange_weights(): parts = [lax.all_to_all(s, 'pool', 0, 0, tiled=True) for s in scores]  5.65 us
    pallas_call x1, Pallas kernels, exchange_weights(): pl.pallas_call(functools.partial(list_kernel, n), grid_spec=pltpu.Prefetc...  5.54 us
  transfers between devices with their start and end apart: 14, of which 9 were waited for; matrix products, arithmetic and copies ran while one was open for 11% of the time, Pallas kernels for 12%

profile of v16, /device:TPU:0, one launch (start us, length us, event | category | flops | bytes accessed | tf_op | source)
XLA Modules:
  0.0 131.8 jit_solution(9461391269108568348)
XLA Ops:
  0.0 4.0 %collective-permute-start.1 = (bf16[8,32,128]{2,1,0:T(8,128)(2,1)}, bf16[8,32,128]{2,1,0:T(8,128)(2,1)S(1)}, u32[]{:S(2)}, u32[]{:S(2)}) collective-permute-start(bf16[8,32,128]{2,1,0:T(8,128)(2,1)} %param.18), channel_id=1, source_target_pairs={{0,8},{2,10},{4,12},{6,14},{8,0},{10,2},{12,4},{14,6},{1,9},{3,11}... | collective-permute-start | bytes 196616 | tf_op jit(solution)/shard_map/ppermute | solution.py:457
  4.2 4.9 %pack_live_tokens.3 = bf16[8,96,1024]{2,1,0:T(8,128)(2,1)} custom-call(s32[2]{0:T(128)S(1)} %pad_add_fusion.at_ref, s32[256]{0:T(256)} %fill_ref.1, s32[256]{0:T(256)} %bitcast.53, bf16[256,8192]{1,0:T(8,128)(2,1)} %x_ref.1), custom_call_target="tpu_custom_call" | custom-call | flops 402653184 | bytes 67108864 | tf_op jit(solution)/shard_map/pack_live_tokens/pallas_call | solution.py:62
  9.1 4.4 %all-to-all-start.7 = ((bf16[8,96,1024]{2,1,0:T(8,128)(2,1)}), bf16[8,96,1024]{2,1,0:T(8,128)(2,1)}, u32[]{:S(2)}, u32[]{:S(2)}) async-start(bf16[8,96,1024]{2,1,0:T(8,128)(2,1)} %pack_live_tokens.3), calls=%async_computation.7 | async-start | bytes 3145728 | tf_op jit(solution)/shard_map/all_to_all | solution.py:511
  13.6 0.2 select_reduce_fusion.4
  13.8 0.1 reduce_sum.116
  14.0 0.1 fusion.69
  14.1 0.1 select_reduce_fusion.6
  14.3 0.6 reduce_max.37
  14.9 0.1 reduce_sum.112
  15.0 0.6 reduce_max.36
  15.7 1.3 pad_add_fusion.1
  16.9 1.5 %collective-permute-start.2 = (s32[2]{0:T(128)S(1)}, s32[2]{0:T(128)S(1)}, u32[]{:S(2)}, u32[]{:S(2)}) collective-permute-start(s32[2]{0:T(128)S(1)} %pad_add_fusion.1), channel_id=1, source_target_pairs={{0,16},{16,0},{1,17},{17,1},{2,18},{18,2},{3,19},{19,3},{4,20},{20... | collective-permute-start | bytes 32 | tf_op jit(solution)/shard_map/ppermute | solution.py:557
  18.5 2.1 %collective-permute-start.3 = (bf16[2,8,32,128]{3,2,1,0:T(8,128)(2,1)S(1)}, bf16[2,8,32,128]{3,2,1,0:T(8,128)(2,1)S(1)}, u32[]{:S(2)}, u32[]{:S(2)}) collective-permute-start(bf16[2,8,32,128]{3,2,1,0:T(8,128)(2,1)S(1)} %pad_maximum_fusion.1), channel_id=1, source_target_pairs={{0,4},{2,6},{4,0},{6,2},{8,12},{10,14},{12,8},{14,10},{1,5},{3,7},... | collective-permute-start | bytes 393224 | tf_op jit(solution)/shard_map/ppermute | solution.py:457
  20.5 0.1 select_reduce_fusion.3
  20.6 0.3 select_reduce_fusion.2
  21.0 1.0 select_reduce_fusion
  22.0 1.6 %copy.28 = bf16[1024,4,256]{2,0,1:T(8,128)(2,1)} copy(bf16[1024,4,256]{2,1,0:T(4,128)(2,1)S(1)} %copy-done.9) | data formatting | bytes 4194304 | tf_op jit(solution)/shard_map/optimization_barrier | solution.py:506
  23.6 0.1 fusion.53
  23.7 18.4 %collective-permute-done.3 = bf16[2,8,32,128]{3,2,1,0:T(8,128)(2,1)S(1)} collective-permute-done((bf16[2,8,32,128]{3,2,1,0:T(8,128)(2,1)S(1)}, bf16[2,8,32,128]{3,2,1,0:T(8,128)(2,1)S(1)}, u32[]{:S(2)}, u32[]{:S(2)}) %collective-permute-start.3) | collective-permute-done | bytes 131104 | tf_op jit(solution)/shard_map/ppermute | solution.py:457
  42.2 1.3 %collective-permute-start.4 = (bf16[4,8,32,128]{3,2,1,0:T(8,128)(2,1)S(1)}, bf16[4,8,32,128]{3,2,1,0:T(8,128)(2,1)S(1)}, u32[]{:S(2)}, u32[]{:S(2)}) collective-permute-start(bf16[4,8,32,128]{3,2,1,0:T(8,128)(2,1)S(1)} %pad_maximum_fusion), channel_id=1, source_target_pairs={{0,2},{2,0},{4,6},{6,4},{8,10},{10,8},{12,14},{14,12},{1,3},{3,1},... | collective-permute-start | bytes 786440 | tf_op jit(solution)/shard_map/ppermute | solution.py:457
  43.5 1.3 fusion.75
  44.8 0.7 fusion.73
  46.1 0.1 concatenate.10.meta_ref
  46.2 3.2 %key_projection.2.refs_4_ = bf16[4,256,1024]{2,1,0:T(8,128)(2,1)S(1)} custom-call(bf16[32,32,128]{2,1,0:T(8,128)(2,1)S(1)} %bitcast.39, bf16[4,1024,256]{2,1,0:T(8,128)(2,1)} %bitcast.41), custom_call_target="tpu_custom_call" | custom-call | bytes 1024 | tf_op jit(solution)/shard_map/key_projection/pallas_call | solution.py:577
  49.4 0.6 collective-permute-done.4
  50.0 1.3 key_projection.3.refs_5_
  51.3 1.3 %copy-done = bf16[4,256,1024]{2,1,0:T(8,128)(2,1)} copy-done((bf16[4,256,1024]{2,1,0:T(8,128)(2,1)}, bf16[4,256,1024]{2,1,0:T(8,128)(2,1)S(1)}, u32[]{:S(2)}) %copy-start) | copy-done | bytes 2097176
  53.3 1.7 %conditional.2 = (bf16[256,1024]{1,0:T(8,128)(2,1)}, bf16[256,1024]{1,0:T(8,128)(2,1)}) conditional(s32[]{:T(128)} %bitcast.19, () %tuple.25, (s32[2]{0:T(128)S(1)}, s32[256]{0:T(256)S(1)}, s32[256]{0:T(256)S(1)}, bf16[256,8192]{1,0:T(8,128)(2,1)}) %tuple.57), branch_computations={%region_12.13_spmd, %region_13.14_spmd} | conditional | flops 134217728 | bytes 70254648 | solution.py:570
  53.3 0.8 broadcast.406.clone
  54.2 0.8 broadcast.406
  55.0 1.4 %collective-permute-done.5.refs_1_ = bf16[768,1024]{1,0:T(8,128)(2,1)} collective-permute-done((bf16[768,1024]{1,0:T(8,128)(2,1)}, bf16[768,1024]{1,0:T(8,128)(2,1)}, u32[]{:S(2)}, u32[]{:S(2)}) %collective-permute-start.5) | collective-permute-done | bytes 1572896 | tf_op jit(solution)/shard_map/ppermute | solution.py:597
  56.4 1.6 %copy-done.1 = bf16[4,256,1024]{2,1,0:T(8,128)(2,1)S(1)} copy-done((bf16[4,256,1024]{2,1,0:T(8,128)(2,1)S(1)}, bf16[4,256,1024]{2,1,0:T(8,128)(2,1)}, u32[]{:S(2)}) %copy-start.1) | copy-done | bytes 2097176
  58.0 7.4 %prompt_scores.1 = (bf16[8,32,384]{2,1,0:T(8,128)(2,1)}, bf16[8,32,256]{2,1,0:T(8,128)(2,1)}) custom-call(s32[651]{0:T(1024)S(1)} %concatenate.10.meta_ref, bf16[768,1024]{1,0:T(8,128)(2,1)} %bitcast.12.refs_0_, bf16[768,1024]{1,0:T(8,128)(2,1)} %collective-permute-done.5.refs_1_, bf16[256,1024]{1,0:T(8,128)(2,1)} %get-tuple-element.124.refs_2_, ...), custom_call_target="tpu_custom_call" | custom-call | tf_op jit(solution)/shard_map/prompt_scores/pallas_call | solution.py:619
  65.5 37.0 %conditional.3 = (bf16[4,2,4,64,128]{4,3,2,1,0:T(8,128)(2,1)}, f32[8,32,128]{2,1,0:T(8,128)S(1)}) conditional(s32[]{:T(128)} %bitcast.11, (bf16[8,32,384]{2,1,0:T(8,128)(2,1)}, s32[1,640]{1,0:T(1,128)S(1)}, s32[8]{0:T(128)S(1)}, bf16[8,32,128]{2,1,0:T(8,128)(2,1)S(1)}, bf16[8,256,4,256]{3,2,1,0:T(4,128)(2,1)}, /*index=5*/s32[651]{0:T(1024)S(1)}, ...), branch_computations={%region_14.17_spmd, %region_17.20_spmd} | conditional | flops 34047488 | bytes 74289376 | solution.py:724
  65.5 5.7 %all-to-all-start.1 = ((bf16[8,32,384]{2,1,0:T(8,128)(2,1)}), bf16[8,32,384]{2,1,0:T(8,128)(2,1)S(1)}, u32[]{:S(2)}, u32[]{:S(2)}) async-start(bf16[8,32,384]{2,1,0:T(8,128)(2,1)} %get-tuple-element.68), calls=%async_computation.1 | async-start | bytes 393216 | tf_op jit(solution)/shard_map/cond/branch_0_fun/all_to_all | solution.py:649
  71.2 3.0 %copy.25 = bf16[8,256,4,256]{3,1,2,0:T(8,128)(2,1)S(1)} copy(bf16[8,256,4,256]{3,2,1,0:T(4,128)(2,1)} %get-tuple-element.189) | data formatting | bytes 8388608 | tf_op jit(solution)/shard_map
  74.2 0.7 fusion.71
  74.9 1.3 copy-done.7
  76.3 0.1 broadcast_in_dim.162.refs_2_
  76.4 0.2 fusion.17
  76.6 0.1 broadcast_in_dim.163.refs_3_
  76.7 2.7 %all-to-all-done.1.refs_0_ = bf16[8,32,384]{2,1,0:T(8,128)(2,1)S(1)} async-done(((bf16[8,32,384]{2,1,0:T(8,128)(2,1)}), bf16[8,32,384]{2,1,0:T(8,128)(2,1)S(1)}, u32[]{:S(2)}, u32[]{:S(2)}) %all-to-all-start.1) | async-done | bytes 196640 | tf_op jit(solution)/shard_map/cond/branch_0_fun/all_to_all | solution.py:649
  79.4 1.7 %softmax_weights.2 = (bf16[8,32,384]{2,1,0:T(8,128)(2,1)}, f32[8,32,1]{2,1,0:T(8,128)S(1)}) custom-call(bf16[8,32,384]{2,1,0:T(8,128)(2,1)S(1)} %all-to-all-done.1.refs_0_, s32[1,384]{1,0:T(1,128)S(1)} %slice.18.refs_1_, f32[8,32,1]{2,1,0:T(8,128)S(1)} %broadcast_in_dim.162.refs_2_, f32[8,32,1]{2,1,0:T(8,128)S(1)} %broadcast_in_dim.163.refs_3_), custom_call_target="tpu_custom_call" | custom-call | tf_op jit(solution)/shard_map/cond/branch_0_fun/softmax_weights/pallas_call | solution.py:663
  81.1 3.6 %all-to-all-start.2 = ((bf16[8,32,384]{2,1,0:T(8,128)(2,1)}), bf16[8,32,384]{2,1,0:T(8,128)(2,1)S(1)}, u32[]{:S(2)}, u32[]{:S(2)}) async-start(bf16[8,32,384]{2,1,0:T(8,128)(2,1)} %get-tuple-element.73.refs_4_), calls=%async_computation.2 | async-start | bytes 393216 | tf_op jit(solution)/shard_map/cond/branch_0_fun/all_to_all | solution.py:695
  84.7 0.1 reduce
  84.8 5.5 %owner_lists.2.refs_2_ = bf16[8,640,1024]{2,1,0:T(8,128)(2,1)} custom-call(s32[651]{0:T(1024)S(1)} %get-tuple-element.67.meta_ref, bf16[768,1024]{1,0:T(8,128)(2,1)} %get-tuple-element.75.refs_0_, bf16[768,1024]{1,0:T(8,128)(2,1)} %get-tuple-element.76.refs_1_, bf16[256,1024]{1,0:T(8,128)(2,1)} %get-tuple-element.77.refs_2_, ...), custom_call_target="tpu_custom_call" | custom-call | bytes 16777216 | tf_op jit(solution)/shard_map/cond/branch_0_fun/owner_lists/pallas_call | solution.py:674
  90.4 0.4 fusion.13
  90.8 1.4 %all-to-all-done.2.refs_0_ = bf16[8,32,384]{2,1,0:T(8,128)(2,1)S(1)} async-done(((bf16[8,32,384]{2,1,0:T(8,128)(2,1)}), bf16[8,32,384]{2,1,0:T(8,128)(2,1)S(1)}, u32[]{:S(2)}, u32[]{:S(2)}) %all-to-all-start.2) | async-done | bytes 196640 | tf_op jit(solution)/shard_map/cond/branch_0_fun/all_to_all | solution.py:695
  92.2 0.7 copy-done.12
  92.9 9.4 %weighted_values.2 = bf16[4,2,4,64,128]{4,3,2,1,0:T(8,128)(2,1)} custom-call(s32[651]{0:T(1024)S(1)} %get-tuple-element.67.meta_ref, bf16[8,32,384]{2,1,0:T(8,128)(2,1)} %copy-done.12, s32[8,1,640]{2,1,0:T(1,128)S(1)} %get-tuple-element.74.refs_1_, bf16[8,640,1024]{2,1,0:T(8,128)(2,1)} %owner_lists.2.refs_2_, bf16[4,1024,256]{2,1,0:T(8,128)(2,1)S(1)} %copy-done.4), custom_call_target="tpu_custom_call" | custom-call | tf_op jit(solution)/shard_map/cond/branch_0_fun/weighted_values/pallas_call | solution.py:702
  102.5 3.5 %all-to-all-start.8 = ((bf16[4,2,4,64,128]{4,3,2,1,0:T(8,128)(2,1)}), bf16[4,2,4,64,128]{4,3,2,1,0:T(8,128)(2,1)S(1)}, u32[]{:S(2)}, u32[]{:S(2)}) async-start(bf16[4,2,4,64,128]{4,3,2,1,0:T(8,128)(2,1)} %get-tuple-element.131), calls=%async_computation.8 | async-start | bytes 1048576 | tf_op jit(solution)/shard_map/all_to_all | solution.py:731
  106.0 6.6 %all-to-all-done.8.parts_ref = bf16[4,2,4,64,128]{4,3,2,1,0:T(8,128)(2,1)S(1)} async-done(((bf16[4,2,4,64,128]{4,3,2,1,0:T(8,128)(2,1)}), bf16[4,2,4,64,128]{4,3,2,1,0:T(8,128)(2,1)S(1)}, u32[]{:S(2)}, u32[]{:S(2)}) %all-to-all-start.8) | async-done | bytes 524320 | tf_op jit(solution)/shard_map/all_to_all | solution.py:731
  112.6 0.1 half_pool_sum.1
  112.7 2.1 %collective-permute-start.6 = (bf16[2,4,64,128]{3,2,1,0:T(8,128)(2,1)S(1)}, bf16[2,4,64,128]{3,2,1,0:T(8,128)(2,1)S(1)}, u32[]{:S(2)}, u32[]{:S(2)}) collective-permute-start(bf16[2,4,64,128]{3,2,1,0:T(8,128)(2,1)S(1)} %get-tuple-element.134.after_ref), channel_id=1, source_target_pairs={{0,8},{2,10},{4,12},{6,14},{8,0},{10,2},{12,4},{14,6},{1,9},{3,11}... | collective-permute-start | bytes 393224 | tf_op jit(solution)/shard_map/ppermute | solution.py:457
  114.8 5.2 %collective-permute-done.6.got_ref = bf16[2,4,64,128]{3,2,1,0:T(8,128)(2,1)S(1)} collective-permute-done((bf16[2,4,64,128]{3,2,1,0:T(8,128)(2,1)S(1)}, bf16[2,4,64,128]{3,2,1,0:T(8,128)(2,1)S(1)}, u32[]{:S(2)}, u32[]{:S(2)}) %collective-permute-start.6) | collective-permute-done | bytes 131104 | tf_op jit(solution)/shard_map/ppermute | solution.py:457
  120.1 0.9 collective-permute-start.9
  121.0 2.1 %collective-permute-start.8 = (bf16[16,4096]{1,0:T(8,128)(2,1)S(1)}, bf16[16,4096]{1,0:T(8,128)(2,1)S(1)}, u32[]{:S(2)}, u32[]{:S(2)}) collective-permute-start(bf16[16,4096]{1,0:T(8,128)(2,1)S(1)} %attended_sum.1), channel_id=1, source_target_pairs={{0,4},{2,6},{4,0},{6,2},{8,12},{10,14},{12,8},{14,10},{1,5},{3,7},... | collective-permute-start | bytes 393224 | tf_op jit(solution)/shard_map/ppermute | solution.py:457
  123.1 0.6 collective-permute-start.7
  123.7 3.4 %copy-done.2 = bf16[4096,1024]{1,0:T(8,128)(2,1)S(1)} copy-done((bf16[4096,1024]{1,0:T(8,128)(2,1)S(1)}, bf16[4096,1024]{1,0:T(8,128)(2,1)}, u32[]{:S(2)}) %copy-start.2) | copy-done | bytes 8388632
  127.1 0.6 stage_out_weight.1
  127.7 0.4 collective-permute-done.7
  128.1 1.6 %fusion.43 = f32[64,1024]{1,0:T(8,128)S(1)} fusion(bf16[4096,1024]{1,0:T(8,128)(2,1)S(1)} %stage_out_weight.1, bf16[16,4096]{1,0:T(8,128)(2,1)S(1)} %collective-permute-done.9, bf16[16,4096]{1,0:T(8,128)(2,1)S(1)} %collective-permute-done.8, bf16[16,4096]{1,0:T(8,128)(2,1)S(1)} %collective-permute-done.7, bf16[16,4096]{1,0:T(8,128)(2,1)S(1)} %attended_sum.1), kind=kOutput, calls=%fused_computation.33 | convolution fusion | flops 538968064 | bytes 9175040 | tf_op jit(solution)/shard_map/dot_general | solution.py:767
  129.8 1.3 %collective-permute-done.10.got_ref = f32[64,512]{1,0:T(8,128)S(1)} collective-permute-done((f32[64,512]{1,0:T(8,128)S(1)}, f32[64,512]{1,0:T(8,128)S(1)}, u32[]{:S(2)}, u32[]{:S(2)}) %collective-permute-start.10) | collective-permute-done | bytes 131104 | tf_op jit(solution)/shard_map/ppermute | solution.py:774
  131.2 0.6 order_rows.1
  (50 shorter events, 0.7 us)
Async XLA Ops:
  0.0 9.1 %collective-permute-start.1 = (bf16[8,32,128]{2,1,0:T(8,128)(2,1)}, bf16[8,32,128]{2,1,0:T(8,128)(2,1)S(1)}, u32[]{:S(2)}, u32[]{:S(2)}) collective-permute-start(bf16[8,32,128]{2,1,0:T(8,128)(2,1)} %param.18), channel_id=1, source_target_pairs={{0,8},{2,10},{4,12},{6,14},{8,0},{10,2},{12,4},{14,6},{1,9},{3,11}... | collective-permute-start | bytes 196616 | tf_op jit(solution)/shard_map/ppermute | solution.py:457
  4.1 9.4 %copy-start.14 = (s32[256]{0:T(256)S(1)}, s32[256]{0:T(256)}, u32[]{:S(2)}) copy-start(s32[256]{0:T(256)} %fill_ref.1) | copy-start | bytes 3076
  4.1 9.5 %copy-start.13 = (s32[256,1]{0,1:T(1,128)S(1)}, s32[256,1]{0,1:T(1,128)}, u32[]{:S(2)}) copy-start(s32[256,1]{0,1:T(1,128)} %param.15) | copy-start | bytes 3076
  4.1 14.3 %copy-start.10 = (bf16[8,32,128]{2,1,0:T(8,128)(2,1)S(1)}, bf16[8,32,128]{2,1,0:T(8,128)(2,1)}, u32[]{:S(2)}) copy-start(bf16[8,32,128]{2,1,0:T(8,128)(2,1)} %param.18) | copy-start | bytes 196612
  4.1 16.4 %copy-start.16 = (s32[256]{0:T(256)S(1)}, s32[256]{0:T(256)}, u32[]{:S(2)}) copy-start(s32[256]{0:T(256)} %param.16) | copy-start | bytes 3076
  4.2 17.9 %copy-start.9 = (bf16[1024,4,256]{2,1,0:T(4,128)(2,1)S(1)}, bf16[1024,4,256]{2,1,0:T(4,128)(2,1)}, u32[]{:S(2)}) copy-start(bf16[1024,4,256]{2,1,0:T(4,128)(2,1)} %param.14) | copy-start | bytes 6291460
  9.1 43.6 %all-to-all-start.7 = ((bf16[8,96,1024]{2,1,0:T(8,128)(2,1)}), bf16[8,96,1024]{2,1,0:T(8,128)(2,1)}, u32[]{:S(2)}, u32[]{:S(2)}) async-start(bf16[8,96,1024]{2,1,0:T(8,128)(2,1)} %pack_live_tokens.3), calls=%async_computation.7 | async-start | bytes 3145728 | tf_op jit(solution)/shard_map/all_to_all | solution.py:511
  16.9 26.6 %collective-permute-start.2 = (s32[2]{0:T(128)S(1)}, s32[2]{0:T(128)S(1)}, u32[]{:S(2)}, u32[]{:S(2)}) collective-permute-start(s32[2]{0:T(128)S(1)} %pad_add_fusion.1), channel_id=1, source_target_pairs={{0,16},{16,0},{1,17},{17,1},{2,18},{18,2},{3,19},{19,3},{4,20},{20... | collective-permute-start | bytes 32 | tf_op jit(solution)/shard_map/ppermute | solution.py:557
  18.5 23.7 %collective-permute-start.3 = (bf16[2,8,32,128]{3,2,1,0:T(8,128)(2,1)S(1)}, bf16[2,8,32,128]{3,2,1,0:T(8,128)(2,1)S(1)}, u32[]{:S(2)}, u32[]{:S(2)}) collective-permute-start(bf16[2,8,32,128]{3,2,1,0:T(8,128)(2,1)S(1)} %pad_maximum_fusion.1), channel_id=1, source_target_pairs={{0,4},{2,6},{4,0},{6,2},{8,12},{10,14},{12,8},{14,10},{1,5},{3,7},... | collective-permute-start | bytes 393224 | tf_op jit(solution)/shard_map/ppermute | solution.py:457
  42.2 7.9 %collective-permute-start.4 = (bf16[4,8,32,128]{3,2,1,0:T(8,128)(2,1)S(1)}, bf16[4,8,32,128]{3,2,1,0:T(8,128)(2,1)S(1)}, u32[]{:S(2)}, u32[]{:S(2)}) collective-permute-start(bf16[4,8,32,128]{3,2,1,0:T(8,128)(2,1)S(1)} %pad_maximum_fusion), channel_id=1, source_target_pairs={{0,2},{2,0},{4,6},{6,4},{8,10},{10,8},{12,14},{14,12},{1,3},{3,1},... | collective-permute-start | bytes 786440 | tf_op jit(solution)/shard_map/ppermute | solution.py:457
  46.2 3.9 %copy-start.3 = (bf16[1024,4,256]{2,0,1:T(8,128)(2,1)S(1)}, bf16[1024,4,256]{2,0,1:T(8,128)(2,1)}, u32[]{:S(2)}) copy-start(bf16[1024,4,256]{2,0,1:T(8,128)(2,1)} %copy.28) | copy-start | bytes 6291460
  51.3 1.3 %copy-start = (bf16[4,256,1024]{2,1,0:T(8,128)(2,1)}, bf16[4,256,1024]{2,1,0:T(8,128)(2,1)S(1)}, u32[]{:S(2)}) copy-start(bf16[4,256,1024]{2,1,0:T(8,128)(2,1)S(1)} %key_projection.3.refs_5_) | copy-start | bytes 6291460
  52.7 3.8 %collective-permute-start.5 = (bf16[768,1024]{1,0:T(8,128)(2,1)}, bf16[768,1024]{1,0:T(8,128)(2,1)}, u32[]{:S(2)}, u32[]{:S(2)}) collective-permute-start(bf16[768,1024]{1,0:T(8,128)(2,1)} %bitcast.12.refs_0_), channel_id=1, source_target_pairs={{0,1},{1,0},{2,3},{3,2},{4,5},{5,4},{6,7},{7,6},{8,9},{9,8},{10,11... | collective-permute-start | bytes 4718600 | tf_op jit(solution)/shard_map/ppermute | solution.py:597
  56.4 1.6 %copy-start.1 = (bf16[4,256,1024]{2,1,0:T(8,128)(2,1)S(1)}, bf16[4,256,1024]{2,1,0:T(8,128)(2,1)}, u32[]{:S(2)}) copy-start(bf16[4,256,1024]{2,1,0:T(8,128)(2,1)} %copy-done) | copy-start | bytes 6291460
  58.0 7.4 %copy-start.15 = (s32[8]{0:T(128)S(1)}, s32[8]{0:T(128)}, u32[]{:S(2)}) copy-start(s32[8]{0:T(128)} %param.20) | copy-start | bytes 100
  65.5 13.9 %all-to-all-start.1 = ((bf16[8,32,384]{2,1,0:T(8,128)(2,1)}), bf16[8,32,384]{2,1,0:T(8,128)(2,1)S(1)}, u32[]{:S(2)}, u32[]{:S(2)}) async-start(bf16[8,32,384]{2,1,0:T(8,128)(2,1)} %get-tuple-element.68), calls=%async_computation.1 | async-start | bytes 393216 | tf_op jit(solution)/shard_map/cond/branch_0_fun/all_to_all | solution.py:649
  74.2 2.1 %copy-start.7 = (bf16[8,256,4,256]{3,1,2,0:T(8,128)(2,1)}, bf16[8,256,4,256]{3,1,2,0:T(8,128)(2,1)S(1)}, u32[]{:S(2)}) copy-start(bf16[8,256,4,256]{3,1,2,0:T(8,128)(2,1)S(1)} %copy.25) | copy-start | bytes 12582916 | tf_op jit(solution)/shard_map/cond
  81.1 11.1 %all-to-all-start.2 = ((bf16[8,32,384]{2,1,0:T(8,128)(2,1)}), bf16[8,32,384]{2,1,0:T(8,128)(2,1)S(1)}, u32[]{:S(2)}, u32[]{:S(2)}) async-start(bf16[8,32,384]{2,1,0:T(8,128)(2,1)} %get-tuple-element.73.refs_4_), calls=%async_computation.2 | async-start | bytes 393216 | tf_op jit(solution)/shard_map/cond/branch_0_fun/all_to_all | solution.py:695
  84.8 5.6 %copy-start.8 = (bf16[8,256,4,256]{3,1,2,0:T(8,128)(2,1)S(1)}, bf16[8,256,4,256]{3,1,2,0:T(8,128)(2,1)}, u32[]{:S(2)}) copy-start(bf16[8,256,4,256]{3,1,2,0:T(8,128)(2,1)} %copy-done.7) | copy-start | bytes 12582916 | tf_op jit(solution)/shard_map/cond
  84.8 8.1 %copy-start.4 = (bf16[4,1024,256]{2,1,0:T(8,128)(2,1)S(1)}, bf16[4,1024,256]{2,1,0:T(8,128)(2,1)}, u32[]{:S(2)}) copy-start(bf16[4,1024,256]{2,1,0:T(8,128)(2,1)} %get-tuple-element.79.refs_3_) | copy-start | bytes 6291460 | tf_op jit(solution)/shard_map/cond
  92.2 0.7 copy-start.12
  102.5 10.1 %all-to-all-start.8 = ((bf16[4,2,4,64,128]{4,3,2,1,0:T(8,128)(2,1)}), bf16[4,2,4,64,128]{4,3,2,1,0:T(8,128)(2,1)S(1)}, u32[]{:S(2)}, u32[]{:S(2)}) async-start(bf16[4,2,4,64,128]{4,3,2,1,0:T(8,128)(2,1)} %get-tuple-element.131), calls=%async_computation.8 | async-start | bytes 1048576 | tf_op jit(solution)/shard_map/all_to_all | solution.py:731
  112.7 7.3 %collective-permute-start.6 = (bf16[2,4,64,128]{3,2,1,0:T(8,128)(2,1)S(1)}, bf16[2,4,64,128]{3,2,1,0:T(8,128)(2,1)S(1)}, u32[]{:S(2)}, u32[]{:S(2)}) collective-permute-start(bf16[2,4,64,128]{3,2,1,0:T(8,128)(2,1)S(1)} %get-tuple-element.134.after_ref), channel_id=1, source_target_pairs={{0,8},{2,10},{4,12},{6,14},{8,0},{10,2},{12,4},{14,6},{1,9},{3,11}... | collective-permute-start | bytes 393224 | tf_op jit(solution)/shard_map/ppermute | solution.py:457
  120.1 7.6 %collective-permute-start.9 = (bf16[16,4096]{1,0:T(8,128)(2,1)S(1)}, bf16[16,4096]{1,0:T(8,128)(2,1)S(1)}, u32[]{:S(2)}, u32[]{:S(2)}) collective-permute-start(bf16[16,4096]{1,0:T(8,128)(2,1)S(1)} %attended_sum.1), channel_id=1, source_target_pairs={{0,6},{2,4},{4,2},{6,0},{8,14},{10,12},{12,10},{14,8},{1,7},{3,5},... | collective-permute-start | bytes 393224 | tf_op jit(solution)/shard_map/ppermute | solution.py:457
  121.0 6.7 %collective-permute-start.8 = (bf16[16,4096]{1,0:T(8,128)(2,1)S(1)}, bf16[16,4096]{1,0:T(8,128)(2,1)S(1)}, u32[]{:S(2)}, u32[]{:S(2)}) collective-permute-start(bf16[16,4096]{1,0:T(8,128)(2,1)S(1)} %attended_sum.1), channel_id=1, source_target_pairs={{0,4},{2,6},{4,0},{6,2},{8,12},{10,14},{12,8},{14,10},{1,5},{3,7},... | collective-permute-start | bytes 393224 | tf_op jit(solution)/shard_map/ppermute | solution.py:457
  123.1 5.0 %collective-permute-start.7 = (bf16[16,4096]{1,0:T(8,128)(2,1)S(1)}, bf16[16,4096]{1,0:T(8,128)(2,1)S(1)}, u32[]{:S(2)}, u32[]{:S(2)}) collective-permute-start(bf16[16,4096]{1,0:T(8,128)(2,1)S(1)} %attended_sum.1), channel_id=1, source_target_pairs={{0,2},{2,0},{4,6},{6,4},{8,10},{10,8},{12,14},{14,12},{1,3},{3,1},... | collective-permute-start | bytes 393224 | tf_op jit(solution)/shard_map/ppermute | solution.py:457
  123.7 3.4 %copy-start.2 = (bf16[4096,1024]{1,0:T(8,128)(2,1)S(1)}, bf16[4096,1024]{1,0:T(8,128)(2,1)}, u32[]{:S(2)}) copy-start(bf16[4096,1024]{1,0:T(8,128)(2,1)} %weight_ref.1) | copy-start | bytes 25165828
  129.7 1.4 %collective-permute-start.10 = (f32[64,512]{1,0:T(8,128)S(1)}, f32[64,512]{1,0:T(8,128)S(1)}, u32[]{:S(2)}, u32[]{:S(2)}) collective-permute-start(f32[64,512]{1,0:T(8,128)S(1)} %get-tuple-element.222), channel_id=1, source_target_pairs={{0,1},{1,0},{2,3},{3,2},{4,5},{5,4},{6,7},{7,6},{8,9},{9,8},{10,11... | collective-permute-start | bytes 393224 | tf_op jit(solution)/shard_map/ppermute | solution.py:774

commit v17 on v16

--- a/solution.py
+++ b/solution.py
@@ -307,9 +307,10 @@
 
 
 def value_kernel(n, rows, count, meta_ref, *refs):
-    w_refs, (row_ref, list_ref, weight_ref, out_ref) = refs[:count], refs[count : count + 4]
-    values, lists, acc, mixed, value_sem, sem = refs[count + 4 :]
-    q = pl.program_id(0)
+    w_refs, (row_ref, list_ref, weight_ref) = refs[:count], refs[count : count + 3]
+    out_refs, scratch = refs[count + 3 : count + 3 + n // 2], refs[count + 3 + n // 2 :]
+    values, lists, acc, mixed, value_sem, sem = scratch
+    step = pl.program_id(0)
     kvh, _, hd = values.shape
     load_values = [
         pltpu.make_async_copy(
@@ -322,22 +323,24 @@
     per = rows * heads // kvh
     cuts = tile_cuts(lanes)
     at_size = n * lanes // BLK
+    me = meta_ref[at_size + n]
+    q = partner_owner(step, me, n)
     size = meta_ref[at_size + q]
     copies = list_copies(n, lanes, lambda o: meta_ref[at_size + o], list_ref, lists, sem)
     ahead = min(3, n)
 
-    def fetch(o):
-        for used, copy in copies(o):
+    def fetch(i):
+        for used, copy in copies(partner_owner(i, me, n)):
             pl.when(used)(copy.start)
 
-    @pl.when(q == 0)
+    @pl.when(step == 0)
     def _():
-        for o in range(ahead):
-            fetch(o)
-
-    pl.when(q + ahead < n)(lambda: fetch(jnp.minimum(q + ahead, n - 1)))
-
-    @pl.when(q == n // 2)
+        for i in range(ahead):
+            fetch(i)
+
+    pl.when(step + ahead < n)(lambda: fetch(jnp.minimum(step + ahead, n - 1)))
+
+    @pl.when(step == n // 2)
     def _():
         for load in load_values:
             load.start()
@@ -370,7 +373,7 @@
 
     def keep(sums):
         for h in range(kvh):
-            mixed[h, pl.ds(pl.multiple_of(q * per, per), per), :] = sums[
+            mixed[h, pl.ds(pl.multiple_of(step * per, per), per), :] = sums[
                 h * per : (h + 1) * per
             ].astype(mixed.dtype)
 
@@ -380,33 +383,39 @@
             pl.when(size > cuts[t])(functools.partial(one, t))
     pl.when(size > cuts[1])(lambda: keep(acc[...]))
 
-    @pl.when(q == n - 1)
+    @pl.when(step == n - 1)
     def _():
         for load in load_values:
             load.wait()
         for h in range(kvh):
             done = jnp.dot(mixed[h], values[h], preferred_element_type=jnp.float32)
-            done = done.reshape(2, n // 2, per, done.shape[1]).astype(out_ref.dtype)
-            for side in range(2):
-                out_ref[:, side, h] = done[side]
-
-
-def half_sum_kernel(side_ref, parts_ref, kept_ref, send_ref, mine_ref):
-    half, sides, kvh, per, hd = parts_ref.shape
+            done = done.astype(jnp.bfloat16)
+            for i in range(n):
+                out_refs[i // 2][i % 2, h] = done[i * per : (i + 1) * per]
+
+
+def half_sum_kernel(side_ref, *refs):
+    *part_refs, kept_ref, send_ref, mine_ref = refs
+    sides, kvh, _, _ = part_refs[0].shape
     rows, heads = kept_ref.shape[:2]
     group = heads // kvh
     for side in range(sides):
         own = side_ref[0] == side
         for h in range(kvh):
-            terms = parts_ref[0, side, h].astype(jnp.float32)
-            for i in range(1, half):
-                terms = terms + parts_ref[i, side, h].astype(jnp.float32)
+            terms = part_refs[0][side, h].astype(jnp.float32)
+            for ref in part_refs[1:]:
+                terms = terms + ref[side, h].astype(jnp.float32)
             kept = jnp.concatenate(
                 [kept_ref[r, h * group : (h + 1) * group, :] for r in range(rows)]
             )
             terms = terms + jnp.where(own, kept, 0.0)
             mine_ref[side, h] = terms
             send_ref[side, h] = terms.astype(send_ref.dtype)
+
+
+def partner_owner(i, me, n):
+    half = n // 2
+    return i % 2 * half + ((me % half) ^ (i // 2))
 
 
 def whole_sum_kernel(mine_ref, got_ref, out_ref, total):
@@ -458,7 +467,7 @@
 
 
 def from_rest(held, n):
-    k = n // 4
+    k = n // 8
     while k >= 2:
         held = jnp.concatenate([held, with_partner(held, k, n)])
         k //= 2
@@ -502,12 +511,12 @@
     pack_fill, pack_dest = block_fill, block_dest[:, 0]
     packed = pack(x_prompt, pack_fill, pack_dest, at, n, 0, size)
     dest = pack_dest
-    far = with_partner(queries, n // 2, n)
+    far = [with_partner(queries, k, n) for k in (n // 2, n // 4, n // 2 + n // 4)]
     packed, far, dest, block_row, block_fill, kv_weight = lax.optimization_barrier(
         (packed, far, dest, block_row, block_fill, kv_weight)
     )
     kv_weight = kv_weight.transpose(1, 0, 2)
-    even = from_rest(jnp.stack([queries, far]), n)
+    even = from_rest(jnp.stack([queries, *far]), n)
     mine = lax.all_to_all(packed, "pool", 0, 0, tiled=True).reshape(n * size, part)
 
     index = jnp.arange(n * blocks, dtype=jnp.int32)
@@ -597,10 +606,7 @@
     other = lax.ppermute(mine, "tp", swap)
 
     anywhere = pl.BlockSpec(memory_space=pl.ANY)
-    row_spec = pl.BlockSpec((1, 1, lanes), lambda q, m: (q, 0, 0))
-    slot_specs = [
-        pl.BlockSpec((1, heads, length), lambda q, m: (q, 0, 0)) for length in (near, lanes - near)
-    ]
+    pair_shape = (2, kvh, per, hd)
     slot_shapes = [
         jax.ShapeDtypeStruct((n, heads, length), jnp.bfloat16) for length in (near, lanes - near)
     ]
@@ -704,8 +710,21 @@
             grid_spec=pltpu.PrefetchScalarGridSpec(
                 num_scalar_prefetch=1,
                 grid=(n,),
-                in_specs=[*slot_specs[:count], row_spec, anywhere, anywhere],
-                out_specs=pl.BlockSpec((n // 2, 2, kvh, per, hd), lambda q, m: (0, 0, 0, 0, 0)),
+                in_specs=[
+                    *[
+                        pl.BlockSpec(
+                            (1, heads, shape.shape[2]),
+                            lambda i, m: (partner_owner(i, m[at_me], n), 0, 0),
+                        )
+                        for shape in slot_shapes[:count]
+                    ],
+                    pl.BlockSpec(
+                        (1, 1, lanes), lambda i, m: (partner_owner(i, m[at_me], n), 0, 0)
+                    ),
+                    pl.BlockSpec(memory_space=pltpu.HBM),
+                    anywhere,
+                ],
+                out_specs=[pl.BlockSpec(pair_shape, lambda i, m: (0, 0, 0, 0))] * (n // 2),
                 scratch_shapes=[
                     pltpu.VMEM((kvh, part, hd), jnp.bfloat16),
                     pltpu.VMEM((n, lanes, part), jnp.bfloat16),
@@ -715,33 +734,29 @@
                     pltpu.SemaphoreType.DMA((n, len(tile_cuts(lanes)) - 1)),
                 ],
             ),
-            out_shape=jax.ShapeDtypeStruct((n // 2, 2, kvh, per, hd), jnp.bfloat16),
-            compiler_params=pltpu.CompilerParams(vmem_limit_bytes=56 * MIB),
+            out_shape=[jax.ShapeDtypeStruct(pair_shape, jnp.bfloat16)] * (n // 2),
+            compiler_params=pltpu.CompilerParams(vmem_limit_bytes=24 * MIB),
             name="weighted_values",
         )(meta, *weights, rowof, lists, kv_weight)
-        return terms, cached.reshape(rows, heads, hd) * share
-
-    terms, kept = lax.cond(
+        return *terms, cached.reshape(rows, heads, hd) * share
+
+    *terms, kept = lax.cond(
         longer,
         lambda: exchange_weights(score_near, score_rest),
         lambda: exchange_weights(score_near),
     )
 
-    halves = [list(range(n // 2)), list(range(n // 2, n))]
-    term_parts = lax.all_to_all(
-        terms, "pool", 0, 0, axis_index_groups=halves, tiled=True
-    )
-    pair_shape = (2, kvh, per, hd)
+    term_parts = [terms[0]] + [with_partner(terms[k], k, n) for k in range(1, n // 2)]
     send, held = pl.pallas_call(
         half_sum_kernel,
-        in_specs=[pl.BlockSpec(memory_space=pltpu.SMEM), in_vmem, in_vmem],
+        in_specs=[pl.BlockSpec(memory_space=pltpu.SMEM), *[in_vmem] * (n // 2 + 1)],
         out_shape=[
             jax.ShapeDtypeStruct(pair_shape, jnp.bfloat16),
             jax.ShapeDtypeStruct(pair_shape, jnp.float32),
         ],
         compiler_params=pltpu.CompilerParams(vmem_limit_bytes=8 * MIB),
         name="half_pool_sum",
-    )((me // (n // 2)).reshape(1), term_parts, kept)
+    )((me // (n // 2)).reshape(1), *term_parts, kept)
     attended = pl.pallas_call(
         whole_sum_kernel,
         out_shape=jax.ShapeDtypeStruct((2 * rows, heads * hd), jnp.bfloat16),

time: 133 us -> 129 us (0.970)
  waiting for transfers between devices: 38.1 us -> 35.4 us
  Pallas kernels: 34.9 us -> 32.3 us
  local copies, waits for them, and re-layouts: 15.9 us -> 17.9 us
    all_to_all x1, waiting for transfers between devices: 0.01 us -> 11.2 us  [local(): lax.all_to_all(packed, 'pool', 0, 0, tiled=True).reshape(n * size, part)]
    ppermute x7 -> x11, waiting for transfers between devices: 24.6 us -> 17.3 us  [with_partner(): return lax.ppermute(x, 'pool', [(i, i ^ k) for i in range(n)])]
    all_to_all x1 -> x0, waiting for transfers between devices: 6.61 us -> none  [local(): lax.all_to_all(terms, 'pool', 0, 0, axis_index_groups=halves, tiled=True)]
    ppermute x7 -> x11, starting transfers between devices: 13.2 us -> 17.2 us  [with_partner(): return lax.ppermute(x, 'pool', [(i, i ^ k) for i in range(n)])]
    all_to_all x1 -> x0, starting transfers between devices: 3.48 us -> none  [local(): lax.all_to_all(terms, 'pool', 0, 0, axis_index_groups=halves, tiled=True)]
    cond x8, local copies, waits for them, and re-layouts: 2 us -> 5.3 us
    pallas_call x1, Pallas kernels: 9.37 us -> 6.58 us  [exchange_weights(): pl.pallas_call(functools.partial(value_kernel, n, rows, count), grid_spec...]
    all_to_all x1, starting transfers between devices: 5.65 us -> 3.52 us  [exchange_weights(): parts = [lax.all_to_all(s, 'pool', 0, 0, tiled=True) for s in scores]]
  transfers between devices with their start and end apart: 14 -> 17, of which waited for: 9 -> 10; matrix products, arithmetic and copies ran while one was open for 11% -> 11% of each run, Pallas kernels for 12% -> 12%
where the time goes in v17:
time: 129 us
  waiting for transfers between devices  35.4 us (27%)
  Pallas kernels  32.3 us (25%)
  starting transfers between devices  31.7 us (25%)
  local copies, waits for them, and re-layouts  17.9 us (14%)
  other arithmetic  6.64 us (5%)
  matrix products  2.77 us (2%)
  between operations  1.6 us (1%)
    ppermute x11, waiting for transfers between devices, with_partner(): return lax.ppermute(x, 'pool', [(i, i ^ k) for i in range(n)])  17.3 us
    ppermute x11, starting transfers between devices, with_partner(): return lax.ppermute(x, 'pool', [(i, i ^ k) for i in range(n)])  17.2 us
    all_to_all x1, waiting for transfers between devices, local(): lax.all_to_all(packed, 'pool', 0, 0, tiled=True).reshape(n * size, part)  11.2 us
    pallas_call x1, Pallas kernels, local(): pl.pallas_call(functools.partial(score_kernel, n, rows), grid_spec=pltpu....  7.71 us
    pallas_call x1, Pallas kernels, exchange_weights(): pl.pallas_call(functools.partial(value_kernel, n, rows, count), grid_spec...  6.58 us
    unnamed x20, local copies, waits for them, and re-layouts  6.32 us
    all_to_all x1, starting transfers between devices, local(): lax.all_to_all(packed, 'pool', 0, 0, tiled=True).reshape(n * size, part)  5.87 us
    pallas_call x1, Pallas kernels, exchange_weights(): pl.pallas_call(functools.partial(list_kernel, n), grid_spec=pltpu.Prefetc...  5.53 us
  transfers between devices with their start and end apart: 17, of which 10 were waited for; matrix products, arithmetic and copies ran while one was open for 11% of the time, Pallas kernels for 12%

profile of v17, /device:TPU:0, one launch (start us, length us, event | category | flops | bytes accessed | tf_op | source)
XLA Modules:
  0.0 128.7 jit_solution(8509912556969257001)
XLA Ops:
  0.0 5.0 %collective-permute-start.3 = (bf16[8,32,128]{2,1,0:T(8,128)(2,1)}, bf16[8,32,128]{2,1,0:T(8,128)(2,1)S(1)}, u32[]{:S(2)}, u32[]{:S(2)}) collective-permute-start(bf16[8,32,128]{2,1,0:T(8,128)(2,1)} %param.18), channel_id=1, source_target_pairs={{0,12},{2,14},{4,8},{6,10},{8,4},{10,6},{12,0},{14,2},{1,13},{3,15... | collective-permute-start | bytes 196616 | tf_op jit(solution)/shard_map/ppermute | solution.py:466
  5.1 0.6 collective-permute-start.1
  5.7 4.9 %pack_live_tokens.3 = bf16[8,96,1024]{2,1,0:T(8,128)(2,1)} custom-call(s32[2]{0:T(128)S(1)} %pad_add_fusion.at_ref, s32[256]{0:T(256)} %fill_ref.1, s32[256]{0:T(256)} %bitcast.55, bf16[256,8192]{1,0:T(8,128)(2,1)} %x_ref.1), custom_call_target="tpu_custom_call" | custom-call | flops 402653184 | bytes 67108864 | tf_op jit(solution)/shard_map/pack_live_tokens/pallas_call | solution.py:62
  10.7 0.2 collective-permute-done.1
  10.9 5.9 %all-to-all-start.7 = ((bf16[8,96,1024]{2,1,0:T(8,128)(2,1)}), bf16[8,96,1024]{2,1,0:T(8,128)(2,1)}, u32[]{:S(2)}, u32[]{:S(2)}) async-start(bf16[8,96,1024]{2,1,0:T(8,128)(2,1)} %pack_live_tokens.3), calls=%async_computation.7 | async-start | bytes 3145728 | tf_op jit(solution)/shard_map/all_to_all | solution.py:520
  16.9 0.2 select_reduce_fusion.4
  17.2 0.1 fusion.69
  17.4 0.1 select_reduce_fusion.6
  17.5 0.6 reduce_max.37
  18.2 0.1 reduce_sum.112
  18.3 0.7 reduce_max.36
  19.0 1.3 %pad_add_fusion.1 = s32[2]{0:T(128)S(1)} fusion(s32[1]{0:T(128)} %bitcast.10, s32[1]{0:T(128)} %bitcast.9), kind=kLoop, calls=%fused_computation.109 | loop fusion | flops 2 | bytes 16 | tf_op jit(solution)/shard_map/stack | solution.py:561
  20.3 1.5 %collective-permute-start.4 = (s32[2]{0:T(128)S(1)}, s32[2]{0:T(128)S(1)}, u32[]{:S(2)}, u32[]{:S(2)}) collective-permute-start(s32[2]{0:T(128)S(1)} %pad_add_fusion.1), channel_id=1, source_target_pairs={{0,16},{16,0},{1,17},{17,1},{2,18},{18,2},{3,19},{19,3},{4,20},{20... | collective-permute-start | bytes 32 | tf_op jit(solution)/shard_map/ppermute | solution.py:566
  21.9 2.1 %collective-permute-start.5 = (bf16[4,8,32,128]{3,2,1,0:T(8,128)(2,1)S(1)}, bf16[4,8,32,128]{3,2,1,0:T(8,128)(2,1)S(1)}, u32[]{:S(2)}, u32[]{:S(2)}) collective-permute-start(bf16[4,8,32,128]{3,2,1,0:T(8,128)(2,1)S(1)} %pad_maximum_fusion), channel_id=1, source_target_pairs={{0,2},{2,0},{4,6},{6,4},{8,10},{10,8},{12,14},{14,12},{1,3},{3,1},... | collective-permute-start | bytes 786440 | tf_op jit(solution)/shard_map/ppermute | solution.py:466
  24.0 0.3 copy.28
  24.3 1.3 %key_projection.2.refs_4_ = bf16[4,256,1024]{2,1,0:T(8,128)(2,1)S(1)} custom-call(bf16[32,32,128]{2,1,0:T(8,128)(2,1)S(1)} %bitcast.41, bf16[4,1024,256]{2,1,0:T(8,128)(2,1)S(1)} %bitcast.43), custom_call_target="tpu_custom_call" | custom-call | bytes 1024 | tf_op jit(solution)/shard_map/key_projection/pallas_call | solution.py:586
  25.6 0.1 select_reduce_fusion.3
  25.7 0.1 fusion.53
  25.8 0.3 select_reduce_fusion.2
  26.1 1.0 select_reduce_fusion
  27.2 1.3 %fusion.75 = s32[2]{0:T(128)S(1)} fusion(s32[2]{0:T(128)S(1)} %collective-permute-done.4, s32[1]{0:T(128)} %bitcast.10, s32[1]{0:T(128)} %bitcast.9), kind=kLoop, calls=%fused_computation.120 | loop fusion | flops 4 | bytes 24 | tf_op jit(solution)/shard_map/max | solution.py:565
  28.5 0.6 fusion.73
  29.9 7.5 %collective-permute-done.5 = bf16[4,8,32,128]{3,2,1,0:T(8,128)(2,1)S(1)} collective-permute-done((bf16[4,8,32,128]{3,2,1,0:T(8,128)(2,1)S(1)}, bf16[4,8,32,128]{3,2,1,0:T(8,128)(2,1)S(1)}, u32[]{:S(2)}, u32[]{:S(2)}) %collective-permute-start.5) | collective-permute-done | bytes 262176 | tf_op jit(solution)/shard_map/ppermute | solution.py:466
  37.5 3.1 %key_projection.3.refs_5_ = bf16[4,256,1024]{2,1,0:T(8,128)(2,1)S(1)} custom-call(bf16[32,32,128]{2,1,0:T(8,128)(2,1)S(1)} %bitcast.42, bf16[4,1024,256]{2,1,0:T(8,128)(2,1)} %bitcast.44), custom_call_target="tpu_custom_call" | custom-call | bytes 1024 | tf_op jit(solution)/shard_map/key_projection/pallas_call | solution.py:586
  40.6 1.3 %copy-done.2 = bf16[4,256,1024]{2,1,0:T(8,128)(2,1)} copy-done((bf16[4,256,1024]{2,1,0:T(8,128)(2,1)}, bf16[4,256,1024]{2,1,0:T(8,128)(2,1)S(1)}, u32[]{:S(2)}) %copy-start.2) | copy-done | bytes 2097176
  41.9 11.2 %all-to-all-done.7 = bf16[8,96,1024]{2,1,0:T(8,128)(2,1)} async-done(((bf16[8,96,1024]{2,1,0:T(8,128)(2,1)}), bf16[8,96,1024]{2,1,0:T(8,128)(2,1)}, u32[]{:S(2)}, u32[]{:S(2)}) %all-to-all-start.7) | async-done | bytes 1572896 | tf_op jit(solution)/shard_map/all_to_all | solution.py:520
  53.8 1.8 %conditional.2 = (bf16[256,1024]{1,0:T(8,128)(2,1)}, bf16[256,1024]{1,0:T(8,128)(2,1)}) conditional(s32[]{:T(128)} %bitcast.21, () %tuple.25, (s32[2]{0:T(128)S(1)}, s32[256]{0:T(256)S(1)}, s32[256]{0:T(256)S(1)}, bf16[256,8192]{1,0:T(8,128)(2,1)}) %tuple.57), branch_computations={%region_12.13_spmd, %region_13.14_spmd} | conditional | flops 134217728 | bytes 70254648 | solution.py:579
  53.8 0.9 broadcast.406.clone
  54.7 0.9 broadcast.406
  55.6 1.3 %collective-permute-done.6.refs_1_ = bf16[768,1024]{1,0:T(8,128)(2,1)} collective-permute-done((bf16[768,1024]{1,0:T(8,128)(2,1)}, bf16[768,1024]{1,0:T(8,128)(2,1)}, u32[]{:S(2)}, u32[]{:S(2)}) %collective-permute-start.6) | collective-permute-done | bytes 1572896 | tf_op jit(solution)/shard_map/ppermute | solution.py:606
  56.9 1.6 %copy-done.3 = bf16[4,256,1024]{2,1,0:T(8,128)(2,1)S(1)} copy-done((bf16[4,256,1024]{2,1,0:T(8,128)(2,1)S(1)}, bf16[4,256,1024]{2,1,0:T(8,128)(2,1)}, u32[]{:S(2)}) %copy-start.3) | copy-done | bytes 2097176
  58.5 7.7 %prompt_scores.1 = (bf16[8,32,384]{2,1,0:T(8,128)(2,1)}, bf16[8,32,256]{2,1,0:T(8,128)(2,1)}) custom-call(s32[651]{0:T(1024)S(1)} %concatenate.6.meta_ref, bf16[768,1024]{1,0:T(8,128)(2,1)} %bitcast.12.refs_0_, bf16[768,1024]{1,0:T(8,128)(2,1)} %collective-permute-done.6.refs_1_, bf16[256,1024]{1,0:T(8,128)(2,1)} %get-tuple-element.139.refs_2_, ...), custom_call_target="tpu_custom_call" | custom-call | tf_op jit(solution)/shard_map/prompt_scores/pallas_call | solution.py:625
  66.2 35.5 %conditional.3 = (bf16[2,4,64,128]{3,2,1,0:T(8,128)(2,1)S(1)}, bf16[2,4,64,128]{3,2,1,0:T(8,128)(2,1)S(1)}, bf16[2,4,64,128]{3,2,1,0:T(8,128)(2,1)S(1)}, bf16[2,...) conditional(s32[]{:T(128)} %bitcast.11, (bf16[8,32,384]{2,1,0:T(8,128)(2,1)}, s32[1,640]{1,0:T(1,128)S(1)}, ...), branch_computations={%region_14.17_spmd, %region_17.20_spmd} | conditional | flops 34047488 | bytes 115446024 | solution.py:743
  66.2 3.5 %all-to-all-start.1 = ((bf16[8,32,384]{2,1,0:T(8,128)(2,1)}), bf16[8,32,384]{2,1,0:T(8,128)(2,1)S(1)}, u32[]{:S(2)}, u32[]{:S(2)}) async-start(bf16[8,32,384]{2,1,0:T(8,128)(2,1)} %get-tuple-element.68), calls=%async_computation.1 | async-start | bytes 393216 | tf_op jit(solution)/shard_map/cond/branch_0_fun/all_to_all | solution.py:655
  69.8 3.0 %copy.25 = bf16[8,256,4,256]{3,1,2,0:T(8,128)(2,1)S(1)} copy(bf16[8,256,4,256]{3,2,1,0:T(4,128)(2,1)} %get-tuple-element.207) | data formatting | bytes 8388608 | tf_op jit(solution)/shard_map
  72.8 0.7 fusion.71
  73.5 1.3 %copy-done.9 = bf16[8,256,4,256]{3,1,2,0:T(8,128)(2,1)} copy-done((bf16[8,256,4,256]{3,1,2,0:T(8,128)(2,1)}, bf16[8,256,4,256]{3,1,2,0:T(8,128)(2,1)S(1)}, u32[]{:S(2)}) %copy-start.9) | copy-done | bytes 4194328 | tf_op jit(solution)/shard_map/cond
  74.8 0.1 broadcast_in_dim.162.refs_2_
  74.9 0.2 fusion.17
  75.2 0.1 broadcast_in_dim.163.refs_3_
  75.3 2.8 %all-to-all-done.1.refs_0_ = bf16[8,32,384]{2,1,0:T(8,128)(2,1)S(1)} async-done(((bf16[8,32,384]{2,1,0:T(8,128)(2,1)}), bf16[8,32,384]{2,1,0:T(8,128)(2,1)S(1)}, u32[]{:S(2)}, u32[]{:S(2)}) %all-to-all-start.1) | async-done | bytes 196640 | tf_op jit(solution)/shard_map/cond/branch_0_fun/all_to_all | solution.py:655
  78.1 1.7 %softmax_weights.2 = (bf16[8,32,384]{2,1,0:T(8,128)(2,1)}, f32[8,32,1]{2,1,0:T(8,128)S(1)}) custom-call(bf16[8,32,384]{2,1,0:T(8,128)(2,1)S(1)} %all-to-all-done.1.refs_0_, s32[1,384]{1,0:T(1,128)S(1)} %slice.18.refs_1_, f32[8,32,1]{2,1,0:T(8,128)S(1)} %broadcast_in_dim.162.refs_2_, f32[8,32,1]{2,1,0:T(8,128)S(1)} %broadcast_in_dim.163.refs_3_), custom_call_target="tpu_custom_call" | custom-call | tf_op jit(solution)/shard_map/cond/branch_0_fun/softmax_weights/pallas_call | solution.py:669
  79.8 3.6 %all-to-all-start.2 = ((bf16[8,32,384]{2,1,0:T(8,128)(2,1)}), bf16[8,32,384]{2,1,0:T(8,128)(2,1)S(1)}, u32[]{:S(2)}, u32[]{:S(2)}) async-start(bf16[8,32,384]{2,1,0:T(8,128)(2,1)} %get-tuple-element.73.refs_4_), calls=%async_computation.2 | async-start | bytes 393216 | tf_op jit(solution)/shard_map/cond/branch_0_fun/all_to_all | solution.py:701
  83.4 0.1 reduce
  83.5 5.5 %owner_lists.2.refs_2_ = bf16[8,640,1024]{2,1,0:T(8,128)(2,1)} custom-call(s32[651]{0:T(1024)S(1)} %get-tuple-element.67.meta_ref, bf16[768,1024]{1,0:T(8,128)(2,1)} %get-tuple-element.75.refs_0_, bf16[768,1024]{1,0:T(8,128)(2,1)} %get-tuple-element.76.refs_1_, bf16[256,1024]{1,0:T(8,128)(2,1)} %get-tuple-element.77.refs_2_, ...), custom_call_target="tpu_custom_call" | custom-call | bytes 16777216 | tf_op jit(solution)/shard_map/cond/branch_0_fun/owner_lists/pallas_call | solution.py:680
  89.1 0.4 fusion.13
  89.5 1.4 %all-to-all-done.2.refs_0_ = bf16[8,32,384]{2,1,0:T(8,128)(2,1)S(1)} async-done(((bf16[8,32,384]{2,1,0:T(8,128)(2,1)}), bf16[8,32,384]{2,1,0:T(8,128)(2,1)S(1)}, u32[]{:S(2)}, u32[]{:S(2)}) %all-to-all-start.2) | async-done | bytes 196640 | tf_op jit(solution)/shard_map/cond/branch_0_fun/all_to_all | solution.py:701
  90.9 4.0 %copy-done.1 = bf16[8,640,1024]{2,1,0:T(8,128)(2,1)S(1)} copy-done((bf16[8,640,1024]{2,1,0:T(8,128)(2,1)S(1)}, bf16[8,640,1024]{2,1,0:T(8,128)(2,1)}, u32[]{:S(2)}) %copy-start.1) | copy-done | bytes 10485784 | tf_op jit(solution)/shard_map/cond
  94.9 6.6 %weighted_values.2 = (bf16[2,4,64,128]{3,2,1,0:T(8,128)(2,1)S(1)}, bf16[2,4,64,128]{3,2,1,0:T(8,128)(2,1)S(1)}, bf16[2,4,64,128]{3,2,1,0:T(8,128)(2,1)S(1)}, bf16[2,4,64,128]{3,2,1,0:T(8,128)(2,1)S(1)}) custom-call(s32[651]{0:T(1024)S(1)} %get-tuple-element.67.meta_ref, bf16[8,32,384]{2,1,0:T(8,128)(2,1)S(1)} %all-to-all-done.2.refs_0_, ...), custom_call_target="tpu_custom_call" | custom-call | tf_op jit(solution)/shard_map/cond/branch_0_fun/weighted_values/pallas_call | solution.py:708
  101.7 1.0 collective-permute-start.7
  102.8 0.8 collective-permute-start.8
  103.6 1.7 %collective-permute-start.9 = (bf16[2,4,64,128]{3,2,1,0:T(8,128)(2,1)S(1)}, bf16[2,4,64,128]{3,2,1,0:T(8,128)(2,1)S(1)}, u32[]{:S(2)}, u32[]{:S(2)}) collective-permute-start(bf16[2,4,64,128]{3,2,1,0:T(8,128)(2,1)S(1)} %get-tuple-element.149), channel_id=1, source_target_pairs={{0,6},{2,4},{4,2},{6,0},{8,14},{10,12},{12,10},{14,8},{1,7},{3,5},... | collective-permute-start | bytes 393224 | tf_op jit(solution)/shard_map/ppermute | solution.py:466
  105.3 2.9 %collective-permute-done.7.refs_1_ = bf16[2,4,64,128]{3,2,1,0:T(8,128)(2,1)S(1)} collective-permute-done((bf16[2,4,64,128]{3,2,1,0:T(8,128)(2,1)S(1)}, bf16[2,4,64,128]{3,2,1,0:T(8,128)(2,1)S(1)}, u32[]{:S(2)}, u32[]{:S(2)}) %collective-permute-start.7) | collective-permute-done | bytes 131104 | tf_op jit(solution)/shard_map/ppermute | solution.py:466
  108.2 1.6 %collective-permute-done.9.refs_3_ = bf16[2,4,64,128]{3,2,1,0:T(8,128)(2,1)S(1)} collective-permute-done((bf16[2,4,64,128]{3,2,1,0:T(8,128)(2,1)S(1)}, bf16[2,4,64,128]{3,2,1,0:T(8,128)(2,1)S(1)}, u32[]{:S(2)}, u32[]{:S(2)}) %collective-permute-start.9) | collective-permute-done | bytes 131104 | tf_op jit(solution)/shard_map/ppermute | solution.py:466
  109.9 2.4 %collective-permute-start.10 = (bf16[2,4,64,128]{3,2,1,0:T(8,128)(2,1)S(1)}, bf16[2,4,64,128]{3,2,1,0:T(8,128)(2,1)S(1)}, u32[]{:S(2)}, u32[]{:S(2)}) collective-permute-start(bf16[2,4,64,128]{3,2,1,0:T(8,128)(2,1)S(1)} %get-tuple-element.152.after_ref), channel_id=1, source_target_pairs={{0,8},{2,10},{4,12},{6,14},{8,0},{10,2},{12,4},{14,6},{1,9},{3,11}... | collective-permute-start | bytes 393224 | tf_op jit(solution)/shard_map/ppermute | solution.py:466
  112.3 5.1 %collective-permute-done.10.got_ref = bf16[2,4,64,128]{3,2,1,0:T(8,128)(2,1)S(1)} collective-permute-done((bf16[2,4,64,128]{3,2,1,0:T(8,128)(2,1)S(1)}, bf16[2,4,64,128]{3,2,1,0:T(8,128)(2,1)S(1)}, u32[]{:S(2)}, u32[]{:S(2)}) %collective-permute-start.10) | collective-permute-done | bytes 131104 | tf_op jit(solution)/shard_map/ppermute | solution.py:466
  117.4 0.6 collective-permute-start.13
  118.0 1.6 %collective-permute-start.12 = (bf16[16,4096]{1,0:T(8,128)(2,1)S(1)}, bf16[16,4096]{1,0:T(8,128)(2,1)S(1)}, u32[]{:S(2)}, u32[]{:S(2)}) collective-permute-start(bf16[16,4096]{1,0:T(8,128)(2,1)S(1)} %attended_sum.1), channel_id=1, source_target_pairs={{0,4},{2,6},{4,0},{6,2},{8,12},{10,14},{12,8},{14,10},{1,5},{3,7},... | collective-permute-start | bytes 393224 | tf_op jit(solution)/shard_map/ppermute | solution.py:466
  119.6 1.3 %collective-permute-start.11 = (bf16[16,4096]{1,0:T(8,128)(2,1)S(1)}, bf16[16,4096]{1,0:T(8,128)(2,1)S(1)}, u32[]{:S(2)}, u32[]{:S(2)}) collective-permute-start(bf16[16,4096]{1,0:T(8,128)(2,1)S(1)} %attended_sum.1), channel_id=1, source_target_pairs={{0,2},{2,0},{4,6},{6,4},{8,10},{10,8},{12,14},{14,12},{1,3},{3,1},... | collective-permute-start | bytes 393224 | tf_op jit(solution)/shard_map/ppermute | solution.py:466
  121.0 3.4 %copy-done.4 = bf16[4096,1024]{1,0:T(8,128)(2,1)S(1)} copy-done((bf16[4096,1024]{1,0:T(8,128)(2,1)S(1)}, bf16[4096,1024]{1,0:T(8,128)(2,1)}, u32[]{:S(2)}) %copy-start.4) | copy-done | bytes 8388632
  124.3 0.6 stage_out_weight.1
  125.0 1.6 %fusion.43 = f32[64,1024]{1,0:T(8,128)S(1)} fusion(bf16[4096,1024]{1,0:T(8,128)(2,1)S(1)} %stage_out_weight.1, bf16[16,4096]{1,0:T(8,128)(2,1)S(1)} %collective-permute-done.13, bf16[16,4096]{1,0:T(8,128)(2,1)S(1)} %collective-permute-done.12, bf16[16,4096]{1,0:T(8,128)(2,1)S(1)} %collective-permute-done.11, bf16[16,4096]{1,0:T(8,128)(2,1)S(1)} %attended_sum.1), kind=kOutput, calls=%fused_computation.33 | convolution fusion | flops 538968064 | bytes 9175040 | tf_op jit(solution)/shard_map/dot_general | solution.py:782
  126.7 1.3 %collective-permute-done.14.got_ref = f32[64,512]{1,0:T(8,128)S(1)} collective-permute-done((f32[64,512]{1,0:T(8,128)S(1)}, f32[64,512]{1,0:T(8,128)S(1)}, u32[]{:S(2)}, u32[]{:S(2)}) %collective-permute-start.14) | collective-permute-done | bytes 131104 | tf_op jit(solution)/shard_map/ppermute | solution.py:789
  128.1 0.6 order_rows.1
  (55 shorter events, 1.0 us)
Async XLA Ops:
  0.0 10.7 %collective-permute-start.3 = (bf16[8,32,128]{2,1,0:T(8,128)(2,1)}, bf16[8,32,128]{2,1,0:T(8,128)(2,1)S(1)}, u32[]{:S(2)}, u32[]{:S(2)}) collective-permute-start(bf16[8,32,128]{2,1,0:T(8,128)(2,1)} %param.18), channel_id=1, source_target_pairs={{0,12},{2,14},{4,8},{6,10},{8,4},{10,6},{12,0},{14,2},{1,13},{3,15... | collective-permute-start | bytes 196616 | tf_op jit(solution)/shard_map/ppermute | solution.py:466
  5.0 5.6 %collective-permute-start.2 = (bf16[8,32,128]{2,1,0:T(8,128)(2,1)}, bf16[8,32,128]{2,1,0:T(8,128)(2,1)S(1)}, u32[]{:S(2)}, u32[]{:S(2)}) collective-permute-start(bf16[8,32,128]{2,1,0:T(8,128)(2,1)} %param.18), channel_id=1, source_target_pairs={{0,4},{2,6},{4,0},{6,2},{8,12},{10,14},{12,8},{14,10},{1,5},{3,7},... | collective-permute-start | bytes 196616 | tf_op jit(solution)/shard_map/ppermute | solution.py:466
  5.1 5.8 %collective-permute-start.1 = (bf16[8,32,128]{2,1,0:T(8,128)(2,1)}, bf16[8,32,128]{2,1,0:T(8,128)(2,1)S(1)}, u32[]{:S(2)}, u32[]{:S(2)}) collective-permute-start(bf16[8,32,128]{2,1,0:T(8,128)(2,1)} %param.18), channel_id=1, source_target_pairs={{0,8},{2,10},{4,12},{6,14},{8,0},{10,2},{12,4},{14,6},{1,9},{3,11}... | collective-permute-start | bytes 196616 | tf_op jit(solution)/shard_map/ppermute | solution.py:466
  5.7 11.1 %copy-start.14 = (s32[256]{0:T(256)S(1)}, s32[256]{0:T(256)}, u32[]{:S(2)}) copy-start(s32[256]{0:T(256)} %fill_ref.1) | copy-start | bytes 3076
  5.7 11.2 %copy-start.13 = (s32[256,1]{0,1:T(1,128)S(1)}, s32[256,1]{0,1:T(1,128)}, u32[]{:S(2)}) copy-start(s32[256,1]{0,1:T(1,128)} %param.15) | copy-start | bytes 3076
  5.7 16.1 %copy-start.12 = (bf16[8,32,128]{2,1,0:T(8,128)(2,1)S(1)}, bf16[8,32,128]{2,1,0:T(8,128)(2,1)}, u32[]{:S(2)}) copy-start(bf16[8,32,128]{2,1,0:T(8,128)(2,1)} %param.18) | copy-start | bytes 196612
  5.7 18.3 %copy-start.11 = (bf16[1024,4,256]{2,1,0:T(4,128)(2,1)S(1)}, bf16[1024,4,256]{2,1,0:T(4,128)(2,1)}, u32[]{:S(2)}) copy-start(bf16[1024,4,256]{2,1,0:T(4,128)(2,1)} %param.14) | copy-start | bytes 6291460
  10.9 42.2 %all-to-all-start.7 = ((bf16[8,96,1024]{2,1,0:T(8,128)(2,1)}), bf16[8,96,1024]{2,1,0:T(8,128)(2,1)}, u32[]{:S(2)}, u32[]{:S(2)}) async-start(bf16[8,96,1024]{2,1,0:T(8,128)(2,1)} %pack_live_tokens.3), calls=%async_computation.7 | async-start | bytes 3145728 | tf_op jit(solution)/shard_map/all_to_all | solution.py:520
  20.3 6.8 %collective-permute-start.4 = (s32[2]{0:T(128)S(1)}, s32[2]{0:T(128)S(1)}, u32[]{:S(2)}, u32[]{:S(2)}) collective-permute-start(s32[2]{0:T(128)S(1)} %pad_add_fusion.1), channel_id=1, source_target_pairs={{0,16},{16,0},{1,17},{17,1},{2,18},{18,2},{3,19},{19,3},{4,20},{20... | collective-permute-start | bytes 32 | tf_op jit(solution)/shard_map/ppermute | solution.py:566
  21.9 3.7 %copy-start.16 = (s32[256]{0:T(256)S(1)}, s32[256]{0:T(256)}, u32[]{:S(2)}) copy-start(s32[256]{0:T(256)} %param.16) | copy-start | bytes 3076
  21.9 15.6 %collective-permute-start.5 = (bf16[4,8,32,128]{3,2,1,0:T(8,128)(2,1)S(1)}, bf16[4,8,32,128]{3,2,1,0:T(8,128)(2,1)S(1)}, u32[]{:S(2)}, u32[]{:S(2)}) collective-permute-start(bf16[4,8,32,128]{3,2,1,0:T(8,128)(2,1)S(1)} %pad_maximum_fusion), channel_id=1, source_target_pairs={{0,2},{2,0},{4,6},{6,4},{8,10},{10,8},{12,14},{14,12},{1,3},{3,1},... | collective-permute-start | bytes 786440 | tf_op jit(solution)/shard_map/ppermute | solution.py:466
  24.2 1.3 %copy-start.5 = (bf16[1024,4,256]{2,0,1:T(8,128)(2,1)}, bf16[1024,4,256]{2,0,1:T(8,128)(2,1)S(1)}, u32[]{:S(2)}) copy-start(bf16[1024,4,256]{2,0,1:T(8,128)(2,1)S(1)} %copy.28) | copy-start | bytes 6291460
  40.5 1.3 %copy-start.2 = (bf16[4,256,1024]{2,1,0:T(8,128)(2,1)}, bf16[4,256,1024]{2,1,0:T(8,128)(2,1)S(1)}, u32[]{:S(2)}) copy-start(bf16[4,256,1024]{2,1,0:T(8,128)(2,1)S(1)} %key_projection.3.refs_5_) | copy-start | bytes 6291460
  53.1 3.8 %collective-permute-start.6 = (bf16[768,1024]{1,0:T(8,128)(2,1)}, bf16[768,1024]{1,0:T(8,128)(2,1)}, u32[]{:S(2)}, u32[]{:S(2)}) collective-permute-start(bf16[768,1024]{1,0:T(8,128)(2,1)} %bitcast.12.refs_0_), channel_id=1, source_target_pairs={{0,1},{1,0},{2,3},{3,2},{4,5},{5,4},{6,7},{7,6},{8,9},{9,8},{10,11... | collective-permute-start | bytes 4718600 | tf_op jit(solution)/shard_map/ppermute | solution.py:606
  56.9 1.6 %copy-start.3 = (bf16[4,256,1024]{2,1,0:T(8,128)(2,1)S(1)}, bf16[4,256,1024]{2,1,0:T(8,128)(2,1)}, u32[]{:S(2)}) copy-start(bf16[4,256,1024]{2,1,0:T(8,128)(2,1)} %copy-done.2) | copy-start | bytes 6291460
  58.5 7.7 %copy-start.15 = (s32[8]{0:T(128)S(1)}, s32[8]{0:T(128)}, u32[]{:S(2)}) copy-start(s32[8]{0:T(128)} %param.20) | copy-start | bytes 100
  66.2 11.9 %all-to-all-start.1 = ((bf16[8,32,384]{2,1,0:T(8,128)(2,1)}), bf16[8,32,384]{2,1,0:T(8,128)(2,1)S(1)}, u32[]{:S(2)}, u32[]{:S(2)}) async-start(bf16[8,32,384]{2,1,0:T(8,128)(2,1)} %get-tuple-element.68), calls=%async_computation.1 | async-start | bytes 393216 | tf_op jit(solution)/shard_map/cond/branch_0_fun/all_to_all | solution.py:655
  72.8 2.1 %copy-start.9 = (bf16[8,256,4,256]{3,1,2,0:T(8,128)(2,1)}, bf16[8,256,4,256]{3,1,2,0:T(8,128)(2,1)S(1)}, u32[]{:S(2)}) copy-start(bf16[8,256,4,256]{3,1,2,0:T(8,128)(2,1)S(1)} %copy.25) | copy-start | bytes 12582916 | tf_op jit(solution)/shard_map/cond
  79.8 11.1 %all-to-all-start.2 = ((bf16[8,32,384]{2,1,0:T(8,128)(2,1)}), bf16[8,32,384]{2,1,0:T(8,128)(2,1)S(1)}, u32[]{:S(2)}, u32[]{:S(2)}) async-start(bf16[8,32,384]{2,1,0:T(8,128)(2,1)} %get-tuple-element.73.refs_4_), calls=%async_computation.2 | async-start | bytes 393216 | tf_op jit(solution)/shard_map/cond/branch_0_fun/all_to_all | solution.py:701
  83.5 5.6 %copy-start.10 = (bf16[8,256,4,256]{3,1,2,0:T(8,128)(2,1)S(1)}, bf16[8,256,4,256]{3,1,2,0:T(8,128)(2,1)}, u32[]{:S(2)}) copy-start(bf16[8,256,4,256]{3,1,2,0:T(8,128)(2,1)} %copy-done.9) | copy-start | bytes 12582916 | tf_op jit(solution)/shard_map/cond
  83.5 7.4 %copy-start.6 = (bf16[4,1024,256]{2,1,0:T(8,128)(2,1)S(1)}, bf16[4,1024,256]{2,1,0:T(8,128)(2,1)}, u32[]{:S(2)}) copy-start(bf16[4,1024,256]{2,1,0:T(8,128)(2,1)} %get-tuple-element.79.refs_3_) | copy-start | bytes 6291460 | tf_op jit(solution)/shard_map/cond
  90.9 4.0 %copy-start.1 = (bf16[8,640,1024]{2,1,0:T(8,128)(2,1)S(1)}, bf16[8,640,1024]{2,1,0:T(8,128)(2,1)}, u32[]{:S(2)}) copy-start(bf16[8,640,1024]{2,1,0:T(8,128)(2,1)} %owner_lists.2.refs_2_) | copy-start | bytes 31457284 | tf_op jit(solution)/shard_map/cond
  101.7 6.4 %collective-permute-start.7 = (bf16[2,4,64,128]{3,2,1,0:T(8,128)(2,1)S(1)}, bf16[2,4,64,128]{3,2,1,0:T(8,128)(2,1)S(1)}, u32[]{:S(2)}, u32[]{:S(2)}) collective-permute-start(bf16[2,4,64,128]{3,2,1,0:T(8,128)(2,1)S(1)} %get-tuple-element.147), channel_id=1, source_target_pairs={{0,2},{2,0},{4,6},{6,4},{8,10},{10,8},{12,14},{14,12},{1,3},{3,1},... | collective-permute-start | bytes 393224 | tf_op jit(solution)/shard_map/ppermute | solution.py:466
  102.8 5.4 %collective-permute-start.8 = (bf16[2,4,64,128]{3,2,1,0:T(8,128)(2,1)S(1)}, bf16[2,4,64,128]{3,2,1,0:T(8,128)(2,1)S(1)}, u32[]{:S(2)}, u32[]{:S(2)}) collective-permute-start(bf16[2,4,64,128]{3,2,1,0:T(8,128)(2,1)S(1)} %get-tuple-element.148), channel_id=1, source_target_pairs={{0,4},{2,6},{4,0},{6,2},{8,12},{10,14},{12,8},{14,10},{1,5},{3,7},... | collective-permute-start | bytes 393224 | tf_op jit(solution)/shard_map/ppermute | solution.py:466
  103.6 6.2 %collective-permute-start.9 = (bf16[2,4,64,128]{3,2,1,0:T(8,128)(2,1)S(1)}, bf16[2,4,64,128]{3,2,1,0:T(8,128)(2,1)S(1)}, u32[]{:S(2)}, u32[]{:S(2)}) collective-permute-start(bf16[2,4,64,128]{3,2,1,0:T(8,128)(2,1)S(1)} %get-tuple-element.149), channel_id=1, source_target_pairs={{0,6},{2,4},{4,2},{6,0},{8,14},{10,12},{12,10},{14,8},{1,7},{3,5},... | collective-permute-start | bytes 393224 | tf_op jit(solution)/shard_map/ppermute | solution.py:466
  109.9 7.4 %collective-permute-start.10 = (bf16[2,4,64,128]{3,2,1,0:T(8,128)(2,1)S(1)}, bf16[2,4,64,128]{3,2,1,0:T(8,128)(2,1)S(1)}, u32[]{:S(2)}, u32[]{:S(2)}) collective-permute-start(bf16[2,4,64,128]{3,2,1,0:T(8,128)(2,1)S(1)} %get-tuple-element.152.after_ref), channel_id=1, source_target_pairs={{0,8},{2,10},{4,12},{6,14},{8,0},{10,2},{12,4},{14,6},{1,9},{3,11}... | collective-permute-start | bytes 393224 | tf_op jit(solution)/shard_map/ppermute | solution.py:466
  117.4 7.6 %collective-permute-start.13 = (bf16[16,4096]{1,0:T(8,128)(2,1)S(1)}, bf16[16,4096]{1,0:T(8,128)(2,1)S(1)}, u32[]{:S(2)}, u32[]{:S(2)}) collective-permute-start(bf16[16,4096]{1,0:T(8,128)(2,1)S(1)} %attended_sum.1), channel_id=1, source_target_pairs={{0,6},{2,4},{4,2},{6,0},{8,14},{10,12},{12,10},{14,8},{1,7},{3,5},... | collective-permute-start | bytes 393224 | tf_op jit(solution)/shard_map/ppermute | solution.py:466
  118.0 7.0 %collective-permute-start.12 = (bf16[16,4096]{1,0:T(8,128)(2,1)S(1)}, bf16[16,4096]{1,0:T(8,128)(2,1)S(1)}, u32[]{:S(2)}, u32[]{:S(2)}) collective-permute-start(bf16[16,4096]{1,0:T(8,128)(2,1)S(1)} %attended_sum.1), channel_id=1, source_target_pairs={{0,4},{2,6},{4,0},{6,2},{8,12},{10,14},{12,8},{14,10},{1,5},{3,7},... | collective-permute-start | bytes 393224 | tf_op jit(solution)/shard_map/ppermute | solution.py:466
  119.6 5.4 %collective-permute-start.11 = (bf16[16,4096]{1,0:T(8,128)(2,1)S(1)}, bf16[16,4096]{1,0:T(8,128)(2,1)S(1)}, u32[]{:S(2)}, u32[]{:S(2)}) collective-permute-start(bf16[16,4096]{1,0:T(8,128)(2,1)S(1)} %attended_sum.1), channel_id=1, source_target_pairs={{0,2},{2,0},{4,6},{6,4},{8,10},{10,8},{12,14},{14,12},{1,3},{3,1},... | collective-permute-start | bytes 393224 | tf_op jit(solution)/shard_map/ppermute | solution.py:466
  121.0 3.4 %copy-start.4 = (bf16[4096,1024]{1,0:T(8,128)(2,1)S(1)}, bf16[4096,1024]{1,0:T(8,128)(2,1)}, u32[]{:S(2)}) copy-start(bf16[4096,1024]{1,0:T(8,128)(2,1)} %weight_ref.1) | copy-start | bytes 25165828
  126.7 1.4 %collective-permute-start.14 = (f32[64,512]{1,0:T(8,128)S(1)}, f32[64,512]{1,0:T(8,128)S(1)}, u32[]{:S(2)}, u32[]{:S(2)}) collective-permute-start(f32[64,512]{1,0:T(8,128)S(1)} %get-tuple-element.240), channel_id=1, source_target_pairs={{0,1},{1,0},{2,3},{3,2},{4,5},{5,4},{6,7},{7,6},{8,9},{9,8},{10,11... | collective-permute-start | bytes 393224 | tf_op jit(solution)/shard_map/ppermute | solution.py:789

commit v18 on v17

--- a/solution.py
+++ b/solution.py
@@ -242,23 +242,31 @@
             got = got + part_ref[i].astype(jnp.float32)
         scores.append(got * scale)
         owner_rows.append(row_ref[...])
-    weights = [jnp.zeros(s.shape, jnp.float32) for s in scores]
-    for r in range(top_ref.shape[0]):
-        own = [jnp.where(o == r, s, -jnp.inf) for o, s in zip(owner_rows, scores)]
-        cache_top = top_ref[r]
-        top = cache_top
-        for o in own:
-            top = jnp.maximum(top, jnp.max(o, 1, keepdims=True))
-        held = [jnp.exp(o - top) for o in own]
-        fade = jnp.exp(cache_top - top)
+    rows = range(top_ref.shape[0])
+    spread = [jnp.zeros(s.shape, jnp.float32) for s in scores]
+    tops = []
+    for r in rows:
+        top = top_ref[r]
+        for o, s in zip(owner_rows, scores):
+            top = jnp.maximum(top, jnp.max(jnp.where(o == r, s, -jnp.inf), 1, keepdims=True))
+        tops.append(top)
+        spread = [jnp.where(o == r, top, t) for o, t in zip(owner_rows, spread)]
+    held = [
+        jnp.exp(jnp.where(o >= 0, s - t, -jnp.inf))
+        for o, s, t in zip(owner_rows, scores, spread)
+    ]
+    shares = [jnp.zeros(s.shape, jnp.float32) for s in scores]
+    for r in rows:
+        fade = jnp.exp(top_ref[r] - tops[r])
         total = sum_ref[r] * fade
-        for h in held:
-            total = total + jnp.sum(h, 1, keepdims=True)
-        weights = [w + h / total for w, h in zip(weights, held)]
+        for o, h in zip(owner_rows, held):
+            total = total + jnp.sum(jnp.where(o == r, h, 0.0), 1, keepdims=True)
+        shares = [jnp.where(o == r, 1.0 / total, t) for o, t in zip(owner_rows, shares)]
         share_ref[r] = fade / total
-    for w, w_ref in zip(weights, w_refs):
+    for h, t, w_ref in zip(held, shares, w_refs):
+        weights = (h * t).astype(w_ref.dtype)
         for i in range(n):
-            w_ref[i] = w.astype(w_ref.dtype)
+            w_ref[i] = weights
 
 
 def list_copies(n, lanes, sizes, source, target, sem):
@@ -273,14 +281,14 @@
     return copies
 
 
-def list_kernel(n, meta_ref, *refs):
+def list_kernel(n, lanes, meta_ref, *refs):
     x_refs, (_, out_ref, held, more, wide, lists, sem, out_sem) = refs[:4], refs[4:]
     q = pl.program_id(0)
-    lanes = lists.shape[1]
-    cuts = tile_cuts(lanes)
+    length = lists.shape[1]
+    cuts = tile_cuts(length)
     groups = lanes // BLK
     at_size = n * groups
-    copies = list_copies(n, lanes, lambda o: meta_ref[at_size + o], lists, out_ref, out_sem)
+    copies = list_copies(n, length, lambda o: meta_ref[at_size + o], lists, out_ref, out_sem)
 
     @pl.when(q == 0)
     def _():
@@ -306,7 +314,7 @@
                 pl.when(used)(copy.wait)
 
 
-def value_kernel(n, rows, count, meta_ref, *refs):
+def value_kernel(n, rows, lanes, count, meta_ref, *refs):
     w_refs, (row_ref, list_ref, weight_ref) = refs[:count], refs[count : count + 3]
     out_refs, scratch = refs[count + 3 : count + 3 + n // 2], refs[count + 3 + n // 2 :]
     values, lists, acc, mixed, value_sem, sem = scratch
@@ -319,14 +327,14 @@
         for h in range(kvh)
     ]
     _, heads, near = w_refs[0].shape
-    lanes = lists.shape[1]
+    length = lists.shape[1]
     per = rows * heads // kvh
-    cuts = tile_cuts(lanes)
+    cuts = tile_cuts(length)
     at_size = n * lanes // BLK
     me = meta_ref[at_size + n]
     q = partner_owner(step, me, n)
     size = meta_ref[at_size + q]
-    copies = list_copies(n, lanes, lambda o: meta_ref[at_size + o], list_ref, lists, sem)
+    copies = list_copies(n, length, lambda o: meta_ref[at_size + o], list_ref, lists, sem)
     ahead = min(3, n)
 
     def fetch(i):
@@ -379,8 +387,7 @@
 
     one(0)
     for t in range(1, len(cuts) - 1):
-        if cuts[t] < near or count > 1:
-            pl.when(size > cuts[t])(functools.partial(one, t))
+        pl.when(size > cuts[t])(functools.partial(one, t))
     pl.when(size > cuts[1])(lambda: keep(acc[...]))
 
     @pl.when(step == n - 1)
@@ -435,13 +442,18 @@
             )
 
 
-def stage_kernel(after_ref, weight_ref, out_ref, sem):
-    cuts = sem.shape[0]
-    span = out_ref.shape[0] // cuts
+def stage_kernel(core_ref, after_ref, weight_ref, own_ref, away_ref, sem):
+    cuts = sem.shape[1]
+    span, cols = own_ref.shape[0] // cuts, own_ref.shape[1]
     copies = [
         pltpu.make_async_copy(
-            weight_ref.at[pl.ds(i * span, span)], out_ref.at[pl.ds(i * span, span)], sem.at[i]
+            weight_ref.at[
+                pl.ds(i * span, span), pl.ds(pl.multiple_of(side * cols, 128), cols)
+            ],
+            ref.at[pl.ds(i * span, span)],
+            sem.at[j, i],
         )
+        for j, (side, ref) in enumerate(((1 - core_ref[0], away_ref), (core_ref[0], own_ref)))
         for i in range(cuts)
     ]
     for copy in copies:
@@ -677,8 +689,9 @@
             cache_top.reshape(rows, heads, 1),
             cache_sum.reshape(rows, heads, 1),
         )
+        length = near if count == 1 else lanes
         lists = pl.pallas_call(
-            functools.partial(list_kernel, n),
+            functools.partial(list_kernel, n, lanes),
             grid_spec=pltpu.PrefetchScalarGridSpec(
                 num_scalar_prefetch=1,
                 grid=(n,),
@@ -686,12 +699,12 @@
                 out_specs=anywhere,
                 scratch_shapes=[
                     *x_scratch,
-                    pltpu.VMEM((n, lanes, part), jnp.bfloat16),
+                    pltpu.VMEM((n, length, part), jnp.bfloat16),
                     pltpu.SemaphoreType.DMA((ntp, 4)),
-                    pltpu.SemaphoreType.DMA((n, len(tile_cuts(lanes)) - 1)),
+                    pltpu.SemaphoreType.DMA((n, len(tile_cuts(length)) - 1)),
                 ],
             ),
-            out_shape=jax.ShapeDtypeStruct((n, lanes, part), jnp.bfloat16),
+            out_shape=jax.ShapeDtypeStruct((n, length, part), jnp.bfloat16),
             compiler_params=pltpu.CompilerParams(vmem_limit_bytes=56 * MIB),
             cost_estimate=pl.CostEstimate(
                 flops=0, bytes_accessed=16 * MIB, transcendentals=0
@@ -706,7 +719,7 @@
             preferred_element_type=jnp.float32,
         )
         terms = pl.pallas_call(
-            functools.partial(value_kernel, n, rows, count),
+            functools.partial(value_kernel, n, rows, lanes, count),
             grid_spec=pltpu.PrefetchScalarGridSpec(
                 num_scalar_prefetch=1,
                 grid=(n,),
@@ -727,11 +740,11 @@
                 out_specs=[pl.BlockSpec(pair_shape, lambda i, m: (0, 0, 0, 0))] * (n // 2),
                 scratch_shapes=[
                     pltpu.VMEM((kvh, part, hd), jnp.bfloat16),
-                    pltpu.VMEM((n, lanes, part), jnp.bfloat16),
+                    pltpu.VMEM((n, length, part), jnp.bfloat16),
                     pltpu.VMEM((kvh * per, part), jnp.float32),
                     pltpu.VMEM((kvh, n * per, part), jnp.bfloat16),
                     pltpu.SemaphoreType.DMA((kvh,)),
-                    pltpu.SemaphoreType.DMA((n, len(tile_cuts(lanes)) - 1)),
+                    pltpu.SemaphoreType.DMA((n, len(tile_cuts(length)) - 1)),
                 ],
             ),
             out_shape=[jax.ShapeDtypeStruct(pair_shape, jnp.bfloat16)] * (n // 2),
@@ -765,28 +778,30 @@
         name="attended_sum",
     )(held, with_partner(send, n // 2, n))
 
-    staged = pl.pallas_call(
+    cols = out_weight.shape[1] // ntp
+    own_weight, away_weight = pl.pallas_call(
         stage_kernel,
-        in_specs=[anywhere, pl.BlockSpec(memory_space=pltpu.HBM)],
-        out_specs=in_vmem,
-        out_shape=jax.ShapeDtypeStruct(out_weight.shape, jnp.bfloat16),
-        scratch_shapes=[pltpu.SemaphoreType.DMA((8,))],
+        in_specs=[
+            pl.BlockSpec(memory_space=pltpu.SMEM),
+            anywhere,
+            pl.BlockSpec(memory_space=pltpu.HBM),
+        ],
+        out_specs=[in_vmem] * 2,
+        out_shape=[jax.ShapeDtypeStruct((out_weight.shape[0], cols), jnp.bfloat16)] * 2,
+        scratch_shapes=[pltpu.SemaphoreType.DMA((2, 4))],
         compiler_params=pltpu.CompilerParams(vmem_limit_bytes=16 * MIB),
         cost_estimate=pl.CostEstimate(
             flops=0, bytes_accessed=2 * out_weight.size * 2, transcendentals=0
         ),
         name="stage_out_weight",
-    )(send, out_weight)
+    )(core.reshape(1), send, out_weight)
 
     everyone = [attended] + [with_partner(attended, k, n) for k in range(1, n // 2)]
-    product = jnp.dot(
-        jnp.concatenate(everyone), staged, preferred_element_type=jnp.float32
-    )
-    cols = out_weight.shape[1] // ntp
+    everyone = jnp.concatenate(everyone)
+    away = jnp.dot(everyone, away_weight, preferred_element_type=jnp.float32)
     half_spec = pl.BlockSpec((n * rows, cols), lambda i, m: (0, 0))
-    own = lax.dynamic_slice_in_dim(product, core * cols, cols, 1)
-    away = lax.dynamic_slice_in_dim(product, (1 - core) * cols, cols, 1)
     got = lax.ppermute(away, "tp", swap)
+    own = jnp.dot(everyone, own_weight, preferred_element_type=jnp.float32)
     return pl.pallas_call(
         functools.partial(order_kernel, n),
         grid_spec=pltpu.PrefetchScalarGridSpec(

time: 129 us -> 126 us (0.977)
  Pallas kernels: 32.3 us -> 31 us
  local copies, waits for them, and re-layouts: 17.9 us -> 16.6 us
  transfers between devices with their start and end apart: 17 -> 17, of which waited for: 10 -> 10; matrix products, arithmetic and copies ran while one was open for 11% -> 12% of each run, Pallas kernels for 12% -> 12%
where the time goes in v18:
time: 126 us
  waiting for transfers between devices  35.4 us (28%)
  starting transfers between devices  31.5 us (25%)
  Pallas kernels  31 us (25%)
  local copies, waits for them, and re-layouts  16.6 us (13%)
  other arithmetic  6.46 us (5%)
  matrix products  2.83 us (2%)
  between operations  1.5 us (1%)
    ppermute x11, waiting for transfers between devices, with_partner(): return lax.ppermute(x, 'pool', [(i, i ^ k) for i in range(n)])  17.6 us
    ppermute x11, starting transfers between devices, with_partner(): return lax.ppermute(x, 'pool', [(i, i ^ k) for i in range(n)])  16.9 us
    all_to_all x1, waiting for transfers between devices, local(): lax.all_to_all(packed, 'pool', 0, 0, tiled=True).reshape(n * size, part)  11.2 us
    pallas_call x1, Pallas kernels, local(): pl.pallas_call(functools.partial(score_kernel, n, rows), grid_spec=pltpu....  7.43 us
    unnamed x20, local copies, waits for them, and re-layouts  6.32 us
    pallas_call x1, Pallas kernels, exchange_weights(): pl.pallas_call(functools.partial(value_kernel, n, rows, lanes, count), gr...  6 us
    all_to_all x1, starting transfers between devices, local(): lax.all_to_all(packed, 'pool', 0, 0, tiled=True).reshape(n * size, part)  5.88 us
    pallas_call x1, Pallas kernels, exchange_weights(): pl.pallas_call(functools.partial(list_kernel, n, lanes), grid_spec=pltpu....  5.15 us
  transfers between devices with their start and end apart: 17, of which 10 were waited for; matrix products, arithmetic and copies ran while one was open for 12% of the time, Pallas kernels for 12%

profile of v18, /device:TPU:0, one launch (start us, length us, event | category | flops | bytes accessed | tf_op | source)
XLA Modules:
  0.0 125.6 jit_solution(10805583036799551443)
XLA Ops:
  0.0 5.0 %collective-permute-start.3 = (bf16[8,32,128]{2,1,0:T(8,128)(2,1)}, bf16[8,32,128]{2,1,0:T(8,128)(2,1)S(1)}, u32[]{:S(2)}, u32[]{:S(2)}) collective-permute-start(bf16[8,32,128]{2,1,0:T(8,128)(2,1)} %param.18), channel_id=1, source_target_pairs={{0,12},{2,14},{4,8},{6,10},{8,4},{10,6},{12,0},{14,2},{1,13},{3,15... | collective-permute-start | bytes 196616 | tf_op jit(solution)/shard_map/ppermute | solution.py:478
  5.1 0.6 collective-permute-start.1
  5.7 4.9 %pack_live_tokens.3 = bf16[8,96,1024]{2,1,0:T(8,128)(2,1)} custom-call(s32[2]{0:T(128)S(1)} %pad_add_fusion.at_ref, s32[256]{0:T(256)} %fill_ref.1, s32[256]{0:T(256)} %bitcast.56, bf16[256,8192]{1,0:T(8,128)(2,1)} %x_ref.1), custom_call_target="tpu_custom_call" | custom-call | flops 402653184 | bytes 67108864 | tf_op jit(solution)/shard_map/pack_live_tokens/pallas_call | solution.py:62
  10.7 0.2 collective-permute-done.1
  10.9 5.9 %all-to-all-start.7 = ((bf16[8,96,1024]{2,1,0:T(8,128)(2,1)}), bf16[8,96,1024]{2,1,0:T(8,128)(2,1)}, u32[]{:S(2)}, u32[]{:S(2)}) async-start(bf16[8,96,1024]{2,1,0:T(8,128)(2,1)} %pack_live_tokens.3), calls=%async_computation.7 | async-start | bytes 3145728 | tf_op jit(solution)/shard_map/all_to_all | solution.py:532
  16.8 0.2 select_reduce_fusion.4
  17.2 0.1 fusion.64
  17.5 0.7 reduce_max.37
  18.2 0.1 reduce_sum.112
  18.3 0.6 reduce_max.36
  19.0 1.3 %pad_add_fusion.1 = s32[2]{0:T(128)S(1)} fusion(s32[1]{0:T(128)} %bitcast.10, s32[1]{0:T(128)} %bitcast.9), kind=kLoop, calls=%fused_computation.102 | loop fusion | flops 2 | bytes 16 | tf_op jit(solution)/shard_map/stack | solution.py:573
  20.2 1.5 %collective-permute-start.4 = (s32[2]{0:T(128)S(1)}, s32[2]{0:T(128)S(1)}, u32[]{:S(2)}, u32[]{:S(2)}) collective-permute-start(s32[2]{0:T(128)S(1)} %pad_add_fusion.1), channel_id=1, source_target_pairs={{0,16},{16,0},{1,17},{17,1},{2,18},{18,2},{3,19},{19,3},{4,20},{20... | collective-permute-start | bytes 32 | tf_op jit(solution)/shard_map/ppermute | solution.py:578
  21.8 2.1 %collective-permute-start.5 = (bf16[4,8,32,128]{3,2,1,0:T(8,128)(2,1)S(1)}, bf16[4,8,32,128]{3,2,1,0:T(8,128)(2,1)S(1)}, u32[]{:S(2)}, u32[]{:S(2)}) collective-permute-start(bf16[4,8,32,128]{3,2,1,0:T(8,128)(2,1)S(1)} %pad_maximum_fusion.1), channel_id=1, source_target_pairs={{0,2},{2,0},{4,6},{6,4},{8,10},{10,8},{12,14},{14,12},{1,3},{3,1},... | collective-permute-start | bytes 786440 | tf_op jit(solution)/shard_map/ppermute | solution.py:478
  23.9 0.3 copy.28
  24.1 1.3 %key_projection.2.refs_4_ = bf16[4,256,1024]{2,1,0:T(8,128)(2,1)S(1)} custom-call(bf16[32,32,128]{2,1,0:T(8,128)(2,1)S(1)} %bitcast.42, bf16[4,1024,256]{2,1,0:T(8,128)(2,1)S(1)} %bitcast.44), custom_call_target="tpu_custom_call" | custom-call | bytes 1024 | tf_op jit(solution)/shard_map/key_projection/pallas_call | solution.py:598
  25.5 0.1 select_reduce_fusion.3
  25.6 0.1 fusion.45
  25.7 0.3 select_reduce_fusion.2
  26.0 1.0 select_reduce_fusion
  27.1 1.3 %fusion.71 = s32[2]{0:T(128)S(1)} fusion(s32[2]{0:T(128)S(1)} %collective-permute-done.4, s32[1]{0:T(128)} %bitcast.10, s32[1]{0:T(128)} %bitcast.9), kind=kLoop, calls=%fused_computation.114 | loop fusion | flops 4 | bytes 24 | tf_op jit(solution)/shard_map/max | solution.py:577
  28.3 0.6 fusion.68
  29.7 7.8 %collective-permute-done.5 = bf16[4,8,32,128]{3,2,1,0:T(8,128)(2,1)S(1)} collective-permute-done((bf16[4,8,32,128]{3,2,1,0:T(8,128)(2,1)S(1)}, bf16[4,8,32,128]{3,2,1,0:T(8,128)(2,1)S(1)}, u32[]{:S(2)}, u32[]{:S(2)}) %collective-permute-start.5) | collective-permute-done | bytes 262176 | tf_op jit(solution)/shard_map/ppermute | solution.py:478
  37.5 3.1 %key_projection.3.refs_5_ = bf16[4,256,1024]{2,1,0:T(8,128)(2,1)S(1)} custom-call(bf16[32,32,128]{2,1,0:T(8,128)(2,1)S(1)} %bitcast.43, bf16[4,1024,256]{2,1,0:T(8,128)(2,1)} %bitcast.45), custom_call_target="tpu_custom_call" | custom-call | bytes 1024 | tf_op jit(solution)/shard_map/key_projection/pallas_call | solution.py:598
  40.6 1.3 %copy-done.2 = bf16[4,256,1024]{2,1,0:T(8,128)(2,1)} copy-done((bf16[4,256,1024]{2,1,0:T(8,128)(2,1)}, bf16[4,256,1024]{2,1,0:T(8,128)(2,1)S(1)}, u32[]{:S(2)}) %copy-start.2) | copy-done | bytes 2097176
  41.9 11.2 %all-to-all-done.7 = bf16[8,96,1024]{2,1,0:T(8,128)(2,1)} async-done(((bf16[8,96,1024]{2,1,0:T(8,128)(2,1)}), bf16[8,96,1024]{2,1,0:T(8,128)(2,1)}, u32[]{:S(2)}, u32[]{:S(2)}) %all-to-all-start.7) | async-done | bytes 1572896 | tf_op jit(solution)/shard_map/all_to_all | solution.py:532
  53.7 1.7 %conditional.2 = (bf16[256,1024]{1,0:T(8,128)(2,1)}, bf16[256,1024]{1,0:T(8,128)(2,1)}) conditional(s32[]{:T(128)} %bitcast.21, () %tuple.25, (s32[2]{0:T(128)S(1)}, s32[256]{0:T(256)S(1)}, s32[256]{0:T(256)S(1)}, bf16[256,8192]{1,0:T(8,128)(2,1)}) %tuple.56), branch_computations={%region_12.13_spmd, %region_13.14_spmd} | conditional | flops 134217728 | bytes 70254648 | solution.py:591
  53.7 0.9 broadcast.406.clone
  54.5 0.9 broadcast.406
  55.4 1.4 %collective-permute-done.6.refs_1_ = bf16[768,1024]{1,0:T(8,128)(2,1)} collective-permute-done((bf16[768,1024]{1,0:T(8,128)(2,1)}, bf16[768,1024]{1,0:T(8,128)(2,1)}, u32[]{:S(2)}, u32[]{:S(2)}) %collective-permute-start.6) | collective-permute-done | bytes 1572896 | tf_op jit(solution)/shard_map/ppermute | solution.py:618
  56.9 1.6 %copy-done.3 = bf16[4,256,1024]{2,1,0:T(8,128)(2,1)S(1)} copy-done((bf16[4,256,1024]{2,1,0:T(8,128)(2,1)S(1)}, bf16[4,256,1024]{2,1,0:T(8,128)(2,1)}, u32[]{:S(2)}) %copy-start.3) | copy-done | bytes 2097176
  58.5 7.4 %prompt_scores.1 = (bf16[8,32,384]{2,1,0:T(8,128)(2,1)}, bf16[8,32,256]{2,1,0:T(8,128)(2,1)}) custom-call(s32[651]{0:T(1024)S(1)} %concatenate.6.meta_ref, bf16[768,1024]{1,0:T(8,128)(2,1)} %bitcast.12.refs_0_, bf16[768,1024]{1,0:T(8,128)(2,1)} %collective-permute-done.6.refs_1_, bf16[256,1024]{1,0:T(8,128)(2,1)} %get-tuple-element.141.refs_2_, ...), custom_call_target="tpu_custom_call" | custom-call | tf_op jit(solution)/shard_map/prompt_scores/pallas_call | solution.py:637
  65.9 33.1 %conditional.3 = (bf16[2,4,64,128]{3,2,1,0:T(8,128)(2,1)S(1)}, bf16[2,4,64,128]{3,2,1,0:T(8,128)(2,1)S(1)}, bf16[2,4,64,128]{3,2,1,0:T(8,128)(2,1)S(1)}, bf16[2,...) conditional(s32[]{:T(128)} %bitcast.11, (bf16[8,32,384]{2,1,0:T(8,128)(2,1)}, s32[1,640]{1,0:T(1,128)S(1)}, ...), branch_computations={%region_14.17_spmd, %region_17.20_spmd} | conditional | flops 34047488 | bytes 99326216 | solution.py:756
  65.9 3.5 %all-to-all-start.1 = ((bf16[8,32,384]{2,1,0:T(8,128)(2,1)}), bf16[8,32,384]{2,1,0:T(8,128)(2,1)S(1)}, u32[]{:S(2)}, u32[]{:S(2)}) async-start(bf16[8,32,384]{2,1,0:T(8,128)(2,1)} %get-tuple-element.68), calls=%async_computation.1 | async-start | bytes 393216 | tf_op jit(solution)/shard_map/cond/branch_0_fun/all_to_all | solution.py:667
  69.5 3.0 %copy.25 = bf16[8,256,4,256]{3,1,2,0:T(8,128)(2,1)S(1)} copy(bf16[8,256,4,256]{3,2,1,0:T(4,128)(2,1)} %get-tuple-element.211) | data formatting | bytes 8388608 | tf_op jit(solution)/shard_map
  72.5 0.7 fusion.66
  73.3 1.3 %copy-done.9 = bf16[8,256,4,256]{3,1,2,0:T(8,128)(2,1)} copy-done((bf16[8,256,4,256]{3,1,2,0:T(8,128)(2,1)}, bf16[8,256,4,256]{3,1,2,0:T(8,128)(2,1)S(1)}, u32[]{:S(2)}) %copy-start.9) | copy-done | bytes 4194328 | tf_op jit(solution)/shard_map/cond
  74.5 0.1 broadcast_in_dim.162.refs_2_
  74.7 0.2 fusion.17
  74.9 0.1 broadcast_in_dim.163.refs_3_
  75.0 2.8 %all-to-all-done.1.refs_0_ = bf16[8,32,384]{2,1,0:T(8,128)(2,1)S(1)} async-done(((bf16[8,32,384]{2,1,0:T(8,128)(2,1)}), bf16[8,32,384]{2,1,0:T(8,128)(2,1)S(1)}, u32[]{:S(2)}, u32[]{:S(2)}) %all-to-all-start.1) | async-done | bytes 196640 | tf_op jit(solution)/shard_map/cond/branch_0_fun/all_to_all | solution.py:667
  77.8 1.1 softmax_weights.2
  78.9 3.6 %all-to-all-start.2 = ((bf16[8,32,384]{2,1,0:T(8,128)(2,1)}), bf16[8,32,384]{2,1,0:T(8,128)(2,1)S(1)}, u32[]{:S(2)}, u32[]{:S(2)}) async-start(bf16[8,32,384]{2,1,0:T(8,128)(2,1)} %get-tuple-element.73.refs_4_), calls=%async_computation.2 | async-start | bytes 393216 | tf_op jit(solution)/shard_map/cond/branch_0_fun/all_to_all | solution.py:714
  82.5 0.1 reduce
  82.6 5.1 %owner_lists.2.refs_2_ = bf16[8,384,1024]{2,1,0:T(8,128)(2,1)} custom-call(s32[651]{0:T(1024)S(1)} %get-tuple-element.67.meta_ref, bf16[768,1024]{1,0:T(8,128)(2,1)} %get-tuple-element.75.refs_0_, bf16[768,1024]{1,0:T(8,128)(2,1)} %get-tuple-element.76.refs_1_, bf16[256,1024]{1,0:T(8,128)(2,1)} %get-tuple-element.77.refs_2_, ...), custom_call_target="tpu_custom_call" | custom-call | bytes 16777216 | tf_op jit(solution)/shard_map/cond/branch_0_fun/owner_lists/pallas_call | solution.py:693
  87.8 0.4 fusion.13
  88.2 1.8 %all-to-all-done.2.refs_0_ = bf16[8,32,384]{2,1,0:T(8,128)(2,1)S(1)} async-done(((bf16[8,32,384]{2,1,0:T(8,128)(2,1)}), bf16[8,32,384]{2,1,0:T(8,128)(2,1)S(1)}, u32[]{:S(2)}, u32[]{:S(2)}) %all-to-all-start.2) | async-done | bytes 196640 | tf_op jit(solution)/shard_map/cond/branch_0_fun/all_to_all | solution.py:714
  90.0 2.8 %copy-done.1 = bf16[8,384,1024]{2,1,0:T(8,128)(2,1)S(1)} copy-done((bf16[8,384,1024]{2,1,0:T(8,128)(2,1)S(1)}, bf16[8,384,1024]{2,1,0:T(8,128)(2,1)}, u32[]{:S(2)}) %copy-start.1) | copy-done | bytes 6291480 | tf_op jit(solution)/shard_map/cond
  92.8 6.0 %weighted_values.2 = (bf16[2,4,64,128]{3,2,1,0:T(8,128)(2,1)S(1)}, bf16[2,4,64,128]{3,2,1,0:T(8,128)(2,1)S(1)}, bf16[2,4,64,128]{3,2,1,0:T(8,128)(2,1)S(1)}, bf16[2,4,64,128]{3,2,1,0:T(8,128)(2,1)S(1)}) custom-call(s32[651]{0:T(1024)S(1)} %get-tuple-element.67.meta_ref, bf16[8,32,384]{2,1,0:T(8,128)(2,1)S(1)} %all-to-all-done.2.refs_0_, ...), custom_call_target="tpu_custom_call" | custom-call | tf_op jit(solution)/shard_map/cond/branch_0_fun/weighted_values/pallas_call | solution.py:721
  99.1 1.0 collective-permute-start.7
  100.1 0.5 collective-permute-start.8
  100.6 2.1 %collective-permute-start.9 = (bf16[2,4,64,128]{3,2,1,0:T(8,128)(2,1)S(1)}, bf16[2,4,64,128]{3,2,1,0:T(8,128)(2,1)S(1)}, u32[]{:S(2)}, u32[]{:S(2)}) collective-permute-start(bf16[2,4,64,128]{3,2,1,0:T(8,128)(2,1)S(1)} %get-tuple-element.151), channel_id=1, source_target_pairs={{0,6},{2,4},{4,2},{6,0},{8,14},{10,12},{12,10},{14,8},{1,7},{3,5},... | collective-permute-start | bytes 393224 | tf_op jit(solution)/shard_map/ppermute | solution.py:478
  102.6 2.7 %collective-permute-done.7.refs_1_ = bf16[2,4,64,128]{3,2,1,0:T(8,128)(2,1)S(1)} collective-permute-done((bf16[2,4,64,128]{3,2,1,0:T(8,128)(2,1)S(1)}, bf16[2,4,64,128]{3,2,1,0:T(8,128)(2,1)S(1)}, u32[]{:S(2)}, u32[]{:S(2)}) %collective-permute-start.7) | collective-permute-done | bytes 131104 | tf_op jit(solution)/shard_map/ppermute | solution.py:478
  105.3 1.7 %collective-permute-done.9.refs_3_ = bf16[2,4,64,128]{3,2,1,0:T(8,128)(2,1)S(1)} collective-permute-done((bf16[2,4,64,128]{3,2,1,0:T(8,128)(2,1)S(1)}, bf16[2,4,64,128]{3,2,1,0:T(8,128)(2,1)S(1)}, u32[]{:S(2)}, u32[]{:S(2)}) %collective-permute-start.9) | collective-permute-done | bytes 131104 | tf_op jit(solution)/shard_map/ppermute | solution.py:478
  107.1 2.1 %collective-permute-start.10 = (bf16[2,4,64,128]{3,2,1,0:T(8,128)(2,1)S(1)}, bf16[2,4,64,128]{3,2,1,0:T(8,128)(2,1)S(1)}, u32[]{:S(2)}, u32[]{:S(2)}) collective-permute-start(bf16[2,4,64,128]{3,2,1,0:T(8,128)(2,1)S(1)} %get-tuple-element.154.after_ref), channel_id=1, source_target_pairs={{0,8},{2,10},{4,12},{6,14},{8,0},{10,2},{12,4},{14,6},{1,9},{3,11}... | collective-permute-start | bytes 393224 | tf_op jit(solution)/shard_map/ppermute | solution.py:478
  109.2 5.3 %collective-permute-done.10.got_ref = bf16[2,4,64,128]{3,2,1,0:T(8,128)(2,1)S(1)} collective-permute-done((bf16[2,4,64,128]{3,2,1,0:T(8,128)(2,1)S(1)}, bf16[2,4,64,128]{3,2,1,0:T(8,128)(2,1)S(1)}, u32[]{:S(2)}, u32[]{:S(2)}) %collective-permute-start.10) | collective-permute-done | bytes 131104 | tf_op jit(solution)/shard_map/ppermute | solution.py:478
  114.6 0.4 collective-permute-start.13
  115.0 2.1 %collective-permute-start.12 = (bf16[16,4096]{1,0:T(8,128)(2,1)S(1)}, bf16[16,4096]{1,0:T(8,128)(2,1)S(1)}, u32[]{:S(2)}, u32[]{:S(2)}) collective-permute-start(bf16[16,4096]{1,0:T(8,128)(2,1)S(1)} %attended_sum.1), channel_id=1, source_target_pairs={{0,4},{2,6},{4,0},{6,2},{8,12},{10,14},{12,8},{14,10},{1,5},{3,7},... | collective-permute-start | bytes 393224 | tf_op jit(solution)/shard_map/ppermute | solution.py:478
  117.0 1.1 collective-permute-start.11
  118.1 3.4 %copy-done.4 = bf16[4096,1024]{1,0:T(8,128)(2,1)S(1)} copy-done((bf16[4096,1024]{1,0:T(8,128)(2,1)S(1)}, bf16[4096,1024]{1,0:T(8,128)(2,1)}, u32[]{:S(2)}) %copy-start.4) | copy-done | bytes 8388632
  121.5 1.2 stage_out_weight.1
  122.7 0.8 fusion.47
  123.6 0.8 fusion.48.own_ref
  124.5 0.5 collective-permute-done.14.got_ref
  125.0 0.6 order_rows.1
  (55 shorter events, 1.0 us)
Async XLA Ops:
  0.0 10.7 %collective-permute-start.3 = (bf16[8,32,128]{2,1,0:T(8,128)(2,1)}, bf16[8,32,128]{2,1,0:T(8,128)(2,1)S(1)}, u32[]{:S(2)}, u32[]{:S(2)}) collective-permute-start(bf16[8,32,128]{2,1,0:T(8,128)(2,1)} %param.18), channel_id=1, source_target_pairs={{0,12},{2,14},{4,8},{6,10},{8,4},{10,6},{12,0},{14,2},{1,13},{3,15... | collective-permute-start | bytes 196616 | tf_op jit(solution)/shard_map/ppermute | solution.py:478
  5.0 5.6 %collective-permute-start.2 = (bf16[8,32,128]{2,1,0:T(8,128)(2,1)}, bf16[8,32,128]{2,1,0:T(8,128)(2,1)S(1)}, u32[]{:S(2)}, u32[]{:S(2)}) collective-permute-start(bf16[8,32,128]{2,1,0:T(8,128)(2,1)} %param.18), channel_id=1, source_target_pairs={{0,4},{2,6},{4,0},{6,2},{8,12},{10,14},{12,8},{14,10},{1,5},{3,7},... | collective-permute-start | bytes 196616 | tf_op jit(solution)/shard_map/ppermute | solution.py:478
  5.1 5.8 %collective-permute-start.1 = (bf16[8,32,128]{2,1,0:T(8,128)(2,1)}, bf16[8,32,128]{2,1,0:T(8,128)(2,1)S(1)}, u32[]{:S(2)}, u32[]{:S(2)}) collective-permute-start(bf16[8,32,128]{2,1,0:T(8,128)(2,1)} %param.18), channel_id=1, source_target_pairs={{0,8},{2,10},{4,12},{6,14},{8,0},{10,2},{12,4},{14,6},{1,9},{3,11}... | collective-permute-start | bytes 196616 | tf_op jit(solution)/shard_map/ppermute | solution.py:478
  5.7 11.1 %copy-start.13 = (s32[256,1]{0,1:T(1,128)S(1)}, s32[256,1]{0,1:T(1,128)}, u32[]{:S(2)}) copy-start(s32[256,1]{0,1:T(1,128)} %param.15) | copy-start | bytes 3076
  5.7 11.1 %copy-start.14 = (s32[256]{0:T(256)S(1)}, s32[256]{0:T(256)}, u32[]{:S(2)}) copy-start(s32[256]{0:T(256)} %fill_ref.1) | copy-start | bytes 3076
  5.7 16.0 %copy-start.12 = (bf16[8,32,128]{2,1,0:T(8,128)(2,1)S(1)}, bf16[8,32,128]{2,1,0:T(8,128)(2,1)}, u32[]{:S(2)}) copy-start(bf16[8,32,128]{2,1,0:T(8,128)(2,1)} %param.18) | copy-start | bytes 196612
  5.7 18.1 %copy-start.11 = (bf16[1024,4,256]{2,1,0:T(4,128)(2,1)S(1)}, bf16[1024,4,256]{2,1,0:T(4,128)(2,1)}, u32[]{:S(2)}) copy-start(bf16[1024,4,256]{2,1,0:T(4,128)(2,1)} %param.14) | copy-start | bytes 6291460
  10.9 42.2 %all-to-all-start.7 = ((bf16[8,96,1024]{2,1,0:T(8,128)(2,1)}), bf16[8,96,1024]{2,1,0:T(8,128)(2,1)}, u32[]{:S(2)}, u32[]{:S(2)}) async-start(bf16[8,96,1024]{2,1,0:T(8,128)(2,1)} %pack_live_tokens.3), calls=%async_computation.7 | async-start | bytes 3145728 | tf_op jit(solution)/shard_map/all_to_all | solution.py:532
  20.2 6.8 %collective-permute-start.4 = (s32[2]{0:T(128)S(1)}, s32[2]{0:T(128)S(1)}, u32[]{:S(2)}, u32[]{:S(2)}) collective-permute-start(s32[2]{0:T(128)S(1)} %pad_add_fusion.1), channel_id=1, source_target_pairs={{0,16},{16,0},{1,17},{17,1},{2,18},{18,2},{3,19},{19,3},{4,20},{20... | collective-permute-start | bytes 32 | tf_op jit(solution)/shard_map/ppermute | solution.py:578
  21.8 3.7 %copy-start.16 = (s32[256]{0:T(256)S(1)}, s32[256]{0:T(256)}, u32[]{:S(2)}) copy-start(s32[256]{0:T(256)} %param.16) | copy-start | bytes 3076
  21.8 15.7 %collective-permute-start.5 = (bf16[4,8,32,128]{3,2,1,0:T(8,128)(2,1)S(1)}, bf16[4,8,32,128]{3,2,1,0:T(8,128)(2,1)S(1)}, u32[]{:S(2)}, u32[]{:S(2)}) collective-permute-start(bf16[4,8,32,128]{3,2,1,0:T(8,128)(2,1)S(1)} %pad_maximum_fusion.1), channel_id=1, source_target_pairs={{0,2},{2,0},{4,6},{6,4},{8,10},{10,8},{12,14},{14,12},{1,3},{3,1},... | collective-permute-start | bytes 786440 | tf_op jit(solution)/shard_map/ppermute | solution.py:478
  24.1 1.3 %copy-start.5 = (bf16[1024,4,256]{2,0,1:T(8,128)(2,1)}, bf16[1024,4,256]{2,0,1:T(8,128)(2,1)S(1)}, u32[]{:S(2)}) copy-start(bf16[1024,4,256]{2,0,1:T(8,128)(2,1)S(1)} %copy.28) | copy-start | bytes 6291460
  40.6 1.3 %copy-start.2 = (bf16[4,256,1024]{2,1,0:T(8,128)(2,1)}, bf16[4,256,1024]{2,1,0:T(8,128)(2,1)S(1)}, u32[]{:S(2)}) copy-start(bf16[4,256,1024]{2,1,0:T(8,128)(2,1)S(1)} %key_projection.3.refs_5_) | copy-start | bytes 6291460
  53.1 3.8 %collective-permute-start.6 = (bf16[768,1024]{1,0:T(8,128)(2,1)}, bf16[768,1024]{1,0:T(8,128)(2,1)}, u32[]{:S(2)}, u32[]{:S(2)}) collective-permute-start(bf16[768,1024]{1,0:T(8,128)(2,1)} %bitcast.12.refs_0_), channel_id=1, source_target_pairs={{0,1},{1,0},{2,3},{3,2},{4,5},{5,4},{6,7},{7,6},{8,9},{9,8},{10,11... | collective-permute-start | bytes 4718600 | tf_op jit(solution)/shard_map/ppermute | solution.py:618
  56.9 1.6 %copy-start.3 = (bf16[4,256,1024]{2,1,0:T(8,128)(2,1)S(1)}, bf16[4,256,1024]{2,1,0:T(8,128)(2,1)}, u32[]{:S(2)}) copy-start(bf16[4,256,1024]{2,1,0:T(8,128)(2,1)} %copy-done.2) | copy-start | bytes 6291460
  58.5 7.4 %copy-start.15 = (s32[8]{0:T(128)S(1)}, s32[8]{0:T(128)}, u32[]{:S(2)}) copy-start(s32[8]{0:T(128)} %param.20) | copy-start | bytes 100
  65.9 11.9 %all-to-all-start.1 = ((bf16[8,32,384]{2,1,0:T(8,128)(2,1)}), bf16[8,32,384]{2,1,0:T(8,128)(2,1)S(1)}, u32[]{:S(2)}, u32[]{:S(2)}) async-start(bf16[8,32,384]{2,1,0:T(8,128)(2,1)} %get-tuple-element.68), calls=%async_computation.1 | async-start | bytes 393216 | tf_op jit(solution)/shard_map/cond/branch_0_fun/all_to_all | solution.py:667
  72.5 2.0 %copy-start.9 = (bf16[8,256,4,256]{3,1,2,0:T(8,128)(2,1)}, bf16[8,256,4,256]{3,1,2,0:T(8,128)(2,1)S(1)}, u32[]{:S(2)}) copy-start(bf16[8,256,4,256]{3,1,2,0:T(8,128)(2,1)S(1)} %copy.25) | copy-start | bytes 12582916 | tf_op jit(solution)/shard_map/cond
  78.9 11.1 %all-to-all-start.2 = ((bf16[8,32,384]{2,1,0:T(8,128)(2,1)}), bf16[8,32,384]{2,1,0:T(8,128)(2,1)S(1)}, u32[]{:S(2)}, u32[]{:S(2)}) async-start(bf16[8,32,384]{2,1,0:T(8,128)(2,1)} %get-tuple-element.73.refs_4_), calls=%async_computation.2 | async-start | bytes 393216 | tf_op jit(solution)/shard_map/cond/branch_0_fun/all_to_all | solution.py:714
  82.6 5.2 %copy-start.10 = (bf16[8,256,4,256]{3,1,2,0:T(8,128)(2,1)S(1)}, bf16[8,256,4,256]{3,1,2,0:T(8,128)(2,1)}, u32[]{:S(2)}) copy-start(bf16[8,256,4,256]{3,1,2,0:T(8,128)(2,1)} %copy-done.9) | copy-start | bytes 12582916 | tf_op jit(solution)/shard_map/cond
  82.6 7.4 %copy-start.6 = (bf16[4,1024,256]{2,1,0:T(8,128)(2,1)S(1)}, bf16[4,1024,256]{2,1,0:T(8,128)(2,1)}, u32[]{:S(2)}) copy-start(bf16[4,1024,256]{2,1,0:T(8,128)(2,1)} %get-tuple-element.79.refs_3_) | copy-start | bytes 6291460 | tf_op jit(solution)/shard_map/cond
  90.0 2.8 %copy-start.1 = (bf16[8,384,1024]{2,1,0:T(8,128)(2,1)S(1)}, bf16[8,384,1024]{2,1,0:T(8,128)(2,1)}, u32[]{:S(2)}) copy-start(bf16[8,384,1024]{2,1,0:T(8,128)(2,1)} %owner_lists.2.refs_2_) | copy-start | bytes 18874372 | tf_op jit(solution)/shard_map/cond
  99.1 6.2 %collective-permute-start.7 = (bf16[2,4,64,128]{3,2,1,0:T(8,128)(2,1)S(1)}, bf16[2,4,64,128]{3,2,1,0:T(8,128)(2,1)S(1)}, u32[]{:S(2)}, u32[]{:S(2)}) collective-permute-start(bf16[2,4,64,128]{3,2,1,0:T(8,128)(2,1)S(1)} %get-tuple-element.149), channel_id=1, source_target_pairs={{0,2},{2,0},{4,6},{6,4},{8,10},{10,8},{12,14},{14,12},{1,3},{3,1},... | collective-permute-start | bytes 393224 | tf_op jit(solution)/shard_map/ppermute | solution.py:478
  100.1 5.2 %collective-permute-start.8 = (bf16[2,4,64,128]{3,2,1,0:T(8,128)(2,1)S(1)}, bf16[2,4,64,128]{3,2,1,0:T(8,128)(2,1)S(1)}, u32[]{:S(2)}, u32[]{:S(2)}) collective-permute-start(bf16[2,4,64,128]{3,2,1,0:T(8,128)(2,1)S(1)} %get-tuple-element.150), channel_id=1, source_target_pairs={{0,4},{2,6},{4,0},{6,2},{8,12},{10,14},{12,8},{14,10},{1,5},{3,7},... | collective-permute-start | bytes 393224 | tf_op jit(solution)/shard_map/ppermute | solution.py:478
  100.6 6.4 %collective-permute-start.9 = (bf16[2,4,64,128]{3,2,1,0:T(8,128)(2,1)S(1)}, bf16[2,4,64,128]{3,2,1,0:T(8,128)(2,1)S(1)}, u32[]{:S(2)}, u32[]{:S(2)}) collective-permute-start(bf16[2,4,64,128]{3,2,1,0:T(8,128)(2,1)S(1)} %get-tuple-element.151), channel_id=1, source_target_pairs={{0,6},{2,4},{4,2},{6,0},{8,14},{10,12},{12,10},{14,8},{1,7},{3,5},... | collective-permute-start | bytes 393224 | tf_op jit(solution)/shard_map/ppermute | solution.py:478
  107.1 7.4 %collective-permute-start.10 = (bf16[2,4,64,128]{3,2,1,0:T(8,128)(2,1)S(1)}, bf16[2,4,64,128]{3,2,1,0:T(8,128)(2,1)S(1)}, u32[]{:S(2)}, u32[]{:S(2)}) collective-permute-start(bf16[2,4,64,128]{3,2,1,0:T(8,128)(2,1)S(1)} %get-tuple-element.154.after_ref), channel_id=1, source_target_pairs={{0,8},{2,10},{4,12},{6,14},{8,0},{10,2},{12,4},{14,6},{1,9},{3,11}... | collective-permute-start | bytes 393224 | tf_op jit(solution)/shard_map/ppermute | solution.py:478
  114.6 8.1 %collective-permute-start.13 = (bf16[16,4096]{1,0:T(8,128)(2,1)S(1)}, bf16[16,4096]{1,0:T(8,128)(2,1)S(1)}, u32[]{:S(2)}, u32[]{:S(2)}) collective-permute-start(bf16[16,4096]{1,0:T(8,128)(2,1)S(1)} %attended_sum.1), channel_id=1, source_target_pairs={{0,6},{2,4},{4,2},{6,0},{8,14},{10,12},{12,10},{14,8},{1,7},{3,5},... | collective-permute-start | bytes 393224 | tf_op jit(solution)/shard_map/ppermute | solution.py:478
  115.0 7.7 %collective-permute-start.12 = (bf16[16,4096]{1,0:T(8,128)(2,1)S(1)}, bf16[16,4096]{1,0:T(8,128)(2,1)S(1)}, u32[]{:S(2)}, u32[]{:S(2)}) collective-permute-start(bf16[16,4096]{1,0:T(8,128)(2,1)S(1)} %attended_sum.1), channel_id=1, source_target_pairs={{0,4},{2,6},{4,0},{6,2},{8,12},{10,14},{12,8},{14,10},{1,5},{3,7},... | collective-permute-start | bytes 393224 | tf_op jit(solution)/shard_map/ppermute | solution.py:478
  117.0 5.7 %collective-permute-start.11 = (bf16[16,4096]{1,0:T(8,128)(2,1)S(1)}, bf16[16,4096]{1,0:T(8,128)(2,1)S(1)}, u32[]{:S(2)}, u32[]{:S(2)}) collective-permute-start(bf16[16,4096]{1,0:T(8,128)(2,1)S(1)} %attended_sum.1), channel_id=1, source_target_pairs={{0,2},{2,0},{4,6},{6,4},{8,10},{10,8},{12,14},{14,12},{1,3},{3,1},... | collective-permute-start | bytes 393224 | tf_op jit(solution)/shard_map/ppermute | solution.py:478
  118.1 3.4 %copy-start.4 = (bf16[4096,1024]{1,0:T(8,128)(2,1)S(1)}, bf16[4096,1024]{1,0:T(8,128)(2,1)}, u32[]{:S(2)}) copy-start(bf16[4096,1024]{1,0:T(8,128)(2,1)} %weight_ref.1) | copy-start | bytes 25165828
  123.6 1.4 %collective-permute-start.14 = (f32[64,512]{1,0:T(8,128)S(1)}, f32[64,512]{1,0:T(8,128)S(1)}, u32[]{:S(2)}, u32[]{:S(2)}) collective-permute-start(f32[64,512]{1,0:T(8,128)S(1)} %fusion.47), channel_id=1, source_target_pairs={{0,1},{1,0},{2,3},{3,2},{4,5},{5,4},{6,7},{7,6},{8,9},{9,8},{10,11... | collective-permute-start | bytes 393224 | tf_op jit(solution)/shard_map/ppermute | solution.py:803

commit v19 on v18

--- a/solution.py
+++ b/solution.py
@@ -170,16 +170,19 @@
 
 
 def score_kernel(n, rows, meta_ref, *refs):
-    x_refs, keyed_refs, (row_ref, near_ref, rest_ref) = refs[:4], refs[4:6], refs[6:9]
-    held, more, wide, tile, keyed, sem, keyed_sem = refs[9:]
+    x_refs, keyed_refs, row_ref, out_refs = refs[:4], refs[4:6], refs[6], refs[7 : 7 + n]
+    held, more, wide, tile, keyed, sem, keyed_sem = refs[7 + n :]
+    half = n // 2
     step = pl.program_id(0)
     part = wide.shape[1]
-    near = near_ref.shape[2]
-    lanes = near + rest_ref.shape[2]
+    near = out_refs[0].shape[2]
+    lanes = near + out_refs[half].shape[2]
     cuts = tile_cuts(lanes)
     groups = lanes // BLK
     at_size = n * groups
-    q = meta_ref[at_size + n] ^ reversed_bits(step, n)
+    me = meta_ref[at_size + n]
+    apart = reversed_bits(step, n)
+    q = me ^ apart
     kvh, per = keyed.shape[0], keyed.shape[1] // n
     group = per // rows
 
@@ -219,29 +222,43 @@
         picked = jnp.zeros((kvh, group, count * BLK), jnp.float32)
         for r in range(rows):
             picked = picked + jnp.where((owner_row == r)[None], raw[:, r], 0.0)
-        picked = picked.reshape(kvh * group, -1).astype(near_ref.dtype)
-        if cuts[t] < near:
-            near_ref[0, :, here] = picked
-        else:
-            rest_ref[0, :, cuts[t] - near : cuts[t + 1] - near] = picked
+        picked = picked.reshape(kvh * group, -1).astype(out_refs[0].dtype)
+        piece = 0 if cuts[t] < near else 1
+        for k in range(half):
+
+            @pl.when(apart % half == k)
+            def _(k=k):
+                out_refs[piece * half + k][
+                    q // half, :, cuts[t] - piece * near : cuts[t + 1] - piece * near
+                ] = picked
 
     one(0)
     for t in range(1, len(cuts) - 1):
         pl.when(meta_ref[at_size + q] > cuts[t])(functools.partial(one, t))
 
 
+def half_score_kernel(side_ref, *refs):
+    *part_refs, mine_ref, send_ref = refs
+    sums = []
+    for side in (side_ref[0], 1 - side_ref[0]):
+        got = part_refs[0][side].astype(jnp.float32)
+        for ref in part_refs[1:]:
+            got = got + ref[side].astype(jnp.float32)
+        sums.append(got)
+    mine_ref[...] = sums[0]
+    send_ref[...] = sums[1].astype(send_ref.dtype)
+
+
 def weight_kernel(scale, count, *refs):
-    part_refs, row_refs = refs[:count], refs[count : 2 * count]
-    top_ref, sum_ref = refs[2 * count : 2 * count + 2]
-    w_refs, share_ref = refs[2 * count + 2 : -1], refs[-1]
-    n = part_refs[0].shape[0]
-    scores, owner_rows = [], []
-    for part_ref, row_ref in zip(part_refs, row_refs):
-        got = part_ref[0].astype(jnp.float32)
-        for i in range(1, n):
-            got = got + part_ref[i].astype(jnp.float32)
-        scores.append(got * scale)
-        owner_rows.append(row_ref[...])
+    mine_refs, got_refs, row_refs = refs[:count], refs[count : 2 * count], refs[2 * count : 3 * count]
+    top_ref, sum_ref = refs[3 * count : 3 * count + 2]
+    w_refs, share_ref = refs[3 * count + 2 : -1], refs[-1]
+    n = w_refs[0].shape[0]
+    scores = [
+        (mine[...] + got[...].astype(jnp.float32)) * scale
+        for mine, got in zip(mine_refs, got_refs)
+    ]
+    owner_rows = [ref[...] for ref in row_refs]
     rows = range(top_ref.shape[0])
     spread = [jnp.zeros(s.shape, jnp.float32) for s in scores]
     tops = []
@@ -524,8 +541,8 @@
     packed = pack(x_prompt, pack_fill, pack_dest, at, n, 0, size)
     dest = pack_dest
     far = [with_partner(queries, k, n) for k in (n // 2, n // 4, n // 2 + n // 4)]
-    packed, far, dest, block_row, block_fill, kv_weight = lax.optimization_barrier(
-        (packed, far, dest, block_row, block_fill, kv_weight)
+    packed, far[0], dest, block_row, block_fill, kv_weight = lax.optimization_barrier(
+        (packed, far[0], dest, block_row, block_fill, kv_weight)
     )
     kv_weight = kv_weight.transpose(1, 0, 2)
     even = from_rest(jnp.stack([queries, *far]), n)
@@ -634,7 +651,9 @@
     def owner(i, m):
         return m[at_me] ^ reversed_bits(i, n)
 
-    score_near, score_rest = pl.pallas_call(
+    half = n // 2
+    lengths = (near, lanes - near)
+    score_parts = pl.pallas_call(
         functools.partial(score_kernel, n, rows),
         grid_spec=pltpu.PrefetchScalarGridSpec(
             num_scalar_prefetch=1,
@@ -644,8 +663,9 @@
                 pl.BlockSpec((1, 1, lanes), lambda i, m: (owner(i, m), 0, 0)),
             ],
             out_specs=[
-                pl.BlockSpec((1, heads, length), lambda i, m: (owner(i, m), 0, 0))
-                for length in (near, lanes - near)
+                pl.BlockSpec((2, heads, length), lambda i, m: (0, 0, 0))
+                for length in lengths
+                for _ in range(half)
             ],
             scratch_shapes=[
                 *x_scratch,
@@ -655,7 +675,11 @@
                 pltpu.SemaphoreType.DMA((2, kvh)),
             ],
         ),
-        out_shape=slot_shapes,
+        out_shape=[
+            jax.ShapeDtypeStruct((2, heads, length), jnp.bfloat16)
+            for length in lengths
+            for _ in range(half)
+        ],
         compiler_params=pltpu.CompilerParams(vmem_limit_bytes=24 * MIB),
         name="prompt_scores",
     )(meta, *x_parts, keyed_even, keyed_odd, rowof)
@@ -664,7 +688,21 @@
 
     def exchange_weights(*scores):
         count = len(scores)
-        parts = [lax.all_to_all(s, "pool", 0, 0, tiled=True) for s in scores]
+        mine_sums, got_sums = [], []
+        for parts, length in zip(scores, lengths):
+            parts = [parts[0]] + [with_partner(parts[k], k, n) for k in range(1, half)]
+            mine_sum, send_sum = pl.pallas_call(
+                half_score_kernel,
+                in_specs=[pl.BlockSpec(memory_space=pltpu.SMEM), *[in_vmem] * half],
+                out_shape=[
+                    jax.ShapeDtypeStruct((heads, length), jnp.float32),
+                    jax.ShapeDtypeStruct((heads, length), jnp.bfloat16),
+                ],
+                compiler_params=pltpu.CompilerParams(vmem_limit_bytes=4 * MIB),
+                name="half_pool_scores",
+            )((me // half).reshape(1), *parts)
+            mine_sums.append(mine_sum)
+            got_sums.append(with_partner(send_sum, half, n))
         query = queries.reshape(rows, kvh, group, hd)
         cache_scores = (
             jnp.einsum(
@@ -684,7 +722,8 @@
             compiler_params=pltpu.CompilerParams(vmem_limit_bytes=8 * MIB),
             name="softmax_weights",
         )(
-            *parts,
+            *mine_sums,
+            *got_sums,
             *row_parts,
             cache_top.reshape(rows, heads, 1),
             cache_sum.reshape(rows, heads, 1),
@@ -755,8 +794,8 @@
 
     *terms, kept = lax.cond(
         longer,
-        lambda: exchange_weights(score_near, score_rest),
-        lambda: exchange_weights(score_near),
+        lambda: exchange_weights(score_parts[:half], score_parts[half:]),
+        lambda: exchange_weights(score_parts[:half]),
     )
 
     term_parts = [terms[0]] + [with_partner(terms[k], k, n) for k in range(1, n // 2)]

time: 126 us -> 126 us (level)
  waiting for transfers between devices: 35.4 us -> 37.3 us
  local copies, waits for them, and re-layouts: 16.6 us -> 15.2 us
    ppermute x11 -> x15, waiting for transfers between devices: 17.6 us -> 22.2 us  [with_partner(): return lax.ppermute(x, 'pool', [(i, i ^ k) for i in range(n)])]
    all_to_all x1 -> x0, starting transfers between devices: 3.53 us -> none  [exchange_weights(): parts = [lax.all_to_all(s, 'pool', 0, 0, tiled=True) for s in scores]]
    ppermute x11 -> x15, starting transfers between devices: 16.9 us -> 20 us  [with_partner(): return lax.ppermute(x, 'pool', [(i, i ^ k) for i in range(n)])]
    all_to_all x1 -> x0, waiting for transfers between devices: 2.82 us -> none  [exchange_weights(): parts = [lax.all_to_all(s, 'pool', 0, 0, tiled=True) for s in scores]]
    another operation x3, local copies, waits for them, and re-layouts: 4.7 us -> 2.48 us
    unnamed x20 -> x22, local copies, waits for them, and re-layouts: 6.32 us -> 6.33 us
  transfers between devices with their start and end apart: 17 -> 20, of which waited for: 10 -> 11; matrix products, arithmetic and copies ran while one was open for 12% -> 10% of each run, Pallas kernels for 12% -> 12%
where the time goes in v19:
time: 126 us
  waiting for transfers between devices  37.3 us (30%)
  starting transfers between devices  31 us (25%)
  Pallas kernels  30.9 us (25%)
  local copies, waits for them, and re-layouts  15.2 us (12%)
  other arithmetic  6.65 us (5%)
  matrix products  2.82 us (2%)
  between operations  1.6 us (1%)
    ppermute x15, waiting for transfers between devices, with_partner(): return lax.ppermute(x, 'pool', [(i, i ^ k) for i in range(n)])  22.2 us
    ppermute x15, starting transfers between devices, with_partner(): return lax.ppermute(x, 'pool', [(i, i ^ k) for i in range(n)])  20 us
    all_to_all x1, waiting for transfers between devices, local(): lax.all_to_all(packed, 'pool', 0, 0, tiled=True).reshape(n * size, part)  11.2 us
    pallas_call x1, Pallas kernels, local(): pl.pallas_call(functools.partial(score_kernel, n, rows), grid_spec=pltpu....  7.41 us
    unnamed x22, local copies, waits for them, and re-layouts  6.33 us
    pallas_call x1, Pallas kernels, exchange_weights(): pl.pallas_call(functools.partial(value_kernel, n, rows, lanes, count), gr...  6 us
    all_to_all x1, starting transfers between devices, local(): lax.all_to_all(packed, 'pool', 0, 0, tiled=True).reshape(n * size, part)  5.84 us
    pallas_call x1, Pallas kernels, exchange_weights(): pl.pallas_call(functools.partial(list_kernel, n, lanes), grid_spec=pltpu....  5.13 us
  transfers between devices with their start and end apart: 20, of which 11 were waited for; matrix products, arithmetic and copies ran while one was open for 10% of the time, Pallas kernels for 12%

profile of v19, /device:TPU:0, one launch (start us, length us, event | category | flops | bytes accessed | tf_op | source)
XLA Modules:
  0.0 125.9 jit_solution(18191289929208460929)
XLA Ops:
  0.0 5.0 %collective-permute-start.16 = (bf16[8,32,128]{2,1,0:T(8,128)(2,1)}, bf16[8,32,128]{2,1,0:T(8,128)(2,1)S(1)}, u32[]{:S(2)}, u32[]{:S(2)}) collective-permute-start(bf16[8,32,128]{2,1,0:T(8,128)(2,1)} %param.18), channel_id=1, source_target_pairs={{0,12},{2,14},{4,8},{6,10},{8,4},{10,6},{12,0},{14,2},{1,13},{3,15... | collective-permute-start | bytes 196616 | tf_op jit(solution)/shard_map/ppermute | solution.py:495
  5.1 0.6 collective-permute-start.13
  5.7 4.9 %pack_live_tokens.3 = bf16[8,96,1024]{2,1,0:T(8,128)(2,1)} custom-call(s32[2]{0:T(128)S(1)} %pad_add_fusion.at_ref, s32[256]{0:T(256)} %fill_ref.1, s32[256]{0:T(256)} %bitcast.54, bf16[256,8192]{1,0:T(8,128)(2,1)} %x_ref.1), custom_call_target="tpu_custom_call" | custom-call | flops 402653184 | bytes 67108864 | tf_op jit(solution)/shard_map/pack_live_tokens/pallas_call | solution.py:62
  10.7 0.2 collective-permute-done.13
  10.9 5.8 %all-to-all-start.4 = ((bf16[8,96,1024]{2,1,0:T(8,128)(2,1)}), bf16[8,96,1024]{2,1,0:T(8,128)(2,1)}, u32[]{:S(2)}, u32[]{:S(2)}) async-start(bf16[8,96,1024]{2,1,0:T(8,128)(2,1)} %pack_live_tokens.3), calls=%async_computation.4 | async-start | bytes 3145728 | tf_op jit(solution)/shard_map/all_to_all | solution.py:549
  16.8 0.2 select_reduce_fusion.4
  17.2 0.1 fusion.58
  17.5 0.6 reduce_max.37
  18.1 0.1 reduce_sum.112
  18.3 0.7 reduce_max.36
  19.0 1.3 %pad_add_fusion.1 = s32[2]{0:T(128)S(1)} fusion(s32[1]{0:T(128)} %bitcast.12, s32[1]{0:T(128)} %bitcast.11), kind=kLoop, calls=%fused_computation.102 | loop fusion | flops 2 | bytes 16 | tf_op jit(solution)/shard_map/stack | solution.py:590
  20.3 1.5 %collective-permute-start.14 = (s32[2]{0:T(128)S(1)}, s32[2]{0:T(128)S(1)}, u32[]{:S(2)}, u32[]{:S(2)}) collective-permute-start(s32[2]{0:T(128)S(1)} %pad_add_fusion.1), channel_id=1, source_target_pairs={{0,16},{16,0},{1,17},{17,1},{2,18},{18,2},{3,19},{19,3},{4,20},{20... | collective-permute-start | bytes 32 | tf_op jit(solution)/shard_map/ppermute | solution.py:595
  21.9 2.1 %collective-permute-start.17 = (bf16[4,8,32,128]{3,2,1,0:T(8,128)(2,1)S(1)}, bf16[4,8,32,128]{3,2,1,0:T(8,128)(2,1)S(1)}, u32[]{:S(2)}, u32[]{:S(2)}) collective-permute-start(bf16[4,8,32,128]{3,2,1,0:T(8,128)(2,1)S(1)} %pad_maximum_fusion.1), channel_id=1, source_target_pairs={{0,2},{2,0},{4,6},{6,4},{8,10},{10,8},{12,14},{14,12},{1,3},{3,1},... | collective-permute-start | bytes 786440 | tf_op jit(solution)/shard_map/ppermute | solution.py:495
  23.9 0.3 copy.28
  24.2 1.3 %key_projection.2.refs_4_ = bf16[4,256,1024]{2,1,0:T(8,128)(2,1)S(1)} custom-call(bf16[32,32,128]{2,1,0:T(8,128)(2,1)S(1)} %bitcast.40, bf16[4,1024,256]{2,1,0:T(8,128)(2,1)S(1)} %bitcast.42), custom_call_target="tpu_custom_call" | custom-call | bytes 1024 | tf_op jit(solution)/shard_map/key_projection/pallas_call | solution.py:615
  25.7 0.1 fusion.39
  25.8 0.3 select_reduce_fusion.2
  26.1 1.0 select_reduce_fusion
  27.2 1.3 %fusion.65 = s32[2]{0:T(128)S(1)} fusion(s32[2]{0:T(128)S(1)} %collective-permute-done.14, s32[1]{0:T(128)} %bitcast.12, s32[1]{0:T(128)} %bitcast.11), kind=kLoop, calls=%fused_computation.114 | loop fusion | flops 4 | bytes 24 | tf_op jit(solution)/shard_map/max | solution.py:594
  28.5 0.7 fusion.62
  29.9 7.5 %collective-permute-done.17 = bf16[4,8,32,128]{3,2,1,0:T(8,128)(2,1)S(1)} collective-permute-done((bf16[4,8,32,128]{3,2,1,0:T(8,128)(2,1)S(1)}, bf16[4,8,32,128]{3,2,1,0:T(8,128)(2,1)S(1)}, u32[]{:S(2)}, u32[]{:S(2)}) %collective-permute-start.17) | collective-permute-done | bytes 262176 | tf_op jit(solution)/shard_map/ppermute | solution.py:495
  37.4 3.1 %key_projection.3.refs_5_ = bf16[4,256,1024]{2,1,0:T(8,128)(2,1)S(1)} custom-call(bf16[32,32,128]{2,1,0:T(8,128)(2,1)S(1)} %bitcast.41, bf16[4,1024,256]{2,1,0:T(8,128)(2,1)} %bitcast.43), custom_call_target="tpu_custom_call" | custom-call | bytes 1024 | tf_op jit(solution)/shard_map/key_projection/pallas_call | solution.py:615
  40.5 1.3 %copy-done.2 = bf16[4,256,1024]{2,1,0:T(8,128)(2,1)} copy-done((bf16[4,256,1024]{2,1,0:T(8,128)(2,1)}, bf16[4,256,1024]{2,1,0:T(8,128)(2,1)S(1)}, u32[]{:S(2)}) %copy-start.2) | copy-done | bytes 2097176
  41.8 11.2 %all-to-all-done.4 = bf16[8,96,1024]{2,1,0:T(8,128)(2,1)} async-done(((bf16[8,96,1024]{2,1,0:T(8,128)(2,1)}), bf16[8,96,1024]{2,1,0:T(8,128)(2,1)}, u32[]{:S(2)}, u32[]{:S(2)}) %all-to-all-start.4) | async-done | bytes 1572896 | tf_op jit(solution)/shard_map/all_to_all | solution.py:549
  53.8 1.7 %conditional.2 = (bf16[256,1024]{1,0:T(8,128)(2,1)}, bf16[256,1024]{1,0:T(8,128)(2,1)}) conditional(s32[]{:T(128)} %bitcast.23, () %tuple.25, (s32[2]{0:T(128)S(1)}, s32[256]{0:T(256)S(1)}, s32[256]{0:T(256)S(1)}, bf16[256,8192]{1,0:T(8,128)(2,1)}) %tuple.58), branch_computations={%region_12.13_spmd, %region_13.14_spmd} | conditional | flops 134217728 | bytes 70254648 | solution.py:608
  53.8 0.9 broadcast.408.clone
  54.6 0.8 broadcast.408
  55.5 1.4 %collective-permute-done.18.refs_1_ = bf16[768,1024]{1,0:T(8,128)(2,1)} collective-permute-done((bf16[768,1024]{1,0:T(8,128)(2,1)}, bf16[768,1024]{1,0:T(8,128)(2,1)}, u32[]{:S(2)}, u32[]{:S(2)}) %collective-permute-start.18) | collective-permute-done | bytes 1572896 | tf_op jit(solution)/shard_map/ppermute | solution.py:635
  56.8 1.6 %copy-done.3 = bf16[4,256,1024]{2,1,0:T(8,128)(2,1)S(1)} copy-done((bf16[4,256,1024]{2,1,0:T(8,128)(2,1)S(1)}, bf16[4,256,1024]{2,1,0:T(8,128)(2,1)}, u32[]{:S(2)}) %copy-start.3) | copy-done | bytes 2097176
  58.4 7.4 %prompt_scores.1 = (bf16[2,32,384]{2,1,0:T(8,128)(2,1)S(1)}, bf16[2,32,384]{2,1,0:T(8,128)(2,1)}, bf16[2,32,384]{2,1,0:T(8,128)(2,1)}, bf16[2,32,384]{2,1,0:T(8,...) custom-call(s32[651]{0:T(1024)S(1)} %concatenate.6.meta_ref, ...), custom_call_target="tpu_custom_call" | custom-call | tf_op jit(solution)/shard_map/prompt_scores/pallas_call | solution.py:656
  65.9 33.5 %conditional.3 = (bf16[2,4,64,128]{3,2,1,0:T(8,128)(2,1)S(1)}, bf16[2,4,64,128]{3,2,1,0:T(8,128)(2,1)S(1)}, bf16[2,4,64,128]{3,2,1,0:T(8,128)(2,1)S(1)}, bf16[2,...) conditional(s32[]{:T(128)} %bitcast.13, (s32[]{:T(128)}, bf16[2,32,384]{2,1,0:T(8,128)(2,1)}, ...), branch_computations={%region_14.17_spmd, %region_17.20_spmd} | conditional | flops 34047504 | bytes 116267696 | solution.py:795
  66.0 2.8 %collective-permute-start.2 = (bf16[2,32,384]{2,1,0:T(8,128)(2,1)}, bf16[2,32,384]{2,1,0:T(8,128)(2,1)S(1)}, u32[]{:S(2)}, u32[]{:S(2)}) collective-permute-start(bf16[2,32,384]{2,1,0:T(8,128)(2,1)} %get-tuple-element.93), channel_id=1, source_target_pairs={{0,4},{2,6},{4,0},{6,2},{8,12},{10,14},{12,8},{14,10},{1,5},{3,7},... | collective-permute-start | bytes 147464 | tf_op jit(solution)/shard_map/cond/branch_0_fun/ppermute | solution.py:495
  68.8 0.7 collective-permute-start.1
  69.5 0.8 copy.25
  70.3 2.1 %copy-done.11 = bf16[8,256,4,256]{3,1,2,0:T(8,128)(2,1)} copy-done((bf16[8,256,4,256]{3,1,2,0:T(8,128)(2,1)}, bf16[8,256,4,256]{3,1,2,0:T(8,128)(2,1)S(1)}, u32[]{:S(2)}) %copy-start.11) | copy-done | bytes 4194328 | tf_op jit(solution)/shard_map/cond
  72.4 0.7 fusion.60
  73.2 0.2 fusion.14
  73.5 0.1 broadcast_in_dim.162.refs_3_
  73.6 0.1 broadcast_in_dim.163.refs_4_
  73.7 4.3 %collective-permute-done.4.refs_1_ = bf16[32,384]{1,0:T(8,128)(2,1)S(1)} collective-permute-done((bf16[32,384]{1,0:T(8,128)(2,1)S(1)}, bf16[32,384]{1,0:T(8,128)(2,1)S(1)}, u32[]{:S(2)}, u32[]{:S(2)}) %collective-permute-start.4) | collective-permute-done | bytes 24608 | tf_op jit(solution)/shard_map/cond/branch_0_fun/ppermute | solution.py:495
  78.0 1.1 softmax_weights.2
  79.0 3.6 %all-to-all-start.1 = ((bf16[8,32,384]{2,1,0:T(8,128)(2,1)}), bf16[8,32,384]{2,1,0:T(8,128)(2,1)S(1)}, u32[]{:S(2)}, u32[]{:S(2)}) async-start(bf16[8,32,384]{2,1,0:T(8,128)(2,1)} %get-tuple-element.101.refs_4_), calls=%async_computation.1 | async-start | bytes 393216 | tf_op jit(solution)/shard_map/cond/branch_0_fun/all_to_all | solution.py:753
  82.6 0.1 reduce
  82.8 5.1 %owner_lists.2.refs_2_ = bf16[8,384,1024]{2,1,0:T(8,128)(2,1)} custom-call(s32[651]{0:T(1024)S(1)} %get-tuple-element.89.meta_ref, bf16[768,1024]{1,0:T(8,128)(2,1)} %get-tuple-element.103.refs_0_, bf16[768,1024]{1,0:T(8,128)(2,1)} %get-tuple-element.104.refs_1_, bf16[256,1024]{1,0:T(8,128)(2,1)} %get-tuple-element.105.refs_2_, ...), custom_call_target="tpu_custom_call" | custom-call | bytes 16777216 | tf_op jit(solution)/shard_map/cond/branch_0_fun/owner_lists/pallas_call | solution.py:732
  87.9 0.4 broadcast_multiply_fusion
  88.3 2.0 %all-to-all-done.1.refs_0_ = bf16[8,32,384]{2,1,0:T(8,128)(2,1)S(1)} async-done(((bf16[8,32,384]{2,1,0:T(8,128)(2,1)}), bf16[8,32,384]{2,1,0:T(8,128)(2,1)S(1)}, u32[]{:S(2)}, u32[]{:S(2)}) %all-to-all-start.1) | async-done | bytes 196640 | tf_op jit(solution)/shard_map/cond/branch_0_fun/all_to_all | solution.py:753
  90.4 2.8 %copy-done.1 = bf16[8,384,1024]{2,1,0:T(8,128)(2,1)S(1)} copy-done((bf16[8,384,1024]{2,1,0:T(8,128)(2,1)S(1)}, bf16[8,384,1024]{2,1,0:T(8,128)(2,1)}, u32[]{:S(2)}) %copy-start.1) | copy-done | bytes 6291480 | tf_op jit(solution)/shard_map/cond
  93.1 6.0 %weighted_values.2 = (bf16[2,4,64,128]{3,2,1,0:T(8,128)(2,1)S(1)}, bf16[2,4,64,128]{3,2,1,0:T(8,128)(2,1)S(1)}, bf16[2,4,64,128]{3,2,1,0:T(8,128)(2,1)S(1)}, bf16[2,4,64,128]{3,2,1,0:T(8,128)(2,1)S(1)}) custom-call(s32[651]{0:T(1024)S(1)} %get-tuple-element.89.meta_ref, bf16[8,32,384]{2,1,0:T(8,128)(2,1)S(1)} %all-to-all-done.1.refs_0_, ...), custom_call_target="tpu_custom_call" | custom-call | tf_op jit(solution)/shard_map/cond/branch_0_fun/weighted_values/pallas_call | solution.py:760
  99.4 0.1 collective-permute-start.19
  99.5 1.4 %collective-permute-start.20 = (bf16[2,4,64,128]{3,2,1,0:T(8,128)(2,1)S(1)}, bf16[2,4,64,128]{3,2,1,0:T(8,128)(2,1)S(1)}, u32[]{:S(2)}, u32[]{:S(2)}) collective-permute-start(bf16[2,4,64,128]{3,2,1,0:T(8,128)(2,1)S(1)} %get-tuple-element.197), channel_id=1, source_target_pairs={{0,4},{2,6},{4,0},{6,2},{8,12},{10,14},{12,8},{14,10},{1,5},{3,7},... | collective-permute-start | bytes 393224 | tf_op jit(solution)/shard_map/ppermute | solution.py:495
  100.9 2.1 %collective-permute-start.21 = (bf16[2,4,64,128]{3,2,1,0:T(8,128)(2,1)S(1)}, bf16[2,4,64,128]{3,2,1,0:T(8,128)(2,1)S(1)}, u32[]{:S(2)}, u32[]{:S(2)}) collective-permute-start(bf16[2,4,64,128]{3,2,1,0:T(8,128)(2,1)S(1)} %get-tuple-element.198), channel_id=1, source_target_pairs={{0,6},{2,4},{4,2},{6,0},{8,14},{10,12},{12,10},{14,8},{1,7},{3,5},... | collective-permute-start | bytes 393224 | tf_op jit(solution)/shard_map/ppermute | solution.py:495
  102.9 1.5 %collective-permute-done.19.refs_1_ = bf16[2,4,64,128]{3,2,1,0:T(8,128)(2,1)S(1)} collective-permute-done((bf16[2,4,64,128]{3,2,1,0:T(8,128)(2,1)S(1)}, bf16[2,4,64,128]{3,2,1,0:T(8,128)(2,1)S(1)}, u32[]{:S(2)}, u32[]{:S(2)}) %collective-permute-start.19) | collective-permute-done | bytes 131104 | tf_op jit(solution)/shard_map/ppermute | solution.py:495
  104.5 4.2 %collective-permute-done.21.refs_3_ = bf16[2,4,64,128]{3,2,1,0:T(8,128)(2,1)S(1)} collective-permute-done((bf16[2,4,64,128]{3,2,1,0:T(8,128)(2,1)S(1)}, bf16[2,4,64,128]{3,2,1,0:T(8,128)(2,1)S(1)}, u32[]{:S(2)}, u32[]{:S(2)}) %collective-permute-start.21) | collective-permute-done | bytes 131104 | tf_op jit(solution)/shard_map/ppermute | solution.py:495
  108.8 1.6 %collective-permute-start.22 = (bf16[2,4,64,128]{3,2,1,0:T(8,128)(2,1)S(1)}, bf16[2,4,64,128]{3,2,1,0:T(8,128)(2,1)S(1)}, u32[]{:S(2)}, u32[]{:S(2)}) collective-permute-start(bf16[2,4,64,128]{3,2,1,0:T(8,128)(2,1)S(1)} %get-tuple-element.201.after_ref), channel_id=1, source_target_pairs={{0,8},{2,10},{4,12},{6,14},{8,0},{10,2},{12,4},{14,6},{1,9},{3,11}... | collective-permute-start | bytes 393224 | tf_op jit(solution)/shard_map/ppermute | solution.py:495
  110.4 4.4 %collective-permute-done.22.got_ref = bf16[2,4,64,128]{3,2,1,0:T(8,128)(2,1)S(1)} collective-permute-done((bf16[2,4,64,128]{3,2,1,0:T(8,128)(2,1)S(1)}, bf16[2,4,64,128]{3,2,1,0:T(8,128)(2,1)S(1)}, u32[]{:S(2)}, u32[]{:S(2)}) %collective-permute-start.22) | collective-permute-done | bytes 131104 | tf_op jit(solution)/shard_map/ppermute | solution.py:495
  114.9 0.8 collective-permute-start.25
  115.7 0.9 collective-permute-start.24
  116.6 1.9 %collective-permute-start.23 = (bf16[16,4096]{1,0:T(8,128)(2,1)S(1)}, bf16[16,4096]{1,0:T(8,128)(2,1)S(1)}, u32[]{:S(2)}, u32[]{:S(2)}) collective-permute-start(bf16[16,4096]{1,0:T(8,128)(2,1)S(1)} %attended_sum.1), channel_id=1, source_target_pairs={{0,2},{2,0},{4,6},{6,4},{8,10},{10,8},{12,14},{14,12},{1,3},{3,1},... | collective-permute-start | bytes 393224 | tf_op jit(solution)/shard_map/ppermute | solution.py:495
  118.4 3.4 %copy-done.4 = bf16[4096,1024]{1,0:T(8,128)(2,1)S(1)} copy-done((bf16[4096,1024]{1,0:T(8,128)(2,1)S(1)}, bf16[4096,1024]{1,0:T(8,128)(2,1)}, u32[]{:S(2)}) %copy-start.4) | copy-done | bytes 8388632
  121.8 1.2 stage_out_weight.1
  123.0 0.8 fusion.41
  124.0 0.8 fusion.42.own_ref
  124.8 0.5 collective-permute-done.26.got_ref
  125.3 0.6 order_rows.1
  (64 shorter events, 1.4 us)
Async XLA Ops:
  0.0 21.8 %collective-permute-start.16 = (bf16[8,32,128]{2,1,0:T(8,128)(2,1)}, bf16[8,32,128]{2,1,0:T(8,128)(2,1)S(1)}, u32[]{:S(2)}, u32[]{:S(2)}) collective-permute-start(bf16[8,32,128]{2,1,0:T(8,128)(2,1)} %param.18), channel_id=1, source_target_pairs={{0,12},{2,14},{4,8},{6,10},{8,4},{10,6},{12,0},{14,2},{1,13},{3,15... | collective-permute-start | bytes 196616 | tf_op jit(solution)/shard_map/ppermute | solution.py:495
  5.0 16.7 %collective-permute-start.15 = (bf16[8,32,128]{2,1,0:T(8,128)(2,1)}, bf16[8,32,128]{2,1,0:T(8,128)(2,1)S(1)}, u32[]{:S(2)}, u32[]{:S(2)}) collective-permute-start(bf16[8,32,128]{2,1,0:T(8,128)(2,1)} %param.18), channel_id=1, source_target_pairs={{0,4},{2,6},{4,0},{6,2},{8,12},{10,14},{12,8},{14,10},{1,5},{3,7},... | collective-permute-start | bytes 196616 | tf_op jit(solution)/shard_map/ppermute | solution.py:495
  5.1 5.8 %collective-permute-start.13 = (bf16[8,32,128]{2,1,0:T(8,128)(2,1)}, bf16[8,32,128]{2,1,0:T(8,128)(2,1)S(1)}, u32[]{:S(2)}, u32[]{:S(2)}) collective-permute-start(bf16[8,32,128]{2,1,0:T(8,128)(2,1)} %param.18), channel_id=1, source_target_pairs={{0,8},{2,10},{4,12},{6,14},{8,0},{10,2},{12,4},{14,6},{1,9},{3,11}... | collective-permute-start | bytes 196616 | tf_op jit(solution)/shard_map/ppermute | solution.py:495
  5.7 11.0 %copy-start.15 = (s32[256,1]{0,1:T(1,128)S(1)}, s32[256,1]{0,1:T(1,128)}, u32[]{:S(2)}) copy-start(s32[256,1]{0,1:T(1,128)} %param.15) | copy-start | bytes 3076
  5.7 11.0 %copy-start.16 = (s32[256]{0:T(256)S(1)}, s32[256]{0:T(256)}, u32[]{:S(2)}) copy-start(s32[256]{0:T(256)} %fill_ref.1) | copy-start | bytes 3076
  5.7 16.1 %copy-start.14 = (bf16[8,32,128]{2,1,0:T(8,128)(2,1)S(1)}, bf16[8,32,128]{2,1,0:T(8,128)(2,1)}, u32[]{:S(2)}) copy-start(bf16[8,32,128]{2,1,0:T(8,128)(2,1)} %param.18) | copy-start | bytes 196612
  5.7 18.2 %copy-start.13 = (bf16[1024,4,256]{2,1,0:T(4,128)(2,1)S(1)}, bf16[1024,4,256]{2,1,0:T(4,128)(2,1)}, u32[]{:S(2)}) copy-start(bf16[1024,4,256]{2,1,0:T(4,128)(2,1)} %param.14) | copy-start | bytes 6291460
  10.9 42.2 %all-to-all-start.4 = ((bf16[8,96,1024]{2,1,0:T(8,128)(2,1)}), bf16[8,96,1024]{2,1,0:T(8,128)(2,1)}, u32[]{:S(2)}, u32[]{:S(2)}) async-start(bf16[8,96,1024]{2,1,0:T(8,128)(2,1)} %pack_live_tokens.3), calls=%async_computation.4 | async-start | bytes 3145728 | tf_op jit(solution)/shard_map/all_to_all | solution.py:549
  20.3 6.9 %collective-permute-start.14 = (s32[2]{0:T(128)S(1)}, s32[2]{0:T(128)S(1)}, u32[]{:S(2)}, u32[]{:S(2)}) collective-permute-start(s32[2]{0:T(128)S(1)} %pad_add_fusion.1), channel_id=1, source_target_pairs={{0,16},{16,0},{1,17},{17,1},{2,18},{18,2},{3,19},{19,3},{4,20},{20... | collective-permute-start | bytes 32 | tf_op jit(solution)/shard_map/ppermute | solution.py:595
  21.8 3.7 %copy-start.18 = (s32[256]{0:T(256)S(1)}, s32[256]{0:T(256)}, u32[]{:S(2)}) copy-start(s32[256]{0:T(256)} %param.16) | copy-start | bytes 3076
  21.9 15.6 %collective-permute-start.17 = (bf16[4,8,32,128]{3,2,1,0:T(8,128)(2,1)S(1)}, bf16[4,8,32,128]{3,2,1,0:T(8,128)(2,1)S(1)}, u32[]{:S(2)}, u32[]{:S(2)}) collective-permute-start(bf16[4,8,32,128]{3,2,1,0:T(8,128)(2,1)S(1)} %pad_maximum_fusion.1), channel_id=1, source_target_pairs={{0,2},{2,0},{4,6},{6,4},{8,10},{10,8},{12,14},{14,12},{1,3},{3,1},... | collective-permute-start | bytes 786440 | tf_op jit(solution)/shard_map/ppermute | solution.py:495
  24.2 1.3 %copy-start.5 = (bf16[1024,4,256]{2,0,1:T(8,128)(2,1)}, bf16[1024,4,256]{2,0,1:T(8,128)(2,1)S(1)}, u32[]{:S(2)}) copy-start(bf16[1024,4,256]{2,0,1:T(8,128)(2,1)S(1)} %copy.28) | copy-start | bytes 6291460
  40.5 1.3 %copy-start.2 = (bf16[4,256,1024]{2,1,0:T(8,128)(2,1)}, bf16[4,256,1024]{2,1,0:T(8,128)(2,1)S(1)}, u32[]{:S(2)}) copy-start(bf16[4,256,1024]{2,1,0:T(8,128)(2,1)S(1)} %key_projection.3.refs_5_) | copy-start | bytes 6291460
  53.1 3.8 %collective-permute-start.18 = (bf16[768,1024]{1,0:T(8,128)(2,1)}, bf16[768,1024]{1,0:T(8,128)(2,1)}, u32[]{:S(2)}, u32[]{:S(2)}) collective-permute-start(bf16[768,1024]{1,0:T(8,128)(2,1)} %bitcast.14.refs_0_), channel_id=1, source_target_pairs={{0,1},{1,0},{2,3},{3,2},{4,5},{5,4},{6,7},{7,6},{8,9},{9,8},{10,11... | collective-permute-start | bytes 4718600 | tf_op jit(solution)/shard_map/ppermute | solution.py:635
  56.8 1.6 %copy-start.3 = (bf16[4,256,1024]{2,1,0:T(8,128)(2,1)S(1)}, bf16[4,256,1024]{2,1,0:T(8,128)(2,1)}, u32[]{:S(2)}) copy-start(bf16[4,256,1024]{2,1,0:T(8,128)(2,1)} %copy-done.2) | copy-start | bytes 6291460
  58.4 7.4 %copy-start.8 = (bf16[8,256,4,256]{3,2,1,0:T(4,128)(2,1)S(1)}, bf16[8,256,4,256]{3,2,1,0:T(4,128)(2,1)}, u32[]{:S(2)}) copy-start(bf16[8,256,4,256]{3,2,1,0:T(4,128)(2,1)} %param.19) | copy-start | bytes 12582916
  58.4 7.4 %copy-start.17 = (s32[8]{0:T(128)S(1)}, s32[8]{0:T(128)}, u32[]{:S(2)}) copy-start(s32[8]{0:T(128)} %param.20) | copy-start | bytes 100
  65.9 7.2 %collective-permute-start.3 = (bf16[2,32,384]{2,1,0:T(8,128)(2,1)}, bf16[2,32,384]{2,1,0:T(8,128)(2,1)S(1)}, u32[]{:S(2)}, u32[]{:S(2)}) collective-permute-start(bf16[2,32,384]{2,1,0:T(8,128)(2,1)} %get-tuple-element.94), channel_id=1, source_target_pairs={{0,6},{2,4},{4,2},{6,0},{8,14},{10,12},{12,10},{14,8},{1,7},{3,5},... | collective-permute-start | bytes 147464 | tf_op jit(solution)/shard_map/cond/branch_0_fun/ppermute | solution.py:495
  66.0 7.2 %collective-permute-start.2 = (bf16[2,32,384]{2,1,0:T(8,128)(2,1)}, bf16[2,32,384]{2,1,0:T(8,128)(2,1)S(1)}, u32[]{:S(2)}, u32[]{:S(2)}) collective-permute-start(bf16[2,32,384]{2,1,0:T(8,128)(2,1)} %get-tuple-element.93), channel_id=1, source_target_pairs={{0,4},{2,6},{4,0},{6,2},{8,12},{10,14},{12,8},{14,10},{1,5},{3,7},... | collective-permute-start | bytes 147464 | tf_op jit(solution)/shard_map/cond/branch_0_fun/ppermute | solution.py:495
  68.8 4.4 %collective-permute-start.1 = (bf16[2,32,384]{2,1,0:T(8,128)(2,1)}, bf16[2,32,384]{2,1,0:T(8,128)(2,1)S(1)}, u32[]{:S(2)}, u32[]{:S(2)}) collective-permute-start(bf16[2,32,384]{2,1,0:T(8,128)(2,1)} %get-tuple-element.92), channel_id=1, source_target_pairs={{0,2},{2,0},{4,6},{6,4},{8,10},{10,8},{12,14},{14,12},{1,3},{3,1},... | collective-permute-start | bytes 147464 | tf_op jit(solution)/shard_map/cond/branch_0_fun/ppermute | solution.py:495
  70.3 2.1 %copy-start.11 = (bf16[8,256,4,256]{3,1,2,0:T(8,128)(2,1)}, bf16[8,256,4,256]{3,1,2,0:T(8,128)(2,1)S(1)}, u32[]{:S(2)}) copy-start(bf16[8,256,4,256]{3,1,2,0:T(8,128)(2,1)S(1)} %copy.25) | copy-start | bytes 12582916 | tf_op jit(solution)/shard_map/cond
  73.2 4.8 %collective-permute-start.4 = (bf16[32,384]{1,0:T(8,128)(2,1)S(1)}, bf16[32,384]{1,0:T(8,128)(2,1)S(1)}, u32[]{:S(2)}, u32[]{:S(2)}) collective-permute-start(bf16[32,384]{1,0:T(8,128)(2,1)S(1)} %get-tuple-element.96), channel_id=1, source_target_pairs={{0,8},{2,10},{4,12},{6,14},{8,0},{10,2},{12,4},{14,6},{1,9},{3,11}... | collective-permute-start | bytes 73736 | tf_op jit(solution)/shard_map/cond/branch_0_fun/ppermute | solution.py:495
  79.0 11.3 %all-to-all-start.1 = ((bf16[8,32,384]{2,1,0:T(8,128)(2,1)}), bf16[8,32,384]{2,1,0:T(8,128)(2,1)S(1)}, u32[]{:S(2)}, u32[]{:S(2)}) async-start(bf16[8,32,384]{2,1,0:T(8,128)(2,1)} %get-tuple-element.101.refs_4_), calls=%async_computation.1 | async-start | bytes 393216 | tf_op jit(solution)/shard_map/cond/branch_0_fun/all_to_all | solution.py:753
  82.7 5.2 %copy-start.12 = (bf16[8,256,4,256]{3,1,2,0:T(8,128)(2,1)S(1)}, bf16[8,256,4,256]{3,1,2,0:T(8,128)(2,1)}, u32[]{:S(2)}) copy-start(bf16[8,256,4,256]{3,1,2,0:T(8,128)(2,1)} %copy-done.11) | copy-start | bytes 12582916 | tf_op jit(solution)/shard_map/cond
  82.7 7.6 %copy-start.6 = (bf16[4,1024,256]{2,1,0:T(8,128)(2,1)S(1)}, bf16[4,1024,256]{2,1,0:T(8,128)(2,1)}, u32[]{:S(2)}) copy-start(bf16[4,1024,256]{2,1,0:T(8,128)(2,1)} %get-tuple-element.107.refs_3_) | copy-start | bytes 6291460 | tf_op jit(solution)/shard_map/cond
  90.3 2.8 %copy-start.1 = (bf16[8,384,1024]{2,1,0:T(8,128)(2,1)S(1)}, bf16[8,384,1024]{2,1,0:T(8,128)(2,1)}, u32[]{:S(2)}) copy-start(bf16[8,384,1024]{2,1,0:T(8,128)(2,1)} %owner_lists.2.refs_2_) | copy-start | bytes 18874372 | tf_op jit(solution)/shard_map/cond
  99.4 5.0 %collective-permute-start.19 = (bf16[2,4,64,128]{3,2,1,0:T(8,128)(2,1)S(1)}, bf16[2,4,64,128]{3,2,1,0:T(8,128)(2,1)S(1)}, u32[]{:S(2)}, u32[]{:S(2)}) collective-permute-start(bf16[2,4,64,128]{3,2,1,0:T(8,128)(2,1)S(1)} %get-tuple-element.196), channel_id=1, source_target_pairs={{0,2},{2,0},{4,6},{6,4},{8,10},{10,8},{12,14},{14,12},{1,3},{3,1},... | collective-permute-start | bytes 393224 | tf_op jit(solution)/shard_map/ppermute | solution.py:495
  99.5 5.0 %collective-permute-start.20 = (bf16[2,4,64,128]{3,2,1,0:T(8,128)(2,1)S(1)}, bf16[2,4,64,128]{3,2,1,0:T(8,128)(2,1)S(1)}, u32[]{:S(2)}, u32[]{:S(2)}) collective-permute-start(bf16[2,4,64,128]{3,2,1,0:T(8,128)(2,1)S(1)} %get-tuple-element.197), channel_id=1, source_target_pairs={{0,4},{2,6},{4,0},{6,2},{8,12},{10,14},{12,8},{14,10},{1,5},{3,7},... | collective-permute-start | bytes 393224 | tf_op jit(solution)/shard_map/ppermute | solution.py:495
  100.9 7.8 %collective-permute-start.21 = (bf16[2,4,64,128]{3,2,1,0:T(8,128)(2,1)S(1)}, bf16[2,4,64,128]{3,2,1,0:T(8,128)(2,1)S(1)}, u32[]{:S(2)}, u32[]{:S(2)}) collective-permute-start(bf16[2,4,64,128]{3,2,1,0:T(8,128)(2,1)S(1)} %get-tuple-element.198), channel_id=1, source_target_pairs={{0,6},{2,4},{4,2},{6,0},{8,14},{10,12},{12,10},{14,8},{1,7},{3,5},... | collective-permute-start | bytes 393224 | tf_op jit(solution)/shard_map/ppermute | solution.py:495
  108.8 6.0 %collective-permute-start.22 = (bf16[2,4,64,128]{3,2,1,0:T(8,128)(2,1)S(1)}, bf16[2,4,64,128]{3,2,1,0:T(8,128)(2,1)S(1)}, u32[]{:S(2)}, u32[]{:S(2)}) collective-permute-start(bf16[2,4,64,128]{3,2,1,0:T(8,128)(2,1)S(1)} %get-tuple-element.201.after_ref), channel_id=1, source_target_pairs={{0,8},{2,10},{4,12},{6,14},{8,0},{10,2},{12,4},{14,6},{1,9},{3,11}... | collective-permute-start | bytes 393224 | tf_op jit(solution)/shard_map/ppermute | solution.py:495
  114.9 8.1 %collective-permute-start.25 = (bf16[16,4096]{1,0:T(8,128)(2,1)S(1)}, bf16[16,4096]{1,0:T(8,128)(2,1)S(1)}, u32[]{:S(2)}, u32[]{:S(2)}) collective-permute-start(bf16[16,4096]{1,0:T(8,128)(2,1)S(1)} %attended_sum.1), channel_id=1, source_target_pairs={{0,6},{2,4},{4,2},{6,0},{8,14},{10,12},{12,10},{14,8},{1,7},{3,5},... | collective-permute-start | bytes 393224 | tf_op jit(solution)/shard_map/ppermute | solution.py:495
  115.7 7.3 %collective-permute-start.24 = (bf16[16,4096]{1,0:T(8,128)(2,1)S(1)}, bf16[16,4096]{1,0:T(8,128)(2,1)S(1)}, u32[]{:S(2)}, u32[]{:S(2)}) collective-permute-start(bf16[16,4096]{1,0:T(8,128)(2,1)S(1)} %attended_sum.1), channel_id=1, source_target_pairs={{0,4},{2,6},{4,0},{6,2},{8,12},{10,14},{12,8},{14,10},{1,5},{3,7},... | collective-permute-start | bytes 393224 | tf_op jit(solution)/shard_map/ppermute | solution.py:495
  116.6 6.5 %collective-permute-start.23 = (bf16[16,4096]{1,0:T(8,128)(2,1)S(1)}, bf16[16,4096]{1,0:T(8,128)(2,1)S(1)}, u32[]{:S(2)}, u32[]{:S(2)}) collective-permute-start(bf16[16,4096]{1,0:T(8,128)(2,1)S(1)} %attended_sum.1), channel_id=1, source_target_pairs={{0,2},{2,0},{4,6},{6,4},{8,10},{10,8},{12,14},{14,12},{1,3},{3,1},... | collective-permute-start | bytes 393224 | tf_op jit(solution)/shard_map/ppermute | solution.py:495
  118.4 3.4 %copy-start.4 = (bf16[4096,1024]{1,0:T(8,128)(2,1)S(1)}, bf16[4096,1024]{1,0:T(8,128)(2,1)}, u32[]{:S(2)}) copy-start(bf16[4096,1024]{1,0:T(8,128)(2,1)} %weight_ref.1) | copy-start | bytes 25165828
  123.9 1.4 %collective-permute-start.26 = (f32[64,512]{1,0:T(8,128)S(1)}, f32[64,512]{1,0:T(8,128)S(1)}, u32[]{:S(2)}, u32[]{:S(2)}) collective-permute-start(f32[64,512]{1,0:T(8,128)S(1)} %fusion.41), channel_id=1, source_target_pairs={{0,1},{1,0},{2,3},{3,2},{4,5},{5,4},{6,7},{7,6},{8,9},{9,8},{10,11... | collective-permute-start | bytes 393224 | tf_op jit(solution)/shard_map/ppermute | solution.py:842

commit v20 on v18

--- a/solution.py
+++ b/solution.py
@@ -23,28 +23,22 @@
     for q in range(n):
         count[q] = 0
 
-    @pl.loop(0, blocks)
-    def _(b):
-        owner = dest_ref[first + b]
-        count[owner] = count[owner] + fill_ref[first + b]
-
-    def starts(q, total):
+    owners = [dest_ref[first + b] for b in range(blocks)]
+    fills = [fill_ref[first + b] for b in range(blocks)]
+    for owner, fill in zip(owners, fills):
+        count[owner] = count[owner] + fill
+    total = jnp.int32(0)
+    for q in range(n):
         here = count[q]
         count[q] = total
-        return total + here
-
-    lax.fori_loop(0, n, starts, jnp.int32(0))
+        total = total + here
     token = lax.broadcasted_iota(jnp.int32, (1, tokens), 1)
-
-    def place(b, ranks):
-        owner = dest_ref[first + b]
-        fill = fill_ref[first + b]
+    ranks = jnp.full((1, tokens), -1, jnp.int32)
+    for b, (owner, fill) in enumerate(zip(owners, fills)):
         start = count[owner]
         count[owner] = start + fill
         inner = token - b * BLK
-        return jnp.where((inner >= 0) & (inner < fill), start + inner, ranks)
-
-    ranks = lax.fori_loop(0, blocks, place, jnp.full((1, tokens), -1, jnp.int32))
+        ranks = jnp.where((inner >= 0) & (inner < fill), start + inner, ranks)
     wanted = base + at_ref[1] * size + lax.broadcasted_iota(jnp.int32, (size, tokens), 0)
     pick = (wanted == ranks).astype(jnp.bfloat16)
     for q in range(n):
@@ -56,7 +50,7 @@
         store(q).wait()
 
 
-def pack(x_prompt, fill, dest, at, n, base, size):
+def pack(x_prompt, fill, dest, at, n, base, size, grant=16):
     tokens, width = x_prompt.shape
     part = width // n
     return pl.pallas_call(
@@ -73,7 +67,7 @@
             ],
         ),
         out_shape=jax.ShapeDtypeStruct((n, size, part), jnp.bfloat16),
-        compiler_params=pltpu.CompilerParams(vmem_limit_bytes=16 * MIB),
+        compiler_params=pltpu.CompilerParams(vmem_limit_bytes=grant * MIB),
         cost_estimate=pl.CostEstimate(
             flops=2 * size * tokens * width, bytes_accessed=64 * MIB, transcendentals=0
         ),
@@ -581,7 +575,7 @@
     over, longer = most[0] > ntp * size, most[1] > near
 
     def exchange_rest():
-        rest = pack(x_prompt, pack_fill, pack_dest, at, n, ntp * size, extra)
+        rest = pack(x_prompt, pack_fill, pack_dest, at, n, ntp * size, extra, 59)
         rest = lax.all_to_all(rest, "pool", 0, 0, tiled=True).reshape(n * extra, part)
         return rest, lax.ppermute(rest, "tp", swap)
 

time: 126 us -> 126 us (level)
  no operation moved by 1% of the time
where the time goes in v20:
time: 126 us
  waiting for transfers between devices  35.5 us (28%)
  starting transfers between devices  31.4 us (25%)
  Pallas kernels  30.9 us (25%)
  local copies, waits for them, and re-layouts  16.6 us (13%)
  other arithmetic  6.46 us (5%)
  matrix products  2.83 us (2%)
  between operations  1.5 us (1%)
    ppermute x11, waiting for transfers between devices, with_partner(): return lax.ppermute(x, 'pool', [(i, i ^ k) for i in range(n)])  17.7 us
    ppermute x11, starting transfers between devices, with_partner(): return lax.ppermute(x, 'pool', [(i, i ^ k) for i in range(n)])  16.9 us
    all_to_all x1, waiting for transfers between devices, local(): lax.all_to_all(packed, 'pool', 0, 0, tiled=True).reshape(n * size, part)  11.2 us
    pallas_call x1, Pallas kernels, local(): pl.pallas_call(functools.partial(score_kernel, n, rows), grid_spec=pltpu....  7.44 us
    unnamed x20, local copies, waits for them, and re-layouts  6.32 us
    pallas_call x1, Pallas kernels, exchange_weights(): pl.pallas_call(functools.partial(value_kernel, n, rows, lanes, count), gr...  6 us
    all_to_all x1, starting transfers between devices, local(): lax.all_to_all(packed, 'pool', 0, 0, tiled=True).reshape(n * size, part)  5.79 us
    pallas_call x1, Pallas kernels, exchange_weights(): pl.pallas_call(functools.partial(list_kernel, n, lanes), grid_spec=pltpu....  5.15 us
  transfers between devices with their start and end apart: 17, of which 10 were waited for; matrix products, arithmetic and copies ran while one was open for 12% of the time, Pallas kernels for 12%

profile of v20, /device:TPU:0, one launch (start us, length us, event | category | flops | bytes accessed | tf_op | source)
XLA Modules:
  0.0 125.5 jit_solution(8867633285218660487)
XLA Ops:
  0.0 5.0 %collective-permute-start.3 = (bf16[8,32,128]{2,1,0:T(8,128)(2,1)}, bf16[8,32,128]{2,1,0:T(8,128)(2,1)S(1)}, u32[]{:S(2)}, u32[]{:S(2)}) collective-permute-start(bf16[8,32,128]{2,1,0:T(8,128)(2,1)} %param.18), channel_id=1, source_target_pairs={{0,12},{2,14},{4,8},{6,10},{8,4},{10,6},{12,0},{14,2},{1,13},{3,15... | collective-permute-start | bytes 196616 | tf_op jit(solution)/shard_map/ppermute | solution.py:472
  5.1 0.6 collective-permute-start.1
  5.7 4.8 %pack_live_tokens.3 = bf16[8,96,1024]{2,1,0:T(8,128)(2,1)} custom-call(s32[2]{0:T(128)S(1)} %pad_add_fusion.at_ref, s32[256]{0:T(256)} %fill_ref.1, s32[256]{0:T(256)} %bitcast.56, bf16[256,8192]{1,0:T(8,128)(2,1)} %x_ref.1), custom_call_target="tpu_custom_call" | custom-call | flops 402653184 | bytes 67108864 | tf_op jit(solution)/shard_map/pack_live_tokens/pallas_call | solution.py:56
  10.6 0.3 collective-permute-done.1
  10.9 5.8 %all-to-all-start.7 = ((bf16[8,96,1024]{2,1,0:T(8,128)(2,1)}), bf16[8,96,1024]{2,1,0:T(8,128)(2,1)}, u32[]{:S(2)}, u32[]{:S(2)}) async-start(bf16[8,96,1024]{2,1,0:T(8,128)(2,1)} %pack_live_tokens.3), calls=%async_computation.7 | async-start | bytes 3145728 | tf_op jit(solution)/shard_map/all_to_all | solution.py:526
  16.7 0.2 select_reduce_fusion.4
  17.1 0.1 fusion.64
  17.5 0.7 reduce_max.37
  18.1 0.1 reduce_sum.112
  18.2 0.6 reduce_max.36
  18.9 1.3 %pad_add_fusion.1 = s32[2]{0:T(128)S(1)} fusion(s32[1]{0:T(128)} %bitcast.10, s32[1]{0:T(128)} %bitcast.9), kind=kLoop, calls=%fused_computation.102 | loop fusion | flops 2 | bytes 16 | tf_op jit(solution)/shard_map/stack | solution.py:567
  20.1 1.5 %collective-permute-start.4 = (s32[2]{0:T(128)S(1)}, s32[2]{0:T(128)S(1)}, u32[]{:S(2)}, u32[]{:S(2)}) collective-permute-start(s32[2]{0:T(128)S(1)} %pad_add_fusion.1), channel_id=1, source_target_pairs={{0,16},{16,0},{1,17},{17,1},{2,18},{18,2},{3,19},{19,3},{4,20},{20... | collective-permute-start | bytes 32 | tf_op jit(solution)/shard_map/ppermute | solution.py:572
  21.7 2.1 %collective-permute-start.5 = (bf16[4,8,32,128]{3,2,1,0:T(8,128)(2,1)S(1)}, bf16[4,8,32,128]{3,2,1,0:T(8,128)(2,1)S(1)}, u32[]{:S(2)}, u32[]{:S(2)}) collective-permute-start(bf16[4,8,32,128]{3,2,1,0:T(8,128)(2,1)S(1)} %pad_maximum_fusion.1), channel_id=1, source_target_pairs={{0,2},{2,0},{4,6},{6,4},{8,10},{10,8},{12,14},{14,12},{1,3},{3,1},... | collective-permute-start | bytes 786440 | tf_op jit(solution)/shard_map/ppermute | solution.py:472
  23.8 0.3 copy.28
  24.1 1.3 %key_projection.2.refs_4_ = bf16[4,256,1024]{2,1,0:T(8,128)(2,1)S(1)} custom-call(bf16[32,32,128]{2,1,0:T(8,128)(2,1)S(1)} %bitcast.42, bf16[4,1024,256]{2,1,0:T(8,128)(2,1)S(1)} %bitcast.44), custom_call_target="tpu_custom_call" | custom-call | bytes 1024 | tf_op jit(solution)/shard_map/key_projection/pallas_call | solution.py:592
  25.4 0.1 select_reduce_fusion.3
  25.5 0.1 fusion.45
  25.6 0.3 select_reduce_fusion.2
  25.9 1.0 select_reduce_fusion
  27.0 1.3 %fusion.71 = s32[2]{0:T(128)S(1)} fusion(s32[2]{0:T(128)S(1)} %collective-permute-done.4, s32[1]{0:T(128)} %bitcast.10, s32[1]{0:T(128)} %bitcast.9), kind=kLoop, calls=%fused_computation.114 | loop fusion | flops 4 | bytes 24 | tf_op jit(solution)/shard_map/max | solution.py:571
  28.2 0.6 fusion.68
  29.6 7.8 %collective-permute-done.5 = bf16[4,8,32,128]{3,2,1,0:T(8,128)(2,1)S(1)} collective-permute-done((bf16[4,8,32,128]{3,2,1,0:T(8,128)(2,1)S(1)}, bf16[4,8,32,128]{3,2,1,0:T(8,128)(2,1)S(1)}, u32[]{:S(2)}, u32[]{:S(2)}) %collective-permute-start.5) | collective-permute-done | bytes 262176 | tf_op jit(solution)/shard_map/ppermute | solution.py:472
  37.4 3.1 %key_projection.3.refs_5_ = bf16[4,256,1024]{2,1,0:T(8,128)(2,1)S(1)} custom-call(bf16[32,32,128]{2,1,0:T(8,128)(2,1)S(1)} %bitcast.43, bf16[4,1024,256]{2,1,0:T(8,128)(2,1)} %bitcast.45), custom_call_target="tpu_custom_call" | custom-call | bytes 1024 | tf_op jit(solution)/shard_map/key_projection/pallas_call | solution.py:592
  40.5 1.3 %copy-done.2 = bf16[4,256,1024]{2,1,0:T(8,128)(2,1)} copy-done((bf16[4,256,1024]{2,1,0:T(8,128)(2,1)}, bf16[4,256,1024]{2,1,0:T(8,128)(2,1)S(1)}, u32[]{:S(2)}) %copy-start.2) | copy-done | bytes 2097176
  41.8 11.2 %all-to-all-done.7 = bf16[8,96,1024]{2,1,0:T(8,128)(2,1)} async-done(((bf16[8,96,1024]{2,1,0:T(8,128)(2,1)}), bf16[8,96,1024]{2,1,0:T(8,128)(2,1)}, u32[]{:S(2)}, u32[]{:S(2)}) %all-to-all-start.7) | async-done | bytes 1572896 | tf_op jit(solution)/shard_map/all_to_all | solution.py:526
  53.6 1.7 %conditional.2 = (bf16[256,1024]{1,0:T(8,128)(2,1)}, bf16[256,1024]{1,0:T(8,128)(2,1)}) conditional(s32[]{:T(128)} %bitcast.21, () %tuple.25, (s32[2]{0:T(128)S(1)}, s32[256]{0:T(256)S(1)}, s32[256]{0:T(256)S(1)}, bf16[256,8192]{1,0:T(8,128)(2,1)}) %tuple.56), branch_computations={%region_12.13_spmd, %region_13.14_spmd} | conditional | flops 134217728 | bytes 70254648 | solution.py:585
  53.6 0.9 broadcast.406.clone
  54.4 0.9 broadcast.406
  55.3 1.4 %collective-permute-done.6.refs_1_ = bf16[768,1024]{1,0:T(8,128)(2,1)} collective-permute-done((bf16[768,1024]{1,0:T(8,128)(2,1)}, bf16[768,1024]{1,0:T(8,128)(2,1)}, u32[]{:S(2)}, u32[]{:S(2)}) %collective-permute-start.6) | collective-permute-done | bytes 1572896 | tf_op jit(solution)/shard_map/ppermute | solution.py:612
  56.8 1.6 %copy-done.3 = bf16[4,256,1024]{2,1,0:T(8,128)(2,1)S(1)} copy-done((bf16[4,256,1024]{2,1,0:T(8,128)(2,1)S(1)}, bf16[4,256,1024]{2,1,0:T(8,128)(2,1)}, u32[]{:S(2)}) %copy-start.3) | copy-done | bytes 2097176
  58.4 7.4 %prompt_scores.1 = (bf16[8,32,384]{2,1,0:T(8,128)(2,1)}, bf16[8,32,256]{2,1,0:T(8,128)(2,1)}) custom-call(s32[651]{0:T(1024)S(1)} %concatenate.6.meta_ref, bf16[768,1024]{1,0:T(8,128)(2,1)} %bitcast.12.refs_0_, bf16[768,1024]{1,0:T(8,128)(2,1)} %collective-permute-done.6.refs_1_, bf16[256,1024]{1,0:T(8,128)(2,1)} %get-tuple-element.141.refs_2_, ...), custom_call_target="tpu_custom_call" | custom-call | tf_op jit(solution)/shard_map/prompt_scores/pallas_call | solution.py:631
  65.8 33.1 %conditional.3 = (bf16[2,4,64,128]{3,2,1,0:T(8,128)(2,1)S(1)}, bf16[2,4,64,128]{3,2,1,0:T(8,128)(2,1)S(1)}, bf16[2,4,64,128]{3,2,1,0:T(8,128)(2,1)S(1)}, bf16[2,...) conditional(s32[]{:T(128)} %bitcast.11, (bf16[8,32,384]{2,1,0:T(8,128)(2,1)}, s32[1,640]{1,0:T(1,128)S(1)}, ...), branch_computations={%region_14.17_spmd, %region_17.20_spmd} | conditional | flops 34047488 | bytes 99326216 | solution.py:750
  65.8 3.5 %all-to-all-start.1 = ((bf16[8,32,384]{2,1,0:T(8,128)(2,1)}), bf16[8,32,384]{2,1,0:T(8,128)(2,1)S(1)}, u32[]{:S(2)}, u32[]{:S(2)}) async-start(bf16[8,32,384]{2,1,0:T(8,128)(2,1)} %get-tuple-element.68), calls=%async_computation.1 | async-start | bytes 393216 | tf_op jit(solution)/shard_map/cond/branch_0_fun/all_to_all | solution.py:661
  69.5 3.0 %copy.25 = bf16[8,256,4,256]{3,1,2,0:T(8,128)(2,1)S(1)} copy(bf16[8,256,4,256]{3,2,1,0:T(4,128)(2,1)} %get-tuple-element.211) | data formatting | bytes 8388608 | tf_op jit(solution)/shard_map
  72.4 0.7 fusion.66
  73.2 1.3 %copy-done.9 = bf16[8,256,4,256]{3,1,2,0:T(8,128)(2,1)} copy-done((bf16[8,256,4,256]{3,1,2,0:T(8,128)(2,1)}, bf16[8,256,4,256]{3,1,2,0:T(8,128)(2,1)S(1)}, u32[]{:S(2)}) %copy-start.9) | copy-done | bytes 4194328 | tf_op jit(solution)/shard_map/cond
  74.5 0.1 broadcast_in_dim.162.refs_2_
  74.6 0.2 fusion.17
  74.8 0.1 broadcast_in_dim.163.refs_3_
  74.9 2.8 %all-to-all-done.1.refs_0_ = bf16[8,32,384]{2,1,0:T(8,128)(2,1)S(1)} async-done(((bf16[8,32,384]{2,1,0:T(8,128)(2,1)}), bf16[8,32,384]{2,1,0:T(8,128)(2,1)S(1)}, u32[]{:S(2)}, u32[]{:S(2)}) %all-to-all-start.1) | async-done | bytes 196640 | tf_op jit(solution)/shard_map/cond/branch_0_fun/all_to_all | solution.py:661
  77.7 1.1 softmax_weights.2
  78.8 3.6 %all-to-all-start.2 = ((bf16[8,32,384]{2,1,0:T(8,128)(2,1)}), bf16[8,32,384]{2,1,0:T(8,128)(2,1)S(1)}, u32[]{:S(2)}, u32[]{:S(2)}) async-start(bf16[8,32,384]{2,1,0:T(8,128)(2,1)} %get-tuple-element.73.refs_4_), calls=%async_computation.2 | async-start | bytes 393216 | tf_op jit(solution)/shard_map/cond/branch_0_fun/all_to_all | solution.py:708
  82.4 0.1 reduce
  82.5 5.1 %owner_lists.2.refs_2_ = bf16[8,384,1024]{2,1,0:T(8,128)(2,1)} custom-call(s32[651]{0:T(1024)S(1)} %get-tuple-element.67.meta_ref, bf16[768,1024]{1,0:T(8,128)(2,1)} %get-tuple-element.75.refs_0_, bf16[768,1024]{1,0:T(8,128)(2,1)} %get-tuple-element.76.refs_1_, bf16[256,1024]{1,0:T(8,128)(2,1)} %get-tuple-element.77.refs_2_, ...), custom_call_target="tpu_custom_call" | custom-call | bytes 16777216 | tf_op jit(solution)/shard_map/cond/branch_0_fun/owner_lists/pallas_call | solution.py:687
  87.7 0.4 fusion.13
  88.1 1.8 %all-to-all-done.2.refs_0_ = bf16[8,32,384]{2,1,0:T(8,128)(2,1)S(1)} async-done(((bf16[8,32,384]{2,1,0:T(8,128)(2,1)}), bf16[8,32,384]{2,1,0:T(8,128)(2,1)S(1)}, u32[]{:S(2)}, u32[]{:S(2)}) %all-to-all-start.2) | async-done | bytes 196640 | tf_op jit(solution)/shard_map/cond/branch_0_fun/all_to_all | solution.py:708
  90.0 2.8 %copy-done.1 = bf16[8,384,1024]{2,1,0:T(8,128)(2,1)S(1)} copy-done((bf16[8,384,1024]{2,1,0:T(8,128)(2,1)S(1)}, bf16[8,384,1024]{2,1,0:T(8,128)(2,1)}, u32[]{:S(2)}) %copy-start.1) | copy-done | bytes 6291480 | tf_op jit(solution)/shard_map/cond
  92.8 6.0 %weighted_values.2 = (bf16[2,4,64,128]{3,2,1,0:T(8,128)(2,1)S(1)}, bf16[2,4,64,128]{3,2,1,0:T(8,128)(2,1)S(1)}, bf16[2,4,64,128]{3,2,1,0:T(8,128)(2,1)S(1)}, bf16[2,4,64,128]{3,2,1,0:T(8,128)(2,1)S(1)}) custom-call(s32[651]{0:T(1024)S(1)} %get-tuple-element.67.meta_ref, bf16[8,32,384]{2,1,0:T(8,128)(2,1)S(1)} %all-to-all-done.2.refs_0_, ...), custom_call_target="tpu_custom_call" | custom-call | tf_op jit(solution)/shard_map/cond/branch_0_fun/weighted_values/pallas_call | solution.py:715
  99.0 1.0 collective-permute-start.7
  100.0 0.5 collective-permute-start.8
  100.5 2.1 %collective-permute-start.9 = (bf16[2,4,64,128]{3,2,1,0:T(8,128)(2,1)S(1)}, bf16[2,4,64,128]{3,2,1,0:T(8,128)(2,1)S(1)}, u32[]{:S(2)}, u32[]{:S(2)}) collective-permute-start(bf16[2,4,64,128]{3,2,1,0:T(8,128)(2,1)S(1)} %get-tuple-element.151), channel_id=1, source_target_pairs={{0,6},{2,4},{4,2},{6,0},{8,14},{10,12},{12,10},{14,8},{1,7},{3,5},... | collective-permute-start | bytes 393224 | tf_op jit(solution)/shard_map/ppermute | solution.py:472
  102.5 2.7 %collective-permute-done.7.refs_1_ = bf16[2,4,64,128]{3,2,1,0:T(8,128)(2,1)S(1)} collective-permute-done((bf16[2,4,64,128]{3,2,1,0:T(8,128)(2,1)S(1)}, bf16[2,4,64,128]{3,2,1,0:T(8,128)(2,1)S(1)}, u32[]{:S(2)}, u32[]{:S(2)}) %collective-permute-start.7) | collective-permute-done | bytes 131104 | tf_op jit(solution)/shard_map/ppermute | solution.py:472
  105.2 1.7 %collective-permute-done.9.refs_3_ = bf16[2,4,64,128]{3,2,1,0:T(8,128)(2,1)S(1)} collective-permute-done((bf16[2,4,64,128]{3,2,1,0:T(8,128)(2,1)S(1)}, bf16[2,4,64,128]{3,2,1,0:T(8,128)(2,1)S(1)}, u32[]{:S(2)}, u32[]{:S(2)}) %collective-permute-start.9) | collective-permute-done | bytes 131104 | tf_op jit(solution)/shard_map/ppermute | solution.py:472
  107.0 2.1 %collective-permute-start.10 = (bf16[2,4,64,128]{3,2,1,0:T(8,128)(2,1)S(1)}, bf16[2,4,64,128]{3,2,1,0:T(8,128)(2,1)S(1)}, u32[]{:S(2)}, u32[]{:S(2)}) collective-permute-start(bf16[2,4,64,128]{3,2,1,0:T(8,128)(2,1)S(1)} %get-tuple-element.154.after_ref), channel_id=1, source_target_pairs={{0,8},{2,10},{4,12},{6,14},{8,0},{10,2},{12,4},{14,6},{1,9},{3,11}... | collective-permute-start | bytes 393224 | tf_op jit(solution)/shard_map/ppermute | solution.py:472
  109.1 5.3 %collective-permute-done.10.got_ref = bf16[2,4,64,128]{3,2,1,0:T(8,128)(2,1)S(1)} collective-permute-done((bf16[2,4,64,128]{3,2,1,0:T(8,128)(2,1)S(1)}, bf16[2,4,64,128]{3,2,1,0:T(8,128)(2,1)S(1)}, u32[]{:S(2)}, u32[]{:S(2)}) %collective-permute-start.10) | collective-permute-done | bytes 131104 | tf_op jit(solution)/shard_map/ppermute | solution.py:472
  114.5 0.4 collective-permute-start.13
  114.9 2.0 %collective-permute-start.12 = (bf16[16,4096]{1,0:T(8,128)(2,1)S(1)}, bf16[16,4096]{1,0:T(8,128)(2,1)S(1)}, u32[]{:S(2)}, u32[]{:S(2)}) collective-permute-start(bf16[16,4096]{1,0:T(8,128)(2,1)S(1)} %attended_sum.1), channel_id=1, source_target_pairs={{0,4},{2,6},{4,0},{6,2},{8,12},{10,14},{12,8},{14,10},{1,5},{3,7},... | collective-permute-start | bytes 393224 | tf_op jit(solution)/shard_map/ppermute | solution.py:472
  116.9 1.1 collective-permute-start.11
  118.0 3.4 %copy-done.4 = bf16[4096,1024]{1,0:T(8,128)(2,1)S(1)} copy-done((bf16[4096,1024]{1,0:T(8,128)(2,1)S(1)}, bf16[4096,1024]{1,0:T(8,128)(2,1)}, u32[]{:S(2)}) %copy-start.4) | copy-done | bytes 8388632
  121.4 1.2 stage_out_weight.1
  122.6 0.8 fusion.47
  123.6 0.8 fusion.48.own_ref
  124.4 0.5 collective-permute-done.14.got_ref
  124.9 0.6 order_rows.1
  (55 shorter events, 1.0 us)
Async XLA Ops:
  0.0 10.6 %collective-permute-start.3 = (bf16[8,32,128]{2,1,0:T(8,128)(2,1)}, bf16[8,32,128]{2,1,0:T(8,128)(2,1)S(1)}, u32[]{:S(2)}, u32[]{:S(2)}) collective-permute-start(bf16[8,32,128]{2,1,0:T(8,128)(2,1)} %param.18), channel_id=1, source_target_pairs={{0,12},{2,14},{4,8},{6,10},{8,4},{10,6},{12,0},{14,2},{1,13},{3,15... | collective-permute-start | bytes 196616 | tf_op jit(solution)/shard_map/ppermute | solution.py:472
  5.0 5.6 %collective-permute-start.2 = (bf16[8,32,128]{2,1,0:T(8,128)(2,1)}, bf16[8,32,128]{2,1,0:T(8,128)(2,1)S(1)}, u32[]{:S(2)}, u32[]{:S(2)}) collective-permute-start(bf16[8,32,128]{2,1,0:T(8,128)(2,1)} %param.18), channel_id=1, source_target_pairs={{0,4},{2,6},{4,0},{6,2},{8,12},{10,14},{12,8},{14,10},{1,5},{3,7},... | collective-permute-start | bytes 196616 | tf_op jit(solution)/shard_map/ppermute | solution.py:472
  5.1 5.8 %collective-permute-start.1 = (bf16[8,32,128]{2,1,0:T(8,128)(2,1)}, bf16[8,32,128]{2,1,0:T(8,128)(2,1)S(1)}, u32[]{:S(2)}, u32[]{:S(2)}) collective-permute-start(bf16[8,32,128]{2,1,0:T(8,128)(2,1)} %param.18), channel_id=1, source_target_pairs={{0,8},{2,10},{4,12},{6,14},{8,0},{10,2},{12,4},{14,6},{1,9},{3,11}... | collective-permute-start | bytes 196616 | tf_op jit(solution)/shard_map/ppermute | solution.py:472
  5.7 11.0 %copy-start.13 = (s32[256,1]{0,1:T(1,128)S(1)}, s32[256,1]{0,1:T(1,128)}, u32[]{:S(2)}) copy-start(s32[256,1]{0,1:T(1,128)} %param.15) | copy-start | bytes 3076
  5.7 11.0 %copy-start.14 = (s32[256]{0:T(256)S(1)}, s32[256]{0:T(256)}, u32[]{:S(2)}) copy-start(s32[256]{0:T(256)} %fill_ref.1) | copy-start | bytes 3076
  5.7 15.9 %copy-start.12 = (bf16[8,32,128]{2,1,0:T(8,128)(2,1)S(1)}, bf16[8,32,128]{2,1,0:T(8,128)(2,1)}, u32[]{:S(2)}) copy-start(bf16[8,32,128]{2,1,0:T(8,128)(2,1)} %param.18) | copy-start | bytes 196612
  5.7 18.0 %copy-start.11 = (bf16[1024,4,256]{2,1,0:T(4,128)(2,1)S(1)}, bf16[1024,4,256]{2,1,0:T(4,128)(2,1)}, u32[]{:S(2)}) copy-start(bf16[1024,4,256]{2,1,0:T(4,128)(2,1)} %param.14) | copy-start | bytes 6291460
  10.9 42.1 %all-to-all-start.7 = ((bf16[8,96,1024]{2,1,0:T(8,128)(2,1)}), bf16[8,96,1024]{2,1,0:T(8,128)(2,1)}, u32[]{:S(2)}, u32[]{:S(2)}) async-start(bf16[8,96,1024]{2,1,0:T(8,128)(2,1)} %pack_live_tokens.3), calls=%async_computation.7 | async-start | bytes 3145728 | tf_op jit(solution)/shard_map/all_to_all | solution.py:526
  20.1 6.8 %collective-permute-start.4 = (s32[2]{0:T(128)S(1)}, s32[2]{0:T(128)S(1)}, u32[]{:S(2)}, u32[]{:S(2)}) collective-permute-start(s32[2]{0:T(128)S(1)} %pad_add_fusion.1), channel_id=1, source_target_pairs={{0,16},{16,0},{1,17},{17,1},{2,18},{18,2},{3,19},{19,3},{4,20},{20... | collective-permute-start | bytes 32 | tf_op jit(solution)/shard_map/ppermute | solution.py:572
  21.7 3.7 %copy-start.16 = (s32[256]{0:T(256)S(1)}, s32[256]{0:T(256)}, u32[]{:S(2)}) copy-start(s32[256]{0:T(256)} %param.16) | copy-start | bytes 3076
  21.7 15.7 %collective-permute-start.5 = (bf16[4,8,32,128]{3,2,1,0:T(8,128)(2,1)S(1)}, bf16[4,8,32,128]{3,2,1,0:T(8,128)(2,1)S(1)}, u32[]{:S(2)}, u32[]{:S(2)}) collective-permute-start(bf16[4,8,32,128]{3,2,1,0:T(8,128)(2,1)S(1)} %pad_maximum_fusion.1), channel_id=1, source_target_pairs={{0,2},{2,0},{4,6},{6,4},{8,10},{10,8},{12,14},{14,12},{1,3},{3,1},... | collective-permute-start | bytes 786440 | tf_op jit(solution)/shard_map/ppermute | solution.py:472
  24.0 1.3 %copy-start.5 = (bf16[1024,4,256]{2,0,1:T(8,128)(2,1)}, bf16[1024,4,256]{2,0,1:T(8,128)(2,1)S(1)}, u32[]{:S(2)}) copy-start(bf16[1024,4,256]{2,0,1:T(8,128)(2,1)S(1)} %copy.28) | copy-start | bytes 6291460
  40.5 1.3 %copy-start.2 = (bf16[4,256,1024]{2,1,0:T(8,128)(2,1)}, bf16[4,256,1024]{2,1,0:T(8,128)(2,1)S(1)}, u32[]{:S(2)}) copy-start(bf16[4,256,1024]{2,1,0:T(8,128)(2,1)S(1)} %key_projection.3.refs_5_) | copy-start | bytes 6291460
  53.0 3.8 %collective-permute-start.6 = (bf16[768,1024]{1,0:T(8,128)(2,1)}, bf16[768,1024]{1,0:T(8,128)(2,1)}, u32[]{:S(2)}, u32[]{:S(2)}) collective-permute-start(bf16[768,1024]{1,0:T(8,128)(2,1)} %bitcast.12.refs_0_), channel_id=1, source_target_pairs={{0,1},{1,0},{2,3},{3,2},{4,5},{5,4},{6,7},{7,6},{8,9},{9,8},{10,11... | collective-permute-start | bytes 4718600 | tf_op jit(solution)/shard_map/ppermute | solution.py:612
  56.8 1.6 %copy-start.3 = (bf16[4,256,1024]{2,1,0:T(8,128)(2,1)S(1)}, bf16[4,256,1024]{2,1,0:T(8,128)(2,1)}, u32[]{:S(2)}) copy-start(bf16[4,256,1024]{2,1,0:T(8,128)(2,1)} %copy-done.2) | copy-start | bytes 6291460
  58.4 7.5 %copy-start.15 = (s32[8]{0:T(128)S(1)}, s32[8]{0:T(128)}, u32[]{:S(2)}) copy-start(s32[8]{0:T(128)} %param.20) | copy-start | bytes 100
  65.8 11.9 %all-to-all-start.1 = ((bf16[8,32,384]{2,1,0:T(8,128)(2,1)}), bf16[8,32,384]{2,1,0:T(8,128)(2,1)S(1)}, u32[]{:S(2)}, u32[]{:S(2)}) async-start(bf16[8,32,384]{2,1,0:T(8,128)(2,1)} %get-tuple-element.68), calls=%async_computation.1 | async-start | bytes 393216 | tf_op jit(solution)/shard_map/cond/branch_0_fun/all_to_all | solution.py:661
  72.4 2.0 %copy-start.9 = (bf16[8,256,4,256]{3,1,2,0:T(8,128)(2,1)}, bf16[8,256,4,256]{3,1,2,0:T(8,128)(2,1)S(1)}, u32[]{:S(2)}) copy-start(bf16[8,256,4,256]{3,1,2,0:T(8,128)(2,1)S(1)} %copy.25) | copy-start | bytes 12582916 | tf_op jit(solution)/shard_map/cond
  78.8 11.1 %all-to-all-start.2 = ((bf16[8,32,384]{2,1,0:T(8,128)(2,1)}), bf16[8,32,384]{2,1,0:T(8,128)(2,1)S(1)}, u32[]{:S(2)}, u32[]{:S(2)}) async-start(bf16[8,32,384]{2,1,0:T(8,128)(2,1)} %get-tuple-element.73.refs_4_), calls=%async_computation.2 | async-start | bytes 393216 | tf_op jit(solution)/shard_map/cond/branch_0_fun/all_to_all | solution.py:708
  82.5 5.2 %copy-start.10 = (bf16[8,256,4,256]{3,1,2,0:T(8,128)(2,1)S(1)}, bf16[8,256,4,256]{3,1,2,0:T(8,128)(2,1)}, u32[]{:S(2)}) copy-start(bf16[8,256,4,256]{3,1,2,0:T(8,128)(2,1)} %copy-done.9) | copy-start | bytes 12582916 | tf_op jit(solution)/shard_map/cond
  82.5 7.4 %copy-start.6 = (bf16[4,1024,256]{2,1,0:T(8,128)(2,1)S(1)}, bf16[4,1024,256]{2,1,0:T(8,128)(2,1)}, u32[]{:S(2)}) copy-start(bf16[4,1024,256]{2,1,0:T(8,128)(2,1)} %get-tuple-element.79.refs_3_) | copy-start | bytes 6291460 | tf_op jit(solution)/shard_map/cond
  90.0 2.8 %copy-start.1 = (bf16[8,384,1024]{2,1,0:T(8,128)(2,1)S(1)}, bf16[8,384,1024]{2,1,0:T(8,128)(2,1)}, u32[]{:S(2)}) copy-start(bf16[8,384,1024]{2,1,0:T(8,128)(2,1)} %owner_lists.2.refs_2_) | copy-start | bytes 18874372 | tf_op jit(solution)/shard_map/cond
  99.0 6.2 %collective-permute-start.7 = (bf16[2,4,64,128]{3,2,1,0:T(8,128)(2,1)S(1)}, bf16[2,4,64,128]{3,2,1,0:T(8,128)(2,1)S(1)}, u32[]{:S(2)}, u32[]{:S(2)}) collective-permute-start(bf16[2,4,64,128]{3,2,1,0:T(8,128)(2,1)S(1)} %get-tuple-element.149), channel_id=1, source_target_pairs={{0,2},{2,0},{4,6},{6,4},{8,10},{10,8},{12,14},{14,12},{1,3},{3,1},... | collective-permute-start | bytes 393224 | tf_op jit(solution)/shard_map/ppermute | solution.py:472
  100.0 5.2 %collective-permute-start.8 = (bf16[2,4,64,128]{3,2,1,0:T(8,128)(2,1)S(1)}, bf16[2,4,64,128]{3,2,1,0:T(8,128)(2,1)S(1)}, u32[]{:S(2)}, u32[]{:S(2)}) collective-permute-start(bf16[2,4,64,128]{3,2,1,0:T(8,128)(2,1)S(1)} %get-tuple-element.150), channel_id=1, source_target_pairs={{0,4},{2,6},{4,0},{6,2},{8,12},{10,14},{12,8},{14,10},{1,5},{3,7},... | collective-permute-start | bytes 393224 | tf_op jit(solution)/shard_map/ppermute | solution.py:472
  100.5 6.4 %collective-permute-start.9 = (bf16[2,4,64,128]{3,2,1,0:T(8,128)(2,1)S(1)}, bf16[2,4,64,128]{3,2,1,0:T(8,128)(2,1)S(1)}, u32[]{:S(2)}, u32[]{:S(2)}) collective-permute-start(bf16[2,4,64,128]{3,2,1,0:T(8,128)(2,1)S(1)} %get-tuple-element.151), channel_id=1, source_target_pairs={{0,6},{2,4},{4,2},{6,0},{8,14},{10,12},{12,10},{14,8},{1,7},{3,5},... | collective-permute-start | bytes 393224 | tf_op jit(solution)/shard_map/ppermute | solution.py:472
  107.0 7.4 %collective-permute-start.10 = (bf16[2,4,64,128]{3,2,1,0:T(8,128)(2,1)S(1)}, bf16[2,4,64,128]{3,2,1,0:T(8,128)(2,1)S(1)}, u32[]{:S(2)}, u32[]{:S(2)}) collective-permute-start(bf16[2,4,64,128]{3,2,1,0:T(8,128)(2,1)S(1)} %get-tuple-element.154.after_ref), channel_id=1, source_target_pairs={{0,8},{2,10},{4,12},{6,14},{8,0},{10,2},{12,4},{14,6},{1,9},{3,11}... | collective-permute-start | bytes 393224 | tf_op jit(solution)/shard_map/ppermute | solution.py:472
  114.5 8.1 %collective-permute-start.13 = (bf16[16,4096]{1,0:T(8,128)(2,1)S(1)}, bf16[16,4096]{1,0:T(8,128)(2,1)S(1)}, u32[]{:S(2)}, u32[]{:S(2)}) collective-permute-start(bf16[16,4096]{1,0:T(8,128)(2,1)S(1)} %attended_sum.1), channel_id=1, source_target_pairs={{0,6},{2,4},{4,2},{6,0},{8,14},{10,12},{12,10},{14,8},{1,7},{3,5},... | collective-permute-start | bytes 393224 | tf_op jit(solution)/shard_map/ppermute | solution.py:472
  114.9 7.7 %collective-permute-start.12 = (bf16[16,4096]{1,0:T(8,128)(2,1)S(1)}, bf16[16,4096]{1,0:T(8,128)(2,1)S(1)}, u32[]{:S(2)}, u32[]{:S(2)}) collective-permute-start(bf16[16,4096]{1,0:T(8,128)(2,1)S(1)} %attended_sum.1), channel_id=1, source_target_pairs={{0,4},{2,6},{4,0},{6,2},{8,12},{10,14},{12,8},{14,10},{1,5},{3,7},... | collective-permute-start | bytes 393224 | tf_op jit(solution)/shard_map/ppermute | solution.py:472
  116.9 5.7 %collective-permute-start.11 = (bf16[16,4096]{1,0:T(8,128)(2,1)S(1)}, bf16[16,4096]{1,0:T(8,128)(2,1)S(1)}, u32[]{:S(2)}, u32[]{:S(2)}) collective-permute-start(bf16[16,4096]{1,0:T(8,128)(2,1)S(1)} %attended_sum.1), channel_id=1, source_target_pairs={{0,2},{2,0},{4,6},{6,4},{8,10},{10,8},{12,14},{14,12},{1,3},{3,1},... | collective-permute-start | bytes 393224 | tf_op jit(solution)/shard_map/ppermute | solution.py:472
  118.0 3.4 %copy-start.4 = (bf16[4096,1024]{1,0:T(8,128)(2,1)S(1)}, bf16[4096,1024]{1,0:T(8,128)(2,1)}, u32[]{:S(2)}) copy-start(bf16[4096,1024]{1,0:T(8,128)(2,1)} %weight_ref.1) | copy-start | bytes 25165828
  123.5 1.4 %collective-permute-start.14 = (f32[64,512]{1,0:T(8,128)S(1)}, f32[64,512]{1,0:T(8,128)S(1)}, u32[]{:S(2)}, u32[]{:S(2)}) collective-permute-start(f32[64,512]{1,0:T(8,128)S(1)} %fusion.47), channel_id=1, source_target_pairs={{0,1},{1,0},{2,3},{3,2},{4,5},{5,4},{6,7},{7,6},{8,9},{9,8},{10,11... | collective-permute-start | bytes 393224 | tf_op jit(solution)/shard_map/ppermute | solution.py:797

commit v21 on v18

--- a/solution.py
+++ b/solution.py
@@ -523,10 +523,11 @@
     pack_fill, pack_dest = block_fill, block_dest[:, 0]
     packed = pack(x_prompt, pack_fill, pack_dest, at, n, 0, size)
     dest = pack_dest
-    far = [with_partner(queries, k, n) for k in (n // 2, n // 4, n // 2 + n // 4)]
-    packed, far, dest, block_row, block_fill, kv_weight = lax.optimization_barrier(
-        (packed, far, dest, block_row, block_fill, kv_weight)
+    farthest = with_partner(queries, n // 2, n)
+    packed, farthest, later, dest, block_row, block_fill, kv_weight = lax.optimization_barrier(
+        (packed, farthest, queries, dest, block_row, block_fill, kv_weight)
     )
+    far = [farthest] + [with_partner(later, k, n) for k in (n // 4, n // 2 + n // 4)]
     kv_weight = kv_weight.transpose(1, 0, 2)
     even = from_rest(jnp.stack([queries, *far]), n)
     mine = lax.all_to_all(packed, "pool", 0, 0, tiled=True).reshape(n * size, part)

time: 126 us -> 126 us (level)
  waiting for transfers between devices: 35.4 us -> 34 us
  local copies, waits for them, and re-layouts: 16.6 us -> 17.9 us
    ppermute x11, waiting for transfers between devices: 17.6 us -> 15.4 us  [with_partner(): return lax.ppermute(x, 'pool', [(i, i ^ k) for i in range(n)])]
    optimization_barrier x1, local copies, waits for them, and re-layouts: 0.27 us -> 1.57 us  [local(): lax.optimization_barrier((packed, farthest, queries, dest, block_row, blo...]
  transfers between devices with their start and end apart: 17 -> 17, of which waited for: 10 -> 9; matrix products, arithmetic and copies ran while one was open for 12% -> 13% of each run, Pallas kernels for 12% -> 13%
where the time goes in v21:
time: 126 us; the launch traced here: 125 us
  waiting for transfers between devices  34 us (27%)
  Pallas kernels  31.1 us (25%)
  starting transfers between devices  31 us (25%)
  local copies, waits for them, and re-layouts  17.9 us (14%)
  other arithmetic  6.47 us (5%)
  matrix products  2.83 us (2%)
  between operations  1.47 us (1%)
    ppermute x11, starting transfers between devices, with_partner(): return lax.ppermute(x, 'pool', [(i, i ^ k) for i in range(n)])  17.5 us
    ppermute x11, waiting for transfers between devices, with_partner(): return lax.ppermute(x, 'pool', [(i, i ^ k) for i in range(n)])  15.4 us
    all_to_all x1, waiting for transfers between devices, local(): lax.all_to_all(packed, 'pool', 0, 0, tiled=True).reshape(n * size, part)  12.1 us
    pallas_call x1, Pallas kernels, local(): pl.pallas_call(functools.partial(score_kernel, n, rows), grid_spec=pltpu....  7.44 us
    unnamed x20, local copies, waits for them, and re-layouts  6.32 us
    pallas_call x1, Pallas kernels, exchange_weights(): pl.pallas_call(functools.partial(value_kernel, n, rows, lanes, count), gr...  5.99 us
    pallas_call x1, Pallas kernels, exchange_weights(): pl.pallas_call(functools.partial(list_kernel, n, lanes), grid_spec=pltpu....  5.14 us
    pallas_call x1, Pallas kernels, pack(): pl.pallas_call(functools.partial(pack_kernel, base), grid_spec=pltpu.Pref...  4.94 us
  transfers between devices with their start and end apart: 17, of which 9 were waited for; matrix products, arithmetic and copies ran while one was open for 13% of the time, Pallas kernels for 13%

profile of v21, /device:TPU:0, one launch (start us, length us, event | category | flops | bytes accessed | tf_op | source)
XLA Modules:
  0.0 125.1 jit_solution(1145817330149640808)
XLA Ops:
  0.0 4.0 %collective-permute-start.1 = (bf16[8,32,128]{2,1,0:T(8,128)(2,1)}, bf16[8,32,128]{2,1,0:T(8,128)(2,1)S(1)}, u32[]{:S(2)}, u32[]{:S(2)}) collective-permute-start(bf16[8,32,128]{2,1,0:T(8,128)(2,1)} %param.18), channel_id=1, source_target_pairs={{0,8},{2,10},{4,12},{6,14},{8,0},{10,2},{12,4},{14,6},{1,9},{3,11}... | collective-permute-start | bytes 196616 | tf_op jit(solution)/shard_map/ppermute | solution.py:478
  4.2 4.9 %pack_live_tokens.3 = bf16[8,96,1024]{2,1,0:T(8,128)(2,1)} custom-call(s32[2]{0:T(128)S(1)} %pad_add_fusion.at_ref, s32[256]{0:T(256)} %fill_ref.1, s32[256]{0:T(256)} %bitcast.56, bf16[256,8192]{1,0:T(8,128)(2,1)} %x_ref.1), custom_call_target="tpu_custom_call" | custom-call | flops 402653184 | bytes 67108864 | tf_op jit(solution)/shard_map/pack_live_tokens/pallas_call | solution.py:62
  9.1 2.2 %collective-permute-start.4 = (bf16[8,32,128]{2,1,0:T(8,128)(2,1)S(1)}, bf16[8,32,128]{2,1,0:T(8,128)(2,1)S(1)}, u32[]{:S(2)}, u32[]{:S(2)}) collective-permute-start(bf16[8,32,128]{2,1,0:T(8,128)(2,1)S(1)} %copy-done.12), channel_id=1, source_target_pairs={{0,12},{2,14},{4,8},{6,10},{8,4},{10,6},{12,0},{14,2},{1,13},{3,15... | collective-permute-start | bytes 196616 | tf_op jit(solution)/shard_map/ppermute | solution.py:478
  11.4 4.6 %all-to-all-start.7 = ((bf16[8,96,1024]{2,1,0:T(8,128)(2,1)}), bf16[8,96,1024]{2,1,0:T(8,128)(2,1)}, u32[]{:S(2)}, u32[]{:S(2)}) async-start(bf16[8,96,1024]{2,1,0:T(8,128)(2,1)} %pack_live_tokens.3), calls=%async_computation.7 | async-start | bytes 3145728 | tf_op jit(solution)/shard_map/all_to_all | solution.py:533
  16.0 0.2 select_reduce_fusion.4
  16.4 0.1 fusion.64
  16.5 0.1 select_reduce_fusion.6
  16.7 0.7 reduce_max.37
  17.3 0.1 reduce_sum.112
  17.5 0.6 reduce_max.36
  18.1 1.3 %pad_add_fusion.1 = s32[2]{0:T(128)S(1)} fusion(s32[1]{0:T(128)} %bitcast.10, s32[1]{0:T(128)} %bitcast.9), kind=kLoop, calls=%fused_computation.102 | loop fusion | flops 2 | bytes 16 | tf_op jit(solution)/shard_map/stack | solution.py:574
  19.4 1.5 %collective-permute-start.2 = (s32[2]{0:T(128)S(1)}, s32[2]{0:T(128)S(1)}, u32[]{:S(2)}, u32[]{:S(2)}) collective-permute-start(s32[2]{0:T(128)S(1)} %pad_add_fusion.1), channel_id=1, source_target_pairs={{0,16},{16,0},{1,17},{17,1},{2,18},{18,2},{3,19},{19,3},{4,20},{20... | collective-permute-start | bytes 32 | tf_op jit(solution)/shard_map/ppermute | solution.py:579
  20.9 1.6 %copy.28 = bf16[1024,4,256]{2,0,1:T(8,128)(2,1)} copy(bf16[1024,4,256]{2,1,0:T(4,128)(2,1)S(1)} %copy-done.11) | data formatting | bytes 4194304 | tf_op jit(solution)/shard_map/optimization_barrier | solution.py:527
  22.4 0.1 select_reduce_fusion.3
  22.5 0.3 select_reduce_fusion.2
  22.9 1.0 select_reduce_fusion
  23.9 0.1 fusion.45
  24.1 2.1 %collective-permute-start.5 = (bf16[4,8,32,128]{3,2,1,0:T(8,128)(2,1)S(1)}, bf16[4,8,32,128]{3,2,1,0:T(8,128)(2,1)S(1)}, u32[]{:S(2)}, u32[]{:S(2)}) collective-permute-start(bf16[4,8,32,128]{3,2,1,0:T(8,128)(2,1)S(1)} %pad_maximum_fusion.1), channel_id=1, source_target_pairs={{0,2},{2,0},{4,6},{6,4},{8,10},{10,8},{12,14},{14,12},{1,3},{3,1},... | collective-permute-start | bytes 786440 | tf_op jit(solution)/shard_map/ppermute | solution.py:478
  26.2 1.3 %fusion.71 = s32[2]{0:T(128)S(1)} fusion(s32[2]{0:T(128)S(1)} %collective-permute-done.2, s32[1]{0:T(128)} %bitcast.10, s32[1]{0:T(128)} %bitcast.9), kind=kLoop, calls=%fused_computation.114 | loop fusion | flops 4 | bytes 24 | tf_op jit(solution)/shard_map/max | solution.py:578
  27.4 0.6 fusion.68
  28.8 3.2 %key_projection.2.refs_4_ = bf16[4,256,1024]{2,1,0:T(8,128)(2,1)S(1)} custom-call(bf16[32,32,128]{2,1,0:T(8,128)(2,1)S(1)} %bitcast.42, bf16[4,1024,256]{2,1,0:T(8,128)(2,1)} %bitcast.44), custom_call_target="tpu_custom_call" | custom-call | bytes 1024 | tf_op jit(solution)/shard_map/key_projection/pallas_call | solution.py:599
  32.0 5.8 %collective-permute-done.5 = bf16[4,8,32,128]{3,2,1,0:T(8,128)(2,1)S(1)} collective-permute-done((bf16[4,8,32,128]{3,2,1,0:T(8,128)(2,1)S(1)}, bf16[4,8,32,128]{3,2,1,0:T(8,128)(2,1)S(1)}, u32[]{:S(2)}, u32[]{:S(2)}) %collective-permute-start.5) | collective-permute-done | bytes 262176 | tf_op jit(solution)/shard_map/ppermute | solution.py:478
  37.8 1.3 %key_projection.3.refs_5_ = bf16[4,256,1024]{2,1,0:T(8,128)(2,1)S(1)} custom-call(bf16[32,32,128]{2,1,0:T(8,128)(2,1)S(1)} %bitcast.43, bf16[4,1024,256]{2,1,0:T(8,128)(2,1)S(1)} %bitcast.47), custom_call_target="tpu_custom_call" | custom-call | bytes 1024 | tf_op jit(solution)/shard_map/key_projection/pallas_call | solution.py:599
  39.1 1.3 %copy-done.2 = bf16[4,256,1024]{2,1,0:T(8,128)(2,1)} copy-done((bf16[4,256,1024]{2,1,0:T(8,128)(2,1)}, bf16[4,256,1024]{2,1,0:T(8,128)(2,1)S(1)}, u32[]{:S(2)}) %copy-start.2) | copy-done | bytes 2097176
  40.4 12.1 %all-to-all-done.7 = bf16[8,96,1024]{2,1,0:T(8,128)(2,1)} async-done(((bf16[8,96,1024]{2,1,0:T(8,128)(2,1)}), bf16[8,96,1024]{2,1,0:T(8,128)(2,1)}, u32[]{:S(2)}, u32[]{:S(2)}) %all-to-all-start.7) | async-done | bytes 1572896 | tf_op jit(solution)/shard_map/all_to_all | solution.py:533
  53.1 1.7 %conditional.2 = (bf16[256,1024]{1,0:T(8,128)(2,1)}, bf16[256,1024]{1,0:T(8,128)(2,1)}) conditional(s32[]{:T(128)} %bitcast.21, () %tuple.25, (s32[2]{0:T(128)S(1)}, s32[256]{0:T(256)S(1)}, s32[256]{0:T(256)S(1)}, bf16[256,8192]{1,0:T(8,128)(2,1)}) %tuple.56), branch_computations={%region_12.13_spmd, %region_13.14_spmd} | conditional | flops 134217728 | bytes 70254648 | solution.py:592
  53.1 0.9 broadcast.406.clone
  53.9 0.9 broadcast.406
  54.8 1.4 %collective-permute-done.6.refs_1_ = bf16[768,1024]{1,0:T(8,128)(2,1)} collective-permute-done((bf16[768,1024]{1,0:T(8,128)(2,1)}, bf16[768,1024]{1,0:T(8,128)(2,1)}, u32[]{:S(2)}, u32[]{:S(2)}) %collective-permute-start.6) | collective-permute-done | bytes 1572896 | tf_op jit(solution)/shard_map/ppermute | solution.py:619
  56.3 1.6 %copy-done.3 = bf16[4,256,1024]{2,1,0:T(8,128)(2,1)S(1)} copy-done((bf16[4,256,1024]{2,1,0:T(8,128)(2,1)S(1)}, bf16[4,256,1024]{2,1,0:T(8,128)(2,1)}, u32[]{:S(2)}) %copy-start.3) | copy-done | bytes 2097176
  57.9 7.4 %prompt_scores.1 = (bf16[8,32,384]{2,1,0:T(8,128)(2,1)}, bf16[8,32,256]{2,1,0:T(8,128)(2,1)}) custom-call(s32[651]{0:T(1024)S(1)} %concatenate.6.meta_ref, bf16[768,1024]{1,0:T(8,128)(2,1)} %bitcast.12.refs_0_, bf16[768,1024]{1,0:T(8,128)(2,1)} %collective-permute-done.6.refs_1_, bf16[256,1024]{1,0:T(8,128)(2,1)} %get-tuple-element.139.refs_2_, ...), custom_call_target="tpu_custom_call" | custom-call | tf_op jit(solution)/shard_map/prompt_scores/pallas_call | solution.py:638
  65.3 33.2 %conditional.3 = (bf16[2,4,64,128]{3,2,1,0:T(8,128)(2,1)S(1)}, bf16[2,4,64,128]{3,2,1,0:T(8,128)(2,1)S(1)}, bf16[2,4,64,128]{3,2,1,0:T(8,128)(2,1)S(1)}, bf16[2,...) conditional(s32[]{:T(128)} %bitcast.11, (bf16[8,32,384]{2,1,0:T(8,128)(2,1)}, s32[1,640]{1,0:T(1,128)S(1)}, ...), branch_computations={%region_14.17_spmd, %region_17.20_spmd} | conditional | flops 34047488 | bytes 99326216 | solution.py:757
  65.3 3.7 %all-to-all-start.1 = ((bf16[8,32,384]{2,1,0:T(8,128)(2,1)}), bf16[8,32,384]{2,1,0:T(8,128)(2,1)S(1)}, u32[]{:S(2)}, u32[]{:S(2)}) async-start(bf16[8,32,384]{2,1,0:T(8,128)(2,1)} %get-tuple-element.68), calls=%async_computation.1 | async-start | bytes 393216 | tf_op jit(solution)/shard_map/cond/branch_0_fun/all_to_all | solution.py:668
  69.1 3.0 %copy.25 = bf16[8,256,4,256]{3,1,2,0:T(8,128)(2,1)S(1)} copy(bf16[8,256,4,256]{3,2,1,0:T(4,128)(2,1)} %get-tuple-element.209) | data formatting | bytes 8388608 | tf_op jit(solution)/shard_map
  72.1 0.7 fusion.66
  72.8 1.3 %copy-done.9 = bf16[8,256,4,256]{3,1,2,0:T(8,128)(2,1)} copy-done((bf16[8,256,4,256]{3,1,2,0:T(8,128)(2,1)}, bf16[8,256,4,256]{3,1,2,0:T(8,128)(2,1)S(1)}, u32[]{:S(2)}) %copy-start.9) | copy-done | bytes 4194328 | tf_op jit(solution)/shard_map/cond
  74.1 0.1 broadcast_in_dim.162.refs_2_
  74.2 0.2 fusion.17
  74.4 0.1 broadcast_in_dim.163.refs_3_
  74.5 2.7 %all-to-all-done.1.refs_0_ = bf16[8,32,384]{2,1,0:T(8,128)(2,1)S(1)} async-done(((bf16[8,32,384]{2,1,0:T(8,128)(2,1)}), bf16[8,32,384]{2,1,0:T(8,128)(2,1)S(1)}, u32[]{:S(2)}, u32[]{:S(2)}) %all-to-all-start.1) | async-done | bytes 196640 | tf_op jit(solution)/shard_map/cond/branch_0_fun/all_to_all | solution.py:668
  77.3 1.1 softmax_weights.2
  78.4 3.6 %all-to-all-start.2 = ((bf16[8,32,384]{2,1,0:T(8,128)(2,1)}), bf16[8,32,384]{2,1,0:T(8,128)(2,1)S(1)}, u32[]{:S(2)}, u32[]{:S(2)}) async-start(bf16[8,32,384]{2,1,0:T(8,128)(2,1)} %get-tuple-element.73.refs_4_), calls=%async_computation.2 | async-start | bytes 393216 | tf_op jit(solution)/shard_map/cond/branch_0_fun/all_to_all | solution.py:715
  81.9 0.1 reduce
  82.1 5.1 %owner_lists.2.refs_2_ = bf16[8,384,1024]{2,1,0:T(8,128)(2,1)} custom-call(s32[651]{0:T(1024)S(1)} %get-tuple-element.67.meta_ref, bf16[768,1024]{1,0:T(8,128)(2,1)} %get-tuple-element.75.refs_0_, bf16[768,1024]{1,0:T(8,128)(2,1)} %get-tuple-element.76.refs_1_, bf16[256,1024]{1,0:T(8,128)(2,1)} %get-tuple-element.77.refs_2_, ...), custom_call_target="tpu_custom_call" | custom-call | bytes 16777216 | tf_op jit(solution)/shard_map/cond/branch_0_fun/owner_lists/pallas_call | solution.py:694
  87.2 0.4 fusion.13
  87.7 1.8 %all-to-all-done.2.refs_0_ = bf16[8,32,384]{2,1,0:T(8,128)(2,1)S(1)} async-done(((bf16[8,32,384]{2,1,0:T(8,128)(2,1)}), bf16[8,32,384]{2,1,0:T(8,128)(2,1)S(1)}, u32[]{:S(2)}, u32[]{:S(2)}) %all-to-all-start.2) | async-done | bytes 196640 | tf_op jit(solution)/shard_map/cond/branch_0_fun/all_to_all | solution.py:715
  89.5 2.8 %copy-done.1 = bf16[8,384,1024]{2,1,0:T(8,128)(2,1)S(1)} copy-done((bf16[8,384,1024]{2,1,0:T(8,128)(2,1)S(1)}, bf16[8,384,1024]{2,1,0:T(8,128)(2,1)}, u32[]{:S(2)}) %copy-start.1) | copy-done | bytes 6291480 | tf_op jit(solution)/shard_map/cond
  92.3 6.0 %weighted_values.2 = (bf16[2,4,64,128]{3,2,1,0:T(8,128)(2,1)S(1)}, bf16[2,4,64,128]{3,2,1,0:T(8,128)(2,1)S(1)}, bf16[2,4,64,128]{3,2,1,0:T(8,128)(2,1)S(1)}, bf16[2,4,64,128]{3,2,1,0:T(8,128)(2,1)S(1)}) custom-call(s32[651]{0:T(1024)S(1)} %get-tuple-element.67.meta_ref, bf16[8,32,384]{2,1,0:T(8,128)(2,1)S(1)} %all-to-all-done.2.refs_0_, ...), custom_call_target="tpu_custom_call" | custom-call | tf_op jit(solution)/shard_map/cond/branch_0_fun/weighted_values/pallas_call | solution.py:722
  98.5 1.0 collective-permute-start.7
  99.5 0.4 collective-permute-start.8
  100.0 2.1 %collective-permute-start.9 = (bf16[2,4,64,128]{3,2,1,0:T(8,128)(2,1)S(1)}, bf16[2,4,64,128]{3,2,1,0:T(8,128)(2,1)S(1)}, u32[]{:S(2)}, u32[]{:S(2)}) collective-permute-start(bf16[2,4,64,128]{3,2,1,0:T(8,128)(2,1)S(1)} %get-tuple-element.149), channel_id=1, source_target_pairs={{0,6},{2,4},{4,2},{6,0},{8,14},{10,12},{12,10},{14,8},{1,7},{3,5},... | collective-permute-start | bytes 393224 | tf_op jit(solution)/shard_map/ppermute | solution.py:478
  102.1 2.6 %collective-permute-done.7.refs_1_ = bf16[2,4,64,128]{3,2,1,0:T(8,128)(2,1)S(1)} collective-permute-done((bf16[2,4,64,128]{3,2,1,0:T(8,128)(2,1)S(1)}, bf16[2,4,64,128]{3,2,1,0:T(8,128)(2,1)S(1)}, u32[]{:S(2)}, u32[]{:S(2)}) %collective-permute-start.7) | collective-permute-done | bytes 131104 | tf_op jit(solution)/shard_map/ppermute | solution.py:478
  104.7 1.7 %collective-permute-done.9.refs_3_ = bf16[2,4,64,128]{3,2,1,0:T(8,128)(2,1)S(1)} collective-permute-done((bf16[2,4,64,128]{3,2,1,0:T(8,128)(2,1)S(1)}, bf16[2,4,64,128]{3,2,1,0:T(8,128)(2,1)S(1)}, u32[]{:S(2)}, u32[]{:S(2)}) %collective-permute-start.9) | collective-permute-done | bytes 131104 | tf_op jit(solution)/shard_map/ppermute | solution.py:478
  106.5 2.1 %collective-permute-start.10 = (bf16[2,4,64,128]{3,2,1,0:T(8,128)(2,1)S(1)}, bf16[2,4,64,128]{3,2,1,0:T(8,128)(2,1)S(1)}, u32[]{:S(2)}, u32[]{:S(2)}) collective-permute-start(bf16[2,4,64,128]{3,2,1,0:T(8,128)(2,1)S(1)} %get-tuple-element.152.after_ref), channel_id=1, source_target_pairs={{0,8},{2,10},{4,12},{6,14},{8,0},{10,2},{12,4},{14,6},{1,9},{3,11}... | collective-permute-start | bytes 393224 | tf_op jit(solution)/shard_map/ppermute | solution.py:478
  108.6 5.3 %collective-permute-done.10.got_ref = bf16[2,4,64,128]{3,2,1,0:T(8,128)(2,1)S(1)} collective-permute-done((bf16[2,4,64,128]{3,2,1,0:T(8,128)(2,1)S(1)}, bf16[2,4,64,128]{3,2,1,0:T(8,128)(2,1)S(1)}, u32[]{:S(2)}, u32[]{:S(2)}) %collective-permute-start.10) | collective-permute-done | bytes 131104 | tf_op jit(solution)/shard_map/ppermute | solution.py:478
  114.0 0.4 collective-permute-start.13
  114.4 2.1 %collective-permute-start.12 = (bf16[16,4096]{1,0:T(8,128)(2,1)S(1)}, bf16[16,4096]{1,0:T(8,128)(2,1)S(1)}, u32[]{:S(2)}, u32[]{:S(2)}) collective-permute-start(bf16[16,4096]{1,0:T(8,128)(2,1)S(1)} %attended_sum.1), channel_id=1, source_target_pairs={{0,4},{2,6},{4,0},{6,2},{8,12},{10,14},{12,8},{14,10},{1,5},{3,7},... | collective-permute-start | bytes 393224 | tf_op jit(solution)/shard_map/ppermute | solution.py:478
  116.5 1.1 collective-permute-start.11
  117.6 3.4 %copy-done.4 = bf16[4096,1024]{1,0:T(8,128)(2,1)S(1)} copy-done((bf16[4096,1024]{1,0:T(8,128)(2,1)S(1)}, bf16[4096,1024]{1,0:T(8,128)(2,1)}, u32[]{:S(2)}) %copy-start.4) | copy-done | bytes 8388632
  120.9 1.2 stage_out_weight.1
  122.2 0.8 fusion.47
  123.1 0.8 fusion.48.own_ref
  123.9 0.5 collective-permute-done.14.got_ref
  124.4 0.6 order_rows.1
  (55 shorter events, 1.0 us)
Async XLA Ops:
  0.0 9.1 %copy-start.12 = (bf16[8,32,128]{2,1,0:T(8,128)(2,1)S(1)}, bf16[8,32,128]{2,1,0:T(8,128)(2,1)}, u32[]{:S(2)}) copy-start(bf16[8,32,128]{2,1,0:T(8,128)(2,1)} %param.18) | copy-start | bytes 196612
  0.0 11.3 %copy-start.14 = (s32[256]{0:T(256)S(1)}, s32[256]{0:T(256)}, u32[]{:S(2)}) copy-start(s32[256]{0:T(256)} %fill_ref.1) | copy-start | bytes 3076
  0.0 9.1 %collective-permute-start.1 = (bf16[8,32,128]{2,1,0:T(8,128)(2,1)}, bf16[8,32,128]{2,1,0:T(8,128)(2,1)S(1)}, u32[]{:S(2)}, u32[]{:S(2)}) collective-permute-start(bf16[8,32,128]{2,1,0:T(8,128)(2,1)} %param.18), channel_id=1, source_target_pairs={{0,8},{2,10},{4,12},{6,14},{8,0},{10,2},{12,4},{14,6},{1,9},{3,11}... | collective-permute-start | bytes 196616 | tf_op jit(solution)/shard_map/ppermute | solution.py:478
  4.1 11.9 %copy-start.13 = (s32[256,1]{0,1:T(1,128)S(1)}, s32[256,1]{0,1:T(1,128)}, u32[]{:S(2)}) copy-start(s32[256,1]{0,1:T(1,128)} %param.15) | copy-start | bytes 3076
  4.1 16.7 %copy-start.11 = (bf16[1024,4,256]{2,1,0:T(4,128)(2,1)S(1)}, bf16[1024,4,256]{2,1,0:T(4,128)(2,1)}, u32[]{:S(2)}) copy-start(bf16[1024,4,256]{2,1,0:T(4,128)(2,1)} %param.14) | copy-start | bytes 6291460
  9.1 13.3 %copy-start.16 = (s32[256]{0:T(256)S(1)}, s32[256]{0:T(256)}, u32[]{:S(2)}) copy-start(s32[256]{0:T(256)} %param.16) | copy-start | bytes 3076
  9.1 14.9 %collective-permute-start.4 = (bf16[8,32,128]{2,1,0:T(8,128)(2,1)S(1)}, bf16[8,32,128]{2,1,0:T(8,128)(2,1)S(1)}, u32[]{:S(2)}, u32[]{:S(2)}) collective-permute-start(bf16[8,32,128]{2,1,0:T(8,128)(2,1)S(1)} %copy-done.12), channel_id=1, source_target_pairs={{0,12},{2,14},{4,8},{6,10},{8,4},{10,6},{12,0},{14,2},{1,13},{3,15... | collective-permute-start | bytes 196616 | tf_op jit(solution)/shard_map/ppermute | solution.py:478
  11.3 12.7 %collective-permute-start.3 = (bf16[8,32,128]{2,1,0:T(8,128)(2,1)S(1)}, bf16[8,32,128]{2,1,0:T(8,128)(2,1)S(1)}, u32[]{:S(2)}, u32[]{:S(2)}) collective-permute-start(bf16[8,32,128]{2,1,0:T(8,128)(2,1)S(1)} %copy-done.12), channel_id=1, source_target_pairs={{0,4},{2,6},{4,0},{6,2},{8,12},{10,14},{12,8},{14,10},{1,5},{3,7},... | collective-permute-start | bytes 196616 | tf_op jit(solution)/shard_map/ppermute | solution.py:478
  11.4 41.1 %all-to-all-start.7 = ((bf16[8,96,1024]{2,1,0:T(8,128)(2,1)}), bf16[8,96,1024]{2,1,0:T(8,128)(2,1)}, u32[]{:S(2)}, u32[]{:S(2)}) async-start(bf16[8,96,1024]{2,1,0:T(8,128)(2,1)} %pack_live_tokens.3), calls=%async_computation.7 | async-start | bytes 3145728 | tf_op jit(solution)/shard_map/all_to_all | solution.py:533
  19.4 6.8 %collective-permute-start.2 = (s32[2]{0:T(128)S(1)}, s32[2]{0:T(128)S(1)}, u32[]{:S(2)}, u32[]{:S(2)}) collective-permute-start(s32[2]{0:T(128)S(1)} %pad_add_fusion.1), channel_id=1, source_target_pairs={{0,16},{16,0},{1,17},{17,1},{2,18},{18,2},{3,19},{19,3},{4,20},{20... | collective-permute-start | bytes 32 | tf_op jit(solution)/shard_map/ppermute | solution.py:579
  24.1 13.7 %collective-permute-start.5 = (bf16[4,8,32,128]{3,2,1,0:T(8,128)(2,1)S(1)}, bf16[4,8,32,128]{3,2,1,0:T(8,128)(2,1)S(1)}, u32[]{:S(2)}, u32[]{:S(2)}) collective-permute-start(bf16[4,8,32,128]{3,2,1,0:T(8,128)(2,1)S(1)} %pad_maximum_fusion.1), channel_id=1, source_target_pairs={{0,2},{2,0},{4,6},{6,4},{8,10},{10,8},{12,14},{14,12},{1,3},{3,1},... | collective-permute-start | bytes 786440 | tf_op jit(solution)/shard_map/ppermute | solution.py:478
  28.8 9.0 %copy-start.5 = (bf16[1024,4,256]{2,0,1:T(8,128)(2,1)S(1)}, bf16[1024,4,256]{2,0,1:T(8,128)(2,1)}, u32[]{:S(2)}) copy-start(bf16[1024,4,256]{2,0,1:T(8,128)(2,1)} %copy.28) | copy-start | bytes 6291460
  39.1 1.3 %copy-start.2 = (bf16[4,256,1024]{2,1,0:T(8,128)(2,1)}, bf16[4,256,1024]{2,1,0:T(8,128)(2,1)S(1)}, u32[]{:S(2)}) copy-start(bf16[4,256,1024]{2,1,0:T(8,128)(2,1)S(1)} %key_projection.3.refs_5_) | copy-start | bytes 6291460
  52.5 3.8 %collective-permute-start.6 = (bf16[768,1024]{1,0:T(8,128)(2,1)}, bf16[768,1024]{1,0:T(8,128)(2,1)}, u32[]{:S(2)}, u32[]{:S(2)}) collective-permute-start(bf16[768,1024]{1,0:T(8,128)(2,1)} %bitcast.12.refs_0_), channel_id=1, source_target_pairs={{0,1},{1,0},{2,3},{3,2},{4,5},{5,4},{6,7},{7,6},{8,9},{9,8},{10,11... | collective-permute-start | bytes 4718600 | tf_op jit(solution)/shard_map/ppermute | solution.py:619
  56.3 1.6 %copy-start.3 = (bf16[4,256,1024]{2,1,0:T(8,128)(2,1)S(1)}, bf16[4,256,1024]{2,1,0:T(8,128)(2,1)}, u32[]{:S(2)}) copy-start(bf16[4,256,1024]{2,1,0:T(8,128)(2,1)} %copy-done.2) | copy-start | bytes 6291460
  57.9 7.4 %copy-start.15 = (s32[8]{0:T(128)S(1)}, s32[8]{0:T(128)}, u32[]{:S(2)}) copy-start(s32[8]{0:T(128)} %param.20) | copy-start | bytes 100
  65.3 11.9 %all-to-all-start.1 = ((bf16[8,32,384]{2,1,0:T(8,128)(2,1)}), bf16[8,32,384]{2,1,0:T(8,128)(2,1)S(1)}, u32[]{:S(2)}, u32[]{:S(2)}) async-start(bf16[8,32,384]{2,1,0:T(8,128)(2,1)} %get-tuple-element.68), calls=%async_computation.1 | async-start | bytes 393216 | tf_op jit(solution)/shard_map/cond/branch_0_fun/all_to_all | solution.py:668
  72.1 2.0 %copy-start.9 = (bf16[8,256,4,256]{3,1,2,0:T(8,128)(2,1)}, bf16[8,256,4,256]{3,1,2,0:T(8,128)(2,1)S(1)}, u32[]{:S(2)}) copy-start(bf16[8,256,4,256]{3,1,2,0:T(8,128)(2,1)S(1)} %copy.25) | copy-start | bytes 12582916 | tf_op jit(solution)/shard_map/cond
  78.4 11.1 %all-to-all-start.2 = ((bf16[8,32,384]{2,1,0:T(8,128)(2,1)}), bf16[8,32,384]{2,1,0:T(8,128)(2,1)S(1)}, u32[]{:S(2)}, u32[]{:S(2)}) async-start(bf16[8,32,384]{2,1,0:T(8,128)(2,1)} %get-tuple-element.73.refs_4_), calls=%async_computation.2 | async-start | bytes 393216 | tf_op jit(solution)/shard_map/cond/branch_0_fun/all_to_all | solution.py:715
  82.1 5.2 %copy-start.10 = (bf16[8,256,4,256]{3,1,2,0:T(8,128)(2,1)S(1)}, bf16[8,256,4,256]{3,1,2,0:T(8,128)(2,1)}, u32[]{:S(2)}) copy-start(bf16[8,256,4,256]{3,1,2,0:T(8,128)(2,1)} %copy-done.9) | copy-start | bytes 12582916 | tf_op jit(solution)/shard_map/cond
  82.1 7.4 %copy-start.6 = (bf16[4,1024,256]{2,1,0:T(8,128)(2,1)S(1)}, bf16[4,1024,256]{2,1,0:T(8,128)(2,1)}, u32[]{:S(2)}) copy-start(bf16[4,1024,256]{2,1,0:T(8,128)(2,1)} %get-tuple-element.79.refs_3_) | copy-start | bytes 6291460 | tf_op jit(solution)/shard_map/cond
  89.5 2.8 %copy-start.1 = (bf16[8,384,1024]{2,1,0:T(8,128)(2,1)S(1)}, bf16[8,384,1024]{2,1,0:T(8,128)(2,1)}, u32[]{:S(2)}) copy-start(bf16[8,384,1024]{2,1,0:T(8,128)(2,1)} %owner_lists.2.refs_2_) | copy-start | bytes 18874372 | tf_op jit(solution)/shard_map/cond
  98.5 6.2 %collective-permute-start.7 = (bf16[2,4,64,128]{3,2,1,0:T(8,128)(2,1)S(1)}, bf16[2,4,64,128]{3,2,1,0:T(8,128)(2,1)S(1)}, u32[]{:S(2)}, u32[]{:S(2)}) collective-permute-start(bf16[2,4,64,128]{3,2,1,0:T(8,128)(2,1)S(1)} %get-tuple-element.147), channel_id=1, source_target_pairs={{0,2},{2,0},{4,6},{6,4},{8,10},{10,8},{12,14},{14,12},{1,3},{3,1},... | collective-permute-start | bytes 393224 | tf_op jit(solution)/shard_map/ppermute | solution.py:478
  99.5 5.2 %collective-permute-start.8 = (bf16[2,4,64,128]{3,2,1,0:T(8,128)(2,1)S(1)}, bf16[2,4,64,128]{3,2,1,0:T(8,128)(2,1)S(1)}, u32[]{:S(2)}, u32[]{:S(2)}) collective-permute-start(bf16[2,4,64,128]{3,2,1,0:T(8,128)(2,1)S(1)} %get-tuple-element.148), channel_id=1, source_target_pairs={{0,4},{2,6},{4,0},{6,2},{8,12},{10,14},{12,8},{14,10},{1,5},{3,7},... | collective-permute-start | bytes 393224 | tf_op jit(solution)/shard_map/ppermute | solution.py:478
  100.0 6.4 %collective-permute-start.9 = (bf16[2,4,64,128]{3,2,1,0:T(8,128)(2,1)S(1)}, bf16[2,4,64,128]{3,2,1,0:T(8,128)(2,1)S(1)}, u32[]{:S(2)}, u32[]{:S(2)}) collective-permute-start(bf16[2,4,64,128]{3,2,1,0:T(8,128)(2,1)S(1)} %get-tuple-element.149), channel_id=1, source_target_pairs={{0,6},{2,4},{4,2},{6,0},{8,14},{10,12},{12,10},{14,8},{1,7},{3,5},... | collective-permute-start | bytes 393224 | tf_op jit(solution)/shard_map/ppermute | solution.py:478
  106.5 7.4 %collective-permute-start.10 = (bf16[2,4,64,128]{3,2,1,0:T(8,128)(2,1)S(1)}, bf16[2,4,64,128]{3,2,1,0:T(8,128)(2,1)S(1)}, u32[]{:S(2)}, u32[]{:S(2)}) collective-permute-start(bf16[2,4,64,128]{3,2,1,0:T(8,128)(2,1)S(1)} %get-tuple-element.152.after_ref), channel_id=1, source_target_pairs={{0,8},{2,10},{4,12},{6,14},{8,0},{10,2},{12,4},{14,6},{1,9},{3,11}... | collective-permute-start | bytes 393224 | tf_op jit(solution)/shard_map/ppermute | solution.py:478
  114.0 8.1 %collective-permute-start.13 = (bf16[16,4096]{1,0:T(8,128)(2,1)S(1)}, bf16[16,4096]{1,0:T(8,128)(2,1)S(1)}, u32[]{:S(2)}, u32[]{:S(2)}) collective-permute-start(bf16[16,4096]{1,0:T(8,128)(2,1)S(1)} %attended_sum.1), channel_id=1, source_target_pairs={{0,6},{2,4},{4,2},{6,0},{8,14},{10,12},{12,10},{14,8},{1,7},{3,5},... | collective-permute-start | bytes 393224 | tf_op jit(solution)/shard_map/ppermute | solution.py:478
  114.4 7.8 %collective-permute-start.12 = (bf16[16,4096]{1,0:T(8,128)(2,1)S(1)}, bf16[16,4096]{1,0:T(8,128)(2,1)S(1)}, u32[]{:S(2)}, u32[]{:S(2)}) collective-permute-start(bf16[16,4096]{1,0:T(8,128)(2,1)S(1)} %attended_sum.1), channel_id=1, source_target_pairs={{0,4},{2,6},{4,0},{6,2},{8,12},{10,14},{12,8},{14,10},{1,5},{3,7},... | collective-permute-start | bytes 393224 | tf_op jit(solution)/shard_map/ppermute | solution.py:478
  116.5 5.7 %collective-permute-start.11 = (bf16[16,4096]{1,0:T(8,128)(2,1)S(1)}, bf16[16,4096]{1,0:T(8,128)(2,1)S(1)}, u32[]{:S(2)}, u32[]{:S(2)}) collective-permute-start(bf16[16,4096]{1,0:T(8,128)(2,1)S(1)} %attended_sum.1), channel_id=1, source_target_pairs={{0,2},{2,0},{4,6},{6,4},{8,10},{10,8},{12,14},{14,12},{1,3},{3,1},... | collective-permute-start | bytes 393224 | tf_op jit(solution)/shard_map/ppermute | solution.py:478
  117.6 3.4 %copy-start.4 = (bf16[4096,1024]{1,0:T(8,128)(2,1)S(1)}, bf16[4096,1024]{1,0:T(8,128)(2,1)}, u32[]{:S(2)}) copy-start(bf16[4096,1024]{1,0:T(8,128)(2,1)} %weight_ref.1) | copy-start | bytes 25165828
  123.0 1.4 %collective-permute-start.14 = (f32[64,512]{1,0:T(8,128)S(1)}, f32[64,512]{1,0:T(8,128)S(1)}, u32[]{:S(2)}, u32[]{:S(2)}) collective-permute-start(f32[64,512]{1,0:T(8,128)S(1)} %fusion.47), channel_id=1, source_target_pairs={{0,1},{1,0},{2,3},{3,2},{4,5},{5,4},{6,7},{7,6},{8,9},{9,8},{10,11... | collective-permute-start | bytes 393224 | tf_op jit(solution)/shard_map/ppermute | solution.py:804
